TPU v7x, 32 devices: a whole 2x2x4 slice. The times are simulated.
32 devices in a mesh: groups: 2 (over y), row: 4 (over x, core), col: 4 (over z).
Axes of the slice: x: 2, y: 2, z: 4, core: 2. Of those that a mesh axis runs over, the one named last changes fastest.
Arguments:
- features: bfloat16 [4096, 128], P(('groups', 'row', 'col')), parts along dimension 0, may hold values from -6 to 6
- weight: bfloat16 [128, 256], replicated, may hold values from -0.5 to 0.5
- cotangent: bfloat16 [4096, 256], P(('groups', 'row', 'col')), parts along dimension 0, may hold values from -6 to 6
- tile_values: bfloat16 [8, 4, 8, 128, 128], P(('groups', 'row'), 'col'), parts along dimension 0, may hold values from -0.3125 to 0.3125
- tile_rows: int32 [8, 4, 8], P(('groups', 'row'), 'col'), parts along dimension 0, may hold values from 0 to 3, as said below
- tile_cols: int32 [8, 4, 8], P(('groups', 'row'), 'col'), parts along dimension 0, may hold values from 0 to 3
- tile_count: int32 [8, 4], P(('groups', 'row'), 'col'), parts along dimension 0, may hold values from 2 to 8, as said below
Outputs:
- act: bfloat16 [4096, 256], P(('groups', 'row', 'col')), parts along dimension 0
- grad_features: bfloat16 [4096, 128], P(('groups', 'row', 'col')), parts along dimension 0
- grad_weight: float32 [256, 256], P('groups'), parts along dimension 0
There are 2 independent parts, one for each index of `groups`. A program takes and returns all parts, laid end to end along the dimension named above; an argument that names none is the same for every part. Nothing has to cross between parts.
Inputs may be any that keep to these rules, and one draw needn't show every extreme that they name: Within one grid cell the pairs (tile_rows, tile_cols) of all 8 slots are distinct. `tile_count`: some grid cell has all 8 slots live.
All inputs are finite; a program needn't handle non-finite values.
Results may differ from a plain program's by a relative error of at most 0.009.
Values may be sent and summed in bfloat16 or wider, within the bound.
No kernel may reach another device: no remote copies, remote signals or barrier semaphores. Data moves between devices by JAX's collectives and lax.ppermute only.
A program may use at most 64 MiB of HBM per device.

v0:
```python
import math

import jax
import jax.numpy as jnp
from jax import lax
from jax.sharding import PartitionSpec as P


def tile_product(tile_vals, take_ids, place_ids, live_slots, operand, out_tiles, transposed):
    tiles_total = tile_vals.shape[0]
    tile_side = tile_vals.shape[1]
    width = operand.shape[1]
    precise = operand.dtype == jnp.float32
    high_part = operand.astype(jnp.bfloat16)
    low_part = (operand - high_part.astype(jnp.float32)).astype(jnp.bfloat16)
    stacked = (high_part.reshape(-1, tile_side, width), low_part.reshape(-1, tile_side, width))
    group_size = math.gcd(16, tiles_total)
    turns = tiles_total // group_size
    targets = jnp.arange(out_tiles, dtype=jnp.int32)
    if transposed:
        form = "tab,taf->tbf"
    else:
        form = "tab,tbf->taf"

    def accumulate(total, inputs):
        block_vals, block_take, block_place, block_live = inputs
        product = jnp.zeros((block_vals.shape[0], tile_side, width), jnp.float32)
        for member in stacked:
            taken = jnp.take(member, block_take, axis=0)
            product = product + jnp.einsum(
                form, block_vals, taken, preferred_element_type=jnp.float32
            )
        selector = ((block_place[:, None] == targets[None, :]) & block_live[:, None]).astype(
            jnp.float32
        )
        added = jnp.einsum("tk,taf->kaf", selector, product, precision=lax.Precision.HIGHEST)
        return (total + added, None)

    inputs = (
        tile_vals.reshape(turns, group_size, tile_side, tile_side),
        take_ids.reshape(turns, group_size),
        place_ids.reshape(turns, group_size),
        live_slots.reshape(turns, group_size),
    )
    start = jnp.zeros((out_tiles, tile_side, width), jnp.float32)
    total, _ = lax.scan(accumulate, start, inputs)
    return total.reshape(out_tiles * tile_side, width)


def per_device(features, weight, cotangent, tile_values, tile_rows, tile_cols, tile_count):
    highest = lax.Precision.HIGHEST
    tile_vals = tile_values.reshape(tile_values.shape[2:])
    row_take = tile_rows.reshape(-1)
    col_take = tile_cols.reshape(-1)
    count = tile_count.reshape(())
    grid_rows = lax.axis_size("row")
    grid_cols = lax.axis_size("col")
    tile_side = tile_vals.shape[1]
    node_rows = features.shape[0]
    piece_tiles = node_rows // tile_side
    block_tiles = grid_cols * piece_tiles
    set_tiles = grid_rows * piece_tiles
    live_slots = jnp.arange(tile_vals.shape[0], dtype=jnp.int32) < count
    weight_wide = weight.astype(jnp.float32)
    projected = jnp.dot(features, weight, preferred_element_type=jnp.float32)
    gathered = lax.all_gather(projected, "row", axis=0, tiled=True)
    partial_value = tile_product(
        tile_vals, col_take, row_take, live_slots, gathered, block_tiles, False
    )
    pre = lax.psum_scatter(partial_value, "col", scatter_dimension=0, tiled=True)
    sigma = jax.nn.sigmoid(pre)
    grad_pre = cotangent.astype(jnp.float32) * sigma * (1.0 + pre * (1.0 - sigma))
    spread = lax.all_gather(grad_pre, "col", axis=0, tiled=True)
    partial_back = tile_product(tile_vals, row_take, col_take, live_slots, spread, set_tiles, True)
    grad_projected = lax.psum_scatter(partial_back, "row", scatter_dimension=0, tiled=True)
    grad_features = jnp.dot(grad_projected, weight_wide.T, precision=highest).astype(jnp.bfloat16)
    weight_term = jnp.dot(features.astype(jnp.float32).T, grad_projected, precision=highest)
    act = jax.nn.silu(pre).astype(jnp.bfloat16)
    node_total = node_rows * grid_rows * grid_cols
    grad_weight = lax.psum(weight_term, ("row", "col")) * float(node_total) ** (-0.5)
    return (act, grad_features, grad_weight)


def solution(mesh):
    placed = (
        P(("groups", "row", "col"), None),
        P(),
        P(("groups", "row", "col"), None),
        P(("groups", "row"), "col", None, None, None),
        P(("groups", "row"), "col", None),
        P(("groups", "row"), "col", None),
        P(("groups", "row"), "col"),
    )
    return jax.shard_map(
        per_device,
        mesh=mesh,
        in_specs=placed,
        out_specs=(
            P(("groups", "row", "col"), None),
            P(("groups", "row", "col"), None),
            P("groups", None),
        ),
        check_vma=False,
    )
```

profile of v0, /device:TPU:0, one launch (start us, length us, event | category | flops | bytes accessed | tf_op | source)
XLA Modules:
  0.0 191.6 jit_solution(14439890701117968805)
XLA Ops:
  7.2 0.0 copy-start
  7.2 0.0 copy-start.6
  7.2 0.0 reduce-scatter.3.cloned.1.call-start
  7.2 0.7 compare_and_fusion.1
  7.9 0.0 copy-done.6
  8.6 1.0 fusion.40
  9.6 8.6 %all_gather.6 = f32[512,256]{1,0:T(8,128)S(1)} all-gather(f32[128,256]{1,0:T(8,128)S(1)} %fusion.40), channel_id=1, replica_groups=mesh['groups'=2,'row'=4,'col'=4] {'row'}, dimensions={0}, use_global_device_ids=true | all-gather | bytes 655360 | tf_op jit(solution)/shard_map/all_gather | solution.py:66
  18.2 0.1 subtract_convert_fusion.1
  18.3 1.4 gather_fusion
  19.7 0.6 gather_fusion.1
  20.3 0.0 copy-done
  20.3 0.4 fusion.10
  20.7 0.5 copy.15
  21.2 1.5 fusion.12
  22.7 0.5 copy.14
  23.1 0.0 copy-start.5
  23.1 0.6 copy-done.5
  23.8 0.6 fusion.2
  24.4 0.9 copy.11
  25.3 0.0 copy-start.4
  25.3 0.0 reduce-scatter.3.cloned.1.call-update
  25.3 0.0 reduce-scatter.5.cloned.1.call-start
  25.4 22.6 %reduce-scatter.3.cloned.1.call-done = f32[128,256]{1,0:T(8,128)} async-done(((f32[512,256]{1,0:T(8,128)}), f32[128,256]{1,0:T(8,128)}) %reduce-scatter.3.cloned.1.call-update) | async-done | bytes 131088 | tf_op jit(solution)/shard_map/reduce_scatter | solution.py:70
  48.0 0.0 copy-done.4
  48.0 1.6 add_multiply_fusion
  49.6 15.9 %all_gather.7 = f32[512,256]{1,0:T(8,128)S(1)} all-gather(f32[128,256]{1,0:T(8,128)S(1)} %get-tuple-element.59), channel_id=1, replica_groups=mesh['groups'=2,'row'=4,'col'=4] {'col'}, dimensions={0}, use_global_device_ids=true | all-gather | bytes 655360 | tf_op jit(solution)/shard_map/all_gather | solution.py:73
  65.5 0.1 subtract_convert_fusion
  65.5 1.4 gather_fusion.2
  66.9 0.6 gather_fusion.3
  67.5 0.4 fusion.6
  67.9 0.5 copy.17
  68.4 1.5 fusion.8
  69.9 0.5 copy.16
  70.4 0.6 fusion
  71.0 0.9 copy.12
  71.9 0.0 copy-start.3
  71.9 0.0 reduce-scatter.5.cloned.1.call-update
  71.9 0.0 all-reduce.2.cloned.1.call-start
  72.0 20.0 %reduce-scatter.5.cloned.1.call-done = f32[128,256]{1,0:T(8,128)} async-done(((f32[512,256]{1,0:T(8,128)}), f32[128,256]{1,0:T(8,128)}) %reduce-scatter.5.cloned.1.call-update) | async-done | bytes 131088 | tf_op jit(solution)/shard_map/reduce_scatter | solution.py:75
  91.9 0.0 copy-done.3
  91.9 1.8 convolution_bitcast_fusion
  93.8 0.0 all-reduce.2.cloned.1.call-update
  93.8 0.0 copy-done.2
  93.8 0.9 copy-done.1
  94.7 0.8 convolution_convert_fusion
  95.5 87.9 %all-reduce.2.cloned.1.call-done = f32[128,256]{0,1:T(8,128)} async-done(((f32[128,256]{0,1:T(8,128)}), f32[128,256]{0,1:T(8,128)}) %all-reduce.2.cloned.1.call-update) | async-done | bytes 131088 | tf_op jit(solution)/shard_map/psum | solution.py:80
  183.4 0.9 broadcast_multiply_fusion
  184.4 0.8 copy.13
  (8 shorter events, 0.0 us)
Async XLA Ops:
  7.2 13.1 %copy-start = (bf16[1,1,8,128,128]{4,3,2,1,0:T(8,128)(2,1)S(1)}, bf16[1,1,8,128,128]{4,3,2,1,0:T(8,128)(2,1)}, u32[]{:S(2)}) copy-start(bf16[1,1,8,128,128]{4,3,2,1,0:T(8,128)(2,1)} %param.12) | copy-start | bytes 786436
  7.2 0.8 copy-start.6
  7.2 40.8 %reduce-scatter.3.cloned.1.call-start = ((), (), s32[]{:S(2)}) async-start(), calls=%async_computation.2 | async-start | bytes 655360 | tf_op jit(solution)/shard_map/reduce_scatter | solution.py:70
  23.1 0.7 copy-start.5
  25.3 22.7 %copy-start.4 = (bf16[128,256]{1,0:T(8,128)(2,1)S(1)}, bf16[128,256]{1,0:T(8,128)(2,1)}, u32[]{:S(2)}) copy-start(bf16[128,256]{1,0:T(8,128)(2,1)} %param.11) | copy-start | bytes 196612
  25.3 66.6 %reduce-scatter.5.cloned.1.call-start = ((), (), s32[]{:S(2)}) async-start(), calls=%async_computation.3 | async-start | bytes 655360 | tf_op jit(solution)/shard_map/reduce_scatter | solution.py:75
  71.9 20.1 %copy-start.3 = (bf16[128,128]{1,0:T(8,128)(2,1)S(1)}, bf16[128,128]{1,0:T(8,128)(2,1)}, u32[]{:S(2)}) copy-start(bf16[128,128]{1,0:T(8,128)(2,1)} %param.9) | copy-start | bytes 98308
  71.9 21.9 %copy-start.2 = (bf16[128,256]{1,0:T(8,128)(2,1)S(1)}, bf16[128,256]{1,0:T(8,128)(2,1)}, u32[]{:S(2)}) copy-start(bf16[128,256]{1,0:T(8,128)(2,1)} %param.10) | copy-start | bytes 196612
  71.9 111.5 %all-reduce.2.cloned.1.call-start = ((), (), s32[]{:S(2)}) async-start(), calls=%async_computation.4 | async-start | bytes 262144 | tf_op jit(solution)/shard_map/psum | solution.py:80
  93.8 0.9 copy-start.1
Sparse Core Ops, SparseCore 0:
  25.5 22.5 reduce-scatter.2
  72.0 19.8 reduce-scatter.4
  96.4 87.0 all-reduce.1
where the time goes:
time: 193 us; the launch traced here: 192 us
  waiting for transfers between devices  131 us (68%)
  blocking collectives  24.5 us (13%)
  between operations  14.6 us (8%)
  local copies, waits for them, and re-layouts  9.88 us (5%)
  matrix products  8.72 us (5%)
  other arithmetic  3.37 us (2%)
    psum x1, waiting for transfers between devices, per_device(): lax.psum(weight_term, ('row', 'col')) * float(node_total) ** (-0.5)  87.9 us
    reduce_scatter x1, waiting for transfers between devices, per_device(): lax.psum_scatter(partial_value, 'col', scatter_dimension=0, tiled=True)  22.6 us
    reduce_scatter x1, waiting for transfers between devices, per_device(): lax.psum_scatter(partial_back, 'row', scatter_dimension=0, tiled=True)  20 us
    all_gather x1, blocking collectives, per_device(): spread = lax.all_gather(grad_pre, 'col', axis=0, tiled=True)  15.9 us
    all_gather x1, blocking collectives, per_device(): gathered = lax.all_gather(projected, 'row', axis=0, tiled=True)  8.62 us
    gather x4, local copies, waits for them, and re-layouts, accumulate(): taken = jnp.take(member, block_take, axis=0)  3.9 us
  transfers between devices with their start and end apart: 3, of which 3 were waited for; matrix products, arithmetic and copies ran while one was open for 0% of the time, Pallas kernels for 0%

commit v1 on v0

v1 whole, which is shorter than its diff:
```python
import functools

import jax
import jax.numpy as jnp
from jax import lax
from jax.experimental import pallas as pl
from jax.experimental.pallas import tpu as pltpu
from jax.sharding import PartitionSpec as P

VMEM = pl.BlockSpec(memory_space=pltpu.VMEM)
SMEM = pl.BlockSpec(memory_space=pltpu.SMEM)


def call(kernel, outs, in_specs, flops=0, bytes_accessed=0):
    return pl.pallas_call(
        kernel,
        out_shape=outs,
        in_specs=in_specs,
        out_specs=jax.tree.map(lambda _: VMEM, outs),
        compiler_params=pltpu.CompilerParams(vmem_limit_bytes=48 * 1024 * 1024),
        cost_estimate=pl.CostEstimate(
            flops=flops, bytes_accessed=bytes_accessed, transcendentals=0
        ),
    )


def gather(own, axis):
    n = lax.axis_size(axis)
    return [own] + [
        lax.ppermute(own, axis, [(s, (s - d) % n) for s in range(n)]) for d in range(1, n)
    ]


def exchange(sends, axis):
    n = lax.axis_size(axis)
    return [
        lax.ppermute(sends[d - 1], axis, [(s, (s + d) % n) for s in range(n)])
        for d in range(1, n)
    ]


def split(value):
    high = value.astype(jnp.bfloat16)
    return high, (value - high.astype(jnp.float32)).astype(jnp.bfloat16)


def dot(left, right, dims=((1,), (0,))):
    return lax.dot_general(left, right, (dims, ((), ())), preferred_element_type=jnp.float32)


def dense_kernel(n_row, n_col, piece, vals, rows, cols, count, place, near, far):
    side = vals.shape[1]
    near[...] = jnp.zeros_like(near)
    far[...] = jnp.zeros_like(far)
    my_row, my_col = place[0], place[1]

    def add(t, _):
        row, col = rows[t], cols[t]
        row = lax.rem(row // piece - my_col + n_col, n_col) * piece + lax.rem(row, piece)
        col = lax.rem(col // piece - my_row + n_row, n_row) * piece + lax.rem(col, piece)
        down = pl.ds(pl.multiple_of(row * side, side), side)
        across = pl.ds(pl.multiple_of(col * side, side), side)
        tile = vals[t]
        near[down, across] = tile
        far[across, down] = tile.T
        return 0

    lax.fori_loop(0, count[0], add, 0)


def spread_kernel(n, matrix, *refs):
    operands, own, sends = refs[:n], refs[n], refs[n + 1 :]
    rows = own.shape[0]
    stacked = jnp.concatenate([operand[...] for operand in operands], axis=0)
    product = dot(matrix[...], stacked)
    own[...] = product[:rows]
    for d, send in enumerate(sends, 1):
        send[...] = product[d * rows : (d + 1) * rows].astype(send.dtype)


def layer_kernel(own, *refs):
    *parts, weight, cotangent, act, back, term = refs
    total = own[...]
    for part in parts:
        total = total + part[...].astype(jnp.float32)
    high, low = split(total)
    pre = dot(high, weight[...]) + dot(low, weight[...])
    sigma = jax.nn.sigmoid(pre)
    act[...] = (pre * sigma).astype(act.dtype)
    grad = cotangent[...].astype(jnp.float32) * sigma * (1.0 + pre * (1.0 - sigma))
    grad_high, grad_low = split(grad)
    across = ((1,), (1,))
    back[...] = (dot(grad_high, weight[...], across) + dot(grad_low, weight[...], across)).astype(
        back.dtype
    )
    down = ((0,), (0,))
    term[...] = (
        dot(high, grad_high, down) + dot(low, grad_high, down) + dot(high, grad_low, down)
    ).astype(term.dtype)


def sum_kernel(scale, *refs):
    *parts, out = refs
    total = parts[0][...].astype(jnp.float32)
    for part in parts[1:]:
        total = total + part[...].astype(jnp.float32)
    if scale is not None:
        total = total * scale
    out[...] = total.astype(out.dtype)


def per_device(features, weight, cotangent, tile_values, tile_rows, tile_cols, tile_count):
    narrow = jnp.bfloat16
    vals = tile_values.reshape(tile_values.shape[2:])
    slots, side = vals.shape[:2]
    n_row, n_col = lax.axis_size("row"), lax.axis_size("col")
    nodes, width = features.shape
    hidden = weight.shape[1]
    down, across = n_col * nodes, n_row * nodes
    place = jnp.stack([lax.axis_index("row"), lax.axis_index("col")]).astype(jnp.int32)

    def like(shape, dtype=narrow):
        return jax.ShapeDtypeStruct(shape, dtype)

    gathered = gather(features, "row")
    near, far = call(
        functools.partial(dense_kernel, n_row, n_col, nodes // side),
        (like((down, across)), like((across, down))),
        [VMEM, SMEM, SMEM, SMEM, SMEM],
        bytes_accessed=6 * down * across,
    )(vals, tile_rows.reshape(-1), tile_cols.reshape(-1), tile_count.reshape(-1), place)

    own, *sends = call(
        functools.partial(spread_kernel, n_row),
        (like((nodes, width), jnp.float32),) + (like((nodes, width)),) * (n_col - 1),
        [VMEM] * (1 + n_row),
        flops=2 * down * across * width,
    )(near, *gathered)
    parts = exchange(sends, "col")

    act, back, term = call(
        layer_kernel,
        (like((nodes, hidden)), like((nodes, width)), like((width, hidden))),
        [VMEM] * (n_col + 2),
        flops=14 * nodes * width * hidden,
    )(own, *parts, weight, cotangent)
    spread = gather(back, "col")
    terms = gather(term, "row")

    own, *sends = call(
        functools.partial(spread_kernel, n_col),
        (like((nodes, width), jnp.float32),) + (like((nodes, width)),) * (n_row - 1),
        [VMEM] * (1 + n_col),
        flops=2 * down * across * width,
    )(far, *spread)
    parts = exchange(sends, "row")

    row_sum = call(
        functools.partial(sum_kernel, None), like((width, hidden)), [VMEM] * n_row
    )(*terms)
    terms = gather(row_sum, "col")
    grad_features = call(
        functools.partial(sum_kernel, None), like((nodes, width)), [VMEM] * n_row
    )(own, *parts)
    scale = float(nodes * n_row * n_col) ** -0.5
    grad_weight = call(
        functools.partial(sum_kernel, scale), like((width, hidden), jnp.float32), [VMEM] * n_col
    )(*terms)
    return act, grad_features, grad_weight


def solution(mesh):
    placed = (
        P(("groups", "row", "col"), None),
        P(),
        P(("groups", "row", "col"), None),
        P(("groups", "row"), "col", None, None, None),
        P(("groups", "row"), "col", None),
        P(("groups", "row"), "col", None),
        P(("groups", "row"), "col"),
    )
    return jax.shard_map(
        per_device,
        mesh=mesh,
        in_specs=placed,
        out_specs=(
            P(("groups", "row", "col"), None),
            P(("groups", "row", "col"), None),
            P("groups", None),
        ),
        check_vma=False,
    )
```

time: 193 us -> 37.6 us (0.19)
  waiting for transfers between devices: 131 us -> 8.51 us
  blocking collectives: 24.5 us -> 0 us
  starting transfers between devices: 0.12 us -> 22.1 us
  between operations: 14.6 us -> 1.42 us
  matrix products: 8.72 us -> 0 us
  local copies, waits for them, and re-layouts: 9.88 us -> 1.62 us
  Pallas kernels: 0 us -> 3.68 us
  other arithmetic: 3.37 us -> 0.07 us
    psum x1 -> x0, waiting for transfers between devices: 87.9 us -> none  [per_device(): lax.psum(weight_term, ('row', 'col')) * float(node_total) ** (-0.5)]
    reduce_scatter x2 -> x0, waiting for transfers between devices: 42.6 us -> none  [the longest x1 22.6 us: per_device(): lax.psum_scatter(partial_value, 'col', scatter_dimension=0, tiled=True)]
    all_gather x2 -> x0, blocking collectives: 24.5 us -> none  [the longest x1 15.9 us: per_device(): spread = lax.all_gather(grad_pre, 'col', axis=0, tiled=True)]
    ppermute x0 -> x18, starting transfers between devices: none -> 22.1 us  [the longest x12 14.5 us: gather(): lax.ppermute(own, axis, [(s, (s - d) % n) for s in range(n)])]
    dot_general x9 -> x0, matrix products: 8.72 us -> none  [the longest x4 3.78 us: accumulate(): jnp.einsum(form, block_vals, taken, preferred_element_type=jnp.float32)]
    ppermute x0 -> x18, waiting for transfers between devices: none -> 8.51 us  [the longest x6 4.49 us: exchange(): lax.ppermute(sends[d - 1], axis, [(s, (s + d) % n) for s in range(n)])]
    gather x4 -> x0, local copies, waits for them, and re-layouts: 3.9 us -> none  [accumulate(): taken = jnp.take(member, block_take, axis=0)]
    pallas_call x0 -> x7, Pallas kernels: none -> 3.68 us  [the longest x1 0.9 us: per_device(): call(functools.partial(dense_kernel, n_row, n_col, nodes // side), (like(...]
  transfers between devices with their start and end apart: 3 -> 18, of which waited for: 3 -> 7; matrix products, arithmetic and copies ran while one was open for 0% -> 0% of each run, Pallas kernels for 0% -> 5%
where the time goes in v1:
time: 37.6 us; the launch traced here: 37.4 us
  starting transfers between devices  22.1 us (59%)
  waiting for transfers between devices  8.51 us (23%)
  Pallas kernels  3.68 us (10%)
  local copies, waits for them, and re-layouts  1.62 us (4%)
  between operations  1.42 us (4%)
    ppermute x12, starting transfers between devices, gather(): lax.ppermute(own, axis, [(s, (s - d) % n) for s in range(n)])  14.5 us
    ppermute x6, starting transfers between devices, exchange(): lax.ppermute(sends[d - 1], axis, [(s, (s + d) % n) for s in range(n)])  7.54 us
    ppermute x6, waiting for transfers between devices, exchange(): lax.ppermute(sends[d - 1], axis, [(s, (s + d) % n) for s in range(n)])  4.49 us
    ppermute x12, waiting for transfers between devices, gather(): lax.ppermute(own, axis, [(s, (s - d) % n) for s in range(n)])  4.02 us
    unnamed x12, local copies, waits for them, and re-layouts  1.62 us
    pallas_call x1, Pallas kernels, per_device(): call(functools.partial(dense_kernel, n_row, n_col, nodes // side), (like(...  0.9 us
    pallas_call x1, Pallas kernels, per_device(): call(layer_kernel, (like((nodes, hidden)), like((nodes, width)), like((wi...  0.83 us
  transfers between devices with their start and end apart: 18, of which 7 were waited for; matrix products, arithmetic and copies ran while one was open for 0% of the time, Pallas kernels for 5%

profile of v1, /device:TPU:0, one launch (start us, length us, event | category | flops | bytes accessed | tf_op | source)
XLA Modules:
  0.0 37.4 jit_solution(3809847168906821319)
XLA Ops:
  0.6 3.0 %collective-permute-start.1 = (bf16[128,128]{1,0:T(8,128)(2,1)}, bf16[128,128]{1,0:T(8,128)(2,1)S(1)}, u32[]{:S(2)}, u32[]{:S(2)}) collective-permute-start(bf16[128,128]{1,0:T(8,128)(2,1)} %refs_0_.1), channel_id=1, source_target_pairs={{0,8},{4,12},{8,0},{12,4},{1,9},{5,13},{9,1},{13,5},{2,10},{6,14},... | collective-permute-start | bytes 98312 | tf_op jit(solution)/shard_map/ppermute | solution.py:30
  3.6 0.0 collective-permute-start
  3.6 0.5 %collective-permute-start.2 = (bf16[128,128]{1,0:T(8,128)(2,1)}, bf16[128,128]{1,0:T(8,128)(2,1)S(1)}, u32[]{:S(2)}, u32[]{:S(2)}) collective-permute-start(bf16[128,128]{1,0:T(8,128)(2,1)} %refs_0_.1), channel_id=1, source_target_pairs={{0,4},{4,8},{8,12},{12,0},{1,5},{5,9},{9,13},{13,1},{2,6},{6,10},{... | collective-permute-start | bytes 98312 | tf_op jit(solution)/shard_map/ppermute | solution.py:30
  4.1 0.1 pad_add_fusion.place
  4.9 0.0 copy-start.4
  4.9 0.0 copy-start.5
  4.9 0.6 %copy-done.4 = s32[1,1,8]{2,1,0:T(1,128)S(1)} copy-done((s32[1,1,8]{2,1,0:T(1,128)S(1)}, s32[1,1,8]{2,1,0:T(1,128)}, u32[]{:S(2)}) %copy-start.4) | copy-done | bytes 56
  5.5 0.0 copy-done.5
  5.5 0.9 %copy-done = bf16[1,1,8,128,128]{4,3,2,1,0:T(8,128)(2,1)S(1)} copy-done((bf16[1,1,8,128,128]{4,3,2,1,0:T(8,128)(2,1)S(1)}, bf16[1,1,8,128,128]{4,3,2,1,0:T(8,128)(2,1)}, u32[]{:S(2)}) %copy-start) | copy-done | bytes 262168
  6.5 0.9 %shard_map.94 = (bf16[512,512]{1,0:T(8,128)(2,1)S(1)}, bf16[512,512]{1,0:T(8,128)(2,1)S(1)}) custom-call(bf16[8,128,128]{2,1,0:T(8,128)(2,1)S(1)} %bitcast.7, s32[8]{0:T(128)S(1)} %bitcast.8, s32[8]{0:T(128)S(1)} %bitcast.9, s32[1]{0:T(128)} %bitcast.6.count, s32[2]{0:T(128)S(1)} %pad_add_fusion.place), custom_call_target="tpu_custom_call" | custom-call | bytes 1572864 | tf_op jit(solution)/shard_map/pallas_call | solution.py:126
  7.4 0.0 collective-permute-done.1.refs_2_
  7.4 0.0 collective-permute-done.refs_1_
  7.4 0.0 collective-permute-done.2.refs_3_
  7.4 0.0 copy-start.1
  7.5 0.0 copy-start.2
  7.5 0.3 shard_map.95
  7.8 1.6 %collective-permute-start.3 = (bf16[128,128]{1,0:T(8,128)(2,1)S(1)}, bf16[128,128]{1,0:T(8,128)(2,1)S(1)}, u32[]{:S(2)}, u32[]{:S(2)}) collective-permute-start(bf16[128,128]{1,0:T(8,128)(2,1)S(1)} %get-tuple-element.18), channel_id=1, source_target_pairs={{0,1},{1,2},{2,3},{3,0},{4,5},{5,6},{6,7},{7,4},{8,9},{9,10},{10,1... | collective-permute-start | bytes 98312 | tf_op jit(solution)/shard_map/ppermute | solution.py:37
  9.4 2.5 %collective-permute-start.4 = (bf16[128,128]{1,0:T(8,128)(2,1)S(1)}, bf16[128,128]{1,0:T(8,128)(2,1)S(1)}, u32[]{:S(2)}, u32[]{:S(2)}) collective-permute-start(bf16[128,128]{1,0:T(8,128)(2,1)S(1)} %get-tuple-element.19), channel_id=1, source_target_pairs={{0,2},{1,3},{2,0},{3,1},{4,6},{5,7},{6,4},{7,5},{8,10},{9,11},{10,... | collective-permute-start | bytes 98312 | tf_op jit(solution)/shard_map/ppermute | solution.py:37
  11.9 1.4 %collective-permute-start.5 = (bf16[128,128]{1,0:T(8,128)(2,1)S(1)}, bf16[128,128]{1,0:T(8,128)(2,1)S(1)}, u32[]{:S(2)}, u32[]{:S(2)}) collective-permute-start(bf16[128,128]{1,0:T(8,128)(2,1)S(1)} %get-tuple-element.20), channel_id=1, source_target_pairs={{0,3},{1,0},{2,1},{3,2},{4,7},{5,4},{6,5},{7,6},{8,11},{9,8},{10,9... | collective-permute-start | bytes 98312 | tf_op jit(solution)/shard_map/ppermute | solution.py:37
  13.3 0.4 collective-permute-done.3.refs_0_
  13.7 0.7 %collective-permute-done.4.refs_1_ = bf16[128,128]{1,0:T(8,128)(2,1)S(1)} collective-permute-done((bf16[128,128]{1,0:T(8,128)(2,1)S(1)}, bf16[128,128]{1,0:T(8,128)(2,1)S(1)}, u32[]{:S(2)}, u32[]{:S(2)}) %collective-permute-start.4) | collective-permute-done | bytes 32800 | tf_op jit(solution)/shard_map/ppermute | solution.py:37
  14.4 1.4 %collective-permute-done.5.refs_2_ = bf16[128,128]{1,0:T(8,128)(2,1)S(1)} collective-permute-done((bf16[128,128]{1,0:T(8,128)(2,1)S(1)}, bf16[128,128]{1,0:T(8,128)(2,1)S(1)}, u32[]{:S(2)}, u32[]{:S(2)}) %collective-permute-start.5) | collective-permute-done | bytes 32800 | tf_op jit(solution)/shard_map/ppermute | solution.py:37
  15.8 0.8 %shard_map.96 = (bf16[128,256]{1,0:T(8,128)(2,1)}, bf16[128,128]{1,0:T(8,128)(2,1)S(1)}, bf16[128,256]{1,0:T(8,128)(2,1)S(1)}) custom-call(f32[128,128]{1,0:T(8,128)S(1)} %get-tuple-element.17.own, bf16[128,128]{1,0:T(8,128)(2,1)S(1)} %collective-permute-done.3.refs_0_, bf16[128,128]{1,0:T(8,128)(2,1)S(1)} %collective-permute-done.4.refs_1_, ...), custom_call_target="tpu_custom_call" | custom-call | flops 58720256 | tf_op jit(solution)/shard_map/pallas_call | solution.py:141
  16.7 0.5 %collective-permute-start.8 = (bf16[128,128]{1,0:T(8,128)(2,1)S(1)}, bf16[128,128]{1,0:T(8,128)(2,1)S(1)}, u32[]{:S(2)}, u32[]{:S(2)}) collective-permute-start(bf16[128,128]{1,0:T(8,128)(2,1)S(1)} %get-tuple-element.23.refs_0_), channel_id=1, source_target_pairs={{0,1},{1,2},{2,3},{3,0},{4,5},{5,6},{6,7},{7,4},{8,9},{9,10},{10,1... | collective-permute-start | bytes 98312 | tf_op jit(solution)/shard_map/ppermute | solution.py:30
  17.2 0.0 collective-permute-start.14
  17.2 0.9 %collective-permute-start.13 = (bf16[128,256]{1,0:T(8,128)(2,1)S(1)}, bf16[128,256]{1,0:T(8,128)(2,1)S(1)}, u32[]{:S(2)}, u32[]{:S(2)}) collective-permute-start(bf16[128,256]{1,0:T(8,128)(2,1)S(1)} %get-tuple-element.28.refs_0_), channel_id=1, source_target_pairs={{0,8},{4,12},{8,0},{12,4},{1,9},{5,13},{9,1},{13,5},{2,10},{6,14},... | collective-permute-start | bytes 196616 | tf_op jit(solution)/shard_map/ppermute | solution.py:30
  18.1 1.4 %collective-permute-start.12 = (bf16[128,256]{1,0:T(8,128)(2,1)S(1)}, bf16[128,256]{1,0:T(8,128)(2,1)S(1)}, u32[]{:S(2)}, u32[]{:S(2)}) collective-permute-start(bf16[128,256]{1,0:T(8,128)(2,1)S(1)} %get-tuple-element.28.refs_0_), channel_id=1, source_target_pairs={{0,12},{4,0},{8,4},{12,8},{1,13},{5,1},{9,5},{13,9},{2,14},{6,2},{... | collective-permute-start | bytes 196616 | tf_op jit(solution)/shard_map/ppermute | solution.py:30
  19.5 3.4 %collective-permute-start.7 = (bf16[128,128]{1,0:T(8,128)(2,1)S(1)}, bf16[128,128]{1,0:T(8,128)(2,1)S(1)}, u32[]{:S(2)}, u32[]{:S(2)}) collective-permute-start(bf16[128,128]{1,0:T(8,128)(2,1)S(1)} %get-tuple-element.23.refs_0_), channel_id=1, source_target_pairs={{0,2},{1,3},{2,0},{3,1},{4,6},{5,7},{6,4},{7,5},{8,10},{9,11},{10,... | collective-permute-start | bytes 98312 | tf_op jit(solution)/shard_map/ppermute | solution.py:30
  22.9 0.0 collective-permute-done.8.refs_3_
  22.9 0.9 %collective-permute-start.6 = (bf16[128,128]{1,0:T(8,128)(2,1)S(1)}, bf16[128,128]{1,0:T(8,128)(2,1)S(1)}, u32[]{:S(2)}, u32[]{:S(2)}) collective-permute-start(bf16[128,128]{1,0:T(8,128)(2,1)S(1)} %get-tuple-element.23.refs_0_), channel_id=1, source_target_pairs={{0,3},{1,0},{2,1},{3,2},{4,7},{5,4},{6,5},{7,6},{8,11},{9,8},{10,9... | collective-permute-start | bytes 98312 | tf_op jit(solution)/shard_map/ppermute | solution.py:30
  23.8 1.5 %collective-permute-done.7.refs_2_ = bf16[128,128]{1,0:T(8,128)(2,1)S(1)} collective-permute-done((bf16[128,128]{1,0:T(8,128)(2,1)S(1)}, bf16[128,128]{1,0:T(8,128)(2,1)S(1)}, u32[]{:S(2)}, u32[]{:S(2)}) %collective-permute-start.7) | collective-permute-done | bytes 32800 | tf_op jit(solution)/shard_map/ppermute | solution.py:30
  25.3 1.5 %collective-permute-done.6.refs_1_ = bf16[128,128]{1,0:T(8,128)(2,1)S(1)} collective-permute-done((bf16[128,128]{1,0:T(8,128)(2,1)S(1)}, bf16[128,128]{1,0:T(8,128)(2,1)S(1)}, u32[]{:S(2)}, u32[]{:S(2)}) %collective-permute-start.6) | collective-permute-done | bytes 32800 | tf_op jit(solution)/shard_map/ppermute | solution.py:30
  26.8 0.3 shard_map.97
  27.1 0.1 collective-permute-start.9
  27.2 0.0 collective-permute-done.14.refs_3_
  27.2 0.0 collective-permute-done.13.refs_2_
  27.2 0.0 collective-permute-done.12.refs_1_
  27.3 0.7 %collective-permute-start.17 = (bf16[128,256]{1,0:T(8,128)(2,1)S(1)}, bf16[128,256]{1,0:T(8,128)(2,1)S(1)}, u32[]{:S(2)}, u32[]{:S(2)}) collective-permute-start(bf16[128,256]{1,0:T(8,128)(2,1)S(1)} %shard_map.99.refs_0_), channel_id=1, source_target_pairs={{0,1},{1,2},{2,3},{3,0},{4,5},{5,6},{6,7},{7,4},{8,9},{9,10},{10,1... | collective-permute-start | bytes 196616 | tf_op jit(solution)/shard_map/ppermute | solution.py:30
  28.0 2.6 %collective-permute-start.16 = (bf16[128,256]{1,0:T(8,128)(2,1)S(1)}, bf16[128,256]{1,0:T(8,128)(2,1)S(1)}, u32[]{:S(2)}, u32[]{:S(2)}) collective-permute-start(bf16[128,256]{1,0:T(8,128)(2,1)S(1)} %shard_map.99.refs_0_), channel_id=1, source_target_pairs={{0,2},{1,3},{2,0},{3,1},{4,6},{5,7},{6,4},{7,5},{8,10},{9,11},{10,... | collective-permute-start | bytes 196616 | tf_op jit(solution)/shard_map/ppermute | solution.py:30
  30.6 0.6 %collective-permute-start.15 = (bf16[128,256]{1,0:T(8,128)(2,1)S(1)}, bf16[128,256]{1,0:T(8,128)(2,1)S(1)}, u32[]{:S(2)}, u32[]{:S(2)}) collective-permute-start(bf16[128,256]{1,0:T(8,128)(2,1)S(1)} %shard_map.99.refs_0_), channel_id=1, source_target_pairs={{0,3},{1,0},{2,1},{3,2},{4,7},{5,4},{6,5},{7,6},{8,11},{9,8},{10,9... | collective-permute-start | bytes 196616 | tf_op jit(solution)/shard_map/ppermute | solution.py:30
  31.2 1.0 %collective-permute-start.10 = (bf16[128,128]{1,0:T(8,128)(2,1)S(1)}, bf16[128,128]{1,0:T(8,128)(2,1)S(1)}, u32[]{:S(2)}, u32[]{:S(2)}) collective-permute-start(bf16[128,128]{1,0:T(8,128)(2,1)S(1)} %get-tuple-element.26), channel_id=1, source_target_pairs={{0,8},{4,12},{8,0},{12,4},{1,9},{5,13},{9,1},{13,5},{2,10},{6,14},... | collective-permute-start | bytes 98312 | tf_op jit(solution)/shard_map/ppermute | solution.py:37
  32.2 0.9 %collective-permute-start.11 = (bf16[128,128]{1,0:T(8,128)(2,1)S(1)}, bf16[128,128]{1,0:T(8,128)(2,1)S(1)}, u32[]{:S(2)}, u32[]{:S(2)}) collective-permute-start(bf16[128,128]{1,0:T(8,128)(2,1)S(1)} %get-tuple-element.27), channel_id=1, source_target_pairs={{0,12},{4,0},{8,4},{12,8},{1,13},{5,1},{9,5},{13,9},{2,14},{6,2},{... | collective-permute-start | bytes 98312 | tf_op jit(solution)/shard_map/ppermute | solution.py:37
  33.1 2.0 %collective-permute-done.10.refs_2_ = bf16[128,128]{1,0:T(8,128)(2,1)S(1)} collective-permute-done((bf16[128,128]{1,0:T(8,128)(2,1)S(1)}, bf16[128,128]{1,0:T(8,128)(2,1)S(1)}, u32[]{:S(2)}, u32[]{:S(2)}) %collective-permute-start.10) | collective-permute-done | bytes 32800 | tf_op jit(solution)/shard_map/ppermute | solution.py:37
  35.1 0.6 %shard_map.98 = bf16[128,128]{1,0:T(8,128)(2,1)} custom-call(f32[128,128]{1,0:T(8,128)S(1)} %get-tuple-element.24.refs_0_, bf16[128,128]{1,0:T(8,128)(2,1)S(1)} %collective-permute-done.9.refs_1_, bf16[128,128]{1,0:T(8,128)(2,1)S(1)} %collective-permute-done.10.refs_2_, bf16[128,128]{1,0:T(8,128)(2,1)S(1)} %collective-permute-done.11.refs_3_), custom_call_target="tpu_custom_call" | custom-call | tf_op jit(solution)/shard_map/pallas_call | solution.py:162
  35.7 0.0 collective-permute-done.17.refs_3_
  35.7 1.0 %collective-permute-done.16.refs_2_ = bf16[128,256]{1,0:T(8,128)(2,1)S(1)} collective-permute-done((bf16[128,256]{1,0:T(8,128)(2,1)S(1)}, bf16[128,256]{1,0:T(8,128)(2,1)S(1)}, u32[]{:S(2)}, u32[]{:S(2)}) %collective-permute-start.16) | collective-permute-done | bytes 65568 | tf_op jit(solution)/shard_map/ppermute | solution.py:30
  36.7 0.0 collective-permute-done.15.refs_1_
  36.7 0.7 %shard_map.100 = f32[128,256]{1,0:T(8,128)} custom-call(bf16[128,256]{1,0:T(8,128)(2,1)S(1)} %shard_map.99.refs_0_, bf16[128,256]{1,0:T(8,128)(2,1)S(1)} %collective-permute-done.15.refs_1_, bf16[128,256]{1,0:T(8,128)(2,1)S(1)} %collective-permute-done.16.refs_2_, bf16[128,256]{1,0:T(8,128)(2,1)S(1)} %collective-permute-done.17.refs_3_), custom_call_target="tpu_custom_call" | custom-call | tf_op jit(solution)/shard_map/pallas_call | solution.py:166
  (8 shorter events, 0.1 us)
Async XLA Ops:
  0.6 6.8 %collective-permute-start.1 = (bf16[128,128]{1,0:T(8,128)(2,1)}, bf16[128,128]{1,0:T(8,128)(2,1)S(1)}, u32[]{:S(2)}, u32[]{:S(2)}) collective-permute-start(bf16[128,128]{1,0:T(8,128)(2,1)} %refs_0_.1), channel_id=1, source_target_pairs={{0,8},{4,12},{8,0},{12,4},{1,9},{5,13},{9,1},{13,5},{2,10},{6,14},... | collective-permute-start | bytes 98312 | tf_op jit(solution)/shard_map/ppermute | solution.py:30
  3.6 3.8 %collective-permute-start = (bf16[128,128]{1,0:T(8,128)(2,1)}, bf16[128,128]{1,0:T(8,128)(2,1)S(1)}, u32[]{:S(2)}, u32[]{:S(2)}) collective-permute-start(bf16[128,128]{1,0:T(8,128)(2,1)} %refs_0_.1), channel_id=1, source_target_pairs={{0,12},{4,0},{8,4},{12,8},{1,13},{5,1},{9,5},{13,9},{2,14},{6,2},{... | collective-permute-start | bytes 98312 | tf_op jit(solution)/shard_map/ppermute | solution.py:30
  3.6 3.8 %collective-permute-start.2 = (bf16[128,128]{1,0:T(8,128)(2,1)}, bf16[128,128]{1,0:T(8,128)(2,1)S(1)}, u32[]{:S(2)}, u32[]{:S(2)}) collective-permute-start(bf16[128,128]{1,0:T(8,128)(2,1)} %refs_0_.1), channel_id=1, source_target_pairs={{0,4},{4,8},{8,12},{12,0},{1,5},{5,9},{9,13},{13,1},{2,6},{6,10},{... | collective-permute-start | bytes 98312 | tf_op jit(solution)/shard_map/ppermute | solution.py:30
  4.9 0.7 %copy-start.4 = (s32[1,1,8]{2,1,0:T(1,128)S(1)}, s32[1,1,8]{2,1,0:T(1,128)}, u32[]{:S(2)}) copy-start(s32[1,1,8]{2,1,0:T(1,128)} %param.11) | copy-start | bytes 100
  4.9 0.7 %copy-start.5 = (s32[1,1,8]{2,1,0:T(1,128)S(1)}, s32[1,1,8]{2,1,0:T(1,128)}, u32[]{:S(2)}) copy-start(s32[1,1,8]{2,1,0:T(1,128)} %param.12) | copy-start | bytes 100
  5.5 0.9 %copy-start = (bf16[1,1,8,128,128]{4,3,2,1,0:T(8,128)(2,1)S(1)}, bf16[1,1,8,128,128]{4,3,2,1,0:T(8,128)(2,1)}, u32[]{:S(2)}) copy-start(bf16[1,1,8,128,128]{4,3,2,1,0:T(8,128)(2,1)} %param.10) | copy-start | bytes 786436
  6.5 0.9 %copy-start.3 = (bf16[128,128]{1,0:T(8,128)(2,1)S(1)}, bf16[128,128]{1,0:T(8,128)(2,1)}, u32[]{:S(2)}) copy-start(bf16[128,128]{1,0:T(8,128)(2,1)} %refs_0_.1) | copy-start | bytes 98308
  7.4 8.4 %copy-start.1 = (bf16[128,256]{1,0:T(8,128)(2,1)S(1)}, bf16[128,256]{1,0:T(8,128)(2,1)}, u32[]{:S(2)}) copy-start(bf16[128,256]{1,0:T(8,128)(2,1)} %refs_3_.1) | copy-start | bytes 196612
  7.5 8.4 %copy-start.2 = (bf16[128,256]{1,0:T(8,128)(2,1)S(1)}, bf16[128,256]{1,0:T(8,128)(2,1)}, u32[]{:S(2)}) copy-start(bf16[128,256]{1,0:T(8,128)(2,1)} %refs_4_.1) | copy-start | bytes 196612
  7.8 5.9 %collective-permute-start.3 = (bf16[128,128]{1,0:T(8,128)(2,1)S(1)}, bf16[128,128]{1,0:T(8,128)(2,1)S(1)}, u32[]{:S(2)}, u32[]{:S(2)}) collective-permute-start(bf16[128,128]{1,0:T(8,128)(2,1)S(1)} %get-tuple-element.18), channel_id=1, source_target_pairs={{0,1},{1,2},{2,3},{3,0},{4,5},{5,6},{6,7},{7,4},{8,9},{9,10},{10,1... | collective-permute-start | bytes 98312 | tf_op jit(solution)/shard_map/ppermute | solution.py:37
  9.4 5.0 %collective-permute-start.4 = (bf16[128,128]{1,0:T(8,128)(2,1)S(1)}, bf16[128,128]{1,0:T(8,128)(2,1)S(1)}, u32[]{:S(2)}, u32[]{:S(2)}) collective-permute-start(bf16[128,128]{1,0:T(8,128)(2,1)S(1)} %get-tuple-element.19), channel_id=1, source_target_pairs={{0,2},{1,3},{2,0},{3,1},{4,6},{5,7},{6,4},{7,5},{8,10},{9,11},{10,... | collective-permute-start | bytes 98312 | tf_op jit(solution)/shard_map/ppermute | solution.py:37
  11.9 3.9 %collective-permute-start.5 = (bf16[128,128]{1,0:T(8,128)(2,1)S(1)}, bf16[128,128]{1,0:T(8,128)(2,1)S(1)}, u32[]{:S(2)}, u32[]{:S(2)}) collective-permute-start(bf16[128,128]{1,0:T(8,128)(2,1)S(1)} %get-tuple-element.20), channel_id=1, source_target_pairs={{0,3},{1,0},{2,1},{3,2},{4,7},{5,4},{6,5},{7,6},{8,11},{9,8},{10,9... | collective-permute-start | bytes 98312 | tf_op jit(solution)/shard_map/ppermute | solution.py:37
  16.7 6.2 %collective-permute-start.8 = (bf16[128,128]{1,0:T(8,128)(2,1)S(1)}, bf16[128,128]{1,0:T(8,128)(2,1)S(1)}, u32[]{:S(2)}, u32[]{:S(2)}) collective-permute-start(bf16[128,128]{1,0:T(8,128)(2,1)S(1)} %get-tuple-element.23.refs_0_), channel_id=1, source_target_pairs={{0,1},{1,2},{2,3},{3,0},{4,5},{5,6},{6,7},{7,4},{8,9},{9,10},{10,1... | collective-permute-start | bytes 98312 | tf_op jit(solution)/shard_map/ppermute | solution.py:30
  17.2 10.0 %collective-permute-start.14 = (bf16[128,256]{1,0:T(8,128)(2,1)S(1)}, bf16[128,256]{1,0:T(8,128)(2,1)S(1)}, u32[]{:S(2)}, u32[]{:S(2)}) collective-permute-start(bf16[128,256]{1,0:T(8,128)(2,1)S(1)} %get-tuple-element.28.refs_0_), channel_id=1, source_target_pairs={{0,4},{4,8},{8,12},{12,0},{1,5},{5,9},{9,13},{13,1},{2,6},{6,10},{... | collective-permute-start | bytes 196616 | tf_op jit(solution)/shard_map/ppermute | solution.py:30
  17.2 10.0 %collective-permute-start.13 = (bf16[128,256]{1,0:T(8,128)(2,1)S(1)}, bf16[128,256]{1,0:T(8,128)(2,1)S(1)}, u32[]{:S(2)}, u32[]{:S(2)}) collective-permute-start(bf16[128,256]{1,0:T(8,128)(2,1)S(1)} %get-tuple-element.28.refs_0_), channel_id=1, source_target_pairs={{0,8},{4,12},{8,0},{12,4},{1,9},{5,13},{9,1},{13,5},{2,10},{6,14},... | collective-permute-start | bytes 196616 | tf_op jit(solution)/shard_map/ppermute | solution.py:30
  18.1 9.1 %collective-permute-start.12 = (bf16[128,256]{1,0:T(8,128)(2,1)S(1)}, bf16[128,256]{1,0:T(8,128)(2,1)S(1)}, u32[]{:S(2)}, u32[]{:S(2)}) collective-permute-start(bf16[128,256]{1,0:T(8,128)(2,1)S(1)} %get-tuple-element.28.refs_0_), channel_id=1, source_target_pairs={{0,12},{4,0},{8,4},{12,8},{1,13},{5,1},{9,5},{13,9},{2,14},{6,2},{... | collective-permute-start | bytes 196616 | tf_op jit(solution)/shard_map/ppermute | solution.py:30
  19.5 5.8 %collective-permute-start.7 = (bf16[128,128]{1,0:T(8,128)(2,1)S(1)}, bf16[128,128]{1,0:T(8,128)(2,1)S(1)}, u32[]{:S(2)}, u32[]{:S(2)}) collective-permute-start(bf16[128,128]{1,0:T(8,128)(2,1)S(1)} %get-tuple-element.23.refs_0_), channel_id=1, source_target_pairs={{0,2},{1,3},{2,0},{3,1},{4,6},{5,7},{6,4},{7,5},{8,10},{9,11},{10,... | collective-permute-start | bytes 98312 | tf_op jit(solution)/shard_map/ppermute | solution.py:30
  22.9 3.9 %collective-permute-start.6 = (bf16[128,128]{1,0:T(8,128)(2,1)S(1)}, bf16[128,128]{1,0:T(8,128)(2,1)S(1)}, u32[]{:S(2)}, u32[]{:S(2)}) collective-permute-start(bf16[128,128]{1,0:T(8,128)(2,1)S(1)} %get-tuple-element.23.refs_0_), channel_id=1, source_target_pairs={{0,3},{1,0},{2,1},{3,2},{4,7},{5,4},{6,5},{7,6},{8,11},{9,8},{10,9... | collective-permute-start | bytes 98312 | tf_op jit(solution)/shard_map/ppermute | solution.py:30
  27.1 5.1 %collective-permute-start.9 = (bf16[128,128]{1,0:T(8,128)(2,1)S(1)}, bf16[128,128]{1,0:T(8,128)(2,1)S(1)}, u32[]{:S(2)}, u32[]{:S(2)}) collective-permute-start(bf16[128,128]{1,0:T(8,128)(2,1)S(1)} %get-tuple-element.25), channel_id=1, source_target_pairs={{0,4},{4,8},{8,12},{12,0},{1,5},{5,9},{9,13},{13,1},{2,6},{6,10},{... | collective-permute-start | bytes 98312 | tf_op jit(solution)/shard_map/ppermute | solution.py:37
  27.3 8.4 %collective-permute-start.17 = (bf16[128,256]{1,0:T(8,128)(2,1)S(1)}, bf16[128,256]{1,0:T(8,128)(2,1)S(1)}, u32[]{:S(2)}, u32[]{:S(2)}) collective-permute-start(bf16[128,256]{1,0:T(8,128)(2,1)S(1)} %shard_map.99.refs_0_), channel_id=1, source_target_pairs={{0,1},{1,2},{2,3},{3,0},{4,5},{5,6},{6,7},{7,4},{8,9},{9,10},{10,1... | collective-permute-start | bytes 196616 | tf_op jit(solution)/shard_map/ppermute | solution.py:30
  28.0 8.7 %collective-permute-start.16 = (bf16[128,256]{1,0:T(8,128)(2,1)S(1)}, bf16[128,256]{1,0:T(8,128)(2,1)S(1)}, u32[]{:S(2)}, u32[]{:S(2)}) collective-permute-start(bf16[128,256]{1,0:T(8,128)(2,1)S(1)} %shard_map.99.refs_0_), channel_id=1, source_target_pairs={{0,2},{1,3},{2,0},{3,1},{4,6},{5,7},{6,4},{7,5},{8,10},{9,11},{10,... | collective-permute-start | bytes 196616 | tf_op jit(solution)/shard_map/ppermute | solution.py:30
  30.6 6.1 %collective-permute-start.15 = (bf16[128,256]{1,0:T(8,128)(2,1)S(1)}, bf16[128,256]{1,0:T(8,128)(2,1)S(1)}, u32[]{:S(2)}, u32[]{:S(2)}) collective-permute-start(bf16[128,256]{1,0:T(8,128)(2,1)S(1)} %shard_map.99.refs_0_), channel_id=1, source_target_pairs={{0,3},{1,0},{2,1},{3,2},{4,7},{5,4},{6,5},{7,6},{8,11},{9,8},{10,9... | collective-permute-start | bytes 196616 | tf_op jit(solution)/shard_map/ppermute | solution.py:30
  31.2 3.9 %collective-permute-start.10 = (bf16[128,128]{1,0:T(8,128)(2,1)S(1)}, bf16[128,128]{1,0:T(8,128)(2,1)S(1)}, u32[]{:S(2)}, u32[]{:S(2)}) collective-permute-start(bf16[128,128]{1,0:T(8,128)(2,1)S(1)} %get-tuple-element.26), channel_id=1, source_target_pairs={{0,8},{4,12},{8,0},{12,4},{1,9},{5,13},{9,1},{13,5},{2,10},{6,14},... | collective-permute-start | bytes 98312 | tf_op jit(solution)/shard_map/ppermute | solution.py:37
  32.2 2.9 %collective-permute-start.11 = (bf16[128,128]{1,0:T(8,128)(2,1)S(1)}, bf16[128,128]{1,0:T(8,128)(2,1)S(1)}, u32[]{:S(2)}, u32[]{:S(2)}) collective-permute-start(bf16[128,128]{1,0:T(8,128)(2,1)S(1)} %get-tuple-element.27), channel_id=1, source_target_pairs={{0,12},{4,0},{8,4},{12,8},{1,13},{5,1},{9,5},{13,9},{2,14},{6,2},{... | collective-permute-start | bytes 98312 | tf_op jit(solution)/shard_map/ppermute | solution.py:37

commit v2 on v1

v2 whole, which is shorter than its diff:
```python
import functools

import jax
import jax.numpy as jnp
from jax import lax
from jax.experimental import pallas as pl
from jax.experimental.pallas import tpu as pltpu
from jax.sharding import PartitionSpec as P

VMEM = pl.BlockSpec(memory_space=pltpu.VMEM)
SMEM = pl.BlockSpec(memory_space=pltpu.SMEM)


def call(kernel, outs, in_specs, flops=0, bytes_accessed=0):
    return pl.pallas_call(
        kernel,
        out_shape=outs,
        in_specs=in_specs,
        out_specs=jax.tree.map(lambda _: VMEM, outs),
        compiler_params=pltpu.CompilerParams(vmem_limit_bytes=48 * 1024 * 1024),
        cost_estimate=pl.CostEstimate(
            flops=flops, bytes_accessed=bytes_accessed, transcendentals=0
        ),
    )


def gather(own, axis):
    n = lax.axis_size(axis)
    return [own] + [
        lax.ppermute(own, axis, [(s, (s - d) % n) for s in range(n)]) for d in range(1, n)
    ]


def split(value):
    high = value.astype(jnp.bfloat16)
    return high, (value - high.astype(jnp.float32)).astype(jnp.bfloat16)


def dot(left, right, dims=((1,), (0,))):
    return lax.dot_general(left, right, (dims, ((), ())), preferred_element_type=jnp.float32)


def dense_kernel(vals, rows, cols, count, near, far):
    side = vals.shape[1]
    near[...] = jnp.zeros_like(near)
    far[...] = jnp.zeros_like(far)

    def add(t, _):
        down = pl.ds(pl.multiple_of(rows[t] * side, side), side)
        across = pl.ds(pl.multiple_of(cols[t] * side, side), side)
        tile = vals[t]
        near[down, across] = tile
        far[across, down] = tile.T
        return 0

    lax.fori_loop(0, count[0], add, 0)


def spread_kernel(matrix, operand, out):
    out[...] = dot(matrix[...], operand[...]).astype(out.dtype)


def add_pieces(pieces, rows):
    total = pieces[:rows].astype(jnp.float32)
    for start in range(rows, pieces.shape[0], rows):
        total = total + pieces[start : start + rows].astype(jnp.float32)
    return total


def layer_kernel(pieces, weight, cotangent, act, back, term):
    total = add_pieces(pieces, act.shape[0])
    high, low = split(total)
    pre = dot(high, weight[...]) + dot(low, weight[...])
    sigma = jax.nn.sigmoid(pre)
    act[...] = (pre * sigma).astype(act.dtype)
    grad = cotangent[...].astype(jnp.float32) * sigma * (1.0 + pre * (1.0 - sigma))
    grad_high, grad_low = split(grad)
    across = ((1,), (1,))
    back[...] = (dot(grad_high, weight[...], across) + dot(grad_low, weight[...], across)).astype(
        back.dtype
    )
    down = ((0,), (0,))
    term[...] = (
        dot(high, grad_high, down) + dot(low, grad_high, down) + dot(high, grad_low, down)
    ).astype(term.dtype)


def fold_kernel(pieces, out):
    out[...] = add_pieces(pieces, out.shape[0]).astype(out.dtype)


def sum_kernel(scale, *refs):
    *parts, out = refs
    total = parts[0][...].astype(jnp.float32)
    for part in parts[1:]:
        total = total + part[...].astype(jnp.float32)
    if scale is not None:
        total = total * scale
    out[...] = total.astype(out.dtype)


def per_device(features, weight, cotangent, tile_values, tile_rows, tile_cols, tile_count):
    narrow = jnp.bfloat16
    vals = tile_values.reshape(tile_values.shape[2:])
    slots, side = vals.shape[:2]
    n_row, n_col = lax.axis_size("row"), lax.axis_size("col")
    nodes, width = features.shape
    hidden = weight.shape[1]
    down, across = n_col * nodes, n_row * nodes
    def like(shape, dtype=narrow):
        return jax.ShapeDtypeStruct(shape, dtype)

    gathered = lax.all_gather(features, "row", axis=0, tiled=True)
    near, far = call(
        dense_kernel,
        (like((down, across)), like((across, down))),
        [VMEM, SMEM, SMEM, SMEM],
        bytes_accessed=6 * down * across,
    )(vals, tile_rows.reshape(-1), tile_cols.reshape(-1), tile_count.reshape(-1))

    sends = call(
        spread_kernel,
        like((down, width)),
        [VMEM] * 2,
        flops=2 * down * across * width,
    )(near, gathered)
    parts = lax.all_to_all(sends, "col", 0, 0, tiled=True)

    act, back, term = call(
        layer_kernel,
        (like((nodes, hidden)), like((nodes, width)), like((width, hidden))),
        [VMEM] * 3,
        flops=14 * nodes * width * hidden,
    )(parts, weight, cotangent)
    spread = lax.all_gather(back, "col", axis=0, tiled=True)
    terms = gather(term, "row")

    sends = call(
        spread_kernel,
        like((across, width)),
        [VMEM] * 2,
        flops=2 * down * across * width,
    )(far, spread)
    parts = lax.all_to_all(sends, "row", 0, 0, tiled=True)

    row_sum = call(
        functools.partial(sum_kernel, None), like((width, hidden)), [VMEM] * n_row
    )(*terms)
    terms = gather(row_sum, "col")
    grad_features = call(fold_kernel, like((nodes, width)), [VMEM])(parts)
    scale = float(nodes * n_row * n_col) ** -0.5
    grad_weight = call(
        functools.partial(sum_kernel, scale), like((width, hidden), jnp.float32), [VMEM] * n_col
    )(*terms)
    return act, grad_features, grad_weight


def solution(mesh):
    placed = (
        P(("groups", "row", "col"), None),
        P(),
        P(("groups", "row", "col"), None),
        P(("groups", "row"), "col", None, None, None),
        P(("groups", "row"), "col", None),
        P(("groups", "row"), "col", None),
        P(("groups", "row"), "col"),
    )
    return jax.shard_map(
        per_device,
        mesh=mesh,
        in_specs=placed,
        out_specs=(
            P(("groups", "row", "col"), None),
            P(("groups", "row", "col"), None),
            P("groups", None),
        ),
        check_vma=False,
    )
```

time: 37.6 us -> 53.9 us (1.43)
  blocking collectives: 0 us -> 31.9 us
  starting transfers between devices: 22.1 us -> 10.3 us
  waiting for transfers between devices: 8.51 us -> 4.26 us
  Pallas kernels: 3.68 us -> 4.26 us
    all_gather x0 -> x2, blocking collectives: none -> 20.2 us  [the longest x1 13.5 us: per_device(): spread = lax.all_gather(back, 'col', axis=0, tiled=True)]
    all_to_all x0 -> x1, blocking collectives: none -> 11.7 us  [per_device(): parts = lax.all_to_all(sends, 'col', 0, 0, tiled=True)]
    ppermute x12 -> x6, starting transfers between devices: 14.5 us -> 6.93 us  [gather(): lax.ppermute(own, axis, [(s, (s - d) % n) for s in range(n)])]
    ppermute x6 -> x0, starting transfers between devices: 7.54 us -> none  [exchange(): lax.ppermute(sends[d - 1], axis, [(s, (s + d) % n) for s in range(n)])]
    ppermute x6 -> x0, waiting for transfers between devices: 4.49 us -> none  [exchange(): lax.ppermute(sends[d - 1], axis, [(s, (s + d) % n) for s in range(n)])]
    all_to_all x0 -> x1, starting transfers between devices: none -> 3.33 us  [per_device(): parts = lax.all_to_all(sends, 'row', 0, 0, tiled=True)]
    all_to_all x0 -> x1, waiting for transfers between devices: none -> 0.64 us  [per_device(): parts = lax.all_to_all(sends, 'row', 0, 0, tiled=True)]
    pallas_call x4, Pallas kernels: 2.11 us -> 2.7 us  [the longest x1 0.95 us: per_device(): call(spread_kernel, like((across, width)), [VMEM] * 2, flops=2 * down * a...]
  transfers between devices with their start and end apart: 18 -> 7, of which waited for: 7 -> 3; matrix products, arithmetic and copies ran while one was open for 0% -> 0% of each run, Pallas kernels for 5% -> 3%
where the time goes in v2:
time: 53.9 us; the launch traced here: 53.6 us
  blocking collectives  31.9 us (59%)
  starting transfers between devices  10.3 us (19%)
  Pallas kernels  4.26 us (8%)
  waiting for transfers between devices  4.26 us (8%)
  local copies, waits for them, and re-layouts  1.63 us (3%)
  between operations  1.36 us (3%)
    all_gather x1, blocking collectives, per_device(): spread = lax.all_gather(back, 'col', axis=0, tiled=True)  13.5 us
    all_to_all x1, blocking collectives, per_device(): parts = lax.all_to_all(sends, 'col', 0, 0, tiled=True)  11.7 us
    ppermute x6, starting transfers between devices, gather(): lax.ppermute(own, axis, [(s, (s - d) % n) for s in range(n)])  6.93 us
    all_gather x1, blocking collectives, per_device(): gathered = lax.all_gather(features, 'row', axis=0, tiled=True)  6.69 us
    ppermute x6, waiting for transfers between devices, gather(): lax.ppermute(own, axis, [(s, (s - d) % n) for s in range(n)])  3.62 us
    all_to_all x1, starting transfers between devices, per_device(): parts = lax.all_to_all(sends, 'row', 0, 0, tiled=True)  3.33 us
    unnamed x10, local copies, waits for them, and re-layouts  1.63 us
  transfers between devices with their start and end apart: 7, of which 3 were waited for; matrix products, arithmetic and copies ran while one was open for 0% of the time, Pallas kernels for 3%

profile of v2, /device:TPU:0, one launch (start us, length us, event | category | flops | bytes accessed | tf_op | source)
XLA Modules:
  0.0 53.6 jit_solution(12345249473904312996)
XLA Ops:
  1.3 6.7 %all_gather.6.operand = bf16[512,128]{1,0:T(8,128)(2,1)S(1)} all-gather(bf16[128,128]{1,0:T(8,128)(2,1)} %param.7), channel_id=1, replica_groups=mesh['groups'=2,'row'=4,'col'=4] {'row'}, dimensions={0}, use_global_device_ids=true | all-gather | bytes 163840 | tf_op jit(solution)/shard_map/all_gather | solution.py:113
  8.0 0.0 copy-start.3
  8.0 0.0 copy-start.4
  8.0 0.7 %copy-done.3 = s32[1,1,8]{2,1,0:T(1,128)S(1)} copy-done((s32[1,1,8]{2,1,0:T(1,128)S(1)}, s32[1,1,8]{2,1,0:T(1,128)}, u32[]{:S(2)}) %copy-start.3) | copy-done | bytes 56
  8.6 0.0 copy-done.4
  8.6 0.0 copy-start
  8.6 0.9 %copy-done = bf16[1,1,8,128,128]{4,3,2,1,0:T(8,128)(2,1)S(1)} copy-done((bf16[1,1,8,128,128]{4,3,2,1,0:T(8,128)(2,1)S(1)}, bf16[1,1,8,128,128]{4,3,2,1,0:T(8,128)(2,1)}, u32[]{:S(2)}) %copy-start) | copy-done | bytes 262168
  9.6 0.8 %shard_map.94 = (bf16[512,512]{1,0:T(8,128)(2,1)S(1)}, bf16[512,512]{1,0:T(8,128)(2,1)S(1)}) custom-call(bf16[8,128,128]{2,1,0:T(8,128)(2,1)S(1)} %bitcast.12, s32[8]{0:T(128)S(1)} %bitcast.13, s32[8]{0:T(128)S(1)} %bitcast.14, s32[1]{0:T(128)} %bitcast.8.count), custom_call_target="tpu_custom_call" | custom-call | bytes 1572864 | tf_op jit(solution)/shard_map/pallas_call | solution.py:114
  10.4 0.3 shard_map.95
  10.7 0.0 copy-start.1
  10.7 0.0 copy-start.2
  10.7 11.7 %all_to_all.22 = bf16[4,128,128]{2,1,0:T(8,128)(2,1)S(1)} all-to-all(bf16[4,128,128]{2,1,0:T(8,128)(2,1)S(1)} %bitcast.11), channel_id=1, replica_groups=mesh['groups'=2,'row'=4,'col'=4] {'col'}, dimensions={0} | all-to-all | bytes 262144 | tf_op jit(solution)/shard_map/all_to_all | solution.py:127
  22.4 0.0 copy-done.1
  22.4 0.0 copy-done.2
  22.4 0.8 %shard_map.96 = (bf16[128,256]{1,0:T(8,128)(2,1)}, bf16[128,128]{1,0:T(8,128)(2,1)S(1)}, bf16[128,256]{1,0:T(8,128)(2,1)S(1)}) custom-call(bf16[512,128]{1,0:T(8,128)(2,1)S(1)} %bitcast.10, bf16[128,256]{1,0:T(8,128)(2,1)S(1)} %copy-done.1, bf16[128,256]{1,0:T(8,128)(2,1)S(1)} %copy-done.2), custom_call_target="tpu_custom_call" | custom-call | flops 58720256 | tf_op jit(solution)/shard_map/pallas_call | solution.py:129
  23.3 0.0 collective-permute-start.2
  23.3 1.6 %collective-permute-start.1 = (bf16[128,256]{1,0:T(8,128)(2,1)S(1)}, bf16[128,256]{1,0:T(8,128)(2,1)S(1)}, u32[]{:S(2)}, u32[]{:S(2)}) collective-permute-start(bf16[128,256]{1,0:T(8,128)(2,1)S(1)} %get-tuple-element.12.refs_0_), channel_id=1, source_target_pairs={{0,8},{4,12},{8,0},{12,4},{1,9},{5,13},{9,1},{13,5},{2,10},{6,14},... | collective-permute-start | bytes 196616 | tf_op jit(solution)/shard_map/ppermute | solution.py:30
  24.9 1.4 %collective-permute-start = (bf16[128,256]{1,0:T(8,128)(2,1)S(1)}, bf16[128,256]{1,0:T(8,128)(2,1)S(1)}, u32[]{:S(2)}, u32[]{:S(2)}) collective-permute-start(bf16[128,256]{1,0:T(8,128)(2,1)S(1)} %get-tuple-element.12.refs_0_), channel_id=1, source_target_pairs={{0,12},{4,0},{8,4},{12,8},{1,13},{5,1},{9,5},{13,9},{2,14},{6,2},{... | collective-permute-start | bytes 196616 | tf_op jit(solution)/shard_map/ppermute | solution.py:30
  26.3 13.5 %all_gather.7.operand = bf16[512,128]{1,0:T(8,128)(2,1)S(1)} all-gather(bf16[128,128]{1,0:T(8,128)(2,1)S(1)} %get-tuple-element.11), channel_id=1, replica_groups=mesh['groups'=2,'row'=4,'col'=4] {'col'}, dimensions={0}, use_global_device_ids=true | all-gather | bytes 163840 | tf_op jit(solution)/shard_map/all_gather | solution.py:135
  39.8 1.0 %shard_map.97 = bf16[512,128]{1,0:T(8,128)(2,1)} custom-call(bf16[512,512]{1,0:T(8,128)(2,1)S(1)} %get-tuple-element.10.matrix, bf16[512,128]{1,0:T(8,128)(2,1)S(1)} %all_gather.7.operand), custom_call_target="tpu_custom_call" | custom-call | flops 67108864 | tf_op jit(solution)/shard_map/pallas_call | solution.py:138
  40.8 3.3 %all-to-all-start.1 = ((bf16[4,128,128]{2,1,0:T(8,128)(2,1)}), bf16[4,128,128]{2,1,0:T(8,128)(2,1)S(1)}, u32[]{:S(2)}, u32[]{:S(2)}) async-start(bf16[4,128,128]{2,1,0:T(8,128)(2,1)} %bitcast.6), calls=%async_computation.1 | async-start | bytes 262144 | tf_op jit(solution)/shard_map/all_to_all | solution.py:144
  44.1 0.0 collective-permute-done.2.refs_3_
  44.1 0.0 collective-permute-done.1.refs_2_
  44.1 0.0 collective-permute-done.refs_1_
  44.2 0.2 collective-permute-start.5
  44.4 2.4 %collective-permute-start.4 = (bf16[128,256]{1,0:T(8,128)(2,1)S(1)}, bf16[128,256]{1,0:T(8,128)(2,1)S(1)}, u32[]{:S(2)}, u32[]{:S(2)}) collective-permute-start(bf16[128,256]{1,0:T(8,128)(2,1)S(1)} %shard_map.99.refs_0_), channel_id=1, source_target_pairs={{0,2},{1,3},{2,0},{3,1},{4,6},{5,7},{6,4},{7,5},{8,10},{9,11},{10,... | collective-permute-start | bytes 196616 | tf_op jit(solution)/shard_map/ppermute | solution.py:30
  46.8 1.2 %collective-permute-start.3 = (bf16[128,256]{1,0:T(8,128)(2,1)S(1)}, bf16[128,256]{1,0:T(8,128)(2,1)S(1)}, u32[]{:S(2)}, u32[]{:S(2)}) collective-permute-start(bf16[128,256]{1,0:T(8,128)(2,1)S(1)} %shard_map.99.refs_0_), channel_id=1, source_target_pairs={{0,3},{1,0},{2,1},{3,2},{4,7},{5,4},{6,5},{7,6},{8,11},{9,8},{10,9... | collective-permute-start | bytes 196616 | tf_op jit(solution)/shard_map/ppermute | solution.py:30
  48.0 0.6 %all-to-all-done.1 = bf16[4,128,128]{2,1,0:T(8,128)(2,1)S(1)} async-done(((bf16[4,128,128]{2,1,0:T(8,128)(2,1)}), bf16[4,128,128]{2,1,0:T(8,128)(2,1)S(1)}, u32[]{:S(2)}, u32[]{:S(2)}) %all-to-all-start.1) | async-done | bytes 131104 | tf_op jit(solution)/shard_map/all_to_all | solution.py:144
  48.7 0.6 %shard_map.98 = bf16[128,128]{1,0:T(8,128)(2,1)} custom-call(bf16[512,128]{1,0:T(8,128)(2,1)S(1)} %bitcast.9), custom_call_target="tpu_custom_call" | custom-call | tf_op jit(solution)/shard_map/pallas_call | solution.py:150
  49.3 1.7 %collective-permute-done.5.refs_3_ = bf16[128,256]{1,0:T(8,128)(2,1)S(1)} collective-permute-done((bf16[128,256]{1,0:T(8,128)(2,1)S(1)}, bf16[128,256]{1,0:T(8,128)(2,1)S(1)}, u32[]{:S(2)}, u32[]{:S(2)}) %collective-permute-start.5) | collective-permute-done | bytes 65568 | tf_op jit(solution)/shard_map/ppermute | solution.py:30
  51.0 1.9 %collective-permute-done.4.refs_2_ = bf16[128,256]{1,0:T(8,128)(2,1)S(1)} collective-permute-done((bf16[128,256]{1,0:T(8,128)(2,1)S(1)}, bf16[128,256]{1,0:T(8,128)(2,1)S(1)}, u32[]{:S(2)}, u32[]{:S(2)}) %collective-permute-start.4) | collective-permute-done | bytes 65568 | tf_op jit(solution)/shard_map/ppermute | solution.py:30
  52.9 0.0 collective-permute-done.3.refs_1_
  52.9 0.7 %shard_map.100 = f32[128,256]{1,0:T(8,128)} custom-call(bf16[128,256]{1,0:T(8,128)(2,1)S(1)} %shard_map.99.refs_0_, bf16[128,256]{1,0:T(8,128)(2,1)S(1)} %collective-permute-done.3.refs_1_, bf16[128,256]{1,0:T(8,128)(2,1)S(1)} %collective-permute-done.4.refs_2_, bf16[128,256]{1,0:T(8,128)(2,1)S(1)} %collective-permute-done.5.refs_3_), custom_call_target="tpu_custom_call" | custom-call | tf_op jit(solution)/shard_map/pallas_call | solution.py:152
  (1 shorter events, 0.0 us)
Async XLA Ops:
  8.0 0.7 %copy-start.3 = (s32[1,1,8]{2,1,0:T(1,128)S(1)}, s32[1,1,8]{2,1,0:T(1,128)}, u32[]{:S(2)}) copy-start(s32[1,1,8]{2,1,0:T(1,128)} %param.11) | copy-start | bytes 100
  8.0 0.7 %copy-start.4 = (s32[1,1,8]{2,1,0:T(1,128)S(1)}, s32[1,1,8]{2,1,0:T(1,128)}, u32[]{:S(2)}) copy-start(s32[1,1,8]{2,1,0:T(1,128)} %param.12) | copy-start | bytes 100
  8.6 0.9 %copy-start = (bf16[1,1,8,128,128]{4,3,2,1,0:T(8,128)(2,1)S(1)}, bf16[1,1,8,128,128]{4,3,2,1,0:T(8,128)(2,1)}, u32[]{:S(2)}) copy-start(bf16[1,1,8,128,128]{4,3,2,1,0:T(8,128)(2,1)} %param.10) | copy-start | bytes 786436
  10.7 11.7 %copy-start.1 = (bf16[128,256]{1,0:T(8,128)(2,1)S(1)}, bf16[128,256]{1,0:T(8,128)(2,1)}, u32[]{:S(2)}) copy-start(bf16[128,256]{1,0:T(8,128)(2,1)} %weight.1) | copy-start | bytes 196612
  10.7 11.7 %copy-start.2 = (bf16[128,256]{1,0:T(8,128)(2,1)S(1)}, bf16[128,256]{1,0:T(8,128)(2,1)}, u32[]{:S(2)}) copy-start(bf16[128,256]{1,0:T(8,128)(2,1)} %cotangent.1) | copy-start | bytes 196612
  23.3 20.8 %collective-permute-start.2 = (bf16[128,256]{1,0:T(8,128)(2,1)S(1)}, bf16[128,256]{1,0:T(8,128)(2,1)S(1)}, u32[]{:S(2)}, u32[]{:S(2)}) collective-permute-start(bf16[128,256]{1,0:T(8,128)(2,1)S(1)} %get-tuple-element.12.refs_0_), channel_id=1, source_target_pairs={{0,4},{4,8},{8,12},{12,0},{1,5},{5,9},{9,13},{13,1},{2,6},{6,10},{... | collective-permute-start | bytes 196616 | tf_op jit(solution)/shard_map/ppermute | solution.py:30
  23.3 20.8 %collective-permute-start.1 = (bf16[128,256]{1,0:T(8,128)(2,1)S(1)}, bf16[128,256]{1,0:T(8,128)(2,1)S(1)}, u32[]{:S(2)}, u32[]{:S(2)}) collective-permute-start(bf16[128,256]{1,0:T(8,128)(2,1)S(1)} %get-tuple-element.12.refs_0_), channel_id=1, source_target_pairs={{0,8},{4,12},{8,0},{12,4},{1,9},{5,13},{9,1},{13,5},{2,10},{6,14},... | collective-permute-start | bytes 196616 | tf_op jit(solution)/shard_map/ppermute | solution.py:30
  24.9 19.2 %collective-permute-start = (bf16[128,256]{1,0:T(8,128)(2,1)S(1)}, bf16[128,256]{1,0:T(8,128)(2,1)S(1)}, u32[]{:S(2)}, u32[]{:S(2)}) collective-permute-start(bf16[128,256]{1,0:T(8,128)(2,1)S(1)} %get-tuple-element.12.refs_0_), channel_id=1, source_target_pairs={{0,12},{4,0},{8,4},{12,8},{1,13},{5,1},{9,5},{13,9},{2,14},{6,2},{... | collective-permute-start | bytes 196616 | tf_op jit(solution)/shard_map/ppermute | solution.py:30
  40.8 7.9 %all-to-all-start.1 = ((bf16[4,128,128]{2,1,0:T(8,128)(2,1)}), bf16[4,128,128]{2,1,0:T(8,128)(2,1)S(1)}, u32[]{:S(2)}, u32[]{:S(2)}) async-start(bf16[4,128,128]{2,1,0:T(8,128)(2,1)} %bitcast.6), calls=%async_computation.1 | async-start | bytes 262144 | tf_op jit(solution)/shard_map/all_to_all | solution.py:144
  44.2 6.8 %collective-permute-start.5 = (bf16[128,256]{1,0:T(8,128)(2,1)S(1)}, bf16[128,256]{1,0:T(8,128)(2,1)S(1)}, u32[]{:S(2)}, u32[]{:S(2)}) collective-permute-start(bf16[128,256]{1,0:T(8,128)(2,1)S(1)} %shard_map.99.refs_0_), channel_id=1, source_target_pairs={{0,1},{1,2},{2,3},{3,0},{4,5},{5,6},{6,7},{7,4},{8,9},{9,10},{10,1... | collective-permute-start | bytes 196616 | tf_op jit(solution)/shard_map/ppermute | solution.py:30
  44.4 8.5 %collective-permute-start.4 = (bf16[128,256]{1,0:T(8,128)(2,1)S(1)}, bf16[128,256]{1,0:T(8,128)(2,1)S(1)}, u32[]{:S(2)}, u32[]{:S(2)}) collective-permute-start(bf16[128,256]{1,0:T(8,128)(2,1)S(1)} %shard_map.99.refs_0_), channel_id=1, source_target_pairs={{0,2},{1,3},{2,0},{3,1},{4,6},{5,7},{6,4},{7,5},{8,10},{9,11},{10,... | collective-permute-start | bytes 196616 | tf_op jit(solution)/shard_map/ppermute | solution.py:30
  46.8 6.1 %collective-permute-start.3 = (bf16[128,256]{1,0:T(8,128)(2,1)S(1)}, bf16[128,256]{1,0:T(8,128)(2,1)S(1)}, u32[]{:S(2)}, u32[]{:S(2)}) collective-permute-start(bf16[128,256]{1,0:T(8,128)(2,1)S(1)} %shard_map.99.refs_0_), channel_id=1, source_target_pairs={{0,3},{1,0},{2,1},{3,2},{4,7},{5,4},{6,5},{7,6},{8,11},{9,8},{10,9... | collective-permute-start | bytes 196616 | tf_op jit(solution)/shard_map/ppermute | solution.py:30

commit v3 on v1

v3 whole, which is shorter than its diff:
```python
import functools

import jax
import jax.numpy as jnp
from jax import lax
from jax.experimental import pallas as pl
from jax.experimental.pallas import tpu as pltpu
from jax.sharding import PartitionSpec as P

VMEM = pl.BlockSpec(memory_space=pltpu.VMEM)
ANY = pl.BlockSpec(memory_space=pl.ANY)
HBM = pl.BlockSpec(memory_space=pltpu.HBM)
LEAST = 16 * 1024 * 1024
NARROW = jnp.bfloat16


def call(kernel, outs, in_specs, scratch=(), flops=0, need=0, after=()):
    outs = tuple(jax.ShapeDtypeStruct(shape, dtype) for shape, dtype in outs)
    late = len(after)
    run = pl.pallas_call(
        (lambda *refs: kernel(*refs[late:])) if late else kernel,
        out_shape=outs,
        in_specs=[ANY] * late + list(in_specs),
        out_specs=(VMEM,) * len(outs),
        scratch_shapes=scratch,
        compiler_params=pltpu.CompilerParams(vmem_limit_bytes=LEAST + need),
        cost_estimate=pl.CostEstimate(flops=flops, bytes_accessed=need, transcendentals=0),
    )
    return functools.partial(run, *after)


def swap(value, axis, distance):
    n = lax.axis_size(axis)
    return lax.ppermute(value, axis, [(s, s ^ distance) for s in range(n)])


def wide(value):
    return value.astype(jnp.float32)


def split(value):
    high = value.astype(NARROW)
    return high, (value - wide(high)).astype(NARROW)


def dot(left, right, dims=((1,), (0,))):
    return lax.dot_general(left, right, (dims, ((), ())), preferred_element_type=jnp.float32)


def dense_kernel(piece, vals_in, rows_in, cols_in, count_in, near, vals, rows, cols, count, sems):
    copies = [
        pltpu.make_async_copy(source, target, sems.at[k])
        for k, (source, target) in enumerate(
            ((rows_in, rows), (cols_in, cols), (count_in, count), (vals_in, vals))
        )
    ]
    for copy in copies:
        copy.start()
    my_row, my_col = lax.axis_index("row"), lax.axis_index("col")
    side = vals.shape[-1]
    near[...] = jnp.zeros_like(near)
    for copy in copies:
        copy.wait()

    def add(t, _):
        row, col = rows[0, 0, t], cols[0, 0, t]
        row = ((row // piece) ^ my_col) * piece + lax.rem(row, piece)
        col = ((col // piece) ^ my_row) * piece + lax.rem(col, piece)
        down = pl.ds(pl.multiple_of(row * side, side), side)
        across = pl.ds(pl.multiple_of(col * side, side), side)
        near[down, across] = vals[0, 0, t]
        return 0

    lax.fori_loop(0, count[0, 0], add, 0)


def turn_kernel(step, near, far):
    def turn(k, _):
        band = pl.ds(pl.multiple_of(k * step, step), step)
        far[:, band] = near[band, :].T
        return 0

    lax.fori_loop(0, near.shape[0] // step, turn, 0)


def tree(terms):
    while len(terms) > 1:
        terms = [left + right for left, right in zip(terms[::2], terms[1::2])]
    return terms[0]


def forward_kernel(n, matrix, *refs):
    operands, own, sends = refs[:n], refs[n], refs[n + 1 :]
    rows = own.shape[0]
    stacked = jnp.concatenate([operand[...] for operand in operands], axis=0)
    product = dot(matrix[...], stacked)
    own[...] = product[:rows]
    for d, send in enumerate(sends, 1):
        send[...] = product[d * rows : (d + 1) * rows].astype(send.dtype)


def layer_kernel(*refs):
    *parts, weight, cotangent, same, other, pre_out = refs
    nodes, hidden = cotangent.shape
    half = hidden // 2
    total = tree([wide(part[...]) for part in parts])
    high, low = split(total)
    pre = dot(high, weight[...]) + dot(low, weight[...])
    pre_out[...] = pre
    sigma = jax.nn.sigmoid(pre)
    grad = wide(cotangent[...]) * sigma * (1.0 + pre * (1.0 - sigma))
    grad_high, grad_low = split(grad)
    across = ((1,), (1,))
    back = dot(grad_high, weight[...], across) + dot(grad_low, weight[...], across)
    same[:nodes] = back.astype(same.dtype)
    other[:nodes] = back.astype(other.dtype)
    down = ((0,), (0,))
    term = dot(high, grad_high, down) + dot(low, grad_high, down) + dot(high, grad_low, down)
    term = term.astype(same.dtype)
    odd = lax.rem(lax.axis_index("col"), 2) == 1
    left, right = term[:, :half], term[:, half:]
    same[nodes:] = jnp.where(odd, right, left)
    other[nodes:] = jnp.where(odd, left, right)


def act_kernel(pre, act):
    act[...] = (pre[...] * jax.nn.sigmoid(pre[...])).astype(act.dtype)


def backward_kernel(n, matrix, *refs):
    messages, own, kept, sends = refs[:n], refs[n], refs[n + 1], refs[n + 2 :]
    rows = own.shape[0]
    stacked = jnp.concatenate([message[:rows] for message in messages], axis=0)
    product = dot(matrix[...], stacked)
    own[...] = product[:rows]
    term = tree([wide(message[rows:]) for message in messages]).astype(kept.dtype)
    kept[...] = term
    for d, send in enumerate(sends, 1):
        send[:rows] = product[d * rows : (d + 1) * rows].astype(send.dtype)
        send[rows:] = term


def term_kernel(scale, kept, *refs):
    *messages, half = refs
    rows = messages[0].shape[0] - kept.shape[0]
    half[...] = tree([wide(kept[...])] + [wide(message[rows:]) for message in messages]) * scale


def feature_kernel(own, *refs):
    *messages, out = refs
    rows = own.shape[0]
    out[...] = tree([own[...]] + [wide(message[:rows]) for message in messages]).astype(out.dtype)


def join_kernel(mine, other, out):
    half = mine.shape[1]
    odd = lax.rem(lax.axis_index("col"), 2) == 1
    out[:, :half] = jnp.where(odd, other[...], mine[...])
    out[:, half:] = jnp.where(odd, mine[...], other[...])


def per_device(features, weight, cotangent, tile_values, tile_rows, tile_cols, tile_count):
    slots, side = tile_values.shape[2:4]
    n_row, n_col = lax.axis_size("row"), lax.axis_size("col")
    nodes, width = features.shape
    hidden = weight.shape[1]
    half = hidden // 2
    down, across = n_col * nodes, n_row * nodes
    dense_bytes = 2 * down * across

    gathered = [swap(features, "row", d) for d in range(n_row - 1, 0, -1)][::-1]
    (near,) = call(
        functools.partial(dense_kernel, nodes // side),
        [((down, across), NARROW)],
        [HBM] * 4,
        scratch=[
            pltpu.VMEM(tile_values.shape, NARROW),
            pltpu.SMEM(tile_rows.shape, jnp.int32),
            pltpu.SMEM(tile_cols.shape, jnp.int32),
            pltpu.SMEM(tile_count.shape, jnp.int32),
            pltpu.SemaphoreType.DMA((4,)),
        ],
        need=2 * dense_bytes,
    )(tile_values, tile_rows, tile_cols, tile_count)

    own, *sends = call(
        functools.partial(forward_kernel, n_row),
        [((nodes, width), jnp.float32)] + [((nodes, width), NARROW)] * (n_col - 1),
        [VMEM] * (1 + n_row),
        flops=2 * down * across * width,
        need=2 * dense_bytes,
    )(near, features, *gathered)
    parts = [swap(sends[d - 1], "col", d) for d in range(n_col - 1, 0, -1)][::-1]
    (far,) = call(
        functools.partial(turn_kernel, side),
        [((across, down), NARROW)],
        [VMEM],
        need=3 * dense_bytes,
    )(near)

    message = ((nodes + width, width), NARROW)
    same, other, pre = call(
        layer_kernel,
        [message, message, ((nodes, hidden), jnp.float32)],
        [VMEM] * (n_col + 2),
        flops=14 * nodes * width * hidden,
        after=[far],
    )(own, *parts, weight, cotangent)
    spread = [swap((same, other)[d % 2], "col", d) for d in range(n_col - 1, 0, -1)][::-1]
    (act,) = call(act_kernel, [((nodes, hidden), NARROW)], [VMEM])(pre)

    own, kept, *sends = call(
        functools.partial(backward_kernel, n_col),
        [((nodes, width), jnp.float32), ((width, half), NARROW)] + [message] * (n_row - 1),
        [VMEM] * (1 + n_col),
        flops=2 * down * across * width,
        need=2 * dense_bytes,
    )(far, same, *spread)
    parts = [swap(sends[d - 1], "row", d) for d in range(n_row - 1, 0, -1)][::-1]

    scale = float(nodes * n_row * n_col) ** -0.5
    (mine,) = call(
        functools.partial(term_kernel, scale), [((width, half), jnp.float32)], [VMEM] * n_row
    )(kept, *parts)
    (grad_features,) = call(feature_kernel, [((nodes, width), NARROW)], [VMEM] * n_row)(
        own, *parts
    )
    (grad_weight,) = call(join_kernel, [((width, hidden), jnp.float32)], [VMEM] * 2)(
        mine, swap(mine, "col", 1)
    )
    return act, grad_features, grad_weight


def solution(mesh):
    placed = (
        P(("groups", "row", "col"), None),
        P(),
        P(("groups", "row", "col"), None),
        P(("groups", "row"), "col", None, None, None),
        P(("groups", "row"), "col", None),
        P(("groups", "row"), "col", None),
        P(("groups", "row"), "col"),
    )
    return jax.shard_map(
        per_device,
        mesh=mesh,
        in_specs=placed,
        out_specs=(
            P(("groups", "row", "col"), None),
            P(("groups", "row", "col"), None),
            P("groups", None),
        ),
        check_vma=False,
    )
```

time: 37.6 us -> 35.9 us (0.955)
  starting transfers between devices: 22.1 us -> 14.1 us
  waiting for transfers between devices: 8.51 us -> 15.3 us
  local copies, waits for them, and re-layouts: 1.62 us -> 0.96 us
    ppermute x18 -> x13, starting transfers between devices: 22.1 us -> 14.1 us  [swap(): return lax.ppermute(value, axis, [(s, s ^ distance) for s in range(n)])]
    ppermute x18 -> x13, waiting for transfers between devices: 8.51 us -> 15.3 us  [swap(): return lax.ppermute(value, axis, [(s, s ^ distance) for s in range(n)])]
    unnamed x12, local copies, waits for them, and re-layouts: 1.62 us -> 0.96 us
    pallas_call x7 -> x9, Pallas kernels: 3.68 us -> 3.96 us  [the longest x1 0.67 us: per_device(): call(join_kernel, [((width, hidden), jnp.float32)], [VMEM] * 2)]
  transfers between devices with their start and end apart: 18 -> 13, of which waited for: 7 -> 8; matrix products, arithmetic and copies ran while one was open for 0% -> 0% of each run, Pallas kernels for 5% -> 6%
where the time goes in v3:
time: 35.9 us; the launch traced here: 35.7 us
  waiting for transfers between devices  15.3 us (43%)
  starting transfers between devices  14.1 us (39%)
  Pallas kernels  3.96 us (11%)
  between operations  1.41 us (4%)
  local copies, waits for them, and re-layouts  0.96 us (3%)
    ppermute x13, waiting for transfers between devices, swap(): return lax.ppermute(value, axis, [(s, s ^ distance) for s in range(n)])  15.3 us
    ppermute x13, starting transfers between devices, swap(): return lax.ppermute(value, axis, [(s, s ^ distance) for s in range(n)])  14.1 us
    unnamed x12, local copies, waits for them, and re-layouts  0.96 us
  transfers between devices with their start and end apart: 13, of which 8 were waited for; matrix products, arithmetic and copies ran while one was open for 0% of the time, Pallas kernels for 6%

profile of v3, /device:TPU:0, one launch (start us, length us, event | category | flops | bytes accessed | tf_op | source)
XLA Modules:
  0.0 35.7 jit_solution(15001951481003387966)
XLA Ops:
  0.6 0.0 copy-start.5
  0.6 0.0 copy-start.4
  0.7 3.0 %collective-permute-start.1 = (bf16[128,128]{1,0:T(8,128)(2,1)}, bf16[128,128]{1,0:T(8,128)(2,1)S(1)}, u32[]{:S(2)}, u32[]{:S(2)}) collective-permute-start(bf16[128,128]{1,0:T(8,128)(2,1)} %refs_0_.1), channel_id=1, source_target_pairs={{0,8},{4,12},{8,0},{12,4},{1,9},{5,13},{9,1},{13,5},{2,10},{6,14},... | collective-permute-start | bytes 98312 | tf_op jit(solution)/shard_map/ppermute | solution.py:34
  3.7 0.0 collective-permute-start
  3.7 0.2 collective-permute-start.2
  4.5 0.0 copy-done.5
  4.5 0.0 copy-done.4
  4.5 0.0 copy-start
  4.5 0.9 %copy-done = bf16[1,1,8,128,128]{4,3,2,1,0:T(8,128)(2,1)S(1)} copy-done((bf16[1,1,8,128,128]{4,3,2,1,0:T(8,128)(2,1)S(1)}, bf16[1,1,8,128,128]{4,3,2,1,0:T(8,128)(2,1)}, u32[]{:S(2)}) %copy-start) | copy-done | bytes 262168
  5.5 0.0 copy-start.3
  5.5 0.6 %shard_map.94.near.matrix = bf16[512,512]{1,0:T(8,128)(2,1)S(1)} custom-call(bf16[1,1,8,128,128]{4,3,2,1,0:T(8,128)(2,1)S(1)} %copy-done, s32[1,1,8]{2,1,0:T(1,128)S(1)} %copy-done.4, s32[1,1,8]{2,1,0:T(1,128)S(1)} %copy-done.5, s32[1,1]{1,0:T(1,128)S(6)} %copy.10.count_in), custom_call_target="tpu_custom_call" | custom-call | bytes 1048576 | tf_op jit(solution)/shard_map/pallas_call | solution.py:172
  6.1 0.0 collective-permute-done.1.refs_2_
  6.1 0.0 collective-permute-done.refs_1_
  6.2 1.1 %collective-permute-done.2.refs_3_ = bf16[128,128]{1,0:T(8,128)(2,1)S(1)} collective-permute-done((bf16[128,128]{1,0:T(8,128)(2,1)}, bf16[128,128]{1,0:T(8,128)(2,1)S(1)}, u32[]{:S(2)}, u32[]{:S(2)}) %collective-permute-start.2) | collective-permute-done | bytes 32800 | tf_op jit(solution)/shard_map/ppermute | solution.py:34
  7.2 0.0 copy-done.3
  7.2 0.3 shard_map.96
  7.5 1.6 %collective-permute-start.3 = (bf16[128,128]{1,0:T(8,128)(2,1)S(1)}, bf16[128,128]{1,0:T(8,128)(2,1)S(1)}, u32[]{:S(2)}, u32[]{:S(2)}) collective-permute-start(bf16[128,128]{1,0:T(8,128)(2,1)S(1)} %get-tuple-element.16), channel_id=1, source_target_pairs={{0,1},{1,0},{2,3},{3,2},{4,5},{5,4},{6,7},{7,6},{8,9},{9,8},{10,11... | collective-permute-start | bytes 98312 | tf_op jit(solution)/shard_map/ppermute | solution.py:34
  9.2 2.6 %collective-permute-start.4 = (bf16[128,128]{1,0:T(8,128)(2,1)S(1)}, bf16[128,128]{1,0:T(8,128)(2,1)S(1)}, u32[]{:S(2)}, u32[]{:S(2)}) collective-permute-start(bf16[128,128]{1,0:T(8,128)(2,1)S(1)} %get-tuple-element.17), channel_id=1, source_target_pairs={{0,2},{1,3},{2,0},{3,1},{4,6},{5,7},{6,4},{7,5},{8,10},{9,11},{10,... | collective-permute-start | bytes 98312 | tf_op jit(solution)/shard_map/ppermute | solution.py:34
  11.7 0.0 copy-start.1
  11.7 0.0 copy-start.2
  11.7 0.2 collective-permute-start.5
  12.0 0.3 shard_map.95.refs_0_.matrix
  12.3 0.0 collective-permute-done.3.refs_2_
  12.3 2.2 %collective-permute-done.4.refs_3_ = bf16[128,128]{1,0:T(8,128)(2,1)S(1)} collective-permute-done((bf16[128,128]{1,0:T(8,128)(2,1)S(1)}, bf16[128,128]{1,0:T(8,128)(2,1)S(1)}, u32[]{:S(2)}, u32[]{:S(2)}) %collective-permute-start.4) | collective-permute-done | bytes 32800 | tf_op jit(solution)/shard_map/ppermute | solution.py:34
  14.6 2.9 %collective-permute-done.5.refs_4_ = bf16[128,128]{1,0:T(8,128)(2,1)S(1)} collective-permute-done((bf16[128,128]{1,0:T(8,128)(2,1)S(1)}, bf16[128,128]{1,0:T(8,128)(2,1)S(1)}, u32[]{:S(2)}, u32[]{:S(2)}) %collective-permute-start.5) | collective-permute-done | bytes 32800 | tf_op jit(solution)/shard_map/ppermute | solution.py:34
  17.5 0.0 copy-done.1
  17.5 0.0 copy-done.2
  17.5 0.4 %shard_map.97 = (bf16[256,128]{1,0:T(8,128)(2,1)S(1)}, bf16[256,128]{1,0:T(8,128)(2,1)S(1)}, f32[128,256]{1,0:T(8,128)S(1)}) custom-call(bf16[512,512]{1,0:T(8,128)(2,1)S(1)} %shard_map.95.refs_0_.matrix, f32[128,128]{1,0:T(8,128)S(1)} %get-tuple-element.15.refs_1_, bf16[128,128]{1,0:T(8,128)(2,1)S(1)} %collective-permute-done.3.refs_2_, ...), custom_call_target="tpu_custom_call" | custom-call | flops 58720256 | tf_op jit(solution)/shard_map/pallas_call | solution.py:202
  17.9 0.1 collective-permute-start.7
  18.0 1.0 %collective-permute-start.8 = (bf16[256,128]{1,0:T(8,128)(2,1)S(1)}, bf16[256,128]{1,0:T(8,128)(2,1)S(1)}, u32[]{:S(2)}, u32[]{:S(2)}) collective-permute-start(bf16[256,128]{1,0:T(8,128)(2,1)S(1)} %get-tuple-element.21), channel_id=1, source_target_pairs={{0,3},{1,2},{2,1},{3,0},{4,7},{5,6},{6,5},{7,4},{8,11},{9,10},{10,... | collective-permute-start | bytes 196616 | tf_op jit(solution)/shard_map/ppermute | solution.py:34
  18.9 2.5 %collective-permute-start.6 = (bf16[256,128]{1,0:T(8,128)(2,1)S(1)}, bf16[256,128]{1,0:T(8,128)(2,1)S(1)}, u32[]{:S(2)}, u32[]{:S(2)}) collective-permute-start(bf16[256,128]{1,0:T(8,128)(2,1)S(1)} %get-tuple-element.21), channel_id=1, source_target_pairs={{0,1},{1,0},{2,3},{3,2},{4,5},{5,4},{6,7},{7,6},{8,9},{9,8},{10,11... | collective-permute-start | bytes 196616 | tf_op jit(solution)/shard_map/ppermute | solution.py:34
  21.4 3.0 %collective-permute-done.7.refs_2_ = bf16[256,128]{1,0:T(8,128)(2,1)S(1)} collective-permute-done((bf16[256,128]{1,0:T(8,128)(2,1)S(1)}, bf16[256,128]{1,0:T(8,128)(2,1)S(1)}, u32[]{:S(2)}, u32[]{:S(2)}) %collective-permute-start.7) | collective-permute-done | bytes 65568 | tf_op jit(solution)/shard_map/ppermute | solution.py:34
  24.5 0.0 collective-permute-done.8.refs_3_
  24.5 0.4 %collective-permute-done.6.refs_1_ = bf16[256,128]{1,0:T(8,128)(2,1)S(1)} collective-permute-done((bf16[256,128]{1,0:T(8,128)(2,1)S(1)}, bf16[256,128]{1,0:T(8,128)(2,1)S(1)}, u32[]{:S(2)}, u32[]{:S(2)}) %collective-permute-start.6) | collective-permute-done | bytes 65568 | tf_op jit(solution)/shard_map/ppermute | solution.py:34
  24.8 0.3 shard_map.99
  25.1 0.1 collective-permute-start.9
  25.2 0.9 %collective-permute-start.10 = (bf16[256,128]{1,0:T(8,128)(2,1)S(1)}, bf16[256,128]{1,0:T(8,128)(2,1)S(1)}, u32[]{:S(2)}, u32[]{:S(2)}) collective-permute-start(bf16[256,128]{1,0:T(8,128)(2,1)S(1)} %get-tuple-element.24), channel_id=1, source_target_pairs={{0,8},{4,12},{8,0},{12,4},{1,9},{5,13},{9,1},{13,5},{2,10},{6,14},... | collective-permute-start | bytes 196616 | tf_op jit(solution)/shard_map/ppermute | solution.py:34
  26.1 0.9 %collective-permute-start.11 = (bf16[256,128]{1,0:T(8,128)(2,1)S(1)}, bf16[256,128]{1,0:T(8,128)(2,1)S(1)}, u32[]{:S(2)}, u32[]{:S(2)}) collective-permute-start(bf16[256,128]{1,0:T(8,128)(2,1)S(1)} %get-tuple-element.25), channel_id=1, source_target_pairs={{0,12},{4,8},{8,4},{12,0},{1,13},{5,9},{9,5},{13,1},{2,14},{6,10},... | collective-permute-start | bytes 196616 | tf_op jit(solution)/shard_map/ppermute | solution.py:34
  27.1 0.0 collective-permute-done.9.refs_0_
  27.1 3.1 %collective-permute-done.10.refs_1_ = bf16[256,128]{1,0:T(8,128)(2,1)S(1)} collective-permute-done((bf16[256,128]{1,0:T(8,128)(2,1)S(1)}, bf16[256,128]{1,0:T(8,128)(2,1)S(1)}, u32[]{:S(2)}, u32[]{:S(2)}) %collective-permute-start.10) | collective-permute-done | bytes 65568 | tf_op jit(solution)/shard_map/ppermute | solution.py:34
  30.2 0.5 %collective-permute-done.11.refs_2_ = bf16[256,128]{1,0:T(8,128)(2,1)S(1)} collective-permute-done((bf16[256,128]{1,0:T(8,128)(2,1)S(1)}, bf16[256,128]{1,0:T(8,128)(2,1)S(1)}, u32[]{:S(2)}, u32[]{:S(2)}) %collective-permute-start.11) | collective-permute-done | bytes 65568 | tf_op jit(solution)/shard_map/ppermute | solution.py:34
  30.7 1.0 %collective-permute-start.12 = (f32[128,128]{1,0:T(8,128)S(1)}, f32[128,128]{1,0:T(8,128)S(1)}, u32[]{:S(2)}, u32[]{:S(2)}) collective-permute-start(f32[128,128]{1,0:T(8,128)S(1)} %shard_map.101.mine), channel_id=1, source_target_pairs={{0,1},{1,0},{2,3},{3,2},{4,5},{5,4},{6,7},{7,6},{8,9},{9,8},{10,11... | collective-permute-start | bytes 196616 | tf_op jit(solution)/shard_map/ppermute | solution.py:34
  31.6 0.7 %shard_map.98 = bf16[128,256]{1,0:T(8,128)(2,1)} custom-call(f32[128,256]{1,0:T(8,128)S(1)} %get-tuple-element.19.pre), custom_call_target="tpu_custom_call" | custom-call | tf_op jit(solution)/shard_map/pallas_call | solution.py:210
  32.3 0.6 %shard_map.100 = bf16[128,128]{1,0:T(8,128)(2,1)} custom-call(f32[128,128]{1,0:T(8,128)S(1)} %get-tuple-element.22.own, bf16[256,128]{1,0:T(8,128)(2,1)S(1)} %collective-permute-done.9.refs_0_, bf16[256,128]{1,0:T(8,128)(2,1)S(1)} %collective-permute-done.10.refs_1_, bf16[256,128]{1,0:T(8,128)(2,1)S(1)} %collective-permute-done.11.refs_2_), custom_call_target="tpu_custom_call" | custom-call | tf_op jit(solution)/shard_map/pallas_call | solution.py:225
  32.9 2.1 %collective-permute-done.12.other = f32[128,128]{1,0:T(8,128)S(1)} collective-permute-done((f32[128,128]{1,0:T(8,128)S(1)}, f32[128,128]{1,0:T(8,128)S(1)}, u32[]{:S(2)}, u32[]{:S(2)}) %collective-permute-start.12) | collective-permute-done | bytes 65568 | tf_op jit(solution)/shard_map/ppermute | solution.py:34
  35.0 0.7 %shard_map.102 = f32[128,256]{1,0:T(8,128)} custom-call(f32[128,128]{1,0:T(8,128)S(1)} %shard_map.101.mine, f32[128,128]{1,0:T(8,128)S(1)} %collective-permute-done.12.other), custom_call_target="tpu_custom_call" | custom-call | tf_op jit(solution)/shard_map/pallas_call | solution.py:228
  (1 shorter events, 0.0 us)
Async XLA Ops:
  0.6 3.9 %copy-start.5 = (s32[1,1,8]{2,1,0:T(1,128)S(1)}, s32[1,1,8]{2,1,0:T(1,128)}, u32[]{:S(2)}) copy-start(s32[1,1,8]{2,1,0:T(1,128)} %cols_in.1) | copy-start | bytes 100
  0.6 3.9 %copy-start.4 = (s32[1,1,8]{2,1,0:T(1,128)S(1)}, s32[1,1,8]{2,1,0:T(1,128)}, u32[]{:S(2)}) copy-start(s32[1,1,8]{2,1,0:T(1,128)} %rows_in.1) | copy-start | bytes 100
  0.7 5.5 %collective-permute-start.1 = (bf16[128,128]{1,0:T(8,128)(2,1)}, bf16[128,128]{1,0:T(8,128)(2,1)S(1)}, u32[]{:S(2)}, u32[]{:S(2)}) collective-permute-start(bf16[128,128]{1,0:T(8,128)(2,1)} %refs_0_.1), channel_id=1, source_target_pairs={{0,8},{4,12},{8,0},{12,4},{1,9},{5,13},{9,1},{13,5},{2,10},{6,14},... | collective-permute-start | bytes 98312 | tf_op jit(solution)/shard_map/ppermute | solution.py:34
  3.7 2.5 %collective-permute-start = (bf16[128,128]{1,0:T(8,128)(2,1)}, bf16[128,128]{1,0:T(8,128)(2,1)S(1)}, u32[]{:S(2)}, u32[]{:S(2)}) collective-permute-start(bf16[128,128]{1,0:T(8,128)(2,1)} %refs_0_.1), channel_id=1, source_target_pairs={{0,4},{4,0},{8,12},{12,8},{1,5},{5,1},{9,13},{13,9},{2,6},{6,2},{1... | collective-permute-start | bytes 98312 | tf_op jit(solution)/shard_map/ppermute | solution.py:34
  3.7 3.6 %collective-permute-start.2 = (bf16[128,128]{1,0:T(8,128)(2,1)}, bf16[128,128]{1,0:T(8,128)(2,1)S(1)}, u32[]{:S(2)}, u32[]{:S(2)}) collective-permute-start(bf16[128,128]{1,0:T(8,128)(2,1)} %refs_0_.1), channel_id=1, source_target_pairs={{0,12},{4,8},{8,4},{12,0},{1,13},{5,9},{9,5},{13,1},{2,14},{6,10},... | collective-permute-start | bytes 98312 | tf_op jit(solution)/shard_map/ppermute | solution.py:34
  4.5 1.0 %copy-start = (bf16[1,1,8,128,128]{4,3,2,1,0:T(8,128)(2,1)S(1)}, bf16[1,1,8,128,128]{4,3,2,1,0:T(8,128)(2,1)}, u32[]{:S(2)}) copy-start(bf16[1,1,8,128,128]{4,3,2,1,0:T(8,128)(2,1)} %vals_in.1) | copy-start | bytes 786436
  5.5 1.7 %copy-start.3 = (bf16[128,128]{1,0:T(8,128)(2,1)S(1)}, bf16[128,128]{1,0:T(8,128)(2,1)}, u32[]{:S(2)}) copy-start(bf16[128,128]{1,0:T(8,128)(2,1)} %refs_0_.1) | copy-start | bytes 98308
  7.5 4.8 %collective-permute-start.3 = (bf16[128,128]{1,0:T(8,128)(2,1)S(1)}, bf16[128,128]{1,0:T(8,128)(2,1)S(1)}, u32[]{:S(2)}, u32[]{:S(2)}) collective-permute-start(bf16[128,128]{1,0:T(8,128)(2,1)S(1)} %get-tuple-element.16), channel_id=1, source_target_pairs={{0,1},{1,0},{2,3},{3,2},{4,5},{5,4},{6,7},{7,6},{8,9},{9,8},{10,11... | collective-permute-start | bytes 98312 | tf_op jit(solution)/shard_map/ppermute | solution.py:34
  9.2 5.4 %collective-permute-start.4 = (bf16[128,128]{1,0:T(8,128)(2,1)S(1)}, bf16[128,128]{1,0:T(8,128)(2,1)S(1)}, u32[]{:S(2)}, u32[]{:S(2)}) collective-permute-start(bf16[128,128]{1,0:T(8,128)(2,1)S(1)} %get-tuple-element.17), channel_id=1, source_target_pairs={{0,2},{1,3},{2,0},{3,1},{4,6},{5,7},{6,4},{7,5},{8,10},{9,11},{10,... | collective-permute-start | bytes 98312 | tf_op jit(solution)/shard_map/ppermute | solution.py:34
  11.7 5.7 %copy-start.1 = (bf16[128,256]{1,0:T(8,128)(2,1)S(1)}, bf16[128,256]{1,0:T(8,128)(2,1)}, u32[]{:S(2)}) copy-start(bf16[128,256]{1,0:T(8,128)(2,1)} %refs_5_.1) | copy-start | bytes 196612
  11.7 5.7 %copy-start.2 = (bf16[128,256]{1,0:T(8,128)(2,1)S(1)}, bf16[128,256]{1,0:T(8,128)(2,1)}, u32[]{:S(2)}) copy-start(bf16[128,256]{1,0:T(8,128)(2,1)} %refs_6_.1) | copy-start | bytes 196612
  11.7 5.7 %collective-permute-start.5 = (bf16[128,128]{1,0:T(8,128)(2,1)S(1)}, bf16[128,128]{1,0:T(8,128)(2,1)S(1)}, u32[]{:S(2)}, u32[]{:S(2)}) collective-permute-start(bf16[128,128]{1,0:T(8,128)(2,1)S(1)} %get-tuple-element.18), channel_id=1, source_target_pairs={{0,3},{1,2},{2,1},{3,0},{4,7},{5,6},{6,5},{7,4},{8,11},{9,10},{10,... | collective-permute-start | bytes 98312 | tf_op jit(solution)/shard_map/ppermute | solution.py:34
  17.9 6.6 %collective-permute-start.7 = (bf16[256,128]{1,0:T(8,128)(2,1)S(1)}, bf16[256,128]{1,0:T(8,128)(2,1)S(1)}, u32[]{:S(2)}, u32[]{:S(2)}) collective-permute-start(bf16[256,128]{1,0:T(8,128)(2,1)S(1)} %get-tuple-element.20.refs_0_), channel_id=1, source_target_pairs={{0,2},{1,3},{2,0},{3,1},{4,6},{5,7},{6,4},{7,5},{8,10},{9,11},{10,... | collective-permute-start | bytes 196616 | tf_op jit(solution)/shard_map/ppermute | solution.py:34
  18.0 6.5 %collective-permute-start.8 = (bf16[256,128]{1,0:T(8,128)(2,1)S(1)}, bf16[256,128]{1,0:T(8,128)(2,1)S(1)}, u32[]{:S(2)}, u32[]{:S(2)}) collective-permute-start(bf16[256,128]{1,0:T(8,128)(2,1)S(1)} %get-tuple-element.21), channel_id=1, source_target_pairs={{0,3},{1,2},{2,1},{3,0},{4,7},{5,6},{6,5},{7,4},{8,11},{9,10},{10,... | collective-permute-start | bytes 196616 | tf_op jit(solution)/shard_map/ppermute | solution.py:34
  18.9 5.9 %collective-permute-start.6 = (bf16[256,128]{1,0:T(8,128)(2,1)S(1)}, bf16[256,128]{1,0:T(8,128)(2,1)S(1)}, u32[]{:S(2)}, u32[]{:S(2)}) collective-permute-start(bf16[256,128]{1,0:T(8,128)(2,1)S(1)} %get-tuple-element.21), channel_id=1, source_target_pairs={{0,1},{1,0},{2,3},{3,2},{4,5},{5,4},{6,7},{7,6},{8,9},{9,8},{10,11... | collective-permute-start | bytes 196616 | tf_op jit(solution)/shard_map/ppermute | solution.py:34
  25.1 1.9 %collective-permute-start.9 = (bf16[256,128]{1,0:T(8,128)(2,1)S(1)}, bf16[256,128]{1,0:T(8,128)(2,1)S(1)}, u32[]{:S(2)}, u32[]{:S(2)}) collective-permute-start(bf16[256,128]{1,0:T(8,128)(2,1)S(1)} %get-tuple-element.23), channel_id=1, source_target_pairs={{0,4},{4,0},{8,12},{12,8},{1,5},{5,1},{9,13},{13,9},{2,6},{6,2},{1... | collective-permute-start | bytes 196616 | tf_op jit(solution)/shard_map/ppermute | solution.py:34
  25.2 5.0 %collective-permute-start.10 = (bf16[256,128]{1,0:T(8,128)(2,1)S(1)}, bf16[256,128]{1,0:T(8,128)(2,1)S(1)}, u32[]{:S(2)}, u32[]{:S(2)}) collective-permute-start(bf16[256,128]{1,0:T(8,128)(2,1)S(1)} %get-tuple-element.24), channel_id=1, source_target_pairs={{0,8},{4,12},{8,0},{12,4},{1,9},{5,13},{9,1},{13,5},{2,10},{6,14},... | collective-permute-start | bytes 196616 | tf_op jit(solution)/shard_map/ppermute | solution.py:34
  26.1 4.5 %collective-permute-start.11 = (bf16[256,128]{1,0:T(8,128)(2,1)S(1)}, bf16[256,128]{1,0:T(8,128)(2,1)S(1)}, u32[]{:S(2)}, u32[]{:S(2)}) collective-permute-start(bf16[256,128]{1,0:T(8,128)(2,1)S(1)} %get-tuple-element.25), channel_id=1, source_target_pairs={{0,12},{4,8},{8,4},{12,0},{1,13},{5,9},{9,5},{13,1},{2,14},{6,10},... | collective-permute-start | bytes 196616 | tf_op jit(solution)/shard_map/ppermute | solution.py:34
  30.7 4.3 %collective-permute-start.12 = (f32[128,128]{1,0:T(8,128)S(1)}, f32[128,128]{1,0:T(8,128)S(1)}, u32[]{:S(2)}, u32[]{:S(2)}) collective-permute-start(f32[128,128]{1,0:T(8,128)S(1)} %shard_map.101.mine), channel_id=1, source_target_pairs={{0,1},{1,0},{2,3},{3,2},{4,5},{5,4},{6,7},{7,6},{8,9},{9,8},{10,11... | collective-permute-start | bytes 196616 | tf_op jit(solution)/shard_map/ppermute | solution.py:34

commit v4 on v3

--- a/solution.py
+++ b/solution.py
@@ -32,6 +32,17 @@
 def swap(value, axis, distance):
     n = lax.axis_size(axis)
     return lax.ppermute(value, axis, [(s, s ^ distance) for s in range(n)])
+
+
+def bits(n):
+    return [1 << k for k in range(n.bit_length() - 1)]
+
+
+def gather(own, axis):
+    held = {0: own}
+    for bit in reversed(bits(lax.axis_size(axis))):
+        held.update({d | bit: swap(value, axis, bit) for d, value in held.items()})
+    return [held[d] for d in range(len(held))]
 
 
 def wide(value):
@@ -100,9 +111,8 @@
 
 
 def layer_kernel(*refs):
-    *parts, weight, cotangent, same, other, pre_out = refs
-    nodes, hidden = cotangent.shape
-    half = hidden // 2
+    *parts, weight, cotangent, back, pre_out, mine, other = refs
+    half = mine.shape[1]
     total = tree([wide(part[...]) for part in parts])
     high, low = split(total)
     pre = dot(high, weight[...]) + dot(low, weight[...])
@@ -111,50 +121,59 @@
     grad = wide(cotangent[...]) * sigma * (1.0 + pre * (1.0 - sigma))
     grad_high, grad_low = split(grad)
     across = ((1,), (1,))
-    back = dot(grad_high, weight[...], across) + dot(grad_low, weight[...], across)
-    same[:nodes] = back.astype(same.dtype)
-    other[:nodes] = back.astype(other.dtype)
+    back[...] = (dot(grad_high, weight[...], across) + dot(grad_low, weight[...], across)).astype(
+        back.dtype
+    )
     down = ((0,), (0,))
     term = dot(high, grad_high, down) + dot(low, grad_high, down) + dot(high, grad_low, down)
-    term = term.astype(same.dtype)
-    odd = lax.rem(lax.axis_index("col"), 2) == 1
+    odd = lax.rem(lax.axis_index("row"), 2) == 1
     left, right = term[:, :half], term[:, half:]
-    same[nodes:] = jnp.where(odd, right, left)
-    other[nodes:] = jnp.where(odd, left, right)
+    mine[...] = jnp.where(odd, right, left).astype(mine.dtype)
+    other[...] = jnp.where(odd, left, right).astype(other.dtype)
 
 
 def act_kernel(pre, act):
     act[...] = (pre[...] * jax.nn.sigmoid(pre[...])).astype(act.dtype)
 
 
-def backward_kernel(n, matrix, *refs):
-    messages, own, kept, sends = refs[:n], refs[n], refs[n + 1], refs[n + 2 :]
-    rows = own.shape[0]
-    stacked = jnp.concatenate([message[:rows] for message in messages], axis=0)
+def add_kernel(scale, left, right, out):
+    out[...] = ((wide(left[...]) + wide(right[...])) * scale).astype(out.dtype)
+
+
+def add(left, right, dtype=NARROW, scale=1.0, after=()):
+    (out,) = call(
+        functools.partial(add_kernel, scale), [(left.shape, dtype)], [VMEM] * 2, after=after
+    )(left, right)
+    return out
+
+
+def fold(pieces, distance):
+    stay = [piece for d, piece in enumerate(pieces) if not d & distance]
+    return stay, jnp.concatenate([piece for d, piece in enumerate(pieces) if d & distance], axis=0)
+
+
+def backward_kernel(n, n_out, matrix, left, right, *refs):
+    messages, (stay, send, summed) = refs[:n], refs[n:]
+    rows = messages[0].shape[0]
+    stacked = jnp.concatenate([message[...] for message in messages], axis=0)
     product = dot(matrix[...], stacked)
-    own[...] = product[:rows]
-    term = tree([wide(message[rows:]) for message in messages]).astype(kept.dtype)
-    kept[...] = term
-    for d, send in enumerate(sends, 1):
-        send[:rows] = product[d * rows : (d + 1) * rows].astype(send.dtype)
-        send[rows:] = term
-
-
-def term_kernel(scale, kept, *refs):
-    *messages, half = refs
-    rows = messages[0].shape[0] - kept.shape[0]
-    half[...] = tree([wide(kept[...])] + [wide(message[rows:]) for message in messages]) * scale
-
-
-def feature_kernel(own, *refs):
-    *messages, out = refs
-    rows = own.shape[0]
-    out[...] = tree([own[...]] + [wide(message[:rows]) for message in messages]).astype(out.dtype)
+    kept, going = fold([product[d * rows : (d + 1) * rows] for d in range(n_out)], 1)
+    stay[...] = jnp.concatenate(kept, axis=0)
+    send[...] = going.astype(send.dtype)
+    summed[...] = (wide(left[...]) + wide(right[...])).astype(summed.dtype)
+
+
+def fold_kernel(rows, kept, came, stay, send):
+    total = kept[...] + wide(came[...])
+    pieces = [total[k : k + rows] for k in range(0, total.shape[0], rows)]
+    left, going = fold(pieces, 1)
+    stay[...] = jnp.concatenate(left, axis=0)
+    send[...] = going.astype(send.dtype)
 
 
 def join_kernel(mine, other, out):
     half = mine.shape[1]
-    odd = lax.rem(lax.axis_index("col"), 2) == 1
+    odd = lax.rem(lax.axis_index("row"), 2) == 1
     out[:, :half] = jnp.where(odd, other[...], mine[...])
     out[:, half:] = jnp.where(odd, mine[...], other[...])
 
@@ -168,7 +187,7 @@
     down, across = n_col * nodes, n_row * nodes
     dense_bytes = 2 * down * across
 
-    gathered = [swap(features, "row", d) for d in range(n_row - 1, 0, -1)][::-1]
+    gathered = gather(features, "row")
     (near,) = call(
         functools.partial(dense_kernel, nodes // side),
         [((down, across), NARROW)],
@@ -189,7 +208,7 @@
         [VMEM] * (1 + n_row),
         flops=2 * down * across * width,
         need=2 * dense_bytes,
-    )(near, features, *gathered)
+    )(near, *gathered)
     parts = [swap(sends[d - 1], "col", d) for d in range(n_col - 1, 0, -1)][::-1]
     (far,) = call(
         functools.partial(turn_kernel, side),
@@ -198,35 +217,51 @@
         need=3 * dense_bytes,
     )(near)
 
-    message = ((nodes + width, width), NARROW)
-    same, other, pre = call(
+    square = (width, half)
+    back, pre, term, other = call(
         layer_kernel,
-        [message, message, ((nodes, hidden), jnp.float32)],
+        [
+            ((nodes, width), NARROW),
+            ((nodes, hidden), jnp.float32),
+            (square, jnp.float32),
+            (square, NARROW),
+        ],
         [VMEM] * (n_col + 2),
         flops=14 * nodes * width * hidden,
         after=[far],
     )(own, *parts, weight, cotangent)
-    spread = [swap((same, other)[d % 2], "col", d) for d in range(n_col - 1, 0, -1)][::-1]
+    spread = gather(back, "col")
     (act,) = call(act_kernel, [((nodes, hidden), NARROW)], [VMEM])(pre)
 
-    own, kept, *sends = call(
-        functools.partial(backward_kernel, n_col),
-        [((nodes, width), jnp.float32), ((width, half), NARROW)] + [message] * (n_row - 1),
-        [VMEM] * (1 + n_col),
+    term = add(term, swap(other, "row", 1))
+    *early, last = bits(n_row)[1:]
+    for bit in early:
+        term = add(term, swap(term, "row", bit))
+
+    pieces = n_row // 2
+    stay, send, term = call(
+        functools.partial(backward_kernel, n_col, n_row),
+        [((pieces * nodes, width), jnp.float32), ((pieces * nodes, width), NARROW), (square, NARROW)],
+        [VMEM] * (3 + n_col),
         flops=2 * down * across * width,
         need=2 * dense_bytes,
-    )(far, same, *spread)
-    parts = [swap(sends[d - 1], "row", d) for d in range(n_row - 1, 0, -1)][::-1]
-
+    )(far, term, swap(term, "row", last), *spread)
+
+    for bit in bits(n_row)[1:]:
+        pieces //= 2
+        shape = (pieces * nodes, width)
+        stay, send = call(
+            functools.partial(fold_kernel, nodes), [(shape, jnp.float32), (shape, NARROW)], [VMEM] * 2
+        )(stay, swap(send, "row", bit // 2))
+    grad_features = add(stay, swap(send, "row", n_row // 2))
+
+    *early, last = bits(n_col)
+    for bit in early:
+        term = add(term, swap(term, "col", bit), after=[stay])
     scale = float(nodes * n_row * n_col) ** -0.5
-    (mine,) = call(
-        functools.partial(term_kernel, scale), [((width, half), jnp.float32)], [VMEM] * n_row
-    )(kept, *parts)
-    (grad_features,) = call(feature_kernel, [((nodes, width), NARROW)], [VMEM] * n_row)(
-        own, *parts
-    )
+    mine = add(term, swap(term, "col", last), jnp.float32, scale)
     (grad_weight,) = call(join_kernel, [((width, hidden), jnp.float32)], [VMEM] * 2)(
-        mine, swap(mine, "col", 1)
+        mine, swap(mine, "row", 1)
     )
     return act, grad_features, grad_weight
 

time: 35.9 us -> 43.1 us (1.20)
  waiting for transfers between devices: 15.3 us -> 23.8 us
  starting transfers between devices: 14.1 us -> 12.6 us
    ppermute x13 -> x16, waiting for transfers between devices: 15.3 us -> 23.8 us  [swap(): return lax.ppermute(value, axis, [(s, s ^ distance) for s in range(n)])]
    ppermute x13 -> x16, starting transfers between devices: 14.1 us -> 12.6 us  [swap(): return lax.ppermute(value, axis, [(s, s ^ distance) for s in range(n)])]
    pallas_call x4 -> x7, Pallas kernels: 1.35 us -> 1.36 us  [the longest x4 0.66 us: add(): call(functools.partial(add_kernel, scale), [(left.shape, dtype)], [VMEM]...]
  transfers between devices with their start and end apart: 13 -> 16, of which waited for: 8 -> 11; matrix products, arithmetic and copies ran while one was open for 0% -> 0% of each run, Pallas kernels for 6% -> 5%
where the time goes in v4:
time: 43.1 us; the launch traced here: 42.8 us
  waiting for transfers between devices  23.8 us (55%)
  starting transfers between devices  12.6 us (29%)
  Pallas kernels  4.02 us (9%)
  between operations  1.45 us (3%)
  local copies, waits for them, and re-layouts  1 us (2%)
    ppermute x16, waiting for transfers between devices, swap(): return lax.ppermute(value, axis, [(s, s ^ distance) for s in range(n)])  23.8 us
    ppermute x16, starting transfers between devices, swap(): return lax.ppermute(value, axis, [(s, s ^ distance) for s in range(n)])  12.6 us
    unnamed x12, local copies, waits for them, and re-layouts  1 us
  transfers between devices with their start and end apart: 16, of which 11 were waited for; matrix products, arithmetic and copies ran while one was open for 0% of the time, Pallas kernels for 5%

profile of v4, /device:TPU:0, one launch (start us, length us, event | category | flops | bytes accessed | tf_op | source)
XLA Modules:
  0.0 42.8 jit_solution(14549312878807107226)
XLA Ops:
  0.6 0.0 copy-start.4
  0.6 0.0 copy-start.5
  0.7 3.0 %collective-permute-start.1 = (bf16[128,128]{1,0:T(8,128)(2,1)}, bf16[128,128]{1,0:T(8,128)(2,1)S(1)}, u32[]{:S(2)}, u32[]{:S(2)}) collective-permute-start(bf16[128,128]{1,0:T(8,128)(2,1)} %refs_0_.1), channel_id=1, source_target_pairs={{0,8},{4,12},{8,0},{12,4},{1,9},{5,13},{9,1},{13,5},{2,10},{6,14},... | collective-permute-start | bytes 98312 | tf_op jit(solution)/shard_map/ppermute | solution.py:34
  3.7 0.0 collective-permute-start
  3.7 2.1 %collective-permute-done.1.refs_2_ = bf16[128,128]{1,0:T(8,128)(2,1)S(1)} collective-permute-done((bf16[128,128]{1,0:T(8,128)(2,1)}, bf16[128,128]{1,0:T(8,128)(2,1)S(1)}, u32[]{:S(2)}, u32[]{:S(2)}) %collective-permute-start.1) | collective-permute-done | bytes 32800 | tf_op jit(solution)/shard_map/ppermute | solution.py:34
  5.8 0.0 collective-permute-start.2
  6.4 0.0 copy-done.4
  6.4 0.0 copy-done.5
  6.4 0.0 copy-start
  6.4 0.9 %copy-done = bf16[1,1,8,128,128]{4,3,2,1,0:T(8,128)(2,1)S(1)} copy-done((bf16[1,1,8,128,128]{4,3,2,1,0:T(8,128)(2,1)S(1)}, bf16[1,1,8,128,128]{4,3,2,1,0:T(8,128)(2,1)}, u32[]{:S(2)}) %copy-start) | copy-done | bytes 262168
  7.4 0.7 %shard_map.94.near.matrix = bf16[512,512]{1,0:T(8,128)(2,1)S(1)} custom-call(bf16[1,1,8,128,128]{4,3,2,1,0:T(8,128)(2,1)S(1)} %copy-done, s32[1,1,8]{2,1,0:T(1,128)S(1)} %copy-done.4, s32[1,1,8]{2,1,0:T(1,128)S(1)} %copy-done.5, s32[1,1]{1,0:T(1,128)S(6)} %copy.10.count_in), custom_call_target="tpu_custom_call" | custom-call | bytes 1048576 | tf_op jit(solution)/shard_map/pallas_call | solution.py:191
  8.1 0.0 collective-permute-done.refs_1_
  8.1 0.0 collective-permute-done.2.refs_3_
  8.1 0.0 copy-done.3
  8.1 0.3 shard_map.96
  8.4 2.2 %collective-permute-start.3 = (bf16[128,128]{1,0:T(8,128)(2,1)S(1)}, bf16[128,128]{1,0:T(8,128)(2,1)S(1)}, u32[]{:S(2)}, u32[]{:S(2)}) collective-permute-start(bf16[128,128]{1,0:T(8,128)(2,1)S(1)} %get-tuple-element.17), channel_id=1, source_target_pairs={{0,1},{1,0},{2,3},{3,2},{4,5},{5,4},{6,7},{7,6},{8,9},{9,8},{10,11... | collective-permute-start | bytes 98312 | tf_op jit(solution)/shard_map/ppermute | solution.py:34
  10.6 2.6 %collective-permute-start.4 = (bf16[128,128]{1,0:T(8,128)(2,1)S(1)}, bf16[128,128]{1,0:T(8,128)(2,1)S(1)}, u32[]{:S(2)}, u32[]{:S(2)}) collective-permute-start(bf16[128,128]{1,0:T(8,128)(2,1)S(1)} %get-tuple-element.18), channel_id=1, source_target_pairs={{0,2},{1,3},{2,0},{3,1},{4,6},{5,7},{6,4},{7,5},{8,10},{9,11},{10,... | collective-permute-start | bytes 98312 | tf_op jit(solution)/shard_map/ppermute | solution.py:34
  13.2 0.0 collective-permute-start.5
  13.2 0.3 shard_map.95.refs_0_.matrix
  13.6 0.0 collective-permute-done.3.refs_2_
  13.6 2.4 %collective-permute-done.4.refs_3_ = bf16[128,128]{1,0:T(8,128)(2,1)S(1)} collective-permute-done((bf16[128,128]{1,0:T(8,128)(2,1)S(1)}, bf16[128,128]{1,0:T(8,128)(2,1)S(1)}, u32[]{:S(2)}, u32[]{:S(2)}) %collective-permute-start.4) | collective-permute-done | bytes 32800 | tf_op jit(solution)/shard_map/ppermute | solution.py:34
  16.0 2.9 %collective-permute-done.5.refs_4_ = bf16[128,128]{1,0:T(8,128)(2,1)S(1)} collective-permute-done((bf16[128,128]{1,0:T(8,128)(2,1)S(1)}, bf16[128,128]{1,0:T(8,128)(2,1)S(1)}, u32[]{:S(2)}, u32[]{:S(2)}) %collective-permute-start.5) | collective-permute-done | bytes 32800 | tf_op jit(solution)/shard_map/ppermute | solution.py:34
  18.9 0.0 copy-done.1
  18.9 0.4 shard_map.97
  19.3 0.1 collective-permute-start.6
  19.4 0.1 collective-permute-start.9
  19.5 1.0 %collective-permute-start.8 = (bf16[128,128]{1,0:T(8,128)(2,1)S(1)}, bf16[128,128]{1,0:T(8,128)(2,1)S(1)}, u32[]{:S(2)}, u32[]{:S(2)}) collective-permute-start(bf16[128,128]{1,0:T(8,128)(2,1)S(1)} %get-tuple-element.23.refs_0_), channel_id=1, source_target_pairs={{0,1},{1,0},{2,3},{3,2},{4,5},{5,4},{6,7},{7,6},{8,9},{9,8},{10,11... | collective-permute-start | bytes 98312 | tf_op jit(solution)/shard_map/ppermute | solution.py:34
  20.4 0.2 collective-permute-done.6.right
  20.6 1.6 %collective-permute-start.7 = (bf16[128,128]{1,0:T(8,128)(2,1)S(1)}, bf16[128,128]{1,0:T(8,128)(2,1)S(1)}, u32[]{:S(2)}, u32[]{:S(2)}) collective-permute-start(bf16[128,128]{1,0:T(8,128)(2,1)S(1)} %shard_map.99.left), channel_id=1, source_target_pairs={{0,8},{4,12},{8,0},{12,4},{1,9},{5,13},{9,1},{13,5},{2,10},{6,14},... | collective-permute-start | bytes 98312 | tf_op jit(solution)/shard_map/ppermute | solution.py:34
  22.2 2.1 %collective-permute-done.9.refs_2_ = bf16[128,128]{1,0:T(8,128)(2,1)S(1)} collective-permute-done((bf16[128,128]{1,0:T(8,128)(2,1)S(1)}, bf16[128,128]{1,0:T(8,128)(2,1)S(1)}, u32[]{:S(2)}, u32[]{:S(2)}) %collective-permute-start.9) | collective-permute-done | bytes 32800 | tf_op jit(solution)/shard_map/ppermute | solution.py:34
  24.3 0.0 collective-permute-start.10
  24.3 0.0 collective-permute-done.8.refs_1_
  24.3 0.3 collective-permute-done.7.right
  24.6 3.6 %collective-permute-done.10.refs_3_ = bf16[128,128]{1,0:T(8,128)(2,1)S(1)} collective-permute-done((bf16[128,128]{1,0:T(8,128)(2,1)S(1)}, bf16[128,128]{1,0:T(8,128)(2,1)S(1)}, u32[]{:S(2)}, u32[]{:S(2)}) %collective-permute-start.10) | collective-permute-done | bytes 32800 | tf_op jit(solution)/shard_map/ppermute | solution.py:34
  28.2 0.3 shard_map.100
  28.5 0.1 collective-permute-start.11
  28.6 0.1 collective-permute-start.13
  28.7 1.2 %collective-permute-done.11.came = bf16[256,128]{1,0:T(8,128)(2,1)S(1)} collective-permute-done((bf16[256,128]{1,0:T(8,128)(2,1)S(1)}, bf16[256,128]{1,0:T(8,128)(2,1)S(1)}, u32[]{:S(2)}, u32[]{:S(2)}) %collective-permute-start.11) | collective-permute-done | bytes 65568 | tf_op jit(solution)/shard_map/ppermute | solution.py:34
  29.9 2.7 %collective-permute-done.13.refs_2_ = bf16[128,128]{1,0:T(8,128)(2,1)S(1)} collective-permute-done((bf16[128,128]{1,0:T(8,128)(2,1)S(1)}, bf16[128,128]{1,0:T(8,128)(2,1)S(1)}, u32[]{:S(2)}, u32[]{:S(2)}) %collective-permute-start.13) | collective-permute-done | bytes 32800 | tf_op jit(solution)/shard_map/ppermute | solution.py:34
  32.6 0.4 collective-permute-start.14
  33.0 4.5 %collective-permute-done.14.right = bf16[128,128]{1,0:T(8,128)(2,1)S(1)} collective-permute-done((bf16[128,128]{1,0:T(8,128)(2,1)S(1)}, bf16[128,128]{1,0:T(8,128)(2,1)S(1)}, u32[]{:S(2)}, u32[]{:S(2)}) %collective-permute-start.14) | collective-permute-done | bytes 32800 | tf_op jit(solution)/shard_map/ppermute | solution.py:34
  37.5 0.1 collective-permute-start.15
  37.6 1.6 %collective-permute-start.12 = (bf16[128,128]{1,0:T(8,128)(2,1)S(1)}, bf16[128,128]{1,0:T(8,128)(2,1)S(1)}, u32[]{:S(2)}, u32[]{:S(2)}) collective-permute-start(bf16[128,128]{1,0:T(8,128)(2,1)S(1)} %get-tuple-element.27), channel_id=1, source_target_pairs={{0,8},{4,12},{8,0},{12,4},{1,9},{5,13},{9,1},{13,5},{2,10},{6,14},... | collective-permute-start | bytes 98312 | tf_op jit(solution)/shard_map/ppermute | solution.py:34
  39.1 0.7 %shard_map.98 = bf16[128,256]{1,0:T(8,128)(2,1)} custom-call(f32[128,256]{1,0:T(8,128)S(1)} %get-tuple-element.20.pre), custom_call_target="tpu_custom_call" | custom-call | tf_op jit(solution)/shard_map/pallas_call | solution.py:234
  39.8 1.8 %collective-permute-done.12.right = bf16[128,128]{1,0:T(8,128)(2,1)S(1)} collective-permute-done((bf16[128,128]{1,0:T(8,128)(2,1)S(1)}, bf16[128,128]{1,0:T(8,128)(2,1)S(1)}, u32[]{:S(2)}, u32[]{:S(2)}) %collective-permute-start.12) | collective-permute-done | bytes 32800 | tf_op jit(solution)/shard_map/ppermute | solution.py:34
  41.5 0.6 %shard_map.102 = bf16[128,128]{1,0:T(8,128)(2,1)} custom-call(f32[128,128]{1,0:T(8,128)S(1)} %get-tuple-element.26.left.refs_0_, bf16[128,128]{1,0:T(8,128)(2,1)S(1)} %collective-permute-done.12.right), custom_call_target="tpu_custom_call" | custom-call | tf_op jit(solution)/shard_map/pallas_call | solution.py:144
  42.2 0.0 collective-permute-done.15.other
  42.2 0.7 %shard_map.105 = f32[128,256]{1,0:T(8,128)} custom-call(f32[128,128]{1,0:T(8,128)S(1)} %shard_map.104.mine, f32[128,128]{1,0:T(8,128)S(1)} %collective-permute-done.15.other), custom_call_target="tpu_custom_call" | custom-call | tf_op jit(solution)/shard_map/pallas_call | solution.py:263
  (8 shorter events, 0.1 us)
Async XLA Ops:
  0.6 5.8 %copy-start.4 = (s32[1,1,8]{2,1,0:T(1,128)S(1)}, s32[1,1,8]{2,1,0:T(1,128)}, u32[]{:S(2)}) copy-start(s32[1,1,8]{2,1,0:T(1,128)} %rows_in.1) | copy-start | bytes 100
  0.6 5.8 %copy-start.5 = (s32[1,1,8]{2,1,0:T(1,128)S(1)}, s32[1,1,8]{2,1,0:T(1,128)}, u32[]{:S(2)}) copy-start(s32[1,1,8]{2,1,0:T(1,128)} %cols_in.1) | copy-start | bytes 100
  0.7 5.1 %collective-permute-start.1 = (bf16[128,128]{1,0:T(8,128)(2,1)}, bf16[128,128]{1,0:T(8,128)(2,1)S(1)}, u32[]{:S(2)}, u32[]{:S(2)}) collective-permute-start(bf16[128,128]{1,0:T(8,128)(2,1)} %refs_0_.1), channel_id=1, source_target_pairs={{0,8},{4,12},{8,0},{12,4},{1,9},{5,13},{9,1},{13,5},{2,10},{6,14},... | collective-permute-start | bytes 98312 | tf_op jit(solution)/shard_map/ppermute | solution.py:34
  3.7 4.4 %collective-permute-start = (bf16[128,128]{1,0:T(8,128)(2,1)}, bf16[128,128]{1,0:T(8,128)(2,1)S(1)}, u32[]{:S(2)}, u32[]{:S(2)}) collective-permute-start(bf16[128,128]{1,0:T(8,128)(2,1)} %refs_0_.1), channel_id=1, source_target_pairs={{0,4},{4,0},{8,12},{12,8},{1,5},{5,1},{9,13},{13,9},{2,6},{6,2},{1... | collective-permute-start | bytes 98312 | tf_op jit(solution)/shard_map/ppermute | solution.py:34
  5.8 2.3 %collective-permute-start.2 = (bf16[128,128]{1,0:T(8,128)(2,1)S(1)}, bf16[128,128]{1,0:T(8,128)(2,1)S(1)}, u32[]{:S(2)}, u32[]{:S(2)}) collective-permute-start(bf16[128,128]{1,0:T(8,128)(2,1)S(1)} %collective-permute-done.1.refs_2_), channel_id=1, source_target_pairs={{0,4},{4,0},{8,12},{12,8},{1,5},{5,1},{9,13},{13,9},{2,6},{6,2},{1... | collective-permute-start | bytes 98312 | tf_op jit(solution)/shard_map/ppermute | solution.py:34
  6.4 1.0 %copy-start = (bf16[1,1,8,128,128]{4,3,2,1,0:T(8,128)(2,1)S(1)}, bf16[1,1,8,128,128]{4,3,2,1,0:T(8,128)(2,1)}, u32[]{:S(2)}) copy-start(bf16[1,1,8,128,128]{4,3,2,1,0:T(8,128)(2,1)} %vals_in.1) | copy-start | bytes 786436
  7.4 0.8 %copy-start.3 = (bf16[128,128]{1,0:T(8,128)(2,1)S(1)}, bf16[128,128]{1,0:T(8,128)(2,1)}, u32[]{:S(2)}) copy-start(bf16[128,128]{1,0:T(8,128)(2,1)} %refs_0_.1) | copy-start | bytes 98308
  8.4 5.1 %collective-permute-start.3 = (bf16[128,128]{1,0:T(8,128)(2,1)S(1)}, bf16[128,128]{1,0:T(8,128)(2,1)S(1)}, u32[]{:S(2)}, u32[]{:S(2)}) collective-permute-start(bf16[128,128]{1,0:T(8,128)(2,1)S(1)} %get-tuple-element.17), channel_id=1, source_target_pairs={{0,1},{1,0},{2,3},{3,2},{4,5},{5,4},{6,7},{7,6},{8,9},{9,8},{10,11... | collective-permute-start | bytes 98312 | tf_op jit(solution)/shard_map/ppermute | solution.py:34
  10.6 5.4 %collective-permute-start.4 = (bf16[128,128]{1,0:T(8,128)(2,1)S(1)}, bf16[128,128]{1,0:T(8,128)(2,1)S(1)}, u32[]{:S(2)}, u32[]{:S(2)}) collective-permute-start(bf16[128,128]{1,0:T(8,128)(2,1)S(1)} %get-tuple-element.18), channel_id=1, source_target_pairs={{0,2},{1,3},{2,0},{3,1},{4,6},{5,7},{6,4},{7,5},{8,10},{9,11},{10,... | collective-permute-start | bytes 98312 | tf_op jit(solution)/shard_map/ppermute | solution.py:34
  13.2 5.7 %copy-start.1 = (bf16[128,256]{1,0:T(8,128)(2,1)S(1)}, bf16[128,256]{1,0:T(8,128)(2,1)}, u32[]{:S(2)}) copy-start(bf16[128,256]{1,0:T(8,128)(2,1)} %refs_5_.1) | copy-start | bytes 196612
  13.2 5.7 %copy-start.2 = (bf16[128,256]{1,0:T(8,128)(2,1)S(1)}, bf16[128,256]{1,0:T(8,128)(2,1)}, u32[]{:S(2)}) copy-start(bf16[128,256]{1,0:T(8,128)(2,1)} %refs_6_.1) | copy-start | bytes 196612
  13.2 5.7 %collective-permute-start.5 = (bf16[128,128]{1,0:T(8,128)(2,1)S(1)}, bf16[128,128]{1,0:T(8,128)(2,1)S(1)}, u32[]{:S(2)}, u32[]{:S(2)}) collective-permute-start(bf16[128,128]{1,0:T(8,128)(2,1)S(1)} %get-tuple-element.19), channel_id=1, source_target_pairs={{0,3},{1,2},{2,1},{3,0},{4,7},{5,6},{6,5},{7,4},{8,11},{9,10},{10,... | collective-permute-start | bytes 98312 | tf_op jit(solution)/shard_map/ppermute | solution.py:34
  19.3 1.3 %collective-permute-start.6 = (bf16[128,128]{1,0:T(8,128)(2,1)S(1)}, bf16[128,128]{1,0:T(8,128)(2,1)S(1)}, u32[]{:S(2)}, u32[]{:S(2)}) collective-permute-start(bf16[128,128]{1,0:T(8,128)(2,1)S(1)} %get-tuple-element.22), channel_id=1, source_target_pairs={{0,4},{4,0},{8,12},{12,8},{1,5},{5,1},{9,13},{13,9},{2,6},{6,2},{1... | collective-permute-start | bytes 98312 | tf_op jit(solution)/shard_map/ppermute | solution.py:34
  19.4 4.9 %collective-permute-start.9 = (bf16[128,128]{1,0:T(8,128)(2,1)S(1)}, bf16[128,128]{1,0:T(8,128)(2,1)S(1)}, u32[]{:S(2)}, u32[]{:S(2)}) collective-permute-start(bf16[128,128]{1,0:T(8,128)(2,1)S(1)} %get-tuple-element.23.refs_0_), channel_id=1, source_target_pairs={{0,2},{1,3},{2,0},{3,1},{4,6},{5,7},{6,4},{7,5},{8,10},{9,11},{10,... | collective-permute-start | bytes 98312 | tf_op jit(solution)/shard_map/ppermute | solution.py:34
  19.5 4.8 %collective-permute-start.8 = (bf16[128,128]{1,0:T(8,128)(2,1)S(1)}, bf16[128,128]{1,0:T(8,128)(2,1)S(1)}, u32[]{:S(2)}, u32[]{:S(2)}) collective-permute-start(bf16[128,128]{1,0:T(8,128)(2,1)S(1)} %get-tuple-element.23.refs_0_), channel_id=1, source_target_pairs={{0,1},{1,0},{2,3},{3,2},{4,5},{5,4},{6,7},{7,6},{8,9},{9,8},{10,11... | collective-permute-start | bytes 98312 | tf_op jit(solution)/shard_map/ppermute | solution.py:34
  20.6 4.0 %collective-permute-start.7 = (bf16[128,128]{1,0:T(8,128)(2,1)S(1)}, bf16[128,128]{1,0:T(8,128)(2,1)S(1)}, u32[]{:S(2)}, u32[]{:S(2)}) collective-permute-start(bf16[128,128]{1,0:T(8,128)(2,1)S(1)} %shard_map.99.left), channel_id=1, source_target_pairs={{0,8},{4,12},{8,0},{12,4},{1,9},{5,13},{9,1},{13,5},{2,10},{6,14},... | collective-permute-start | bytes 98312 | tf_op jit(solution)/shard_map/ppermute | solution.py:34
  24.3 3.9 %collective-permute-start.10 = (bf16[128,128]{1,0:T(8,128)(2,1)S(1)}, bf16[128,128]{1,0:T(8,128)(2,1)S(1)}, u32[]{:S(2)}, u32[]{:S(2)}) collective-permute-start(bf16[128,128]{1,0:T(8,128)(2,1)S(1)} %collective-permute-done.9.refs_2_), channel_id=1, source_target_pairs={{0,1},{1,0},{2,3},{3,2},{4,5},{5,4},{6,7},{7,6},{8,9},{9,8},{10,11... | collective-permute-start | bytes 98312 | tf_op jit(solution)/shard_map/ppermute | solution.py:34
  28.5 1.3 %collective-permute-start.11 = (bf16[256,128]{1,0:T(8,128)(2,1)S(1)}, bf16[256,128]{1,0:T(8,128)(2,1)S(1)}, u32[]{:S(2)}, u32[]{:S(2)}) collective-permute-start(bf16[256,128]{1,0:T(8,128)(2,1)S(1)} %get-tuple-element.25), channel_id=1, source_target_pairs={{0,4},{4,0},{8,12},{12,8},{1,5},{5,1},{9,13},{13,9},{2,6},{6,2},{1... | collective-permute-start | bytes 196616 | tf_op jit(solution)/shard_map/ppermute | solution.py:34
  28.6 4.0 %collective-permute-start.13 = (bf16[128,128]{1,0:T(8,128)(2,1)S(1)}, bf16[128,128]{1,0:T(8,128)(2,1)S(1)}, u32[]{:S(2)}, u32[]{:S(2)}) collective-permute-start(bf16[128,128]{1,0:T(8,128)(2,1)S(1)} %get-tuple-element.28.refs_1_), channel_id=1, source_target_pairs={{0,1},{1,0},{2,3},{3,2},{4,5},{5,4},{6,7},{7,6},{8,9},{9,8},{10,11... | collective-permute-start | bytes 98312 | tf_op jit(solution)/shard_map/ppermute | solution.py:34
  32.6 4.9 %collective-permute-start.14 = (bf16[128,128]{1,0:T(8,128)(2,1)S(1)}, bf16[128,128]{1,0:T(8,128)(2,1)S(1)}, u32[]{:S(2)}, u32[]{:S(2)}) collective-permute-start(bf16[128,128]{1,0:T(8,128)(2,1)S(1)} %shard_map.103.left), channel_id=1, source_target_pairs={{0,2},{1,3},{2,0},{3,1},{4,6},{5,7},{6,4},{7,5},{8,10},{9,11},{10,... | collective-permute-start | bytes 98312 | tf_op jit(solution)/shard_map/ppermute | solution.py:34
  37.5 4.7 %collective-permute-start.15 = (f32[128,128]{1,0:T(8,128)S(1)}, f32[128,128]{1,0:T(8,128)S(1)}, u32[]{:S(2)}, u32[]{:S(2)}) collective-permute-start(f32[128,128]{1,0:T(8,128)S(1)} %shard_map.104.mine), channel_id=1, source_target_pairs={{0,4},{4,0},{8,12},{12,8},{1,5},{5,1},{9,13},{13,9},{2,6},{6,2},{1... | collective-permute-start | bytes 196616 | tf_op jit(solution)/shard_map/ppermute | solution.py:34
  37.6 4.0 %collective-permute-start.12 = (bf16[128,128]{1,0:T(8,128)(2,1)S(1)}, bf16[128,128]{1,0:T(8,128)(2,1)S(1)}, u32[]{:S(2)}, u32[]{:S(2)}) collective-permute-start(bf16[128,128]{1,0:T(8,128)(2,1)S(1)} %get-tuple-element.27), channel_id=1, source_target_pairs={{0,8},{4,12},{8,0},{12,4},{1,9},{5,13},{9,1},{13,5},{2,10},{6,14},... | collective-permute-start | bytes 98312 | tf_op jit(solution)/shard_map/ppermute | solution.py:34

commit v5 on v3

--- a/solution.py
+++ b/solution.py
@@ -9,7 +9,6 @@
 
 VMEM = pl.BlockSpec(memory_space=pltpu.VMEM)
 ANY = pl.BlockSpec(memory_space=pl.ANY)
-HBM = pl.BlockSpec(memory_space=pltpu.HBM)
 LEAST = 16 * 1024 * 1024
 NARROW = jnp.bfloat16
 
@@ -29,9 +28,17 @@
     return functools.partial(run, *after)
 
 
-def swap(value, axis, distance):
+def exchange(sends, axis, ahead):
     n = lax.axis_size(axis)
-    return lax.ppermute(value, axis, [(s, s ^ distance) for s in range(n)])
+    return [
+        lax.ppermute(send, axis, [(s, (s + (d if ahead else -d)) % n) for s in range(n)])
+        for d, send in enumerate(sends, 1)
+    ]
+
+
+def neighbour(value, axis):
+    n = lax.axis_size(axis)
+    return lax.ppermute(value, axis, [(s, s ^ 1) for s in range(n)])
 
 
 def wide(value):
@@ -47,12 +54,10 @@
     return lax.dot_general(left, right, (dims, ((), ())), preferred_element_type=jnp.float32)
 
 
-def dense_kernel(piece, vals_in, rows_in, cols_in, count_in, near, vals, rows, cols, count, sems):
+def dense_kernel(n_row, n_col, piece, vals, rows_in, cols_in, count_in, near, rows, cols, count, sems):
     copies = [
         pltpu.make_async_copy(source, target, sems.at[k])
-        for k, (source, target) in enumerate(
-            ((rows_in, rows), (cols_in, cols), (count_in, count), (vals_in, vals))
-        )
+        for k, (source, target) in enumerate(((rows_in, rows), (cols_in, cols), (count_in, count)))
     ]
     for copy in copies:
         copy.start()
@@ -64,8 +69,8 @@
 
     def add(t, _):
         row, col = rows[0, 0, t], cols[0, 0, t]
-        row = ((row // piece) ^ my_col) * piece + lax.rem(row, piece)
-        col = ((col // piece) ^ my_row) * piece + lax.rem(col, piece)
+        row = lax.rem(row // piece - my_col + n_col, n_col) * piece + lax.rem(row, piece)
+        col = lax.rem(col // piece - my_row + n_row, n_row) * piece + lax.rem(col, piece)
         down = pl.ds(pl.multiple_of(row * side, side), side)
         across = pl.ds(pl.multiple_of(col * side, side), side)
         near[down, across] = vals[0, 0, t]
@@ -85,7 +90,8 @@
 
 def tree(terms):
     while len(terms) > 1:
-        terms = [left + right for left, right in zip(terms[::2], terms[1::2])]
+        middle = len(terms) // 2
+        terms = [left + right for left, right in zip(terms[:middle], terms[middle:])]
     return terms[0]
 
 
@@ -143,7 +149,8 @@
 def term_kernel(scale, kept, *refs):
     *messages, half = refs
     rows = messages[0].shape[0] - kept.shape[0]
-    half[...] = tree([wide(kept[...])] + [wide(message[rows:]) for message in messages]) * scale
+    total = tree([wide(kept[...])] + [wide(message[rows:]) for message in messages])
+    half[...] = (total * scale).astype(half.dtype)
 
 
 def feature_kernel(own, *refs):
@@ -155,8 +162,8 @@
 def join_kernel(mine, other, out):
     half = mine.shape[1]
     odd = lax.rem(lax.axis_index("col"), 2) == 1
-    out[:, :half] = jnp.where(odd, other[...], mine[...])
-    out[:, half:] = jnp.where(odd, mine[...], other[...])
+    out[:, :half] = jnp.where(odd, wide(other[...]), wide(mine[...]))
+    out[:, half:] = jnp.where(odd, wide(mine[...]), wide(other[...]))
 
 
 def per_device(features, weight, cotangent, tile_values, tile_rows, tile_cols, tile_count):
@@ -168,17 +175,16 @@
     down, across = n_col * nodes, n_row * nodes
     dense_bytes = 2 * down * across
 
-    gathered = [swap(features, "row", d) for d in range(n_row - 1, 0, -1)][::-1]
+    gathered = exchange([features] * (n_row - 1), "row", False)
     (near,) = call(
-        functools.partial(dense_kernel, nodes // side),
+        functools.partial(dense_kernel, n_row, n_col, nodes // side),
         [((down, across), NARROW)],
-        [HBM] * 4,
+        [VMEM] * 4,
         scratch=[
-            pltpu.VMEM(tile_values.shape, NARROW),
             pltpu.SMEM(tile_rows.shape, jnp.int32),
             pltpu.SMEM(tile_cols.shape, jnp.int32),
             pltpu.SMEM(tile_count.shape, jnp.int32),
-            pltpu.SemaphoreType.DMA((4,)),
+            pltpu.SemaphoreType.DMA((3,)),
         ],
         need=2 * dense_bytes,
     )(tile_values, tile_rows, tile_cols, tile_count)
@@ -190,7 +196,7 @@
         flops=2 * down * across * width,
         need=2 * dense_bytes,
     )(near, features, *gathered)
-    parts = [swap(sends[d - 1], "col", d) for d in range(n_col - 1, 0, -1)][::-1]
+    parts = exchange(sends, "col", True)
     (far,) = call(
         functools.partial(turn_kernel, side),
         [((across, down), NARROW)],
@@ -206,7 +212,7 @@
         flops=14 * nodes * width * hidden,
         after=[far],
     )(own, *parts, weight, cotangent)
-    spread = [swap((same, other)[d % 2], "col", d) for d in range(n_col - 1, 0, -1)][::-1]
+    spread = exchange([(same, other)[d % 2] for d in range(1, n_col)], "col", False)
     (act,) = call(act_kernel, [((nodes, hidden), NARROW)], [VMEM])(pre)
 
     own, kept, *sends = call(
@@ -216,17 +222,17 @@
         flops=2 * down * across * width,
         need=2 * dense_bytes,
     )(far, same, *spread)
-    parts = [swap(sends[d - 1], "row", d) for d in range(n_row - 1, 0, -1)][::-1]
+    parts = exchange(sends, "row", True)
 
     scale = float(nodes * n_row * n_col) ** -0.5
     (mine,) = call(
-        functools.partial(term_kernel, scale), [((width, half), jnp.float32)], [VMEM] * n_row
+        functools.partial(term_kernel, scale), [((width, half), NARROW)], [VMEM] * n_row
     )(kept, *parts)
     (grad_features,) = call(feature_kernel, [((nodes, width), NARROW)], [VMEM] * n_row)(
         own, *parts
     )
     (grad_weight,) = call(join_kernel, [((width, hidden), jnp.float32)], [VMEM] * 2)(
-        mine, swap(mine, "col", 1)
+        mine, neighbour(mine, "col")
     )
     return act, grad_features, grad_weight
 

time: 35.9 us -> 34.4 us (0.958)
  waiting for transfers between devices: 15.3 us -> 10.4 us
  starting transfers between devices: 14.1 us -> 17.5 us
    ppermute x13, waiting for transfers between devices: 15.3 us -> 10.4 us  [the longest x12 8.33 us: exchange(): lax.ppermute(send, axis, [(s, (s + (d if ahead else -d)) % n) for s in ra...]
    ppermute x13, starting transfers between devices: 14.1 us -> 17.5 us  [the longest x12 16.8 us: exchange(): lax.ppermute(send, axis, [(s, (s + (d if ahead else -d)) % n) for s in ra...]
  transfers between devices with their start and end apart: 13 -> 13, of which waited for: 8 -> 8; matrix products, arithmetic and copies ran while one was open for 0% -> 0% of each run, Pallas kernels for 6% -> 7%
where the time goes in v5:
time: 34.4 us; the launch traced here: 34.3 us
  starting transfers between devices  17.5 us (51%)
  waiting for transfers between devices  10.4 us (30%)
  Pallas kernels  4.04 us (12%)
  between operations  1.4 us (4%)
  local copies, waits for them, and re-layouts  0.96 us (3%)
    ppermute x12, starting transfers between devices, exchange(): lax.ppermute(send, axis, [(s, (s + (d if ahead else -d)) % n) for s in ra...  16.8 us
    ppermute x12, waiting for transfers between devices, exchange(): lax.ppermute(send, axis, [(s, (s + (d if ahead else -d)) % n) for s in ra...  8.33 us
    ppermute x1, waiting for transfers between devices, neighbour(): return lax.ppermute(value, axis, [(s, s ^ 1) for s in range(n)])  2.05 us
    unnamed x12, local copies, waits for them, and re-layouts  0.96 us
    pallas_call x1, Pallas kernels, per_device(): call(functools.partial(dense_kernel, n_row, n_col, nodes // side), [((dow...  0.72 us
    ppermute x1, starting transfers between devices, neighbour(): return lax.ppermute(value, axis, [(s, s ^ 1) for s in range(n)])  0.71 us
  transfers between devices with their start and end apart: 13, of which 8 were waited for; matrix products, arithmetic and copies ran while one was open for 0% of the time, Pallas kernels for 7%

profile of v5, /device:TPU:0, one launch (start us, length us, event | category | flops | bytes accessed | tf_op | source)
XLA Modules:
  0.0 34.3 jit_solution(9849289751322210574)
XLA Ops:
  0.6 0.0 copy-start.5
  0.6 0.0 copy-start.4
  0.7 3.0 %collective-permute-start.1 = (bf16[128,128]{1,0:T(8,128)(2,1)}, bf16[128,128]{1,0:T(8,128)(2,1)S(1)}, u32[]{:S(2)}, u32[]{:S(2)}) collective-permute-start(bf16[128,128]{1,0:T(8,128)(2,1)} %refs_0_.1), channel_id=1, source_target_pairs={{0,8},{4,12},{8,0},{12,4},{1,9},{5,13},{9,1},{13,5},{2,10},{6,14},... | collective-permute-start | bytes 98312 | tf_op jit(solution)/shard_map/ppermute | solution.py:34
  3.7 0.0 collective-permute-start
  3.7 0.5 %collective-permute-start.2 = (bf16[128,128]{1,0:T(8,128)(2,1)}, bf16[128,128]{1,0:T(8,128)(2,1)S(1)}, u32[]{:S(2)}, u32[]{:S(2)}) collective-permute-start(bf16[128,128]{1,0:T(8,128)(2,1)} %refs_0_.1), channel_id=1, source_target_pairs={{0,4},{4,8},{8,12},{12,0},{1,5},{5,9},{9,13},{13,1},{2,6},{6,10},{... | collective-permute-start | bytes 98312 | tf_op jit(solution)/shard_map/ppermute | solution.py:34
  4.8 0.0 copy-done.5
  4.8 0.0 copy-done.4
  4.8 0.0 copy-start
  4.8 0.9 %copy-done = bf16[1,1,8,128,128]{4,3,2,1,0:T(8,128)(2,1)S(1)} copy-done((bf16[1,1,8,128,128]{4,3,2,1,0:T(8,128)(2,1)S(1)}, bf16[1,1,8,128,128]{4,3,2,1,0:T(8,128)(2,1)}, u32[]{:S(2)}) %copy-start) | copy-done | bytes 262168
  5.8 0.0 copy-start.3
  5.8 0.7 %shard_map.94.near.matrix = bf16[512,512]{1,0:T(8,128)(2,1)S(1)} custom-call(bf16[1,1,8,128,128]{4,3,2,1,0:T(8,128)(2,1)S(1)} %copy-done, s32[1,1,8]{2,1,0:T(1,128)S(1)} %copy-done.4, s32[1,1,8]{2,1,0:T(1,128)S(1)} %copy-done.5, s32[1,1]{1,0:T(1,128)S(6)} %copy.10.count_in), custom_call_target="tpu_custom_call" | custom-call | bytes 1048576 | tf_op jit(solution)/shard_map/pallas_call | solution.py:179
  6.5 0.0 collective-permute-done.1.refs_2_
  6.5 0.0 collective-permute-done.refs_1_
  6.5 0.7 %collective-permute-done.2.refs_3_ = bf16[128,128]{1,0:T(8,128)(2,1)S(1)} collective-permute-done((bf16[128,128]{1,0:T(8,128)(2,1)}, bf16[128,128]{1,0:T(8,128)(2,1)S(1)}, u32[]{:S(2)}, u32[]{:S(2)}) %collective-permute-start.2) | collective-permute-done | bytes 32800 | tf_op jit(solution)/shard_map/ppermute | solution.py:34
  7.3 0.0 copy-done.3
  7.3 0.3 shard_map.96
  7.6 1.6 %collective-permute-start.3 = (bf16[128,128]{1,0:T(8,128)(2,1)S(1)}, bf16[128,128]{1,0:T(8,128)(2,1)S(1)}, u32[]{:S(2)}, u32[]{:S(2)}) collective-permute-start(bf16[128,128]{1,0:T(8,128)(2,1)S(1)} %get-tuple-element.16), channel_id=1, source_target_pairs={{0,1},{1,2},{2,3},{3,0},{4,5},{5,6},{6,7},{7,4},{8,9},{9,10},{10,1... | collective-permute-start | bytes 98312 | tf_op jit(solution)/shard_map/ppermute | solution.py:34
  9.2 2.6 %collective-permute-start.4 = (bf16[128,128]{1,0:T(8,128)(2,1)S(1)}, bf16[128,128]{1,0:T(8,128)(2,1)S(1)}, u32[]{:S(2)}, u32[]{:S(2)}) collective-permute-start(bf16[128,128]{1,0:T(8,128)(2,1)S(1)} %get-tuple-element.17), channel_id=1, source_target_pairs={{0,2},{1,3},{2,0},{3,1},{4,6},{5,7},{6,4},{7,5},{8,10},{9,11},{10,... | collective-permute-start | bytes 98312 | tf_op jit(solution)/shard_map/ppermute | solution.py:34
  11.8 0.0 copy-start.1
  11.8 0.0 copy-start.2
  11.8 1.3 %collective-permute-start.5 = (bf16[128,128]{1,0:T(8,128)(2,1)S(1)}, bf16[128,128]{1,0:T(8,128)(2,1)S(1)}, u32[]{:S(2)}, u32[]{:S(2)}) collective-permute-start(bf16[128,128]{1,0:T(8,128)(2,1)S(1)} %get-tuple-element.18), channel_id=1, source_target_pairs={{0,3},{1,0},{2,1},{3,2},{4,7},{5,4},{6,5},{7,6},{8,11},{9,8},{10,9... | collective-permute-start | bytes 98312 | tf_op jit(solution)/shard_map/ppermute | solution.py:34
  13.2 0.3 %shard_map.95.refs_0_.matrix = bf16[512,512]{1,0:T(8,128)(2,1)S(1)} custom-call(bf16[512,512]{1,0:T(8,128)(2,1)S(1)} %shard_map.94.near.matrix), custom_call_target="tpu_custom_call" | custom-call | bytes 1572864 | tf_op jit(solution)/shard_map/pallas_call | solution.py:200
  13.5 0.0 collective-permute-done.3.refs_2_
  13.5 1.0 %collective-permute-done.4.refs_3_ = bf16[128,128]{1,0:T(8,128)(2,1)S(1)} collective-permute-done((bf16[128,128]{1,0:T(8,128)(2,1)S(1)}, bf16[128,128]{1,0:T(8,128)(2,1)S(1)}, u32[]{:S(2)}, u32[]{:S(2)}) %collective-permute-start.4) | collective-permute-done | bytes 32800 | tf_op jit(solution)/shard_map/ppermute | solution.py:34
  14.5 1.2 %collective-permute-done.5.refs_4_ = bf16[128,128]{1,0:T(8,128)(2,1)S(1)} collective-permute-done((bf16[128,128]{1,0:T(8,128)(2,1)S(1)}, bf16[128,128]{1,0:T(8,128)(2,1)S(1)}, u32[]{:S(2)}, u32[]{:S(2)}) %collective-permute-start.5) | collective-permute-done | bytes 32800 | tf_op jit(solution)/shard_map/ppermute | solution.py:34
  15.7 0.0 copy-done.1
  15.7 0.0 copy-done.2
  15.7 0.4 %shard_map.97 = (bf16[256,128]{1,0:T(8,128)(2,1)S(1)}, bf16[256,128]{1,0:T(8,128)(2,1)S(1)}, f32[128,256]{1,0:T(8,128)S(1)}) custom-call(bf16[512,512]{1,0:T(8,128)(2,1)S(1)} %shard_map.95.refs_0_.matrix, f32[128,128]{1,0:T(8,128)S(1)} %get-tuple-element.15.refs_1_, bf16[128,128]{1,0:T(8,128)(2,1)S(1)} %collective-permute-done.3.refs_2_, ...), custom_call_target="tpu_custom_call" | custom-call | flops 58720256 | tf_op jit(solution)/shard_map/pallas_call | solution.py:208
  16.1 1.2 %collective-permute-start.7 = (bf16[256,128]{1,0:T(8,128)(2,1)S(1)}, bf16[256,128]{1,0:T(8,128)(2,1)S(1)}, u32[]{:S(2)}, u32[]{:S(2)}) collective-permute-start(bf16[256,128]{1,0:T(8,128)(2,1)S(1)} %get-tuple-element.20.refs_0_), channel_id=1, source_target_pairs={{0,2},{1,3},{2,0},{3,1},{4,6},{5,7},{6,4},{7,5},{8,10},{9,11},{10,... | collective-permute-start | bytes 196616 | tf_op jit(solution)/shard_map/ppermute | solution.py:34
  17.3 2.6 %collective-permute-start.8 = (bf16[256,128]{1,0:T(8,128)(2,1)S(1)}, bf16[256,128]{1,0:T(8,128)(2,1)S(1)}, u32[]{:S(2)}, u32[]{:S(2)}) collective-permute-start(bf16[256,128]{1,0:T(8,128)(2,1)S(1)} %get-tuple-element.21), channel_id=1, source_target_pairs={{0,1},{1,2},{2,3},{3,0},{4,5},{5,6},{6,7},{7,4},{8,9},{9,10},{10,1... | collective-permute-start | bytes 196616 | tf_op jit(solution)/shard_map/ppermute | solution.py:34
  19.9 1.2 %collective-permute-start.6 = (bf16[256,128]{1,0:T(8,128)(2,1)S(1)}, bf16[256,128]{1,0:T(8,128)(2,1)S(1)}, u32[]{:S(2)}, u32[]{:S(2)}) collective-permute-start(bf16[256,128]{1,0:T(8,128)(2,1)S(1)} %get-tuple-element.21), channel_id=1, source_target_pairs={{0,3},{1,0},{2,1},{3,2},{4,7},{5,4},{6,5},{7,6},{8,11},{9,8},{10,9... | collective-permute-start | bytes 196616 | tf_op jit(solution)/shard_map/ppermute | solution.py:34
  21.2 2.4 %collective-permute-done.7.refs_2_ = bf16[256,128]{1,0:T(8,128)(2,1)S(1)} collective-permute-done((bf16[256,128]{1,0:T(8,128)(2,1)S(1)}, bf16[256,128]{1,0:T(8,128)(2,1)S(1)}, u32[]{:S(2)}, u32[]{:S(2)}) %collective-permute-start.7) | collective-permute-done | bytes 65568 | tf_op jit(solution)/shard_map/ppermute | solution.py:34
  23.5 0.0 collective-permute-done.8.refs_3_
  23.5 0.7 %collective-permute-done.6.refs_1_ = bf16[256,128]{1,0:T(8,128)(2,1)S(1)} collective-permute-done((bf16[256,128]{1,0:T(8,128)(2,1)S(1)}, bf16[256,128]{1,0:T(8,128)(2,1)S(1)}, u32[]{:S(2)}, u32[]{:S(2)}) %collective-permute-start.6) | collective-permute-done | bytes 65568 | tf_op jit(solution)/shard_map/ppermute | solution.py:34
  24.2 0.3 shard_map.99
  24.5 0.1 collective-permute-start.9
  24.6 1.2 %collective-permute-start.10 = (bf16[256,128]{1,0:T(8,128)(2,1)S(1)}, bf16[256,128]{1,0:T(8,128)(2,1)S(1)}, u32[]{:S(2)}, u32[]{:S(2)}) collective-permute-start(bf16[256,128]{1,0:T(8,128)(2,1)S(1)} %get-tuple-element.24), channel_id=1, source_target_pairs={{0,8},{4,12},{8,0},{12,4},{1,9},{5,13},{9,1},{13,5},{2,10},{6,14},... | collective-permute-start | bytes 196616 | tf_op jit(solution)/shard_map/ppermute | solution.py:34
  25.8 1.4 %collective-permute-start.11 = (bf16[256,128]{1,0:T(8,128)(2,1)S(1)}, bf16[256,128]{1,0:T(8,128)(2,1)S(1)}, u32[]{:S(2)}, u32[]{:S(2)}) collective-permute-start(bf16[256,128]{1,0:T(8,128)(2,1)S(1)} %get-tuple-element.25), channel_id=1, source_target_pairs={{0,12},{4,0},{8,4},{12,8},{1,13},{5,1},{9,5},{13,9},{2,14},{6,2},{... | collective-permute-start | bytes 196616 | tf_op jit(solution)/shard_map/ppermute | solution.py:34
  27.2 1.2 %collective-permute-done.9.refs_0_ = bf16[256,128]{1,0:T(8,128)(2,1)S(1)} collective-permute-done((bf16[256,128]{1,0:T(8,128)(2,1)S(1)}, bf16[256,128]{1,0:T(8,128)(2,1)S(1)}, u32[]{:S(2)}, u32[]{:S(2)}) %collective-permute-start.9) | collective-permute-done | bytes 65568 | tf_op jit(solution)/shard_map/ppermute | solution.py:34
  28.4 1.1 %collective-permute-done.10.refs_1_ = bf16[256,128]{1,0:T(8,128)(2,1)S(1)} collective-permute-done((bf16[256,128]{1,0:T(8,128)(2,1)S(1)}, bf16[256,128]{1,0:T(8,128)(2,1)S(1)}, u32[]{:S(2)}, u32[]{:S(2)}) %collective-permute-start.10) | collective-permute-done | bytes 65568 | tf_op jit(solution)/shard_map/ppermute | solution.py:34
  29.5 0.0 collective-permute-done.11.refs_2_
  29.5 0.7 %collective-permute-start.12 = (bf16[128,128]{1,0:T(8,128)(2,1)S(1)}, bf16[128,128]{1,0:T(8,128)(2,1)S(1)}, u32[]{:S(2)}, u32[]{:S(2)}) collective-permute-start(bf16[128,128]{1,0:T(8,128)(2,1)S(1)} %shard_map.101.mine), channel_id=1, source_target_pairs={{0,1},{1,0},{2,3},{3,2},{4,5},{5,4},{6,7},{7,6},{8,9},{9,8},{10,11... | collective-permute-start | bytes 98312 | tf_op jit(solution)/shard_map/ppermute | solution.py:41
  30.2 0.7 %shard_map.98 = bf16[128,256]{1,0:T(8,128)(2,1)} custom-call(f32[128,256]{1,0:T(8,128)S(1)} %get-tuple-element.19.pre), custom_call_target="tpu_custom_call" | custom-call | tf_op jit(solution)/shard_map/pallas_call | solution.py:216
  30.9 0.6 %shard_map.100 = bf16[128,128]{1,0:T(8,128)(2,1)} custom-call(f32[128,128]{1,0:T(8,128)S(1)} %get-tuple-element.22.own, bf16[256,128]{1,0:T(8,128)(2,1)S(1)} %collective-permute-done.9.refs_0_, bf16[256,128]{1,0:T(8,128)(2,1)S(1)} %collective-permute-done.10.refs_1_, bf16[256,128]{1,0:T(8,128)(2,1)S(1)} %collective-permute-done.11.refs_2_), custom_call_target="tpu_custom_call" | custom-call | tf_op jit(solution)/shard_map/pallas_call | solution.py:231
  31.5 2.1 %collective-permute-done.12.other = bf16[128,128]{1,0:T(8,128)(2,1)S(1)} collective-permute-done((bf16[128,128]{1,0:T(8,128)(2,1)S(1)}, bf16[128,128]{1,0:T(8,128)(2,1)S(1)}, u32[]{:S(2)}, u32[]{:S(2)}) %collective-permute-start.12) | collective-permute-done | bytes 32800 | tf_op jit(solution)/shard_map/ppermute | solution.py:41
  33.6 0.7 %shard_map.102 = f32[128,256]{1,0:T(8,128)} custom-call(bf16[128,128]{1,0:T(8,128)(2,1)S(1)} %shard_map.101.mine, bf16[128,128]{1,0:T(8,128)(2,1)S(1)} %collective-permute-done.12.other), custom_call_target="tpu_custom_call" | custom-call | tf_op jit(solution)/shard_map/pallas_call | solution.py:234
  (1 shorter events, 0.0 us)
Async XLA Ops:
  0.6 4.2 %copy-start.5 = (s32[1,1,8]{2,1,0:T(1,128)S(1)}, s32[1,1,8]{2,1,0:T(1,128)}, u32[]{:S(2)}) copy-start(s32[1,1,8]{2,1,0:T(1,128)} %cols_in.1) | copy-start | bytes 100
  0.6 4.2 %copy-start.4 = (s32[1,1,8]{2,1,0:T(1,128)S(1)}, s32[1,1,8]{2,1,0:T(1,128)}, u32[]{:S(2)}) copy-start(s32[1,1,8]{2,1,0:T(1,128)} %rows_in.1) | copy-start | bytes 100
  0.7 5.9 %collective-permute-start.1 = (bf16[128,128]{1,0:T(8,128)(2,1)}, bf16[128,128]{1,0:T(8,128)(2,1)S(1)}, u32[]{:S(2)}, u32[]{:S(2)}) collective-permute-start(bf16[128,128]{1,0:T(8,128)(2,1)} %refs_0_.1), channel_id=1, source_target_pairs={{0,8},{4,12},{8,0},{12,4},{1,9},{5,13},{9,1},{13,5},{2,10},{6,14},... | collective-permute-start | bytes 98312 | tf_op jit(solution)/shard_map/ppermute | solution.py:34
  3.7 2.9 %collective-permute-start = (bf16[128,128]{1,0:T(8,128)(2,1)}, bf16[128,128]{1,0:T(8,128)(2,1)S(1)}, u32[]{:S(2)}, u32[]{:S(2)}) collective-permute-start(bf16[128,128]{1,0:T(8,128)(2,1)} %refs_0_.1), channel_id=1, source_target_pairs={{0,12},{4,0},{8,4},{12,8},{1,13},{5,1},{9,5},{13,9},{2,14},{6,2},{... | collective-permute-start | bytes 98312 | tf_op jit(solution)/shard_map/ppermute | solution.py:34
  3.7 3.6 %collective-permute-start.2 = (bf16[128,128]{1,0:T(8,128)(2,1)}, bf16[128,128]{1,0:T(8,128)(2,1)S(1)}, u32[]{:S(2)}, u32[]{:S(2)}) collective-permute-start(bf16[128,128]{1,0:T(8,128)(2,1)} %refs_0_.1), channel_id=1, source_target_pairs={{0,4},{4,8},{8,12},{12,0},{1,5},{5,9},{9,13},{13,1},{2,6},{6,10},{... | collective-permute-start | bytes 98312 | tf_op jit(solution)/shard_map/ppermute | solution.py:34
  4.8 1.0 %copy-start = (bf16[1,1,8,128,128]{4,3,2,1,0:T(8,128)(2,1)S(1)}, bf16[1,1,8,128,128]{4,3,2,1,0:T(8,128)(2,1)}, u32[]{:S(2)}) copy-start(bf16[1,1,8,128,128]{4,3,2,1,0:T(8,128)(2,1)} %vals.1) | copy-start | bytes 786436
  5.8 1.5 %copy-start.3 = (bf16[128,128]{1,0:T(8,128)(2,1)S(1)}, bf16[128,128]{1,0:T(8,128)(2,1)}, u32[]{:S(2)}) copy-start(bf16[128,128]{1,0:T(8,128)(2,1)} %refs_0_.1) | copy-start | bytes 98308
  7.6 5.9 %collective-permute-start.3 = (bf16[128,128]{1,0:T(8,128)(2,1)S(1)}, bf16[128,128]{1,0:T(8,128)(2,1)S(1)}, u32[]{:S(2)}, u32[]{:S(2)}) collective-permute-start(bf16[128,128]{1,0:T(8,128)(2,1)S(1)} %get-tuple-element.16), channel_id=1, source_target_pairs={{0,1},{1,2},{2,3},{3,0},{4,5},{5,6},{6,7},{7,4},{8,9},{9,10},{10,1... | collective-permute-start | bytes 98312 | tf_op jit(solution)/shard_map/ppermute | solution.py:34
  9.2 5.3 %collective-permute-start.4 = (bf16[128,128]{1,0:T(8,128)(2,1)S(1)}, bf16[128,128]{1,0:T(8,128)(2,1)S(1)}, u32[]{:S(2)}, u32[]{:S(2)}) collective-permute-start(bf16[128,128]{1,0:T(8,128)(2,1)S(1)} %get-tuple-element.17), channel_id=1, source_target_pairs={{0,2},{1,3},{2,0},{3,1},{4,6},{5,7},{6,4},{7,5},{8,10},{9,11},{10,... | collective-permute-start | bytes 98312 | tf_op jit(solution)/shard_map/ppermute | solution.py:34
  11.8 3.9 %copy-start.1 = (bf16[128,256]{1,0:T(8,128)(2,1)S(1)}, bf16[128,256]{1,0:T(8,128)(2,1)}, u32[]{:S(2)}) copy-start(bf16[128,256]{1,0:T(8,128)(2,1)} %refs_5_.1) | copy-start | bytes 196612
  11.8 3.9 %copy-start.2 = (bf16[128,256]{1,0:T(8,128)(2,1)S(1)}, bf16[128,256]{1,0:T(8,128)(2,1)}, u32[]{:S(2)}) copy-start(bf16[128,256]{1,0:T(8,128)(2,1)} %refs_6_.1) | copy-start | bytes 196612
  11.8 3.9 %collective-permute-start.5 = (bf16[128,128]{1,0:T(8,128)(2,1)S(1)}, bf16[128,128]{1,0:T(8,128)(2,1)S(1)}, u32[]{:S(2)}, u32[]{:S(2)}) collective-permute-start(bf16[128,128]{1,0:T(8,128)(2,1)S(1)} %get-tuple-element.18), channel_id=1, source_target_pairs={{0,3},{1,0},{2,1},{3,2},{4,7},{5,4},{6,5},{7,6},{8,11},{9,8},{10,9... | collective-permute-start | bytes 98312 | tf_op jit(solution)/shard_map/ppermute | solution.py:34
  16.1 7.4 %collective-permute-start.7 = (bf16[256,128]{1,0:T(8,128)(2,1)S(1)}, bf16[256,128]{1,0:T(8,128)(2,1)S(1)}, u32[]{:S(2)}, u32[]{:S(2)}) collective-permute-start(bf16[256,128]{1,0:T(8,128)(2,1)S(1)} %get-tuple-element.20.refs_0_), channel_id=1, source_target_pairs={{0,2},{1,3},{2,0},{3,1},{4,6},{5,7},{6,4},{7,5},{8,10},{9,11},{10,... | collective-permute-start | bytes 196616 | tf_op jit(solution)/shard_map/ppermute | solution.py:34
  17.3 6.2 %collective-permute-start.8 = (bf16[256,128]{1,0:T(8,128)(2,1)S(1)}, bf16[256,128]{1,0:T(8,128)(2,1)S(1)}, u32[]{:S(2)}, u32[]{:S(2)}) collective-permute-start(bf16[256,128]{1,0:T(8,128)(2,1)S(1)} %get-tuple-element.21), channel_id=1, source_target_pairs={{0,1},{1,2},{2,3},{3,0},{4,5},{5,6},{6,7},{7,4},{8,9},{9,10},{10,1... | collective-permute-start | bytes 196616 | tf_op jit(solution)/shard_map/ppermute | solution.py:34
  19.9 4.3 %collective-permute-start.6 = (bf16[256,128]{1,0:T(8,128)(2,1)S(1)}, bf16[256,128]{1,0:T(8,128)(2,1)S(1)}, u32[]{:S(2)}, u32[]{:S(2)}) collective-permute-start(bf16[256,128]{1,0:T(8,128)(2,1)S(1)} %get-tuple-element.21), channel_id=1, source_target_pairs={{0,3},{1,0},{2,1},{3,2},{4,7},{5,4},{6,5},{7,6},{8,11},{9,8},{10,9... | collective-permute-start | bytes 196616 | tf_op jit(solution)/shard_map/ppermute | solution.py:34
  24.5 3.8 %collective-permute-start.9 = (bf16[256,128]{1,0:T(8,128)(2,1)S(1)}, bf16[256,128]{1,0:T(8,128)(2,1)S(1)}, u32[]{:S(2)}, u32[]{:S(2)}) collective-permute-start(bf16[256,128]{1,0:T(8,128)(2,1)S(1)} %get-tuple-element.23), channel_id=1, source_target_pairs={{0,4},{4,8},{8,12},{12,0},{1,5},{5,9},{9,13},{13,1},{2,6},{6,10},{... | collective-permute-start | bytes 196616 | tf_op jit(solution)/shard_map/ppermute | solution.py:34
  24.6 4.9 %collective-permute-start.10 = (bf16[256,128]{1,0:T(8,128)(2,1)S(1)}, bf16[256,128]{1,0:T(8,128)(2,1)S(1)}, u32[]{:S(2)}, u32[]{:S(2)}) collective-permute-start(bf16[256,128]{1,0:T(8,128)(2,1)S(1)} %get-tuple-element.24), channel_id=1, source_target_pairs={{0,8},{4,12},{8,0},{12,4},{1,9},{5,13},{9,1},{13,5},{2,10},{6,14},... | collective-permute-start | bytes 196616 | tf_op jit(solution)/shard_map/ppermute | solution.py:34
  25.8 3.7 %collective-permute-start.11 = (bf16[256,128]{1,0:T(8,128)(2,1)S(1)}, bf16[256,128]{1,0:T(8,128)(2,1)S(1)}, u32[]{:S(2)}, u32[]{:S(2)}) collective-permute-start(bf16[256,128]{1,0:T(8,128)(2,1)S(1)} %get-tuple-element.25), channel_id=1, source_target_pairs={{0,12},{4,0},{8,4},{12,8},{1,13},{5,1},{9,5},{13,9},{2,14},{6,2},{... | collective-permute-start | bytes 196616 | tf_op jit(solution)/shard_map/ppermute | solution.py:34
  29.5 4.1 %collective-permute-start.12 = (bf16[128,128]{1,0:T(8,128)(2,1)S(1)}, bf16[128,128]{1,0:T(8,128)(2,1)S(1)}, u32[]{:S(2)}, u32[]{:S(2)}) collective-permute-start(bf16[128,128]{1,0:T(8,128)(2,1)S(1)} %shard_map.101.mine), channel_id=1, source_target_pairs={{0,1},{1,0},{2,3},{3,2},{4,5},{5,4},{6,7},{7,6},{8,9},{9,8},{10,11... | collective-permute-start | bytes 98312 | tf_op jit(solution)/shard_map/ppermute | solution.py:41

commit v6 on v5

--- a/solution.py
+++ b/solution.py
@@ -36,11 +36,6 @@
     ]
 
 
-def neighbour(value, axis):
-    n = lax.axis_size(axis)
-    return lax.ppermute(value, axis, [(s, s ^ 1) for s in range(n)])
-
-
 def wide(value):
     return value.astype(jnp.float32)
 
@@ -106,9 +101,8 @@
 
 
 def layer_kernel(*refs):
-    *parts, weight, cotangent, same, other, pre_out = refs
-    nodes, hidden = cotangent.shape
-    half = hidden // 2
+    *parts, weight, cotangent, message, pre_out = refs
+    nodes = cotangent.shape[0]
     total = tree([wide(part[...]) for part in parts])
     high, low = split(total)
     pre = dot(high, weight[...]) + dot(low, weight[...])
@@ -118,15 +112,14 @@
     grad_high, grad_low = split(grad)
     across = ((1,), (1,))
     back = dot(grad_high, weight[...], across) + dot(grad_low, weight[...], across)
-    same[:nodes] = back.astype(same.dtype)
-    other[:nodes] = back.astype(other.dtype)
+    message[:nodes] = back.astype(message.dtype)
     down = ((0,), (0,))
     term = dot(high, grad_high, down) + dot(low, grad_high, down) + dot(high, grad_low, down)
-    term = term.astype(same.dtype)
-    odd = lax.rem(lax.axis_index("col"), 2) == 1
-    left, right = term[:, :half], term[:, half:]
-    same[nodes:] = jnp.where(odd, right, left)
-    other[nodes:] = jnp.where(odd, left, right)
+    half = message.shape[1]
+    rows = total.shape[1]
+    for k in range(term.shape[1] // half):
+        start = nodes + k * rows
+        message[start : start + rows] = term[:, k * half : (k + 1) * half].astype(message.dtype)
 
 
 def act_kernel(pre, act):
@@ -146,24 +139,16 @@
         send[rows:] = term
 
 
-def term_kernel(scale, kept, *refs):
-    *messages, half = refs
-    rows = messages[0].shape[0] - kept.shape[0]
-    total = tree([wide(kept[...])] + [wide(message[rows:]) for message in messages])
-    half[...] = (total * scale).astype(half.dtype)
-
-
-def feature_kernel(own, *refs):
-    *messages, out = refs
-    rows = own.shape[0]
-    out[...] = tree([own[...]] + [wide(message[:rows]) for message in messages]).astype(out.dtype)
-
-
-def join_kernel(mine, other, out):
-    half = mine.shape[1]
-    odd = lax.rem(lax.axis_index("col"), 2) == 1
-    out[:, :half] = jnp.where(odd, wide(other[...]), wide(mine[...]))
-    out[:, half:] = jnp.where(odd, wide(mine[...]), wide(other[...]))
+def last_kernel(scale, own, kept, *refs):
+    *messages, features_out, weight_out = refs
+    nodes = own.shape[0]
+    rows, half = weight_out.shape[0], kept.shape[1]
+    features_out[...] = tree(
+        [own[...]] + [wide(message[:nodes]) for message in messages]
+    ).astype(features_out.dtype)
+    total = tree([wide(kept[...])] + [wide(message[nodes:]) for message in messages]) * scale
+    for k in range(weight_out.shape[1] // half):
+        weight_out[:, k * half : (k + 1) * half] = total[k * rows : (k + 1) * rows]
 
 
 def per_device(features, weight, cotangent, tile_values, tile_rows, tile_cols, tile_count):
@@ -171,7 +156,6 @@
     n_row, n_col = lax.axis_size("row"), lax.axis_size("col")
     nodes, width = features.shape
     hidden = weight.shape[1]
-    half = hidden // 2
     down, across = n_col * nodes, n_row * nodes
     dense_bytes = 2 * down * across
 
@@ -204,36 +188,33 @@
         need=3 * dense_bytes,
     )(near)
 
-    message = ((nodes + width, width), NARROW)
-    same, other, pre = call(
+    stacked = hidden // width * width
+    message = ((nodes + stacked, width), NARROW)
+    sent, pre = call(
         layer_kernel,
-        [message, message, ((nodes, hidden), jnp.float32)],
+        [message, ((nodes, hidden), jnp.float32)],
         [VMEM] * (n_col + 2),
         flops=14 * nodes * width * hidden,
         after=[far],
     )(own, *parts, weight, cotangent)
-    spread = exchange([(same, other)[d % 2] for d in range(1, n_col)], "col", False)
+    spread = exchange([sent] * (n_col - 1), "col", False)
     (act,) = call(act_kernel, [((nodes, hidden), NARROW)], [VMEM])(pre)
 
     own, kept, *sends = call(
         functools.partial(backward_kernel, n_col),
-        [((nodes, width), jnp.float32), ((width, half), NARROW)] + [message] * (n_row - 1),
+        [((nodes, width), jnp.float32), ((stacked, width), NARROW)] + [message] * (n_row - 1),
         [VMEM] * (1 + n_col),
         flops=2 * down * across * width,
         need=2 * dense_bytes,
-    )(far, same, *spread)
+    )(far, sent, *spread)
     parts = exchange(sends, "row", True)
 
     scale = float(nodes * n_row * n_col) ** -0.5
-    (mine,) = call(
-        functools.partial(term_kernel, scale), [((width, half), NARROW)], [VMEM] * n_row
-    )(kept, *parts)
-    (grad_features,) = call(feature_kernel, [((nodes, width), NARROW)], [VMEM] * n_row)(
-        own, *parts
-    )
-    (grad_weight,) = call(join_kernel, [((width, hidden), jnp.float32)], [VMEM] * 2)(
-        mine, neighbour(mine, "col")
-    )
+    grad_features, grad_weight = call(
+        functools.partial(last_kernel, scale),
+        [((nodes, width), NARROW), ((width, hidden), jnp.float32)],
+        [VMEM] * (n_row + 1),
+    )(own, kept, *parts)
     return act, grad_features, grad_weight
 
 

time: 34.4 us -> 33.8 us (0.983)
  the two profiles are of different devices: /device:TPU:0 before, /device:TPU:1 now
where the time goes in v6:
time: 33.8 us; the launch traced here: 33.6 us
  starting transfers between devices  16.1 us (48%)
  waiting for transfers between devices  11.7 us (35%)
  Pallas kernels  3.38 us (10%)
  between operations  1.41 us (4%)
  local copies, waits for them, and re-layouts  1.01 us (3%)
    ppermute x12, starting transfers between devices, exchange(): lax.ppermute(send, axis, [(s, (s + (d if ahead else -d)) % n) for s in ra...  16.1 us
    ppermute x12, waiting for transfers between devices, exchange(): lax.ppermute(send, axis, [(s, (s + (d if ahead else -d)) % n) for s in ra...  11.7 us
    unnamed x12, local copies, waits for them, and re-layouts  1.01 us
    pallas_call x1, Pallas kernels, per_device(): call(functools.partial(last_kernel, scale), [((nodes, width), NARROW), ((...  0.71 us
  transfers between devices with their start and end apart: 12, of which 6 were waited for; matrix products, arithmetic and copies ran while one was open for 0% of the time, Pallas kernels for 5%

profile of v6, /device:TPU:1, one launch (start us, length us, event | category | flops | bytes accessed | tf_op | source)
XLA Modules:
  0.0 33.6 jit_solution(10097181519563548287)
XLA Ops:
  0.6 0.0 copy-start.5
  0.6 0.0 copy-start.4
  0.7 2.1 %collective-permute-start.1 = (bf16[128,128]{1,0:T(8,128)(2,1)}, bf16[128,128]{1,0:T(8,128)(2,1)S(1)}, u32[]{:S(2)}, u32[]{:S(2)}) collective-permute-start(bf16[128,128]{1,0:T(8,128)(2,1)} %refs_0_.1), channel_id=1, source_target_pairs={{0,8},{4,12},{8,0},{12,4},{1,9},{5,13},{9,1},{13,5},{2,10},{6,14},... | collective-permute-start | bytes 98312 | tf_op jit(solution)/shard_map/ppermute | solution.py:34
  2.8 1.0 %collective-permute-start = (bf16[128,128]{1,0:T(8,128)(2,1)}, bf16[128,128]{1,0:T(8,128)(2,1)S(1)}, u32[]{:S(2)}, u32[]{:S(2)}) collective-permute-start(bf16[128,128]{1,0:T(8,128)(2,1)} %refs_0_.1), channel_id=1, source_target_pairs={{0,12},{4,0},{8,4},{12,8},{1,13},{5,1},{9,5},{13,9},{2,14},{6,2},{... | collective-permute-start | bytes 98312 | tf_op jit(solution)/shard_map/ppermute | solution.py:34
  3.7 0.8 %collective-permute-start.2 = (bf16[128,128]{1,0:T(8,128)(2,1)}, bf16[128,128]{1,0:T(8,128)(2,1)S(1)}, u32[]{:S(2)}, u32[]{:S(2)}) collective-permute-start(bf16[128,128]{1,0:T(8,128)(2,1)} %refs_0_.1), channel_id=1, source_target_pairs={{0,4},{4,8},{8,12},{12,0},{1,5},{5,9},{9,13},{13,1},{2,6},{6,10},{... | collective-permute-start | bytes 98312 | tf_op jit(solution)/shard_map/ppermute | solution.py:34
  5.2 0.0 copy-done.5
  5.2 0.0 copy-done.4
  5.2 0.0 copy-start
  5.2 0.9 %copy-done = bf16[1,1,8,128,128]{4,3,2,1,0:T(8,128)(2,1)S(1)} copy-done((bf16[1,1,8,128,128]{4,3,2,1,0:T(8,128)(2,1)S(1)}, bf16[1,1,8,128,128]{4,3,2,1,0:T(8,128)(2,1)}, u32[]{:S(2)}) %copy-start) | copy-done | bytes 262168
  6.1 0.0 copy-start.3
  6.1 0.7 %shard_map.94.near.matrix = bf16[512,512]{1,0:T(8,128)(2,1)S(1)} custom-call(bf16[1,1,8,128,128]{4,3,2,1,0:T(8,128)(2,1)S(1)} %copy-done, s32[1,1,8]{2,1,0:T(1,128)S(1)} %copy-done.4, s32[1,1,8]{2,1,0:T(1,128)S(1)} %copy-done.5, s32[1,1]{1,0:T(1,128)S(6)} %copy.10.count_in), custom_call_target="tpu_custom_call" | custom-call | bytes 1048576 | tf_op jit(solution)/shard_map/pallas_call | solution.py:163
  6.8 0.0 collective-permute-done.1.refs_2_
  6.8 0.0 collective-permute-done.refs_1_
  6.8 0.0 collective-permute-done.2.refs_3_
  6.8 0.1 copy-done.3
  6.9 0.3 shard_map.96
  7.2 1.3 %collective-permute-start.3 = (bf16[128,128]{1,0:T(8,128)(2,1)S(1)}, bf16[128,128]{1,0:T(8,128)(2,1)S(1)}, u32[]{:S(2)}, u32[]{:S(2)}) collective-permute-start(bf16[128,128]{1,0:T(8,128)(2,1)S(1)} %get-tuple-element.17), channel_id=1, source_target_pairs={{0,1},{1,2},{2,3},{3,0},{4,5},{5,6},{6,7},{7,4},{8,9},{9,10},{10,1... | collective-permute-start | bytes 98312 | tf_op jit(solution)/shard_map/ppermute | solution.py:34
  8.5 2.3 %collective-permute-start.4 = (bf16[128,128]{1,0:T(8,128)(2,1)S(1)}, bf16[128,128]{1,0:T(8,128)(2,1)S(1)}, u32[]{:S(2)}, u32[]{:S(2)}) collective-permute-start(bf16[128,128]{1,0:T(8,128)(2,1)S(1)} %get-tuple-element.18), channel_id=1, source_target_pairs={{0,2},{1,3},{2,0},{3,1},{4,6},{5,7},{6,4},{7,5},{8,10},{9,11},{10,... | collective-permute-start | bytes 98312 | tf_op jit(solution)/shard_map/ppermute | solution.py:34
  10.9 0.0 copy-start.1
  10.9 0.0 copy-start.2
  10.9 1.0 %collective-permute-start.5 = (bf16[128,128]{1,0:T(8,128)(2,1)S(1)}, bf16[128,128]{1,0:T(8,128)(2,1)S(1)}, u32[]{:S(2)}, u32[]{:S(2)}) collective-permute-start(bf16[128,128]{1,0:T(8,128)(2,1)S(1)} %get-tuple-element.19), channel_id=1, source_target_pairs={{0,3},{1,0},{2,1},{3,2},{4,7},{5,4},{6,5},{7,6},{8,11},{9,8},{10,9... | collective-permute-start | bytes 98312 | tf_op jit(solution)/shard_map/ppermute | solution.py:34
  11.9 0.3 %shard_map.95.refs_0_.matrix = bf16[512,512]{1,0:T(8,128)(2,1)S(1)} custom-call(bf16[512,512]{1,0:T(8,128)(2,1)S(1)} %shard_map.94.near.matrix), custom_call_target="tpu_custom_call" | custom-call | bytes 1572864 | tf_op jit(solution)/shard_map/pallas_call | solution.py:184
  12.3 0.0 collective-permute-done.3.refs_2_
  12.3 0.0 collective-permute-done.4.refs_3_
  12.3 1.9 %collective-permute-done.5.refs_4_ = bf16[128,128]{1,0:T(8,128)(2,1)S(1)} collective-permute-done((bf16[128,128]{1,0:T(8,128)(2,1)S(1)}, bf16[128,128]{1,0:T(8,128)(2,1)S(1)}, u32[]{:S(2)}, u32[]{:S(2)}) %collective-permute-start.5) | collective-permute-done | bytes 32800 | tf_op jit(solution)/shard_map/ppermute | solution.py:34
  14.2 0.0 copy-done.1
  14.2 0.0 copy-done.2
  14.2 0.4 %shard_map.97 = (bf16[384,128]{1,0:T(8,128)(2,1)S(1)}, f32[128,256]{1,0:T(8,128)S(1)}) custom-call(bf16[512,512]{1,0:T(8,128)(2,1)S(1)} %shard_map.95.refs_0_.matrix, f32[128,128]{1,0:T(8,128)S(1)} %get-tuple-element.16.refs_1_, bf16[128,128]{1,0:T(8,128)(2,1)S(1)} %collective-permute-done.3.refs_2_, bf16[128,128]{1,0:T(8,128)(2,1)S(1)} %collective-permute-done.4.refs_3_, ...), custom_call_target="tpu_custom_call" | custom-call | flops 58720256 | tf_op jit(solution)/shard_map/pallas_call | solution.py:193
  14.6 0.1 collective-permute-start.8
  14.7 2.8 %collective-permute-start.7 = (bf16[384,128]{1,0:T(8,128)(2,1)S(1)}, bf16[384,128]{1,0:T(8,128)(2,1)S(1)}, u32[]{:S(2)}, u32[]{:S(2)}) collective-permute-start(bf16[384,128]{1,0:T(8,128)(2,1)S(1)} %get-tuple-element.21.refs_0_), channel_id=1, source_target_pairs={{0,2},{1,3},{2,0},{3,1},{4,6},{5,7},{6,4},{7,5},{8,10},{9,11},{10,... | collective-permute-start | bytes 294920 | tf_op jit(solution)/shard_map/ppermute | solution.py:34
  17.4 0.5 %collective-permute-start.6 = (bf16[384,128]{1,0:T(8,128)(2,1)S(1)}, bf16[384,128]{1,0:T(8,128)(2,1)S(1)}, u32[]{:S(2)}, u32[]{:S(2)}) collective-permute-start(bf16[384,128]{1,0:T(8,128)(2,1)S(1)} %get-tuple-element.21.refs_0_), channel_id=1, source_target_pairs={{0,3},{1,0},{2,1},{3,2},{4,7},{5,4},{6,5},{7,6},{8,11},{9,8},{10,9... | collective-permute-start | bytes 294920 | tf_op jit(solution)/shard_map/ppermute | solution.py:34
  17.9 2.1 %collective-permute-done.8.refs_3_ = bf16[384,128]{1,0:T(8,128)(2,1)S(1)} collective-permute-done((bf16[384,128]{1,0:T(8,128)(2,1)S(1)}, bf16[384,128]{1,0:T(8,128)(2,1)S(1)}, u32[]{:S(2)}, u32[]{:S(2)}) %collective-permute-start.8) | collective-permute-done | bytes 98336 | tf_op jit(solution)/shard_map/ppermute | solution.py:34
  20.1 3.2 %collective-permute-done.7.refs_2_ = bf16[384,128]{1,0:T(8,128)(2,1)S(1)} collective-permute-done((bf16[384,128]{1,0:T(8,128)(2,1)S(1)}, bf16[384,128]{1,0:T(8,128)(2,1)S(1)}, u32[]{:S(2)}, u32[]{:S(2)}) %collective-permute-start.7) | collective-permute-done | bytes 98336 | tf_op jit(solution)/shard_map/ppermute | solution.py:34
  23.2 0.0 collective-permute-done.6.refs_1_
  23.2 0.3 shard_map.99
  23.5 3.6 %collective-permute-start.9 = (bf16[384,128]{1,0:T(8,128)(2,1)S(1)}, bf16[384,128]{1,0:T(8,128)(2,1)S(1)}, u32[]{:S(2)}, u32[]{:S(2)}) collective-permute-start(bf16[384,128]{1,0:T(8,128)(2,1)S(1)} %get-tuple-element.24), channel_id=1, source_target_pairs={{0,4},{4,8},{8,12},{12,0},{1,5},{5,9},{9,13},{13,1},{2,6},{6,10},{... | collective-permute-start | bytes 294920 | tf_op jit(solution)/shard_map/ppermute | solution.py:34
  27.1 0.7 %collective-permute-start.10 = (bf16[384,128]{1,0:T(8,128)(2,1)S(1)}, bf16[384,128]{1,0:T(8,128)(2,1)S(1)}, u32[]{:S(2)}, u32[]{:S(2)}) collective-permute-start(bf16[384,128]{1,0:T(8,128)(2,1)S(1)} %get-tuple-element.25), channel_id=1, source_target_pairs={{0,8},{4,12},{8,0},{12,4},{1,9},{5,13},{9,1},{13,5},{2,10},{6,14},... | collective-permute-start | bytes 294920 | tf_op jit(solution)/shard_map/ppermute | solution.py:34
  27.8 0.0 collective-permute-start.11
  27.8 0.7 %shard_map.98 = bf16[128,256]{1,0:T(8,128)(2,1)} custom-call(f32[128,256]{1,0:T(8,128)S(1)} %get-tuple-element.20.pre), custom_call_target="tpu_custom_call" | custom-call | tf_op jit(solution)/shard_map/pallas_call | solution.py:201
  28.4 0.7 %collective-permute-done.9.refs_0_ = bf16[384,128]{1,0:T(8,128)(2,1)S(1)} collective-permute-done((bf16[384,128]{1,0:T(8,128)(2,1)S(1)}, bf16[384,128]{1,0:T(8,128)(2,1)S(1)}, u32[]{:S(2)}, u32[]{:S(2)}) %collective-permute-start.9) | collective-permute-done | bytes 98336 | tf_op jit(solution)/shard_map/ppermute | solution.py:34
  29.1 3.2 %collective-permute-done.10.refs_1_ = bf16[384,128]{1,0:T(8,128)(2,1)S(1)} collective-permute-done((bf16[384,128]{1,0:T(8,128)(2,1)S(1)}, bf16[384,128]{1,0:T(8,128)(2,1)S(1)}, u32[]{:S(2)}, u32[]{:S(2)}) %collective-permute-start.10) | collective-permute-done | bytes 98336 | tf_op jit(solution)/shard_map/ppermute | solution.py:34
  32.3 0.6 %collective-permute-done.11.refs_2_ = bf16[384,128]{1,0:T(8,128)(2,1)S(1)} collective-permute-done((bf16[384,128]{1,0:T(8,128)(2,1)S(1)}, bf16[384,128]{1,0:T(8,128)(2,1)S(1)}, u32[]{:S(2)}, u32[]{:S(2)}) %collective-permute-start.11) | collective-permute-done | bytes 98336 | tf_op jit(solution)/shard_map/ppermute | solution.py:34
  32.9 0.7 %shard_map.100 = (bf16[128,128]{1,0:T(8,128)(2,1)}, f32[128,256]{1,0:T(8,128)}) custom-call(f32[128,128]{1,0:T(8,128)S(1)} %get-tuple-element.22.own, bf16[256,128]{1,0:T(8,128)(2,1)S(1)} %get-tuple-element.23.kept, bf16[384,128]{1,0:T(8,128)(2,1)S(1)} %collective-permute-done.9.refs_0_, bf16[384,128]{1,0:T(8,128)(2,1)S(1)} %collective-permute-done.10.refs_1_, ...), custom_call_target="tpu_custom_call" | custom-call | tf_op jit(solution)/shard_map/pallas_call | solution.py:213
Async XLA Ops:
  0.6 4.5 %copy-start.5 = (s32[1,1,8]{2,1,0:T(1,128)S(1)}, s32[1,1,8]{2,1,0:T(1,128)}, u32[]{:S(2)}) copy-start(s32[1,1,8]{2,1,0:T(1,128)} %cols_in.1) | copy-start | bytes 100
  0.6 4.5 %copy-start.4 = (s32[1,1,8]{2,1,0:T(1,128)S(1)}, s32[1,1,8]{2,1,0:T(1,128)}, u32[]{:S(2)}) copy-start(s32[1,1,8]{2,1,0:T(1,128)} %rows_in.1) | copy-start | bytes 100
  0.7 6.2 %collective-permute-start.1 = (bf16[128,128]{1,0:T(8,128)(2,1)}, bf16[128,128]{1,0:T(8,128)(2,1)S(1)}, u32[]{:S(2)}, u32[]{:S(2)}) collective-permute-start(bf16[128,128]{1,0:T(8,128)(2,1)} %refs_0_.1), channel_id=1, source_target_pairs={{0,8},{4,12},{8,0},{12,4},{1,9},{5,13},{9,1},{13,5},{2,10},{6,14},... | collective-permute-start | bytes 98312 | tf_op jit(solution)/shard_map/ppermute | solution.py:34
  2.8 4.1 %collective-permute-start = (bf16[128,128]{1,0:T(8,128)(2,1)}, bf16[128,128]{1,0:T(8,128)(2,1)S(1)}, u32[]{:S(2)}, u32[]{:S(2)}) collective-permute-start(bf16[128,128]{1,0:T(8,128)(2,1)} %refs_0_.1), channel_id=1, source_target_pairs={{0,12},{4,0},{8,4},{12,8},{1,13},{5,1},{9,5},{13,9},{2,14},{6,2},{... | collective-permute-start | bytes 98312 | tf_op jit(solution)/shard_map/ppermute | solution.py:34
  3.7 3.1 %collective-permute-start.2 = (bf16[128,128]{1,0:T(8,128)(2,1)}, bf16[128,128]{1,0:T(8,128)(2,1)S(1)}, u32[]{:S(2)}, u32[]{:S(2)}) collective-permute-start(bf16[128,128]{1,0:T(8,128)(2,1)} %refs_0_.1), channel_id=1, source_target_pairs={{0,4},{4,8},{8,12},{12,0},{1,5},{5,9},{9,13},{13,1},{2,6},{6,10},{... | collective-permute-start | bytes 98312 | tf_op jit(solution)/shard_map/ppermute | solution.py:34
  5.2 1.0 %copy-start = (bf16[1,1,8,128,128]{4,3,2,1,0:T(8,128)(2,1)S(1)}, bf16[1,1,8,128,128]{4,3,2,1,0:T(8,128)(2,1)}, u32[]{:S(2)}) copy-start(bf16[1,1,8,128,128]{4,3,2,1,0:T(8,128)(2,1)} %vals.1) | copy-start | bytes 786436
  6.1 0.8 %copy-start.3 = (bf16[128,128]{1,0:T(8,128)(2,1)S(1)}, bf16[128,128]{1,0:T(8,128)(2,1)}, u32[]{:S(2)}) copy-start(bf16[128,128]{1,0:T(8,128)(2,1)} %refs_0_.1) | copy-start | bytes 98308
  7.2 5.1 %collective-permute-start.3 = (bf16[128,128]{1,0:T(8,128)(2,1)S(1)}, bf16[128,128]{1,0:T(8,128)(2,1)S(1)}, u32[]{:S(2)}, u32[]{:S(2)}) collective-permute-start(bf16[128,128]{1,0:T(8,128)(2,1)S(1)} %get-tuple-element.17), channel_id=1, source_target_pairs={{0,1},{1,2},{2,3},{3,0},{4,5},{5,6},{6,7},{7,4},{8,9},{9,10},{10,1... | collective-permute-start | bytes 98312 | tf_op jit(solution)/shard_map/ppermute | solution.py:34
  8.5 3.7 %collective-permute-start.4 = (bf16[128,128]{1,0:T(8,128)(2,1)S(1)}, bf16[128,128]{1,0:T(8,128)(2,1)S(1)}, u32[]{:S(2)}, u32[]{:S(2)}) collective-permute-start(bf16[128,128]{1,0:T(8,128)(2,1)S(1)} %get-tuple-element.18), channel_id=1, source_target_pairs={{0,2},{1,3},{2,0},{3,1},{4,6},{5,7},{6,4},{7,5},{8,10},{9,11},{10,... | collective-permute-start | bytes 98312 | tf_op jit(solution)/shard_map/ppermute | solution.py:34
  10.9 3.3 %copy-start.1 = (bf16[128,256]{1,0:T(8,128)(2,1)S(1)}, bf16[128,256]{1,0:T(8,128)(2,1)}, u32[]{:S(2)}) copy-start(bf16[128,256]{1,0:T(8,128)(2,1)} %refs_5_.1) | copy-start | bytes 196612
  10.9 3.3 %copy-start.2 = (bf16[128,256]{1,0:T(8,128)(2,1)S(1)}, bf16[128,256]{1,0:T(8,128)(2,1)}, u32[]{:S(2)}) copy-start(bf16[128,256]{1,0:T(8,128)(2,1)} %refs_6_.1) | copy-start | bytes 196612
  10.9 3.3 %collective-permute-start.5 = (bf16[128,128]{1,0:T(8,128)(2,1)S(1)}, bf16[128,128]{1,0:T(8,128)(2,1)S(1)}, u32[]{:S(2)}, u32[]{:S(2)}) collective-permute-start(bf16[128,128]{1,0:T(8,128)(2,1)S(1)} %get-tuple-element.19), channel_id=1, source_target_pairs={{0,3},{1,0},{2,1},{3,2},{4,7},{5,4},{6,5},{7,6},{8,11},{9,8},{10,9... | collective-permute-start | bytes 98312 | tf_op jit(solution)/shard_map/ppermute | solution.py:34
  14.6 5.4 %collective-permute-start.8 = (bf16[384,128]{1,0:T(8,128)(2,1)S(1)}, bf16[384,128]{1,0:T(8,128)(2,1)S(1)}, u32[]{:S(2)}, u32[]{:S(2)}) collective-permute-start(bf16[384,128]{1,0:T(8,128)(2,1)S(1)} %get-tuple-element.21.refs_0_), channel_id=1, source_target_pairs={{0,1},{1,2},{2,3},{3,0},{4,5},{5,6},{6,7},{7,4},{8,9},{9,10},{10,1... | collective-permute-start | bytes 294920 | tf_op jit(solution)/shard_map/ppermute | solution.py:34
  14.7 8.5 %collective-permute-start.7 = (bf16[384,128]{1,0:T(8,128)(2,1)S(1)}, bf16[384,128]{1,0:T(8,128)(2,1)S(1)}, u32[]{:S(2)}, u32[]{:S(2)}) collective-permute-start(bf16[384,128]{1,0:T(8,128)(2,1)S(1)} %get-tuple-element.21.refs_0_), channel_id=1, source_target_pairs={{0,2},{1,3},{2,0},{3,1},{4,6},{5,7},{6,4},{7,5},{8,10},{9,11},{10,... | collective-permute-start | bytes 294920 | tf_op jit(solution)/shard_map/ppermute | solution.py:34
  17.4 5.8 %collective-permute-start.6 = (bf16[384,128]{1,0:T(8,128)(2,1)S(1)}, bf16[384,128]{1,0:T(8,128)(2,1)S(1)}, u32[]{:S(2)}, u32[]{:S(2)}) collective-permute-start(bf16[384,128]{1,0:T(8,128)(2,1)S(1)} %get-tuple-element.21.refs_0_), channel_id=1, source_target_pairs={{0,3},{1,0},{2,1},{3,2},{4,7},{5,4},{6,5},{7,6},{8,11},{9,8},{10,9... | collective-permute-start | bytes 294920 | tf_op jit(solution)/shard_map/ppermute | solution.py:34
  23.5 5.6 %collective-permute-start.9 = (bf16[384,128]{1,0:T(8,128)(2,1)S(1)}, bf16[384,128]{1,0:T(8,128)(2,1)S(1)}, u32[]{:S(2)}, u32[]{:S(2)}) collective-permute-start(bf16[384,128]{1,0:T(8,128)(2,1)S(1)} %get-tuple-element.24), channel_id=1, source_target_pairs={{0,4},{4,8},{8,12},{12,0},{1,5},{5,9},{9,13},{13,1},{2,6},{6,10},{... | collective-permute-start | bytes 294920 | tf_op jit(solution)/shard_map/ppermute | solution.py:34
  27.1 5.2 %collective-permute-start.10 = (bf16[384,128]{1,0:T(8,128)(2,1)S(1)}, bf16[384,128]{1,0:T(8,128)(2,1)S(1)}, u32[]{:S(2)}, u32[]{:S(2)}) collective-permute-start(bf16[384,128]{1,0:T(8,128)(2,1)S(1)} %get-tuple-element.25), channel_id=1, source_target_pairs={{0,8},{4,12},{8,0},{12,4},{1,9},{5,13},{9,1},{13,5},{2,10},{6,14},... | collective-permute-start | bytes 294920 | tf_op jit(solution)/shard_map/ppermute | solution.py:34
  27.8 5.2 %collective-permute-start.11 = (bf16[384,128]{1,0:T(8,128)(2,1)S(1)}, bf16[384,128]{1,0:T(8,128)(2,1)S(1)}, u32[]{:S(2)}, u32[]{:S(2)}) collective-permute-start(bf16[384,128]{1,0:T(8,128)(2,1)S(1)} %get-tuple-element.26), channel_id=1, source_target_pairs={{0,12},{4,0},{8,4},{12,8},{1,13},{5,1},{9,5},{13,9},{2,14},{6,2},{... | collective-permute-start | bytes 294920 | tf_op jit(solution)/shard_map/ppermute | solution.py:34

commit v7 on v6

--- a/solution.py
+++ b/solution.py
@@ -36,6 +36,10 @@
     ]
 
 
+def send(value, axis, pairs):
+    return lax.ppermute(value, axis, pairs)
+
+
 def wide(value):
     return value.astype(jnp.float32)
 
@@ -49,7 +53,7 @@
     return lax.dot_general(left, right, (dims, ((), ())), preferred_element_type=jnp.float32)
 
 
-def dense_kernel(n_row, n_col, piece, vals, rows_in, cols_in, count_in, near, rows, cols, count, sems):
+def dense_kernel(n_row, n_col, piece, sides, vals, rows_in, cols_in, count_in, near, rows, cols, count, sems):
     copies = [
         pltpu.make_async_copy(source, target, sems.at[k])
         for k, (source, target) in enumerate(((rows_in, rows), (cols_in, cols), (count_in, count)))
@@ -64,7 +68,11 @@
 
     def add(t, _):
         row, col = rows[0, 0, t], cols[0, 0, t]
-        row = lax.rem(row // piece - my_col + n_col, n_col) * piece + lax.rem(row, piece)
+        if sides:
+            place = (row // piece) ^ (2 * (my_col // 2))
+        else:
+            place = lax.rem(row // piece - my_col + n_col, n_col)
+        row = place * piece + lax.rem(row, piece)
         col = lax.rem(col // piece - my_row + n_row, n_row) * piece + lax.rem(col, piece)
         down = pl.ds(pl.multiple_of(row * side, side), side)
         across = pl.ds(pl.multiple_of(col * side, side), side)
@@ -100,26 +108,85 @@
         send[...] = product[d * rows : (d + 1) * rows].astype(send.dtype)
 
 
+def layer(total, weight, cotangent):
+    high, low = split(total)
+    pre = dot(high, weight) + dot(low, weight)
+    sigma = jax.nn.sigmoid(pre)
+    grad = wide(cotangent) * sigma * (1.0 + pre * (1.0 - sigma))
+    grad_high, grad_low = split(grad)
+    across, down = ((1,), (1,)), ((0,), (0,))
+    back = dot(grad_high, weight, across) + dot(grad_low, weight, across)
+    term = dot(high, grad_high, down) + dot(low, grad_high, down) + dot(high, grad_low, down)
+    return pre, sigma, back, term
+
+
+def fill_message(message, back, term):
+    nodes, width = back.shape
+    rows = term.shape[0]
+    message[:nodes] = back.astype(message.dtype)
+    for k in range(term.shape[1] // width):
+        start = nodes + k * rows
+        message[start : start + rows] = term[:, k * width : (k + 1) * width].astype(message.dtype)
+
+
 def layer_kernel(*refs):
     *parts, weight, cotangent, message, pre_out = refs
-    nodes = cotangent.shape[0]
     total = tree([wide(part[...]) for part in parts])
-    high, low = split(total)
-    pre = dot(high, weight[...]) + dot(low, weight[...])
+    pre, _, back, term = layer(total, weight[...], cotangent[...])
     pre_out[...] = pre
-    sigma = jax.nn.sigmoid(pre)
-    grad = wide(cotangent[...]) * sigma * (1.0 + pre * (1.0 - sigma))
-    grad_high, grad_low = split(grad)
-    across = ((1,), (1,))
-    back = dot(grad_high, weight[...], across) + dot(grad_low, weight[...], across)
-    message[:nodes] = back.astype(message.dtype)
-    down = ((0,), (0,))
-    term = dot(high, grad_high, down) + dot(low, grad_high, down) + dot(high, grad_low, down)
-    half = message.shape[1]
-    rows = total.shape[1]
-    for k in range(term.shape[1] // half):
-        start = nodes + k * rows
-        message[start : start + rows] = term[:, k * half : (k + 1) * half].astype(message.dtype)
+    fill_message(message, back, term)
+
+
+def middle_forward_kernel(n, matrix, *refs):
+    operands, (own, near, far) = refs[:n], refs[n:]
+    rows = own.shape[0]
+    stacked = jnp.concatenate([operand[...] for operand in operands], axis=0)
+    product = dot(matrix[...], stacked)
+    own[...] = product[:rows]
+    near[...] = product[:rows].astype(near.dtype)
+    far[...] = product[rows:].astype(far.dtype)
+
+
+def middle_layer_kernel(own, first, second, third, weight, mine, ends, message, pre_out, act_out):
+    nodes = mine.shape[0]
+    high_side = lax.axis_index("col") >= 2
+    total = (own[...] + wide(first[...])) + (wide(second[...]) + wide(third[...]))
+    cotangent = jnp.concatenate(
+        [
+            jnp.where(high_side, mine[...], ends[...]),
+            jnp.where(high_side, ends[...], mine[...]),
+        ],
+        axis=0,
+    )
+    pre, sigma, back, term = layer(total, weight[...], cotangent)
+    fill_message(message, back, term)
+    act = pre * sigma
+    pre_out[...] = jnp.where(high_side, pre[:nodes], pre[nodes:])
+    act_out[...] = jnp.where(high_side, act[nodes:], act[:nodes]).astype(act_out.dtype)
+
+
+def middle_backward_kernel(matrix, mine, beside, across, beyond, *refs):
+    own, kept, *sends = refs
+    rows = own.shape[0]
+    my_col = lax.axis_index("col")
+    middle = (my_col == 1) | (my_col == 2)
+    near = jnp.where(middle, mine[...], beside[...])
+    far = jnp.where(middle, across[...], beyond[...])
+    backs = 2 * rows
+    product = dot(matrix[...], jnp.concatenate([near[:backs], far[:backs]], axis=0))
+    own[...] = product[:rows]
+    term = (wide(near[backs:]) + wide(far[backs:])).astype(kept.dtype)
+    kept[...] = term
+    for d, target in enumerate(sends, 1):
+        target[:rows] = product[d * rows : (d + 1) * rows].astype(target.dtype)
+        target[rows:] = term
+
+
+def choose_kernel(pre, came, act):
+    my_col = lax.axis_index("col")
+    middle = (my_col == 1) | (my_col == 2)
+    mine = (pre[...] * jax.nn.sigmoid(pre[...])).astype(act.dtype)
+    act[...] = jnp.where(middle, mine, came[...])
 
 
 def act_kernel(pre, act):
@@ -159,9 +226,14 @@
     down, across = n_col * nodes, n_row * nodes
     dense_bytes = 2 * down * across
 
+    sides = n_col == 4
     gathered = exchange([features] * (n_row - 1), "row", False)
+    if sides:
+        inward, outward = [(0, 1), (3, 2)], [(1, 0), (2, 3)]
+        swapped = [(1, 2), (2, 1)]
+        ends = send(cotangent, "col", inward)
     (near,) = call(
-        functools.partial(dense_kernel, n_row, n_col, nodes // side),
+        functools.partial(dense_kernel, n_row, n_col, nodes // side, sides),
         [((down, across), NARROW)],
         [VMEM] * 4,
         scratch=[
@@ -173,14 +245,27 @@
         need=2 * dense_bytes,
     )(tile_values, tile_rows, tile_cols, tile_count)
 
-    own, *sends = call(
-        functools.partial(forward_kernel, n_row),
-        [((nodes, width), jnp.float32)] + [((nodes, width), NARROW)] * (n_col - 1),
-        [VMEM] * (1 + n_row),
-        flops=2 * down * across * width,
-        need=2 * dense_bytes,
-    )(near, features, *gathered)
-    parts = exchange(sends, "col", True)
+    stacked = hidden // width * width
+    message = ((nodes + stacked, width), NARROW)
+    forward = dict(flops=2 * down * across * width, need=2 * dense_bytes)
+    if sides:
+        pair = (2 * nodes, width)
+        own, mine, other = call(
+            functools.partial(middle_forward_kernel, n_row),
+            [(pair, jnp.float32), (pair, NARROW), (pair, NARROW)],
+            [VMEM] * (1 + n_row),
+            **forward,
+        )(near, features, *gathered)
+        beyond = send(other, "col", [(0, 2), (3, 1)])
+        parts = [send(mine, "col", inward), send(other, "col", swapped), beyond]
+    else:
+        own, *sends = call(
+            functools.partial(forward_kernel, n_row),
+            [((nodes, width), jnp.float32)] + [((nodes, width), NARROW)] * (n_col - 1),
+            [VMEM] * (1 + n_row),
+            **forward,
+        )(near, features, *gathered)
+        parts = exchange(sends, "col", True)
     (far,) = call(
         functools.partial(turn_kernel, side),
         [((across, down), NARROW)],
@@ -188,25 +273,40 @@
         need=3 * dense_bytes,
     )(near)
 
-    stacked = hidden // width * width
-    message = ((nodes + stacked, width), NARROW)
-    sent, pre = call(
-        layer_kernel,
-        [message, ((nodes, hidden), jnp.float32)],
-        [VMEM] * (n_col + 2),
-        flops=14 * nodes * width * hidden,
-        after=[far],
-    )(own, *parts, weight, cotangent)
-    spread = exchange([sent] * (n_col - 1), "col", False)
-    (act,) = call(act_kernel, [((nodes, hidden), NARROW)], [VMEM])(pre)
-
-    own, kept, *sends = call(
-        functools.partial(backward_kernel, n_col),
-        [((nodes, width), jnp.float32), ((stacked, width), NARROW)] + [message] * (n_row - 1),
-        [VMEM] * (1 + n_col),
-        flops=2 * down * across * width,
-        need=2 * dense_bytes,
-    )(far, sent, *spread)
+    results = [((nodes, width), jnp.float32), ((stacked, width), NARROW)] + [message] * (n_row - 1)
+    if sides:
+        sent, pre, act = call(
+            middle_layer_kernel,
+            [
+                ((2 * nodes + stacked, width), NARROW),
+                ((nodes, hidden), jnp.float32),
+                ((nodes, hidden), NARROW),
+            ],
+            [VMEM] * 7,
+            flops=28 * nodes * width * hidden,
+            after=[far],
+        )(own, *parts, weight, cotangent, ends)
+        beyond = send(sent, "col", [(2, 0), (1, 3)])
+        spread = [send(sent, "col", outward), send(sent, "col", swapped), beyond]
+        (act,) = call(choose_kernel, [((nodes, hidden), NARROW)], [VMEM] * 2)(
+            pre, send(act, "col", outward)
+        )
+        own, kept, *sends = call(
+            middle_backward_kernel, results, [VMEM] * 5, **forward
+        )(far, sent, *spread)
+    else:
+        sent, pre = call(
+            layer_kernel,
+            [message, ((nodes, hidden), jnp.float32)],
+            [VMEM] * (n_col + 2),
+            flops=14 * nodes * width * hidden,
+            after=[far],
+        )(own, *parts, weight, cotangent)
+        spread = exchange([sent] * (n_col - 1), "col", False)
+        (act,) = call(act_kernel, [((nodes, hidden), NARROW)], [VMEM])(pre)
+        own, kept, *sends = call(
+            functools.partial(backward_kernel, n_col), results, [VMEM] * (1 + n_col), **forward
+        )(far, sent, *spread)
     parts = exchange(sends, "row", True)
 
     scale = float(nodes * n_row * n_col) ** -0.5

time: 33.8 us -> 40.8 us (1.21)
  the two profiles are of different devices: /device:TPU:1 before, /device:TPU:0 now
where the time goes in v7:
time: 40.8 us; the launch traced here: 40.4 us
  starting transfers between devices  18.3 us (45%)
  waiting for transfers between devices  16.2 us (40%)
  Pallas kernels  3.49 us (9%)
  between operations  1.49 us (4%)
  local copies, waits for them, and re-layouts  1.03 us (3%)
    ppermute x8, waiting for transfers between devices, send(): return lax.ppermute(value, axis, pairs)  16.2 us
    ppermute x8, starting transfers between devices, send(): return lax.ppermute(value, axis, pairs)  12.4 us
    ppermute x6, starting transfers between devices, exchange(): lax.ppermute(send, axis, [(s, (s + (d if ahead else -d)) % n) for s in ra...  5.87 us
    unnamed x12, local copies, waits for them, and re-layouts  1.03 us
  transfers between devices with their start and end apart: 14, of which 4 were waited for; matrix products, arithmetic and copies ran while one was open for 0% of the time, Pallas kernels for 5%

profile of v7, /device:TPU:0, one launch (start us, length us, event | category | flops | bytes accessed | tf_op | source)
XLA Modules:
  0.0 40.4 jit_solution(8937586231567813614)
XLA Ops:
  0.6 0.0 copy-start.5
  0.6 0.0 copy-start.4
  0.7 3.0 %collective-permute-start.1 = (bf16[128,128]{1,0:T(8,128)(2,1)}, bf16[128,128]{1,0:T(8,128)(2,1)S(1)}, u32[]{:S(2)}, u32[]{:S(2)}) collective-permute-start(bf16[128,128]{1,0:T(8,128)(2,1)} %refs_0_.1), channel_id=1, source_target_pairs={{0,8},{4,12},{8,0},{12,4},{1,9},{5,13},{9,1},{13,5},{2,10},{6,14},... | collective-permute-start | bytes 98312 | tf_op jit(solution)/shard_map/ppermute | solution.py:34
  3.7 0.0 collective-permute-start
  3.7 0.5 %collective-permute-start.2 = (bf16[128,128]{1,0:T(8,128)(2,1)}, bf16[128,128]{1,0:T(8,128)(2,1)S(1)}, u32[]{:S(2)}, u32[]{:S(2)}) collective-permute-start(bf16[128,128]{1,0:T(8,128)(2,1)} %refs_0_.1), channel_id=1, source_target_pairs={{0,4},{4,8},{8,12},{12,0},{1,5},{5,9},{9,13},{13,1},{2,6},{6,10},{... | collective-permute-start | bytes 98312 | tf_op jit(solution)/shard_map/ppermute | solution.py:34
  4.2 3.5 %collective-permute-start.6 = (bf16[128,256]{1,0:T(8,128)(2,1)}, bf16[128,256]{1,0:T(8,128)(2,1)S(1)}, u32[]{:S(2)}, u32[]{:S(2)}) collective-permute-start(bf16[128,256]{1,0:T(8,128)(2,1)} %refs_6_.1), channel_id=1, source_target_pairs={{0,1},{3,2},{4,5},{7,6},{8,9},{11,10},{12,13},{15,14},{16,17},{19,... | collective-permute-start | bytes 196616 | tf_op jit(solution)/shard_map/ppermute | solution.py:40
  8.3 0.0 copy-done.5
  8.3 0.0 copy-done.4
  8.3 0.0 copy-start
  8.3 0.9 %copy-done = bf16[1,1,8,128,128]{4,3,2,1,0:T(8,128)(2,1)S(1)} copy-done((bf16[1,1,8,128,128]{4,3,2,1,0:T(8,128)(2,1)S(1)}, bf16[1,1,8,128,128]{4,3,2,1,0:T(8,128)(2,1)}, u32[]{:S(2)}) %copy-start) | copy-done | bytes 262168
  9.3 0.0 copy-start.3
  9.3 0.7 %shard_map.94.near.matrix = bf16[512,512]{1,0:T(8,128)(2,1)S(1)} custom-call(bf16[1,1,8,128,128]{4,3,2,1,0:T(8,128)(2,1)S(1)} %copy-done, s32[1,1,8]{2,1,0:T(1,128)S(1)} %copy-done.4, s32[1,1,8]{2,1,0:T(1,128)S(1)} %copy-done.5, s32[1,1]{1,0:T(1,128)S(6)} %copy.10.count_in), custom_call_target="tpu_custom_call" | custom-call | bytes 1048576 | tf_op jit(solution)/shard_map/pallas_call | solution.py:235
  9.9 0.0 collective-permute-done.1.refs_2_
  9.9 0.0 collective-permute-done.refs_1_
  9.9 0.0 collective-permute-done.2.refs_3_
  10.0 0.1 copy-done.3
  10.0 0.3 shard_map.96
  10.3 1.3 %collective-permute-start.3 = (bf16[256,128]{1,0:T(8,128)(2,1)S(1)}, bf16[256,128]{1,0:T(8,128)(2,1)S(1)}, u32[]{:S(2)}, u32[]{:S(2)}) collective-permute-start(bf16[256,128]{1,0:T(8,128)(2,1)S(1)} %get-tuple-element.17), channel_id=1, source_target_pairs={{0,1},{3,2},{4,5},{7,6},{8,9},{11,10},{12,13},{15,14},{16,17},{19,... | collective-permute-start | bytes 196616 | tf_op jit(solution)/shard_map/ppermute | solution.py:40
  11.6 0.0 copy-start.1
  11.6 0.0 copy-start.2
  11.6 2.4 %collective-permute-start.5 = (bf16[256,128]{1,0:T(8,128)(2,1)S(1)}, bf16[256,128]{1,0:T(8,128)(2,1)S(1)}, u32[]{:S(2)}, u32[]{:S(2)}) collective-permute-start(bf16[256,128]{1,0:T(8,128)(2,1)S(1)} %get-tuple-element.18), channel_id=1, source_target_pairs={{0,2},{3,1},{4,6},{7,5},{8,10},{11,9},{12,14},{15,13},{16,18},{19,... | collective-permute-start | bytes 196616 | tf_op jit(solution)/shard_map/ppermute | solution.py:40
  14.1 0.7 %collective-permute-start.4 = (bf16[256,128]{1,0:T(8,128)(2,1)S(1)}, bf16[256,128]{1,0:T(8,128)(2,1)S(1)}, u32[]{:S(2)}, u32[]{:S(2)}) collective-permute-start(bf16[256,128]{1,0:T(8,128)(2,1)S(1)} %get-tuple-element.18), channel_id=1, source_target_pairs={{1,2},{2,1},{5,6},{6,5},{9,10},{10,9},{13,14},{14,13},{17,18},{18,... | collective-permute-start | bytes 196616 | tf_op jit(solution)/shard_map/ppermute | solution.py:40
  14.8 0.3 shard_map.95.refs_0_.matrix
  15.1 0.0 collective-permute-done.6.refs_7_
  15.1 0.0 collective-permute-done.3.refs_2_
  15.1 1.2 %collective-permute-done.5.refs_4_ = bf16[256,128]{1,0:T(8,128)(2,1)S(1)} collective-permute-done((bf16[256,128]{1,0:T(8,128)(2,1)S(1)}, bf16[256,128]{1,0:T(8,128)(2,1)S(1)}, u32[]{:S(2)}, u32[]{:S(2)}) %collective-permute-start.5) | collective-permute-done | bytes 65568 | tf_op jit(solution)/shard_map/ppermute | solution.py:40
  16.4 0.0 collective-permute-done.4.refs_3_
  16.4 0.0 copy-done.1
  16.4 0.0 copy-done.2
  16.4 0.5 %shard_map.97 = (bf16[512,128]{1,0:T(8,128)(2,1)S(1)}, f32[128,256]{1,0:T(8,128)S(1)}, bf16[128,256]{1,0:T(8,128)(2,1)S(1)}) custom-call(bf16[512,512]{1,0:T(8,128)(2,1)S(1)} %shard_map.95.refs_0_.matrix, f32[256,128]{1,0:T(8,128)S(1)} %get-tuple-element.16.refs_1_, bf16[256,128]{1,0:T(8,128)(2,1)S(1)} %collective-permute-done.3.refs_2_, ...), custom_call_target="tpu_custom_call" | custom-call | flops 117440512 | tf_op jit(solution)/shard_map/pallas_call | solution.py:278
  16.9 1.3 %collective-permute-start.10 = (bf16[512,128]{1,0:T(8,128)(2,1)S(1)}, bf16[512,128]{1,0:T(8,128)(2,1)S(1)}, u32[]{:S(2)}, u32[]{:S(2)}) collective-permute-start(bf16[512,128]{1,0:T(8,128)(2,1)S(1)} %get-tuple-element.21.mine), channel_id=1, source_target_pairs={{2,0},{1,3},{6,4},{5,7},{10,8},{9,11},{14,12},{13,15},{18,16},{17,... | collective-permute-start | bytes 393224 | tf_op jit(solution)/shard_map/ppermute | solution.py:40
  18.2 0.7 %collective-permute-start.9 = (bf16[512,128]{1,0:T(8,128)(2,1)S(1)}, bf16[512,128]{1,0:T(8,128)(2,1)S(1)}, u32[]{:S(2)}, u32[]{:S(2)}) collective-permute-start(bf16[512,128]{1,0:T(8,128)(2,1)S(1)} %get-tuple-element.21.mine), channel_id=1, source_target_pairs={{1,2},{2,1},{5,6},{6,5},{9,10},{10,9},{13,14},{14,13},{17,18},{18,... | collective-permute-start | bytes 393224 | tf_op jit(solution)/shard_map/ppermute | solution.py:40
  18.9 1.3 %collective-permute-start.8 = (bf16[512,128]{1,0:T(8,128)(2,1)S(1)}, bf16[512,128]{1,0:T(8,128)(2,1)S(1)}, u32[]{:S(2)}, u32[]{:S(2)}) collective-permute-start(bf16[512,128]{1,0:T(8,128)(2,1)S(1)} %get-tuple-element.21.mine), channel_id=1, source_target_pairs={{1,0},{2,3},{5,4},{6,7},{9,8},{10,11},{13,12},{14,15},{17,16},{18,... | collective-permute-start | bytes 393224 | tf_op jit(solution)/shard_map/ppermute | solution.py:40
  20.2 7.1 %collective-permute-done.10.beyond = bf16[512,128]{1,0:T(8,128)(2,1)S(1)} collective-permute-done((bf16[512,128]{1,0:T(8,128)(2,1)S(1)}, bf16[512,128]{1,0:T(8,128)(2,1)S(1)}, u32[]{:S(2)}, u32[]{:S(2)}) %collective-permute-start.10) | collective-permute-done | bytes 131104 | tf_op jit(solution)/shard_map/ppermute | solution.py:40
  27.3 0.0 collective-permute-done.9.across
  27.3 3.0 %collective-permute-done.8.beside = bf16[512,128]{1,0:T(8,128)(2,1)S(1)} collective-permute-done((bf16[512,128]{1,0:T(8,128)(2,1)S(1)}, bf16[512,128]{1,0:T(8,128)(2,1)S(1)}, u32[]{:S(2)}, u32[]{:S(2)}) %collective-permute-start.8) | collective-permute-done | bytes 131104 | tf_op jit(solution)/shard_map/ppermute | solution.py:40
  30.2 0.3 shard_map.99
  30.5 0.1 collective-permute-start.11
  30.6 0.9 %collective-permute-start.12 = (bf16[384,128]{1,0:T(8,128)(2,1)S(1)}, bf16[384,128]{1,0:T(8,128)(2,1)S(1)}, u32[]{:S(2)}, u32[]{:S(2)}) collective-permute-start(bf16[384,128]{1,0:T(8,128)(2,1)S(1)} %get-tuple-element.25), channel_id=1, source_target_pairs={{0,8},{4,12},{8,0},{12,4},{1,9},{5,13},{9,1},{13,5},{2,10},{6,14},... | collective-permute-start | bytes 294920 | tf_op jit(solution)/shard_map/ppermute | solution.py:34
  31.5 1.4 %collective-permute-start.13 = (bf16[384,128]{1,0:T(8,128)(2,1)S(1)}, bf16[384,128]{1,0:T(8,128)(2,1)S(1)}, u32[]{:S(2)}, u32[]{:S(2)}) collective-permute-start(bf16[384,128]{1,0:T(8,128)(2,1)S(1)} %get-tuple-element.26), channel_id=1, source_target_pairs={{0,12},{4,0},{8,4},{12,8},{1,13},{5,1},{9,5},{13,9},{2,14},{6,2},{... | collective-permute-start | bytes 294920 | tf_op jit(solution)/shard_map/ppermute | solution.py:34
  32.9 1.3 %collective-permute-start.7 = (bf16[128,256]{1,0:T(8,128)(2,1)S(1)}, bf16[128,256]{1,0:T(8,128)(2,1)S(1)}, u32[]{:S(2)}, u32[]{:S(2)}) collective-permute-start(bf16[128,256]{1,0:T(8,128)(2,1)S(1)} %get-tuple-element.20), channel_id=1, source_target_pairs={{1,0},{2,3},{5,4},{6,7},{9,8},{10,11},{13,12},{14,15},{17,16},{18,... | collective-permute-start | bytes 196616 | tf_op jit(solution)/shard_map/ppermute | solution.py:40
  34.2 4.9 %collective-permute-done.7.came = bf16[128,256]{1,0:T(8,128)(2,1)S(1)} collective-permute-done((bf16[128,256]{1,0:T(8,128)(2,1)S(1)}, bf16[128,256]{1,0:T(8,128)(2,1)S(1)}, u32[]{:S(2)}, u32[]{:S(2)}) %collective-permute-start.7) | collective-permute-done | bytes 65568 | tf_op jit(solution)/shard_map/ppermute | solution.py:40
  39.1 0.7 %shard_map.98 = bf16[128,256]{1,0:T(8,128)(2,1)} custom-call(f32[128,256]{1,0:T(8,128)S(1)} %get-tuple-element.19.pre, bf16[128,256]{1,0:T(8,128)(2,1)S(1)} %collective-permute-done.7.came), custom_call_target="tpu_custom_call" | custom-call | tf_op jit(solution)/shard_map/pallas_call | solution.py:291
  39.7 0.0 collective-permute-done.11.refs_0_
  39.7 0.0 collective-permute-done.12.refs_1_
  39.7 0.0 collective-permute-done.13.refs_2_
  39.7 0.7 %shard_map.100 = (bf16[128,128]{1,0:T(8,128)(2,1)}, f32[128,256]{1,0:T(8,128)}) custom-call(f32[128,128]{1,0:T(8,128)S(1)} %get-tuple-element.22.own, bf16[256,128]{1,0:T(8,128)(2,1)S(1)} %get-tuple-element.23.kept, bf16[384,128]{1,0:T(8,128)(2,1)S(1)} %collective-permute-done.11.refs_0_, bf16[384,128]{1,0:T(8,128)(2,1)S(1)} %collective-permute-done.12.refs_1_, ...), custom_call_target="tpu_custom_call" | custom-call | tf_op jit(solution)/shard_map/pallas_call | solution.py:313
Async XLA Ops:
  0.6 7.7 %copy-start.5 = (s32[1,1,8]{2,1,0:T(1,128)S(1)}, s32[1,1,8]{2,1,0:T(1,128)}, u32[]{:S(2)}) copy-start(s32[1,1,8]{2,1,0:T(1,128)} %cols_in.1) | copy-start | bytes 100
  0.6 7.7 %copy-start.4 = (s32[1,1,8]{2,1,0:T(1,128)S(1)}, s32[1,1,8]{2,1,0:T(1,128)}, u32[]{:S(2)}) copy-start(s32[1,1,8]{2,1,0:T(1,128)} %rows_in.1) | copy-start | bytes 100
  0.7 9.3 %collective-permute-start.1 = (bf16[128,128]{1,0:T(8,128)(2,1)}, bf16[128,128]{1,0:T(8,128)(2,1)S(1)}, u32[]{:S(2)}, u32[]{:S(2)}) collective-permute-start(bf16[128,128]{1,0:T(8,128)(2,1)} %refs_0_.1), channel_id=1, source_target_pairs={{0,8},{4,12},{8,0},{12,4},{1,9},{5,13},{9,1},{13,5},{2,10},{6,14},... | collective-permute-start | bytes 98312 | tf_op jit(solution)/shard_map/ppermute | solution.py:34
  3.7 6.3 %collective-permute-start = (bf16[128,128]{1,0:T(8,128)(2,1)}, bf16[128,128]{1,0:T(8,128)(2,1)S(1)}, u32[]{:S(2)}, u32[]{:S(2)}) collective-permute-start(bf16[128,128]{1,0:T(8,128)(2,1)} %refs_0_.1), channel_id=1, source_target_pairs={{0,12},{4,0},{8,4},{12,8},{1,13},{5,1},{9,5},{13,9},{2,14},{6,2},{... | collective-permute-start | bytes 98312 | tf_op jit(solution)/shard_map/ppermute | solution.py:34
  3.7 6.3 %collective-permute-start.2 = (bf16[128,128]{1,0:T(8,128)(2,1)}, bf16[128,128]{1,0:T(8,128)(2,1)S(1)}, u32[]{:S(2)}, u32[]{:S(2)}) collective-permute-start(bf16[128,128]{1,0:T(8,128)(2,1)} %refs_0_.1), channel_id=1, source_target_pairs={{0,4},{4,8},{8,12},{12,0},{1,5},{5,9},{9,13},{13,1},{2,6},{6,10},{... | collective-permute-start | bytes 98312 | tf_op jit(solution)/shard_map/ppermute | solution.py:34
  4.2 10.9 %collective-permute-start.6 = (bf16[128,256]{1,0:T(8,128)(2,1)}, bf16[128,256]{1,0:T(8,128)(2,1)S(1)}, u32[]{:S(2)}, u32[]{:S(2)}) collective-permute-start(bf16[128,256]{1,0:T(8,128)(2,1)} %refs_6_.1), channel_id=1, source_target_pairs={{0,1},{3,2},{4,5},{7,6},{8,9},{11,10},{12,13},{15,14},{16,17},{19,... | collective-permute-start | bytes 196616 | tf_op jit(solution)/shard_map/ppermute | solution.py:40
  8.3 1.0 %copy-start = (bf16[1,1,8,128,128]{4,3,2,1,0:T(8,128)(2,1)S(1)}, bf16[1,1,8,128,128]{4,3,2,1,0:T(8,128)(2,1)}, u32[]{:S(2)}) copy-start(bf16[1,1,8,128,128]{4,3,2,1,0:T(8,128)(2,1)} %vals.1) | copy-start | bytes 786436
  9.3 0.8 %copy-start.3 = (bf16[128,128]{1,0:T(8,128)(2,1)S(1)}, bf16[128,128]{1,0:T(8,128)(2,1)}, u32[]{:S(2)}) copy-start(bf16[128,128]{1,0:T(8,128)(2,1)} %refs_0_.1) | copy-start | bytes 98308
  10.3 4.8 %collective-permute-start.3 = (bf16[256,128]{1,0:T(8,128)(2,1)S(1)}, bf16[256,128]{1,0:T(8,128)(2,1)S(1)}, u32[]{:S(2)}, u32[]{:S(2)}) collective-permute-start(bf16[256,128]{1,0:T(8,128)(2,1)S(1)} %get-tuple-element.17), channel_id=1, source_target_pairs={{0,1},{3,2},{4,5},{7,6},{8,9},{11,10},{12,13},{15,14},{16,17},{19,... | collective-permute-start | bytes 196616 | tf_op jit(solution)/shard_map/ppermute | solution.py:40
  11.6 4.8 %copy-start.1 = (bf16[128,256]{1,0:T(8,128)(2,1)S(1)}, bf16[128,256]{1,0:T(8,128)(2,1)}, u32[]{:S(2)}) copy-start(bf16[128,256]{1,0:T(8,128)(2,1)} %refs_5_.1) | copy-start | bytes 196612
  11.6 4.8 %copy-start.2 = (bf16[128,256]{1,0:T(8,128)(2,1)S(1)}, bf16[128,256]{1,0:T(8,128)(2,1)}, u32[]{:S(2)}) copy-start(bf16[128,256]{1,0:T(8,128)(2,1)} %refs_6_.1) | copy-start | bytes 196612
  11.6 4.7 %collective-permute-start.5 = (bf16[256,128]{1,0:T(8,128)(2,1)S(1)}, bf16[256,128]{1,0:T(8,128)(2,1)S(1)}, u32[]{:S(2)}, u32[]{:S(2)}) collective-permute-start(bf16[256,128]{1,0:T(8,128)(2,1)S(1)} %get-tuple-element.18), channel_id=1, source_target_pairs={{0,2},{3,1},{4,6},{7,5},{8,10},{11,9},{12,14},{15,13},{16,18},{19,... | collective-permute-start | bytes 196616 | tf_op jit(solution)/shard_map/ppermute | solution.py:40
  14.1 2.3 %collective-permute-start.4 = (bf16[256,128]{1,0:T(8,128)(2,1)S(1)}, bf16[256,128]{1,0:T(8,128)(2,1)S(1)}, u32[]{:S(2)}, u32[]{:S(2)}) collective-permute-start(bf16[256,128]{1,0:T(8,128)(2,1)S(1)} %get-tuple-element.18), channel_id=1, source_target_pairs={{1,2},{2,1},{5,6},{6,5},{9,10},{10,9},{13,14},{14,13},{17,18},{18,... | collective-permute-start | bytes 196616 | tf_op jit(solution)/shard_map/ppermute | solution.py:40
  16.9 10.3 %collective-permute-start.10 = (bf16[512,128]{1,0:T(8,128)(2,1)S(1)}, bf16[512,128]{1,0:T(8,128)(2,1)S(1)}, u32[]{:S(2)}, u32[]{:S(2)}) collective-permute-start(bf16[512,128]{1,0:T(8,128)(2,1)S(1)} %get-tuple-element.21.mine), channel_id=1, source_target_pairs={{2,0},{1,3},{6,4},{5,7},{10,8},{9,11},{14,12},{13,15},{18,16},{17,... | collective-permute-start | bytes 393224 | tf_op jit(solution)/shard_map/ppermute | solution.py:40
  18.2 9.0 %collective-permute-start.9 = (bf16[512,128]{1,0:T(8,128)(2,1)S(1)}, bf16[512,128]{1,0:T(8,128)(2,1)S(1)}, u32[]{:S(2)}, u32[]{:S(2)}) collective-permute-start(bf16[512,128]{1,0:T(8,128)(2,1)S(1)} %get-tuple-element.21.mine), channel_id=1, source_target_pairs={{1,2},{2,1},{5,6},{6,5},{9,10},{10,9},{13,14},{14,13},{17,18},{18,... | collective-permute-start | bytes 393224 | tf_op jit(solution)/shard_map/ppermute | solution.py:40
  18.9 11.3 %collective-permute-start.8 = (bf16[512,128]{1,0:T(8,128)(2,1)S(1)}, bf16[512,128]{1,0:T(8,128)(2,1)S(1)}, u32[]{:S(2)}, u32[]{:S(2)}) collective-permute-start(bf16[512,128]{1,0:T(8,128)(2,1)S(1)} %get-tuple-element.21.mine), channel_id=1, source_target_pairs={{1,0},{2,3},{5,4},{6,7},{9,8},{10,11},{13,12},{14,15},{17,16},{18,... | collective-permute-start | bytes 393224 | tf_op jit(solution)/shard_map/ppermute | solution.py:40
  30.5 9.2 %collective-permute-start.11 = (bf16[384,128]{1,0:T(8,128)(2,1)S(1)}, bf16[384,128]{1,0:T(8,128)(2,1)S(1)}, u32[]{:S(2)}, u32[]{:S(2)}) collective-permute-start(bf16[384,128]{1,0:T(8,128)(2,1)S(1)} %get-tuple-element.24), channel_id=1, source_target_pairs={{0,4},{4,8},{8,12},{12,0},{1,5},{5,9},{9,13},{13,1},{2,6},{6,10},{... | collective-permute-start | bytes 294920 | tf_op jit(solution)/shard_map/ppermute | solution.py:34
  30.6 9.1 %collective-permute-start.12 = (bf16[384,128]{1,0:T(8,128)(2,1)S(1)}, bf16[384,128]{1,0:T(8,128)(2,1)S(1)}, u32[]{:S(2)}, u32[]{:S(2)}) collective-permute-start(bf16[384,128]{1,0:T(8,128)(2,1)S(1)} %get-tuple-element.25), channel_id=1, source_target_pairs={{0,8},{4,12},{8,0},{12,4},{1,9},{5,13},{9,1},{13,5},{2,10},{6,14},... | collective-permute-start | bytes 294920 | tf_op jit(solution)/shard_map/ppermute | solution.py:34
  31.5 8.2 %collective-permute-start.13 = (bf16[384,128]{1,0:T(8,128)(2,1)S(1)}, bf16[384,128]{1,0:T(8,128)(2,1)S(1)}, u32[]{:S(2)}, u32[]{:S(2)}) collective-permute-start(bf16[384,128]{1,0:T(8,128)(2,1)S(1)} %get-tuple-element.26), channel_id=1, source_target_pairs={{0,12},{4,0},{8,4},{12,8},{1,13},{5,1},{9,5},{13,9},{2,14},{6,2},{... | collective-permute-start | bytes 294920 | tf_op jit(solution)/shard_map/ppermute | solution.py:34
  32.9 6.1 %collective-permute-start.7 = (bf16[128,256]{1,0:T(8,128)(2,1)S(1)}, bf16[128,256]{1,0:T(8,128)(2,1)S(1)}, u32[]{:S(2)}, u32[]{:S(2)}) collective-permute-start(bf16[128,256]{1,0:T(8,128)(2,1)S(1)} %get-tuple-element.20), channel_id=1, source_target_pairs={{1,0},{2,3},{5,4},{6,7},{9,8},{10,11},{13,12},{14,15},{17,16},{18,... | collective-permute-start | bytes 196616 | tf_op jit(solution)/shard_map/ppermute | solution.py:40

commit v8 on v6

--- a/solution.py
+++ b/solution.py
@@ -36,6 +36,13 @@
     ]
 
 
+def meet(own, axis):
+    n = lax.axis_size(axis)
+    return [own] + [
+        lax.ppermute(own, axis, [(s, s ^ d) for s in range(n)]) for d in range(n - 1, 0, -1)
+    ]
+
+
 def wide(value):
     return value.astype(jnp.float32)
 
@@ -65,7 +72,8 @@
     def add(t, _):
         row, col = rows[0, 0, t], cols[0, 0, t]
         row = lax.rem(row // piece - my_col + n_col, n_col) * piece + lax.rem(row, piece)
-        col = lax.rem(col // piece - my_row + n_row, n_row) * piece + lax.rem(col, piece)
+        place = lax.rem(n_row - ((col // piece) ^ my_row), n_row)
+        col = place * piece + lax.rem(col, piece)
         down = pl.ds(pl.multiple_of(row * side, side), side)
         across = pl.ds(pl.multiple_of(col * side, side), side)
         near[down, across] = vals[0, 0, t]
@@ -126,29 +134,29 @@
     act[...] = (pre[...] * jax.nn.sigmoid(pre[...])).astype(act.dtype)
 
 
-def backward_kernel(n, matrix, *refs):
-    messages, own, kept, sends = refs[:n], refs[n], refs[n + 1], refs[n + 2 :]
-    rows = own.shape[0]
+def backward_kernel(n, n_out, matrix, *refs):
+    messages, out = refs[:n], refs[n]
+    rows = matrix.shape[0] // n_out
+    size = messages[0].shape[0]
     stacked = jnp.concatenate([message[:rows] for message in messages], axis=0)
     product = dot(matrix[...], stacked)
-    own[...] = product[:rows]
-    term = tree([wide(message[rows:]) for message in messages]).astype(kept.dtype)
-    kept[...] = term
-    for d, send in enumerate(sends, 1):
-        send[:rows] = product[d * rows : (d + 1) * rows].astype(send.dtype)
-        send[rows:] = term
-
-
-def last_kernel(scale, own, kept, *refs):
-    *messages, features_out, weight_out = refs
-    nodes = own.shape[0]
-    rows, half = weight_out.shape[0], kept.shape[1]
-    features_out[...] = tree(
-        [own[...]] + [wide(message[:nodes]) for message in messages]
-    ).astype(features_out.dtype)
-    total = tree([wide(kept[...])] + [wide(message[nodes:]) for message in messages]) * scale
+    term = tree([wide(message[rows:]) for message in messages]).astype(out.dtype)
+    my_row = lax.axis_index("row")
+    for d in range(n_out):
+        start = pl.multiple_of((my_row ^ ((n_out - d) % n_out)) * size, size)
+        out[pl.ds(start, rows)] = product[d * rows : (d + 1) * rows].astype(out.dtype)
+        out[pl.ds(pl.multiple_of(start + rows, rows), size - rows)] = term
+
+
+def last_kernel(n, scale, messages, features_out, weight_out):
+    size = messages.shape[0] // n
+    nodes, rows = features_out.shape[0], weight_out.shape[0]
+    half = messages.shape[1]
+    total = tree([wide(messages[k * size : (k + 1) * size]) for k in range(n)])
+    features_out[...] = total[:nodes].astype(features_out.dtype)
     for k in range(weight_out.shape[1] // half):
-        weight_out[:, k * half : (k + 1) * half] = total[k * rows : (k + 1) * rows]
+        start = nodes + k * rows
+        weight_out[:, k * half : (k + 1) * half] = total[start : start + rows] * scale
 
 
 def per_device(features, weight, cotangent, tile_values, tile_rows, tile_cols, tile_count):
@@ -159,7 +167,7 @@
     down, across = n_col * nodes, n_row * nodes
     dense_bytes = 2 * down * across
 
-    gathered = exchange([features] * (n_row - 1), "row", False)
+    gathered = meet(features, "row")
     (near,) = call(
         functools.partial(dense_kernel, n_row, n_col, nodes // side),
         [((down, across), NARROW)],
@@ -179,7 +187,7 @@
         [VMEM] * (1 + n_row),
         flops=2 * down * across * width,
         need=2 * dense_bytes,
-    )(near, features, *gathered)
+    )(near, *gathered)
     parts = exchange(sends, "col", True)
     (far,) = call(
         functools.partial(turn_kernel, side),
@@ -200,21 +208,21 @@
     spread = exchange([sent] * (n_col - 1), "col", False)
     (act,) = call(act_kernel, [((nodes, hidden), NARROW)], [VMEM])(pre)
 
-    own, kept, *sends = call(
-        functools.partial(backward_kernel, n_col),
-        [((nodes, width), jnp.float32), ((stacked, width), NARROW)] + [message] * (n_row - 1),
+    (sends,) = call(
+        functools.partial(backward_kernel, n_col, n_row),
+        [((n_row * message[0][0], width), NARROW)],
         [VMEM] * (1 + n_col),
         flops=2 * down * across * width,
         need=2 * dense_bytes,
     )(far, sent, *spread)
-    parts = exchange(sends, "row", True)
+    parts = lax.all_to_all(sends, "row", 0, 0, tiled=True)
 
     scale = float(nodes * n_row * n_col) ** -0.5
     grad_features, grad_weight = call(
-        functools.partial(last_kernel, scale),
+        functools.partial(last_kernel, n_row, scale),
         [((nodes, width), NARROW), ((width, hidden), jnp.float32)],
-        [VMEM] * (n_row + 1),
-    )(own, kept, *parts)
+        [VMEM],
+    )(parts)
     return act, grad_features, grad_weight
 
 

time: 33.8 us -> 38.7 us (1.14)
  the two profiles are of different devices: /device:TPU:1 before, /device:TPU:0 now
where the time goes in v8:
time: 38.7 us; the launch traced here: 38.5 us
  starting transfers between devices  16.1 us (42%)
  waiting for transfers between devices  15.9 us (41%)
  Pallas kernels  4.14 us (11%)
  between operations  1.39 us (4%)
  local copies, waits for them, and re-layouts  0.96 us (2%)
    ppermute x6, starting transfers between devices, exchange(): lax.ppermute(send, axis, [(s, (s + (d if ahead else -d)) % n) for s in ra...  9.47 us
    ppermute x6, waiting for transfers between devices, exchange(): lax.ppermute(send, axis, [(s, (s + (d if ahead else -d)) % n) for s in ra...  7.98 us
    all_to_all x1, waiting for transfers between devices, per_device(): parts = lax.all_to_all(sends, 'row', 0, 0, tiled=True)  6.75 us
    all_to_all x1, starting transfers between devices, per_device(): parts = lax.all_to_all(sends, 'row', 0, 0, tiled=True)  3.46 us
    ppermute x3, starting transfers between devices, meet(): lax.ppermute(own, axis, [(s, s ^ d) for s in range(n)])  3.2 us
    ppermute x3, waiting for transfers between devices, meet(): lax.ppermute(own, axis, [(s, s ^ d) for s in range(n)])  1.14 us
    pallas_call x1, Pallas kernels, per_device(): call(functools.partial(backward_kernel, n_col, n_row), [((n_row * message...  1.07 us
    unnamed x12, local copies, waits for them, and re-layouts  0.96 us
  transfers between devices with their start and end apart: 10, of which 6 were waited for; matrix products, arithmetic and copies ran while one was open for 0% of the time, Pallas kernels for 4%

profile of v8, /device:TPU:0, one launch (start us, length us, event | category | flops | bytes accessed | tf_op | source)
XLA Modules:
  0.0 38.5 jit_solution(8106984024661637531)
XLA Ops:
  0.6 0.0 copy-start.5
  0.6 0.0 copy-start.4
  0.7 3.0 %collective-permute-start.1 = (bf16[128,128]{1,0:T(8,128)(2,1)}, bf16[128,128]{1,0:T(8,128)(2,1)S(1)}, u32[]{:S(2)}, u32[]{:S(2)}) collective-permute-start(bf16[128,128]{1,0:T(8,128)(2,1)} %refs_0_.1), channel_id=1, source_target_pairs={{0,8},{4,12},{8,0},{12,4},{1,9},{5,13},{9,1},{13,5},{2,10},{6,14},... | collective-permute-start | bytes 98312 | tf_op jit(solution)/shard_map/ppermute | solution.py:42
  3.7 0.0 collective-permute-start
  3.7 0.2 collective-permute-start.2
  4.5 0.0 copy-done.5
  4.5 0.0 copy-done.4
  4.5 0.0 copy-start
  4.5 0.9 %copy-done = bf16[1,1,8,128,128]{4,3,2,1,0:T(8,128)(2,1)S(1)} copy-done((bf16[1,1,8,128,128]{4,3,2,1,0:T(8,128)(2,1)S(1)}, bf16[1,1,8,128,128]{4,3,2,1,0:T(8,128)(2,1)}, u32[]{:S(2)}) %copy-start) | copy-done | bytes 262168
  5.5 0.0 copy-start.3
  5.5 0.7 %shard_map.94.near.matrix = bf16[512,512]{1,0:T(8,128)(2,1)S(1)} custom-call(bf16[1,1,8,128,128]{4,3,2,1,0:T(8,128)(2,1)S(1)} %copy-done, s32[1,1,8]{2,1,0:T(1,128)S(1)} %copy-done.4, s32[1,1,8]{2,1,0:T(1,128)S(1)} %copy-done.5, s32[1,1]{1,0:T(1,128)S(6)} %copy.10.count_in), custom_call_target="tpu_custom_call" | custom-call | bytes 1048576 | tf_op jit(solution)/shard_map/pallas_call | solution.py:171
  6.1 0.0 collective-permute-done.1.refs_2_
  6.2 1.1 %collective-permute-done.refs_1_ = bf16[128,128]{1,0:T(8,128)(2,1)S(1)} collective-permute-done((bf16[128,128]{1,0:T(8,128)(2,1)}, bf16[128,128]{1,0:T(8,128)(2,1)S(1)}, u32[]{:S(2)}, u32[]{:S(2)}) %collective-permute-start) | collective-permute-done | bytes 32800 | tf_op jit(solution)/shard_map/ppermute | solution.py:42
  7.3 0.0 collective-permute-done.2.refs_3_
  7.3 0.0 copy-done.3
  7.3 0.3 shard_map.96
  7.6 1.6 %collective-permute-start.3 = (bf16[128,128]{1,0:T(8,128)(2,1)S(1)}, bf16[128,128]{1,0:T(8,128)(2,1)S(1)}, u32[]{:S(2)}, u32[]{:S(2)}) collective-permute-start(bf16[128,128]{1,0:T(8,128)(2,1)S(1)} %get-tuple-element.12), channel_id=1, source_target_pairs={{0,1},{1,2},{2,3},{3,0},{4,5},{5,6},{6,7},{7,4},{8,9},{9,10},{10,1... | collective-permute-start | bytes 98312 | tf_op jit(solution)/shard_map/ppermute | solution.py:34
  9.2 2.6 %collective-permute-start.4 = (bf16[128,128]{1,0:T(8,128)(2,1)S(1)}, bf16[128,128]{1,0:T(8,128)(2,1)S(1)}, u32[]{:S(2)}, u32[]{:S(2)}) collective-permute-start(bf16[128,128]{1,0:T(8,128)(2,1)S(1)} %get-tuple-element.13), channel_id=1, source_target_pairs={{0,2},{1,3},{2,0},{3,1},{4,6},{5,7},{6,4},{7,5},{8,10},{9,11},{10,... | collective-permute-start | bytes 98312 | tf_op jit(solution)/shard_map/ppermute | solution.py:34
  11.8 0.0 copy-start.1
  11.8 0.0 copy-start.2
  11.8 1.4 %collective-permute-start.5 = (bf16[128,128]{1,0:T(8,128)(2,1)S(1)}, bf16[128,128]{1,0:T(8,128)(2,1)S(1)}, u32[]{:S(2)}, u32[]{:S(2)}) collective-permute-start(bf16[128,128]{1,0:T(8,128)(2,1)S(1)} %get-tuple-element.14), channel_id=1, source_target_pairs={{0,3},{1,0},{2,1},{3,2},{4,7},{5,4},{6,5},{7,6},{8,11},{9,8},{10,9... | collective-permute-start | bytes 98312 | tf_op jit(solution)/shard_map/ppermute | solution.py:34
  13.2 0.3 shard_map.95.refs_0_.matrix
  13.5 0.0 collective-permute-done.3.refs_2_
  13.5 0.9 %collective-permute-done.4.refs_3_ = bf16[128,128]{1,0:T(8,128)(2,1)S(1)} collective-permute-done((bf16[128,128]{1,0:T(8,128)(2,1)S(1)}, bf16[128,128]{1,0:T(8,128)(2,1)S(1)}, u32[]{:S(2)}, u32[]{:S(2)}) %collective-permute-start.4) | collective-permute-done | bytes 32800 | tf_op jit(solution)/shard_map/ppermute | solution.py:34
  14.4 1.3 %collective-permute-done.5.refs_4_ = bf16[128,128]{1,0:T(8,128)(2,1)S(1)} collective-permute-done((bf16[128,128]{1,0:T(8,128)(2,1)S(1)}, bf16[128,128]{1,0:T(8,128)(2,1)S(1)}, u32[]{:S(2)}, u32[]{:S(2)}) %collective-permute-start.5) | collective-permute-done | bytes 32800 | tf_op jit(solution)/shard_map/ppermute | solution.py:34
  15.7 0.0 copy-done.1
  15.7 0.0 copy-done.2
  15.7 0.4 %shard_map.97 = (bf16[384,128]{1,0:T(8,128)(2,1)S(1)}, f32[128,256]{1,0:T(8,128)S(1)}) custom-call(bf16[512,512]{1,0:T(8,128)(2,1)S(1)} %shard_map.95.refs_0_.matrix, f32[128,128]{1,0:T(8,128)S(1)} %get-tuple-element.11.refs_1_, bf16[128,128]{1,0:T(8,128)(2,1)S(1)} %collective-permute-done.3.refs_2_, bf16[128,128]{1,0:T(8,128)(2,1)S(1)} %collective-permute-done.4.refs_3_, ...), custom_call_target="tpu_custom_call" | custom-call | flops 58720256 | tf_op jit(solution)/shard_map/pallas_call | solution.py:201
  16.1 0.3 collective-permute-start.8
  16.4 3.5 %collective-permute-start.7 = (bf16[384,128]{1,0:T(8,128)(2,1)S(1)}, bf16[384,128]{1,0:T(8,128)(2,1)S(1)}, u32[]{:S(2)}, u32[]{:S(2)}) collective-permute-start(bf16[384,128]{1,0:T(8,128)(2,1)S(1)} %get-tuple-element.16.refs_0_), channel_id=1, source_target_pairs={{0,2},{1,3},{2,0},{3,1},{4,6},{5,7},{6,4},{7,5},{8,10},{9,11},{10,... | collective-permute-start | bytes 294920 | tf_op jit(solution)/shard_map/ppermute | solution.py:34
  19.9 0.1 collective-permute-start.6
  20.1 3.6 %collective-permute-done.8.refs_3_ = bf16[384,128]{1,0:T(8,128)(2,1)S(1)} collective-permute-done((bf16[384,128]{1,0:T(8,128)(2,1)S(1)}, bf16[384,128]{1,0:T(8,128)(2,1)S(1)}, u32[]{:S(2)}, u32[]{:S(2)}) %collective-permute-start.8) | collective-permute-done | bytes 98336 | tf_op jit(solution)/shard_map/ppermute | solution.py:34
  23.6 2.2 %collective-permute-done.7.refs_2_ = bf16[384,128]{1,0:T(8,128)(2,1)S(1)} collective-permute-done((bf16[384,128]{1,0:T(8,128)(2,1)S(1)}, bf16[384,128]{1,0:T(8,128)(2,1)S(1)}, u32[]{:S(2)}, u32[]{:S(2)}) %collective-permute-start.7) | collective-permute-done | bytes 98336 | tf_op jit(solution)/shard_map/ppermute | solution.py:34
  25.8 0.0 collective-permute-done.6.refs_1_
  25.8 1.1 %shard_map.99 = bf16[1536,128]{1,0:T(8,128)(2,1)} custom-call(bf16[512,512]{1,0:T(8,128)(2,1)S(1)} %shard_map.95.refs_0_.matrix, bf16[384,128]{1,0:T(8,128)(2,1)S(1)} %get-tuple-element.16.refs_0_, bf16[384,128]{1,0:T(8,128)(2,1)S(1)} %collective-permute-done.6.refs_1_, bf16[384,128]{1,0:T(8,128)(2,1)S(1)} %collective-permute-done.7.refs_2_, ...), custom_call_target="tpu_custom_call" | custom-call | flops 67108864 | bytes 1048576 | tf_op jit(solution)/shard_map/pallas_call | solution.py:211
  26.9 3.5 %all-to-all-start = ((bf16[4,384,128]{2,1,0:T(8,128)(2,1)}), bf16[4,384,128]{2,1,0:T(8,128)(2,1)S(1)}, u32[]{:S(2)}, u32[]{:S(2)}) async-start(bf16[4,384,128]{2,1,0:T(8,128)(2,1)} %bitcast), calls=%async_computation | async-start | bytes 786432 | tf_op jit(solution)/shard_map/all_to_all | solution.py:218
  30.4 0.7 %shard_map.98 = bf16[128,256]{1,0:T(8,128)(2,1)} custom-call(f32[128,256]{1,0:T(8,128)S(1)} %get-tuple-element.15.pre), custom_call_target="tpu_custom_call" | custom-call | tf_op jit(solution)/shard_map/pallas_call | solution.py:209
  31.0 6.8 %all-to-all-done = bf16[4,384,128]{2,1,0:T(8,128)(2,1)S(1)} async-done(((bf16[4,384,128]{2,1,0:T(8,128)(2,1)}), bf16[4,384,128]{2,1,0:T(8,128)(2,1)S(1)}, u32[]{:S(2)}, u32[]{:S(2)}) %all-to-all-start) | async-done | bytes 393248 | tf_op jit(solution)/shard_map/all_to_all | solution.py:218
  37.8 0.7 %shard_map.100 = (bf16[128,128]{1,0:T(8,128)(2,1)}, f32[128,256]{1,0:T(8,128)}) custom-call(bf16[1536,128]{1,0:T(8,128)(2,1)S(1)} %bitcast.2), custom_call_target="tpu_custom_call" | custom-call | tf_op jit(solution)/shard_map/pallas_call | solution.py:221
Async XLA Ops:
  0.6 3.9 %copy-start.5 = (s32[1,1,8]{2,1,0:T(1,128)S(1)}, s32[1,1,8]{2,1,0:T(1,128)}, u32[]{:S(2)}) copy-start(s32[1,1,8]{2,1,0:T(1,128)} %cols_in.1) | copy-start | bytes 100
  0.6 3.9 %copy-start.4 = (s32[1,1,8]{2,1,0:T(1,128)S(1)}, s32[1,1,8]{2,1,0:T(1,128)}, u32[]{:S(2)}) copy-start(s32[1,1,8]{2,1,0:T(1,128)} %rows_in.1) | copy-start | bytes 100
  0.7 5.5 %collective-permute-start.1 = (bf16[128,128]{1,0:T(8,128)(2,1)}, bf16[128,128]{1,0:T(8,128)(2,1)S(1)}, u32[]{:S(2)}, u32[]{:S(2)}) collective-permute-start(bf16[128,128]{1,0:T(8,128)(2,1)} %refs_0_.1), channel_id=1, source_target_pairs={{0,8},{4,12},{8,0},{12,4},{1,9},{5,13},{9,1},{13,5},{2,10},{6,14},... | collective-permute-start | bytes 98312 | tf_op jit(solution)/shard_map/ppermute | solution.py:42
  3.7 3.6 %collective-permute-start = (bf16[128,128]{1,0:T(8,128)(2,1)}, bf16[128,128]{1,0:T(8,128)(2,1)S(1)}, u32[]{:S(2)}, u32[]{:S(2)}) collective-permute-start(bf16[128,128]{1,0:T(8,128)(2,1)} %refs_0_.1), channel_id=1, source_target_pairs={{0,12},{4,8},{8,4},{12,0},{1,13},{5,9},{9,5},{13,1},{2,14},{6,10},... | collective-permute-start | bytes 98312 | tf_op jit(solution)/shard_map/ppermute | solution.py:42
  3.7 3.6 %collective-permute-start.2 = (bf16[128,128]{1,0:T(8,128)(2,1)}, bf16[128,128]{1,0:T(8,128)(2,1)S(1)}, u32[]{:S(2)}, u32[]{:S(2)}) collective-permute-start(bf16[128,128]{1,0:T(8,128)(2,1)} %refs_0_.1), channel_id=1, source_target_pairs={{0,4},{4,0},{8,12},{12,8},{1,5},{5,1},{9,13},{13,9},{2,6},{6,2},{1... | collective-permute-start | bytes 98312 | tf_op jit(solution)/shard_map/ppermute | solution.py:42
  4.5 1.0 %copy-start = (bf16[1,1,8,128,128]{4,3,2,1,0:T(8,128)(2,1)S(1)}, bf16[1,1,8,128,128]{4,3,2,1,0:T(8,128)(2,1)}, u32[]{:S(2)}) copy-start(bf16[1,1,8,128,128]{4,3,2,1,0:T(8,128)(2,1)} %vals.1) | copy-start | bytes 786436
  5.5 1.8 %copy-start.3 = (bf16[128,128]{1,0:T(8,128)(2,1)S(1)}, bf16[128,128]{1,0:T(8,128)(2,1)}, u32[]{:S(2)}) copy-start(bf16[128,128]{1,0:T(8,128)(2,1)} %refs_0_.1) | copy-start | bytes 98308
  7.6 5.9 %collective-permute-start.3 = (bf16[128,128]{1,0:T(8,128)(2,1)S(1)}, bf16[128,128]{1,0:T(8,128)(2,1)S(1)}, u32[]{:S(2)}, u32[]{:S(2)}) collective-permute-start(bf16[128,128]{1,0:T(8,128)(2,1)S(1)} %get-tuple-element.12), channel_id=1, source_target_pairs={{0,1},{1,2},{2,3},{3,0},{4,5},{5,6},{6,7},{7,4},{8,9},{9,10},{10,1... | collective-permute-start | bytes 98312 | tf_op jit(solution)/shard_map/ppermute | solution.py:34
  9.2 5.2 %collective-permute-start.4 = (bf16[128,128]{1,0:T(8,128)(2,1)S(1)}, bf16[128,128]{1,0:T(8,128)(2,1)S(1)}, u32[]{:S(2)}, u32[]{:S(2)}) collective-permute-start(bf16[128,128]{1,0:T(8,128)(2,1)S(1)} %get-tuple-element.13), channel_id=1, source_target_pairs={{0,2},{1,3},{2,0},{3,1},{4,6},{5,7},{6,4},{7,5},{8,10},{9,11},{10,... | collective-permute-start | bytes 98312 | tf_op jit(solution)/shard_map/ppermute | solution.py:34
  11.8 3.9 %copy-start.1 = (bf16[128,256]{1,0:T(8,128)(2,1)S(1)}, bf16[128,256]{1,0:T(8,128)(2,1)}, u32[]{:S(2)}) copy-start(bf16[128,256]{1,0:T(8,128)(2,1)} %refs_5_.1) | copy-start | bytes 196612
  11.8 3.9 %copy-start.2 = (bf16[128,256]{1,0:T(8,128)(2,1)S(1)}, bf16[128,256]{1,0:T(8,128)(2,1)}, u32[]{:S(2)}) copy-start(bf16[128,256]{1,0:T(8,128)(2,1)} %refs_6_.1) | copy-start | bytes 196612
  11.8 3.9 %collective-permute-start.5 = (bf16[128,128]{1,0:T(8,128)(2,1)S(1)}, bf16[128,128]{1,0:T(8,128)(2,1)S(1)}, u32[]{:S(2)}, u32[]{:S(2)}) collective-permute-start(bf16[128,128]{1,0:T(8,128)(2,1)S(1)} %get-tuple-element.14), channel_id=1, source_target_pairs={{0,3},{1,0},{2,1},{3,2},{4,7},{5,4},{6,5},{7,6},{8,11},{9,8},{10,9... | collective-permute-start | bytes 98312 | tf_op jit(solution)/shard_map/ppermute | solution.py:34
  16.1 7.5 %collective-permute-start.8 = (bf16[384,128]{1,0:T(8,128)(2,1)S(1)}, bf16[384,128]{1,0:T(8,128)(2,1)S(1)}, u32[]{:S(2)}, u32[]{:S(2)}) collective-permute-start(bf16[384,128]{1,0:T(8,128)(2,1)S(1)} %get-tuple-element.16.refs_0_), channel_id=1, source_target_pairs={{0,1},{1,2},{2,3},{3,0},{4,5},{5,6},{6,7},{7,4},{8,9},{9,10},{10,1... | collective-permute-start | bytes 294920 | tf_op jit(solution)/shard_map/ppermute | solution.py:34
  16.4 9.4 %collective-permute-start.7 = (bf16[384,128]{1,0:T(8,128)(2,1)S(1)}, bf16[384,128]{1,0:T(8,128)(2,1)S(1)}, u32[]{:S(2)}, u32[]{:S(2)}) collective-permute-start(bf16[384,128]{1,0:T(8,128)(2,1)S(1)} %get-tuple-element.16.refs_0_), channel_id=1, source_target_pairs={{0,2},{1,3},{2,0},{3,1},{4,6},{5,7},{6,4},{7,5},{8,10},{9,11},{10,... | collective-permute-start | bytes 294920 | tf_op jit(solution)/shard_map/ppermute | solution.py:34
  19.9 5.9 %collective-permute-start.6 = (bf16[384,128]{1,0:T(8,128)(2,1)S(1)}, bf16[384,128]{1,0:T(8,128)(2,1)S(1)}, u32[]{:S(2)}, u32[]{:S(2)}) collective-permute-start(bf16[384,128]{1,0:T(8,128)(2,1)S(1)} %get-tuple-element.16.refs_0_), channel_id=1, source_target_pairs={{0,3},{1,0},{2,1},{3,2},{4,7},{5,4},{6,5},{7,6},{8,11},{9,8},{10,9... | collective-permute-start | bytes 294920 | tf_op jit(solution)/shard_map/ppermute | solution.py:34
  26.9 10.9 %all-to-all-start = ((bf16[4,384,128]{2,1,0:T(8,128)(2,1)}), bf16[4,384,128]{2,1,0:T(8,128)(2,1)S(1)}, u32[]{:S(2)}, u32[]{:S(2)}) async-start(bf16[4,384,128]{2,1,0:T(8,128)(2,1)} %bitcast), calls=%async_computation | async-start | bytes 786432 | tf_op jit(solution)/shard_map/all_to_all | solution.py:218

commit v9 on v6

--- a/solution.py
+++ b/solution.py
@@ -34,6 +34,11 @@
         lax.ppermute(send, axis, [(s, (s + (d if ahead else -d)) % n) for s in range(n)])
         for d, send in enumerate(sends, 1)
     ]
+
+
+def neighbour(value, axis):
+    n = lax.axis_size(axis)
+    return lax.ppermute(value, axis, [(s, s ^ 1) for s in range(n)])
 
 
 def wide(value):
@@ -101,8 +106,8 @@
 
 
 def layer_kernel(*refs):
-    *parts, weight, cotangent, message, pre_out = refs
-    nodes = cotangent.shape[0]
+    *parts, weight, cotangent, back, mine, other, pre_out = refs
+    half = mine.shape[1]
     total = tree([wide(part[...]) for part in parts])
     high, low = split(total)
     pre = dot(high, weight[...]) + dot(low, weight[...])
@@ -110,16 +115,22 @@
     sigma = jax.nn.sigmoid(pre)
     grad = wide(cotangent[...]) * sigma * (1.0 + pre * (1.0 - sigma))
     grad_high, grad_low = split(grad)
-    across = ((1,), (1,))
-    back = dot(grad_high, weight[...], across) + dot(grad_low, weight[...], across)
-    message[:nodes] = back.astype(message.dtype)
     down = ((0,), (0,))
     term = dot(high, grad_high, down) + dot(low, grad_high, down) + dot(high, grad_low, down)
-    half = message.shape[1]
-    rows = total.shape[1]
-    for k in range(term.shape[1] // half):
-        start = nodes + k * rows
-        message[start : start + rows] = term[:, k * half : (k + 1) * half].astype(message.dtype)
+    odd = lax.rem(lax.axis_index("row"), 2) == 1
+    left, right = term[:, :half], term[:, half:]
+    mine[...] = jnp.where(odd, right, left)
+    other[...] = jnp.where(odd, left, right).astype(other.dtype)
+    across = ((1,), (1,))
+    back[...] = (dot(grad_high, weight[...], across) + dot(grad_low, weight[...], across)).astype(
+        back.dtype
+    )
+
+
+def message_kernel(back, mine, came, message):
+    nodes = back.shape[0]
+    message[:nodes] = back[...]
+    message[nodes:] = (mine[...] + wide(came[...])).astype(message.dtype)
 
 
 def act_kernel(pre, act):
@@ -141,14 +152,15 @@
 
 def last_kernel(scale, own, kept, *refs):
     *messages, features_out, weight_out = refs
-    nodes = own.shape[0]
-    rows, half = weight_out.shape[0], kept.shape[1]
+    nodes, half = own.shape[0], kept.shape[1]
     features_out[...] = tree(
         [own[...]] + [wide(message[:nodes]) for message in messages]
     ).astype(features_out.dtype)
-    total = tree([wide(kept[...])] + [wide(message[nodes:]) for message in messages]) * scale
-    for k in range(weight_out.shape[1] // half):
-        weight_out[:, k * half : (k + 1) * half] = total[k * rows : (k + 1) * rows]
+    terms = [wide(kept[...])] + [wide(message[nodes:]) for message in messages]
+    mine, other = tree(terms[::2]) * scale, tree(terms[1::2]) * scale
+    odd = lax.rem(lax.axis_index("row"), 2) == 1
+    weight_out[:, :half] = jnp.where(odd, other, mine)
+    weight_out[:, half:] = jnp.where(odd, mine, other)
 
 
 def per_device(features, weight, cotangent, tile_values, tile_rows, tile_cols, tile_count):
@@ -188,21 +200,28 @@
         need=3 * dense_bytes,
     )(near)
 
-    stacked = hidden // width * width
-    message = ((nodes + stacked, width), NARROW)
-    sent, pre = call(
+    half = hidden // 2
+    square = (width, half)
+    message = ((nodes + width, width), NARROW)
+    back, mine, other, pre = call(
         layer_kernel,
-        [message, ((nodes, hidden), jnp.float32)],
+        [
+            ((nodes, width), NARROW),
+            (square, jnp.float32),
+            (square, NARROW),
+            ((nodes, hidden), jnp.float32),
+        ],
         [VMEM] * (n_col + 2),
         flops=14 * nodes * width * hidden,
         after=[far],
     )(own, *parts, weight, cotangent)
+    (sent,) = call(message_kernel, [message], [VMEM] * 3)(back, mine, neighbour(other, "row"))
     spread = exchange([sent] * (n_col - 1), "col", False)
     (act,) = call(act_kernel, [((nodes, hidden), NARROW)], [VMEM])(pre)
 
     own, kept, *sends = call(
         functools.partial(backward_kernel, n_col),
-        [((nodes, width), jnp.float32), ((stacked, width), NARROW)] + [message] * (n_row - 1),
+        [((nodes, width), jnp.float32), (square, NARROW)] + [message] * (n_row - 1),
         [VMEM] * (1 + n_col),
         flops=2 * down * across * width,
         need=2 * dense_bytes,

time: 33.8 us -> 32.9 us (0.973)
  the two profiles are of different devices: /device:TPU:1 before, /device:TPU:0 now
where the time goes in v9:
time: 32.9 us; the launch traced here: 32.4 us
  starting transfers between devices  16 us (49%)
  waiting for transfers between devices  10.7 us (33%)
  Pallas kernels  3.36 us (10%)
  between operations  1.41 us (4%)
  local copies, waits for them, and re-layouts  0.96 us (3%)
    ppermute x12, starting transfers between devices, exchange(): lax.ppermute(send, axis, [(s, (s + (d if ahead else -d)) % n) for s in ra...  15.9 us
    ppermute x12, waiting for transfers between devices, exchange(): lax.ppermute(send, axis, [(s, (s + (d if ahead else -d)) % n) for s in ra...  9.54 us
    ppermute x1, waiting for transfers between devices, neighbour(): return lax.ppermute(value, axis, [(s, s ^ 1) for s in range(n)])  1.19 us
    unnamed x12, local copies, waits for them, and re-layouts  0.96 us
    pallas_call x1, Pallas kernels, per_device(): call(functools.partial(last_kernel, scale), [((nodes, width), NARROW), ((...  0.7 us
  transfers between devices with their start and end apart: 13, of which 9 were waited for; matrix products, arithmetic and copies ran while one was open for 0% of the time, Pallas kernels for 5%

profile of v9, /device:TPU:0, one launch (start us, length us, event | category | flops | bytes accessed | tf_op | source)
XLA Modules:
  0.0 32.4 jit_solution(14193961097994089572)
XLA Ops:
  0.6 0.0 copy-start.5
  0.6 0.0 copy-start.4
  0.7 3.0 %collective-permute-start.1 = (bf16[128,128]{1,0:T(8,128)(2,1)}, bf16[128,128]{1,0:T(8,128)(2,1)S(1)}, u32[]{:S(2)}, u32[]{:S(2)}) collective-permute-start(bf16[128,128]{1,0:T(8,128)(2,1)} %refs_0_.1), channel_id=1, source_target_pairs={{0,8},{4,12},{8,0},{12,4},{1,9},{5,13},{9,1},{13,5},{2,10},{6,14},... | collective-permute-start | bytes 98312 | tf_op jit(solution)/shard_map/ppermute | solution.py:34
  3.7 0.0 collective-permute-start
  3.7 0.5 %collective-permute-start.2 = (bf16[128,128]{1,0:T(8,128)(2,1)}, bf16[128,128]{1,0:T(8,128)(2,1)S(1)}, u32[]{:S(2)}, u32[]{:S(2)}) collective-permute-start(bf16[128,128]{1,0:T(8,128)(2,1)} %refs_0_.1), channel_id=1, source_target_pairs={{0,4},{4,8},{8,12},{12,0},{1,5},{5,9},{9,13},{13,1},{2,6},{6,10},{... | collective-permute-start | bytes 98312 | tf_op jit(solution)/shard_map/ppermute | solution.py:34
  4.8 0.0 copy-done.5
  4.8 0.0 copy-done.4
  4.8 0.0 copy-start
  4.8 0.9 %copy-done = bf16[1,1,8,128,128]{4,3,2,1,0:T(8,128)(2,1)S(1)} copy-done((bf16[1,1,8,128,128]{4,3,2,1,0:T(8,128)(2,1)S(1)}, bf16[1,1,8,128,128]{4,3,2,1,0:T(8,128)(2,1)}, u32[]{:S(2)}) %copy-start) | copy-done | bytes 262168
  5.8 0.0 copy-start.3
  5.8 0.6 %shard_map.94.near.matrix = bf16[512,512]{1,0:T(8,128)(2,1)S(1)} custom-call(bf16[1,1,8,128,128]{4,3,2,1,0:T(8,128)(2,1)S(1)} %copy-done, s32[1,1,8]{2,1,0:T(1,128)S(1)} %copy-done.4, s32[1,1,8]{2,1,0:T(1,128)S(1)} %copy-done.5, s32[1,1]{1,0:T(1,128)S(6)} %copy.10.count_in), custom_call_target="tpu_custom_call" | custom-call | bytes 1048576 | tf_op jit(solution)/shard_map/pallas_call | solution.py:175
  6.4 0.0 collective-permute-done.1.refs_2_
  6.4 0.0 collective-permute-done.refs_1_
  6.5 0.8 %collective-permute-done.2.refs_3_ = bf16[128,128]{1,0:T(8,128)(2,1)S(1)} collective-permute-done((bf16[128,128]{1,0:T(8,128)(2,1)}, bf16[128,128]{1,0:T(8,128)(2,1)S(1)}, u32[]{:S(2)}, u32[]{:S(2)}) %collective-permute-start.2) | collective-permute-done | bytes 32800 | tf_op jit(solution)/shard_map/ppermute | solution.py:34
  7.3 0.0 copy-done.3
  7.3 0.3 shard_map.96
  7.6 1.6 %collective-permute-start.3 = (bf16[128,128]{1,0:T(8,128)(2,1)S(1)}, bf16[128,128]{1,0:T(8,128)(2,1)S(1)}, u32[]{:S(2)}, u32[]{:S(2)}) collective-permute-start(bf16[128,128]{1,0:T(8,128)(2,1)S(1)} %get-tuple-element.19), channel_id=1, source_target_pairs={{0,1},{1,2},{2,3},{3,0},{4,5},{5,6},{6,7},{7,4},{8,9},{9,10},{10,1... | collective-permute-start | bytes 98312 | tf_op jit(solution)/shard_map/ppermute | solution.py:34
  9.2 2.6 %collective-permute-start.4 = (bf16[128,128]{1,0:T(8,128)(2,1)S(1)}, bf16[128,128]{1,0:T(8,128)(2,1)S(1)}, u32[]{:S(2)}, u32[]{:S(2)}) collective-permute-start(bf16[128,128]{1,0:T(8,128)(2,1)S(1)} %get-tuple-element.20), channel_id=1, source_target_pairs={{0,2},{1,3},{2,0},{3,1},{4,6},{5,7},{6,4},{7,5},{8,10},{9,11},{10,... | collective-permute-start | bytes 98312 | tf_op jit(solution)/shard_map/ppermute | solution.py:34
  11.8 0.0 copy-start.1
  11.8 0.0 copy-start.2
  11.8 1.3 %collective-permute-start.5 = (bf16[128,128]{1,0:T(8,128)(2,1)S(1)}, bf16[128,128]{1,0:T(8,128)(2,1)S(1)}, u32[]{:S(2)}, u32[]{:S(2)}) collective-permute-start(bf16[128,128]{1,0:T(8,128)(2,1)S(1)} %get-tuple-element.21), channel_id=1, source_target_pairs={{0,3},{1,0},{2,1},{3,2},{4,7},{5,4},{6,5},{7,6},{8,11},{9,8},{10,9... | collective-permute-start | bytes 98312 | tf_op jit(solution)/shard_map/ppermute | solution.py:34
  13.2 0.3 %shard_map.95.refs_0_.matrix = bf16[512,512]{1,0:T(8,128)(2,1)S(1)} custom-call(bf16[512,512]{1,0:T(8,128)(2,1)S(1)} %shard_map.94.near.matrix), custom_call_target="tpu_custom_call" | custom-call | bytes 1572864 | tf_op jit(solution)/shard_map/pallas_call | solution.py:196
  13.5 0.0 collective-permute-done.3.refs_2_
  13.5 1.0 %collective-permute-done.4.refs_3_ = bf16[128,128]{1,0:T(8,128)(2,1)S(1)} collective-permute-done((bf16[128,128]{1,0:T(8,128)(2,1)S(1)}, bf16[128,128]{1,0:T(8,128)(2,1)S(1)}, u32[]{:S(2)}, u32[]{:S(2)}) %collective-permute-start.4) | collective-permute-done | bytes 32800 | tf_op jit(solution)/shard_map/ppermute | solution.py:34
  14.5 1.2 %collective-permute-done.5.refs_4_ = bf16[128,128]{1,0:T(8,128)(2,1)S(1)} collective-permute-done((bf16[128,128]{1,0:T(8,128)(2,1)S(1)}, bf16[128,128]{1,0:T(8,128)(2,1)S(1)}, u32[]{:S(2)}, u32[]{:S(2)}) %collective-permute-start.5) | collective-permute-done | bytes 32800 | tf_op jit(solution)/shard_map/ppermute | solution.py:34
  15.7 0.0 copy-done.1
  15.7 0.0 copy-done.2
  15.7 0.4 %shard_map.97 = (bf16[128,128]{1,0:T(8,128)(2,1)S(1)}, f32[128,128]{1,0:T(8,128)S(1)}, bf16[128,128]{1,0:T(8,128)(2,1)S(1)}, f32[128,256]{1,0:T(8,128)S(1)}) custom-call(bf16[512,512]{1,0:T(8,128)(2,1)S(1)} %shard_map.95.refs_0_.matrix, f32[128,128]{1,0:T(8,128)S(1)} %get-tuple-element.18.refs_1_, bf16[128,128]{1,0:T(8,128)(2,1)S(1)} %collective-permute-done.3.refs_2_, ...), custom_call_target="tpu_custom_call" | custom-call | flops 58720256 | tf_op jit(solution)/shard_map/pallas_call | solution.py:206
  16.2 0.1 collective-permute-start.6
  16.3 1.2 %collective-permute-done.6.came = bf16[128,128]{1,0:T(8,128)(2,1)S(1)} collective-permute-done((bf16[128,128]{1,0:T(8,128)(2,1)S(1)}, bf16[128,128]{1,0:T(8,128)(2,1)S(1)}, u32[]{:S(2)}, u32[]{:S(2)}) %collective-permute-start.6) | collective-permute-done | bytes 32800 | tf_op jit(solution)/shard_map/ppermute | solution.py:41
  17.5 0.3 collective-permute-start.9
  17.8 3.5 %collective-permute-start.8 = (bf16[256,128]{1,0:T(8,128)(2,1)S(1)}, bf16[256,128]{1,0:T(8,128)(2,1)S(1)}, u32[]{:S(2)}, u32[]{:S(2)}) collective-permute-start(bf16[256,128]{1,0:T(8,128)(2,1)S(1)} %shard_map.99.refs_0_), channel_id=1, source_target_pairs={{0,2},{1,3},{2,0},{3,1},{4,6},{5,7},{6,4},{7,5},{8,10},{9,11},{10,... | collective-permute-start | bytes 196616 | tf_op jit(solution)/shard_map/ppermute | solution.py:34
  21.2 0.3 %collective-permute-start.7 = (bf16[256,128]{1,0:T(8,128)(2,1)S(1)}, bf16[256,128]{1,0:T(8,128)(2,1)S(1)}, u32[]{:S(2)}, u32[]{:S(2)}) collective-permute-start(bf16[256,128]{1,0:T(8,128)(2,1)S(1)} %shard_map.99.refs_0_), channel_id=1, source_target_pairs={{0,3},{1,0},{2,1},{3,2},{4,7},{5,4},{6,5},{7,6},{8,11},{9,8},{10,9... | collective-permute-start | bytes 196616 | tf_op jit(solution)/shard_map/ppermute | solution.py:34
  21.6 2.8 %collective-permute-done.9.refs_3_ = bf16[256,128]{1,0:T(8,128)(2,1)S(1)} collective-permute-done((bf16[256,128]{1,0:T(8,128)(2,1)S(1)}, bf16[256,128]{1,0:T(8,128)(2,1)S(1)}, u32[]{:S(2)}, u32[]{:S(2)}) %collective-permute-start.9) | collective-permute-done | bytes 65568 | tf_op jit(solution)/shard_map/ppermute | solution.py:34
  24.4 2.0 %collective-permute-done.8.refs_2_ = bf16[256,128]{1,0:T(8,128)(2,1)S(1)} collective-permute-done((bf16[256,128]{1,0:T(8,128)(2,1)S(1)}, bf16[256,128]{1,0:T(8,128)(2,1)S(1)}, u32[]{:S(2)}, u32[]{:S(2)}) %collective-permute-start.8) | collective-permute-done | bytes 65568 | tf_op jit(solution)/shard_map/ppermute | solution.py:34
  26.4 0.1 collective-permute-done.7.refs_1_
  26.5 0.3 shard_map.100
  26.8 0.1 collective-permute-start.10
  26.9 1.3 %collective-permute-start.11 = (bf16[256,128]{1,0:T(8,128)(2,1)S(1)}, bf16[256,128]{1,0:T(8,128)(2,1)S(1)}, u32[]{:S(2)}, u32[]{:S(2)}) collective-permute-start(bf16[256,128]{1,0:T(8,128)(2,1)S(1)} %get-tuple-element.29), channel_id=1, source_target_pairs={{0,8},{4,12},{8,0},{12,4},{1,9},{5,13},{9,1},{13,5},{2,10},{6,14},... | collective-permute-start | bytes 196616 | tf_op jit(solution)/shard_map/ppermute | solution.py:34
  28.1 1.4 %collective-permute-start.12 = (bf16[256,128]{1,0:T(8,128)(2,1)S(1)}, bf16[256,128]{1,0:T(8,128)(2,1)S(1)}, u32[]{:S(2)}, u32[]{:S(2)}) collective-permute-start(bf16[256,128]{1,0:T(8,128)(2,1)S(1)} %get-tuple-element.30), channel_id=1, source_target_pairs={{0,12},{4,0},{8,4},{12,8},{1,13},{5,1},{9,5},{13,9},{2,14},{6,2},{... | collective-permute-start | bytes 196616 | tf_op jit(solution)/shard_map/ppermute | solution.py:34
  29.5 0.7 %shard_map.98 = bf16[128,256]{1,0:T(8,128)(2,1)} custom-call(f32[128,256]{1,0:T(8,128)S(1)} %get-tuple-element.22.pre), custom_call_target="tpu_custom_call" | custom-call | tf_op jit(solution)/shard_map/pallas_call | solution.py:220
  30.2 0.5 %collective-permute-done.10.refs_0_ = bf16[256,128]{1,0:T(8,128)(2,1)S(1)} collective-permute-done((bf16[256,128]{1,0:T(8,128)(2,1)S(1)}, bf16[256,128]{1,0:T(8,128)(2,1)S(1)}, u32[]{:S(2)}, u32[]{:S(2)}) %collective-permute-start.10) | collective-permute-done | bytes 65568 | tf_op jit(solution)/shard_map/ppermute | solution.py:34
  30.6 1.1 %collective-permute-done.11.refs_1_ = bf16[256,128]{1,0:T(8,128)(2,1)S(1)} collective-permute-done((bf16[256,128]{1,0:T(8,128)(2,1)S(1)}, bf16[256,128]{1,0:T(8,128)(2,1)S(1)}, u32[]{:S(2)}, u32[]{:S(2)}) %collective-permute-start.11) | collective-permute-done | bytes 65568 | tf_op jit(solution)/shard_map/ppermute | solution.py:34
  31.7 0.0 collective-permute-done.12.refs_2_
  31.7 0.7 %shard_map.101 = (bf16[128,128]{1,0:T(8,128)(2,1)}, f32[128,256]{1,0:T(8,128)}) custom-call(f32[128,128]{1,0:T(8,128)S(1)} %get-tuple-element.26.own, bf16[128,128]{1,0:T(8,128)(2,1)S(1)} %get-tuple-element.27.kept, bf16[256,128]{1,0:T(8,128)(2,1)S(1)} %collective-permute-done.10.refs_0_, bf16[256,128]{1,0:T(8,128)(2,1)S(1)} %collective-permute-done.11.refs_1_, ...), custom_call_target="tpu_custom_call" | custom-call | tf_op jit(solution)/shard_map/pallas_call | solution.py:232
  (1 shorter events, 0.0 us)
Async XLA Ops:
  0.6 4.2 %copy-start.5 = (s32[1,1,8]{2,1,0:T(1,128)S(1)}, s32[1,1,8]{2,1,0:T(1,128)}, u32[]{:S(2)}) copy-start(s32[1,1,8]{2,1,0:T(1,128)} %cols_in.1) | copy-start | bytes 100
  0.6 4.2 %copy-start.4 = (s32[1,1,8]{2,1,0:T(1,128)S(1)}, s32[1,1,8]{2,1,0:T(1,128)}, u32[]{:S(2)}) copy-start(s32[1,1,8]{2,1,0:T(1,128)} %rows_in.1) | copy-start | bytes 100
  0.7 5.8 %collective-permute-start.1 = (bf16[128,128]{1,0:T(8,128)(2,1)}, bf16[128,128]{1,0:T(8,128)(2,1)S(1)}, u32[]{:S(2)}, u32[]{:S(2)}) collective-permute-start(bf16[128,128]{1,0:T(8,128)(2,1)} %refs_0_.1), channel_id=1, source_target_pairs={{0,8},{4,12},{8,0},{12,4},{1,9},{5,13},{9,1},{13,5},{2,10},{6,14},... | collective-permute-start | bytes 98312 | tf_op jit(solution)/shard_map/ppermute | solution.py:34
  3.7 2.8 %collective-permute-start = (bf16[128,128]{1,0:T(8,128)(2,1)}, bf16[128,128]{1,0:T(8,128)(2,1)S(1)}, u32[]{:S(2)}, u32[]{:S(2)}) collective-permute-start(bf16[128,128]{1,0:T(8,128)(2,1)} %refs_0_.1), channel_id=1, source_target_pairs={{0,12},{4,0},{8,4},{12,8},{1,13},{5,1},{9,5},{13,9},{2,14},{6,2},{... | collective-permute-start | bytes 98312 | tf_op jit(solution)/shard_map/ppermute | solution.py:34
  3.7 3.6 %collective-permute-start.2 = (bf16[128,128]{1,0:T(8,128)(2,1)}, bf16[128,128]{1,0:T(8,128)(2,1)S(1)}, u32[]{:S(2)}, u32[]{:S(2)}) collective-permute-start(bf16[128,128]{1,0:T(8,128)(2,1)} %refs_0_.1), channel_id=1, source_target_pairs={{0,4},{4,8},{8,12},{12,0},{1,5},{5,9},{9,13},{13,1},{2,6},{6,10},{... | collective-permute-start | bytes 98312 | tf_op jit(solution)/shard_map/ppermute | solution.py:34
  4.8 1.0 %copy-start = (bf16[1,1,8,128,128]{4,3,2,1,0:T(8,128)(2,1)S(1)}, bf16[1,1,8,128,128]{4,3,2,1,0:T(8,128)(2,1)}, u32[]{:S(2)}) copy-start(bf16[1,1,8,128,128]{4,3,2,1,0:T(8,128)(2,1)} %vals.1) | copy-start | bytes 786436
  5.8 1.5 %copy-start.3 = (bf16[128,128]{1,0:T(8,128)(2,1)S(1)}, bf16[128,128]{1,0:T(8,128)(2,1)}, u32[]{:S(2)}) copy-start(bf16[128,128]{1,0:T(8,128)(2,1)} %refs_0_.1) | copy-start | bytes 98308
  7.6 5.9 %collective-permute-start.3 = (bf16[128,128]{1,0:T(8,128)(2,1)S(1)}, bf16[128,128]{1,0:T(8,128)(2,1)S(1)}, u32[]{:S(2)}, u32[]{:S(2)}) collective-permute-start(bf16[128,128]{1,0:T(8,128)(2,1)S(1)} %get-tuple-element.19), channel_id=1, source_target_pairs={{0,1},{1,2},{2,3},{3,0},{4,5},{5,6},{6,7},{7,4},{8,9},{9,10},{10,1... | collective-permute-start | bytes 98312 | tf_op jit(solution)/shard_map/ppermute | solution.py:34
  9.2 5.3 %collective-permute-start.4 = (bf16[128,128]{1,0:T(8,128)(2,1)S(1)}, bf16[128,128]{1,0:T(8,128)(2,1)S(1)}, u32[]{:S(2)}, u32[]{:S(2)}) collective-permute-start(bf16[128,128]{1,0:T(8,128)(2,1)S(1)} %get-tuple-element.20), channel_id=1, source_target_pairs={{0,2},{1,3},{2,0},{3,1},{4,6},{5,7},{6,4},{7,5},{8,10},{9,11},{10,... | collective-permute-start | bytes 98312 | tf_op jit(solution)/shard_map/ppermute | solution.py:34
  11.8 3.9 %copy-start.1 = (bf16[128,256]{1,0:T(8,128)(2,1)S(1)}, bf16[128,256]{1,0:T(8,128)(2,1)}, u32[]{:S(2)}) copy-start(bf16[128,256]{1,0:T(8,128)(2,1)} %refs_5_.1) | copy-start | bytes 196612
  11.8 3.9 %copy-start.2 = (bf16[128,256]{1,0:T(8,128)(2,1)S(1)}, bf16[128,256]{1,0:T(8,128)(2,1)}, u32[]{:S(2)}) copy-start(bf16[128,256]{1,0:T(8,128)(2,1)} %refs_6_.1) | copy-start | bytes 196612
  11.8 3.9 %collective-permute-start.5 = (bf16[128,128]{1,0:T(8,128)(2,1)S(1)}, bf16[128,128]{1,0:T(8,128)(2,1)S(1)}, u32[]{:S(2)}, u32[]{:S(2)}) collective-permute-start(bf16[128,128]{1,0:T(8,128)(2,1)S(1)} %get-tuple-element.21), channel_id=1, source_target_pairs={{0,3},{1,0},{2,1},{3,2},{4,7},{5,4},{6,5},{7,6},{8,11},{9,8},{10,9... | collective-permute-start | bytes 98312 | tf_op jit(solution)/shard_map/ppermute | solution.py:34
  16.2 1.3 %collective-permute-start.6 = (bf16[128,128]{1,0:T(8,128)(2,1)S(1)}, bf16[128,128]{1,0:T(8,128)(2,1)S(1)}, u32[]{:S(2)}, u32[]{:S(2)}) collective-permute-start(bf16[128,128]{1,0:T(8,128)(2,1)S(1)} %get-tuple-element.25), channel_id=1, source_target_pairs={{0,4},{4,0},{8,12},{12,8},{1,5},{5,1},{9,13},{13,9},{2,6},{6,2},{1... | collective-permute-start | bytes 98312 | tf_op jit(solution)/shard_map/ppermute | solution.py:41
  17.5 6.9 %collective-permute-start.9 = (bf16[256,128]{1,0:T(8,128)(2,1)S(1)}, bf16[256,128]{1,0:T(8,128)(2,1)S(1)}, u32[]{:S(2)}, u32[]{:S(2)}) collective-permute-start(bf16[256,128]{1,0:T(8,128)(2,1)S(1)} %shard_map.99.refs_0_), channel_id=1, source_target_pairs={{0,1},{1,2},{2,3},{3,0},{4,5},{5,6},{6,7},{7,4},{8,9},{9,10},{10,1... | collective-permute-start | bytes 196616 | tf_op jit(solution)/shard_map/ppermute | solution.py:34
  17.8 8.6 %collective-permute-start.8 = (bf16[256,128]{1,0:T(8,128)(2,1)S(1)}, bf16[256,128]{1,0:T(8,128)(2,1)S(1)}, u32[]{:S(2)}, u32[]{:S(2)}) collective-permute-start(bf16[256,128]{1,0:T(8,128)(2,1)S(1)} %shard_map.99.refs_0_), channel_id=1, source_target_pairs={{0,2},{1,3},{2,0},{3,1},{4,6},{5,7},{6,4},{7,5},{8,10},{9,11},{10,... | collective-permute-start | bytes 196616 | tf_op jit(solution)/shard_map/ppermute | solution.py:34
  21.2 5.3 %collective-permute-start.7 = (bf16[256,128]{1,0:T(8,128)(2,1)S(1)}, bf16[256,128]{1,0:T(8,128)(2,1)S(1)}, u32[]{:S(2)}, u32[]{:S(2)}) collective-permute-start(bf16[256,128]{1,0:T(8,128)(2,1)S(1)} %shard_map.99.refs_0_), channel_id=1, source_target_pairs={{0,3},{1,0},{2,1},{3,2},{4,7},{5,4},{6,5},{7,6},{8,11},{9,8},{10,9... | collective-permute-start | bytes 196616 | tf_op jit(solution)/shard_map/ppermute | solution.py:34
  26.8 3.8 %collective-permute-start.10 = (bf16[256,128]{1,0:T(8,128)(2,1)S(1)}, bf16[256,128]{1,0:T(8,128)(2,1)S(1)}, u32[]{:S(2)}, u32[]{:S(2)}) collective-permute-start(bf16[256,128]{1,0:T(8,128)(2,1)S(1)} %get-tuple-element.28), channel_id=1, source_target_pairs={{0,4},{4,8},{8,12},{12,0},{1,5},{5,9},{9,13},{13,1},{2,6},{6,10},{... | collective-permute-start | bytes 196616 | tf_op jit(solution)/shard_map/ppermute | solution.py:34
  26.9 4.9 %collective-permute-start.11 = (bf16[256,128]{1,0:T(8,128)(2,1)S(1)}, bf16[256,128]{1,0:T(8,128)(2,1)S(1)}, u32[]{:S(2)}, u32[]{:S(2)}) collective-permute-start(bf16[256,128]{1,0:T(8,128)(2,1)S(1)} %get-tuple-element.29), channel_id=1, source_target_pairs={{0,8},{4,12},{8,0},{12,4},{1,9},{5,13},{9,1},{13,5},{2,10},{6,14},... | collective-permute-start | bytes 196616 | tf_op jit(solution)/shard_map/ppermute | solution.py:34
  28.1 3.6 %collective-permute-start.12 = (bf16[256,128]{1,0:T(8,128)(2,1)S(1)}, bf16[256,128]{1,0:T(8,128)(2,1)S(1)}, u32[]{:S(2)}, u32[]{:S(2)}) collective-permute-start(bf16[256,128]{1,0:T(8,128)(2,1)S(1)} %get-tuple-element.30), channel_id=1, source_target_pairs={{0,12},{4,0},{8,4},{12,8},{1,13},{5,1},{9,5},{13,9},{2,14},{6,2},{... | collective-permute-start | bytes 196616 | tf_op jit(solution)/shard_map/ppermute | solution.py:34

commit v10 on v9

--- a/solution.py
+++ b/solution.py
@@ -34,6 +34,14 @@
         lax.ppermute(send, axis, [(s, (s + (d if ahead else -d)) % n) for s in range(n)])
         for d, send in enumerate(sends, 1)
     ]
+
+
+def far_first(n, ahead):
+    return sorted(range(1, n), key=lambda d: (-min(d, n - d), d if ahead else -d))
+
+
+def in_order(arrays, offsets):
+    return [array for _, array in sorted(zip(offsets, arrays), key=lambda pair: pair[0])]
 
 
 def neighbour(value, axis):
@@ -106,7 +114,8 @@
 
 
 def layer_kernel(*refs):
-    *parts, weight, cotangent, back, mine, other, pre_out = refs
+    own, *parts, weight, cotangent, back, mine, other, pre_out = refs
+    parts = [own] + in_order(parts, far_first(len(parts) + 1, True))
     half = mine.shape[1]
     total = tree([wide(part[...]) for part in parts])
     high, low = split(total)
@@ -139,6 +148,7 @@
 
 def backward_kernel(n, matrix, *refs):
     messages, own, kept, sends = refs[:n], refs[n], refs[n + 1], refs[n + 2 :]
+    messages = messages[:1] + tuple(in_order(messages[1:], far_first(n, False)[::-1]))
     rows = own.shape[0]
     stacked = jnp.concatenate([message[:rows] for message in messages], axis=0)
     product = dot(matrix[...], stacked)
@@ -214,7 +224,7 @@
         [VMEM] * (n_col + 2),
         flops=14 * nodes * width * hidden,
         after=[far],
-    )(own, *parts, weight, cotangent)
+    )(own, *[parts[d - 1] for d in far_first(n_col, True)], weight, cotangent)
     (sent,) = call(message_kernel, [message], [VMEM] * 3)(back, mine, neighbour(other, "row"))
     spread = exchange([sent] * (n_col - 1), "col", False)
     (act,) = call(act_kernel, [((nodes, hidden), NARROW)], [VMEM])(pre)
@@ -225,7 +235,7 @@
         [VMEM] * (1 + n_col),
         flops=2 * down * across * width,
         need=2 * dense_bytes,
-    )(far, sent, *spread)
+    )(far, sent, *[spread[d - 1] for d in far_first(n_col, False)[::-1]])
     parts = exchange(sends, "row", True)
 
     scale = float(nodes * n_row * n_col) ** -0.5

time: 32.9 us -> 33.6 us (1.021)
  starting transfers between devices: 16 us -> 17.4 us
  waiting for transfers between devices: 10.7 us -> 9.91 us
    ppermute x12, starting transfers between devices: 15.9 us -> 17.4 us  [exchange(): lax.ppermute(send, axis, [(s, (s + (d if ahead else -d)) % n) for s in ra...]
    ppermute x12, waiting for transfers between devices: 9.54 us -> 8.71 us  [exchange(): lax.ppermute(send, axis, [(s, (s + (d if ahead else -d)) % n) for s in ra...]
  transfers between devices with their start and end apart: 13 -> 13, of which waited for: 9 -> 7; matrix products, arithmetic and copies ran while one was open for 0% -> 0% of each run, Pallas kernels for 5% -> 5%
where the time goes in v10:
time: 33.6 us; the launch traced here: 33.1 us
  starting transfers between devices  17.4 us (52%)
  waiting for transfers between devices  9.91 us (29%)
  Pallas kernels  3.37 us (10%)
  between operations  1.41 us (4%)
  local copies, waits for them, and re-layouts  0.96 us (3%)
    ppermute x12, starting transfers between devices, exchange(): lax.ppermute(send, axis, [(s, (s + (d if ahead else -d)) % n) for s in ra...  17.4 us
    ppermute x12, waiting for transfers between devices, exchange(): lax.ppermute(send, axis, [(s, (s + (d if ahead else -d)) % n) for s in ra...  8.71 us
    ppermute x1, waiting for transfers between devices, neighbour(): return lax.ppermute(value, axis, [(s, s ^ 1) for s in range(n)])  1.19 us
    unnamed x12, local copies, waits for them, and re-layouts  0.96 us
    pallas_call x1, Pallas kernels, per_device(): call(functools.partial(last_kernel, scale), [((nodes, width), NARROW), ((...  0.7 us
  transfers between devices with their start and end apart: 13, of which 7 were waited for; matrix products, arithmetic and copies ran while one was open for 0% of the time, Pallas kernels for 5%

profile of v10, /device:TPU:0, one launch (start us, length us, event | category | flops | bytes accessed | tf_op | source)
XLA Modules:
  0.0 33.1 jit_solution(8638780168938892715)
XLA Ops:
  0.6 0.0 copy-start.5
  0.6 0.0 copy-start.4
  0.7 3.0 %collective-permute-start.1 = (bf16[128,128]{1,0:T(8,128)(2,1)}, bf16[128,128]{1,0:T(8,128)(2,1)S(1)}, u32[]{:S(2)}, u32[]{:S(2)}) collective-permute-start(bf16[128,128]{1,0:T(8,128)(2,1)} %refs_0_.1), channel_id=1, source_target_pairs={{0,8},{4,12},{8,0},{12,4},{1,9},{5,13},{9,1},{13,5},{2,10},{6,14},... | collective-permute-start | bytes 98312 | tf_op jit(solution)/shard_map/ppermute | solution.py:34
  3.7 0.0 collective-permute-start
  3.7 0.5 %collective-permute-start.2 = (bf16[128,128]{1,0:T(8,128)(2,1)}, bf16[128,128]{1,0:T(8,128)(2,1)S(1)}, u32[]{:S(2)}, u32[]{:S(2)}) collective-permute-start(bf16[128,128]{1,0:T(8,128)(2,1)} %refs_0_.1), channel_id=1, source_target_pairs={{0,4},{4,8},{8,12},{12,0},{1,5},{5,9},{9,13},{13,1},{2,6},{6,10},{... | collective-permute-start | bytes 98312 | tf_op jit(solution)/shard_map/ppermute | solution.py:34
  4.8 0.0 copy-done.5
  4.8 0.0 copy-done.4
  4.8 0.0 copy-start
  4.8 0.9 %copy-done = bf16[1,1,8,128,128]{4,3,2,1,0:T(8,128)(2,1)S(1)} copy-done((bf16[1,1,8,128,128]{4,3,2,1,0:T(8,128)(2,1)S(1)}, bf16[1,1,8,128,128]{4,3,2,1,0:T(8,128)(2,1)}, u32[]{:S(2)}) %copy-start) | copy-done | bytes 262168
  5.8 0.0 copy-start.3
  5.8 0.7 %shard_map.94.near.matrix = bf16[512,512]{1,0:T(8,128)(2,1)S(1)} custom-call(bf16[1,1,8,128,128]{4,3,2,1,0:T(8,128)(2,1)S(1)} %copy-done, s32[1,1,8]{2,1,0:T(1,128)S(1)} %copy-done.4, s32[1,1,8]{2,1,0:T(1,128)S(1)} %copy-done.5, s32[1,1]{1,0:T(1,128)S(6)} %copy.10.count_in), custom_call_target="tpu_custom_call" | custom-call | bytes 1048576 | tf_op jit(solution)/shard_map/pallas_call | solution.py:185
  6.4 0.0 collective-permute-done.1.refs_2_
  6.5 0.0 collective-permute-done.refs_1_
  6.5 0.8 %collective-permute-done.2.refs_3_ = bf16[128,128]{1,0:T(8,128)(2,1)S(1)} collective-permute-done((bf16[128,128]{1,0:T(8,128)(2,1)}, bf16[128,128]{1,0:T(8,128)(2,1)S(1)}, u32[]{:S(2)}, u32[]{:S(2)}) %collective-permute-start.2) | collective-permute-done | bytes 32800 | tf_op jit(solution)/shard_map/ppermute | solution.py:34
  7.3 0.0 copy-done.3
  7.3 0.3 shard_map.96
  7.6 2.7 %collective-permute-start.3 = (bf16[128,128]{1,0:T(8,128)(2,1)S(1)}, bf16[128,128]{1,0:T(8,128)(2,1)S(1)}, u32[]{:S(2)}, u32[]{:S(2)}) collective-permute-start(bf16[128,128]{1,0:T(8,128)(2,1)S(1)} %get-tuple-element.19), channel_id=1, source_target_pairs={{0,2},{1,3},{2,0},{3,1},{4,6},{5,7},{6,4},{7,5},{8,10},{9,11},{10,... | collective-permute-start | bytes 98312 | tf_op jit(solution)/shard_map/ppermute | solution.py:34
  10.2 1.6 %collective-permute-start.4 = (bf16[128,128]{1,0:T(8,128)(2,1)S(1)}, bf16[128,128]{1,0:T(8,128)(2,1)S(1)}, u32[]{:S(2)}, u32[]{:S(2)}) collective-permute-start(bf16[128,128]{1,0:T(8,128)(2,1)S(1)} %get-tuple-element.20), channel_id=1, source_target_pairs={{0,1},{1,2},{2,3},{3,0},{4,5},{5,6},{6,7},{7,4},{8,9},{9,10},{10,1... | collective-permute-start | bytes 98312 | tf_op jit(solution)/shard_map/ppermute | solution.py:34
  11.8 0.0 copy-start.1
  11.8 0.0 copy-start.2
  11.8 2.2 %collective-permute-start.5 = (bf16[128,128]{1,0:T(8,128)(2,1)S(1)}, bf16[128,128]{1,0:T(8,128)(2,1)S(1)}, u32[]{:S(2)}, u32[]{:S(2)}) collective-permute-start(bf16[128,128]{1,0:T(8,128)(2,1)S(1)} %get-tuple-element.21), channel_id=1, source_target_pairs={{0,3},{1,0},{2,1},{3,2},{4,7},{5,4},{6,5},{7,6},{8,11},{9,8},{10,9... | collective-permute-start | bytes 98312 | tf_op jit(solution)/shard_map/ppermute | solution.py:34
  14.1 0.3 %shard_map.95.refs_0_.matrix = bf16[512,512]{1,0:T(8,128)(2,1)S(1)} custom-call(bf16[512,512]{1,0:T(8,128)(2,1)S(1)} %shard_map.94.near.matrix), custom_call_target="tpu_custom_call" | custom-call | bytes 1572864 | tf_op jit(solution)/shard_map/pallas_call | solution.py:206
  14.4 0.0 collective-permute-done.3.refs_2_
  14.4 1.6 %collective-permute-done.4.refs_3_ = bf16[128,128]{1,0:T(8,128)(2,1)S(1)} collective-permute-done((bf16[128,128]{1,0:T(8,128)(2,1)S(1)}, bf16[128,128]{1,0:T(8,128)(2,1)S(1)}, u32[]{:S(2)}, u32[]{:S(2)}) %collective-permute-start.4) | collective-permute-done | bytes 32800 | tf_op jit(solution)/shard_map/ppermute | solution.py:34
  16.1 0.0 collective-permute-done.5.refs_4_
  16.1 0.0 copy-done.1
  16.1 0.0 copy-done.2
  16.1 0.4 %shard_map.97 = (bf16[128,128]{1,0:T(8,128)(2,1)S(1)}, f32[128,128]{1,0:T(8,128)S(1)}, bf16[128,128]{1,0:T(8,128)(2,1)S(1)}, f32[128,256]{1,0:T(8,128)S(1)}) custom-call(bf16[512,512]{1,0:T(8,128)(2,1)S(1)} %shard_map.95.refs_0_.matrix, f32[128,128]{1,0:T(8,128)S(1)} %get-tuple-element.18.refs_1_, bf16[128,128]{1,0:T(8,128)(2,1)S(1)} %collective-permute-done.3.refs_2_, ...), custom_call_target="tpu_custom_call" | custom-call | flops 58720256 | tf_op jit(solution)/shard_map/pallas_call | solution.py:216
  16.5 0.1 collective-permute-start.6
  16.6 1.2 %collective-permute-done.6.came = bf16[128,128]{1,0:T(8,128)(2,1)S(1)} collective-permute-done((bf16[128,128]{1,0:T(8,128)(2,1)S(1)}, bf16[128,128]{1,0:T(8,128)(2,1)S(1)}, u32[]{:S(2)}, u32[]{:S(2)}) %collective-permute-start.6) | collective-permute-done | bytes 32800 | tf_op jit(solution)/shard_map/ppermute | solution.py:49
  17.8 0.8 %collective-permute-start.9 = (bf16[256,128]{1,0:T(8,128)(2,1)S(1)}, bf16[256,128]{1,0:T(8,128)(2,1)S(1)}, u32[]{:S(2)}, u32[]{:S(2)}) collective-permute-start(bf16[256,128]{1,0:T(8,128)(2,1)S(1)} %shard_map.99.refs_0_), channel_id=1, source_target_pairs={{0,2},{1,3},{2,0},{3,1},{4,6},{5,7},{6,4},{7,5},{8,10},{9,11},{10,... | collective-permute-start | bytes 196616 | tf_op jit(solution)/shard_map/ppermute | solution.py:34
  18.7 3.5 %collective-permute-start.8 = (bf16[256,128]{1,0:T(8,128)(2,1)S(1)}, bf16[256,128]{1,0:T(8,128)(2,1)S(1)}, u32[]{:S(2)}, u32[]{:S(2)}) collective-permute-start(bf16[256,128]{1,0:T(8,128)(2,1)S(1)} %shard_map.99.refs_0_), channel_id=1, source_target_pairs={{0,1},{1,2},{2,3},{3,0},{4,5},{5,6},{6,7},{7,4},{8,9},{9,10},{10,1... | collective-permute-start | bytes 196616 | tf_op jit(solution)/shard_map/ppermute | solution.py:34
  22.2 0.3 %collective-permute-start.7 = (bf16[256,128]{1,0:T(8,128)(2,1)S(1)}, bf16[256,128]{1,0:T(8,128)(2,1)S(1)}, u32[]{:S(2)}, u32[]{:S(2)}) collective-permute-start(bf16[256,128]{1,0:T(8,128)(2,1)S(1)} %shard_map.99.refs_0_), channel_id=1, source_target_pairs={{0,3},{1,0},{2,1},{3,2},{4,7},{5,4},{6,5},{7,6},{8,11},{9,8},{10,9... | collective-permute-start | bytes 196616 | tf_op jit(solution)/shard_map/ppermute | solution.py:34
  22.5 3.7 %collective-permute-done.9.refs_3_ = bf16[256,128]{1,0:T(8,128)(2,1)S(1)} collective-permute-done((bf16[256,128]{1,0:T(8,128)(2,1)S(1)}, bf16[256,128]{1,0:T(8,128)(2,1)S(1)}, u32[]{:S(2)}, u32[]{:S(2)}) %collective-permute-start.9) | collective-permute-done | bytes 65568 | tf_op jit(solution)/shard_map/ppermute | solution.py:34
  26.2 0.0 collective-permute-done.8.refs_2_
  26.2 0.9 %collective-permute-done.7.refs_1_ = bf16[256,128]{1,0:T(8,128)(2,1)S(1)} collective-permute-done((bf16[256,128]{1,0:T(8,128)(2,1)S(1)}, bf16[256,128]{1,0:T(8,128)(2,1)S(1)}, u32[]{:S(2)}, u32[]{:S(2)}) %collective-permute-start.7) | collective-permute-done | bytes 65568 | tf_op jit(solution)/shard_map/ppermute | solution.py:34
  27.2 0.3 shard_map.100
  27.5 0.1 collective-permute-start.10
  27.5 1.3 %collective-permute-start.11 = (bf16[256,128]{1,0:T(8,128)(2,1)S(1)}, bf16[256,128]{1,0:T(8,128)(2,1)S(1)}, u32[]{:S(2)}, u32[]{:S(2)}) collective-permute-start(bf16[256,128]{1,0:T(8,128)(2,1)S(1)} %get-tuple-element.29), channel_id=1, source_target_pairs={{0,8},{4,12},{8,0},{12,4},{1,9},{5,13},{9,1},{13,5},{2,10},{6,14},... | collective-permute-start | bytes 196616 | tf_op jit(solution)/shard_map/ppermute | solution.py:34
  28.8 1.4 %collective-permute-start.12 = (bf16[256,128]{1,0:T(8,128)(2,1)S(1)}, bf16[256,128]{1,0:T(8,128)(2,1)S(1)}, u32[]{:S(2)}, u32[]{:S(2)}) collective-permute-start(bf16[256,128]{1,0:T(8,128)(2,1)S(1)} %get-tuple-element.30), channel_id=1, source_target_pairs={{0,12},{4,0},{8,4},{12,8},{1,13},{5,1},{9,5},{13,9},{2,14},{6,2},{... | collective-permute-start | bytes 196616 | tf_op jit(solution)/shard_map/ppermute | solution.py:34
  30.2 0.7 %shard_map.98 = bf16[128,256]{1,0:T(8,128)(2,1)} custom-call(f32[128,256]{1,0:T(8,128)S(1)} %get-tuple-element.22.pre), custom_call_target="tpu_custom_call" | custom-call | tf_op jit(solution)/shard_map/pallas_call | solution.py:230
  30.8 0.5 %collective-permute-done.10.refs_0_ = bf16[256,128]{1,0:T(8,128)(2,1)S(1)} collective-permute-done((bf16[256,128]{1,0:T(8,128)(2,1)S(1)}, bf16[256,128]{1,0:T(8,128)(2,1)S(1)}, u32[]{:S(2)}, u32[]{:S(2)}) %collective-permute-start.10) | collective-permute-done | bytes 65568 | tf_op jit(solution)/shard_map/ppermute | solution.py:34
  31.3 1.1 %collective-permute-done.11.refs_1_ = bf16[256,128]{1,0:T(8,128)(2,1)S(1)} collective-permute-done((bf16[256,128]{1,0:T(8,128)(2,1)S(1)}, bf16[256,128]{1,0:T(8,128)(2,1)S(1)}, u32[]{:S(2)}, u32[]{:S(2)}) %collective-permute-start.11) | collective-permute-done | bytes 65568 | tf_op jit(solution)/shard_map/ppermute | solution.py:34
  32.4 0.0 collective-permute-done.12.refs_2_
  32.4 0.7 %shard_map.101 = (bf16[128,128]{1,0:T(8,128)(2,1)}, f32[128,256]{1,0:T(8,128)}) custom-call(f32[128,128]{1,0:T(8,128)S(1)} %get-tuple-element.26.own, bf16[128,128]{1,0:T(8,128)(2,1)S(1)} %get-tuple-element.27.kept, bf16[256,128]{1,0:T(8,128)(2,1)S(1)} %collective-permute-done.10.refs_0_, bf16[256,128]{1,0:T(8,128)(2,1)S(1)} %collective-permute-done.11.refs_1_, ...), custom_call_target="tpu_custom_call" | custom-call | tf_op jit(solution)/shard_map/pallas_call | solution.py:242
  (1 shorter events, 0.0 us)
Async XLA Ops:
  0.6 4.2 %copy-start.5 = (s32[1,1,8]{2,1,0:T(1,128)S(1)}, s32[1,1,8]{2,1,0:T(1,128)}, u32[]{:S(2)}) copy-start(s32[1,1,8]{2,1,0:T(1,128)} %cols_in.1) | copy-start | bytes 100
  0.6 4.2 %copy-start.4 = (s32[1,1,8]{2,1,0:T(1,128)S(1)}, s32[1,1,8]{2,1,0:T(1,128)}, u32[]{:S(2)}) copy-start(s32[1,1,8]{2,1,0:T(1,128)} %rows_in.1) | copy-start | bytes 100
  0.7 5.8 %collective-permute-start.1 = (bf16[128,128]{1,0:T(8,128)(2,1)}, bf16[128,128]{1,0:T(8,128)(2,1)S(1)}, u32[]{:S(2)}, u32[]{:S(2)}) collective-permute-start(bf16[128,128]{1,0:T(8,128)(2,1)} %refs_0_.1), channel_id=1, source_target_pairs={{0,8},{4,12},{8,0},{12,4},{1,9},{5,13},{9,1},{13,5},{2,10},{6,14},... | collective-permute-start | bytes 98312 | tf_op jit(solution)/shard_map/ppermute | solution.py:34
  3.7 2.8 %collective-permute-start = (bf16[128,128]{1,0:T(8,128)(2,1)}, bf16[128,128]{1,0:T(8,128)(2,1)S(1)}, u32[]{:S(2)}, u32[]{:S(2)}) collective-permute-start(bf16[128,128]{1,0:T(8,128)(2,1)} %refs_0_.1), channel_id=1, source_target_pairs={{0,12},{4,0},{8,4},{12,8},{1,13},{5,1},{9,5},{13,9},{2,14},{6,2},{... | collective-permute-start | bytes 98312 | tf_op jit(solution)/shard_map/ppermute | solution.py:34
  3.7 3.6 %collective-permute-start.2 = (bf16[128,128]{1,0:T(8,128)(2,1)}, bf16[128,128]{1,0:T(8,128)(2,1)S(1)}, u32[]{:S(2)}, u32[]{:S(2)}) collective-permute-start(bf16[128,128]{1,0:T(8,128)(2,1)} %refs_0_.1), channel_id=1, source_target_pairs={{0,4},{4,8},{8,12},{12,0},{1,5},{5,9},{9,13},{13,1},{2,6},{6,10},{... | collective-permute-start | bytes 98312 | tf_op jit(solution)/shard_map/ppermute | solution.py:34
  4.8 1.0 %copy-start = (bf16[1,1,8,128,128]{4,3,2,1,0:T(8,128)(2,1)S(1)}, bf16[1,1,8,128,128]{4,3,2,1,0:T(8,128)(2,1)}, u32[]{:S(2)}) copy-start(bf16[1,1,8,128,128]{4,3,2,1,0:T(8,128)(2,1)} %vals.1) | copy-start | bytes 786436
  5.8 1.5 %copy-start.3 = (bf16[128,128]{1,0:T(8,128)(2,1)S(1)}, bf16[128,128]{1,0:T(8,128)(2,1)}, u32[]{:S(2)}) copy-start(bf16[128,128]{1,0:T(8,128)(2,1)} %refs_0_.1) | copy-start | bytes 98308
  7.6 6.8 %collective-permute-start.3 = (bf16[128,128]{1,0:T(8,128)(2,1)S(1)}, bf16[128,128]{1,0:T(8,128)(2,1)S(1)}, u32[]{:S(2)}, u32[]{:S(2)}) collective-permute-start(bf16[128,128]{1,0:T(8,128)(2,1)S(1)} %get-tuple-element.19), channel_id=1, source_target_pairs={{0,2},{1,3},{2,0},{3,1},{4,6},{5,7},{6,4},{7,5},{8,10},{9,11},{10,... | collective-permute-start | bytes 98312 | tf_op jit(solution)/shard_map/ppermute | solution.py:34
  10.2 5.8 %collective-permute-start.4 = (bf16[128,128]{1,0:T(8,128)(2,1)S(1)}, bf16[128,128]{1,0:T(8,128)(2,1)S(1)}, u32[]{:S(2)}, u32[]{:S(2)}) collective-permute-start(bf16[128,128]{1,0:T(8,128)(2,1)S(1)} %get-tuple-element.20), channel_id=1, source_target_pairs={{0,1},{1,2},{2,3},{3,0},{4,5},{5,6},{6,7},{7,4},{8,9},{9,10},{10,1... | collective-permute-start | bytes 98312 | tf_op jit(solution)/shard_map/ppermute | solution.py:34
  11.8 4.3 %copy-start.1 = (bf16[128,256]{1,0:T(8,128)(2,1)S(1)}, bf16[128,256]{1,0:T(8,128)(2,1)}, u32[]{:S(2)}) copy-start(bf16[128,256]{1,0:T(8,128)(2,1)} %refs_5_.1) | copy-start | bytes 196612
  11.8 4.3 %copy-start.2 = (bf16[128,256]{1,0:T(8,128)(2,1)S(1)}, bf16[128,256]{1,0:T(8,128)(2,1)}, u32[]{:S(2)}) copy-start(bf16[128,256]{1,0:T(8,128)(2,1)} %refs_6_.1) | copy-start | bytes 196612
  11.8 4.3 %collective-permute-start.5 = (bf16[128,128]{1,0:T(8,128)(2,1)S(1)}, bf16[128,128]{1,0:T(8,128)(2,1)S(1)}, u32[]{:S(2)}, u32[]{:S(2)}) collective-permute-start(bf16[128,128]{1,0:T(8,128)(2,1)S(1)} %get-tuple-element.21), channel_id=1, source_target_pairs={{0,3},{1,0},{2,1},{3,2},{4,7},{5,4},{6,5},{7,6},{8,11},{9,8},{10,9... | collective-permute-start | bytes 98312 | tf_op jit(solution)/shard_map/ppermute | solution.py:34
  16.5 1.3 %collective-permute-start.6 = (bf16[128,128]{1,0:T(8,128)(2,1)S(1)}, bf16[128,128]{1,0:T(8,128)(2,1)S(1)}, u32[]{:S(2)}, u32[]{:S(2)}) collective-permute-start(bf16[128,128]{1,0:T(8,128)(2,1)S(1)} %get-tuple-element.25), channel_id=1, source_target_pairs={{0,4},{4,0},{8,12},{12,8},{1,5},{5,1},{9,13},{13,9},{2,6},{6,2},{1... | collective-permute-start | bytes 98312 | tf_op jit(solution)/shard_map/ppermute | solution.py:49
  17.8 8.4 %collective-permute-start.9 = (bf16[256,128]{1,0:T(8,128)(2,1)S(1)}, bf16[256,128]{1,0:T(8,128)(2,1)S(1)}, u32[]{:S(2)}, u32[]{:S(2)}) collective-permute-start(bf16[256,128]{1,0:T(8,128)(2,1)S(1)} %shard_map.99.refs_0_), channel_id=1, source_target_pairs={{0,2},{1,3},{2,0},{3,1},{4,6},{5,7},{6,4},{7,5},{8,10},{9,11},{10,... | collective-permute-start | bytes 196616 | tf_op jit(solution)/shard_map/ppermute | solution.py:34
  18.7 7.6 %collective-permute-start.8 = (bf16[256,128]{1,0:T(8,128)(2,1)S(1)}, bf16[256,128]{1,0:T(8,128)(2,1)S(1)}, u32[]{:S(2)}, u32[]{:S(2)}) collective-permute-start(bf16[256,128]{1,0:T(8,128)(2,1)S(1)} %shard_map.99.refs_0_), channel_id=1, source_target_pairs={{0,1},{1,2},{2,3},{3,0},{4,5},{5,6},{6,7},{7,4},{8,9},{9,10},{10,1... | collective-permute-start | bytes 196616 | tf_op jit(solution)/shard_map/ppermute | solution.py:34
  22.2 5.0 %collective-permute-start.7 = (bf16[256,128]{1,0:T(8,128)(2,1)S(1)}, bf16[256,128]{1,0:T(8,128)(2,1)S(1)}, u32[]{:S(2)}, u32[]{:S(2)}) collective-permute-start(bf16[256,128]{1,0:T(8,128)(2,1)S(1)} %shard_map.99.refs_0_), channel_id=1, source_target_pairs={{0,3},{1,0},{2,1},{3,2},{4,7},{5,4},{6,5},{7,6},{8,11},{9,8},{10,9... | collective-permute-start | bytes 196616 | tf_op jit(solution)/shard_map/ppermute | solution.py:34
  27.5 3.8 %collective-permute-start.10 = (bf16[256,128]{1,0:T(8,128)(2,1)S(1)}, bf16[256,128]{1,0:T(8,128)(2,1)S(1)}, u32[]{:S(2)}, u32[]{:S(2)}) collective-permute-start(bf16[256,128]{1,0:T(8,128)(2,1)S(1)} %get-tuple-element.28), channel_id=1, source_target_pairs={{0,4},{4,8},{8,12},{12,0},{1,5},{5,9},{9,13},{13,1},{2,6},{6,10},{... | collective-permute-start | bytes 196616 | tf_op jit(solution)/shard_map/ppermute | solution.py:34
  27.5 4.9 %collective-permute-start.11 = (bf16[256,128]{1,0:T(8,128)(2,1)S(1)}, bf16[256,128]{1,0:T(8,128)(2,1)S(1)}, u32[]{:S(2)}, u32[]{:S(2)}) collective-permute-start(bf16[256,128]{1,0:T(8,128)(2,1)S(1)} %get-tuple-element.29), channel_id=1, source_target_pairs={{0,8},{4,12},{8,0},{12,4},{1,9},{5,13},{9,1},{13,5},{2,10},{6,14},... | collective-permute-start | bytes 196616 | tf_op jit(solution)/shard_map/ppermute | solution.py:34
  28.8 3.6 %collective-permute-start.12 = (bf16[256,128]{1,0:T(8,128)(2,1)S(1)}, bf16[256,128]{1,0:T(8,128)(2,1)S(1)}, u32[]{:S(2)}, u32[]{:S(2)}) collective-permute-start(bf16[256,128]{1,0:T(8,128)(2,1)S(1)} %get-tuple-element.30), channel_id=1, source_target_pairs={{0,12},{4,0},{8,4},{12,8},{1,13},{5,1},{9,5},{13,9},{2,14},{6,2},{... | collective-permute-start | bytes 196616 | tf_op jit(solution)/shard_map/ppermute | solution.py:34

commit v11 on v9

--- a/solution.py
+++ b/solution.py
@@ -28,12 +28,24 @@
     return functools.partial(run, *after)
 
 
+def ring_place(k, n):
+    return k ^ (k >> 1) if n == 4 else k
+
+
 def exchange(sends, axis, ahead):
     n = lax.axis_size(axis)
+
+    def target(s, d):
+        return ring_place((ring_place(s, n) + (d if ahead else -d)) % n, n)
+
     return [
-        lax.ppermute(send, axis, [(s, (s + (d if ahead else -d)) % n) for s in range(n)])
+        lax.ppermute(send, axis, [(s, target(s, d)) for s in range(n)])
         for d, send in enumerate(sends, 1)
     ]
+
+
+def odd_row():
+    return lax.rem(ring_place(lax.axis_index("row"), lax.axis_size("row")), 2) == 1
 
 
 def neighbour(value, axis):
@@ -67,10 +79,13 @@
     for copy in copies:
         copy.wait()
 
+    def ahead(there, here, n):
+        return lax.rem(ring_place(there, n) - ring_place(here, n) + n, n)
+
     def add(t, _):
         row, col = rows[0, 0, t], cols[0, 0, t]
-        row = lax.rem(row // piece - my_col + n_col, n_col) * piece + lax.rem(row, piece)
-        col = lax.rem(col // piece - my_row + n_row, n_row) * piece + lax.rem(col, piece)
+        row = ahead(row // piece, my_col, n_col) * piece + lax.rem(row, piece)
+        col = ahead(col // piece, my_row, n_row) * piece + lax.rem(col, piece)
         down = pl.ds(pl.multiple_of(row * side, side), side)
         across = pl.ds(pl.multiple_of(col * side, side), side)
         near[down, across] = vals[0, 0, t]
@@ -117,7 +132,7 @@
     grad_high, grad_low = split(grad)
     down = ((0,), (0,))
     term = dot(high, grad_high, down) + dot(low, grad_high, down) + dot(high, grad_low, down)
-    odd = lax.rem(lax.axis_index("row"), 2) == 1
+    odd = odd_row()
     left, right = term[:, :half], term[:, half:]
     mine[...] = jnp.where(odd, right, left)
     other[...] = jnp.where(odd, left, right).astype(other.dtype)
@@ -158,7 +173,7 @@
     ).astype(features_out.dtype)
     terms = [wide(kept[...])] + [wide(message[nodes:]) for message in messages]
     mine, other = tree(terms[::2]) * scale, tree(terms[1::2]) * scale
-    odd = lax.rem(lax.axis_index("row"), 2) == 1
+    odd = odd_row()
     weight_out[:, :half] = jnp.where(odd, other, mine)
     weight_out[:, half:] = jnp.where(odd, mine, other)
 

time: 32.9 us -> 33 us (level)
  the two profiles are of different devices: /device:TPU:0 before, /device:TPU:1 now
where the time goes in v11:
time: 33 us; the launch traced here: 32.8 us
  starting transfers between devices  18 us (55%)
  waiting for transfers between devices  9 us (27%)
  Pallas kernels  3.46 us (10%)
  between operations  1.42 us (4%)
  local copies, waits for them, and re-layouts  0.96 us (3%)
    ppermute x12, starting transfers between devices, exchange(): lax.ppermute(send, axis, [(s, target(s, d)) for s in range(n)])  15.6 us
    ppermute x12, waiting for transfers between devices, exchange(): lax.ppermute(send, axis, [(s, target(s, d)) for s in range(n)])  8.14 us
    ppermute x1, starting transfers between devices, neighbour(): return lax.ppermute(value, axis, [(s, s ^ 1) for s in range(n)])  2.39 us
    unnamed x12, local copies, waits for them, and re-layouts  0.96 us
    ppermute x1, waiting for transfers between devices, neighbour(): return lax.ppermute(value, axis, [(s, s ^ 1) for s in range(n)])  0.86 us
    pallas_call x1, Pallas kernels, per_device(): call(functools.partial(dense_kernel, n_row, n_col, nodes // side), [((dow...  0.73 us
    pallas_call x1, Pallas kernels, per_device(): call(functools.partial(last_kernel, scale), [((nodes, width), NARROW), ((...  0.69 us
  transfers between devices with their start and end apart: 13, of which 8 were waited for; matrix products, arithmetic and copies ran while one was open for 0% of the time, Pallas kernels for 5%

profile of v11, /device:TPU:1, one launch (start us, length us, event | category | flops | bytes accessed | tf_op | source)
XLA Modules:
  0.0 32.8 jit_solution(4361743204567427543)
XLA Ops:
  0.6 0.0 copy-start.5
  0.6 0.0 copy-start.4
  0.7 2.7 %collective-permute-start.1 = (bf16[128,128]{1,0:T(8,128)(2,1)}, bf16[128,128]{1,0:T(8,128)(2,1)S(1)}, u32[]{:S(2)}, u32[]{:S(2)}) collective-permute-start(bf16[128,128]{1,0:T(8,128)(2,1)} %refs_0_.1), channel_id=1, source_target_pairs={{0,12},{4,8},{8,4},{12,0},{1,13},{5,9},{9,5},{13,1},{2,14},{6,10},... | collective-permute-start | bytes 98312 | tf_op jit(solution)/shard_map/ppermute | solution.py:42
  3.3 0.0 collective-permute-start
  3.3 1.5 %collective-permute-start.2 = (bf16[128,128]{1,0:T(8,128)(2,1)}, bf16[128,128]{1,0:T(8,128)(2,1)S(1)}, u32[]{:S(2)}, u32[]{:S(2)}) collective-permute-start(bf16[128,128]{1,0:T(8,128)(2,1)} %refs_0_.1), channel_id=1, source_target_pairs={{0,4},{4,12},{8,0},{12,8},{1,5},{5,13},{9,1},{13,9},{2,6},{6,14},{... | collective-permute-start | bytes 98312 | tf_op jit(solution)/shard_map/ppermute | solution.py:42
  5.4 0.0 copy-done.5
  5.4 0.0 copy-done.4
  5.5 0.0 copy-start
  5.5 0.9 %copy-done = bf16[1,1,8,128,128]{4,3,2,1,0:T(8,128)(2,1)S(1)} copy-done((bf16[1,1,8,128,128]{4,3,2,1,0:T(8,128)(2,1)S(1)}, bf16[1,1,8,128,128]{4,3,2,1,0:T(8,128)(2,1)}, u32[]{:S(2)}) %copy-start) | copy-done | bytes 262168
  6.4 0.0 copy-start.3
  6.4 0.7 %shard_map.94.near.matrix = bf16[512,512]{1,0:T(8,128)(2,1)S(1)} custom-call(bf16[1,1,8,128,128]{4,3,2,1,0:T(8,128)(2,1)S(1)} %copy-done, s32[1,1,8]{2,1,0:T(1,128)S(1)} %copy-done.4, s32[1,1,8]{2,1,0:T(1,128)S(1)} %copy-done.5, s32[1,1]{1,0:T(1,128)S(6)} %copy.10.count_in), custom_call_target="tpu_custom_call" | custom-call | bytes 1048576 | tf_op jit(solution)/shard_map/pallas_call | solution.py:190
  7.1 0.0 collective-permute-done.1.refs_2_
  7.2 0.0 collective-permute-done.refs_1_
  7.2 0.0 collective-permute-done.2.refs_3_
  7.2 0.0 copy-done.3
  7.2 0.3 shard_map.96
  7.5 1.3 %collective-permute-start.3 = (bf16[128,128]{1,0:T(8,128)(2,1)S(1)}, bf16[128,128]{1,0:T(8,128)(2,1)S(1)}, u32[]{:S(2)}, u32[]{:S(2)}) collective-permute-start(bf16[128,128]{1,0:T(8,128)(2,1)S(1)} %get-tuple-element.19), channel_id=1, source_target_pairs={{0,1},{1,3},{2,0},{3,2},{4,5},{5,7},{6,4},{7,6},{8,9},{9,11},{10,8... | collective-permute-start | bytes 98312 | tf_op jit(solution)/shard_map/ppermute | solution.py:42
  8.8 2.2 %collective-permute-start.4 = (bf16[128,128]{1,0:T(8,128)(2,1)S(1)}, bf16[128,128]{1,0:T(8,128)(2,1)S(1)}, u32[]{:S(2)}, u32[]{:S(2)}) collective-permute-start(bf16[128,128]{1,0:T(8,128)(2,1)S(1)} %get-tuple-element.20), channel_id=1, source_target_pairs={{0,3},{1,2},{2,1},{3,0},{4,7},{5,6},{6,5},{7,4},{8,11},{9,10},{10,... | collective-permute-start | bytes 98312 | tf_op jit(solution)/shard_map/ppermute | solution.py:42
  11.0 0.0 copy-start.1
  11.0 0.0 copy-start.2
  11.0 1.3 %collective-permute-start.5 = (bf16[128,128]{1,0:T(8,128)(2,1)S(1)}, bf16[128,128]{1,0:T(8,128)(2,1)S(1)}, u32[]{:S(2)}, u32[]{:S(2)}) collective-permute-start(bf16[128,128]{1,0:T(8,128)(2,1)S(1)} %get-tuple-element.21), channel_id=1, source_target_pairs={{0,2},{1,0},{2,3},{3,1},{4,6},{5,4},{6,7},{7,5},{8,10},{9,8},{10,1... | collective-permute-start | bytes 98312 | tf_op jit(solution)/shard_map/ppermute | solution.py:42
  12.3 0.3 %shard_map.95.refs_0_.matrix = bf16[512,512]{1,0:T(8,128)(2,1)S(1)} custom-call(bf16[512,512]{1,0:T(8,128)(2,1)S(1)} %shard_map.94.near.matrix), custom_call_target="tpu_custom_call" | custom-call | bytes 1572864 | tf_op jit(solution)/shard_map/pallas_call | solution.py:211
  12.7 0.0 collective-permute-done.3.refs_2_
  12.7 0.9 %collective-permute-done.4.refs_3_ = bf16[128,128]{1,0:T(8,128)(2,1)S(1)} collective-permute-done((bf16[128,128]{1,0:T(8,128)(2,1)S(1)}, bf16[128,128]{1,0:T(8,128)(2,1)S(1)}, u32[]{:S(2)}, u32[]{:S(2)}) %collective-permute-start.4) | collective-permute-done | bytes 32800 | tf_op jit(solution)/shard_map/ppermute | solution.py:42
  13.6 0.3 collective-permute-done.5.refs_4_
  13.9 0.0 copy-done.1
  13.9 0.0 copy-done.2
  13.9 0.4 %shard_map.97 = (bf16[128,128]{1,0:T(8,128)(2,1)S(1)}, f32[128,128]{1,0:T(8,128)S(1)}, bf16[128,128]{1,0:T(8,128)(2,1)S(1)}, f32[128,256]{1,0:T(8,128)S(1)}) custom-call(bf16[512,512]{1,0:T(8,128)(2,1)S(1)} %shard_map.95.refs_0_.matrix, f32[128,128]{1,0:T(8,128)S(1)} %get-tuple-element.18.refs_1_, bf16[128,128]{1,0:T(8,128)(2,1)S(1)} %collective-permute-done.3.refs_2_, ...), custom_call_target="tpu_custom_call" | custom-call | flops 58720256 | tf_op jit(solution)/shard_map/pallas_call | solution.py:221
  14.3 2.4 %collective-permute-start.6 = (bf16[128,128]{1,0:T(8,128)(2,1)S(1)}, bf16[128,128]{1,0:T(8,128)(2,1)S(1)}, u32[]{:S(2)}, u32[]{:S(2)}) collective-permute-start(bf16[128,128]{1,0:T(8,128)(2,1)S(1)} %get-tuple-element.25), channel_id=1, source_target_pairs={{0,4},{4,0},{8,12},{12,8},{1,5},{5,1},{9,13},{13,9},{2,6},{6,2},{1... | collective-permute-start | bytes 98312 | tf_op jit(solution)/shard_map/ppermute | solution.py:53
  16.7 0.9 %collective-permute-done.6.came = bf16[128,128]{1,0:T(8,128)(2,1)S(1)} collective-permute-done((bf16[128,128]{1,0:T(8,128)(2,1)S(1)}, bf16[128,128]{1,0:T(8,128)(2,1)S(1)}, u32[]{:S(2)}, u32[]{:S(2)}) %collective-permute-start.6) | collective-permute-done | bytes 32800 | tf_op jit(solution)/shard_map/ppermute | solution.py:53
  17.6 0.8 %collective-permute-start.9 = (bf16[256,128]{1,0:T(8,128)(2,1)S(1)}, bf16[256,128]{1,0:T(8,128)(2,1)S(1)}, u32[]{:S(2)}, u32[]{:S(2)}) collective-permute-start(bf16[256,128]{1,0:T(8,128)(2,1)S(1)} %shard_map.99.refs_0_), channel_id=1, source_target_pairs={{0,1},{1,3},{2,0},{3,2},{4,5},{5,7},{6,4},{7,6},{8,9},{9,11},{10,8... | collective-permute-start | bytes 196616 | tf_op jit(solution)/shard_map/ppermute | solution.py:42
  18.4 2.6 %collective-permute-start.8 = (bf16[256,128]{1,0:T(8,128)(2,1)S(1)}, bf16[256,128]{1,0:T(8,128)(2,1)S(1)}, u32[]{:S(2)}, u32[]{:S(2)}) collective-permute-start(bf16[256,128]{1,0:T(8,128)(2,1)S(1)} %shard_map.99.refs_0_), channel_id=1, source_target_pairs={{0,3},{1,2},{2,1},{3,0},{4,7},{5,6},{6,5},{7,4},{8,11},{9,10},{10,... | collective-permute-start | bytes 196616 | tf_op jit(solution)/shard_map/ppermute | solution.py:42
  21.0 0.0 collective-permute-start.7
  21.0 0.6 %collective-permute-done.9.refs_3_ = bf16[256,128]{1,0:T(8,128)(2,1)S(1)} collective-permute-done((bf16[256,128]{1,0:T(8,128)(2,1)S(1)}, bf16[256,128]{1,0:T(8,128)(2,1)S(1)}, u32[]{:S(2)}, u32[]{:S(2)}) %collective-permute-start.9) | collective-permute-done | bytes 65568 | tf_op jit(solution)/shard_map/ppermute | solution.py:42
  21.7 2.3 %collective-permute-done.8.refs_2_ = bf16[256,128]{1,0:T(8,128)(2,1)S(1)} collective-permute-done((bf16[256,128]{1,0:T(8,128)(2,1)S(1)}, bf16[256,128]{1,0:T(8,128)(2,1)S(1)}, u32[]{:S(2)}, u32[]{:S(2)}) %collective-permute-start.8) | collective-permute-done | bytes 65568 | tf_op jit(solution)/shard_map/ppermute | solution.py:42
  24.0 1.1 %collective-permute-done.7.refs_1_ = bf16[256,128]{1,0:T(8,128)(2,1)S(1)} collective-permute-done((bf16[256,128]{1,0:T(8,128)(2,1)S(1)}, bf16[256,128]{1,0:T(8,128)(2,1)S(1)}, u32[]{:S(2)}, u32[]{:S(2)}) %collective-permute-start.7) | collective-permute-done | bytes 65568 | tf_op jit(solution)/shard_map/ppermute | solution.py:42
  25.1 0.3 shard_map.100
  25.4 0.0 collective-permute-start.10
  25.4 3.2 %collective-permute-start.11 = (bf16[256,128]{1,0:T(8,128)(2,1)S(1)}, bf16[256,128]{1,0:T(8,128)(2,1)S(1)}, u32[]{:S(2)}, u32[]{:S(2)}) collective-permute-start(bf16[256,128]{1,0:T(8,128)(2,1)S(1)} %get-tuple-element.29), channel_id=1, source_target_pairs={{0,12},{4,8},{8,4},{12,0},{1,13},{5,9},{9,5},{13,1},{2,14},{6,10},... | collective-permute-start | bytes 196616 | tf_op jit(solution)/shard_map/ppermute | solution.py:42
  28.6 0.0 collective-permute-start.12
  28.6 0.7 %shard_map.98 = bf16[128,256]{1,0:T(8,128)(2,1)} custom-call(f32[128,256]{1,0:T(8,128)S(1)} %get-tuple-element.22.pre), custom_call_target="tpu_custom_call" | custom-call | tf_op jit(solution)/shard_map/pallas_call | solution.py:235
  29.2 0.0 collective-permute-done.10.refs_0_
  29.2 2.6 %collective-permute-done.11.refs_1_ = bf16[256,128]{1,0:T(8,128)(2,1)S(1)} collective-permute-done((bf16[256,128]{1,0:T(8,128)(2,1)S(1)}, bf16[256,128]{1,0:T(8,128)(2,1)S(1)}, u32[]{:S(2)}, u32[]{:S(2)}) %collective-permute-start.11) | collective-permute-done | bytes 65568 | tf_op jit(solution)/shard_map/ppermute | solution.py:42
  31.8 0.3 collective-permute-done.12.refs_2_
  32.1 0.7 %shard_map.101 = (bf16[128,128]{1,0:T(8,128)(2,1)}, f32[128,256]{1,0:T(8,128)}) custom-call(f32[128,128]{1,0:T(8,128)S(1)} %get-tuple-element.26.own, bf16[128,128]{1,0:T(8,128)(2,1)S(1)} %get-tuple-element.27.kept, bf16[256,128]{1,0:T(8,128)(2,1)S(1)} %collective-permute-done.10.refs_0_, bf16[256,128]{1,0:T(8,128)(2,1)S(1)} %collective-permute-done.11.refs_1_, ...), custom_call_target="tpu_custom_call" | custom-call | tf_op jit(solution)/shard_map/pallas_call | solution.py:247
  (1 shorter events, 0.0 us)
Async XLA Ops:
  0.6 4.8 %copy-start.5 = (s32[1,1,8]{2,1,0:T(1,128)S(1)}, s32[1,1,8]{2,1,0:T(1,128)}, u32[]{:S(2)}) copy-start(s32[1,1,8]{2,1,0:T(1,128)} %cols_in.1) | copy-start | bytes 100
  0.6 4.8 %copy-start.4 = (s32[1,1,8]{2,1,0:T(1,128)S(1)}, s32[1,1,8]{2,1,0:T(1,128)}, u32[]{:S(2)}) copy-start(s32[1,1,8]{2,1,0:T(1,128)} %rows_in.1) | copy-start | bytes 100
  0.7 6.5 %collective-permute-start.1 = (bf16[128,128]{1,0:T(8,128)(2,1)}, bf16[128,128]{1,0:T(8,128)(2,1)S(1)}, u32[]{:S(2)}, u32[]{:S(2)}) collective-permute-start(bf16[128,128]{1,0:T(8,128)(2,1)} %refs_0_.1), channel_id=1, source_target_pairs={{0,12},{4,8},{8,4},{12,0},{1,13},{5,9},{9,5},{13,1},{2,14},{6,10},... | collective-permute-start | bytes 98312 | tf_op jit(solution)/shard_map/ppermute | solution.py:42
  3.3 3.8 %collective-permute-start = (bf16[128,128]{1,0:T(8,128)(2,1)}, bf16[128,128]{1,0:T(8,128)(2,1)S(1)}, u32[]{:S(2)}, u32[]{:S(2)}) collective-permute-start(bf16[128,128]{1,0:T(8,128)(2,1)} %refs_0_.1), channel_id=1, source_target_pairs={{0,8},{4,0},{8,12},{12,4},{1,9},{5,1},{9,13},{13,5},{2,10},{6,2},{... | collective-permute-start | bytes 98312 | tf_op jit(solution)/shard_map/ppermute | solution.py:42
  3.3 3.9 %collective-permute-start.2 = (bf16[128,128]{1,0:T(8,128)(2,1)}, bf16[128,128]{1,0:T(8,128)(2,1)S(1)}, u32[]{:S(2)}, u32[]{:S(2)}) collective-permute-start(bf16[128,128]{1,0:T(8,128)(2,1)} %refs_0_.1), channel_id=1, source_target_pairs={{0,4},{4,12},{8,0},{12,8},{1,5},{5,13},{9,1},{13,9},{2,6},{6,14},{... | collective-permute-start | bytes 98312 | tf_op jit(solution)/shard_map/ppermute | solution.py:42
  5.5 1.0 %copy-start = (bf16[1,1,8,128,128]{4,3,2,1,0:T(8,128)(2,1)S(1)}, bf16[1,1,8,128,128]{4,3,2,1,0:T(8,128)(2,1)}, u32[]{:S(2)}) copy-start(bf16[1,1,8,128,128]{4,3,2,1,0:T(8,128)(2,1)} %vals.1) | copy-start | bytes 786436
  6.4 0.8 %copy-start.3 = (bf16[128,128]{1,0:T(8,128)(2,1)S(1)}, bf16[128,128]{1,0:T(8,128)(2,1)}, u32[]{:S(2)}) copy-start(bf16[128,128]{1,0:T(8,128)(2,1)} %refs_0_.1) | copy-start | bytes 98308
  7.5 5.2 %collective-permute-start.3 = (bf16[128,128]{1,0:T(8,128)(2,1)S(1)}, bf16[128,128]{1,0:T(8,128)(2,1)S(1)}, u32[]{:S(2)}, u32[]{:S(2)}) collective-permute-start(bf16[128,128]{1,0:T(8,128)(2,1)S(1)} %get-tuple-element.19), channel_id=1, source_target_pairs={{0,1},{1,3},{2,0},{3,2},{4,5},{5,7},{6,4},{7,6},{8,9},{9,11},{10,8... | collective-permute-start | bytes 98312 | tf_op jit(solution)/shard_map/ppermute | solution.py:42
  8.8 4.8 %collective-permute-start.4 = (bf16[128,128]{1,0:T(8,128)(2,1)S(1)}, bf16[128,128]{1,0:T(8,128)(2,1)S(1)}, u32[]{:S(2)}, u32[]{:S(2)}) collective-permute-start(bf16[128,128]{1,0:T(8,128)(2,1)S(1)} %get-tuple-element.20), channel_id=1, source_target_pairs={{0,3},{1,2},{2,1},{3,0},{4,7},{5,6},{6,5},{7,4},{8,11},{9,10},{10,... | collective-permute-start | bytes 98312 | tf_op jit(solution)/shard_map/ppermute | solution.py:42
  11.0 2.9 %copy-start.1 = (bf16[128,256]{1,0:T(8,128)(2,1)S(1)}, bf16[128,256]{1,0:T(8,128)(2,1)}, u32[]{:S(2)}) copy-start(bf16[128,256]{1,0:T(8,128)(2,1)} %refs_5_.1) | copy-start | bytes 196612
  11.0 2.9 %copy-start.2 = (bf16[128,256]{1,0:T(8,128)(2,1)S(1)}, bf16[128,256]{1,0:T(8,128)(2,1)}, u32[]{:S(2)}) copy-start(bf16[128,256]{1,0:T(8,128)(2,1)} %refs_6_.1) | copy-start | bytes 196612
  11.0 2.9 %collective-permute-start.5 = (bf16[128,128]{1,0:T(8,128)(2,1)S(1)}, bf16[128,128]{1,0:T(8,128)(2,1)S(1)}, u32[]{:S(2)}, u32[]{:S(2)}) collective-permute-start(bf16[128,128]{1,0:T(8,128)(2,1)S(1)} %get-tuple-element.21), channel_id=1, source_target_pairs={{0,2},{1,0},{2,3},{3,1},{4,6},{5,4},{6,7},{7,5},{8,10},{9,8},{10,1... | collective-permute-start | bytes 98312 | tf_op jit(solution)/shard_map/ppermute | solution.py:42
  14.3 3.3 %collective-permute-start.6 = (bf16[128,128]{1,0:T(8,128)(2,1)S(1)}, bf16[128,128]{1,0:T(8,128)(2,1)S(1)}, u32[]{:S(2)}, u32[]{:S(2)}) collective-permute-start(bf16[128,128]{1,0:T(8,128)(2,1)S(1)} %get-tuple-element.25), channel_id=1, source_target_pairs={{0,4},{4,0},{8,12},{12,8},{1,5},{5,1},{9,13},{13,9},{2,6},{6,2},{1... | collective-permute-start | bytes 98312 | tf_op jit(solution)/shard_map/ppermute | solution.py:53
  17.6 4.1 %collective-permute-start.9 = (bf16[256,128]{1,0:T(8,128)(2,1)S(1)}, bf16[256,128]{1,0:T(8,128)(2,1)S(1)}, u32[]{:S(2)}, u32[]{:S(2)}) collective-permute-start(bf16[256,128]{1,0:T(8,128)(2,1)S(1)} %shard_map.99.refs_0_), channel_id=1, source_target_pairs={{0,1},{1,3},{2,0},{3,2},{4,5},{5,7},{6,4},{7,6},{8,9},{9,11},{10,8... | collective-permute-start | bytes 196616 | tf_op jit(solution)/shard_map/ppermute | solution.py:42
  18.4 5.6 %collective-permute-start.8 = (bf16[256,128]{1,0:T(8,128)(2,1)S(1)}, bf16[256,128]{1,0:T(8,128)(2,1)S(1)}, u32[]{:S(2)}, u32[]{:S(2)}) collective-permute-start(bf16[256,128]{1,0:T(8,128)(2,1)S(1)} %shard_map.99.refs_0_), channel_id=1, source_target_pairs={{0,3},{1,2},{2,1},{3,0},{4,7},{5,6},{6,5},{7,4},{8,11},{9,10},{10,... | collective-permute-start | bytes 196616 | tf_op jit(solution)/shard_map/ppermute | solution.py:42
  21.0 4.0 %collective-permute-start.7 = (bf16[256,128]{1,0:T(8,128)(2,1)S(1)}, bf16[256,128]{1,0:T(8,128)(2,1)S(1)}, u32[]{:S(2)}, u32[]{:S(2)}) collective-permute-start(bf16[256,128]{1,0:T(8,128)(2,1)S(1)} %shard_map.99.refs_0_), channel_id=1, source_target_pairs={{0,2},{1,0},{2,3},{3,1},{4,6},{5,4},{6,7},{7,5},{8,10},{9,8},{10,1... | collective-permute-start | bytes 196616 | tf_op jit(solution)/shard_map/ppermute | solution.py:42
  25.4 3.9 %collective-permute-start.10 = (bf16[256,128]{1,0:T(8,128)(2,1)S(1)}, bf16[256,128]{1,0:T(8,128)(2,1)S(1)}, u32[]{:S(2)}, u32[]{:S(2)}) collective-permute-start(bf16[256,128]{1,0:T(8,128)(2,1)S(1)} %get-tuple-element.28), channel_id=1, source_target_pairs={{0,4},{4,12},{8,0},{12,8},{1,5},{5,13},{9,1},{13,9},{2,6},{6,14},{... | collective-permute-start | bytes 196616 | tf_op jit(solution)/shard_map/ppermute | solution.py:42
  25.4 6.4 %collective-permute-start.11 = (bf16[256,128]{1,0:T(8,128)(2,1)S(1)}, bf16[256,128]{1,0:T(8,128)(2,1)S(1)}, u32[]{:S(2)}, u32[]{:S(2)}) collective-permute-start(bf16[256,128]{1,0:T(8,128)(2,1)S(1)} %get-tuple-element.29), channel_id=1, source_target_pairs={{0,12},{4,8},{8,4},{12,0},{1,13},{5,9},{9,5},{13,1},{2,14},{6,10},... | collective-permute-start | bytes 196616 | tf_op jit(solution)/shard_map/ppermute | solution.py:42
  28.6 3.6 %collective-permute-start.12 = (bf16[256,128]{1,0:T(8,128)(2,1)S(1)}, bf16[256,128]{1,0:T(8,128)(2,1)S(1)}, u32[]{:S(2)}, u32[]{:S(2)}) collective-permute-start(bf16[256,128]{1,0:T(8,128)(2,1)S(1)} %get-tuple-element.30), channel_id=1, source_target_pairs={{0,8},{4,0},{8,12},{12,4},{1,9},{5,1},{9,13},{13,5},{2,10},{6,2},{... | collective-permute-start | bytes 196616 | tf_op jit(solution)/shard_map/ppermute | solution.py:42

commit v12 on v11

--- a/solution.py
+++ b/solution.py
@@ -28,15 +28,15 @@
     return functools.partial(run, *after)
 
 
-def ring_place(k, n):
-    return k ^ (k >> 1) if n == 4 else k
+def ring_place(k, axis):
+    return k ^ (k >> 1) if axis == "col" and lax.axis_size(axis) == 4 else k
 
 
 def exchange(sends, axis, ahead):
     n = lax.axis_size(axis)
 
     def target(s, d):
-        return ring_place((ring_place(s, n) + (d if ahead else -d)) % n, n)
+        return ring_place((ring_place(s, axis) + (d if ahead else -d)) % n, axis)
 
     return [
         lax.ppermute(send, axis, [(s, target(s, d)) for s in range(n)])
@@ -45,7 +45,7 @@
 
 
 def odd_row():
-    return lax.rem(ring_place(lax.axis_index("row"), lax.axis_size("row")), 2) == 1
+    return lax.rem(lax.axis_index("row"), 2) == 1
 
 
 def neighbour(value, axis):
@@ -66,26 +66,26 @@
     return lax.dot_general(left, right, (dims, ((), ())), preferred_element_type=jnp.float32)
 
 
-def dense_kernel(n_row, n_col, piece, vals, rows_in, cols_in, count_in, near, rows, cols, count, sems):
+def dense_kernel(piece, vals, rows_in, cols_in, count_in, near, rows, cols, count, sems):
     copies = [
         pltpu.make_async_copy(source, target, sems.at[k])
         for k, (source, target) in enumerate(((rows_in, rows), (cols_in, cols), (count_in, count)))
     ]
     for copy in copies:
         copy.start()
-    my_row, my_col = lax.axis_index("row"), lax.axis_index("col")
     side = vals.shape[-1]
     near[...] = jnp.zeros_like(near)
     for copy in copies:
         copy.wait()
 
-    def ahead(there, here, n):
-        return lax.rem(ring_place(there, n) - ring_place(here, n) + n, n)
+    def ahead(there, axis):
+        n = lax.axis_size(axis)
+        return lax.rem(ring_place(there, axis) - ring_place(lax.axis_index(axis), axis) + n, n)
 
     def add(t, _):
         row, col = rows[0, 0, t], cols[0, 0, t]
-        row = ahead(row // piece, my_col, n_col) * piece + lax.rem(row, piece)
-        col = ahead(col // piece, my_row, n_row) * piece + lax.rem(col, piece)
+        row = ahead(row // piece, "col") * piece + lax.rem(row, piece)
+        col = ahead(col // piece, "row") * piece + lax.rem(col, piece)
         down = pl.ds(pl.multiple_of(row * side, side), side)
         across = pl.ds(pl.multiple_of(col * side, side), side)
         near[down, across] = vals[0, 0, t]
@@ -188,7 +188,7 @@
 
     gathered = exchange([features] * (n_row - 1), "row", False)
     (near,) = call(
-        functools.partial(dense_kernel, n_row, n_col, nodes // side),
+        functools.partial(dense_kernel, nodes // side),
         [((down, across), NARROW)],
         [VMEM] * 4,
         scratch=[

time: 33 us -> 32.4 us (0.982)
  the two profiles are of different devices: /device:TPU:1 before, /device:TPU:0 now
where the time goes in v12:
time: 32.4 us; the launch traced here: 32 us
  starting transfers between devices  16.1 us (50%)
  waiting for transfers between devices  10.1 us (31%)
  Pallas kernels  3.38 us (10%)
  between operations  1.41 us (4%)
  local copies, waits for them, and re-layouts  0.96 us (3%)
    ppermute x12, starting transfers between devices, exchange(): lax.ppermute(send, axis, [(s, target(s, d)) for s in range(n)])  16 us
    ppermute x12, waiting for transfers between devices, exchange(): lax.ppermute(send, axis, [(s, target(s, d)) for s in range(n)])  8.9 us
    ppermute x1, waiting for transfers between devices, neighbour(): return lax.ppermute(value, axis, [(s, s ^ 1) for s in range(n)])  1.19 us
    unnamed x12, local copies, waits for them, and re-layouts  0.96 us
    pallas_call x1, Pallas kernels, per_device(): call(functools.partial(last_kernel, scale), [((nodes, width), NARROW), ((...  0.7 us
    pallas_call x1, Pallas kernels, per_device(): act, = call(act_kernel, [((nodes, hidden), NARROW)], [VMEM])(pre)  0.65 us
    pallas_call x1, Pallas kernels, per_device(): call(functools.partial(dense_kernel, nodes // side), [((down, across), NA...  0.65 us
  transfers between devices with their start and end apart: 13, of which 9 were waited for; matrix products, arithmetic and copies ran while one was open for 0% of the time, Pallas kernels for 5%

profile of v12, /device:TPU:0, one launch (start us, length us, event | category | flops | bytes accessed | tf_op | source)
XLA Modules:
  0.0 32.0 jit_solution(15570470275576125604)
XLA Ops:
  0.6 0.0 copy-start.5
  0.6 0.0 copy-start.4
  0.7 3.0 %collective-permute-start.1 = (bf16[128,128]{1,0:T(8,128)(2,1)}, bf16[128,128]{1,0:T(8,128)(2,1)S(1)}, u32[]{:S(2)}, u32[]{:S(2)}) collective-permute-start(bf16[128,128]{1,0:T(8,128)(2,1)} %refs_0_.1), channel_id=1, source_target_pairs={{0,8},{4,12},{8,0},{12,4},{1,9},{5,13},{9,1},{13,5},{2,10},{6,14},... | collective-permute-start | bytes 98312 | tf_op jit(solution)/shard_map/ppermute | solution.py:42
  3.7 0.0 collective-permute-start
  3.7 0.5 %collective-permute-start.2 = (bf16[128,128]{1,0:T(8,128)(2,1)}, bf16[128,128]{1,0:T(8,128)(2,1)S(1)}, u32[]{:S(2)}, u32[]{:S(2)}) collective-permute-start(bf16[128,128]{1,0:T(8,128)(2,1)} %refs_0_.1), channel_id=1, source_target_pairs={{0,4},{4,8},{8,12},{12,0},{1,5},{5,9},{9,13},{13,1},{2,6},{6,10},{... | collective-permute-start | bytes 98312 | tf_op jit(solution)/shard_map/ppermute | solution.py:42
  4.8 0.0 copy-done.5
  4.8 0.0 copy-done.4
  4.8 0.0 copy-start
  4.8 0.9 %copy-done = bf16[1,1,8,128,128]{4,3,2,1,0:T(8,128)(2,1)S(1)} copy-done((bf16[1,1,8,128,128]{4,3,2,1,0:T(8,128)(2,1)S(1)}, bf16[1,1,8,128,128]{4,3,2,1,0:T(8,128)(2,1)}, u32[]{:S(2)}) %copy-start) | copy-done | bytes 262168
  5.8 0.0 copy-start.3
  5.8 0.7 %shard_map.94.near.matrix = bf16[512,512]{1,0:T(8,128)(2,1)S(1)} custom-call(bf16[1,1,8,128,128]{4,3,2,1,0:T(8,128)(2,1)S(1)} %copy-done, s32[1,1,8]{2,1,0:T(1,128)S(1)} %copy-done.4, s32[1,1,8]{2,1,0:T(1,128)S(1)} %copy-done.5, s32[1,1]{1,0:T(1,128)S(6)} %copy.10.count_in), custom_call_target="tpu_custom_call" | custom-call | bytes 1048576 | tf_op jit(solution)/shard_map/pallas_call | solution.py:190
  6.4 0.0 collective-permute-done.1.refs_2_
  6.5 0.0 collective-permute-done.refs_1_
  6.5 0.8 %collective-permute-done.2.refs_3_ = bf16[128,128]{1,0:T(8,128)(2,1)S(1)} collective-permute-done((bf16[128,128]{1,0:T(8,128)(2,1)}, bf16[128,128]{1,0:T(8,128)(2,1)S(1)}, u32[]{:S(2)}, u32[]{:S(2)}) %collective-permute-start.2) | collective-permute-done | bytes 32800 | tf_op jit(solution)/shard_map/ppermute | solution.py:42
  7.3 0.0 copy-done.3
  7.3 0.3 shard_map.96
  7.6 1.6 %collective-permute-start.3 = (bf16[128,128]{1,0:T(8,128)(2,1)S(1)}, bf16[128,128]{1,0:T(8,128)(2,1)S(1)}, u32[]{:S(2)}, u32[]{:S(2)}) collective-permute-start(bf16[128,128]{1,0:T(8,128)(2,1)S(1)} %get-tuple-element.19), channel_id=1, source_target_pairs={{0,1},{1,3},{2,0},{3,2},{4,5},{5,7},{6,4},{7,6},{8,9},{9,11},{10,8... | collective-permute-start | bytes 98312 | tf_op jit(solution)/shard_map/ppermute | solution.py:42
  9.2 2.5 %collective-permute-start.4 = (bf16[128,128]{1,0:T(8,128)(2,1)S(1)}, bf16[128,128]{1,0:T(8,128)(2,1)S(1)}, u32[]{:S(2)}, u32[]{:S(2)}) collective-permute-start(bf16[128,128]{1,0:T(8,128)(2,1)S(1)} %get-tuple-element.20), channel_id=1, source_target_pairs={{0,3},{1,2},{2,1},{3,0},{4,7},{5,6},{6,5},{7,4},{8,11},{9,10},{10,... | collective-permute-start | bytes 98312 | tf_op jit(solution)/shard_map/ppermute | solution.py:42
  11.7 0.0 copy-start.1
  11.7 0.0 copy-start.2
  11.7 1.6 %collective-permute-start.5 = (bf16[128,128]{1,0:T(8,128)(2,1)S(1)}, bf16[128,128]{1,0:T(8,128)(2,1)S(1)}, u32[]{:S(2)}, u32[]{:S(2)}) collective-permute-start(bf16[128,128]{1,0:T(8,128)(2,1)S(1)} %get-tuple-element.21), channel_id=1, source_target_pairs={{0,2},{1,0},{2,3},{3,1},{4,6},{5,4},{6,7},{7,5},{8,10},{9,8},{10,1... | collective-permute-start | bytes 98312 | tf_op jit(solution)/shard_map/ppermute | solution.py:42
  13.3 0.3 %shard_map.95.refs_0_.matrix = bf16[512,512]{1,0:T(8,128)(2,1)S(1)} custom-call(bf16[512,512]{1,0:T(8,128)(2,1)S(1)} %shard_map.94.near.matrix), custom_call_target="tpu_custom_call" | custom-call | bytes 1572864 | tf_op jit(solution)/shard_map/pallas_call | solution.py:211
  13.6 0.0 collective-permute-done.3.refs_2_
  13.6 1.6 %collective-permute-done.4.refs_3_ = bf16[128,128]{1,0:T(8,128)(2,1)S(1)} collective-permute-done((bf16[128,128]{1,0:T(8,128)(2,1)S(1)}, bf16[128,128]{1,0:T(8,128)(2,1)S(1)}, u32[]{:S(2)}, u32[]{:S(2)}) %collective-permute-start.4) | collective-permute-done | bytes 32800 | tf_op jit(solution)/shard_map/ppermute | solution.py:42
  15.2 0.4 %collective-permute-done.5.refs_4_ = bf16[128,128]{1,0:T(8,128)(2,1)S(1)} collective-permute-done((bf16[128,128]{1,0:T(8,128)(2,1)S(1)}, bf16[128,128]{1,0:T(8,128)(2,1)S(1)}, u32[]{:S(2)}, u32[]{:S(2)}) %collective-permute-start.5) | collective-permute-done | bytes 32800 | tf_op jit(solution)/shard_map/ppermute | solution.py:42
  15.6 0.0 copy-done.1
  15.6 0.0 copy-done.2
  15.6 0.4 %shard_map.97 = (bf16[128,128]{1,0:T(8,128)(2,1)S(1)}, f32[128,128]{1,0:T(8,128)S(1)}, bf16[128,128]{1,0:T(8,128)(2,1)S(1)}, f32[128,256]{1,0:T(8,128)S(1)}) custom-call(bf16[512,512]{1,0:T(8,128)(2,1)S(1)} %shard_map.95.refs_0_.matrix, f32[128,128]{1,0:T(8,128)S(1)} %get-tuple-element.18.refs_1_, bf16[128,128]{1,0:T(8,128)(2,1)S(1)} %collective-permute-done.3.refs_2_, ...), custom_call_target="tpu_custom_call" | custom-call | flops 58720256 | tf_op jit(solution)/shard_map/pallas_call | solution.py:221
  16.1 0.1 collective-permute-start.6
  16.1 1.2 %collective-permute-done.6.came = bf16[128,128]{1,0:T(8,128)(2,1)S(1)} collective-permute-done((bf16[128,128]{1,0:T(8,128)(2,1)S(1)}, bf16[128,128]{1,0:T(8,128)(2,1)S(1)}, u32[]{:S(2)}, u32[]{:S(2)}) %collective-permute-start.6) | collective-permute-done | bytes 32800 | tf_op jit(solution)/shard_map/ppermute | solution.py:53
  17.4 1.1 %collective-permute-start.9 = (bf16[256,128]{1,0:T(8,128)(2,1)S(1)}, bf16[256,128]{1,0:T(8,128)(2,1)S(1)}, u32[]{:S(2)}, u32[]{:S(2)}) collective-permute-start(bf16[256,128]{1,0:T(8,128)(2,1)S(1)} %shard_map.99.refs_0_), channel_id=1, source_target_pairs={{0,1},{1,3},{2,0},{3,2},{4,5},{5,7},{6,4},{7,6},{8,9},{9,11},{10,8... | collective-permute-start | bytes 196616 | tf_op jit(solution)/shard_map/ppermute | solution.py:42
  18.4 2.9 %collective-permute-start.8 = (bf16[256,128]{1,0:T(8,128)(2,1)S(1)}, bf16[256,128]{1,0:T(8,128)(2,1)S(1)}, u32[]{:S(2)}, u32[]{:S(2)}) collective-permute-start(bf16[256,128]{1,0:T(8,128)(2,1)S(1)} %shard_map.99.refs_0_), channel_id=1, source_target_pairs={{0,3},{1,2},{2,1},{3,0},{4,7},{5,6},{6,5},{7,4},{8,11},{9,10},{10,... | collective-permute-start | bytes 196616 | tf_op jit(solution)/shard_map/ppermute | solution.py:42
  21.4 0.1 collective-permute-start.7
  21.5 2.3 %collective-permute-done.9.refs_3_ = bf16[256,128]{1,0:T(8,128)(2,1)S(1)} collective-permute-done((bf16[256,128]{1,0:T(8,128)(2,1)S(1)}, bf16[256,128]{1,0:T(8,128)(2,1)S(1)}, u32[]{:S(2)}, u32[]{:S(2)}) %collective-permute-start.9) | collective-permute-done | bytes 65568 | tf_op jit(solution)/shard_map/ppermute | solution.py:42
  23.8 1.9 %collective-permute-done.8.refs_2_ = bf16[256,128]{1,0:T(8,128)(2,1)S(1)} collective-permute-done((bf16[256,128]{1,0:T(8,128)(2,1)S(1)}, bf16[256,128]{1,0:T(8,128)(2,1)S(1)}, u32[]{:S(2)}, u32[]{:S(2)}) %collective-permute-start.8) | collective-permute-done | bytes 65568 | tf_op jit(solution)/shard_map/ppermute | solution.py:42
  25.6 0.4 %collective-permute-done.7.refs_1_ = bf16[256,128]{1,0:T(8,128)(2,1)S(1)} collective-permute-done((bf16[256,128]{1,0:T(8,128)(2,1)S(1)}, bf16[256,128]{1,0:T(8,128)(2,1)S(1)}, u32[]{:S(2)}, u32[]{:S(2)}) %collective-permute-start.7) | collective-permute-done | bytes 65568 | tf_op jit(solution)/shard_map/ppermute | solution.py:42
  26.0 0.3 shard_map.100
  26.3 0.1 collective-permute-start.10
  26.4 1.3 %collective-permute-start.11 = (bf16[256,128]{1,0:T(8,128)(2,1)S(1)}, bf16[256,128]{1,0:T(8,128)(2,1)S(1)}, u32[]{:S(2)}, u32[]{:S(2)}) collective-permute-start(bf16[256,128]{1,0:T(8,128)(2,1)S(1)} %get-tuple-element.29), channel_id=1, source_target_pairs={{0,8},{4,12},{8,0},{12,4},{1,9},{5,13},{9,1},{13,5},{2,10},{6,14},... | collective-permute-start | bytes 196616 | tf_op jit(solution)/shard_map/ppermute | solution.py:42
  27.6 1.4 %collective-permute-start.12 = (bf16[256,128]{1,0:T(8,128)(2,1)S(1)}, bf16[256,128]{1,0:T(8,128)(2,1)S(1)}, u32[]{:S(2)}, u32[]{:S(2)}) collective-permute-start(bf16[256,128]{1,0:T(8,128)(2,1)S(1)} %get-tuple-element.30), channel_id=1, source_target_pairs={{0,12},{4,0},{8,4},{12,8},{1,13},{5,1},{9,5},{13,9},{2,14},{6,2},{... | collective-permute-start | bytes 196616 | tf_op jit(solution)/shard_map/ppermute | solution.py:42
  29.0 0.7 %shard_map.98 = bf16[128,256]{1,0:T(8,128)(2,1)} custom-call(f32[128,256]{1,0:T(8,128)S(1)} %get-tuple-element.22.pre), custom_call_target="tpu_custom_call" | custom-call | tf_op jit(solution)/shard_map/pallas_call | solution.py:235
  29.7 0.5 %collective-permute-done.10.refs_0_ = bf16[256,128]{1,0:T(8,128)(2,1)S(1)} collective-permute-done((bf16[256,128]{1,0:T(8,128)(2,1)S(1)}, bf16[256,128]{1,0:T(8,128)(2,1)S(1)}, u32[]{:S(2)}, u32[]{:S(2)}) %collective-permute-start.10) | collective-permute-done | bytes 65568 | tf_op jit(solution)/shard_map/ppermute | solution.py:42
  30.2 1.1 %collective-permute-done.11.refs_1_ = bf16[256,128]{1,0:T(8,128)(2,1)S(1)} collective-permute-done((bf16[256,128]{1,0:T(8,128)(2,1)S(1)}, bf16[256,128]{1,0:T(8,128)(2,1)S(1)}, u32[]{:S(2)}, u32[]{:S(2)}) %collective-permute-start.11) | collective-permute-done | bytes 65568 | tf_op jit(solution)/shard_map/ppermute | solution.py:42
  31.3 0.0 collective-permute-done.12.refs_2_
  31.3 0.7 %shard_map.101 = (bf16[128,128]{1,0:T(8,128)(2,1)}, f32[128,256]{1,0:T(8,128)}) custom-call(f32[128,128]{1,0:T(8,128)S(1)} %get-tuple-element.26.own, bf16[128,128]{1,0:T(8,128)(2,1)S(1)} %get-tuple-element.27.kept, bf16[256,128]{1,0:T(8,128)(2,1)S(1)} %collective-permute-done.10.refs_0_, bf16[256,128]{1,0:T(8,128)(2,1)S(1)} %collective-permute-done.11.refs_1_, ...), custom_call_target="tpu_custom_call" | custom-call | tf_op jit(solution)/shard_map/pallas_call | solution.py:247
  (1 shorter events, 0.0 us)
Async XLA Ops:
  0.6 4.2 %copy-start.5 = (s32[1,1,8]{2,1,0:T(1,128)S(1)}, s32[1,1,8]{2,1,0:T(1,128)}, u32[]{:S(2)}) copy-start(s32[1,1,8]{2,1,0:T(1,128)} %cols_in.1) | copy-start | bytes 100
  0.6 4.2 %copy-start.4 = (s32[1,1,8]{2,1,0:T(1,128)S(1)}, s32[1,1,8]{2,1,0:T(1,128)}, u32[]{:S(2)}) copy-start(s32[1,1,8]{2,1,0:T(1,128)} %rows_in.1) | copy-start | bytes 100
  0.7 5.8 %collective-permute-start.1 = (bf16[128,128]{1,0:T(8,128)(2,1)}, bf16[128,128]{1,0:T(8,128)(2,1)S(1)}, u32[]{:S(2)}, u32[]{:S(2)}) collective-permute-start(bf16[128,128]{1,0:T(8,128)(2,1)} %refs_0_.1), channel_id=1, source_target_pairs={{0,8},{4,12},{8,0},{12,4},{1,9},{5,13},{9,1},{13,5},{2,10},{6,14},... | collective-permute-start | bytes 98312 | tf_op jit(solution)/shard_map/ppermute | solution.py:42
  3.7 2.8 %collective-permute-start = (bf16[128,128]{1,0:T(8,128)(2,1)}, bf16[128,128]{1,0:T(8,128)(2,1)S(1)}, u32[]{:S(2)}, u32[]{:S(2)}) collective-permute-start(bf16[128,128]{1,0:T(8,128)(2,1)} %refs_0_.1), channel_id=1, source_target_pairs={{0,12},{4,0},{8,4},{12,8},{1,13},{5,1},{9,5},{13,9},{2,14},{6,2},{... | collective-permute-start | bytes 98312 | tf_op jit(solution)/shard_map/ppermute | solution.py:42
  3.7 3.6 %collective-permute-start.2 = (bf16[128,128]{1,0:T(8,128)(2,1)}, bf16[128,128]{1,0:T(8,128)(2,1)S(1)}, u32[]{:S(2)}, u32[]{:S(2)}) collective-permute-start(bf16[128,128]{1,0:T(8,128)(2,1)} %refs_0_.1), channel_id=1, source_target_pairs={{0,4},{4,8},{8,12},{12,0},{1,5},{5,9},{9,13},{13,1},{2,6},{6,10},{... | collective-permute-start | bytes 98312 | tf_op jit(solution)/shard_map/ppermute | solution.py:42
  4.8 1.0 %copy-start = (bf16[1,1,8,128,128]{4,3,2,1,0:T(8,128)(2,1)S(1)}, bf16[1,1,8,128,128]{4,3,2,1,0:T(8,128)(2,1)}, u32[]{:S(2)}) copy-start(bf16[1,1,8,128,128]{4,3,2,1,0:T(8,128)(2,1)} %vals.1) | copy-start | bytes 786436
  5.8 1.5 %copy-start.3 = (bf16[128,128]{1,0:T(8,128)(2,1)S(1)}, bf16[128,128]{1,0:T(8,128)(2,1)}, u32[]{:S(2)}) copy-start(bf16[128,128]{1,0:T(8,128)(2,1)} %refs_0_.1) | copy-start | bytes 98308
  7.6 6.0 %collective-permute-start.3 = (bf16[128,128]{1,0:T(8,128)(2,1)S(1)}, bf16[128,128]{1,0:T(8,128)(2,1)S(1)}, u32[]{:S(2)}, u32[]{:S(2)}) collective-permute-start(bf16[128,128]{1,0:T(8,128)(2,1)S(1)} %get-tuple-element.19), channel_id=1, source_target_pairs={{0,1},{1,3},{2,0},{3,2},{4,5},{5,7},{6,4},{7,6},{8,9},{9,11},{10,8... | collective-permute-start | bytes 98312 | tf_op jit(solution)/shard_map/ppermute | solution.py:42
  9.2 6.0 %collective-permute-start.4 = (bf16[128,128]{1,0:T(8,128)(2,1)S(1)}, bf16[128,128]{1,0:T(8,128)(2,1)S(1)}, u32[]{:S(2)}, u32[]{:S(2)}) collective-permute-start(bf16[128,128]{1,0:T(8,128)(2,1)S(1)} %get-tuple-element.20), channel_id=1, source_target_pairs={{0,3},{1,2},{2,1},{3,0},{4,7},{5,6},{6,5},{7,4},{8,11},{9,10},{10,... | collective-permute-start | bytes 98312 | tf_op jit(solution)/shard_map/ppermute | solution.py:42
  11.7 3.9 %copy-start.1 = (bf16[128,256]{1,0:T(8,128)(2,1)S(1)}, bf16[128,256]{1,0:T(8,128)(2,1)}, u32[]{:S(2)}) copy-start(bf16[128,256]{1,0:T(8,128)(2,1)} %refs_5_.1) | copy-start | bytes 196612
  11.7 3.9 %copy-start.2 = (bf16[128,256]{1,0:T(8,128)(2,1)S(1)}, bf16[128,256]{1,0:T(8,128)(2,1)}, u32[]{:S(2)}) copy-start(bf16[128,256]{1,0:T(8,128)(2,1)} %refs_6_.1) | copy-start | bytes 196612
  11.7 3.9 %collective-permute-start.5 = (bf16[128,128]{1,0:T(8,128)(2,1)S(1)}, bf16[128,128]{1,0:T(8,128)(2,1)S(1)}, u32[]{:S(2)}, u32[]{:S(2)}) collective-permute-start(bf16[128,128]{1,0:T(8,128)(2,1)S(1)} %get-tuple-element.21), channel_id=1, source_target_pairs={{0,2},{1,0},{2,3},{3,1},{4,6},{5,4},{6,7},{7,5},{8,10},{9,8},{10,1... | collective-permute-start | bytes 98312 | tf_op jit(solution)/shard_map/ppermute | solution.py:42
  16.1 1.3 %collective-permute-start.6 = (bf16[128,128]{1,0:T(8,128)(2,1)S(1)}, bf16[128,128]{1,0:T(8,128)(2,1)S(1)}, u32[]{:S(2)}, u32[]{:S(2)}) collective-permute-start(bf16[128,128]{1,0:T(8,128)(2,1)S(1)} %get-tuple-element.25), channel_id=1, source_target_pairs={{0,4},{4,0},{8,12},{12,8},{1,5},{5,1},{9,13},{13,9},{2,6},{6,2},{1... | collective-permute-start | bytes 98312 | tf_op jit(solution)/shard_map/ppermute | solution.py:53
  17.4 6.4 %collective-permute-start.9 = (bf16[256,128]{1,0:T(8,128)(2,1)S(1)}, bf16[256,128]{1,0:T(8,128)(2,1)S(1)}, u32[]{:S(2)}, u32[]{:S(2)}) collective-permute-start(bf16[256,128]{1,0:T(8,128)(2,1)S(1)} %shard_map.99.refs_0_), channel_id=1, source_target_pairs={{0,1},{1,3},{2,0},{3,2},{4,5},{5,7},{6,4},{7,6},{8,9},{9,11},{10,8... | collective-permute-start | bytes 196616 | tf_op jit(solution)/shard_map/ppermute | solution.py:42
  18.4 7.2 %collective-permute-start.8 = (bf16[256,128]{1,0:T(8,128)(2,1)S(1)}, bf16[256,128]{1,0:T(8,128)(2,1)S(1)}, u32[]{:S(2)}, u32[]{:S(2)}) collective-permute-start(bf16[256,128]{1,0:T(8,128)(2,1)S(1)} %shard_map.99.refs_0_), channel_id=1, source_target_pairs={{0,3},{1,2},{2,1},{3,0},{4,7},{5,6},{6,5},{7,4},{8,11},{9,10},{10,... | collective-permute-start | bytes 196616 | tf_op jit(solution)/shard_map/ppermute | solution.py:42
  21.4 4.7 %collective-permute-start.7 = (bf16[256,128]{1,0:T(8,128)(2,1)S(1)}, bf16[256,128]{1,0:T(8,128)(2,1)S(1)}, u32[]{:S(2)}, u32[]{:S(2)}) collective-permute-start(bf16[256,128]{1,0:T(8,128)(2,1)S(1)} %shard_map.99.refs_0_), channel_id=1, source_target_pairs={{0,2},{1,0},{2,3},{3,1},{4,6},{5,4},{6,7},{7,5},{8,10},{9,8},{10,1... | collective-permute-start | bytes 196616 | tf_op jit(solution)/shard_map/ppermute | solution.py:42
  26.3 3.8 %collective-permute-start.10 = (bf16[256,128]{1,0:T(8,128)(2,1)S(1)}, bf16[256,128]{1,0:T(8,128)(2,1)S(1)}, u32[]{:S(2)}, u32[]{:S(2)}) collective-permute-start(bf16[256,128]{1,0:T(8,128)(2,1)S(1)} %get-tuple-element.28), channel_id=1, source_target_pairs={{0,4},{4,8},{8,12},{12,0},{1,5},{5,9},{9,13},{13,1},{2,6},{6,10},{... | collective-permute-start | bytes 196616 | tf_op jit(solution)/shard_map/ppermute | solution.py:42
  26.4 4.9 %collective-permute-start.11 = (bf16[256,128]{1,0:T(8,128)(2,1)S(1)}, bf16[256,128]{1,0:T(8,128)(2,1)S(1)}, u32[]{:S(2)}, u32[]{:S(2)}) collective-permute-start(bf16[256,128]{1,0:T(8,128)(2,1)S(1)} %get-tuple-element.29), channel_id=1, source_target_pairs={{0,8},{4,12},{8,0},{12,4},{1,9},{5,13},{9,1},{13,5},{2,10},{6,14},... | collective-permute-start | bytes 196616 | tf_op jit(solution)/shard_map/ppermute | solution.py:42
  27.6 3.6 %collective-permute-start.12 = (bf16[256,128]{1,0:T(8,128)(2,1)S(1)}, bf16[256,128]{1,0:T(8,128)(2,1)S(1)}, u32[]{:S(2)}, u32[]{:S(2)}) collective-permute-start(bf16[256,128]{1,0:T(8,128)(2,1)S(1)} %get-tuple-element.30), channel_id=1, source_target_pairs={{0,12},{4,0},{8,4},{12,8},{1,13},{5,1},{9,5},{13,9},{2,14},{6,2},{... | collective-permute-start | bytes 196616 | tf_op jit(solution)/shard_map/ppermute | solution.py:42

commit v13 on v12

--- a/solution.py
+++ b/solution.py
@@ -48,9 +48,9 @@
     return lax.rem(lax.axis_index("row"), 2) == 1
 
 
-def neighbour(value, axis):
+def swap(value, axis, distance):
     n = lax.axis_size(axis)
-    return lax.ppermute(value, axis, [(s, s ^ 1) for s in range(n)])
+    return lax.ppermute(value, axis, [(s, s ^ distance) for s in range(n)])
 
 
 def wide(value):
@@ -66,7 +66,7 @@
     return lax.dot_general(left, right, (dims, ((), ())), preferred_element_type=jnp.float32)
 
 
-def dense_kernel(piece, vals, rows_in, cols_in, count_in, near, rows, cols, count, sems):
+def dense_kernel(piece, paired, vals, rows_in, cols_in, count_in, near, rows, cols, count, sems):
     copies = [
         pltpu.make_async_copy(source, target, sems.at[k])
         for k, (source, target) in enumerate(((rows_in, rows), (cols_in, cols), (count_in, count)))
@@ -84,7 +84,11 @@
 
     def add(t, _):
         row, col = rows[0, 0, t], cols[0, 0, t]
-        row = ahead(row // piece, "col") * piece + lax.rem(row, piece)
+        if paired:
+            place = lax.rem((row // piece) ^ lax.axis_index("col"), 2) * 2 + row // piece // 2
+        else:
+            place = ahead(row // piece, "col")
+        row = place * piece + lax.rem(row, piece)
         col = ahead(col // piece, "row") * piece + lax.rem(col, piece)
         down = pl.ds(pl.multiple_of(row * side, side), side)
         across = pl.ds(pl.multiple_of(col * side, side), side)
@@ -120,26 +124,69 @@
         send[...] = product[d * rows : (d + 1) * rows].astype(send.dtype)
 
 
-def layer_kernel(*refs):
-    *parts, weight, cotangent, back, mine, other, pre_out = refs
+def layer(total, weight, cotangent):
+    high, low = split(total)
+    pre = dot(high, weight) + dot(low, weight)
+    sigma = jax.nn.sigmoid(pre)
+    grad = wide(cotangent) * sigma * (1.0 + pre * (1.0 - sigma))
+    grad_high, grad_low = split(grad)
+    across, down = ((1,), (1,)), ((0,), (0,))
+    back = dot(grad_high, weight, across) + dot(grad_low, weight, across)
+    term = dot(high, grad_high, down) + dot(low, grad_high, down) + dot(high, grad_low, down)
+    return pre, back, term
+
+
+def halve(term, mine, other):
     half = mine.shape[1]
-    total = tree([wide(part[...]) for part in parts])
-    high, low = split(total)
-    pre = dot(high, weight[...]) + dot(low, weight[...])
-    pre_out[...] = pre
-    sigma = jax.nn.sigmoid(pre)
-    grad = wide(cotangent[...]) * sigma * (1.0 + pre * (1.0 - sigma))
-    grad_high, grad_low = split(grad)
-    down = ((0,), (0,))
-    term = dot(high, grad_high, down) + dot(low, grad_high, down) + dot(high, grad_low, down)
     odd = odd_row()
     left, right = term[:, :half], term[:, half:]
     mine[...] = jnp.where(odd, right, left)
     other[...] = jnp.where(odd, left, right).astype(other.dtype)
-    across = ((1,), (1,))
-    back[...] = (dot(grad_high, weight[...], across) + dot(grad_low, weight[...], across)).astype(
-        back.dtype
-    )
+
+
+def layer_kernel(*refs):
+    *parts, weight, cotangent, back_out, mine, other, pre_out = refs
+    total = tree([wide(part[...]) for part in parts])
+    pre, back, term = layer(total, weight[...], cotangent[...])
+    pre_out[...] = pre
+    back_out[...] = back.astype(back_out.dtype)
+    halve(term, mine, other)
+
+
+def in_middle():
+    my_col = lax.axis_index("col")
+    return (my_col == 1) | (my_col == 2)
+
+
+def paired_forward_kernel(n, matrix, *refs):
+    operands, (own, first, second, third) = refs[:n], refs[n:]
+    stacked = jnp.concatenate([operand[...] for operand in operands], axis=0)
+    product = dot(matrix[...], stacked).astype(own.dtype)
+    rows = own.shape[0]
+    same, other = product[:rows], product[rows:]
+    middle = in_middle()
+    own[...] = same
+    first[...] = jnp.where(middle, same, other)
+    second[...] = other
+    third[...] = jnp.where(middle, other, same)
+
+
+def paired_layer_kernel(own, first, second, third, weight, cotangent, beyond, *refs):
+    back_out, mine, other, pre_out = refs
+    nodes = cotangent.shape[0]
+    middle = in_middle()
+    partner = jnp.where(middle, third[...], first[...])
+    side = jnp.where(middle, first[...], third[...])
+    total = (wide(own[...]) + wide(partner)) + (wide(second[...]) + wide(side))
+    high_col = lax.axis_index("col") >= 2
+    here, there = cotangent[...], beyond[...]
+    both = jnp.concatenate(
+        [jnp.where(high_col, there, here), jnp.where(high_col, here, there)], axis=0
+    )
+    pre, back, term = layer(total, weight[...], both)
+    pre_out[...] = jnp.where(high_col, pre[nodes:], pre[:nodes])
+    back_out[...] = back.astype(back_out.dtype)
+    halve(term, mine, other)
 
 
 def message_kernel(back, mine, came, message):
@@ -154,11 +201,11 @@
 
 def backward_kernel(n, matrix, *refs):
     messages, own, kept, sends = refs[:n], refs[n], refs[n + 1], refs[n + 2 :]
-    rows = own.shape[0]
-    stacked = jnp.concatenate([message[:rows] for message in messages], axis=0)
+    rows, backs = own.shape[0], messages[0].shape[0] - kept.shape[0]
+    stacked = jnp.concatenate([message[:backs] for message in messages], axis=0)
     product = dot(matrix[...], stacked)
     own[...] = product[:rows]
-    term = tree([wide(message[rows:]) for message in messages]).astype(kept.dtype)
+    term = tree([wide(message[backs:]) for message in messages]).astype(kept.dtype)
     kept[...] = term
     for d, send in enumerate(sends, 1):
         send[:rows] = product[d * rows : (d + 1) * rows].astype(send.dtype)
@@ -186,9 +233,10 @@
     down, across = n_col * nodes, n_row * nodes
     dense_bytes = 2 * down * across
 
+    paired = n_col == 4
     gathered = exchange([features] * (n_row - 1), "row", False)
     (near,) = call(
-        functools.partial(dense_kernel, nodes // side),
+        functools.partial(dense_kernel, nodes // side, paired),
         [((down, across), NARROW)],
         [VMEM] * 4,
         scratch=[
@@ -200,13 +248,25 @@
         need=2 * dense_bytes,
     )(tile_values, tile_rows, tile_cols, tile_count)
 
-    own, *sends = call(
-        functools.partial(forward_kernel, n_row),
-        [((nodes, width), jnp.float32)] + [((nodes, width), NARROW)] * (n_col - 1),
-        [VMEM] * (1 + n_row),
-        flops=2 * down * across * width,
-        need=2 * dense_bytes,
-    )(near, features, *gathered)
+    forward = dict(flops=2 * down * across * width, need=2 * dense_bytes)
+    if paired:
+        layers = 2
+        own, *sends = call(
+            functools.partial(paired_forward_kernel, n_row),
+            [((2 * nodes, width), NARROW)] * 4,
+            [VMEM] * (1 + n_row),
+            **forward,
+        )(near, features, *gathered)
+        layer_call, cotangents = paired_layer_kernel, [cotangent, swap(cotangent, "col", 2)]
+    else:
+        layers = 1
+        own, *sends = call(
+            functools.partial(forward_kernel, n_row),
+            [((nodes, width), jnp.float32)] + [((nodes, width), NARROW)] * (n_col - 1),
+            [VMEM] * (1 + n_row),
+            **forward,
+        )(near, features, *gathered)
+        layer_call, cotangents = layer_kernel, [cotangent]
     parts = exchange(sends, "col", True)
     (far,) = call(
         functools.partial(turn_kernel, side),
@@ -217,29 +277,33 @@
 
     half = hidden // 2
     square = (width, half)
-    message = ((nodes + width, width), NARROW)
     back, mine, other, pre = call(
-        layer_kernel,
+        layer_call,
         [
-            ((nodes, width), NARROW),
+            ((layers * nodes, width), NARROW),
             (square, jnp.float32),
             (square, NARROW),
             ((nodes, hidden), jnp.float32),
         ],
-        [VMEM] * (n_col + 2),
-        flops=14 * nodes * width * hidden,
+        [VMEM] * (n_col + 1 + len(cotangents)),
+        flops=14 * layers * nodes * width * hidden,
         after=[far],
-    )(own, *parts, weight, cotangent)
-    (sent,) = call(message_kernel, [message], [VMEM] * 3)(back, mine, neighbour(other, "row"))
-    spread = exchange([sent] * (n_col - 1), "col", False)
+    )(own, *parts, weight, *cotangents)
+    (sent,) = call(message_kernel, [((layers * nodes + width, width), NARROW)], [VMEM] * 3)(
+        back, mine, swap(other, "row", 1)
+    )
+    if paired:
+        spread = [swap(sent, "col", 1)]
+    else:
+        spread = exchange([sent] * (n_col - 1), "col", False)
     (act,) = call(act_kernel, [((nodes, hidden), NARROW)], [VMEM])(pre)
 
+    message = ((nodes + width, width), NARROW)
     own, kept, *sends = call(
-        functools.partial(backward_kernel, n_col),
+        functools.partial(backward_kernel, 1 + len(spread)),
         [((nodes, width), jnp.float32), (square, NARROW)] + [message] * (n_row - 1),
-        [VMEM] * (1 + n_col),
-        flops=2 * down * across * width,
-        need=2 * dense_bytes,
+        [VMEM] * (2 + len(spread)),
+        **forward,
     )(far, sent, *spread)
     parts = exchange(sends, "row", True)
 

time: 32.4 us -> 31.4 us (0.969)
  starting transfers between devices: 16.1 us -> 13.4 us
  waiting for transfers between devices: 10.1 us -> 11.8 us
    ppermute x12 -> x9, starting transfers between devices: 16 us -> 8.72 us  [exchange(): lax.ppermute(send, axis, [(s, target(s, d)) for s in range(n)])]
    ppermute x1 -> x3, starting transfers between devices: 0.07 us -> 4.7 us  [swap(): return lax.ppermute(value, axis, [(s, s ^ distance) for s in range(n)])]
    ppermute x1 -> x3, waiting for transfers between devices: 1.19 us -> 4.32 us  [swap(): return lax.ppermute(value, axis, [(s, s ^ distance) for s in range(n)])]
    ppermute x12 -> x9, waiting for transfers between devices: 8.9 us -> 7.52 us  [exchange(): lax.ppermute(send, axis, [(s, target(s, d)) for s in range(n)])]
  transfers between devices with their start and end apart: 13 -> 12, of which waited for: 9 -> 7; matrix products, arithmetic and copies ran while one was open for 0% -> 0% of each run, Pallas kernels for 5% -> 7%
where the time goes in v13:
time: 31.4 us; the launch traced here: 31.3 us
  starting transfers between devices  13.4 us (43%)
  waiting for transfers between devices  11.8 us (38%)
  Pallas kernels  3.62 us (12%)
  between operations  1.42 us (5%)
  local copies, waits for them, and re-layouts  0.96 us (3%)
    ppermute x9, starting transfers between devices, exchange(): lax.ppermute(send, axis, [(s, target(s, d)) for s in range(n)])  8.72 us
    ppermute x9, waiting for transfers between devices, exchange(): lax.ppermute(send, axis, [(s, target(s, d)) for s in range(n)])  7.52 us
    ppermute x3, starting transfers between devices, swap(): return lax.ppermute(value, axis, [(s, s ^ distance) for s in range(n)])  4.7 us
    ppermute x3, waiting for transfers between devices, swap(): return lax.ppermute(value, axis, [(s, s ^ distance) for s in range(n)])  4.32 us
    unnamed x12, local copies, waits for them, and re-layouts  0.96 us
    pallas_call x1, Pallas kernels, per_device(): call(functools.partial(dense_kernel, nodes // side, paired), [((down, acr...  0.81 us
    pallas_call x1, Pallas kernels, per_device(): call(functools.partial(last_kernel, scale), [((nodes, width), NARROW), ((...  0.69 us
    pallas_call x1, Pallas kernels, per_device(): act, = call(act_kernel, [((nodes, hidden), NARROW)], [VMEM])(pre)  0.65 us
  transfers between devices with their start and end apart: 12, of which 7 were waited for; matrix products, arithmetic and copies ran while one was open for 0% of the time, Pallas kernels for 7%

profile of v13, /device:TPU:0, one launch (start us, length us, event | category | flops | bytes accessed | tf_op | source)
XLA Modules:
  0.0 31.3 jit_solution(7667267730962471037)
XLA Ops:
  0.6 0.0 copy-start.4
  0.6 0.0 copy-start.5
  0.7 2.4 %collective-permute-start = (bf16[128,128]{1,0:T(8,128)(2,1)}, bf16[128,128]{1,0:T(8,128)(2,1)S(1)}, u32[]{:S(2)}, u32[]{:S(2)}) collective-permute-start(bf16[128,128]{1,0:T(8,128)(2,1)} %refs_0_.1), channel_id=1, source_target_pairs={{0,12},{4,0},{8,4},{12,8},{1,13},{5,1},{9,5},{13,9},{2,14},{6,2},{... | collective-permute-start | bytes 98312 | tf_op jit(solution)/shard_map/ppermute | solution.py:42
  3.1 0.6 %collective-permute-start.1 = (bf16[128,128]{1,0:T(8,128)(2,1)}, bf16[128,128]{1,0:T(8,128)(2,1)S(1)}, u32[]{:S(2)}, u32[]{:S(2)}) collective-permute-start(bf16[128,128]{1,0:T(8,128)(2,1)} %refs_0_.1), channel_id=1, source_target_pairs={{0,8},{4,12},{8,0},{12,4},{1,9},{5,13},{9,1},{13,5},{2,10},{6,14},... | collective-permute-start | bytes 98312 | tf_op jit(solution)/shard_map/ppermute | solution.py:42
  3.7 0.2 collective-permute-start.2
  3.9 2.6 %collective-permute-start.6 = (bf16[128,256]{1,0:T(8,128)(2,1)}, bf16[128,256]{1,0:T(8,128)(2,1)S(1)}, u32[]{:S(2)}, u32[]{:S(2)}) collective-permute-start(bf16[128,256]{1,0:T(8,128)(2,1)} %refs_6_.1), channel_id=1, source_target_pairs={{0,2},{1,3},{2,0},{3,1},{4,6},{5,7},{6,4},{7,5},{8,10},{9,11},{10,... | collective-permute-start | bytes 196616 | tf_op jit(solution)/shard_map/ppermute | solution.py:53
  7.1 0.0 copy-done.4
  7.1 0.0 copy-done.5
  7.1 0.0 copy-start
  7.2 0.9 %copy-done = bf16[1,1,8,128,128]{4,3,2,1,0:T(8,128)(2,1)S(1)} copy-done((bf16[1,1,8,128,128]{4,3,2,1,0:T(8,128)(2,1)S(1)}, bf16[1,1,8,128,128]{4,3,2,1,0:T(8,128)(2,1)}, u32[]{:S(2)}) %copy-start) | copy-done | bytes 262168
  8.1 0.0 copy-start.3
  8.1 0.8 %shard_map.94.near.matrix = bf16[512,512]{1,0:T(8,128)(2,1)S(1)} custom-call(bf16[1,1,8,128,128]{4,3,2,1,0:T(8,128)(2,1)S(1)} %copy-done, s32[1,1,8]{2,1,0:T(1,128)S(1)} %copy-done.4, s32[1,1,8]{2,1,0:T(1,128)S(1)} %copy-done.5, s32[1,1]{1,0:T(1,128)S(6)} %copy.10.count_in), custom_call_target="tpu_custom_call" | custom-call | bytes 1048576 | tf_op jit(solution)/shard_map/pallas_call | solution.py:238
  8.9 0.0 collective-permute-done.refs_1_
  8.9 0.0 collective-permute-done.1.refs_2_
  8.9 0.0 collective-permute-done.2.refs_3_
  9.0 0.0 copy-done.3
  9.0 0.3 shard_map.96
  9.3 1.5 %collective-permute-start.3 = (bf16[256,128]{1,0:T(8,128)(2,1)S(1)}, bf16[256,128]{1,0:T(8,128)(2,1)S(1)}, u32[]{:S(2)}, u32[]{:S(2)}) collective-permute-start(bf16[256,128]{1,0:T(8,128)(2,1)S(1)} %get-tuple-element.19), channel_id=1, source_target_pairs={{0,1},{1,3},{2,0},{3,2},{4,5},{5,7},{6,4},{7,6},{8,9},{9,11},{10,8... | collective-permute-start | bytes 196616 | tf_op jit(solution)/shard_map/ppermute | solution.py:42
  10.8 1.2 %collective-permute-start.4 = (bf16[256,128]{1,0:T(8,128)(2,1)S(1)}, bf16[256,128]{1,0:T(8,128)(2,1)S(1)}, u32[]{:S(2)}, u32[]{:S(2)}) collective-permute-start(bf16[256,128]{1,0:T(8,128)(2,1)S(1)} %get-tuple-element.20), channel_id=1, source_target_pairs={{0,3},{1,2},{2,1},{3,0},{4,7},{5,6},{6,5},{7,4},{8,11},{9,10},{10,... | collective-permute-start | bytes 196616 | tf_op jit(solution)/shard_map/ppermute | solution.py:42
  12.0 0.0 copy-start.1
  12.0 0.0 copy-start.2
  12.0 1.6 %collective-permute-start.5 = (bf16[256,128]{1,0:T(8,128)(2,1)S(1)}, bf16[256,128]{1,0:T(8,128)(2,1)S(1)}, u32[]{:S(2)}, u32[]{:S(2)}) collective-permute-start(bf16[256,128]{1,0:T(8,128)(2,1)S(1)} %get-tuple-element.21), channel_id=1, source_target_pairs={{0,2},{1,0},{2,3},{3,1},{4,6},{5,4},{6,7},{7,5},{8,10},{9,8},{10,1... | collective-permute-start | bytes 196616 | tf_op jit(solution)/shard_map/ppermute | solution.py:42
  13.5 0.3 %shard_map.95.refs_0_.matrix = bf16[512,512]{1,0:T(8,128)(2,1)S(1)} custom-call(bf16[512,512]{1,0:T(8,128)(2,1)S(1)} %shard_map.94.near.matrix), custom_call_target="tpu_custom_call" | custom-call | bytes 1572864 | tf_op jit(solution)/shard_map/pallas_call | solution.py:271
  13.9 0.0 collective-permute-done.6.refs_7_
  13.9 1.4 %collective-permute-done.3.refs_2_ = bf16[256,128]{1,0:T(8,128)(2,1)S(1)} collective-permute-done((bf16[256,128]{1,0:T(8,128)(2,1)S(1)}, bf16[256,128]{1,0:T(8,128)(2,1)S(1)}, u32[]{:S(2)}, u32[]{:S(2)}) %collective-permute-start.3) | collective-permute-done | bytes 65568 | tf_op jit(solution)/shard_map/ppermute | solution.py:42
  15.3 2.4 %collective-permute-done.4.refs_3_ = bf16[256,128]{1,0:T(8,128)(2,1)S(1)} collective-permute-done((bf16[256,128]{1,0:T(8,128)(2,1)S(1)}, bf16[256,128]{1,0:T(8,128)(2,1)S(1)}, u32[]{:S(2)}, u32[]{:S(2)}) %collective-permute-start.4) | collective-permute-done | bytes 65568 | tf_op jit(solution)/shard_map/ppermute | solution.py:42
  17.7 0.3 %collective-permute-done.5.refs_4_ = bf16[256,128]{1,0:T(8,128)(2,1)S(1)} collective-permute-done((bf16[256,128]{1,0:T(8,128)(2,1)S(1)}, bf16[256,128]{1,0:T(8,128)(2,1)S(1)}, u32[]{:S(2)}, u32[]{:S(2)}) %collective-permute-start.5) | collective-permute-done | bytes 65568 | tf_op jit(solution)/shard_map/ppermute | solution.py:42
  18.0 0.0 copy-done.1
  18.0 0.0 copy-done.2
  18.0 0.5 %shard_map.97 = (bf16[256,128]{1,0:T(8,128)(2,1)S(1)}, f32[128,128]{1,0:T(8,128)S(1)}, bf16[128,128]{1,0:T(8,128)(2,1)S(1)}, f32[128,256]{1,0:T(8,128)S(1)}) custom-call(bf16[512,512]{1,0:T(8,128)(2,1)S(1)} %shard_map.95.refs_0_.matrix, bf16[256,128]{1,0:T(8,128)(2,1)S(1)} %get-tuple-element.18.refs_1_, bf16[256,128]{1,0:T(8,128)(2,1)S(1)} %collective-permute-done.3.refs_2_, ...), custom_call_target="tpu_custom_call" | custom-call | flops 117440512 | tf_op jit(solution)/shard_map/pallas_call | solution.py:280
  18.5 0.1 collective-permute-start.7
  18.6 1.2 %collective-permute-done.7.came = bf16[128,128]{1,0:T(8,128)(2,1)S(1)} collective-permute-done((bf16[128,128]{1,0:T(8,128)(2,1)S(1)}, bf16[128,128]{1,0:T(8,128)(2,1)S(1)}, u32[]{:S(2)}, u32[]{:S(2)}) %collective-permute-start.7) | collective-permute-done | bytes 32800 | tf_op jit(solution)/shard_map/ppermute | solution.py:53
  19.8 2.0 %collective-permute-start.8 = (bf16[384,128]{1,0:T(8,128)(2,1)S(1)}, bf16[384,128]{1,0:T(8,128)(2,1)S(1)}, u32[]{:S(2)}, u32[]{:S(2)}) collective-permute-start(bf16[384,128]{1,0:T(8,128)(2,1)S(1)} %shard_map.99.refs_0_), channel_id=1, source_target_pairs={{0,1},{1,0},{2,3},{3,2},{4,5},{5,4},{6,7},{7,6},{8,9},{9,8},{10,11... | collective-permute-start | bytes 294920 | tf_op jit(solution)/shard_map/ppermute | solution.py:53
  21.8 3.1 %collective-permute-done.8.refs_1_ = bf16[384,128]{1,0:T(8,128)(2,1)S(1)} collective-permute-done((bf16[384,128]{1,0:T(8,128)(2,1)S(1)}, bf16[384,128]{1,0:T(8,128)(2,1)S(1)}, u32[]{:S(2)}, u32[]{:S(2)}) %collective-permute-start.8) | collective-permute-done | bytes 98336 | tf_op jit(solution)/shard_map/ppermute | solution.py:53
  24.9 0.3 shard_map.100
  25.2 0.7 %collective-permute-start.10 = (bf16[256,128]{1,0:T(8,128)(2,1)S(1)}, bf16[256,128]{1,0:T(8,128)(2,1)S(1)}, u32[]{:S(2)}, u32[]{:S(2)}) collective-permute-start(bf16[256,128]{1,0:T(8,128)(2,1)S(1)} %get-tuple-element.29), channel_id=1, source_target_pairs={{0,8},{4,12},{8,0},{12,4},{1,9},{5,13},{9,1},{13,5},{2,10},{6,14},... | collective-permute-start | bytes 196616 | tf_op jit(solution)/shard_map/ppermute | solution.py:42
  25.9 0.3 collective-permute-start.11
  26.3 0.2 collective-permute-start.9
  26.5 0.7 %shard_map.98 = bf16[128,256]{1,0:T(8,128)(2,1)} custom-call(f32[128,256]{1,0:T(8,128)S(1)} %get-tuple-element.22.pre), custom_call_target="tpu_custom_call" | custom-call | tf_op jit(solution)/shard_map/pallas_call | solution.py:299
  27.1 2.9 %collective-permute-done.10.refs_1_ = bf16[256,128]{1,0:T(8,128)(2,1)S(1)} collective-permute-done((bf16[256,128]{1,0:T(8,128)(2,1)S(1)}, bf16[256,128]{1,0:T(8,128)(2,1)S(1)}, u32[]{:S(2)}, u32[]{:S(2)}) %collective-permute-start.10) | collective-permute-done | bytes 65568 | tf_op jit(solution)/shard_map/ppermute | solution.py:42
  30.0 0.0 collective-permute-done.11.refs_2_
  30.0 0.6 %collective-permute-done.9.refs_0_ = bf16[256,128]{1,0:T(8,128)(2,1)S(1)} collective-permute-done((bf16[256,128]{1,0:T(8,128)(2,1)S(1)}, bf16[256,128]{1,0:T(8,128)(2,1)S(1)}, u32[]{:S(2)}, u32[]{:S(2)}) %collective-permute-start.9) | collective-permute-done | bytes 65568 | tf_op jit(solution)/shard_map/ppermute | solution.py:42
  30.6 0.7 %shard_map.101 = (bf16[128,128]{1,0:T(8,128)(2,1)}, f32[128,256]{1,0:T(8,128)}) custom-call(f32[128,128]{1,0:T(8,128)S(1)} %get-tuple-element.26.own, bf16[128,128]{1,0:T(8,128)(2,1)S(1)} %get-tuple-element.27.kept, bf16[256,128]{1,0:T(8,128)(2,1)S(1)} %collective-permute-done.9.refs_0_, bf16[256,128]{1,0:T(8,128)(2,1)S(1)} %collective-permute-done.10.refs_1_, ...), custom_call_target="tpu_custom_call" | custom-call | tf_op jit(solution)/shard_map/pallas_call | solution.py:311
  (1 shorter events, 0.0 us)
Async XLA Ops:
  0.6 6.5 %copy-start.4 = (s32[1,1,8]{2,1,0:T(1,128)S(1)}, s32[1,1,8]{2,1,0:T(1,128)}, u32[]{:S(2)}) copy-start(s32[1,1,8]{2,1,0:T(1,128)} %rows_in.1) | copy-start | bytes 100
  0.6 6.5 %copy-start.5 = (s32[1,1,8]{2,1,0:T(1,128)S(1)}, s32[1,1,8]{2,1,0:T(1,128)}, u32[]{:S(2)}) copy-start(s32[1,1,8]{2,1,0:T(1,128)} %cols_in.1) | copy-start | bytes 100
  0.7 8.3 %collective-permute-start = (bf16[128,128]{1,0:T(8,128)(2,1)}, bf16[128,128]{1,0:T(8,128)(2,1)S(1)}, u32[]{:S(2)}, u32[]{:S(2)}) collective-permute-start(bf16[128,128]{1,0:T(8,128)(2,1)} %refs_0_.1), channel_id=1, source_target_pairs={{0,12},{4,0},{8,4},{12,8},{1,13},{5,1},{9,5},{13,9},{2,14},{6,2},{... | collective-permute-start | bytes 98312 | tf_op jit(solution)/shard_map/ppermute | solution.py:42
  3.1 5.9 %collective-permute-start.1 = (bf16[128,128]{1,0:T(8,128)(2,1)}, bf16[128,128]{1,0:T(8,128)(2,1)S(1)}, u32[]{:S(2)}, u32[]{:S(2)}) collective-permute-start(bf16[128,128]{1,0:T(8,128)(2,1)} %refs_0_.1), channel_id=1, source_target_pairs={{0,8},{4,12},{8,0},{12,4},{1,9},{5,13},{9,1},{13,5},{2,10},{6,14},... | collective-permute-start | bytes 98312 | tf_op jit(solution)/shard_map/ppermute | solution.py:42
  3.7 5.2 %collective-permute-start.2 = (bf16[128,128]{1,0:T(8,128)(2,1)}, bf16[128,128]{1,0:T(8,128)(2,1)S(1)}, u32[]{:S(2)}, u32[]{:S(2)}) collective-permute-start(bf16[128,128]{1,0:T(8,128)(2,1)} %refs_0_.1), channel_id=1, source_target_pairs={{0,4},{4,8},{8,12},{12,0},{1,5},{5,9},{9,13},{13,1},{2,6},{6,10},{... | collective-permute-start | bytes 98312 | tf_op jit(solution)/shard_map/ppermute | solution.py:42
  3.9 10.0 %collective-permute-start.6 = (bf16[128,256]{1,0:T(8,128)(2,1)}, bf16[128,256]{1,0:T(8,128)(2,1)S(1)}, u32[]{:S(2)}, u32[]{:S(2)}) collective-permute-start(bf16[128,256]{1,0:T(8,128)(2,1)} %refs_6_.1), channel_id=1, source_target_pairs={{0,2},{1,3},{2,0},{3,1},{4,6},{5,7},{6,4},{7,5},{8,10},{9,11},{10,... | collective-permute-start | bytes 196616 | tf_op jit(solution)/shard_map/ppermute | solution.py:53
  7.1 1.0 %copy-start = (bf16[1,1,8,128,128]{4,3,2,1,0:T(8,128)(2,1)S(1)}, bf16[1,1,8,128,128]{4,3,2,1,0:T(8,128)(2,1)}, u32[]{:S(2)}) copy-start(bf16[1,1,8,128,128]{4,3,2,1,0:T(8,128)(2,1)} %vals.1) | copy-start | bytes 786436
  8.1 0.9 %copy-start.3 = (bf16[128,128]{1,0:T(8,128)(2,1)S(1)}, bf16[128,128]{1,0:T(8,128)(2,1)}, u32[]{:S(2)}) copy-start(bf16[128,128]{1,0:T(8,128)(2,1)} %refs_0_.1) | copy-start | bytes 98308
  9.3 6.0 %collective-permute-start.3 = (bf16[256,128]{1,0:T(8,128)(2,1)S(1)}, bf16[256,128]{1,0:T(8,128)(2,1)S(1)}, u32[]{:S(2)}, u32[]{:S(2)}) collective-permute-start(bf16[256,128]{1,0:T(8,128)(2,1)S(1)} %get-tuple-element.19), channel_id=1, source_target_pairs={{0,1},{1,3},{2,0},{3,2},{4,5},{5,7},{6,4},{7,6},{8,9},{9,11},{10,8... | collective-permute-start | bytes 196616 | tf_op jit(solution)/shard_map/ppermute | solution.py:42
  10.8 6.9 %collective-permute-start.4 = (bf16[256,128]{1,0:T(8,128)(2,1)S(1)}, bf16[256,128]{1,0:T(8,128)(2,1)S(1)}, u32[]{:S(2)}, u32[]{:S(2)}) collective-permute-start(bf16[256,128]{1,0:T(8,128)(2,1)S(1)} %get-tuple-element.20), channel_id=1, source_target_pairs={{0,3},{1,2},{2,1},{3,0},{4,7},{5,6},{6,5},{7,4},{8,11},{9,10},{10,... | collective-permute-start | bytes 196616 | tf_op jit(solution)/shard_map/ppermute | solution.py:42
  12.0 6.0 %copy-start.1 = (bf16[128,256]{1,0:T(8,128)(2,1)S(1)}, bf16[128,256]{1,0:T(8,128)(2,1)}, u32[]{:S(2)}) copy-start(bf16[128,256]{1,0:T(8,128)(2,1)} %refs_5_.1) | copy-start | bytes 196612
  12.0 6.0 %copy-start.2 = (bf16[128,256]{1,0:T(8,128)(2,1)S(1)}, bf16[128,256]{1,0:T(8,128)(2,1)}, u32[]{:S(2)}) copy-start(bf16[128,256]{1,0:T(8,128)(2,1)} %refs_6_.1) | copy-start | bytes 196612
  12.0 6.0 %collective-permute-start.5 = (bf16[256,128]{1,0:T(8,128)(2,1)S(1)}, bf16[256,128]{1,0:T(8,128)(2,1)S(1)}, u32[]{:S(2)}, u32[]{:S(2)}) collective-permute-start(bf16[256,128]{1,0:T(8,128)(2,1)S(1)} %get-tuple-element.21), channel_id=1, source_target_pairs={{0,2},{1,0},{2,3},{3,1},{4,6},{5,4},{6,7},{7,5},{8,10},{9,8},{10,1... | collective-permute-start | bytes 196616 | tf_op jit(solution)/shard_map/ppermute | solution.py:42
  18.5 1.3 %collective-permute-start.7 = (bf16[128,128]{1,0:T(8,128)(2,1)S(1)}, bf16[128,128]{1,0:T(8,128)(2,1)S(1)}, u32[]{:S(2)}, u32[]{:S(2)}) collective-permute-start(bf16[128,128]{1,0:T(8,128)(2,1)S(1)} %get-tuple-element.25), channel_id=1, source_target_pairs={{0,4},{4,0},{8,12},{12,8},{1,5},{5,1},{9,13},{13,9},{2,6},{6,2},{1... | collective-permute-start | bytes 98312 | tf_op jit(solution)/shard_map/ppermute | solution.py:53
  19.8 5.2 %collective-permute-start.8 = (bf16[384,128]{1,0:T(8,128)(2,1)S(1)}, bf16[384,128]{1,0:T(8,128)(2,1)S(1)}, u32[]{:S(2)}, u32[]{:S(2)}) collective-permute-start(bf16[384,128]{1,0:T(8,128)(2,1)S(1)} %shard_map.99.refs_0_), channel_id=1, source_target_pairs={{0,1},{1,0},{2,3},{3,2},{4,5},{5,4},{6,7},{7,6},{8,9},{9,8},{10,11... | collective-permute-start | bytes 294920 | tf_op jit(solution)/shard_map/ppermute | solution.py:53
  25.2 4.7 %collective-permute-start.10 = (bf16[256,128]{1,0:T(8,128)(2,1)S(1)}, bf16[256,128]{1,0:T(8,128)(2,1)S(1)}, u32[]{:S(2)}, u32[]{:S(2)}) collective-permute-start(bf16[256,128]{1,0:T(8,128)(2,1)S(1)} %get-tuple-element.29), channel_id=1, source_target_pairs={{0,8},{4,12},{8,0},{12,4},{1,9},{5,13},{9,1},{13,5},{2,10},{6,14},... | collective-permute-start | bytes 196616 | tf_op jit(solution)/shard_map/ppermute | solution.py:42
  25.9 4.0 %collective-permute-start.11 = (bf16[256,128]{1,0:T(8,128)(2,1)S(1)}, bf16[256,128]{1,0:T(8,128)(2,1)S(1)}, u32[]{:S(2)}, u32[]{:S(2)}) collective-permute-start(bf16[256,128]{1,0:T(8,128)(2,1)S(1)} %get-tuple-element.30), channel_id=1, source_target_pairs={{0,12},{4,0},{8,4},{12,8},{1,13},{5,1},{9,5},{13,9},{2,14},{6,2},{... | collective-permute-start | bytes 196616 | tf_op jit(solution)/shard_map/ppermute | solution.py:42
  26.3 4.3 %collective-permute-start.9 = (bf16[256,128]{1,0:T(8,128)(2,1)S(1)}, bf16[256,128]{1,0:T(8,128)(2,1)S(1)}, u32[]{:S(2)}, u32[]{:S(2)}) collective-permute-start(bf16[256,128]{1,0:T(8,128)(2,1)S(1)} %get-tuple-element.28), channel_id=1, source_target_pairs={{0,4},{4,8},{8,12},{12,0},{1,5},{5,9},{9,13},{13,1},{2,6},{6,10},{... | collective-permute-start | bytes 196616 | tf_op jit(solution)/shard_map/ppermute | solution.py:42

commit v14 on v13

--- a/solution.py
+++ b/solution.py
@@ -85,7 +85,9 @@
     def add(t, _):
         row, col = rows[0, 0, t], cols[0, 0, t]
         if paired:
-            place = lax.rem((row // piece) ^ lax.axis_index("col"), 2) * 2 + row // piece // 2
+            there, here = row // piece, lax.axis_index("col")
+            apart = lax.rem(ring_place(there, "col") ^ ring_place(here, "col"), 2)
+            place = apart * 2 + there // 2
         else:
             place = ahead(row // piece, "col")
         row = place * piece + lax.rem(row, piece)
@@ -153,31 +155,19 @@
     halve(term, mine, other)
 
 
-def in_middle():
-    my_col = lax.axis_index("col")
-    return (my_col == 1) | (my_col == 2)
-
-
 def paired_forward_kernel(n, matrix, *refs):
-    operands, (own, first, second, third) = refs[:n], refs[n:]
+    operands, (same, other) = refs[:n], refs[n:]
     stacked = jnp.concatenate([operand[...] for operand in operands], axis=0)
-    product = dot(matrix[...], stacked).astype(own.dtype)
-    rows = own.shape[0]
-    same, other = product[:rows], product[rows:]
-    middle = in_middle()
-    own[...] = same
-    first[...] = jnp.where(middle, same, other)
-    second[...] = other
-    third[...] = jnp.where(middle, other, same)
+    product = dot(matrix[...], stacked).astype(same.dtype)
+    rows = same.shape[0]
+    same[...] = product[:rows]
+    other[...] = product[rows:]
 
 
 def paired_layer_kernel(own, first, second, third, weight, cotangent, beyond, *refs):
     back_out, mine, other, pre_out = refs
     nodes = cotangent.shape[0]
-    middle = in_middle()
-    partner = jnp.where(middle, third[...], first[...])
-    side = jnp.where(middle, first[...], third[...])
-    total = (wide(own[...]) + wide(partner)) + (wide(second[...]) + wide(side))
+    total = (wide(own[...]) + wide(second[...])) + (wide(first[...]) + wide(third[...]))
     high_col = lax.axis_index("col") >= 2
     here, there = cotangent[...], beyond[...]
     both = jnp.concatenate(
@@ -251,13 +241,14 @@
     forward = dict(flops=2 * down * across * width, need=2 * dense_bytes)
     if paired:
         layers = 2
-        own, *sends = call(
+        own, other = call(
             functools.partial(paired_forward_kernel, n_row),
-            [((2 * nodes, width), NARROW)] * 4,
+            [((2 * nodes, width), NARROW)] * 2,
             [VMEM] * (1 + n_row),
             **forward,
         )(near, features, *gathered)
-        layer_call, cotangents = paired_layer_kernel, [cotangent, swap(cotangent, "col", 2)]
+        sends = [other, own, other]
+        layer_call, cotangents = paired_layer_kernel, [cotangent, swap(cotangent, "col", 3)]
     else:
         layers = 1
         own, *sends = call(

time: 31.4 us -> 32.9 us (1.048)
  waiting for transfers between devices: 11.8 us -> 14.2 us
  starting transfers between devices: 13.4 us -> 12.4 us
    ppermute x3, waiting for transfers between devices: 4.32 us -> 6 us  [swap(): return lax.ppermute(value, axis, [(s, s ^ distance) for s in range(n)])]
    ppermute x3, starting transfers between devices: 4.7 us -> 3.79 us  [swap(): return lax.ppermute(value, axis, [(s, s ^ distance) for s in range(n)])]
    ppermute x9, waiting for transfers between devices: 7.52 us -> 8.2 us  [exchange(): lax.ppermute(send, axis, [(s, target(s, d)) for s in range(n)])]
  transfers between devices with their start and end apart: 12 -> 12, of which waited for: 7 -> 6; matrix products, arithmetic and copies ran while one was open for 0% -> 0% of each run, Pallas kernels for 7% -> 6%
where the time goes in v14:
time: 32.9 us; the launch traced here: 32.5 us
  waiting for transfers between devices  14.2 us (43%)
  starting transfers between devices  12.4 us (38%)
  Pallas kernels  3.46 us (11%)
  between operations  1.42 us (4%)
  local copies, waits for them, and re-layouts  1.02 us (3%)
    ppermute x9, starting transfers between devices, exchange(): lax.ppermute(send, axis, [(s, target(s, d)) for s in range(n)])  8.64 us
    ppermute x9, waiting for transfers between devices, exchange(): lax.ppermute(send, axis, [(s, target(s, d)) for s in range(n)])  8.2 us
    ppermute x3, waiting for transfers between devices, swap(): return lax.ppermute(value, axis, [(s, s ^ distance) for s in range(n)])  6 us
    ppermute x3, starting transfers between devices, swap(): return lax.ppermute(value, axis, [(s, s ^ distance) for s in range(n)])  3.79 us
    unnamed x12, local copies, waits for them, and re-layouts  1.02 us
    pallas_call x1, Pallas kernels, per_device(): call(functools.partial(last_kernel, scale), [((nodes, width), NARROW), ((...  0.7 us
    pallas_call x1, Pallas kernels, per_device(): call(functools.partial(dense_kernel, nodes // side, paired), [((down, acr...  0.66 us
  transfers between devices with their start and end apart: 12, of which 6 were waited for; matrix products, arithmetic and copies ran while one was open for 0% of the time, Pallas kernels for 6%

profile of v14, /device:TPU:0, one launch (start us, length us, event | category | flops | bytes accessed | tf_op | source)
XLA Modules:
  0.0 32.5 jit_solution(2778284856611890476)
XLA Ops:
  0.6 0.0 copy-start.5
  0.6 0.0 copy-start.4
  0.7 3.0 %collective-permute-start.1 = (bf16[128,128]{1,0:T(8,128)(2,1)}, bf16[128,128]{1,0:T(8,128)(2,1)S(1)}, u32[]{:S(2)}, u32[]{:S(2)}) collective-permute-start(bf16[128,128]{1,0:T(8,128)(2,1)} %refs_0_.1), channel_id=1, source_target_pairs={{0,8},{4,12},{8,0},{12,4},{1,9},{5,13},{9,1},{13,5},{2,10},{6,14},... | collective-permute-start | bytes 98312 | tf_op jit(solution)/shard_map/ppermute | solution.py:42
  3.7 0.0 collective-permute-start
  3.7 0.5 %collective-permute-start.2 = (bf16[128,128]{1,0:T(8,128)(2,1)}, bf16[128,128]{1,0:T(8,128)(2,1)S(1)}, u32[]{:S(2)}, u32[]{:S(2)}) collective-permute-start(bf16[128,128]{1,0:T(8,128)(2,1)} %refs_0_.1), channel_id=1, source_target_pairs={{0,4},{4,8},{8,12},{12,0},{1,5},{5,9},{9,13},{13,1},{2,6},{6,10},{... | collective-permute-start | bytes 98312 | tf_op jit(solution)/shard_map/ppermute | solution.py:42
  4.2 3.6 %collective-permute-start.6 = (bf16[128,256]{1,0:T(8,128)(2,1)}, bf16[128,256]{1,0:T(8,128)(2,1)S(1)}, u32[]{:S(2)}, u32[]{:S(2)}) collective-permute-start(bf16[128,256]{1,0:T(8,128)(2,1)} %refs_6_.1), channel_id=1, source_target_pairs={{0,3},{1,2},{2,1},{3,0},{4,7},{5,6},{6,5},{7,4},{8,11},{9,10},{10,... | collective-permute-start | bytes 196616 | tf_op jit(solution)/shard_map/ppermute | solution.py:53
  8.4 0.0 copy-done.5
  8.4 0.0 copy-done.4
  8.4 0.0 copy-start
  8.4 0.9 %copy-done = bf16[1,1,8,128,128]{4,3,2,1,0:T(8,128)(2,1)S(1)} copy-done((bf16[1,1,8,128,128]{4,3,2,1,0:T(8,128)(2,1)S(1)}, bf16[1,1,8,128,128]{4,3,2,1,0:T(8,128)(2,1)}, u32[]{:S(2)}) %copy-start) | copy-done | bytes 262168
  9.4 0.0 copy-start.3
  9.4 0.7 %shard_map.94.near.matrix = bf16[512,512]{1,0:T(8,128)(2,1)S(1)} custom-call(bf16[1,1,8,128,128]{4,3,2,1,0:T(8,128)(2,1)S(1)} %copy-done, s32[1,1,8]{2,1,0:T(1,128)S(1)} %copy-done.4, s32[1,1,8]{2,1,0:T(1,128)S(1)} %copy-done.5, s32[1,1]{1,0:T(1,128)S(6)} %copy.10.count_in), custom_call_target="tpu_custom_call" | custom-call | bytes 1048576 | tf_op jit(solution)/shard_map/pallas_call | solution.py:228
  10.1 0.0 collective-permute-done.1.refs_2_
  10.1 0.0 collective-permute-done.refs_1_
  10.1 0.0 collective-permute-done.2.refs_3_
  10.1 0.1 copy-done.3
  10.1 0.3 shard_map.96
  10.4 0.8 %collective-permute-start.4 = (bf16[256,128]{1,0:T(8,128)(2,1)S(1)}, bf16[256,128]{1,0:T(8,128)(2,1)S(1)}, u32[]{:S(2)}, u32[]{:S(2)}) collective-permute-start(bf16[256,128]{1,0:T(8,128)(2,1)S(1)} %get-tuple-element.16.refs_1_), channel_id=1, source_target_pairs={{0,3},{1,2},{2,1},{3,0},{4,7},{5,6},{6,5},{7,4},{8,11},{9,10},{10,... | collective-permute-start | bytes 196616 | tf_op jit(solution)/shard_map/ppermute | solution.py:42
  11.3 0.0 copy-start.1
  11.3 0.0 copy-start.2
  11.3 0.3 collective-permute-start.5
  11.5 1.8 %collective-permute-start.3 = (bf16[256,128]{1,0:T(8,128)(2,1)S(1)}, bf16[256,128]{1,0:T(8,128)(2,1)S(1)}, u32[]{:S(2)}, u32[]{:S(2)}) collective-permute-start(bf16[256,128]{1,0:T(8,128)(2,1)S(1)} %get-tuple-element.17), channel_id=1, source_target_pairs={{0,1},{1,3},{2,0},{3,2},{4,5},{5,7},{6,4},{7,6},{8,9},{9,11},{10,8... | collective-permute-start | bytes 196616 | tf_op jit(solution)/shard_map/ppermute | solution.py:42
  13.3 0.3 %shard_map.95.refs_0_.matrix = bf16[512,512]{1,0:T(8,128)(2,1)S(1)} custom-call(bf16[512,512]{1,0:T(8,128)(2,1)S(1)} %shard_map.94.near.matrix), custom_call_target="tpu_custom_call" | custom-call | bytes 1572864 | tf_op jit(solution)/shard_map/pallas_call | solution.py:262
  13.6 0.0 collective-permute-done.6.refs_7_
  13.7 3.7 %collective-permute-done.4.refs_3_ = bf16[256,128]{1,0:T(8,128)(2,1)S(1)} collective-permute-done((bf16[256,128]{1,0:T(8,128)(2,1)S(1)}, bf16[256,128]{1,0:T(8,128)(2,1)S(1)}, u32[]{:S(2)}, u32[]{:S(2)}) %collective-permute-start.4) | collective-permute-done | bytes 65568 | tf_op jit(solution)/shard_map/ppermute | solution.py:42
  17.4 0.0 collective-permute-done.5.refs_4_
  17.4 2.4 %collective-permute-done.3.refs_2_ = bf16[256,128]{1,0:T(8,128)(2,1)S(1)} collective-permute-done((bf16[256,128]{1,0:T(8,128)(2,1)S(1)}, bf16[256,128]{1,0:T(8,128)(2,1)S(1)}, u32[]{:S(2)}, u32[]{:S(2)}) %collective-permute-start.3) | collective-permute-done | bytes 65568 | tf_op jit(solution)/shard_map/ppermute | solution.py:42
  19.7 0.0 copy-done.1
  19.7 0.0 copy-done.2
  19.8 0.5 %shard_map.97 = (bf16[256,128]{1,0:T(8,128)(2,1)S(1)}, f32[128,128]{1,0:T(8,128)S(1)}, bf16[128,128]{1,0:T(8,128)(2,1)S(1)}, f32[128,256]{1,0:T(8,128)S(1)}) custom-call(bf16[512,512]{1,0:T(8,128)(2,1)S(1)} %shard_map.95.refs_0_.matrix, bf16[256,128]{1,0:T(8,128)(2,1)S(1)} %get-tuple-element.16.refs_1_, bf16[256,128]{1,0:T(8,128)(2,1)S(1)} %collective-permute-done.3.refs_2_, ...), custom_call_target="tpu_custom_call" | custom-call | flops 117440512 | tf_op jit(solution)/shard_map/pallas_call | solution.py:271
  20.3 0.1 collective-permute-start.7
  20.4 1.2 %collective-permute-done.7.came = bf16[128,128]{1,0:T(8,128)(2,1)S(1)} collective-permute-done((bf16[128,128]{1,0:T(8,128)(2,1)S(1)}, bf16[128,128]{1,0:T(8,128)(2,1)S(1)}, u32[]{:S(2)}, u32[]{:S(2)}) %collective-permute-start.7) | collective-permute-done | bytes 32800 | tf_op jit(solution)/shard_map/ppermute | solution.py:53
  21.5 0.1 collective-permute-start.8
  21.6 4.8 %collective-permute-done.8.refs_1_ = bf16[384,128]{1,0:T(8,128)(2,1)S(1)} collective-permute-done((bf16[384,128]{1,0:T(8,128)(2,1)S(1)}, bf16[384,128]{1,0:T(8,128)(2,1)S(1)}, u32[]{:S(2)}, u32[]{:S(2)}) %collective-permute-start.8) | collective-permute-done | bytes 98336 | tf_op jit(solution)/shard_map/ppermute | solution.py:53
  26.5 0.3 shard_map.100
  26.8 0.1 collective-permute-start.9
  26.8 0.8 %collective-permute-start.10 = (bf16[256,128]{1,0:T(8,128)(2,1)S(1)}, bf16[256,128]{1,0:T(8,128)(2,1)S(1)}, u32[]{:S(2)}, u32[]{:S(2)}) collective-permute-start(bf16[256,128]{1,0:T(8,128)(2,1)S(1)} %get-tuple-element.25), channel_id=1, source_target_pairs={{0,8},{4,12},{8,0},{12,4},{1,9},{5,13},{9,1},{13,5},{2,10},{6,14},... | collective-permute-start | bytes 196616 | tf_op jit(solution)/shard_map/ppermute | solution.py:42
  27.7 1.4 %collective-permute-start.11 = (bf16[256,128]{1,0:T(8,128)(2,1)S(1)}, bf16[256,128]{1,0:T(8,128)(2,1)S(1)}, u32[]{:S(2)}, u32[]{:S(2)}) collective-permute-start(bf16[256,128]{1,0:T(8,128)(2,1)S(1)} %get-tuple-element.26), channel_id=1, source_target_pairs={{0,12},{4,0},{8,4},{12,8},{1,13},{5,1},{9,5},{13,9},{2,14},{6,2},{... | collective-permute-start | bytes 196616 | tf_op jit(solution)/shard_map/ppermute | solution.py:42
  29.1 0.7 %shard_map.98 = bf16[128,256]{1,0:T(8,128)(2,1)} custom-call(f32[128,256]{1,0:T(8,128)S(1)} %get-tuple-element.18.pre), custom_call_target="tpu_custom_call" | custom-call | tf_op jit(solution)/shard_map/pallas_call | solution.py:290
  29.7 0.9 %collective-permute-done.9.refs_0_ = bf16[256,128]{1,0:T(8,128)(2,1)S(1)} collective-permute-done((bf16[256,128]{1,0:T(8,128)(2,1)S(1)}, bf16[256,128]{1,0:T(8,128)(2,1)S(1)}, u32[]{:S(2)}, u32[]{:S(2)}) %collective-permute-start.9) | collective-permute-done | bytes 65568 | tf_op jit(solution)/shard_map/ppermute | solution.py:42
  30.6 1.2 %collective-permute-done.10.refs_1_ = bf16[256,128]{1,0:T(8,128)(2,1)S(1)} collective-permute-done((bf16[256,128]{1,0:T(8,128)(2,1)S(1)}, bf16[256,128]{1,0:T(8,128)(2,1)S(1)}, u32[]{:S(2)}, u32[]{:S(2)}) %collective-permute-start.10) | collective-permute-done | bytes 65568 | tf_op jit(solution)/shard_map/ppermute | solution.py:42
  31.8 0.0 collective-permute-done.11.refs_2_
  31.8 0.7 %shard_map.101 = (bf16[128,128]{1,0:T(8,128)(2,1)}, f32[128,256]{1,0:T(8,128)}) custom-call(f32[128,128]{1,0:T(8,128)S(1)} %get-tuple-element.22.own, bf16[128,128]{1,0:T(8,128)(2,1)S(1)} %get-tuple-element.23.kept, bf16[256,128]{1,0:T(8,128)(2,1)S(1)} %collective-permute-done.9.refs_0_, bf16[256,128]{1,0:T(8,128)(2,1)S(1)} %collective-permute-done.10.refs_1_, ...), custom_call_target="tpu_custom_call" | custom-call | tf_op jit(solution)/shard_map/pallas_call | solution.py:302
  (1 shorter events, 0.0 us)
Async XLA Ops:
  0.6 7.8 %copy-start.5 = (s32[1,1,8]{2,1,0:T(1,128)S(1)}, s32[1,1,8]{2,1,0:T(1,128)}, u32[]{:S(2)}) copy-start(s32[1,1,8]{2,1,0:T(1,128)} %cols_in.1) | copy-start | bytes 100
  0.6 7.8 %copy-start.4 = (s32[1,1,8]{2,1,0:T(1,128)S(1)}, s32[1,1,8]{2,1,0:T(1,128)}, u32[]{:S(2)}) copy-start(s32[1,1,8]{2,1,0:T(1,128)} %rows_in.1) | copy-start | bytes 100
  0.7 9.4 %collective-permute-start.1 = (bf16[128,128]{1,0:T(8,128)(2,1)}, bf16[128,128]{1,0:T(8,128)(2,1)S(1)}, u32[]{:S(2)}, u32[]{:S(2)}) collective-permute-start(bf16[128,128]{1,0:T(8,128)(2,1)} %refs_0_.1), channel_id=1, source_target_pairs={{0,8},{4,12},{8,0},{12,4},{1,9},{5,13},{9,1},{13,5},{2,10},{6,14},... | collective-permute-start | bytes 98312 | tf_op jit(solution)/shard_map/ppermute | solution.py:42
  3.7 6.4 %collective-permute-start = (bf16[128,128]{1,0:T(8,128)(2,1)}, bf16[128,128]{1,0:T(8,128)(2,1)S(1)}, u32[]{:S(2)}, u32[]{:S(2)}) collective-permute-start(bf16[128,128]{1,0:T(8,128)(2,1)} %refs_0_.1), channel_id=1, source_target_pairs={{0,12},{4,0},{8,4},{12,8},{1,13},{5,1},{9,5},{13,9},{2,14},{6,2},{... | collective-permute-start | bytes 98312 | tf_op jit(solution)/shard_map/ppermute | solution.py:42
  3.7 6.4 %collective-permute-start.2 = (bf16[128,128]{1,0:T(8,128)(2,1)}, bf16[128,128]{1,0:T(8,128)(2,1)S(1)}, u32[]{:S(2)}, u32[]{:S(2)}) collective-permute-start(bf16[128,128]{1,0:T(8,128)(2,1)} %refs_0_.1), channel_id=1, source_target_pairs={{0,4},{4,8},{8,12},{12,0},{1,5},{5,9},{9,13},{13,1},{2,6},{6,10},{... | collective-permute-start | bytes 98312 | tf_op jit(solution)/shard_map/ppermute | solution.py:42
  4.2 9.5 %collective-permute-start.6 = (bf16[128,256]{1,0:T(8,128)(2,1)}, bf16[128,256]{1,0:T(8,128)(2,1)S(1)}, u32[]{:S(2)}, u32[]{:S(2)}) collective-permute-start(bf16[128,256]{1,0:T(8,128)(2,1)} %refs_6_.1), channel_id=1, source_target_pairs={{0,3},{1,2},{2,1},{3,0},{4,7},{5,6},{6,5},{7,4},{8,11},{9,10},{10,... | collective-permute-start | bytes 196616 | tf_op jit(solution)/shard_map/ppermute | solution.py:53
  8.4 1.0 %copy-start = (bf16[1,1,8,128,128]{4,3,2,1,0:T(8,128)(2,1)S(1)}, bf16[1,1,8,128,128]{4,3,2,1,0:T(8,128)(2,1)}, u32[]{:S(2)}) copy-start(bf16[1,1,8,128,128]{4,3,2,1,0:T(8,128)(2,1)} %vals.1) | copy-start | bytes 786436
  9.4 0.8 %copy-start.3 = (bf16[128,128]{1,0:T(8,128)(2,1)S(1)}, bf16[128,128]{1,0:T(8,128)(2,1)}, u32[]{:S(2)}) copy-start(bf16[128,128]{1,0:T(8,128)(2,1)} %refs_0_.1) | copy-start | bytes 98308
  10.4 6.9 %collective-permute-start.4 = (bf16[256,128]{1,0:T(8,128)(2,1)S(1)}, bf16[256,128]{1,0:T(8,128)(2,1)S(1)}, u32[]{:S(2)}, u32[]{:S(2)}) collective-permute-start(bf16[256,128]{1,0:T(8,128)(2,1)S(1)} %get-tuple-element.16.refs_1_), channel_id=1, source_target_pairs={{0,3},{1,2},{2,1},{3,0},{4,7},{5,6},{6,5},{7,4},{8,11},{9,10},{10,... | collective-permute-start | bytes 196616 | tf_op jit(solution)/shard_map/ppermute | solution.py:42
  11.3 8.5 %copy-start.1 = (bf16[128,256]{1,0:T(8,128)(2,1)S(1)}, bf16[128,256]{1,0:T(8,128)(2,1)}, u32[]{:S(2)}) copy-start(bf16[128,256]{1,0:T(8,128)(2,1)} %refs_5_.1) | copy-start | bytes 196612
  11.3 8.5 %copy-start.2 = (bf16[128,256]{1,0:T(8,128)(2,1)S(1)}, bf16[128,256]{1,0:T(8,128)(2,1)}, u32[]{:S(2)}) copy-start(bf16[128,256]{1,0:T(8,128)(2,1)} %refs_6_.1) | copy-start | bytes 196612
  11.3 6.1 %collective-permute-start.5 = (bf16[256,128]{1,0:T(8,128)(2,1)S(1)}, bf16[256,128]{1,0:T(8,128)(2,1)S(1)}, u32[]{:S(2)}, u32[]{:S(2)}) collective-permute-start(bf16[256,128]{1,0:T(8,128)(2,1)S(1)} %get-tuple-element.17), channel_id=1, source_target_pairs={{0,2},{1,0},{2,3},{3,1},{4,6},{5,4},{6,7},{7,5},{8,10},{9,8},{10,1... | collective-permute-start | bytes 196616 | tf_op jit(solution)/shard_map/ppermute | solution.py:42
  11.5 8.2 %collective-permute-start.3 = (bf16[256,128]{1,0:T(8,128)(2,1)S(1)}, bf16[256,128]{1,0:T(8,128)(2,1)S(1)}, u32[]{:S(2)}, u32[]{:S(2)}) collective-permute-start(bf16[256,128]{1,0:T(8,128)(2,1)S(1)} %get-tuple-element.17), channel_id=1, source_target_pairs={{0,1},{1,3},{2,0},{3,2},{4,5},{5,7},{6,4},{7,6},{8,9},{9,11},{10,8... | collective-permute-start | bytes 196616 | tf_op jit(solution)/shard_map/ppermute | solution.py:42
  20.3 1.3 %collective-permute-start.7 = (bf16[128,128]{1,0:T(8,128)(2,1)S(1)}, bf16[128,128]{1,0:T(8,128)(2,1)S(1)}, u32[]{:S(2)}, u32[]{:S(2)}) collective-permute-start(bf16[128,128]{1,0:T(8,128)(2,1)S(1)} %get-tuple-element.21), channel_id=1, source_target_pairs={{0,4},{4,0},{8,12},{12,8},{1,5},{5,1},{9,13},{13,9},{2,6},{6,2},{1... | collective-permute-start | bytes 98312 | tf_op jit(solution)/shard_map/ppermute | solution.py:53
  21.5 4.9 %collective-permute-start.8 = (bf16[384,128]{1,0:T(8,128)(2,1)S(1)}, bf16[384,128]{1,0:T(8,128)(2,1)S(1)}, u32[]{:S(2)}, u32[]{:S(2)}) collective-permute-start(bf16[384,128]{1,0:T(8,128)(2,1)S(1)} %shard_map.99.refs_0_), channel_id=1, source_target_pairs={{0,1},{1,0},{2,3},{3,2},{4,5},{5,4},{6,7},{7,6},{8,9},{9,8},{10,11... | collective-permute-start | bytes 294920 | tf_op jit(solution)/shard_map/ppermute | solution.py:53
  26.8 3.8 %collective-permute-start.9 = (bf16[256,128]{1,0:T(8,128)(2,1)S(1)}, bf16[256,128]{1,0:T(8,128)(2,1)S(1)}, u32[]{:S(2)}, u32[]{:S(2)}) collective-permute-start(bf16[256,128]{1,0:T(8,128)(2,1)S(1)} %get-tuple-element.24), channel_id=1, source_target_pairs={{0,4},{4,8},{8,12},{12,0},{1,5},{5,9},{9,13},{13,1},{2,6},{6,10},{... | collective-permute-start | bytes 196616 | tf_op jit(solution)/shard_map/ppermute | solution.py:42
  26.8 5.0 %collective-permute-start.10 = (bf16[256,128]{1,0:T(8,128)(2,1)S(1)}, bf16[256,128]{1,0:T(8,128)(2,1)S(1)}, u32[]{:S(2)}, u32[]{:S(2)}) collective-permute-start(bf16[256,128]{1,0:T(8,128)(2,1)S(1)} %get-tuple-element.25), channel_id=1, source_target_pairs={{0,8},{4,12},{8,0},{12,4},{1,9},{5,13},{9,1},{13,5},{2,10},{6,14},... | collective-permute-start | bytes 196616 | tf_op jit(solution)/shard_map/ppermute | solution.py:42
  27.7 4.1 %collective-permute-start.11 = (bf16[256,128]{1,0:T(8,128)(2,1)S(1)}, bf16[256,128]{1,0:T(8,128)(2,1)S(1)}, u32[]{:S(2)}, u32[]{:S(2)}) collective-permute-start(bf16[256,128]{1,0:T(8,128)(2,1)S(1)} %get-tuple-element.26), channel_id=1, source_target_pairs={{0,12},{4,0},{8,4},{12,8},{1,13},{5,1},{9,5},{13,9},{2,14},{6,2},{... | collective-permute-start | bytes 196616 | tf_op jit(solution)/shard_map/ppermute | solution.py:42

commit v15 on v13

--- a/solution.py
+++ b/solution.py
@@ -159,7 +159,8 @@
 
 
 def paired_forward_kernel(n, matrix, *refs):
-    operands, (own, first, second, third) = refs[:n], refs[n:]
+    operands, cotangent, (own, first, second, third, passed) = refs[:n], refs[n], refs[n + 1 :]
+    passed[...] = cotangent[...]
     stacked = jnp.concatenate([operand[...] for operand in operands], axis=0)
     product = dot(matrix[...], stacked).astype(own.dtype)
     rows = own.shape[0]
@@ -251,13 +252,13 @@
     forward = dict(flops=2 * down * across * width, need=2 * dense_bytes)
     if paired:
         layers = 2
-        own, *sends = call(
+        own, *sends, passed = call(
             functools.partial(paired_forward_kernel, n_row),
-            [((2 * nodes, width), NARROW)] * 4,
-            [VMEM] * (1 + n_row),
+            [((2 * nodes, width), NARROW)] * 4 + [((nodes, hidden), NARROW)],
+            [VMEM] * (2 + n_row),
             **forward,
-        )(near, features, *gathered)
-        layer_call, cotangents = paired_layer_kernel, [cotangent, swap(cotangent, "col", 2)]
+        )(near, features, *gathered, cotangent)
+        layer_call, cotangents = paired_layer_kernel, [cotangent, swap(passed, "col", 2)]
     else:
         layers = 1
         own, *sends = call(

time: 31.4 us -> 33.9 us (1.080)
  waiting for transfers between devices: 11.8 us -> 17.4 us
  starting transfers between devices: 13.4 us -> 10.5 us
    ppermute x3, waiting for transfers between devices: 4.32 us -> 10.2 us  [swap(): return lax.ppermute(value, axis, [(s, s ^ distance) for s in range(n)])]
    ppermute x3, starting transfers between devices: 4.7 us -> 0.48 us  [swap(): return lax.ppermute(value, axis, [(s, s ^ distance) for s in range(n)])]
    ppermute x9, starting transfers between devices: 8.72 us -> 10 us  [exchange(): lax.ppermute(send, axis, [(s, target(s, d)) for s in range(n)])]
  transfers between devices with their start and end apart: 12 -> 12, of which waited for: 7 -> 9; matrix products, arithmetic and copies ran while one was open for 0% -> 0% of each run, Pallas kernels for 7% -> 5%
where the time goes in v15:
time: 33.9 us; the launch traced here: 33.7 us
  waiting for transfers between devices  17.4 us (51%)
  starting transfers between devices  10.5 us (31%)
  Pallas kernels  3.46 us (10%)
  between operations  1.4 us (4%)
  local copies, waits for them, and re-layouts  0.96 us (3%)
    ppermute x3, waiting for transfers between devices, swap(): return lax.ppermute(value, axis, [(s, s ^ distance) for s in range(n)])  10.2 us
    ppermute x9, starting transfers between devices, exchange(): lax.ppermute(send, axis, [(s, target(s, d)) for s in range(n)])  10 us
    ppermute x9, waiting for transfers between devices, exchange(): lax.ppermute(send, axis, [(s, target(s, d)) for s in range(n)])  7.25 us
    unnamed x12, local copies, waits for them, and re-layouts  0.96 us
    pallas_call x1, Pallas kernels, per_device(): call(functools.partial(last_kernel, scale), [((nodes, width), NARROW), ((...  0.69 us
  transfers between devices with their start and end apart: 12, of which 9 were waited for; matrix products, arithmetic and copies ran while one was open for 0% of the time, Pallas kernels for 5%

profile of v15, /device:TPU:0, one launch (start us, length us, event | category | flops | bytes accessed | tf_op | source)
XLA Modules:
  0.0 33.7 jit_solution(4015102388745480461)
XLA Ops:
  0.6 0.0 copy-start.4
  0.6 0.0 copy-start.5
  0.7 2.4 %collective-permute-start = (bf16[128,128]{1,0:T(8,128)(2,1)}, bf16[128,128]{1,0:T(8,128)(2,1)S(1)}, u32[]{:S(2)}, u32[]{:S(2)}) collective-permute-start(bf16[128,128]{1,0:T(8,128)(2,1)} %refs_0_.1), channel_id=1, source_target_pairs={{0,12},{4,0},{8,4},{12,8},{1,13},{5,1},{9,5},{13,9},{2,14},{6,2},{... | collective-permute-start | bytes 98312 | tf_op jit(solution)/shard_map/ppermute | solution.py:42
  3.1 0.6 %collective-permute-start.1 = (bf16[128,128]{1,0:T(8,128)(2,1)}, bf16[128,128]{1,0:T(8,128)(2,1)S(1)}, u32[]{:S(2)}, u32[]{:S(2)}) collective-permute-start(bf16[128,128]{1,0:T(8,128)(2,1)} %refs_0_.1), channel_id=1, source_target_pairs={{0,8},{4,12},{8,0},{12,4},{1,9},{5,13},{9,1},{13,5},{2,10},{6,14},... | collective-permute-start | bytes 98312 | tf_op jit(solution)/shard_map/ppermute | solution.py:42
  3.7 0.2 collective-permute-start.2
  4.5 0.0 copy-done.4
  4.5 0.0 copy-done.5
  4.6 0.0 copy-start
  4.6 0.9 %copy-done = bf16[1,1,8,128,128]{4,3,2,1,0:T(8,128)(2,1)S(1)} copy-done((bf16[1,1,8,128,128]{4,3,2,1,0:T(8,128)(2,1)S(1)}, bf16[1,1,8,128,128]{4,3,2,1,0:T(8,128)(2,1)}, u32[]{:S(2)}) %copy-start) | copy-done | bytes 262168
  5.5 0.0 copy-start.1
  5.5 0.0 copy-start.3
  5.5 0.7 %shard_map.94.near.matrix = bf16[512,512]{1,0:T(8,128)(2,1)S(1)} custom-call(bf16[1,1,8,128,128]{4,3,2,1,0:T(8,128)(2,1)S(1)} %copy-done, s32[1,1,8]{2,1,0:T(1,128)S(1)} %copy-done.4, s32[1,1,8]{2,1,0:T(1,128)S(1)} %copy-done.5, s32[1,1]{1,0:T(1,128)S(6)} %copy.10.count_in), custom_call_target="tpu_custom_call" | custom-call | bytes 1048576 | tf_op jit(solution)/shard_map/pallas_call | solution.py:239
  6.2 0.0 collective-permute-done.refs_1_
  6.2 1.3 %collective-permute-done.1.refs_2_ = bf16[128,128]{1,0:T(8,128)(2,1)S(1)} collective-permute-done((bf16[128,128]{1,0:T(8,128)(2,1)}, bf16[128,128]{1,0:T(8,128)(2,1)S(1)}, u32[]{:S(2)}, u32[]{:S(2)}) %collective-permute-start.1) | collective-permute-done | bytes 32800 | tf_op jit(solution)/shard_map/ppermute | solution.py:42
  7.5 0.1 collective-permute-done.2.refs_3_
  7.6 0.0 copy-done.1
  7.6 0.0 copy-done.3
  7.6 0.3 shard_map.96
  7.9 1.6 %collective-permute-start.3 = (bf16[256,128]{1,0:T(8,128)(2,1)S(1)}, bf16[256,128]{1,0:T(8,128)(2,1)S(1)}, u32[]{:S(2)}, u32[]{:S(2)}) collective-permute-start(bf16[256,128]{1,0:T(8,128)(2,1)S(1)} %get-tuple-element.20), channel_id=1, source_target_pairs={{0,1},{1,3},{2,0},{3,2},{4,5},{5,7},{6,4},{7,6},{8,9},{9,11},{10,8... | collective-permute-start | bytes 196616 | tf_op jit(solution)/shard_map/ppermute | solution.py:42
  9.5 2.5 %collective-permute-start.4 = (bf16[256,128]{1,0:T(8,128)(2,1)S(1)}, bf16[256,128]{1,0:T(8,128)(2,1)S(1)}, u32[]{:S(2)}, u32[]{:S(2)}) collective-permute-start(bf16[256,128]{1,0:T(8,128)(2,1)S(1)} %get-tuple-element.21), channel_id=1, source_target_pairs={{0,3},{1,2},{2,1},{3,0},{4,7},{5,6},{6,5},{7,4},{8,11},{9,10},{10,... | collective-permute-start | bytes 196616 | tf_op jit(solution)/shard_map/ppermute | solution.py:42
  12.0 1.6 %collective-permute-start.5 = (bf16[256,128]{1,0:T(8,128)(2,1)S(1)}, bf16[256,128]{1,0:T(8,128)(2,1)S(1)}, u32[]{:S(2)}, u32[]{:S(2)}) collective-permute-start(bf16[256,128]{1,0:T(8,128)(2,1)S(1)} %get-tuple-element.22), channel_id=1, source_target_pairs={{0,2},{1,0},{2,3},{3,1},{4,6},{5,4},{6,7},{7,5},{8,10},{9,8},{10,1... | collective-permute-start | bytes 196616 | tf_op jit(solution)/shard_map/ppermute | solution.py:42
  13.5 0.0 copy-start.2
  13.5 0.3 collective-permute-start.6
  13.9 0.3 %shard_map.95.refs_0_.matrix = bf16[512,512]{1,0:T(8,128)(2,1)S(1)} custom-call(bf16[512,512]{1,0:T(8,128)(2,1)S(1)} %shard_map.94.near.matrix), custom_call_target="tpu_custom_call" | custom-call | bytes 1572864 | tf_op jit(solution)/shard_map/pallas_call | solution.py:272
  14.2 0.0 collective-permute-done.3.refs_2_
  14.2 2.1 %collective-permute-done.4.refs_3_ = bf16[256,128]{1,0:T(8,128)(2,1)S(1)} collective-permute-done((bf16[256,128]{1,0:T(8,128)(2,1)S(1)}, bf16[256,128]{1,0:T(8,128)(2,1)S(1)}, u32[]{:S(2)}, u32[]{:S(2)}) %collective-permute-start.4) | collective-permute-done | bytes 65568 | tf_op jit(solution)/shard_map/ppermute | solution.py:42
  16.4 0.4 %collective-permute-done.5.refs_4_ = bf16[256,128]{1,0:T(8,128)(2,1)S(1)} collective-permute-done((bf16[256,128]{1,0:T(8,128)(2,1)S(1)}, bf16[256,128]{1,0:T(8,128)(2,1)S(1)}, u32[]{:S(2)}, u32[]{:S(2)}) %collective-permute-start.5) | collective-permute-done | bytes 65568 | tf_op jit(solution)/shard_map/ppermute | solution.py:42
  16.7 4.1 %collective-permute-done.6.refs_7_ = bf16[128,256]{1,0:T(8,128)(2,1)S(1)} collective-permute-done((bf16[128,256]{1,0:T(8,128)(2,1)S(1)}, bf16[128,256]{1,0:T(8,128)(2,1)S(1)}, u32[]{:S(2)}, u32[]{:S(2)}) %collective-permute-start.6) | collective-permute-done | bytes 65568 | tf_op jit(solution)/shard_map/ppermute | solution.py:53
  20.9 0.0 copy-done.2
  20.9 0.5 %shard_map.97 = (bf16[256,128]{1,0:T(8,128)(2,1)S(1)}, f32[128,128]{1,0:T(8,128)S(1)}, bf16[128,128]{1,0:T(8,128)(2,1)S(1)}, f32[128,256]{1,0:T(8,128)S(1)}) custom-call(bf16[512,512]{1,0:T(8,128)(2,1)S(1)} %shard_map.95.refs_0_.matrix, bf16[256,128]{1,0:T(8,128)(2,1)S(1)} %get-tuple-element.19.refs_1_, bf16[256,128]{1,0:T(8,128)(2,1)S(1)} %collective-permute-done.3.refs_2_, ...), custom_call_target="tpu_custom_call" | custom-call | flops 117440512 | tf_op jit(solution)/shard_map/pallas_call | solution.py:281
  21.4 0.1 collective-permute-start.7
  21.5 1.2 %collective-permute-done.7.came = bf16[128,128]{1,0:T(8,128)(2,1)S(1)} collective-permute-done((bf16[128,128]{1,0:T(8,128)(2,1)S(1)}, bf16[128,128]{1,0:T(8,128)(2,1)S(1)}, u32[]{:S(2)}, u32[]{:S(2)}) %collective-permute-start.7) | collective-permute-done | bytes 32800 | tf_op jit(solution)/shard_map/ppermute | solution.py:53
  22.7 0.1 collective-permute-start.8
  22.7 4.8 %collective-permute-done.8.refs_1_ = bf16[384,128]{1,0:T(8,128)(2,1)S(1)} collective-permute-done((bf16[384,128]{1,0:T(8,128)(2,1)S(1)}, bf16[384,128]{1,0:T(8,128)(2,1)S(1)}, u32[]{:S(2)}, u32[]{:S(2)}) %collective-permute-start.8) | collective-permute-done | bytes 98336 | tf_op jit(solution)/shard_map/ppermute | solution.py:53
  27.6 0.3 shard_map.100
  27.9 0.6 %collective-permute-start.10 = (bf16[256,128]{1,0:T(8,128)(2,1)S(1)}, bf16[256,128]{1,0:T(8,128)(2,1)S(1)}, u32[]{:S(2)}, u32[]{:S(2)}) collective-permute-start(bf16[256,128]{1,0:T(8,128)(2,1)S(1)} %get-tuple-element.31), channel_id=1, source_target_pairs={{0,8},{4,12},{8,0},{12,4},{1,9},{5,13},{9,1},{13,5},{2,10},{6,14},... | collective-permute-start | bytes 196616 | tf_op jit(solution)/shard_map/ppermute | solution.py:42
  28.5 0.2 collective-permute-start.11
  28.6 0.3 %collective-permute-start.9 = (bf16[256,128]{1,0:T(8,128)(2,1)S(1)}, bf16[256,128]{1,0:T(8,128)(2,1)S(1)}, u32[]{:S(2)}, u32[]{:S(2)}) collective-permute-start(bf16[256,128]{1,0:T(8,128)(2,1)S(1)} %get-tuple-element.30), channel_id=1, source_target_pairs={{0,4},{4,8},{8,12},{12,0},{1,5},{5,9},{9,13},{13,1},{2,6},{6,10},{... | collective-permute-start | bytes 196616 | tf_op jit(solution)/shard_map/ppermute | solution.py:42
  29.0 0.7 %shard_map.98 = bf16[128,256]{1,0:T(8,128)(2,1)} custom-call(f32[128,256]{1,0:T(8,128)S(1)} %get-tuple-element.24.pre), custom_call_target="tpu_custom_call" | custom-call | tf_op jit(solution)/shard_map/pallas_call | solution.py:300
  29.6 3.2 %collective-permute-done.10.refs_1_ = bf16[256,128]{1,0:T(8,128)(2,1)S(1)} collective-permute-done((bf16[256,128]{1,0:T(8,128)(2,1)S(1)}, bf16[256,128]{1,0:T(8,128)(2,1)S(1)}, u32[]{:S(2)}, u32[]{:S(2)}) %collective-permute-start.10) | collective-permute-done | bytes 65568 | tf_op jit(solution)/shard_map/ppermute | solution.py:42
  32.8 0.0 collective-permute-done.11.refs_2_
  32.8 0.2 collective-permute-done.9.refs_0_
  33.0 0.7 %shard_map.101 = (bf16[128,128]{1,0:T(8,128)(2,1)}, f32[128,256]{1,0:T(8,128)}) custom-call(f32[128,128]{1,0:T(8,128)S(1)} %get-tuple-element.28.own, bf16[128,128]{1,0:T(8,128)(2,1)S(1)} %get-tuple-element.29.kept, bf16[256,128]{1,0:T(8,128)(2,1)S(1)} %collective-permute-done.9.refs_0_, bf16[256,128]{1,0:T(8,128)(2,1)S(1)} %collective-permute-done.10.refs_1_, ...), custom_call_target="tpu_custom_call" | custom-call | tf_op jit(solution)/shard_map/pallas_call | solution.py:312
  (1 shorter events, 0.0 us)
Async XLA Ops:
  0.6 3.9 %copy-start.4 = (s32[1,1,8]{2,1,0:T(1,128)S(1)}, s32[1,1,8]{2,1,0:T(1,128)}, u32[]{:S(2)}) copy-start(s32[1,1,8]{2,1,0:T(1,128)} %rows_in.1) | copy-start | bytes 100
  0.6 3.9 %copy-start.5 = (s32[1,1,8]{2,1,0:T(1,128)S(1)}, s32[1,1,8]{2,1,0:T(1,128)}, u32[]{:S(2)}) copy-start(s32[1,1,8]{2,1,0:T(1,128)} %cols_in.1) | copy-start | bytes 100
  0.7 5.5 %collective-permute-start = (bf16[128,128]{1,0:T(8,128)(2,1)}, bf16[128,128]{1,0:T(8,128)(2,1)S(1)}, u32[]{:S(2)}, u32[]{:S(2)}) collective-permute-start(bf16[128,128]{1,0:T(8,128)(2,1)} %refs_0_.1), channel_id=1, source_target_pairs={{0,12},{4,0},{8,4},{12,8},{1,13},{5,1},{9,5},{13,9},{2,14},{6,2},{... | collective-permute-start | bytes 98312 | tf_op jit(solution)/shard_map/ppermute | solution.py:42
  3.1 4.4 %collective-permute-start.1 = (bf16[128,128]{1,0:T(8,128)(2,1)}, bf16[128,128]{1,0:T(8,128)(2,1)S(1)}, u32[]{:S(2)}, u32[]{:S(2)}) collective-permute-start(bf16[128,128]{1,0:T(8,128)(2,1)} %refs_0_.1), channel_id=1, source_target_pairs={{0,8},{4,12},{8,0},{12,4},{1,9},{5,13},{9,1},{13,5},{2,10},{6,14},... | collective-permute-start | bytes 98312 | tf_op jit(solution)/shard_map/ppermute | solution.py:42
  3.7 3.8 %collective-permute-start.2 = (bf16[128,128]{1,0:T(8,128)(2,1)}, bf16[128,128]{1,0:T(8,128)(2,1)S(1)}, u32[]{:S(2)}, u32[]{:S(2)}) collective-permute-start(bf16[128,128]{1,0:T(8,128)(2,1)} %refs_0_.1), channel_id=1, source_target_pairs={{0,4},{4,8},{8,12},{12,0},{1,5},{5,9},{9,13},{13,1},{2,6},{6,10},{... | collective-permute-start | bytes 98312 | tf_op jit(solution)/shard_map/ppermute | solution.py:42
  4.6 1.0 %copy-start = (bf16[1,1,8,128,128]{4,3,2,1,0:T(8,128)(2,1)S(1)}, bf16[1,1,8,128,128]{4,3,2,1,0:T(8,128)(2,1)}, u32[]{:S(2)}) copy-start(bf16[1,1,8,128,128]{4,3,2,1,0:T(8,128)(2,1)} %vals.1) | copy-start | bytes 786436
  5.5 2.1 %copy-start.1 = (bf16[128,256]{1,0:T(8,128)(2,1)S(1)}, bf16[128,256]{1,0:T(8,128)(2,1)}, u32[]{:S(2)}) copy-start(bf16[128,256]{1,0:T(8,128)(2,1)} %refs_6_.1) | copy-start | bytes 196612
  5.5 2.1 %copy-start.3 = (bf16[128,128]{1,0:T(8,128)(2,1)S(1)}, bf16[128,128]{1,0:T(8,128)(2,1)}, u32[]{:S(2)}) copy-start(bf16[128,128]{1,0:T(8,128)(2,1)} %refs_0_.1) | copy-start | bytes 98308
  7.9 6.4 %collective-permute-start.3 = (bf16[256,128]{1,0:T(8,128)(2,1)S(1)}, bf16[256,128]{1,0:T(8,128)(2,1)S(1)}, u32[]{:S(2)}, u32[]{:S(2)}) collective-permute-start(bf16[256,128]{1,0:T(8,128)(2,1)S(1)} %get-tuple-element.20), channel_id=1, source_target_pairs={{0,1},{1,3},{2,0},{3,2},{4,5},{5,7},{6,4},{7,6},{8,9},{9,11},{10,8... | collective-permute-start | bytes 196616 | tf_op jit(solution)/shard_map/ppermute | solution.py:42
  9.5 6.9 %collective-permute-start.4 = (bf16[256,128]{1,0:T(8,128)(2,1)S(1)}, bf16[256,128]{1,0:T(8,128)(2,1)S(1)}, u32[]{:S(2)}, u32[]{:S(2)}) collective-permute-start(bf16[256,128]{1,0:T(8,128)(2,1)S(1)} %get-tuple-element.21), channel_id=1, source_target_pairs={{0,3},{1,2},{2,1},{3,0},{4,7},{5,6},{6,5},{7,4},{8,11},{9,10},{10,... | collective-permute-start | bytes 196616 | tf_op jit(solution)/shard_map/ppermute | solution.py:42
  12.0 4.8 %collective-permute-start.5 = (bf16[256,128]{1,0:T(8,128)(2,1)S(1)}, bf16[256,128]{1,0:T(8,128)(2,1)S(1)}, u32[]{:S(2)}, u32[]{:S(2)}) collective-permute-start(bf16[256,128]{1,0:T(8,128)(2,1)S(1)} %get-tuple-element.22), channel_id=1, source_target_pairs={{0,2},{1,0},{2,3},{3,1},{4,6},{5,4},{6,7},{7,5},{8,10},{9,8},{10,1... | collective-permute-start | bytes 196616 | tf_op jit(solution)/shard_map/ppermute | solution.py:42
  13.5 7.3 %copy-start.2 = (bf16[128,256]{1,0:T(8,128)(2,1)S(1)}, bf16[128,256]{1,0:T(8,128)(2,1)}, u32[]{:S(2)}) copy-start(bf16[128,256]{1,0:T(8,128)(2,1)} %refs_5_.1) | copy-start | bytes 196612
  13.5 7.3 %collective-permute-start.6 = (bf16[128,256]{1,0:T(8,128)(2,1)S(1)}, bf16[128,256]{1,0:T(8,128)(2,1)S(1)}, u32[]{:S(2)}, u32[]{:S(2)}) collective-permute-start(bf16[128,256]{1,0:T(8,128)(2,1)S(1)} %get-tuple-element.23), channel_id=1, source_target_pairs={{0,2},{1,3},{2,0},{3,1},{4,6},{5,7},{6,4},{7,5},{8,10},{9,11},{10,... | collective-permute-start | bytes 196616 | tf_op jit(solution)/shard_map/ppermute | solution.py:53
  21.4 1.3 %collective-permute-start.7 = (bf16[128,128]{1,0:T(8,128)(2,1)S(1)}, bf16[128,128]{1,0:T(8,128)(2,1)S(1)}, u32[]{:S(2)}, u32[]{:S(2)}) collective-permute-start(bf16[128,128]{1,0:T(8,128)(2,1)S(1)} %get-tuple-element.27), channel_id=1, source_target_pairs={{0,4},{4,0},{8,12},{12,8},{1,5},{5,1},{9,13},{13,9},{2,6},{6,2},{1... | collective-permute-start | bytes 98312 | tf_op jit(solution)/shard_map/ppermute | solution.py:53
  22.7 4.9 %collective-permute-start.8 = (bf16[384,128]{1,0:T(8,128)(2,1)S(1)}, bf16[384,128]{1,0:T(8,128)(2,1)S(1)}, u32[]{:S(2)}, u32[]{:S(2)}) collective-permute-start(bf16[384,128]{1,0:T(8,128)(2,1)S(1)} %shard_map.99.refs_0_), channel_id=1, source_target_pairs={{0,1},{1,0},{2,3},{3,2},{4,5},{5,4},{6,7},{7,6},{8,9},{9,8},{10,11... | collective-permute-start | bytes 294920 | tf_op jit(solution)/shard_map/ppermute | solution.py:53
  27.9 4.9 %collective-permute-start.10 = (bf16[256,128]{1,0:T(8,128)(2,1)S(1)}, bf16[256,128]{1,0:T(8,128)(2,1)S(1)}, u32[]{:S(2)}, u32[]{:S(2)}) collective-permute-start(bf16[256,128]{1,0:T(8,128)(2,1)S(1)} %get-tuple-element.31), channel_id=1, source_target_pairs={{0,8},{4,12},{8,0},{12,4},{1,9},{5,13},{9,1},{13,5},{2,10},{6,14},... | collective-permute-start | bytes 196616 | tf_op jit(solution)/shard_map/ppermute | solution.py:42
  28.5 4.3 %collective-permute-start.11 = (bf16[256,128]{1,0:T(8,128)(2,1)S(1)}, bf16[256,128]{1,0:T(8,128)(2,1)S(1)}, u32[]{:S(2)}, u32[]{:S(2)}) collective-permute-start(bf16[256,128]{1,0:T(8,128)(2,1)S(1)} %get-tuple-element.32), channel_id=1, source_target_pairs={{0,12},{4,0},{8,4},{12,8},{1,13},{5,1},{9,5},{13,9},{2,14},{6,2},{... | collective-permute-start | bytes 196616 | tf_op jit(solution)/shard_map/ppermute | solution.py:42
  28.6 4.4 %collective-permute-start.9 = (bf16[256,128]{1,0:T(8,128)(2,1)S(1)}, bf16[256,128]{1,0:T(8,128)(2,1)S(1)}, u32[]{:S(2)}, u32[]{:S(2)}) collective-permute-start(bf16[256,128]{1,0:T(8,128)(2,1)S(1)} %get-tuple-element.30), channel_id=1, source_target_pairs={{0,4},{4,8},{8,12},{12,0},{1,5},{5,9},{9,13},{13,1},{2,6},{6,10},{... | collective-permute-start | bytes 196616 | tf_op jit(solution)/shard_map/ppermute | solution.py:42

commit v16 on v13

--- a/solution.py
+++ b/solution.py
@@ -13,7 +13,7 @@
 NARROW = jnp.bfloat16
 
 
-def call(kernel, outs, in_specs, scratch=(), flops=0, need=0, after=()):
+def call(kernel, outs, in_specs, scratch=(), flops=0, need=0, after=(), aliases=None):
     outs = tuple(jax.ShapeDtypeStruct(shape, dtype) for shape, dtype in outs)
     late = len(after)
     run = pl.pallas_call(
@@ -21,6 +21,7 @@
         out_shape=outs,
         in_specs=[ANY] * late + list(in_specs),
         out_specs=(VMEM,) * len(outs),
+        input_output_aliases=aliases or {},
         scratch_shapes=scratch,
         compiler_params=pltpu.CompilerParams(vmem_limit_bytes=LEAST + need),
         cost_estimate=pl.CostEstimate(flops=flops, bytes_accessed=need, transcendentals=0),
@@ -66,7 +67,11 @@
     return lax.dot_general(left, right, (dims, ((), ())), preferred_element_type=jnp.float32)
 
 
-def dense_kernel(piece, paired, vals, rows_in, cols_in, count_in, near, rows, cols, count, sems):
+def zero_kernel(out):
+    out[...] = jnp.zeros_like(out)
+
+
+def dense_kernel(piece, paired, blank, vals, rows_in, cols_in, count_in, near, rows, cols, count, sems):
     copies = [
         pltpu.make_async_copy(source, target, sems.at[k])
         for k, (source, target) in enumerate(((rows_in, rows), (cols_in, cols), (count_in, count)))
@@ -74,7 +79,6 @@
     for copy in copies:
         copy.start()
     side = vals.shape[-1]
-    near[...] = jnp.zeros_like(near)
     for copy in copies:
         copy.wait()
 
@@ -235,10 +239,12 @@
 
     paired = n_col == 4
     gathered = exchange([features] * (n_row - 1), "row", False)
+    (blank,) = call(zero_kernel, [((down, across), NARROW)], [], need=dense_bytes)()
     (near,) = call(
         functools.partial(dense_kernel, nodes // side, paired),
         [((down, across), NARROW)],
-        [VMEM] * 4,
+        [VMEM] * 5,
+        aliases={0: 0},
         scratch=[
             pltpu.SMEM(tile_rows.shape, jnp.int32),
             pltpu.SMEM(tile_cols.shape, jnp.int32),
@@ -246,7 +252,7 @@
             pltpu.SemaphoreType.DMA((3,)),
         ],
         need=2 * dense_bytes,
-    )(tile_values, tile_rows, tile_cols, tile_count)
+    )(blank, tile_values, tile_rows, tile_cols, tile_count)
 
     forward = dict(flops=2 * down * across * width, need=2 * dense_bytes)
     if paired:

time: 31.4 us -> 30.6 us (0.975)
  starting transfers between devices: 13.4 us -> 14.3 us
  local copies, waits for them, and re-layouts: 0.96 us -> 0.07 us
  waiting for transfers between devices: 11.8 us -> 11.1 us
    ppermute x9, starting transfers between devices: 8.72 us -> 9.71 us  [exchange(): lax.ppermute(send, axis, [(s, target(s, d)) for s in range(n)])]
    unnamed x12, local copies, waits for them, and re-layouts: 0.96 us -> 0.07 us
    ppermute x9, waiting for transfers between devices: 7.52 us -> 6.79 us  [exchange(): lax.ppermute(send, axis, [(s, target(s, d)) for s in range(n)])]
where the time goes in v16:
time: 30.6 us; the launch traced here: 30.4 us
  starting transfers between devices  14.3 us (47%)
  waiting for transfers between devices  11.1 us (36%)
  Pallas kernels  3.5 us (11%)
  between operations  1.44 us (5%)
    ppermute x9, starting transfers between devices, exchange(): lax.ppermute(send, axis, [(s, target(s, d)) for s in range(n)])  9.71 us
    ppermute x9, waiting for transfers between devices, exchange(): lax.ppermute(send, axis, [(s, target(s, d)) for s in range(n)])  6.79 us
    ppermute x3, starting transfers between devices, swap(): return lax.ppermute(value, axis, [(s, s ^ distance) for s in range(n)])  4.6 us
    ppermute x3, waiting for transfers between devices, swap(): return lax.ppermute(value, axis, [(s, s ^ distance) for s in range(n)])  4.32 us
    pallas_call x1, Pallas kernels, per_device(): call(functools.partial(last_kernel, scale), [((nodes, width), NARROW), ((...  0.69 us
    pallas_call x1, Pallas kernels, per_device(): call(functools.partial(dense_kernel, nodes // side, paired), [((down, acr...  0.67 us
    pallas_call x1, Pallas kernels, per_device(): act, = call(act_kernel, [((nodes, hidden), NARROW)], [VMEM])(pre)  0.65 us
  transfers between devices with their start and end apart: 12, of which 7 were waited for; matrix products, arithmetic and copies ran while one was open for 0% of the time, Pallas kernels for 7%

profile of v16, /device:TPU:0, one launch (start us, length us, event | category | flops | bytes accessed | tf_op | source)
XLA Modules:
  0.0 30.4 jit_solution(13701106009320490833)
XLA Ops:
  0.6 0.0 copy-start
  0.6 2.4 %collective-permute-start = (bf16[128,128]{1,0:T(8,128)(2,1)}, bf16[128,128]{1,0:T(8,128)(2,1)S(1)}, u32[]{:S(2)}, u32[]{:S(2)}) collective-permute-start(bf16[128,128]{1,0:T(8,128)(2,1)} %refs_0_.1), channel_id=1, source_target_pairs={{0,12},{4,0},{8,4},{12,8},{1,13},{5,1},{9,5},{13,9},{2,14},{6,2},{... | collective-permute-start | bytes 98312 | tf_op jit(solution)/shard_map/ppermute | solution.py:43
  3.1 0.6 %collective-permute-start.1 = (bf16[128,128]{1,0:T(8,128)(2,1)}, bf16[128,128]{1,0:T(8,128)(2,1)S(1)}, u32[]{:S(2)}, u32[]{:S(2)}) collective-permute-start(bf16[128,128]{1,0:T(8,128)(2,1)} %refs_0_.1), channel_id=1, source_target_pairs={{0,8},{4,12},{8,0},{12,4},{1,9},{5,13},{9,1},{13,5},{2,10},{6,14},... | collective-permute-start | bytes 98312 | tf_op jit(solution)/shard_map/ppermute | solution.py:43
  3.7 0.2 collective-permute-start.2
  3.9 2.6 %collective-permute-start.6 = (bf16[128,256]{1,0:T(8,128)(2,1)}, bf16[128,256]{1,0:T(8,128)(2,1)S(1)}, u32[]{:S(2)}, u32[]{:S(2)}) collective-permute-start(bf16[128,256]{1,0:T(8,128)(2,1)} %refs_6_.1), channel_id=1, source_target_pairs={{0,2},{1,3},{2,0},{3,1},{4,6},{5,7},{6,4},{7,5},{8,10},{9,11},{10,... | collective-permute-start | bytes 196616 | tf_op jit(solution)/shard_map/ppermute | solution.py:54
  6.5 0.0 copy-start.4
  6.5 0.0 copy-start.5
  7.2 0.0 copy-done
  7.2 0.0 copy-done.4
  7.2 0.0 copy-done.5
  7.2 0.0 copy-start.3
  7.2 0.7 %shard_map.95.near.matrix = bf16[512,512]{1,0:T(8,128)(2,1)S(1)} custom-call(bf16[512,512]{1,0:T(8,128)(2,1)S(1)} %shard_map.94.blank, bf16[1,1,8,128,128]{4,3,2,1,0:T(8,128)(2,1)S(1)} %copy-done, s32[1,1,8]{2,1,0:T(1,128)S(1)} %copy-done.4, s32[1,1,8]{2,1,0:T(1,128)S(1)} %copy-done.5, s32[1,1]{1,0:T(1,128)S(6)} %copy.12.count_in), custom_call_target="tpu_custom_call", output_to_operand_aliasing={{}: (0, {})} | custom-call | bytes 1048576 | tf_op jit(solution)/shard_map/pallas_call | solution.py:243
  7.9 0.0 collective-permute-done.refs_1_
  7.9 0.0 collective-permute-done.1.refs_2_
  7.9 0.0 collective-permute-done.2.refs_3_
  7.9 0.0 copy-done.3
  8.0 0.3 shard_map.97
  8.3 1.7 %collective-permute-start.3 = (bf16[256,128]{1,0:T(8,128)(2,1)S(1)}, bf16[256,128]{1,0:T(8,128)(2,1)S(1)}, u32[]{:S(2)}, u32[]{:S(2)}) collective-permute-start(bf16[256,128]{1,0:T(8,128)(2,1)S(1)} %get-tuple-element.19), channel_id=1, source_target_pairs={{0,1},{1,3},{2,0},{3,2},{4,5},{5,7},{6,4},{7,6},{8,9},{9,11},{10,8... | collective-permute-start | bytes 196616 | tf_op jit(solution)/shard_map/ppermute | solution.py:43
  10.0 1.9 %collective-permute-start.4 = (bf16[256,128]{1,0:T(8,128)(2,1)S(1)}, bf16[256,128]{1,0:T(8,128)(2,1)S(1)}, u32[]{:S(2)}, u32[]{:S(2)}) collective-permute-start(bf16[256,128]{1,0:T(8,128)(2,1)S(1)} %get-tuple-element.20), channel_id=1, source_target_pairs={{0,3},{1,2},{2,1},{3,0},{4,7},{5,6},{6,5},{7,4},{8,11},{9,10},{10,... | collective-permute-start | bytes 196616 | tf_op jit(solution)/shard_map/ppermute | solution.py:43
  12.0 0.0 copy-start.1
  12.0 0.0 copy-start.2
  12.0 1.6 %collective-permute-start.5 = (bf16[256,128]{1,0:T(8,128)(2,1)S(1)}, bf16[256,128]{1,0:T(8,128)(2,1)S(1)}, u32[]{:S(2)}, u32[]{:S(2)}) collective-permute-start(bf16[256,128]{1,0:T(8,128)(2,1)S(1)} %get-tuple-element.21), channel_id=1, source_target_pairs={{0,2},{1,0},{2,3},{3,1},{4,6},{5,4},{6,7},{7,5},{8,10},{9,8},{10,1... | collective-permute-start | bytes 196616 | tf_op jit(solution)/shard_map/ppermute | solution.py:43
  13.5 0.3 %shard_map.96.refs_0_.matrix = bf16[512,512]{1,0:T(8,128)(2,1)S(1)} custom-call(bf16[512,512]{1,0:T(8,128)(2,1)S(1)} %shard_map.95.near.matrix), custom_call_target="tpu_custom_call" | custom-call | bytes 1572864 | tf_op jit(solution)/shard_map/pallas_call | solution.py:277
  13.9 0.0 collective-permute-done.6.refs_7_
  13.9 0.3 %collective-permute-done.3.refs_2_ = bf16[256,128]{1,0:T(8,128)(2,1)S(1)} collective-permute-done((bf16[256,128]{1,0:T(8,128)(2,1)S(1)}, bf16[256,128]{1,0:T(8,128)(2,1)S(1)}, u32[]{:S(2)}, u32[]{:S(2)}) %collective-permute-start.3) | collective-permute-done | bytes 65568 | tf_op jit(solution)/shard_map/ppermute | solution.py:43
  14.2 2.7 %collective-permute-done.4.refs_3_ = bf16[256,128]{1,0:T(8,128)(2,1)S(1)} collective-permute-done((bf16[256,128]{1,0:T(8,128)(2,1)S(1)}, bf16[256,128]{1,0:T(8,128)(2,1)S(1)}, u32[]{:S(2)}, u32[]{:S(2)}) %collective-permute-start.4) | collective-permute-done | bytes 65568 | tf_op jit(solution)/shard_map/ppermute | solution.py:43
  16.9 0.4 %collective-permute-done.5.refs_4_ = bf16[256,128]{1,0:T(8,128)(2,1)S(1)} collective-permute-done((bf16[256,128]{1,0:T(8,128)(2,1)S(1)}, bf16[256,128]{1,0:T(8,128)(2,1)S(1)}, u32[]{:S(2)}, u32[]{:S(2)}) %collective-permute-start.5) | collective-permute-done | bytes 65568 | tf_op jit(solution)/shard_map/ppermute | solution.py:43
  17.3 0.0 copy-done.1
  17.3 0.0 copy-done.2
  17.3 0.5 %shard_map.98 = (bf16[256,128]{1,0:T(8,128)(2,1)S(1)}, f32[128,128]{1,0:T(8,128)S(1)}, bf16[128,128]{1,0:T(8,128)(2,1)S(1)}, f32[128,256]{1,0:T(8,128)S(1)}) custom-call(bf16[512,512]{1,0:T(8,128)(2,1)S(1)} %shard_map.96.refs_0_.matrix, bf16[256,128]{1,0:T(8,128)(2,1)S(1)} %get-tuple-element.18.refs_1_, bf16[256,128]{1,0:T(8,128)(2,1)S(1)} %collective-permute-done.3.refs_2_, ...), custom_call_target="tpu_custom_call" | custom-call | flops 117440512 | tf_op jit(solution)/shard_map/pallas_call | solution.py:286
  17.8 0.1 collective-permute-start.7
  17.9 1.2 %collective-permute-done.7.came = bf16[128,128]{1,0:T(8,128)(2,1)S(1)} collective-permute-done((bf16[128,128]{1,0:T(8,128)(2,1)S(1)}, bf16[128,128]{1,0:T(8,128)(2,1)S(1)}, u32[]{:S(2)}, u32[]{:S(2)}) %collective-permute-start.7) | collective-permute-done | bytes 32800 | tf_op jit(solution)/shard_map/ppermute | solution.py:54
  19.1 1.9 %collective-permute-start.8 = (bf16[384,128]{1,0:T(8,128)(2,1)S(1)}, bf16[384,128]{1,0:T(8,128)(2,1)S(1)}, u32[]{:S(2)}, u32[]{:S(2)}) collective-permute-start(bf16[384,128]{1,0:T(8,128)(2,1)S(1)} %shard_map.100.refs_0_), channel_id=1, source_target_pairs={{0,1},{1,0},{2,3},{3,2},{4,5},{5,4},{6,7},{7,6},{8,9},{9,8},{10,11... | collective-permute-start | bytes 294920 | tf_op jit(solution)/shard_map/ppermute | solution.py:54
  21.0 3.1 %collective-permute-done.8.refs_1_ = bf16[384,128]{1,0:T(8,128)(2,1)S(1)} collective-permute-done((bf16[384,128]{1,0:T(8,128)(2,1)S(1)}, bf16[384,128]{1,0:T(8,128)(2,1)S(1)}, u32[]{:S(2)}, u32[]{:S(2)}) %collective-permute-start.8) | collective-permute-done | bytes 98336 | tf_op jit(solution)/shard_map/ppermute | solution.py:54
  24.1 0.3 shard_map.101
  24.4 0.7 %collective-permute-start.10 = (bf16[256,128]{1,0:T(8,128)(2,1)S(1)}, bf16[256,128]{1,0:T(8,128)(2,1)S(1)}, u32[]{:S(2)}, u32[]{:S(2)}) collective-permute-start(bf16[256,128]{1,0:T(8,128)(2,1)S(1)} %get-tuple-element.29), channel_id=1, source_target_pairs={{0,8},{4,12},{8,0},{12,4},{1,9},{5,13},{9,1},{13,5},{2,10},{6,14},... | collective-permute-start | bytes 196616 | tf_op jit(solution)/shard_map/ppermute | solution.py:43
  25.2 0.2 collective-permute-start.11
  25.3 0.3 %collective-permute-start.9 = (bf16[256,128]{1,0:T(8,128)(2,1)S(1)}, bf16[256,128]{1,0:T(8,128)(2,1)S(1)}, u32[]{:S(2)}, u32[]{:S(2)}) collective-permute-start(bf16[256,128]{1,0:T(8,128)(2,1)S(1)} %get-tuple-element.28), channel_id=1, source_target_pairs={{0,4},{4,8},{8,12},{12,0},{1,5},{5,9},{9,13},{13,1},{2,6},{6,10},{... | collective-permute-start | bytes 196616 | tf_op jit(solution)/shard_map/ppermute | solution.py:43
  25.7 0.7 %shard_map.99 = bf16[128,256]{1,0:T(8,128)(2,1)} custom-call(f32[128,256]{1,0:T(8,128)S(1)} %get-tuple-element.22.pre), custom_call_target="tpu_custom_call" | custom-call | tf_op jit(solution)/shard_map/pallas_call | solution.py:305
  26.3 2.9 %collective-permute-done.10.refs_1_ = bf16[256,128]{1,0:T(8,128)(2,1)S(1)} collective-permute-done((bf16[256,128]{1,0:T(8,128)(2,1)S(1)}, bf16[256,128]{1,0:T(8,128)(2,1)S(1)}, u32[]{:S(2)}, u32[]{:S(2)}) %collective-permute-start.10) | collective-permute-done | bytes 65568 | tf_op jit(solution)/shard_map/ppermute | solution.py:43
  29.2 0.0 collective-permute-done.11.refs_2_
  29.2 0.5 %collective-permute-done.9.refs_0_ = bf16[256,128]{1,0:T(8,128)(2,1)S(1)} collective-permute-done((bf16[256,128]{1,0:T(8,128)(2,1)S(1)}, bf16[256,128]{1,0:T(8,128)(2,1)S(1)}, u32[]{:S(2)}, u32[]{:S(2)}) %collective-permute-start.9) | collective-permute-done | bytes 65568 | tf_op jit(solution)/shard_map/ppermute | solution.py:43
  29.7 0.7 %shard_map.102 = (bf16[128,128]{1,0:T(8,128)(2,1)}, f32[128,256]{1,0:T(8,128)}) custom-call(f32[128,128]{1,0:T(8,128)S(1)} %get-tuple-element.26.own, bf16[128,128]{1,0:T(8,128)(2,1)S(1)} %get-tuple-element.27.kept, bf16[256,128]{1,0:T(8,128)(2,1)S(1)} %collective-permute-done.9.refs_0_, bf16[256,128]{1,0:T(8,128)(2,1)S(1)} %collective-permute-done.10.refs_1_, ...), custom_call_target="tpu_custom_call" | custom-call | tf_op jit(solution)/shard_map/pallas_call | solution.py:317
  (2 shorter events, 0.0 us)
Async XLA Ops:
  0.6 6.6 %copy-start = (bf16[1,1,8,128,128]{4,3,2,1,0:T(8,128)(2,1)S(1)}, bf16[1,1,8,128,128]{4,3,2,1,0:T(8,128)(2,1)}, u32[]{:S(2)}) copy-start(bf16[1,1,8,128,128]{4,3,2,1,0:T(8,128)(2,1)} %vals.1) | copy-start | bytes 786436
  0.6 7.3 %collective-permute-start = (bf16[128,128]{1,0:T(8,128)(2,1)}, bf16[128,128]{1,0:T(8,128)(2,1)S(1)}, u32[]{:S(2)}, u32[]{:S(2)}) collective-permute-start(bf16[128,128]{1,0:T(8,128)(2,1)} %refs_0_.1), channel_id=1, source_target_pairs={{0,12},{4,0},{8,4},{12,8},{1,13},{5,1},{9,5},{13,9},{2,14},{6,2},{... | collective-permute-start | bytes 98312 | tf_op jit(solution)/shard_map/ppermute | solution.py:43
  3.1 4.9 %collective-permute-start.1 = (bf16[128,128]{1,0:T(8,128)(2,1)}, bf16[128,128]{1,0:T(8,128)(2,1)S(1)}, u32[]{:S(2)}, u32[]{:S(2)}) collective-permute-start(bf16[128,128]{1,0:T(8,128)(2,1)} %refs_0_.1), channel_id=1, source_target_pairs={{0,8},{4,12},{8,0},{12,4},{1,9},{5,13},{9,1},{13,5},{2,10},{6,14},... | collective-permute-start | bytes 98312 | tf_op jit(solution)/shard_map/ppermute | solution.py:43
  3.7 4.2 %collective-permute-start.2 = (bf16[128,128]{1,0:T(8,128)(2,1)}, bf16[128,128]{1,0:T(8,128)(2,1)S(1)}, u32[]{:S(2)}, u32[]{:S(2)}) collective-permute-start(bf16[128,128]{1,0:T(8,128)(2,1)} %refs_0_.1), channel_id=1, source_target_pairs={{0,4},{4,8},{8,12},{12,0},{1,5},{5,9},{9,13},{13,1},{2,6},{6,10},{... | collective-permute-start | bytes 98312 | tf_op jit(solution)/shard_map/ppermute | solution.py:43
  3.9 10.0 %collective-permute-start.6 = (bf16[128,256]{1,0:T(8,128)(2,1)}, bf16[128,256]{1,0:T(8,128)(2,1)S(1)}, u32[]{:S(2)}, u32[]{:S(2)}) collective-permute-start(bf16[128,256]{1,0:T(8,128)(2,1)} %refs_6_.1), channel_id=1, source_target_pairs={{0,2},{1,3},{2,0},{3,1},{4,6},{5,7},{6,4},{7,5},{8,10},{9,11},{10,... | collective-permute-start | bytes 196616 | tf_op jit(solution)/shard_map/ppermute | solution.py:54
  6.5 0.7 %copy-start.4 = (s32[1,1,8]{2,1,0:T(1,128)S(1)}, s32[1,1,8]{2,1,0:T(1,128)}, u32[]{:S(2)}) copy-start(s32[1,1,8]{2,1,0:T(1,128)} %rows_in.1) | copy-start | bytes 100
  6.5 0.7 %copy-start.5 = (s32[1,1,8]{2,1,0:T(1,128)S(1)}, s32[1,1,8]{2,1,0:T(1,128)}, u32[]{:S(2)}) copy-start(s32[1,1,8]{2,1,0:T(1,128)} %cols_in.1) | copy-start | bytes 100
  7.2 0.8 %copy-start.3 = (bf16[128,128]{1,0:T(8,128)(2,1)S(1)}, bf16[128,128]{1,0:T(8,128)(2,1)}, u32[]{:S(2)}) copy-start(bf16[128,128]{1,0:T(8,128)(2,1)} %refs_0_.1) | copy-start | bytes 98308
  8.3 5.9 %collective-permute-start.3 = (bf16[256,128]{1,0:T(8,128)(2,1)S(1)}, bf16[256,128]{1,0:T(8,128)(2,1)S(1)}, u32[]{:S(2)}, u32[]{:S(2)}) collective-permute-start(bf16[256,128]{1,0:T(8,128)(2,1)S(1)} %get-tuple-element.19), channel_id=1, source_target_pairs={{0,1},{1,3},{2,0},{3,2},{4,5},{5,7},{6,4},{7,6},{8,9},{9,11},{10,8... | collective-permute-start | bytes 196616 | tf_op jit(solution)/shard_map/ppermute | solution.py:43
  10.0 6.9 %collective-permute-start.4 = (bf16[256,128]{1,0:T(8,128)(2,1)S(1)}, bf16[256,128]{1,0:T(8,128)(2,1)S(1)}, u32[]{:S(2)}, u32[]{:S(2)}) collective-permute-start(bf16[256,128]{1,0:T(8,128)(2,1)S(1)} %get-tuple-element.20), channel_id=1, source_target_pairs={{0,3},{1,2},{2,1},{3,0},{4,7},{5,6},{6,5},{7,4},{8,11},{9,10},{10,... | collective-permute-start | bytes 196616 | tf_op jit(solution)/shard_map/ppermute | solution.py:43
  12.0 5.3 %copy-start.1 = (bf16[128,256]{1,0:T(8,128)(2,1)S(1)}, bf16[128,256]{1,0:T(8,128)(2,1)}, u32[]{:S(2)}) copy-start(bf16[128,256]{1,0:T(8,128)(2,1)} %refs_5_.1) | copy-start | bytes 196612
  12.0 5.3 %copy-start.2 = (bf16[128,256]{1,0:T(8,128)(2,1)S(1)}, bf16[128,256]{1,0:T(8,128)(2,1)}, u32[]{:S(2)}) copy-start(bf16[128,256]{1,0:T(8,128)(2,1)} %refs_6_.1) | copy-start | bytes 196612
  12.0 5.3 %collective-permute-start.5 = (bf16[256,128]{1,0:T(8,128)(2,1)S(1)}, bf16[256,128]{1,0:T(8,128)(2,1)S(1)}, u32[]{:S(2)}, u32[]{:S(2)}) collective-permute-start(bf16[256,128]{1,0:T(8,128)(2,1)S(1)} %get-tuple-element.21), channel_id=1, source_target_pairs={{0,2},{1,0},{2,3},{3,1},{4,6},{5,4},{6,7},{7,5},{8,10},{9,8},{10,1... | collective-permute-start | bytes 196616 | tf_op jit(solution)/shard_map/ppermute | solution.py:43
  17.8 1.3 %collective-permute-start.7 = (bf16[128,128]{1,0:T(8,128)(2,1)S(1)}, bf16[128,128]{1,0:T(8,128)(2,1)S(1)}, u32[]{:S(2)}, u32[]{:S(2)}) collective-permute-start(bf16[128,128]{1,0:T(8,128)(2,1)S(1)} %get-tuple-element.25), channel_id=1, source_target_pairs={{0,4},{4,0},{8,12},{12,8},{1,5},{5,1},{9,13},{13,9},{2,6},{6,2},{1... | collective-permute-start | bytes 98312 | tf_op jit(solution)/shard_map/ppermute | solution.py:54
  19.1 5.1 %collective-permute-start.8 = (bf16[384,128]{1,0:T(8,128)(2,1)S(1)}, bf16[384,128]{1,0:T(8,128)(2,1)S(1)}, u32[]{:S(2)}, u32[]{:S(2)}) collective-permute-start(bf16[384,128]{1,0:T(8,128)(2,1)S(1)} %shard_map.100.refs_0_), channel_id=1, source_target_pairs={{0,1},{1,0},{2,3},{3,2},{4,5},{5,4},{6,7},{7,6},{8,9},{9,8},{10,11... | collective-permute-start | bytes 294920 | tf_op jit(solution)/shard_map/ppermute | solution.py:54
  24.4 4.8 %collective-permute-start.10 = (bf16[256,128]{1,0:T(8,128)(2,1)S(1)}, bf16[256,128]{1,0:T(8,128)(2,1)S(1)}, u32[]{:S(2)}, u32[]{:S(2)}) collective-permute-start(bf16[256,128]{1,0:T(8,128)(2,1)S(1)} %get-tuple-element.29), channel_id=1, source_target_pairs={{0,8},{4,12},{8,0},{12,4},{1,9},{5,13},{9,1},{13,5},{2,10},{6,14},... | collective-permute-start | bytes 196616 | tf_op jit(solution)/shard_map/ppermute | solution.py:43
  25.2 4.1 %collective-permute-start.11 = (bf16[256,128]{1,0:T(8,128)(2,1)S(1)}, bf16[256,128]{1,0:T(8,128)(2,1)S(1)}, u32[]{:S(2)}, u32[]{:S(2)}) collective-permute-start(bf16[256,128]{1,0:T(8,128)(2,1)S(1)} %get-tuple-element.30), channel_id=1, source_target_pairs={{0,12},{4,0},{8,4},{12,8},{1,13},{5,1},{9,5},{13,9},{2,14},{6,2},{... | collective-permute-start | bytes 196616 | tf_op jit(solution)/shard_map/ppermute | solution.py:43
  25.3 4.4 %collective-permute-start.9 = (bf16[256,128]{1,0:T(8,128)(2,1)S(1)}, bf16[256,128]{1,0:T(8,128)(2,1)S(1)}, u32[]{:S(2)}, u32[]{:S(2)}) collective-permute-start(bf16[256,128]{1,0:T(8,128)(2,1)S(1)} %get-tuple-element.28), channel_id=1, source_target_pairs={{0,4},{4,8},{8,12},{12,0},{1,5},{5,9},{9,13},{13,1},{2,6},{6,10},{... | collective-permute-start | bytes 196616 | tf_op jit(solution)/shard_map/ppermute | solution.py:43

commit v17 on v16

--- a/solution.py
+++ b/solution.py
@@ -49,6 +49,10 @@
     return lax.rem(lax.axis_index("row"), 2) == 1
 
 
+def start_order(n):
+    return [*range(2, n), 1]
+
+
 def swap(value, axis, distance):
     n = lax.axis_size(axis)
     return lax.ppermute(value, axis, [(s, s ^ distance) for s in range(n)])
@@ -82,18 +86,18 @@
     for copy in copies:
         copy.wait()
 
-    def ahead(there, axis):
-        n = lax.axis_size(axis)
-        return lax.rem(ring_place(there, axis) - ring_place(lax.axis_index(axis), axis) + n, n)
+    def ahead(there):
+        n, here = lax.axis_size("col"), lax.axis_index("col")
+        return lax.rem(ring_place(there, "col") - ring_place(here, "col") + n, n)
 
     def add(t, _):
         row, col = rows[0, 0, t], cols[0, 0, t]
         if paired:
             place = lax.rem((row // piece) ^ lax.axis_index("col"), 2) * 2 + row // piece // 2
         else:
-            place = ahead(row // piece, "col")
+            place = ahead(row // piece)
         row = place * piece + lax.rem(row, piece)
-        col = ahead(col // piece, "row") * piece + lax.rem(col, piece)
+        col = ((col // piece) ^ lax.axis_index("row")) * piece + lax.rem(col, piece)
         down = pl.ds(pl.multiple_of(row * side, side), side)
         across = pl.ds(pl.multiple_of(col * side, side), side)
         near[down, across] = vals[0, 0, t]
@@ -118,11 +122,16 @@
     return terms[0]
 
 
+def stack(operands):
+    own, *others = [operand[...] for operand in operands]
+    order = start_order(len(operands))
+    return jnp.concatenate([own] + [others[order.index(d)] for d in range(1, len(operands))], axis=0)
+
+
 def forward_kernel(n, matrix, *refs):
     operands, own, sends = refs[:n], refs[n], refs[n + 1 :]
     rows = own.shape[0]
-    stacked = jnp.concatenate([operand[...] for operand in operands], axis=0)
-    product = dot(matrix[...], stacked)
+    product = dot(matrix[...], stack(operands))
     own[...] = product[:rows]
     for d, send in enumerate(sends, 1):
         send[...] = product[d * rows : (d + 1) * rows].astype(send.dtype)
@@ -164,8 +173,7 @@
 
 def paired_forward_kernel(n, matrix, *refs):
     operands, (own, first, second, third) = refs[:n], refs[n:]
-    stacked = jnp.concatenate([operand[...] for operand in operands], axis=0)
-    product = dot(matrix[...], stacked).astype(own.dtype)
+    product = dot(matrix[...], stack(operands)).astype(own.dtype)
     rows = own.shape[0]
     same, other = product[:rows], product[rows:]
     middle = in_middle()
@@ -238,7 +246,7 @@
     dense_bytes = 2 * down * across
 
     paired = n_col == 4
-    gathered = exchange([features] * (n_row - 1), "row", False)
+    gathered = [swap(features, "row", d) for d in start_order(n_row)]
     (blank,) = call(zero_kernel, [((down, across), NARROW)], [], need=dense_bytes)()
     (near,) = call(
         functools.partial(dense_kernel, nodes // side, paired),
@@ -311,7 +319,7 @@
         [VMEM] * (2 + len(spread)),
         **forward,
     )(far, sent, *spread)
-    parts = exchange(sends, "row", True)
+    parts = [swap(send, "row", d) for d, send in enumerate(sends, 1)]
 
     scale = float(nodes * n_row * n_col) ** -0.5
     grad_features, grad_weight = call(

time: 30.6 us -> 30.9 us (level)
    ppermute x3 -> x9, starting transfers between devices: 4.6 us -> 10 us  [swap(): return lax.ppermute(value, axis, [(s, s ^ distance) for s in range(n)])]
    ppermute x9 -> x3, starting transfers between devices: 9.71 us -> 4.57 us  [exchange(): lax.ppermute(send, axis, [(s, target(s, d)) for s in range(n)])]
    ppermute x9 -> x3, waiting for transfers between devices: 6.79 us -> 3.59 us  [exchange(): lax.ppermute(send, axis, [(s, target(s, d)) for s in range(n)])]
    ppermute x3 -> x9, waiting for transfers between devices: 4.32 us -> 7.48 us  [swap(): return lax.ppermute(value, axis, [(s, s ^ distance) for s in range(n)])]
  transfers between devices with their start and end apart: 12 -> 12, of which waited for: 7 -> 5; matrix products, arithmetic and copies ran while one was open for 0% -> 0% of each run, Pallas kernels for 7% -> 6%
where the time goes in v17:
time: 30.9 us; the launch traced here: 30.7 us
  starting transfers between devices  14.6 us (47%)
  waiting for transfers between devices  11.1 us (36%)
  Pallas kernels  3.47 us (11%)
  between operations  1.45 us (5%)
    ppermute x9, starting transfers between devices, swap(): return lax.ppermute(value, axis, [(s, s ^ distance) for s in range(n)])  10 us
    ppermute x9, waiting for transfers between devices, swap(): return lax.ppermute(value, axis, [(s, s ^ distance) for s in range(n)])  7.48 us
    ppermute x3, starting transfers between devices, exchange(): lax.ppermute(send, axis, [(s, target(s, d)) for s in range(n)])  4.57 us
    ppermute x3, waiting for transfers between devices, exchange(): lax.ppermute(send, axis, [(s, target(s, d)) for s in range(n)])  3.59 us
    pallas_call x1, Pallas kernels, per_device(): call(functools.partial(last_kernel, scale), [((nodes, width), NARROW), ((...  0.7 us
    pallas_call x1, Pallas kernels, per_device(): act, = call(act_kernel, [((nodes, hidden), NARROW)], [VMEM])(pre)  0.65 us
    pallas_call x1, Pallas kernels, per_device(): call(functools.partial(dense_kernel, nodes // side, paired), [((down, acr...  0.64 us
  transfers between devices with their start and end apart: 12, of which 5 were waited for; matrix products, arithmetic and copies ran while one was open for 0% of the time, Pallas kernels for 6%

profile of v17, /device:TPU:0, one launch (start us, length us, event | category | flops | bytes accessed | tf_op | source)
XLA Modules:
  0.0 30.7 jit_solution(9560257164259930013)
XLA Ops:
  0.6 0.0 copy-start
  0.6 3.0 %collective-permute-start = (bf16[128,128]{1,0:T(8,128)(2,1)}, bf16[128,128]{1,0:T(8,128)(2,1)S(1)}, u32[]{:S(2)}, u32[]{:S(2)}) collective-permute-start(bf16[128,128]{1,0:T(8,128)(2,1)} %refs_0_.1), channel_id=1, source_target_pairs={{0,8},{4,12},{8,0},{12,4},{1,9},{5,13},{9,1},{13,5},{2,10},{6,14},... | collective-permute-start | bytes 98312 | tf_op jit(solution)/shard_map/ppermute | solution.py:58
  3.6 0.0 collective-permute-start.1
  3.6 0.2 collective-permute-start.2
  3.8 3.0 %collective-permute-start.6 = (bf16[128,256]{1,0:T(8,128)(2,1)}, bf16[128,256]{1,0:T(8,128)(2,1)S(1)}, u32[]{:S(2)}, u32[]{:S(2)}) collective-permute-start(bf16[128,256]{1,0:T(8,128)(2,1)} %refs_6_.1), channel_id=1, source_target_pairs={{0,2},{1,3},{2,0},{3,1},{4,6},{5,7},{6,4},{7,5},{8,10},{9,11},{10,... | collective-permute-start | bytes 196616 | tf_op jit(solution)/shard_map/ppermute | solution.py:58
  6.9 0.0 copy-start.4
  6.9 0.0 copy-start.5
  7.6 0.0 copy-done
  7.6 0.0 copy-done.4
  7.6 0.0 copy-done.5
  7.6 0.0 copy-start.3
  7.7 0.6 %shard_map.95.near.matrix = bf16[512,512]{1,0:T(8,128)(2,1)S(1)} custom-call(bf16[512,512]{1,0:T(8,128)(2,1)S(1)} %shard_map.94.blank, bf16[1,1,8,128,128]{4,3,2,1,0:T(8,128)(2,1)S(1)} %copy-done, s32[1,1,8]{2,1,0:T(1,128)S(1)} %copy-done.4, s32[1,1,8]{2,1,0:T(1,128)S(1)} %copy-done.5, s32[1,1]{1,0:T(1,128)S(6)} %copy.12.count_in), custom_call_target="tpu_custom_call", output_to_operand_aliasing={{}: (0, {})} | custom-call | bytes 1048576 | tf_op jit(solution)/shard_map/pallas_call | solution.py:251
  8.3 0.0 collective-permute-done.refs_1_
  8.3 0.0 collective-permute-done.1.refs_2_
  8.3 0.0 collective-permute-done.2.refs_3_
  8.3 0.1 copy-done.3
  8.4 0.3 shard_map.97
  8.7 1.6 %collective-permute-start.3 = (bf16[256,128]{1,0:T(8,128)(2,1)S(1)}, bf16[256,128]{1,0:T(8,128)(2,1)S(1)}, u32[]{:S(2)}, u32[]{:S(2)}) collective-permute-start(bf16[256,128]{1,0:T(8,128)(2,1)S(1)} %get-tuple-element.19), channel_id=1, source_target_pairs={{0,1},{1,3},{2,0},{3,2},{4,5},{5,7},{6,4},{7,6},{8,9},{9,11},{10,8... | collective-permute-start | bytes 196616 | tf_op jit(solution)/shard_map/ppermute | solution.py:43
  10.3 1.4 %collective-permute-start.4 = (bf16[256,128]{1,0:T(8,128)(2,1)S(1)}, bf16[256,128]{1,0:T(8,128)(2,1)S(1)}, u32[]{:S(2)}, u32[]{:S(2)}) collective-permute-start(bf16[256,128]{1,0:T(8,128)(2,1)S(1)} %get-tuple-element.20), channel_id=1, source_target_pairs={{0,3},{1,2},{2,1},{3,0},{4,7},{5,6},{6,5},{7,4},{8,11},{9,10},{10,... | collective-permute-start | bytes 196616 | tf_op jit(solution)/shard_map/ppermute | solution.py:43
  11.7 0.0 copy-start.1
  11.7 0.0 copy-start.2
  11.7 1.6 %collective-permute-start.5 = (bf16[256,128]{1,0:T(8,128)(2,1)S(1)}, bf16[256,128]{1,0:T(8,128)(2,1)S(1)}, u32[]{:S(2)}, u32[]{:S(2)}) collective-permute-start(bf16[256,128]{1,0:T(8,128)(2,1)S(1)} %get-tuple-element.21), channel_id=1, source_target_pairs={{0,2},{1,0},{2,3},{3,1},{4,6},{5,4},{6,7},{7,5},{8,10},{9,8},{10,1... | collective-permute-start | bytes 196616 | tf_op jit(solution)/shard_map/ppermute | solution.py:43
  13.3 0.3 %shard_map.96.refs_0_.matrix = bf16[512,512]{1,0:T(8,128)(2,1)S(1)} custom-call(bf16[512,512]{1,0:T(8,128)(2,1)S(1)} %shard_map.95.near.matrix), custom_call_target="tpu_custom_call" | custom-call | bytes 1572864 | tf_op jit(solution)/shard_map/pallas_call | solution.py:285
  13.6 0.0 collective-permute-done.6.refs_7_
  13.6 3.6 %collective-permute-done.3.refs_2_ = bf16[256,128]{1,0:T(8,128)(2,1)S(1)} collective-permute-done((bf16[256,128]{1,0:T(8,128)(2,1)S(1)}, bf16[256,128]{1,0:T(8,128)(2,1)S(1)}, u32[]{:S(2)}, u32[]{:S(2)}) %collective-permute-start.3) | collective-permute-done | bytes 65568 | tf_op jit(solution)/shard_map/ppermute | solution.py:43
  17.2 0.0 collective-permute-done.4.refs_3_
  17.2 0.0 collective-permute-done.5.refs_4_
  17.2 0.0 copy-done.1
  17.2 0.0 copy-done.2
  17.2 0.5 %shard_map.98 = (bf16[256,128]{1,0:T(8,128)(2,1)S(1)}, f32[128,128]{1,0:T(8,128)S(1)}, bf16[128,128]{1,0:T(8,128)(2,1)S(1)}, f32[128,256]{1,0:T(8,128)S(1)}) custom-call(bf16[512,512]{1,0:T(8,128)(2,1)S(1)} %shard_map.96.refs_0_.matrix, bf16[256,128]{1,0:T(8,128)(2,1)S(1)} %get-tuple-element.18.refs_1_, bf16[256,128]{1,0:T(8,128)(2,1)S(1)} %collective-permute-done.3.refs_2_, ...), custom_call_target="tpu_custom_call" | custom-call | flops 117440512 | tf_op jit(solution)/shard_map/pallas_call | solution.py:294
  17.8 0.1 collective-permute-start.7
  17.8 1.2 %collective-permute-done.7.came = bf16[128,128]{1,0:T(8,128)(2,1)S(1)} collective-permute-done((bf16[128,128]{1,0:T(8,128)(2,1)S(1)}, bf16[128,128]{1,0:T(8,128)(2,1)S(1)}, u32[]{:S(2)}, u32[]{:S(2)}) %collective-permute-start.7) | collective-permute-done | bytes 32800 | tf_op jit(solution)/shard_map/ppermute | solution.py:58
  19.0 1.5 %collective-permute-start.8 = (bf16[384,128]{1,0:T(8,128)(2,1)S(1)}, bf16[384,128]{1,0:T(8,128)(2,1)S(1)}, u32[]{:S(2)}, u32[]{:S(2)}) collective-permute-start(bf16[384,128]{1,0:T(8,128)(2,1)S(1)} %shard_map.100.refs_0_), channel_id=1, source_target_pairs={{0,1},{1,0},{2,3},{3,2},{4,5},{5,4},{6,7},{7,6},{8,9},{9,8},{10,11... | collective-permute-start | bytes 294920 | tf_op jit(solution)/shard_map/ppermute | solution.py:58
  20.6 3.4 %collective-permute-done.8.refs_1_ = bf16[384,128]{1,0:T(8,128)(2,1)S(1)} collective-permute-done((bf16[384,128]{1,0:T(8,128)(2,1)S(1)}, bf16[384,128]{1,0:T(8,128)(2,1)S(1)}, u32[]{:S(2)}, u32[]{:S(2)}) %collective-permute-start.8) | collective-permute-done | bytes 98336 | tf_op jit(solution)/shard_map/ppermute | solution.py:58
  24.0 0.3 shard_map.101
  24.3 1.6 %collective-permute-start.10 = (bf16[256,128]{1,0:T(8,128)(2,1)S(1)}, bf16[256,128]{1,0:T(8,128)(2,1)S(1)}, u32[]{:S(2)}, u32[]{:S(2)}) collective-permute-start(bf16[256,128]{1,0:T(8,128)(2,1)S(1)} %get-tuple-element.29), channel_id=1, source_target_pairs={{0,8},{4,12},{8,0},{12,4},{1,9},{5,13},{9,1},{13,5},{2,10},{6,14},... | collective-permute-start | bytes 196616 | tf_op jit(solution)/shard_map/ppermute | solution.py:58
  25.9 0.0 collective-permute-start.11
  25.9 0.6 %collective-permute-start.9 = (bf16[256,128]{1,0:T(8,128)(2,1)S(1)}, bf16[256,128]{1,0:T(8,128)(2,1)S(1)}, u32[]{:S(2)}, u32[]{:S(2)}) collective-permute-start(bf16[256,128]{1,0:T(8,128)(2,1)S(1)} %get-tuple-element.28), channel_id=1, source_target_pairs={{0,4},{4,0},{8,12},{12,8},{1,5},{5,1},{9,13},{13,9},{2,6},{6,2},{1... | collective-permute-start | bytes 196616 | tf_op jit(solution)/shard_map/ppermute | solution.py:58
  26.5 0.7 %shard_map.99 = bf16[128,256]{1,0:T(8,128)(2,1)} custom-call(f32[128,256]{1,0:T(8,128)S(1)} %get-tuple-element.22.pre), custom_call_target="tpu_custom_call" | custom-call | tf_op jit(solution)/shard_map/pallas_call | solution.py:313
  27.1 1.5 %collective-permute-done.10.refs_1_ = bf16[256,128]{1,0:T(8,128)(2,1)S(1)} collective-permute-done((bf16[256,128]{1,0:T(8,128)(2,1)S(1)}, bf16[256,128]{1,0:T(8,128)(2,1)S(1)}, u32[]{:S(2)}, u32[]{:S(2)}) %collective-permute-start.10) | collective-permute-done | bytes 65568 | tf_op jit(solution)/shard_map/ppermute | solution.py:58
  28.6 1.4 %collective-permute-done.11.refs_2_ = bf16[256,128]{1,0:T(8,128)(2,1)S(1)} collective-permute-done((bf16[256,128]{1,0:T(8,128)(2,1)S(1)}, bf16[256,128]{1,0:T(8,128)(2,1)S(1)}, u32[]{:S(2)}, u32[]{:S(2)}) %collective-permute-start.11) | collective-permute-done | bytes 65568 | tf_op jit(solution)/shard_map/ppermute | solution.py:58
  30.0 0.0 collective-permute-done.9.refs_0_
  30.0 0.7 %shard_map.102 = (bf16[128,128]{1,0:T(8,128)(2,1)}, f32[128,256]{1,0:T(8,128)}) custom-call(f32[128,128]{1,0:T(8,128)S(1)} %get-tuple-element.26.own, bf16[128,128]{1,0:T(8,128)(2,1)S(1)} %get-tuple-element.27.kept, bf16[256,128]{1,0:T(8,128)(2,1)S(1)} %collective-permute-done.9.refs_0_, bf16[256,128]{1,0:T(8,128)(2,1)S(1)} %collective-permute-done.10.refs_1_, ...), custom_call_target="tpu_custom_call" | custom-call | tf_op jit(solution)/shard_map/pallas_call | solution.py:325
  (2 shorter events, 0.0 us)
Async XLA Ops:
  0.6 7.0 %copy-start = (bf16[1,1,8,128,128]{4,3,2,1,0:T(8,128)(2,1)S(1)}, bf16[1,1,8,128,128]{4,3,2,1,0:T(8,128)(2,1)}, u32[]{:S(2)}) copy-start(bf16[1,1,8,128,128]{4,3,2,1,0:T(8,128)(2,1)} %vals.1) | copy-start | bytes 786436
  0.6 7.7 %collective-permute-start = (bf16[128,128]{1,0:T(8,128)(2,1)}, bf16[128,128]{1,0:T(8,128)(2,1)S(1)}, u32[]{:S(2)}, u32[]{:S(2)}) collective-permute-start(bf16[128,128]{1,0:T(8,128)(2,1)} %refs_0_.1), channel_id=1, source_target_pairs={{0,8},{4,12},{8,0},{12,4},{1,9},{5,13},{9,1},{13,5},{2,10},{6,14},... | collective-permute-start | bytes 98312 | tf_op jit(solution)/shard_map/ppermute | solution.py:58
  3.6 4.7 %collective-permute-start.1 = (bf16[128,128]{1,0:T(8,128)(2,1)}, bf16[128,128]{1,0:T(8,128)(2,1)S(1)}, u32[]{:S(2)}, u32[]{:S(2)}) collective-permute-start(bf16[128,128]{1,0:T(8,128)(2,1)} %refs_0_.1), channel_id=1, source_target_pairs={{0,12},{4,8},{8,4},{12,0},{1,13},{5,9},{9,5},{13,1},{2,14},{6,10},... | collective-permute-start | bytes 98312 | tf_op jit(solution)/shard_map/ppermute | solution.py:58
  3.6 4.7 %collective-permute-start.2 = (bf16[128,128]{1,0:T(8,128)(2,1)}, bf16[128,128]{1,0:T(8,128)(2,1)S(1)}, u32[]{:S(2)}, u32[]{:S(2)}) collective-permute-start(bf16[128,128]{1,0:T(8,128)(2,1)} %refs_0_.1), channel_id=1, source_target_pairs={{0,4},{4,0},{8,12},{12,8},{1,5},{5,1},{9,13},{13,9},{2,6},{6,2},{1... | collective-permute-start | bytes 98312 | tf_op jit(solution)/shard_map/ppermute | solution.py:58
  3.8 9.8 %collective-permute-start.6 = (bf16[128,256]{1,0:T(8,128)(2,1)}, bf16[128,256]{1,0:T(8,128)(2,1)S(1)}, u32[]{:S(2)}, u32[]{:S(2)}) collective-permute-start(bf16[128,256]{1,0:T(8,128)(2,1)} %refs_6_.1), channel_id=1, source_target_pairs={{0,2},{1,3},{2,0},{3,1},{4,6},{5,7},{6,4},{7,5},{8,10},{9,11},{10,... | collective-permute-start | bytes 196616 | tf_op jit(solution)/shard_map/ppermute | solution.py:58
  6.9 0.7 %copy-start.4 = (s32[1,1,8]{2,1,0:T(1,128)S(1)}, s32[1,1,8]{2,1,0:T(1,128)}, u32[]{:S(2)}) copy-start(s32[1,1,8]{2,1,0:T(1,128)} %rows_in.1) | copy-start | bytes 100
  6.9 0.7 %copy-start.5 = (s32[1,1,8]{2,1,0:T(1,128)S(1)}, s32[1,1,8]{2,1,0:T(1,128)}, u32[]{:S(2)}) copy-start(s32[1,1,8]{2,1,0:T(1,128)} %cols_in.1) | copy-start | bytes 100
  7.6 0.8 %copy-start.3 = (bf16[128,128]{1,0:T(8,128)(2,1)S(1)}, bf16[128,128]{1,0:T(8,128)(2,1)}, u32[]{:S(2)}) copy-start(bf16[128,128]{1,0:T(8,128)(2,1)} %refs_0_.1) | copy-start | bytes 98308
  8.7 8.5 %collective-permute-start.3 = (bf16[256,128]{1,0:T(8,128)(2,1)S(1)}, bf16[256,128]{1,0:T(8,128)(2,1)S(1)}, u32[]{:S(2)}, u32[]{:S(2)}) collective-permute-start(bf16[256,128]{1,0:T(8,128)(2,1)S(1)} %get-tuple-element.19), channel_id=1, source_target_pairs={{0,1},{1,3},{2,0},{3,2},{4,5},{5,7},{6,4},{7,6},{8,9},{9,11},{10,8... | collective-permute-start | bytes 196616 | tf_op jit(solution)/shard_map/ppermute | solution.py:43
  10.3 6.9 %collective-permute-start.4 = (bf16[256,128]{1,0:T(8,128)(2,1)S(1)}, bf16[256,128]{1,0:T(8,128)(2,1)S(1)}, u32[]{:S(2)}, u32[]{:S(2)}) collective-permute-start(bf16[256,128]{1,0:T(8,128)(2,1)S(1)} %get-tuple-element.20), channel_id=1, source_target_pairs={{0,3},{1,2},{2,1},{3,0},{4,7},{5,6},{6,5},{7,4},{8,11},{9,10},{10,... | collective-permute-start | bytes 196616 | tf_op jit(solution)/shard_map/ppermute | solution.py:43
  11.7 5.5 %copy-start.1 = (bf16[128,256]{1,0:T(8,128)(2,1)S(1)}, bf16[128,256]{1,0:T(8,128)(2,1)}, u32[]{:S(2)}) copy-start(bf16[128,256]{1,0:T(8,128)(2,1)} %refs_5_.1) | copy-start | bytes 196612
  11.7 5.5 %copy-start.2 = (bf16[128,256]{1,0:T(8,128)(2,1)S(1)}, bf16[128,256]{1,0:T(8,128)(2,1)}, u32[]{:S(2)}) copy-start(bf16[128,256]{1,0:T(8,128)(2,1)} %refs_6_.1) | copy-start | bytes 196612
  11.7 5.5 %collective-permute-start.5 = (bf16[256,128]{1,0:T(8,128)(2,1)S(1)}, bf16[256,128]{1,0:T(8,128)(2,1)S(1)}, u32[]{:S(2)}, u32[]{:S(2)}) collective-permute-start(bf16[256,128]{1,0:T(8,128)(2,1)S(1)} %get-tuple-element.21), channel_id=1, source_target_pairs={{0,2},{1,0},{2,3},{3,1},{4,6},{5,4},{6,7},{7,5},{8,10},{9,8},{10,1... | collective-permute-start | bytes 196616 | tf_op jit(solution)/shard_map/ppermute | solution.py:43
  17.8 1.3 %collective-permute-start.7 = (bf16[128,128]{1,0:T(8,128)(2,1)S(1)}, bf16[128,128]{1,0:T(8,128)(2,1)S(1)}, u32[]{:S(2)}, u32[]{:S(2)}) collective-permute-start(bf16[128,128]{1,0:T(8,128)(2,1)S(1)} %get-tuple-element.25), channel_id=1, source_target_pairs={{0,4},{4,0},{8,12},{12,8},{1,5},{5,1},{9,13},{13,9},{2,6},{6,2},{1... | collective-permute-start | bytes 98312 | tf_op jit(solution)/shard_map/ppermute | solution.py:58
  19.0 4.9 %collective-permute-start.8 = (bf16[384,128]{1,0:T(8,128)(2,1)S(1)}, bf16[384,128]{1,0:T(8,128)(2,1)S(1)}, u32[]{:S(2)}, u32[]{:S(2)}) collective-permute-start(bf16[384,128]{1,0:T(8,128)(2,1)S(1)} %shard_map.100.refs_0_), channel_id=1, source_target_pairs={{0,1},{1,0},{2,3},{3,2},{4,5},{5,4},{6,7},{7,6},{8,9},{9,8},{10,11... | collective-permute-start | bytes 294920 | tf_op jit(solution)/shard_map/ppermute | solution.py:58
  24.3 4.3 %collective-permute-start.10 = (bf16[256,128]{1,0:T(8,128)(2,1)S(1)}, bf16[256,128]{1,0:T(8,128)(2,1)S(1)}, u32[]{:S(2)}, u32[]{:S(2)}) collective-permute-start(bf16[256,128]{1,0:T(8,128)(2,1)S(1)} %get-tuple-element.29), channel_id=1, source_target_pairs={{0,8},{4,12},{8,0},{12,4},{1,9},{5,13},{9,1},{13,5},{2,10},{6,14},... | collective-permute-start | bytes 196616 | tf_op jit(solution)/shard_map/ppermute | solution.py:58
  25.9 4.2 %collective-permute-start.11 = (bf16[256,128]{1,0:T(8,128)(2,1)S(1)}, bf16[256,128]{1,0:T(8,128)(2,1)S(1)}, u32[]{:S(2)}, u32[]{:S(2)}) collective-permute-start(bf16[256,128]{1,0:T(8,128)(2,1)S(1)} %get-tuple-element.30), channel_id=1, source_target_pairs={{0,12},{4,8},{8,4},{12,0},{1,13},{5,9},{9,5},{13,1},{2,14},{6,10},... | collective-permute-start | bytes 196616 | tf_op jit(solution)/shard_map/ppermute | solution.py:58
  25.9 4.2 %collective-permute-start.9 = (bf16[256,128]{1,0:T(8,128)(2,1)S(1)}, bf16[256,128]{1,0:T(8,128)(2,1)S(1)}, u32[]{:S(2)}, u32[]{:S(2)}) collective-permute-start(bf16[256,128]{1,0:T(8,128)(2,1)S(1)} %get-tuple-element.28), channel_id=1, source_target_pairs={{0,4},{4,0},{8,12},{12,8},{1,5},{5,1},{9,13},{13,9},{2,6},{6,2},{1... | collective-permute-start | bytes 196616 | tf_op jit(solution)/shard_map/ppermute | solution.py:58

commit v18 on v17

--- a/solution.py
+++ b/solution.py
@@ -212,15 +212,17 @@
 
 
 def backward_kernel(n, matrix, *refs):
-    messages, own, kept, sends = refs[:n], refs[n], refs[n + 1], refs[n + 2 :]
+    messages, own, kept, sends, product = refs[:n], refs[n], refs[n + 1], refs[n + 2 : -1], refs[-1]
     rows, backs = own.shape[0], messages[0].shape[0] - kept.shape[0]
     stacked = jnp.concatenate([message[:backs] for message in messages], axis=0)
-    product = dot(matrix[...], stacked)
+    product[...] = dot(matrix[...], stacked)
     own[...] = product[:rows]
     term = tree([wide(message[backs:]) for message in messages]).astype(kept.dtype)
     kept[...] = term
+    here, size = lax.axis_index("row"), lax.axis_size("row")
     for d, send in enumerate(sends, 1):
-        send[:rows] = product[d * rows : (d + 1) * rows].astype(send.dtype)
+        start = pl.multiple_of((lax.rem(here + d, size) ^ here) * rows, rows)
+        send[:rows] = product[pl.ds(start, rows)].astype(send.dtype)
         send[rows:] = term
 
 
@@ -317,9 +319,10 @@
         functools.partial(backward_kernel, 1 + len(spread)),
         [((nodes, width), jnp.float32), (square, NARROW)] + [message] * (n_row - 1),
         [VMEM] * (2 + len(spread)),
+        scratch=[pltpu.VMEM((across, width), jnp.float32)],
         **forward,
     )(far, sent, *spread)
-    parts = [swap(send, "row", d) for d, send in enumerate(sends, 1)]
+    parts = exchange(sends, "row", True)
 
     scale = float(nodes * n_row * n_col) ** -0.5
     grad_features, grad_weight = call(

time: 30.9 us -> 30.9 us (level)
    ppermute x3 -> x6, waiting for transfers between devices: 3.59 us -> 6.58 us  [exchange(): lax.ppermute(send, axis, [(s, target(s, d)) for s in range(n)])]
    ppermute x9 -> x6, waiting for transfers between devices: 7.48 us -> 4.61 us  [swap(): return lax.ppermute(value, axis, [(s, s ^ distance) for s in range(n)])]
    ppermute x9 -> x6, starting transfers between devices: 10 us -> 7.83 us  [swap(): return lax.ppermute(value, axis, [(s, s ^ distance) for s in range(n)])]
    ppermute x3 -> x6, starting transfers between devices: 4.57 us -> 6.66 us  [exchange(): lax.ppermute(send, axis, [(s, target(s, d)) for s in range(n)])]
  transfers between devices with their start and end apart: 12 -> 12, of which waited for: 5 -> 6; matrix products, arithmetic and copies ran while one was open for 0% -> 0% of each run, Pallas kernels for 6% -> 6%
where the time goes in v18:
time: 30.9 us; the launch traced here: 30.7 us
  starting transfers between devices  14.5 us (47%)
  waiting for transfers between devices  11.2 us (36%)
  Pallas kernels  3.48 us (11%)
  between operations  1.45 us (5%)
    ppermute x6, starting transfers between devices, swap(): return lax.ppermute(value, axis, [(s, s ^ distance) for s in range(n)])  7.83 us
    ppermute x6, starting transfers between devices, exchange(): lax.ppermute(send, axis, [(s, target(s, d)) for s in range(n)])  6.66 us
    ppermute x6, waiting for transfers between devices, exchange(): lax.ppermute(send, axis, [(s, target(s, d)) for s in range(n)])  6.58 us
    ppermute x6, waiting for transfers between devices, swap(): return lax.ppermute(value, axis, [(s, s ^ distance) for s in range(n)])  4.61 us
    pallas_call x1, Pallas kernels, per_device(): call(functools.partial(last_kernel, scale), [((nodes, width), NARROW), ((...  0.69 us
    pallas_call x1, Pallas kernels, per_device(): act, = call(act_kernel, [((nodes, hidden), NARROW)], [VMEM])(pre)  0.65 us
    pallas_call x1, Pallas kernels, per_device(): call(functools.partial(dense_kernel, nodes // side, paired), [((down, acr...  0.64 us
  transfers between devices with their start and end apart: 12, of which 6 were waited for; matrix products, arithmetic and copies ran while one was open for 0% of the time, Pallas kernels for 6%

profile of v18, /device:TPU:0, one launch (start us, length us, event | category | flops | bytes accessed | tf_op | source)
XLA Modules:
  0.0 30.7 jit_solution(439482028397185088)
XLA Ops:
  0.6 0.0 copy-start
  0.6 3.0 %collective-permute-start = (bf16[128,128]{1,0:T(8,128)(2,1)}, bf16[128,128]{1,0:T(8,128)(2,1)S(1)}, u32[]{:S(2)}, u32[]{:S(2)}) collective-permute-start(bf16[128,128]{1,0:T(8,128)(2,1)} %refs_0_.1), channel_id=1, source_target_pairs={{0,8},{4,12},{8,0},{12,4},{1,9},{5,13},{9,1},{13,5},{2,10},{6,14},... | collective-permute-start | bytes 98312 | tf_op jit(solution)/shard_map/ppermute | solution.py:58
  3.6 0.0 collective-permute-start.1
  3.6 0.2 collective-permute-start.2
  3.8 3.0 %collective-permute-start.6 = (bf16[128,256]{1,0:T(8,128)(2,1)}, bf16[128,256]{1,0:T(8,128)(2,1)S(1)}, u32[]{:S(2)}, u32[]{:S(2)}) collective-permute-start(bf16[128,256]{1,0:T(8,128)(2,1)} %refs_6_.1), channel_id=1, source_target_pairs={{0,2},{1,3},{2,0},{3,1},{4,6},{5,7},{6,4},{7,5},{8,10},{9,11},{10,... | collective-permute-start | bytes 196616 | tf_op jit(solution)/shard_map/ppermute | solution.py:58
  6.9 0.0 copy-start.4
  6.9 0.0 copy-start.5
  7.6 0.0 copy-done
  7.6 0.0 copy-done.4
  7.6 0.0 copy-done.5
  7.6 0.0 copy-start.3
  7.7 0.6 %shard_map.95.near.matrix = bf16[512,512]{1,0:T(8,128)(2,1)S(1)} custom-call(bf16[512,512]{1,0:T(8,128)(2,1)S(1)} %shard_map.94.blank, bf16[1,1,8,128,128]{4,3,2,1,0:T(8,128)(2,1)S(1)} %copy-done, s32[1,1,8]{2,1,0:T(1,128)S(1)} %copy-done.4, s32[1,1,8]{2,1,0:T(1,128)S(1)} %copy-done.5, s32[1,1]{1,0:T(1,128)S(6)} %copy.12.count_in), custom_call_target="tpu_custom_call", output_to_operand_aliasing={{}: (0, {})} | custom-call | bytes 1048576 | tf_op jit(solution)/shard_map/pallas_call | solution.py:253
  8.3 0.0 collective-permute-done.refs_1_
  8.3 0.0 collective-permute-done.1.refs_2_
  8.3 0.0 collective-permute-done.2.refs_3_
  8.3 0.1 copy-done.3
  8.4 0.3 shard_map.97
  8.7 1.6 %collective-permute-start.3 = (bf16[256,128]{1,0:T(8,128)(2,1)S(1)}, bf16[256,128]{1,0:T(8,128)(2,1)S(1)}, u32[]{:S(2)}, u32[]{:S(2)}) collective-permute-start(bf16[256,128]{1,0:T(8,128)(2,1)S(1)} %get-tuple-element.19), channel_id=1, source_target_pairs={{0,1},{1,3},{2,0},{3,2},{4,5},{5,7},{6,4},{7,6},{8,9},{9,11},{10,8... | collective-permute-start | bytes 196616 | tf_op jit(solution)/shard_map/ppermute | solution.py:43
  10.3 1.4 %collective-permute-start.4 = (bf16[256,128]{1,0:T(8,128)(2,1)S(1)}, bf16[256,128]{1,0:T(8,128)(2,1)S(1)}, u32[]{:S(2)}, u32[]{:S(2)}) collective-permute-start(bf16[256,128]{1,0:T(8,128)(2,1)S(1)} %get-tuple-element.20), channel_id=1, source_target_pairs={{0,3},{1,2},{2,1},{3,0},{4,7},{5,6},{6,5},{7,4},{8,11},{9,10},{10,... | collective-permute-start | bytes 196616 | tf_op jit(solution)/shard_map/ppermute | solution.py:43
  11.7 0.0 copy-start.1
  11.7 0.0 copy-start.2
  11.7 1.6 %collective-permute-start.5 = (bf16[256,128]{1,0:T(8,128)(2,1)S(1)}, bf16[256,128]{1,0:T(8,128)(2,1)S(1)}, u32[]{:S(2)}, u32[]{:S(2)}) collective-permute-start(bf16[256,128]{1,0:T(8,128)(2,1)S(1)} %get-tuple-element.21), channel_id=1, source_target_pairs={{0,2},{1,0},{2,3},{3,1},{4,6},{5,4},{6,7},{7,5},{8,10},{9,8},{10,1... | collective-permute-start | bytes 196616 | tf_op jit(solution)/shard_map/ppermute | solution.py:43
  13.3 0.3 %shard_map.96.refs_0_.matrix = bf16[512,512]{1,0:T(8,128)(2,1)S(1)} custom-call(bf16[512,512]{1,0:T(8,128)(2,1)S(1)} %shard_map.95.near.matrix), custom_call_target="tpu_custom_call" | custom-call | bytes 1572864 | tf_op jit(solution)/shard_map/pallas_call | solution.py:287
  13.6 0.0 collective-permute-done.6.refs_7_
  13.6 3.6 %collective-permute-done.3.refs_2_ = bf16[256,128]{1,0:T(8,128)(2,1)S(1)} collective-permute-done((bf16[256,128]{1,0:T(8,128)(2,1)S(1)}, bf16[256,128]{1,0:T(8,128)(2,1)S(1)}, u32[]{:S(2)}, u32[]{:S(2)}) %collective-permute-start.3) | collective-permute-done | bytes 65568 | tf_op jit(solution)/shard_map/ppermute | solution.py:43
  17.2 0.0 collective-permute-done.4.refs_3_
  17.2 0.0 collective-permute-done.5.refs_4_
  17.2 0.0 copy-done.1
  17.2 0.0 copy-done.2
  17.2 0.5 %shard_map.98 = (bf16[256,128]{1,0:T(8,128)(2,1)S(1)}, f32[128,128]{1,0:T(8,128)S(1)}, bf16[128,128]{1,0:T(8,128)(2,1)S(1)}, f32[128,256]{1,0:T(8,128)S(1)}) custom-call(bf16[512,512]{1,0:T(8,128)(2,1)S(1)} %shard_map.96.refs_0_.matrix, bf16[256,128]{1,0:T(8,128)(2,1)S(1)} %get-tuple-element.18.refs_1_, bf16[256,128]{1,0:T(8,128)(2,1)S(1)} %collective-permute-done.3.refs_2_, ...), custom_call_target="tpu_custom_call" | custom-call | flops 117440512 | tf_op jit(solution)/shard_map/pallas_call | solution.py:296
  17.8 0.1 collective-permute-start.7
  17.8 1.2 %collective-permute-done.7.came = bf16[128,128]{1,0:T(8,128)(2,1)S(1)} collective-permute-done((bf16[128,128]{1,0:T(8,128)(2,1)S(1)}, bf16[128,128]{1,0:T(8,128)(2,1)S(1)}, u32[]{:S(2)}, u32[]{:S(2)}) %collective-permute-start.7) | collective-permute-done | bytes 32800 | tf_op jit(solution)/shard_map/ppermute | solution.py:58
  19.0 1.5 %collective-permute-start.8 = (bf16[384,128]{1,0:T(8,128)(2,1)S(1)}, bf16[384,128]{1,0:T(8,128)(2,1)S(1)}, u32[]{:S(2)}, u32[]{:S(2)}) collective-permute-start(bf16[384,128]{1,0:T(8,128)(2,1)S(1)} %shard_map.100.refs_0_), channel_id=1, source_target_pairs={{0,1},{1,0},{2,3},{3,2},{4,5},{5,4},{6,7},{7,6},{8,9},{9,8},{10,11... | collective-permute-start | bytes 294920 | tf_op jit(solution)/shard_map/ppermute | solution.py:58
  20.6 3.4 %collective-permute-done.8.refs_1_ = bf16[384,128]{1,0:T(8,128)(2,1)S(1)} collective-permute-done((bf16[384,128]{1,0:T(8,128)(2,1)S(1)}, bf16[384,128]{1,0:T(8,128)(2,1)S(1)}, u32[]{:S(2)}, u32[]{:S(2)}) %collective-permute-start.8) | collective-permute-done | bytes 98336 | tf_op jit(solution)/shard_map/ppermute | solution.py:58
  24.0 0.3 shard_map.101
  24.3 1.6 %collective-permute-start.10 = (bf16[256,128]{1,0:T(8,128)(2,1)S(1)}, bf16[256,128]{1,0:T(8,128)(2,1)S(1)}, u32[]{:S(2)}, u32[]{:S(2)}) collective-permute-start(bf16[256,128]{1,0:T(8,128)(2,1)S(1)} %get-tuple-element.29), channel_id=1, source_target_pairs={{0,8},{4,12},{8,0},{12,4},{1,9},{5,13},{9,1},{13,5},{2,10},{6,14},... | collective-permute-start | bytes 196616 | tf_op jit(solution)/shard_map/ppermute | solution.py:43
  25.9 0.0 collective-permute-start.11
  25.9 0.5 %collective-permute-start.9 = (bf16[256,128]{1,0:T(8,128)(2,1)S(1)}, bf16[256,128]{1,0:T(8,128)(2,1)S(1)}, u32[]{:S(2)}, u32[]{:S(2)}) collective-permute-start(bf16[256,128]{1,0:T(8,128)(2,1)S(1)} %get-tuple-element.28), channel_id=1, source_target_pairs={{0,4},{4,8},{8,12},{12,0},{1,5},{5,9},{9,13},{13,1},{2,6},{6,10},{... | collective-permute-start | bytes 196616 | tf_op jit(solution)/shard_map/ppermute | solution.py:43
  26.4 0.7 %shard_map.99 = bf16[128,256]{1,0:T(8,128)(2,1)} custom-call(f32[128,256]{1,0:T(8,128)S(1)} %get-tuple-element.22.pre), custom_call_target="tpu_custom_call" | custom-call | tf_op jit(solution)/shard_map/pallas_call | solution.py:315
  27.0 1.6 %collective-permute-done.10.refs_1_ = bf16[256,128]{1,0:T(8,128)(2,1)S(1)} collective-permute-done((bf16[256,128]{1,0:T(8,128)(2,1)S(1)}, bf16[256,128]{1,0:T(8,128)(2,1)S(1)}, u32[]{:S(2)}, u32[]{:S(2)}) %collective-permute-start.10) | collective-permute-done | bytes 65568 | tf_op jit(solution)/shard_map/ppermute | solution.py:43
  28.6 0.4 %collective-permute-done.11.refs_2_ = bf16[256,128]{1,0:T(8,128)(2,1)S(1)} collective-permute-done((bf16[256,128]{1,0:T(8,128)(2,1)S(1)}, bf16[256,128]{1,0:T(8,128)(2,1)S(1)}, u32[]{:S(2)}, u32[]{:S(2)}) %collective-permute-start.11) | collective-permute-done | bytes 65568 | tf_op jit(solution)/shard_map/ppermute | solution.py:43
  29.1 1.0 %collective-permute-done.9.refs_0_ = bf16[256,128]{1,0:T(8,128)(2,1)S(1)} collective-permute-done((bf16[256,128]{1,0:T(8,128)(2,1)S(1)}, bf16[256,128]{1,0:T(8,128)(2,1)S(1)}, u32[]{:S(2)}, u32[]{:S(2)}) %collective-permute-start.9) | collective-permute-done | bytes 65568 | tf_op jit(solution)/shard_map/ppermute | solution.py:43
  30.0 0.7 %shard_map.102 = (bf16[128,128]{1,0:T(8,128)(2,1)}, f32[128,256]{1,0:T(8,128)}) custom-call(f32[128,128]{1,0:T(8,128)S(1)} %get-tuple-element.26.own, bf16[128,128]{1,0:T(8,128)(2,1)S(1)} %get-tuple-element.27.kept, bf16[256,128]{1,0:T(8,128)(2,1)S(1)} %collective-permute-done.9.refs_0_, bf16[256,128]{1,0:T(8,128)(2,1)S(1)} %collective-permute-done.10.refs_1_, ...), custom_call_target="tpu_custom_call" | custom-call | tf_op jit(solution)/shard_map/pallas_call | solution.py:328
  (2 shorter events, 0.0 us)
Async XLA Ops:
  0.6 7.0 %copy-start = (bf16[1,1,8,128,128]{4,3,2,1,0:T(8,128)(2,1)S(1)}, bf16[1,1,8,128,128]{4,3,2,1,0:T(8,128)(2,1)}, u32[]{:S(2)}) copy-start(bf16[1,1,8,128,128]{4,3,2,1,0:T(8,128)(2,1)} %vals.1) | copy-start | bytes 786436
  0.6 7.7 %collective-permute-start = (bf16[128,128]{1,0:T(8,128)(2,1)}, bf16[128,128]{1,0:T(8,128)(2,1)S(1)}, u32[]{:S(2)}, u32[]{:S(2)}) collective-permute-start(bf16[128,128]{1,0:T(8,128)(2,1)} %refs_0_.1), channel_id=1, source_target_pairs={{0,8},{4,12},{8,0},{12,4},{1,9},{5,13},{9,1},{13,5},{2,10},{6,14},... | collective-permute-start | bytes 98312 | tf_op jit(solution)/shard_map/ppermute | solution.py:58
  3.6 4.7 %collective-permute-start.1 = (bf16[128,128]{1,0:T(8,128)(2,1)}, bf16[128,128]{1,0:T(8,128)(2,1)S(1)}, u32[]{:S(2)}, u32[]{:S(2)}) collective-permute-start(bf16[128,128]{1,0:T(8,128)(2,1)} %refs_0_.1), channel_id=1, source_target_pairs={{0,12},{4,8},{8,4},{12,0},{1,13},{5,9},{9,5},{13,1},{2,14},{6,10},... | collective-permute-start | bytes 98312 | tf_op jit(solution)/shard_map/ppermute | solution.py:58
  3.6 4.7 %collective-permute-start.2 = (bf16[128,128]{1,0:T(8,128)(2,1)}, bf16[128,128]{1,0:T(8,128)(2,1)S(1)}, u32[]{:S(2)}, u32[]{:S(2)}) collective-permute-start(bf16[128,128]{1,0:T(8,128)(2,1)} %refs_0_.1), channel_id=1, source_target_pairs={{0,4},{4,0},{8,12},{12,8},{1,5},{5,1},{9,13},{13,9},{2,6},{6,2},{1... | collective-permute-start | bytes 98312 | tf_op jit(solution)/shard_map/ppermute | solution.py:58
  3.8 9.8 %collective-permute-start.6 = (bf16[128,256]{1,0:T(8,128)(2,1)}, bf16[128,256]{1,0:T(8,128)(2,1)S(1)}, u32[]{:S(2)}, u32[]{:S(2)}) collective-permute-start(bf16[128,256]{1,0:T(8,128)(2,1)} %refs_6_.1), channel_id=1, source_target_pairs={{0,2},{1,3},{2,0},{3,1},{4,6},{5,7},{6,4},{7,5},{8,10},{9,11},{10,... | collective-permute-start | bytes 196616 | tf_op jit(solution)/shard_map/ppermute | solution.py:58
  6.9 0.7 %copy-start.4 = (s32[1,1,8]{2,1,0:T(1,128)S(1)}, s32[1,1,8]{2,1,0:T(1,128)}, u32[]{:S(2)}) copy-start(s32[1,1,8]{2,1,0:T(1,128)} %rows_in.1) | copy-start | bytes 100
  6.9 0.7 %copy-start.5 = (s32[1,1,8]{2,1,0:T(1,128)S(1)}, s32[1,1,8]{2,1,0:T(1,128)}, u32[]{:S(2)}) copy-start(s32[1,1,8]{2,1,0:T(1,128)} %cols_in.1) | copy-start | bytes 100
  7.6 0.8 %copy-start.3 = (bf16[128,128]{1,0:T(8,128)(2,1)S(1)}, bf16[128,128]{1,0:T(8,128)(2,1)}, u32[]{:S(2)}) copy-start(bf16[128,128]{1,0:T(8,128)(2,1)} %refs_0_.1) | copy-start | bytes 98308
  8.7 8.5 %collective-permute-start.3 = (bf16[256,128]{1,0:T(8,128)(2,1)S(1)}, bf16[256,128]{1,0:T(8,128)(2,1)S(1)}, u32[]{:S(2)}, u32[]{:S(2)}) collective-permute-start(bf16[256,128]{1,0:T(8,128)(2,1)S(1)} %get-tuple-element.19), channel_id=1, source_target_pairs={{0,1},{1,3},{2,0},{3,2},{4,5},{5,7},{6,4},{7,6},{8,9},{9,11},{10,8... | collective-permute-start | bytes 196616 | tf_op jit(solution)/shard_map/ppermute | solution.py:43
  10.3 6.9 %collective-permute-start.4 = (bf16[256,128]{1,0:T(8,128)(2,1)S(1)}, bf16[256,128]{1,0:T(8,128)(2,1)S(1)}, u32[]{:S(2)}, u32[]{:S(2)}) collective-permute-start(bf16[256,128]{1,0:T(8,128)(2,1)S(1)} %get-tuple-element.20), channel_id=1, source_target_pairs={{0,3},{1,2},{2,1},{3,0},{4,7},{5,6},{6,5},{7,4},{8,11},{9,10},{10,... | collective-permute-start | bytes 196616 | tf_op jit(solution)/shard_map/ppermute | solution.py:43
  11.7 5.5 %copy-start.1 = (bf16[128,256]{1,0:T(8,128)(2,1)S(1)}, bf16[128,256]{1,0:T(8,128)(2,1)}, u32[]{:S(2)}) copy-start(bf16[128,256]{1,0:T(8,128)(2,1)} %refs_5_.1) | copy-start | bytes 196612
  11.7 5.5 %copy-start.2 = (bf16[128,256]{1,0:T(8,128)(2,1)S(1)}, bf16[128,256]{1,0:T(8,128)(2,1)}, u32[]{:S(2)}) copy-start(bf16[128,256]{1,0:T(8,128)(2,1)} %refs_6_.1) | copy-start | bytes 196612
  11.7 5.5 %collective-permute-start.5 = (bf16[256,128]{1,0:T(8,128)(2,1)S(1)}, bf16[256,128]{1,0:T(8,128)(2,1)S(1)}, u32[]{:S(2)}, u32[]{:S(2)}) collective-permute-start(bf16[256,128]{1,0:T(8,128)(2,1)S(1)} %get-tuple-element.21), channel_id=1, source_target_pairs={{0,2},{1,0},{2,3},{3,1},{4,6},{5,4},{6,7},{7,5},{8,10},{9,8},{10,1... | collective-permute-start | bytes 196616 | tf_op jit(solution)/shard_map/ppermute | solution.py:43
  17.8 1.3 %collective-permute-start.7 = (bf16[128,128]{1,0:T(8,128)(2,1)S(1)}, bf16[128,128]{1,0:T(8,128)(2,1)S(1)}, u32[]{:S(2)}, u32[]{:S(2)}) collective-permute-start(bf16[128,128]{1,0:T(8,128)(2,1)S(1)} %get-tuple-element.25), channel_id=1, source_target_pairs={{0,4},{4,0},{8,12},{12,8},{1,5},{5,1},{9,13},{13,9},{2,6},{6,2},{1... | collective-permute-start | bytes 98312 | tf_op jit(solution)/shard_map/ppermute | solution.py:58
  19.0 4.9 %collective-permute-start.8 = (bf16[384,128]{1,0:T(8,128)(2,1)S(1)}, bf16[384,128]{1,0:T(8,128)(2,1)S(1)}, u32[]{:S(2)}, u32[]{:S(2)}) collective-permute-start(bf16[384,128]{1,0:T(8,128)(2,1)S(1)} %shard_map.100.refs_0_), channel_id=1, source_target_pairs={{0,1},{1,0},{2,3},{3,2},{4,5},{5,4},{6,7},{7,6},{8,9},{9,8},{10,11... | collective-permute-start | bytes 294920 | tf_op jit(solution)/shard_map/ppermute | solution.py:58
  24.3 4.3 %collective-permute-start.10 = (bf16[256,128]{1,0:T(8,128)(2,1)S(1)}, bf16[256,128]{1,0:T(8,128)(2,1)S(1)}, u32[]{:S(2)}, u32[]{:S(2)}) collective-permute-start(bf16[256,128]{1,0:T(8,128)(2,1)S(1)} %get-tuple-element.29), channel_id=1, source_target_pairs={{0,8},{4,12},{8,0},{12,4},{1,9},{5,13},{9,1},{13,5},{2,10},{6,14},... | collective-permute-start | bytes 196616 | tf_op jit(solution)/shard_map/ppermute | solution.py:43
  25.9 3.2 %collective-permute-start.11 = (bf16[256,128]{1,0:T(8,128)(2,1)S(1)}, bf16[256,128]{1,0:T(8,128)(2,1)S(1)}, u32[]{:S(2)}, u32[]{:S(2)}) collective-permute-start(bf16[256,128]{1,0:T(8,128)(2,1)S(1)} %get-tuple-element.30), channel_id=1, source_target_pairs={{0,12},{4,0},{8,4},{12,8},{1,13},{5,1},{9,5},{13,9},{2,14},{6,2},{... | collective-permute-start | bytes 196616 | tf_op jit(solution)/shard_map/ppermute | solution.py:43
  25.9 4.2 %collective-permute-start.9 = (bf16[256,128]{1,0:T(8,128)(2,1)S(1)}, bf16[256,128]{1,0:T(8,128)(2,1)S(1)}, u32[]{:S(2)}, u32[]{:S(2)}) collective-permute-start(bf16[256,128]{1,0:T(8,128)(2,1)S(1)} %get-tuple-element.28), channel_id=1, source_target_pairs={{0,4},{4,8},{8,12},{12,0},{1,5},{5,9},{9,13},{13,1},{2,6},{6,10},{... | collective-permute-start | bytes 196616 | tf_op jit(solution)/shard_map/ppermute | solution.py:43

commit v19 on v18

--- a/solution.py
+++ b/solution.py
@@ -201,10 +201,8 @@
     halve(term, mine, other)
 
 
-def message_kernel(back, mine, came, message):
-    nodes = back.shape[0]
-    message[:nodes] = back[...]
-    message[nodes:] = (mine[...] + wide(came[...])).astype(message.dtype)
+def add_kernel(mine, came, out):
+    out[...] = (mine[...] + wide(came[...])).astype(out.dtype)
 
 
 def act_kernel(pre, act):
@@ -212,12 +210,11 @@
 
 
 def backward_kernel(n, matrix, *refs):
-    messages, own, kept, sends, product = refs[:n], refs[n], refs[n + 1], refs[n + 2 : -1], refs[-1]
-    rows, backs = own.shape[0], messages[0].shape[0] - kept.shape[0]
-    stacked = jnp.concatenate([message[:backs] for message in messages], axis=0)
-    product[...] = dot(matrix[...], stacked)
+    backs, halves, (own, kept, *sends, product) = refs[:n], refs[n : 2 * n], refs[2 * n :]
+    rows = own.shape[0]
+    product[...] = dot(matrix[...], jnp.concatenate([back[...] for back in backs], axis=0))
     own[...] = product[:rows]
-    term = tree([wide(message[backs:]) for message in messages]).astype(kept.dtype)
+    term = tree([wide(half[...]) for half in halves]).astype(kept.dtype)
     kept[...] = term
     here, size = lax.axis_index("row"), lax.axis_size("row")
     for d, send in enumerate(sends, 1):
@@ -305,23 +302,22 @@
         flops=14 * layers * nodes * width * hidden,
         after=[far],
     )(own, *parts, weight, *cotangents)
-    (sent,) = call(message_kernel, [((layers * nodes + width, width), NARROW)], [VMEM] * 3)(
-        back, mine, swap(other, "row", 1)
-    )
+    (term,) = call(add_kernel, [(square, NARROW)], [VMEM] * 2)(mine, swap(other, "row", 1))
     if paired:
-        spread = [swap(sent, "col", 1)]
+        backs, terms = [back, swap(back, "col", 1)], [term, swap(term, "col", 1)]
     else:
-        spread = exchange([sent] * (n_col - 1), "col", False)
+        backs = [back] + exchange([back] * (n_col - 1), "col", False)
+        terms = [term] + exchange([term] * (n_col - 1), "col", False)
     (act,) = call(act_kernel, [((nodes, hidden), NARROW)], [VMEM])(pre)
 
     message = ((nodes + width, width), NARROW)
     own, kept, *sends = call(
-        functools.partial(backward_kernel, 1 + len(spread)),
+        functools.partial(backward_kernel, len(backs)),
         [((nodes, width), jnp.float32), (square, NARROW)] + [message] * (n_row - 1),
-        [VMEM] * (2 + len(spread)),
+        [VMEM] * (1 + 2 * len(backs)),
         scratch=[pltpu.VMEM((across, width), jnp.float32)],
         **forward,
-    )(far, sent, *spread)
+    )(far, *backs, *terms)
     parts = exchange(sends, "row", True)
 
     scale = float(nodes * n_row * n_col) ** -0.5

time: 30.9 us -> 29.8 us (0.964); the launches traced: 30.7 us -> 29.2 us
  waiting for transfers between devices: 11.2 us -> 7.72 us
  starting transfers between devices: 14.5 us -> 16.4 us
    ppermute x6 -> x7, waiting for transfers between devices: 4.61 us -> 2.8 us  [swap(): return lax.ppermute(value, axis, [(s, s ^ distance) for s in range(n)])]
    ppermute x6, waiting for transfers between devices: 6.58 us -> 4.92 us  [exchange(): lax.ppermute(send, axis, [(s, target(s, d)) for s in range(n)])]
    ppermute x6 -> x7, starting transfers between devices: 7.83 us -> 9.03 us  [swap(): return lax.ppermute(value, axis, [(s, s ^ distance) for s in range(n)])]
    ppermute x6, starting transfers between devices: 6.66 us -> 7.4 us  [exchange(): lax.ppermute(send, axis, [(s, target(s, d)) for s in range(n)])]
  transfers between devices with their start and end apart: 12 -> 13, of which waited for: 6 -> 4; matrix products, arithmetic and copies ran while one was open for 0% -> 0% of each run, Pallas kernels for 6% -> 7%
where the time goes in v19:
time: 29.8 us; the launch traced here: 29.2 us
  starting transfers between devices  16.4 us (55%)
  waiting for transfers between devices  7.72 us (26%)
  Pallas kernels  3.52 us (12%)
  between operations  1.46 us (5%)
    ppermute x7, starting transfers between devices, swap(): return lax.ppermute(value, axis, [(s, s ^ distance) for s in range(n)])  9.03 us
    ppermute x6, starting transfers between devices, exchange(): lax.ppermute(send, axis, [(s, target(s, d)) for s in range(n)])  7.4 us
    ppermute x6, waiting for transfers between devices, exchange(): lax.ppermute(send, axis, [(s, target(s, d)) for s in range(n)])  4.92 us
    ppermute x7, waiting for transfers between devices, swap(): return lax.ppermute(value, axis, [(s, s ^ distance) for s in range(n)])  2.8 us
    pallas_call x1, Pallas kernels, per_device(): call(functools.partial(last_kernel, scale), [((nodes, width), NARROW), ((...  0.7 us
    pallas_call x1, Pallas kernels, per_device(): call(functools.partial(dense_kernel, nodes // side, paired), [((down, acr...  0.68 us
    pallas_call x1, Pallas kernels, per_device(): act, = call(act_kernel, [((nodes, hidden), NARROW)], [VMEM])(pre)  0.65 us
  transfers between devices with their start and end apart: 13, of which 4 were waited for; matrix products, arithmetic and copies ran while one was open for 0% of the time, Pallas kernels for 7%

profile of v19, /device:TPU:0, one launch (start us, length us, event | category | flops | bytes accessed | tf_op | source)
XLA Modules:
  0.0 29.2 jit_solution(6825662832150176337)
XLA Ops:
  0.6 0.0 copy-start
  0.6 3.0 %collective-permute-start = (bf16[128,128]{1,0:T(8,128)(2,1)}, bf16[128,128]{1,0:T(8,128)(2,1)S(1)}, u32[]{:S(2)}, u32[]{:S(2)}) collective-permute-start(bf16[128,128]{1,0:T(8,128)(2,1)} %refs_0_.1), channel_id=1, source_target_pairs={{0,8},{4,12},{8,0},{12,4},{1,9},{5,13},{9,1},{13,5},{2,10},{6,14},... | collective-permute-start | bytes 98312 | tf_op jit(solution)/shard_map/ppermute | solution.py:58
  3.6 0.0 collective-permute-start.1
  3.6 0.2 collective-permute-start.2
  3.8 3.0 %collective-permute-start.6 = (bf16[128,256]{1,0:T(8,128)(2,1)}, bf16[128,256]{1,0:T(8,128)(2,1)S(1)}, u32[]{:S(2)}, u32[]{:S(2)}) collective-permute-start(bf16[128,256]{1,0:T(8,128)(2,1)} %refs_6_.1), channel_id=1, source_target_pairs={{0,2},{1,3},{2,0},{3,1},{4,6},{5,7},{6,4},{7,5},{8,10},{9,11},{10,... | collective-permute-start | bytes 196616 | tf_op jit(solution)/shard_map/ppermute | solution.py:58
  6.9 0.0 copy-start.4
  6.9 0.0 copy-start.5
  7.6 0.0 copy-done
  7.6 0.0 copy-done.4
  7.6 0.0 copy-done.5
  7.6 0.0 copy-start.3
  7.7 0.7 %shard_map.95.near.matrix = bf16[512,512]{1,0:T(8,128)(2,1)S(1)} custom-call(bf16[512,512]{1,0:T(8,128)(2,1)S(1)} %shard_map.94.blank, bf16[1,1,8,128,128]{4,3,2,1,0:T(8,128)(2,1)S(1)} %copy-done, s32[1,1,8]{2,1,0:T(1,128)S(1)} %copy-done.4, s32[1,1,8]{2,1,0:T(1,128)S(1)} %copy-done.5, s32[1,1]{1,0:T(1,128)S(6)} %copy.12.count_in), custom_call_target="tpu_custom_call", output_to_operand_aliasing={{}: (0, {})} | custom-call | bytes 1048576 | tf_op jit(solution)/shard_map/pallas_call | solution.py:250
  8.3 0.0 collective-permute-done.refs_1_
  8.4 0.0 collective-permute-done.1.refs_2_
  8.4 0.0 collective-permute-done.2.refs_3_
  8.4 0.0 copy-done.3
  8.4 0.3 shard_map.97
  8.7 1.6 %collective-permute-start.3 = (bf16[256,128]{1,0:T(8,128)(2,1)S(1)}, bf16[256,128]{1,0:T(8,128)(2,1)S(1)}, u32[]{:S(2)}, u32[]{:S(2)}) collective-permute-start(bf16[256,128]{1,0:T(8,128)(2,1)S(1)} %get-tuple-element.19), channel_id=1, source_target_pairs={{0,1},{1,3},{2,0},{3,2},{4,5},{5,7},{6,4},{7,6},{8,9},{9,11},{10,8... | collective-permute-start | bytes 196616 | tf_op jit(solution)/shard_map/ppermute | solution.py:43
  10.3 1.4 %collective-permute-start.4 = (bf16[256,128]{1,0:T(8,128)(2,1)S(1)}, bf16[256,128]{1,0:T(8,128)(2,1)S(1)}, u32[]{:S(2)}, u32[]{:S(2)}) collective-permute-start(bf16[256,128]{1,0:T(8,128)(2,1)S(1)} %get-tuple-element.20), channel_id=1, source_target_pairs={{0,3},{1,2},{2,1},{3,0},{4,7},{5,6},{6,5},{7,4},{8,11},{9,10},{10,... | collective-permute-start | bytes 196616 | tf_op jit(solution)/shard_map/ppermute | solution.py:43
  11.7 0.0 copy-start.1
  11.7 0.0 copy-start.2
  11.7 1.6 %collective-permute-start.5 = (bf16[256,128]{1,0:T(8,128)(2,1)S(1)}, bf16[256,128]{1,0:T(8,128)(2,1)S(1)}, u32[]{:S(2)}, u32[]{:S(2)}) collective-permute-start(bf16[256,128]{1,0:T(8,128)(2,1)S(1)} %get-tuple-element.21), channel_id=1, source_target_pairs={{0,2},{1,0},{2,3},{3,1},{4,6},{5,4},{6,7},{7,5},{8,10},{9,8},{10,1... | collective-permute-start | bytes 196616 | tf_op jit(solution)/shard_map/ppermute | solution.py:43
  13.3 0.3 %shard_map.96.refs_0_.matrix = bf16[512,512]{1,0:T(8,128)(2,1)S(1)} custom-call(bf16[512,512]{1,0:T(8,128)(2,1)S(1)} %shard_map.95.near.matrix), custom_call_target="tpu_custom_call" | custom-call | bytes 1572864 | tf_op jit(solution)/shard_map/pallas_call | solution.py:284
  13.6 0.0 collective-permute-done.6.refs_7_
  13.6 3.6 %collective-permute-done.3.refs_2_ = bf16[256,128]{1,0:T(8,128)(2,1)S(1)} collective-permute-done((bf16[256,128]{1,0:T(8,128)(2,1)S(1)}, bf16[256,128]{1,0:T(8,128)(2,1)S(1)}, u32[]{:S(2)}, u32[]{:S(2)}) %collective-permute-start.3) | collective-permute-done | bytes 65568 | tf_op jit(solution)/shard_map/ppermute | solution.py:43
  17.2 0.0 collective-permute-done.4.refs_3_
  17.2 0.0 collective-permute-done.5.refs_4_
  17.2 0.0 copy-done.1
  17.2 0.0 copy-done.2
  17.2 0.5 %shard_map.98 = (bf16[256,128]{1,0:T(8,128)(2,1)S(1)}, f32[128,128]{1,0:T(8,128)S(1)}, bf16[128,128]{1,0:T(8,128)(2,1)S(1)}, f32[128,256]{1,0:T(8,128)S(1)}) custom-call(bf16[512,512]{1,0:T(8,128)(2,1)S(1)} %shard_map.96.refs_0_.matrix, bf16[256,128]{1,0:T(8,128)(2,1)S(1)} %get-tuple-element.18.refs_1_, bf16[256,128]{1,0:T(8,128)(2,1)S(1)} %collective-permute-done.3.refs_2_, ...), custom_call_target="tpu_custom_call" | custom-call | flops 117440512 | tf_op jit(solution)/shard_map/pallas_call | solution.py:293
  17.8 0.1 collective-permute-start.8
  17.8 1.5 %collective-permute-start.7 = (bf16[256,128]{1,0:T(8,128)(2,1)S(1)}, bf16[256,128]{1,0:T(8,128)(2,1)S(1)}, u32[]{:S(2)}, u32[]{:S(2)}) collective-permute-start(bf16[256,128]{1,0:T(8,128)(2,1)S(1)} %get-tuple-element.23.refs_0_), channel_id=1, source_target_pairs={{0,1},{1,0},{2,3},{3,2},{4,5},{5,4},{6,7},{7,6},{8,9},{9,8},{10,11... | collective-permute-start | bytes 196616 | tf_op jit(solution)/shard_map/ppermute | solution.py:58
  19.4 0.0 collective-permute-done.8.came
  19.4 1.2 %collective-permute-start.9 = (bf16[128,128]{1,0:T(8,128)(2,1)S(1)}, bf16[128,128]{1,0:T(8,128)(2,1)S(1)}, u32[]{:S(2)}, u32[]{:S(2)}) collective-permute-start(bf16[128,128]{1,0:T(8,128)(2,1)S(1)} %shard_map.100.refs_2_), channel_id=1, source_target_pairs={{0,1},{1,0},{2,3},{3,2},{4,5},{5,4},{6,7},{7,6},{8,9},{9,8},{10,11... | collective-permute-start | bytes 98312 | tf_op jit(solution)/shard_map/ppermute | solution.py:58
  20.6 2.8 %collective-permute-done.9.refs_3_ = bf16[128,128]{1,0:T(8,128)(2,1)S(1)} collective-permute-done((bf16[128,128]{1,0:T(8,128)(2,1)S(1)}, bf16[128,128]{1,0:T(8,128)(2,1)S(1)}, u32[]{:S(2)}, u32[]{:S(2)}) %collective-permute-start.9) | collective-permute-done | bytes 32800 | tf_op jit(solution)/shard_map/ppermute | solution.py:58
  23.4 0.0 collective-permute-done.7.refs_1_
  23.4 0.3 %shard_map.101 = (f32[128,128]{1,0:T(8,128)S(1)}, bf16[128,128]{1,0:T(8,128)(2,1)S(1)}, bf16[256,128]{1,0:T(8,128)(2,1)S(1)}, bf16[256,128]{1,0:T(8,128)(2,1)S(1)}, bf16[256,128]{1,0:T(8,128)(2,1)S(1)}) custom-call(bf16[512,512]{1,0:T(8,128)(2,1)S(1)} %shard_map.96.refs_0_.matrix, bf16[256,128]{1,0:T(8,128)(2,1)S(1)} %get-tuple-element.23.refs_0_, ...), custom_call_target="tpu_custom_call" | custom-call | flops 67108864 | bytes 1048576 | tf_op jit(solution)/shard_map/pallas_call | solution.py:314
  23.7 0.1 collective-permute-start.10
  23.7 1.4 %collective-permute-start.11 = (bf16[256,128]{1,0:T(8,128)(2,1)S(1)}, bf16[256,128]{1,0:T(8,128)(2,1)S(1)}, u32[]{:S(2)}, u32[]{:S(2)}) collective-permute-start(bf16[256,128]{1,0:T(8,128)(2,1)S(1)} %get-tuple-element.29), channel_id=1, source_target_pairs={{0,8},{4,12},{8,0},{12,4},{1,9},{5,13},{9,1},{13,5},{2,10},{6,14},... | collective-permute-start | bytes 196616 | tf_op jit(solution)/shard_map/ppermute | solution.py:43
  25.1 1.4 %collective-permute-start.12 = (bf16[256,128]{1,0:T(8,128)(2,1)S(1)}, bf16[256,128]{1,0:T(8,128)(2,1)S(1)}, u32[]{:S(2)}, u32[]{:S(2)}) collective-permute-start(bf16[256,128]{1,0:T(8,128)(2,1)S(1)} %get-tuple-element.30), channel_id=1, source_target_pairs={{0,12},{4,0},{8,4},{12,8},{1,13},{5,1},{9,5},{13,9},{2,14},{6,2},{... | collective-permute-start | bytes 196616 | tf_op jit(solution)/shard_map/ppermute | solution.py:43
  26.5 0.7 %shard_map.99 = bf16[128,256]{1,0:T(8,128)(2,1)} custom-call(f32[128,256]{1,0:T(8,128)S(1)} %get-tuple-element.22.pre), custom_call_target="tpu_custom_call" | custom-call | tf_op jit(solution)/shard_map/pallas_call | solution.py:311
  27.2 0.3 %collective-permute-done.10.refs_0_ = bf16[256,128]{1,0:T(8,128)(2,1)S(1)} collective-permute-done((bf16[256,128]{1,0:T(8,128)(2,1)S(1)}, bf16[256,128]{1,0:T(8,128)(2,1)S(1)}, u32[]{:S(2)}, u32[]{:S(2)}) %collective-permute-start.10) | collective-permute-done | bytes 65568 | tf_op jit(solution)/shard_map/ppermute | solution.py:43
  27.5 1.0 %collective-permute-done.11.refs_1_ = bf16[256,128]{1,0:T(8,128)(2,1)S(1)} collective-permute-done((bf16[256,128]{1,0:T(8,128)(2,1)S(1)}, bf16[256,128]{1,0:T(8,128)(2,1)S(1)}, u32[]{:S(2)}, u32[]{:S(2)}) %collective-permute-start.11) | collective-permute-done | bytes 65568 | tf_op jit(solution)/shard_map/ppermute | solution.py:43
  28.5 0.0 collective-permute-done.12.refs_2_
  28.5 0.7 %shard_map.102 = (bf16[128,128]{1,0:T(8,128)(2,1)}, f32[128,256]{1,0:T(8,128)}) custom-call(f32[128,128]{1,0:T(8,128)S(1)} %get-tuple-element.26.own, bf16[128,128]{1,0:T(8,128)(2,1)S(1)} %get-tuple-element.27.kept, bf16[256,128]{1,0:T(8,128)(2,1)S(1)} %collective-permute-done.10.refs_0_, bf16[256,128]{1,0:T(8,128)(2,1)S(1)} %collective-permute-done.11.refs_1_, ...), custom_call_target="tpu_custom_call" | custom-call | tf_op jit(solution)/shard_map/pallas_call | solution.py:324
  (2 shorter events, 0.0 us)
Async XLA Ops:
  0.6 7.0 %copy-start = (bf16[1,1,8,128,128]{4,3,2,1,0:T(8,128)(2,1)S(1)}, bf16[1,1,8,128,128]{4,3,2,1,0:T(8,128)(2,1)}, u32[]{:S(2)}) copy-start(bf16[1,1,8,128,128]{4,3,2,1,0:T(8,128)(2,1)} %vals.1) | copy-start | bytes 786436
  0.6 7.7 %collective-permute-start = (bf16[128,128]{1,0:T(8,128)(2,1)}, bf16[128,128]{1,0:T(8,128)(2,1)S(1)}, u32[]{:S(2)}, u32[]{:S(2)}) collective-permute-start(bf16[128,128]{1,0:T(8,128)(2,1)} %refs_0_.1), channel_id=1, source_target_pairs={{0,8},{4,12},{8,0},{12,4},{1,9},{5,13},{9,1},{13,5},{2,10},{6,14},... | collective-permute-start | bytes 98312 | tf_op jit(solution)/shard_map/ppermute | solution.py:58
  3.6 4.7 %collective-permute-start.1 = (bf16[128,128]{1,0:T(8,128)(2,1)}, bf16[128,128]{1,0:T(8,128)(2,1)S(1)}, u32[]{:S(2)}, u32[]{:S(2)}) collective-permute-start(bf16[128,128]{1,0:T(8,128)(2,1)} %refs_0_.1), channel_id=1, source_target_pairs={{0,12},{4,8},{8,4},{12,0},{1,13},{5,9},{9,5},{13,1},{2,14},{6,10},... | collective-permute-start | bytes 98312 | tf_op jit(solution)/shard_map/ppermute | solution.py:58
  3.6 4.7 %collective-permute-start.2 = (bf16[128,128]{1,0:T(8,128)(2,1)}, bf16[128,128]{1,0:T(8,128)(2,1)S(1)}, u32[]{:S(2)}, u32[]{:S(2)}) collective-permute-start(bf16[128,128]{1,0:T(8,128)(2,1)} %refs_0_.1), channel_id=1, source_target_pairs={{0,4},{4,0},{8,12},{12,8},{1,5},{5,1},{9,13},{13,9},{2,6},{6,2},{1... | collective-permute-start | bytes 98312 | tf_op jit(solution)/shard_map/ppermute | solution.py:58
  3.8 9.8 %collective-permute-start.6 = (bf16[128,256]{1,0:T(8,128)(2,1)}, bf16[128,256]{1,0:T(8,128)(2,1)S(1)}, u32[]{:S(2)}, u32[]{:S(2)}) collective-permute-start(bf16[128,256]{1,0:T(8,128)(2,1)} %refs_6_.1), channel_id=1, source_target_pairs={{0,2},{1,3},{2,0},{3,1},{4,6},{5,7},{6,4},{7,5},{8,10},{9,11},{10,... | collective-permute-start | bytes 196616 | tf_op jit(solution)/shard_map/ppermute | solution.py:58
  6.9 0.7 %copy-start.4 = (s32[1,1,8]{2,1,0:T(1,128)S(1)}, s32[1,1,8]{2,1,0:T(1,128)}, u32[]{:S(2)}) copy-start(s32[1,1,8]{2,1,0:T(1,128)} %rows_in.1) | copy-start | bytes 100
  6.9 0.7 %copy-start.5 = (s32[1,1,8]{2,1,0:T(1,128)S(1)}, s32[1,1,8]{2,1,0:T(1,128)}, u32[]{:S(2)}) copy-start(s32[1,1,8]{2,1,0:T(1,128)} %cols_in.1) | copy-start | bytes 100
  7.6 0.8 %copy-start.3 = (bf16[128,128]{1,0:T(8,128)(2,1)S(1)}, bf16[128,128]{1,0:T(8,128)(2,1)}, u32[]{:S(2)}) copy-start(bf16[128,128]{1,0:T(8,128)(2,1)} %refs_0_.1) | copy-start | bytes 98308
  8.7 8.5 %collective-permute-start.3 = (bf16[256,128]{1,0:T(8,128)(2,1)S(1)}, bf16[256,128]{1,0:T(8,128)(2,1)S(1)}, u32[]{:S(2)}, u32[]{:S(2)}) collective-permute-start(bf16[256,128]{1,0:T(8,128)(2,1)S(1)} %get-tuple-element.19), channel_id=1, source_target_pairs={{0,1},{1,3},{2,0},{3,2},{4,5},{5,7},{6,4},{7,6},{8,9},{9,11},{10,8... | collective-permute-start | bytes 196616 | tf_op jit(solution)/shard_map/ppermute | solution.py:43
  10.3 6.9 %collective-permute-start.4 = (bf16[256,128]{1,0:T(8,128)(2,1)S(1)}, bf16[256,128]{1,0:T(8,128)(2,1)S(1)}, u32[]{:S(2)}, u32[]{:S(2)}) collective-permute-start(bf16[256,128]{1,0:T(8,128)(2,1)S(1)} %get-tuple-element.20), channel_id=1, source_target_pairs={{0,3},{1,2},{2,1},{3,0},{4,7},{5,6},{6,5},{7,4},{8,11},{9,10},{10,... | collective-permute-start | bytes 196616 | tf_op jit(solution)/shard_map/ppermute | solution.py:43
  11.7 5.5 %copy-start.1 = (bf16[128,256]{1,0:T(8,128)(2,1)S(1)}, bf16[128,256]{1,0:T(8,128)(2,1)}, u32[]{:S(2)}) copy-start(bf16[128,256]{1,0:T(8,128)(2,1)} %refs_5_.1) | copy-start | bytes 196612
  11.7 5.5 %copy-start.2 = (bf16[128,256]{1,0:T(8,128)(2,1)S(1)}, bf16[128,256]{1,0:T(8,128)(2,1)}, u32[]{:S(2)}) copy-start(bf16[128,256]{1,0:T(8,128)(2,1)} %refs_6_.1) | copy-start | bytes 196612
  11.7 5.5 %collective-permute-start.5 = (bf16[256,128]{1,0:T(8,128)(2,1)S(1)}, bf16[256,128]{1,0:T(8,128)(2,1)S(1)}, u32[]{:S(2)}, u32[]{:S(2)}) collective-permute-start(bf16[256,128]{1,0:T(8,128)(2,1)S(1)} %get-tuple-element.21), channel_id=1, source_target_pairs={{0,2},{1,0},{2,3},{3,1},{4,6},{5,4},{6,7},{7,5},{8,10},{9,8},{10,1... | collective-permute-start | bytes 196616 | tf_op jit(solution)/shard_map/ppermute | solution.py:43
  17.8 1.6 %collective-permute-start.8 = (bf16[128,128]{1,0:T(8,128)(2,1)S(1)}, bf16[128,128]{1,0:T(8,128)(2,1)S(1)}, u32[]{:S(2)}, u32[]{:S(2)}) collective-permute-start(bf16[128,128]{1,0:T(8,128)(2,1)S(1)} %get-tuple-element.25), channel_id=1, source_target_pairs={{0,4},{4,0},{8,12},{12,8},{1,5},{5,1},{9,13},{13,9},{2,6},{6,2},{1... | collective-permute-start | bytes 98312 | tf_op jit(solution)/shard_map/ppermute | solution.py:58
  17.8 5.5 %collective-permute-start.7 = (bf16[256,128]{1,0:T(8,128)(2,1)S(1)}, bf16[256,128]{1,0:T(8,128)(2,1)S(1)}, u32[]{:S(2)}, u32[]{:S(2)}) collective-permute-start(bf16[256,128]{1,0:T(8,128)(2,1)S(1)} %get-tuple-element.23.refs_0_), channel_id=1, source_target_pairs={{0,1},{1,0},{2,3},{3,2},{4,5},{5,4},{6,7},{7,6},{8,9},{9,8},{10,11... | collective-permute-start | bytes 196616 | tf_op jit(solution)/shard_map/ppermute | solution.py:58
  19.4 4.0 %collective-permute-start.9 = (bf16[128,128]{1,0:T(8,128)(2,1)S(1)}, bf16[128,128]{1,0:T(8,128)(2,1)S(1)}, u32[]{:S(2)}, u32[]{:S(2)}) collective-permute-start(bf16[128,128]{1,0:T(8,128)(2,1)S(1)} %shard_map.100.refs_2_), channel_id=1, source_target_pairs={{0,1},{1,0},{2,3},{3,2},{4,5},{5,4},{6,7},{7,6},{8,9},{9,8},{10,11... | collective-permute-start | bytes 98312 | tf_op jit(solution)/shard_map/ppermute | solution.py:58
  23.7 3.8 %collective-permute-start.10 = (bf16[256,128]{1,0:T(8,128)(2,1)S(1)}, bf16[256,128]{1,0:T(8,128)(2,1)S(1)}, u32[]{:S(2)}, u32[]{:S(2)}) collective-permute-start(bf16[256,128]{1,0:T(8,128)(2,1)S(1)} %get-tuple-element.28), channel_id=1, source_target_pairs={{0,4},{4,8},{8,12},{12,0},{1,5},{5,9},{9,13},{13,1},{2,6},{6,10},{... | collective-permute-start | bytes 196616 | tf_op jit(solution)/shard_map/ppermute | solution.py:43
  23.7 4.7 %collective-permute-start.11 = (bf16[256,128]{1,0:T(8,128)(2,1)S(1)}, bf16[256,128]{1,0:T(8,128)(2,1)S(1)}, u32[]{:S(2)}, u32[]{:S(2)}) collective-permute-start(bf16[256,128]{1,0:T(8,128)(2,1)S(1)} %get-tuple-element.29), channel_id=1, source_target_pairs={{0,8},{4,12},{8,0},{12,4},{1,9},{5,13},{9,1},{13,5},{2,10},{6,14},... | collective-permute-start | bytes 196616 | tf_op jit(solution)/shard_map/ppermute | solution.py:43
  25.1 3.4 %collective-permute-start.12 = (bf16[256,128]{1,0:T(8,128)(2,1)S(1)}, bf16[256,128]{1,0:T(8,128)(2,1)S(1)}, u32[]{:S(2)}, u32[]{:S(2)}) collective-permute-start(bf16[256,128]{1,0:T(8,128)(2,1)S(1)} %get-tuple-element.30), channel_id=1, source_target_pairs={{0,12},{4,0},{8,4},{12,8},{1,13},{5,1},{9,5},{13,9},{2,14},{6,2},{... | collective-permute-start | bytes 196616 | tf_op jit(solution)/shard_map/ppermute | solution.py:43

commit v20 on v19

--- a/solution.py
+++ b/solution.py
@@ -264,13 +264,15 @@
     forward = dict(flops=2 * down * across * width, need=2 * dense_bytes)
     if paired:
         layers = 2
+        cotangents = [cotangent, swap(cotangent, "col", 2)]
         own, *sends = call(
             functools.partial(paired_forward_kernel, n_row),
             [((2 * nodes, width), NARROW)] * 4,
             [VMEM] * (1 + n_row),
+            after=cotangents[1:],
             **forward,
         )(near, features, *gathered)
-        layer_call, cotangents = paired_layer_kernel, [cotangent, swap(cotangent, "col", 2)]
+        layer_call = paired_layer_kernel
     else:
         layers = 1
         own, *sends = call(

time: 29.8 us -> 30.8 us (1.034)
  waiting for transfers between devices: 7.72 us -> 9.05 us
    ppermute x7, waiting for transfers between devices: 2.8 us -> 4.28 us  [swap(): return lax.ppermute(value, axis, [(s, s ^ distance) for s in range(n)])]
    ppermute x7, starting transfers between devices: 9.03 us -> 9.46 us  [swap(): return lax.ppermute(value, axis, [(s, s ^ distance) for s in range(n)])]
    ppermute x6, starting transfers between devices: 7.4 us -> 6.97 us  [exchange(): lax.ppermute(send, axis, [(s, target(s, d)) for s in range(n)])]
  transfers between devices with their start and end apart: 13 -> 13, of which waited for: 4 -> 8; matrix products, arithmetic and copies ran while one was open for 0% -> 0% of each run, Pallas kernels for 7% -> 6%
where the time goes in v20:
time: 30.8 us; the launch traced here: 30.4 us
  starting transfers between devices  16.4 us (53%)
  waiting for transfers between devices  9.05 us (29%)
  Pallas kernels  3.49 us (11%)
  between operations  1.43 us (5%)
    ppermute x7, starting transfers between devices, swap(): return lax.ppermute(value, axis, [(s, s ^ distance) for s in range(n)])  9.46 us
    ppermute x6, starting transfers between devices, exchange(): lax.ppermute(send, axis, [(s, target(s, d)) for s in range(n)])  6.97 us
    ppermute x6, waiting for transfers between devices, exchange(): lax.ppermute(send, axis, [(s, target(s, d)) for s in range(n)])  4.76 us
    ppermute x7, waiting for transfers between devices, swap(): return lax.ppermute(value, axis, [(s, s ^ distance) for s in range(n)])  4.28 us
    pallas_call x1, Pallas kernels, per_device(): call(functools.partial(last_kernel, scale), [((nodes, width), NARROW), ((...  0.7 us
    pallas_call x1, Pallas kernels, per_device(): act, = call(act_kernel, [((nodes, hidden), NARROW)], [VMEM])(pre)  0.65 us
    pallas_call x1, Pallas kernels, per_device(): call(functools.partial(dense_kernel, nodes // side, paired), [((down, acr...  0.64 us
  transfers between devices with their start and end apart: 13, of which 8 were waited for; matrix products, arithmetic and copies ran while one was open for 0% of the time, Pallas kernels for 6%

profile of v20, /device:TPU:0, one launch (start us, length us, event | category | flops | bytes accessed | tf_op | source)
XLA Modules:
  0.0 30.4 jit_solution(5085121046896757623)
XLA Ops:
  0.6 0.0 copy-start
  0.6 4.1 %collective-permute-start = (bf16[128,256]{1,0:T(8,128)(2,1)}, bf16[128,256]{1,0:T(8,128)(2,1)S(1)}, u32[]{:S(2)}, u32[]{:S(2)}) collective-permute-start(bf16[128,256]{1,0:T(8,128)(2,1)} %refs_6_.1), channel_id=1, source_target_pairs={{0,2},{1,3},{2,0},{3,1},{4,6},{5,7},{6,4},{7,5},{8,10},{9,11},{10,... | collective-permute-start | bytes 196616 | tf_op jit(solution)/shard_map/ppermute | solution.py:58
  4.7 1.5 %collective-permute-start.1 = (bf16[128,128]{1,0:T(8,128)(2,1)}, bf16[128,128]{1,0:T(8,128)(2,1)S(1)}, u32[]{:S(2)}, u32[]{:S(2)}) collective-permute-start(bf16[128,128]{1,0:T(8,128)(2,1)} %refs_2_.1), channel_id=1, source_target_pairs={{0,8},{4,12},{8,0},{12,4},{1,9},{5,13},{9,1},{13,5},{2,10},{6,14},... | collective-permute-start | bytes 98312 | tf_op jit(solution)/shard_map/ppermute | solution.py:58
  6.2 0.0 collective-permute-start.2
  6.2 0.6 %collective-permute-start.3 = (bf16[128,128]{1,0:T(8,128)(2,1)}, bf16[128,128]{1,0:T(8,128)(2,1)S(1)}, u32[]{:S(2)}, u32[]{:S(2)}) collective-permute-start(bf16[128,128]{1,0:T(8,128)(2,1)} %refs_2_.1), channel_id=1, source_target_pairs={{0,4},{4,0},{8,12},{12,8},{1,5},{5,1},{9,13},{13,9},{2,6},{6,2},{1... | collective-permute-start | bytes 98312 | tf_op jit(solution)/shard_map/ppermute | solution.py:58
  6.9 0.0 copy-start.4
  6.9 0.0 copy-start.5
  7.6 0.0 copy-done
  7.6 0.0 copy-done.4
  7.6 0.0 copy-done.5
  7.6 0.0 copy-start.3
  7.7 0.6 %shard_map.95.near.refs_1_ = bf16[512,512]{1,0:T(8,128)(2,1)S(1)} custom-call(bf16[512,512]{1,0:T(8,128)(2,1)S(1)} %shard_map.94.blank, bf16[1,1,8,128,128]{4,3,2,1,0:T(8,128)(2,1)S(1)} %copy-done, s32[1,1,8]{2,1,0:T(1,128)S(1)} %copy-done.4, s32[1,1,8]{2,1,0:T(1,128)S(1)} %copy-done.5, s32[1,1]{1,0:T(1,128)S(6)} %copy.12.count_in), custom_call_target="tpu_custom_call", output_to_operand_aliasing={{}: (0, {})} | custom-call | bytes 1048576 | tf_op jit(solution)/shard_map/pallas_call | solution.py:250
  8.3 0.6 %collective-permute-done.1.refs_3_ = bf16[128,128]{1,0:T(8,128)(2,1)S(1)} collective-permute-done((bf16[128,128]{1,0:T(8,128)(2,1)}, bf16[128,128]{1,0:T(8,128)(2,1)S(1)}, u32[]{:S(2)}, u32[]{:S(2)}) %collective-permute-start.1) | collective-permute-done | bytes 32800 | tf_op jit(solution)/shard_map/ppermute | solution.py:58
  8.9 0.9 %collective-permute-done.2.refs_4_ = bf16[128,128]{1,0:T(8,128)(2,1)S(1)} collective-permute-done((bf16[128,128]{1,0:T(8,128)(2,1)}, bf16[128,128]{1,0:T(8,128)(2,1)S(1)}, u32[]{:S(2)}, u32[]{:S(2)}) %collective-permute-start.2) | collective-permute-done | bytes 32800 | tf_op jit(solution)/shard_map/ppermute | solution.py:58
  9.8 0.0 collective-permute-done.3.refs_5_
  9.8 0.0 collective-permute-done.refs_0_.refs_7_
  9.8 0.0 copy-done.3
  9.8 0.3 shard_map.97
  10.1 1.6 %collective-permute-start.4 = (bf16[256,128]{1,0:T(8,128)(2,1)S(1)}, bf16[256,128]{1,0:T(8,128)(2,1)S(1)}, u32[]{:S(2)}, u32[]{:S(2)}) collective-permute-start(bf16[256,128]{1,0:T(8,128)(2,1)S(1)} %get-tuple-element.19), channel_id=1, source_target_pairs={{0,1},{1,3},{2,0},{3,2},{4,5},{5,7},{6,4},{7,6},{8,9},{9,11},{10,8... | collective-permute-start | bytes 196616 | tf_op jit(solution)/shard_map/ppermute | solution.py:43
  11.7 0.7 %collective-permute-start.5 = (bf16[256,128]{1,0:T(8,128)(2,1)S(1)}, bf16[256,128]{1,0:T(8,128)(2,1)S(1)}, u32[]{:S(2)}, u32[]{:S(2)}) collective-permute-start(bf16[256,128]{1,0:T(8,128)(2,1)S(1)} %get-tuple-element.20), channel_id=1, source_target_pairs={{0,3},{1,2},{2,1},{3,0},{4,7},{5,6},{6,5},{7,4},{8,11},{9,10},{10,... | collective-permute-start | bytes 196616 | tf_op jit(solution)/shard_map/ppermute | solution.py:43
  12.4 0.0 copy-start.1
  12.4 0.0 copy-start.2
  12.4 1.9 %collective-permute-start.6 = (bf16[256,128]{1,0:T(8,128)(2,1)S(1)}, bf16[256,128]{1,0:T(8,128)(2,1)S(1)}, u32[]{:S(2)}, u32[]{:S(2)}) collective-permute-start(bf16[256,128]{1,0:T(8,128)(2,1)S(1)} %get-tuple-element.21), channel_id=1, source_target_pairs={{0,2},{1,0},{2,3},{3,1},{4,6},{5,4},{6,7},{7,5},{8,10},{9,8},{10,1... | collective-permute-start | bytes 196616 | tf_op jit(solution)/shard_map/ppermute | solution.py:43
  14.4 0.3 %shard_map.96.refs_0_.matrix = bf16[512,512]{1,0:T(8,128)(2,1)S(1)} custom-call(bf16[512,512]{1,0:T(8,128)(2,1)S(1)} %shard_map.95.near.refs_1_), custom_call_target="tpu_custom_call" | custom-call | bytes 1572864 | tf_op jit(solution)/shard_map/pallas_call | solution.py:286
  14.7 2.5 %collective-permute-done.4.refs_2_ = bf16[256,128]{1,0:T(8,128)(2,1)S(1)} collective-permute-done((bf16[256,128]{1,0:T(8,128)(2,1)S(1)}, bf16[256,128]{1,0:T(8,128)(2,1)S(1)}, u32[]{:S(2)}, u32[]{:S(2)}) %collective-permute-start.4) | collective-permute-done | bytes 65568 | tf_op jit(solution)/shard_map/ppermute | solution.py:43
  17.2 0.7 %collective-permute-done.5.refs_3_ = bf16[256,128]{1,0:T(8,128)(2,1)S(1)} collective-permute-done((bf16[256,128]{1,0:T(8,128)(2,1)S(1)}, bf16[256,128]{1,0:T(8,128)(2,1)S(1)}, u32[]{:S(2)}, u32[]{:S(2)}) %collective-permute-start.5) | collective-permute-done | bytes 65568 | tf_op jit(solution)/shard_map/ppermute | solution.py:43
  17.9 0.0 collective-permute-done.6.refs_4_
  17.9 0.0 copy-done.1
  17.9 0.0 copy-done.2
  17.9 0.5 %shard_map.98 = (bf16[256,128]{1,0:T(8,128)(2,1)S(1)}, f32[128,128]{1,0:T(8,128)S(1)}, bf16[128,128]{1,0:T(8,128)(2,1)S(1)}, f32[128,256]{1,0:T(8,128)S(1)}) custom-call(bf16[512,512]{1,0:T(8,128)(2,1)S(1)} %shard_map.96.refs_0_.matrix, bf16[256,128]{1,0:T(8,128)(2,1)S(1)} %get-tuple-element.18.refs_1_, bf16[256,128]{1,0:T(8,128)(2,1)S(1)} %collective-permute-done.4.refs_2_, ...), custom_call_target="tpu_custom_call" | custom-call | flops 117440512 | tf_op jit(solution)/shard_map/pallas_call | solution.py:295
  18.4 0.1 collective-permute-start.8
  18.5 2.0 %collective-permute-start.7 = (bf16[256,128]{1,0:T(8,128)(2,1)S(1)}, bf16[256,128]{1,0:T(8,128)(2,1)S(1)}, u32[]{:S(2)}, u32[]{:S(2)}) collective-permute-start(bf16[256,128]{1,0:T(8,128)(2,1)S(1)} %get-tuple-element.23.refs_0_), channel_id=1, source_target_pairs={{0,1},{1,0},{2,3},{3,2},{4,5},{5,4},{6,7},{7,6},{8,9},{9,8},{10,11... | collective-permute-start | bytes 196616 | tf_op jit(solution)/shard_map/ppermute | solution.py:58
  20.5 0.0 collective-permute-done.8.came
  20.5 1.2 %collective-permute-start.9 = (bf16[128,128]{1,0:T(8,128)(2,1)S(1)}, bf16[128,128]{1,0:T(8,128)(2,1)S(1)}, u32[]{:S(2)}, u32[]{:S(2)}) collective-permute-start(bf16[128,128]{1,0:T(8,128)(2,1)S(1)} %shard_map.100.refs_2_), channel_id=1, source_target_pairs={{0,1},{1,0},{2,3},{3,2},{4,5},{5,4},{6,7},{7,6},{8,9},{9,8},{10,11... | collective-permute-start | bytes 98312 | tf_op jit(solution)/shard_map/ppermute | solution.py:58
  21.7 1.5 %collective-permute-done.7.refs_1_ = bf16[256,128]{1,0:T(8,128)(2,1)S(1)} collective-permute-done((bf16[256,128]{1,0:T(8,128)(2,1)S(1)}, bf16[256,128]{1,0:T(8,128)(2,1)S(1)}, u32[]{:S(2)}, u32[]{:S(2)}) %collective-permute-start.7) | collective-permute-done | bytes 65568 | tf_op jit(solution)/shard_map/ppermute | solution.py:58
  23.2 1.3 %collective-permute-done.9.refs_3_ = bf16[128,128]{1,0:T(8,128)(2,1)S(1)} collective-permute-done((bf16[128,128]{1,0:T(8,128)(2,1)S(1)}, bf16[128,128]{1,0:T(8,128)(2,1)S(1)}, u32[]{:S(2)}, u32[]{:S(2)}) %collective-permute-start.9) | collective-permute-done | bytes 32800 | tf_op jit(solution)/shard_map/ppermute | solution.py:58
  24.5 0.3 %shard_map.101 = (f32[128,128]{1,0:T(8,128)S(1)}, bf16[128,128]{1,0:T(8,128)(2,1)S(1)}, bf16[256,128]{1,0:T(8,128)(2,1)S(1)}, bf16[256,128]{1,0:T(8,128)(2,1)S(1)}, bf16[256,128]{1,0:T(8,128)(2,1)S(1)}) custom-call(bf16[512,512]{1,0:T(8,128)(2,1)S(1)} %shard_map.96.refs_0_.matrix, bf16[256,128]{1,0:T(8,128)(2,1)S(1)} %get-tuple-element.23.refs_0_, ...), custom_call_target="tpu_custom_call" | custom-call | flops 67108864 | bytes 1048576 | tf_op jit(solution)/shard_map/pallas_call | solution.py:316
  24.8 0.1 collective-permute-start.10
  24.8 1.3 %collective-permute-start.11 = (bf16[256,128]{1,0:T(8,128)(2,1)S(1)}, bf16[256,128]{1,0:T(8,128)(2,1)S(1)}, u32[]{:S(2)}, u32[]{:S(2)}) collective-permute-start(bf16[256,128]{1,0:T(8,128)(2,1)S(1)} %get-tuple-element.29), channel_id=1, source_target_pairs={{0,8},{4,12},{8,0},{12,4},{1,9},{5,13},{9,1},{13,5},{2,10},{6,14},... | collective-permute-start | bytes 196616 | tf_op jit(solution)/shard_map/ppermute | solution.py:43
  26.1 1.4 %collective-permute-start.12 = (bf16[256,128]{1,0:T(8,128)(2,1)S(1)}, bf16[256,128]{1,0:T(8,128)(2,1)S(1)}, u32[]{:S(2)}, u32[]{:S(2)}) collective-permute-start(bf16[256,128]{1,0:T(8,128)(2,1)S(1)} %get-tuple-element.30), channel_id=1, source_target_pairs={{0,12},{4,0},{8,4},{12,8},{1,13},{5,1},{9,5},{13,9},{2,14},{6,2},{... | collective-permute-start | bytes 196616 | tf_op jit(solution)/shard_map/ppermute | solution.py:43
  27.5 0.7 %shard_map.99 = bf16[128,256]{1,0:T(8,128)(2,1)} custom-call(f32[128,256]{1,0:T(8,128)S(1)} %get-tuple-element.22.pre), custom_call_target="tpu_custom_call" | custom-call | tf_op jit(solution)/shard_map/pallas_call | solution.py:313
  28.1 0.5 %collective-permute-done.10.refs_0_ = bf16[256,128]{1,0:T(8,128)(2,1)S(1)} collective-permute-done((bf16[256,128]{1,0:T(8,128)(2,1)S(1)}, bf16[256,128]{1,0:T(8,128)(2,1)S(1)}, u32[]{:S(2)}, u32[]{:S(2)}) %collective-permute-start.10) | collective-permute-done | bytes 65568 | tf_op jit(solution)/shard_map/ppermute | solution.py:43
  28.6 1.1 %collective-permute-done.11.refs_1_ = bf16[256,128]{1,0:T(8,128)(2,1)S(1)} collective-permute-done((bf16[256,128]{1,0:T(8,128)(2,1)S(1)}, bf16[256,128]{1,0:T(8,128)(2,1)S(1)}, u32[]{:S(2)}, u32[]{:S(2)}) %collective-permute-start.11) | collective-permute-done | bytes 65568 | tf_op jit(solution)/shard_map/ppermute | solution.py:43
  29.7 0.0 collective-permute-done.12.refs_2_
  29.7 0.7 %shard_map.102 = (bf16[128,128]{1,0:T(8,128)(2,1)}, f32[128,256]{1,0:T(8,128)}) custom-call(f32[128,128]{1,0:T(8,128)S(1)} %get-tuple-element.26.own, bf16[128,128]{1,0:T(8,128)(2,1)S(1)} %get-tuple-element.27.kept, bf16[256,128]{1,0:T(8,128)(2,1)S(1)} %collective-permute-done.10.refs_0_, bf16[256,128]{1,0:T(8,128)(2,1)S(1)} %collective-permute-done.11.refs_1_, ...), custom_call_target="tpu_custom_call" | custom-call | tf_op jit(solution)/shard_map/pallas_call | solution.py:326
  (2 shorter events, 0.0 us)
Async XLA Ops:
  0.6 7.0 %copy-start = (bf16[1,1,8,128,128]{4,3,2,1,0:T(8,128)(2,1)S(1)}, bf16[1,1,8,128,128]{4,3,2,1,0:T(8,128)(2,1)}, u32[]{:S(2)}) copy-start(bf16[1,1,8,128,128]{4,3,2,1,0:T(8,128)(2,1)} %vals.1) | copy-start | bytes 786436
  0.6 9.2 %collective-permute-start = (bf16[128,256]{1,0:T(8,128)(2,1)}, bf16[128,256]{1,0:T(8,128)(2,1)S(1)}, u32[]{:S(2)}, u32[]{:S(2)}) collective-permute-start(bf16[128,256]{1,0:T(8,128)(2,1)} %refs_6_.1), channel_id=1, source_target_pairs={{0,2},{1,3},{2,0},{3,1},{4,6},{5,7},{6,4},{7,5},{8,10},{9,11},{10,... | collective-permute-start | bytes 196616 | tf_op jit(solution)/shard_map/ppermute | solution.py:58
  4.7 4.1 %collective-permute-start.1 = (bf16[128,128]{1,0:T(8,128)(2,1)}, bf16[128,128]{1,0:T(8,128)(2,1)S(1)}, u32[]{:S(2)}, u32[]{:S(2)}) collective-permute-start(bf16[128,128]{1,0:T(8,128)(2,1)} %refs_2_.1), channel_id=1, source_target_pairs={{0,8},{4,12},{8,0},{12,4},{1,9},{5,13},{9,1},{13,5},{2,10},{6,14},... | collective-permute-start | bytes 98312 | tf_op jit(solution)/shard_map/ppermute | solution.py:58
  6.2 3.6 %collective-permute-start.2 = (bf16[128,128]{1,0:T(8,128)(2,1)}, bf16[128,128]{1,0:T(8,128)(2,1)S(1)}, u32[]{:S(2)}, u32[]{:S(2)}) collective-permute-start(bf16[128,128]{1,0:T(8,128)(2,1)} %refs_2_.1), channel_id=1, source_target_pairs={{0,12},{4,8},{8,4},{12,0},{1,13},{5,9},{9,5},{13,1},{2,14},{6,10},... | collective-permute-start | bytes 98312 | tf_op jit(solution)/shard_map/ppermute | solution.py:58
  6.2 3.6 %collective-permute-start.3 = (bf16[128,128]{1,0:T(8,128)(2,1)}, bf16[128,128]{1,0:T(8,128)(2,1)S(1)}, u32[]{:S(2)}, u32[]{:S(2)}) collective-permute-start(bf16[128,128]{1,0:T(8,128)(2,1)} %refs_2_.1), channel_id=1, source_target_pairs={{0,4},{4,0},{8,12},{12,8},{1,5},{5,1},{9,13},{13,9},{2,6},{6,2},{1... | collective-permute-start | bytes 98312 | tf_op jit(solution)/shard_map/ppermute | solution.py:58
  6.9 0.7 %copy-start.4 = (s32[1,1,8]{2,1,0:T(1,128)S(1)}, s32[1,1,8]{2,1,0:T(1,128)}, u32[]{:S(2)}) copy-start(s32[1,1,8]{2,1,0:T(1,128)} %rows_in.1) | copy-start | bytes 100
  6.9 0.7 %copy-start.5 = (s32[1,1,8]{2,1,0:T(1,128)S(1)}, s32[1,1,8]{2,1,0:T(1,128)}, u32[]{:S(2)}) copy-start(s32[1,1,8]{2,1,0:T(1,128)} %cols_in.1) | copy-start | bytes 100
  7.6 2.2 %copy-start.3 = (bf16[128,128]{1,0:T(8,128)(2,1)S(1)}, bf16[128,128]{1,0:T(8,128)(2,1)}, u32[]{:S(2)}) copy-start(bf16[128,128]{1,0:T(8,128)(2,1)} %refs_2_.1) | copy-start | bytes 98308
  10.1 7.1 %collective-permute-start.4 = (bf16[256,128]{1,0:T(8,128)(2,1)S(1)}, bf16[256,128]{1,0:T(8,128)(2,1)S(1)}, u32[]{:S(2)}, u32[]{:S(2)}) collective-permute-start(bf16[256,128]{1,0:T(8,128)(2,1)S(1)} %get-tuple-element.19), channel_id=1, source_target_pairs={{0,1},{1,3},{2,0},{3,2},{4,5},{5,7},{6,4},{7,6},{8,9},{9,11},{10,8... | collective-permute-start | bytes 196616 | tf_op jit(solution)/shard_map/ppermute | solution.py:43
  11.7 6.2 %collective-permute-start.5 = (bf16[256,128]{1,0:T(8,128)(2,1)S(1)}, bf16[256,128]{1,0:T(8,128)(2,1)S(1)}, u32[]{:S(2)}, u32[]{:S(2)}) collective-permute-start(bf16[256,128]{1,0:T(8,128)(2,1)S(1)} %get-tuple-element.20), channel_id=1, source_target_pairs={{0,3},{1,2},{2,1},{3,0},{4,7},{5,6},{6,5},{7,4},{8,11},{9,10},{10,... | collective-permute-start | bytes 196616 | tf_op jit(solution)/shard_map/ppermute | solution.py:43
  12.4 5.5 %copy-start.1 = (bf16[128,256]{1,0:T(8,128)(2,1)S(1)}, bf16[128,256]{1,0:T(8,128)(2,1)}, u32[]{:S(2)}) copy-start(bf16[128,256]{1,0:T(8,128)(2,1)} %refs_6_.1) | copy-start | bytes 196612
  12.4 5.5 %copy-start.2 = (bf16[128,256]{1,0:T(8,128)(2,1)S(1)}, bf16[128,256]{1,0:T(8,128)(2,1)}, u32[]{:S(2)}) copy-start(bf16[128,256]{1,0:T(8,128)(2,1)} %refs_5_.1) | copy-start | bytes 196612
  12.4 5.5 %collective-permute-start.6 = (bf16[256,128]{1,0:T(8,128)(2,1)S(1)}, bf16[256,128]{1,0:T(8,128)(2,1)S(1)}, u32[]{:S(2)}, u32[]{:S(2)}) collective-permute-start(bf16[256,128]{1,0:T(8,128)(2,1)S(1)} %get-tuple-element.21), channel_id=1, source_target_pairs={{0,2},{1,0},{2,3},{3,1},{4,6},{5,4},{6,7},{7,5},{8,10},{9,8},{10,1... | collective-permute-start | bytes 196616 | tf_op jit(solution)/shard_map/ppermute | solution.py:43
  18.4 2.0 %collective-permute-start.8 = (bf16[128,128]{1,0:T(8,128)(2,1)S(1)}, bf16[128,128]{1,0:T(8,128)(2,1)S(1)}, u32[]{:S(2)}, u32[]{:S(2)}) collective-permute-start(bf16[128,128]{1,0:T(8,128)(2,1)S(1)} %get-tuple-element.25), channel_id=1, source_target_pairs={{0,4},{4,0},{8,12},{12,8},{1,5},{5,1},{9,13},{13,9},{2,6},{6,2},{1... | collective-permute-start | bytes 98312 | tf_op jit(solution)/shard_map/ppermute | solution.py:58
  18.5 4.6 %collective-permute-start.7 = (bf16[256,128]{1,0:T(8,128)(2,1)S(1)}, bf16[256,128]{1,0:T(8,128)(2,1)S(1)}, u32[]{:S(2)}, u32[]{:S(2)}) collective-permute-start(bf16[256,128]{1,0:T(8,128)(2,1)S(1)} %get-tuple-element.23.refs_0_), channel_id=1, source_target_pairs={{0,1},{1,0},{2,3},{3,2},{4,5},{5,4},{6,7},{7,6},{8,9},{9,8},{10,11... | collective-permute-start | bytes 196616 | tf_op jit(solution)/shard_map/ppermute | solution.py:58
  20.5 4.0 %collective-permute-start.9 = (bf16[128,128]{1,0:T(8,128)(2,1)S(1)}, bf16[128,128]{1,0:T(8,128)(2,1)S(1)}, u32[]{:S(2)}, u32[]{:S(2)}) collective-permute-start(bf16[128,128]{1,0:T(8,128)(2,1)S(1)} %shard_map.100.refs_2_), channel_id=1, source_target_pairs={{0,1},{1,0},{2,3},{3,2},{4,5},{5,4},{6,7},{7,6},{8,9},{9,8},{10,11... | collective-permute-start | bytes 98312 | tf_op jit(solution)/shard_map/ppermute | solution.py:58
  24.8 3.8 %collective-permute-start.10 = (bf16[256,128]{1,0:T(8,128)(2,1)S(1)}, bf16[256,128]{1,0:T(8,128)(2,1)S(1)}, u32[]{:S(2)}, u32[]{:S(2)}) collective-permute-start(bf16[256,128]{1,0:T(8,128)(2,1)S(1)} %get-tuple-element.28), channel_id=1, source_target_pairs={{0,4},{4,8},{8,12},{12,0},{1,5},{5,9},{9,13},{13,1},{2,6},{6,10},{... | collective-permute-start | bytes 196616 | tf_op jit(solution)/shard_map/ppermute | solution.py:43
  24.8 4.9 %collective-permute-start.11 = (bf16[256,128]{1,0:T(8,128)(2,1)S(1)}, bf16[256,128]{1,0:T(8,128)(2,1)S(1)}, u32[]{:S(2)}, u32[]{:S(2)}) collective-permute-start(bf16[256,128]{1,0:T(8,128)(2,1)S(1)} %get-tuple-element.29), channel_id=1, source_target_pairs={{0,8},{4,12},{8,0},{12,4},{1,9},{5,13},{9,1},{13,5},{2,10},{6,14},... | collective-permute-start | bytes 196616 | tf_op jit(solution)/shard_map/ppermute | solution.py:43
  26.1 3.6 %collective-permute-start.12 = (bf16[256,128]{1,0:T(8,128)(2,1)S(1)}, bf16[256,128]{1,0:T(8,128)(2,1)S(1)}, u32[]{:S(2)}, u32[]{:S(2)}) collective-permute-start(bf16[256,128]{1,0:T(8,128)(2,1)S(1)} %get-tuple-element.30), channel_id=1, source_target_pairs={{0,12},{4,0},{8,4},{12,8},{1,13},{5,1},{9,5},{13,9},{2,14},{6,2},{... | collective-permute-start | bytes 196616 | tf_op jit(solution)/shard_map/ppermute | solution.py:43

commit v21 on v19

--- a/solution.py
+++ b/solution.py
@@ -166,30 +166,18 @@
     halve(term, mine, other)
 
 
-def in_middle():
-    my_col = lax.axis_index("col")
-    return (my_col == 1) | (my_col == 2)
-
-
 def paired_forward_kernel(n, matrix, *refs):
-    operands, (own, first, second, third) = refs[:n], refs[n:]
-    product = dot(matrix[...], stack(operands)).astype(own.dtype)
-    rows = own.shape[0]
-    same, other = product[:rows], product[rows:]
-    middle = in_middle()
-    own[...] = same
-    first[...] = jnp.where(middle, same, other)
-    second[...] = other
-    third[...] = jnp.where(middle, other, same)
+    operands, (same, other) = refs[:n], refs[n:]
+    product = dot(matrix[...], stack(operands)).astype(same.dtype)
+    rows = same.shape[0]
+    same[...] = product[:rows]
+    other[...] = product[rows:]
 
 
 def paired_layer_kernel(own, first, second, third, weight, cotangent, beyond, *refs):
     back_out, mine, other, pre_out = refs
     nodes = cotangent.shape[0]
-    middle = in_middle()
-    partner = jnp.where(middle, third[...], first[...])
-    side = jnp.where(middle, first[...], third[...])
-    total = (wide(own[...]) + wide(partner)) + (wide(second[...]) + wide(side))
+    total = (wide(own[...]) + wide(second[...])) + (wide(first[...]) + wide(third[...]))
     high_col = lax.axis_index("col") >= 2
     here, there = cotangent[...], beyond[...]
     both = jnp.concatenate(
@@ -264,12 +252,13 @@
     forward = dict(flops=2 * down * across * width, need=2 * dense_bytes)
     if paired:
         layers = 2
-        own, *sends = call(
+        own, other = call(
             functools.partial(paired_forward_kernel, n_row),
-            [((2 * nodes, width), NARROW)] * 4,
+            [((2 * nodes, width), NARROW)] * 2,
             [VMEM] * (1 + n_row),
             **forward,
         )(near, features, *gathered)
+        parts = [swap(send, "col", d) for d, send in enumerate([other, own, other], 1)]
         layer_call, cotangents = paired_layer_kernel, [cotangent, swap(cotangent, "col", 2)]
     else:
         layers = 1
@@ -280,7 +269,7 @@
             **forward,
         )(near, features, *gathered)
         layer_call, cotangents = layer_kernel, [cotangent]
-    parts = exchange(sends, "col", True)
+        parts = exchange(sends, "col", True)
     (far,) = call(
         functools.partial(turn_kernel, side),
         [((across, down), NARROW)],

time: 29.8 us -> 29.8 us (level)
  waiting for transfers between devices: 7.72 us -> 9.53 us
  starting transfers between devices: 16.4 us -> 14.7 us
    ppermute x7 -> x10, waiting for transfers between devices: 2.8 us -> 8.17 us  [swap(): return lax.ppermute(value, axis, [(s, s ^ distance) for s in range(n)])]
    ppermute x6 -> x3, starting transfers between devices: 7.4 us -> 2.81 us  [exchange(): lax.ppermute(send, axis, [(s, target(s, d)) for s in range(n)])]
    ppermute x6 -> x3, waiting for transfers between devices: 4.92 us -> 1.36 us  [exchange(): lax.ppermute(send, axis, [(s, target(s, d)) for s in range(n)])]
    ppermute x7 -> x10, starting transfers between devices: 9.03 us -> 11.9 us  [swap(): return lax.ppermute(value, axis, [(s, s ^ distance) for s in range(n)])]
  transfers between devices with their start and end apart: 13 -> 13, of which waited for: 4 -> 6; matrix products, arithmetic and copies ran while one was open for 0% -> 0% of each run, Pallas kernels for 7% -> 7%
where the time goes in v21:
time: 29.8 us; the launch traced here: 29.3 us
  starting transfers between devices  14.7 us (49%)
  waiting for transfers between devices  9.53 us (32%)
  Pallas kernels  3.5 us (12%)
  between operations  1.45 us (5%)
    ppermute x10, starting transfers between devices, swap(): return lax.ppermute(value, axis, [(s, s ^ distance) for s in range(n)])  11.9 us
    ppermute x10, waiting for transfers between devices, swap(): return lax.ppermute(value, axis, [(s, s ^ distance) for s in range(n)])  8.17 us
    ppermute x3, starting transfers between devices, exchange(): lax.ppermute(send, axis, [(s, target(s, d)) for s in range(n)])  2.81 us
    ppermute x3, waiting for transfers between devices, exchange(): lax.ppermute(send, axis, [(s, target(s, d)) for s in range(n)])  1.36 us
    pallas_call x1, Pallas kernels, per_device(): call(functools.partial(last_kernel, scale), [((nodes, width), NARROW), ((...  0.7 us
    pallas_call x1, Pallas kernels, per_device(): call(functools.partial(dense_kernel, nodes // side, paired), [((down, acr...  0.66 us
    pallas_call x1, Pallas kernels, per_device(): act, = call(act_kernel, [((nodes, hidden), NARROW)], [VMEM])(pre)  0.65 us
  transfers between devices with their start and end apart: 13, of which 6 were waited for; matrix products, arithmetic and copies ran while one was open for 0% of the time, Pallas kernels for 7%

profile of v21, /device:TPU:0, one launch (start us, length us, event | category | flops | bytes accessed | tf_op | source)
XLA Modules:
  0.0 29.3 jit_solution(3899760583363297538)
XLA Ops:
  0.6 0.0 copy-start
  0.6 2.4 %collective-permute-start.1 = (bf16[128,128]{1,0:T(8,128)(2,1)}, bf16[128,128]{1,0:T(8,128)(2,1)S(1)}, u32[]{:S(2)}, u32[]{:S(2)}) collective-permute-start(bf16[128,128]{1,0:T(8,128)(2,1)} %refs_0_.1), channel_id=1, source_target_pairs={{0,12},{4,8},{8,4},{12,0},{1,13},{5,9},{9,5},{13,1},{2,14},{6,10},... | collective-permute-start | bytes 98312 | tf_op jit(solution)/shard_map/ppermute | solution.py:58
  3.1 0.6 %collective-permute-start = (bf16[128,128]{1,0:T(8,128)(2,1)}, bf16[128,128]{1,0:T(8,128)(2,1)S(1)}, u32[]{:S(2)}, u32[]{:S(2)}) collective-permute-start(bf16[128,128]{1,0:T(8,128)(2,1)} %refs_0_.1), channel_id=1, source_target_pairs={{0,8},{4,12},{8,0},{12,4},{1,9},{5,13},{9,1},{13,5},{2,10},{6,14},... | collective-permute-start | bytes 98312 | tf_op jit(solution)/shard_map/ppermute | solution.py:58
  3.7 0.0 collective-permute-start.2
  3.8 2.8 %collective-permute-start.6 = (bf16[128,256]{1,0:T(8,128)(2,1)}, bf16[128,256]{1,0:T(8,128)(2,1)S(1)}, u32[]{:S(2)}, u32[]{:S(2)}) collective-permute-start(bf16[128,256]{1,0:T(8,128)(2,1)} %refs_6_.1), channel_id=1, source_target_pairs={{0,2},{1,3},{2,0},{3,1},{4,6},{5,7},{6,4},{7,5},{8,10},{9,11},{10,... | collective-permute-start | bytes 196616 | tf_op jit(solution)/shard_map/ppermute | solution.py:58
  6.6 0.0 copy-start.4
  6.7 0.0 copy-start.5
  7.3 0.0 copy-done
  7.3 0.0 copy-done.4
  7.3 0.0 copy-done.5
  7.4 0.0 copy-start.3
  7.4 0.7 %shard_map.95.near.matrix = bf16[512,512]{1,0:T(8,128)(2,1)S(1)} custom-call(bf16[512,512]{1,0:T(8,128)(2,1)S(1)} %shard_map.94.blank, bf16[1,1,8,128,128]{4,3,2,1,0:T(8,128)(2,1)S(1)} %copy-done, s32[1,1,8]{2,1,0:T(1,128)S(1)} %copy-done.4, s32[1,1,8]{2,1,0:T(1,128)S(1)} %copy-done.5, s32[1,1]{1,0:T(1,128)S(6)} %copy.12.count_in), custom_call_target="tpu_custom_call", output_to_operand_aliasing={{}: (0, {})} | custom-call | bytes 1048576 | tf_op jit(solution)/shard_map/pallas_call | solution.py:238
  8.0 0.0 collective-permute-done.1.refs_2_
  8.0 0.0 collective-permute-done.refs_1_
  8.1 0.0 collective-permute-done.2.refs_3_
  8.1 0.1 copy-done.3
  8.1 0.3 %shard_map.97 = (bf16[256,128]{1,0:T(8,128)(2,1)S(1)}, bf16[256,128]{1,0:T(8,128)(2,1)S(1)}) custom-call(bf16[512,512]{1,0:T(8,128)(2,1)S(1)} %shard_map.95.near.matrix, bf16[128,128]{1,0:T(8,128)(2,1)S(1)} %copy-done.3, bf16[128,128]{1,0:T(8,128)(2,1)S(1)} %collective-permute-done.refs_1_, bf16[128,128]{1,0:T(8,128)(2,1)S(1)} %collective-permute-done.1.refs_2_, ...), custom_call_target="tpu_custom_call" | custom-call | flops 67108864 | bytes 1048576 | tf_op jit(solution)/shard_map/pallas_call | solution.py:255
  8.4 1.8 %collective-permute-start.4 = (bf16[256,128]{1,0:T(8,128)(2,1)S(1)}, bf16[256,128]{1,0:T(8,128)(2,1)S(1)}, u32[]{:S(2)}, u32[]{:S(2)}) collective-permute-start(bf16[256,128]{1,0:T(8,128)(2,1)S(1)} %get-tuple-element.16.refs_1_), channel_id=1, source_target_pairs={{0,2},{1,3},{2,0},{3,1},{4,6},{5,7},{6,4},{7,5},{8,10},{9,11},{10,... | collective-permute-start | bytes 196616 | tf_op jit(solution)/shard_map/ppermute | solution.py:58
  10.2 0.0 copy-start.1
  10.2 0.0 copy-start.2
  10.2 2.2 %collective-permute-start.5 = (bf16[256,128]{1,0:T(8,128)(2,1)S(1)}, bf16[256,128]{1,0:T(8,128)(2,1)S(1)}, u32[]{:S(2)}, u32[]{:S(2)}) collective-permute-start(bf16[256,128]{1,0:T(8,128)(2,1)S(1)} %get-tuple-element.17), channel_id=1, source_target_pairs={{0,3},{1,2},{2,1},{3,0},{4,7},{5,6},{6,5},{7,4},{8,11},{9,10},{10,... | collective-permute-start | bytes 196616 | tf_op jit(solution)/shard_map/ppermute | solution.py:58
  12.4 0.0 collective-permute-start.3
  12.4 0.3 %shard_map.96.refs_0_.matrix = bf16[512,512]{1,0:T(8,128)(2,1)S(1)} custom-call(bf16[512,512]{1,0:T(8,128)(2,1)S(1)} %shard_map.95.near.matrix), custom_call_target="tpu_custom_call" | custom-call | bytes 1572864 | tf_op jit(solution)/shard_map/pallas_call | solution.py:273
  12.8 0.0 collective-permute-done.6.refs_7_
  12.8 4.3 %collective-permute-done.4.refs_3_ = bf16[256,128]{1,0:T(8,128)(2,1)S(1)} collective-permute-done((bf16[256,128]{1,0:T(8,128)(2,1)S(1)}, bf16[256,128]{1,0:T(8,128)(2,1)S(1)}, u32[]{:S(2)}, u32[]{:S(2)}) %collective-permute-start.4) | collective-permute-done | bytes 65568 | tf_op jit(solution)/shard_map/ppermute | solution.py:58
  17.1 0.0 collective-permute-done.5.refs_4_
  17.1 0.5 %collective-permute-done.3.refs_2_ = bf16[256,128]{1,0:T(8,128)(2,1)S(1)} collective-permute-done((bf16[256,128]{1,0:T(8,128)(2,1)S(1)}, bf16[256,128]{1,0:T(8,128)(2,1)S(1)}, u32[]{:S(2)}, u32[]{:S(2)}) %collective-permute-start.3) | collective-permute-done | bytes 65568 | tf_op jit(solution)/shard_map/ppermute | solution.py:58
  17.6 0.0 copy-done.1
  17.6 0.0 copy-done.2
  17.6 0.5 %shard_map.98 = (bf16[256,128]{1,0:T(8,128)(2,1)S(1)}, f32[128,128]{1,0:T(8,128)S(1)}, bf16[128,128]{1,0:T(8,128)(2,1)S(1)}, f32[128,256]{1,0:T(8,128)S(1)}) custom-call(bf16[512,512]{1,0:T(8,128)(2,1)S(1)} %shard_map.96.refs_0_.matrix, bf16[256,128]{1,0:T(8,128)(2,1)S(1)} %get-tuple-element.16.refs_1_, bf16[256,128]{1,0:T(8,128)(2,1)S(1)} %collective-permute-done.3.refs_2_, ...), custom_call_target="tpu_custom_call" | custom-call | flops 117440512 | tf_op jit(solution)/shard_map/pallas_call | solution.py:282
  18.1 0.1 collective-permute-start.8
  18.2 0.9 %collective-permute-start.7 = (bf16[256,128]{1,0:T(8,128)(2,1)S(1)}, bf16[256,128]{1,0:T(8,128)(2,1)S(1)}, u32[]{:S(2)}, u32[]{:S(2)}) collective-permute-start(bf16[256,128]{1,0:T(8,128)(2,1)S(1)} %get-tuple-element.19.refs_0_), channel_id=1, source_target_pairs={{0,1},{1,0},{2,3},{3,2},{4,5},{5,4},{6,7},{7,6},{8,9},{9,8},{10,11... | collective-permute-start | bytes 196616 | tf_op jit(solution)/shard_map/ppermute | solution.py:58
  19.1 0.3 %collective-permute-done.8.came = bf16[128,128]{1,0:T(8,128)(2,1)S(1)} collective-permute-done((bf16[128,128]{1,0:T(8,128)(2,1)S(1)}, bf16[128,128]{1,0:T(8,128)(2,1)S(1)}, u32[]{:S(2)}, u32[]{:S(2)}) %collective-permute-start.8) | collective-permute-done | bytes 32800 | tf_op jit(solution)/shard_map/ppermute | solution.py:58
  19.4 1.0 %collective-permute-start.9 = (bf16[128,128]{1,0:T(8,128)(2,1)S(1)}, bf16[128,128]{1,0:T(8,128)(2,1)S(1)}, u32[]{:S(2)}, u32[]{:S(2)}) collective-permute-start(bf16[128,128]{1,0:T(8,128)(2,1)S(1)} %shard_map.100.refs_2_), channel_id=1, source_target_pairs={{0,1},{1,0},{2,3},{3,2},{4,5},{5,4},{6,7},{7,6},{8,9},{9,8},{10,11... | collective-permute-start | bytes 98312 | tf_op jit(solution)/shard_map/ppermute | solution.py:58
  20.4 3.0 %collective-permute-done.9.refs_3_ = bf16[128,128]{1,0:T(8,128)(2,1)S(1)} collective-permute-done((bf16[128,128]{1,0:T(8,128)(2,1)S(1)}, bf16[128,128]{1,0:T(8,128)(2,1)S(1)}, u32[]{:S(2)}, u32[]{:S(2)}) %collective-permute-start.9) | collective-permute-done | bytes 32800 | tf_op jit(solution)/shard_map/ppermute | solution.py:58
  23.4 0.0 collective-permute-done.7.refs_1_
  23.4 0.3 %shard_map.101 = (f32[128,128]{1,0:T(8,128)S(1)}, bf16[128,128]{1,0:T(8,128)(2,1)S(1)}, bf16[256,128]{1,0:T(8,128)(2,1)S(1)}, bf16[256,128]{1,0:T(8,128)(2,1)S(1)}, bf16[256,128]{1,0:T(8,128)(2,1)S(1)}) custom-call(bf16[512,512]{1,0:T(8,128)(2,1)S(1)} %shard_map.96.refs_0_.matrix, bf16[256,128]{1,0:T(8,128)(2,1)S(1)} %get-tuple-element.19.refs_0_, ...), custom_call_target="tpu_custom_call" | custom-call | flops 67108864 | bytes 1048576 | tf_op jit(solution)/shard_map/pallas_call | solution.py:303
  23.7 0.1 collective-permute-start.10
  23.8 1.4 %collective-permute-start.11 = (bf16[256,128]{1,0:T(8,128)(2,1)S(1)}, bf16[256,128]{1,0:T(8,128)(2,1)S(1)}, u32[]{:S(2)}, u32[]{:S(2)}) collective-permute-start(bf16[256,128]{1,0:T(8,128)(2,1)S(1)} %get-tuple-element.25), channel_id=1, source_target_pairs={{0,8},{4,12},{8,0},{12,4},{1,9},{5,13},{9,1},{13,5},{2,10},{6,14},... | collective-permute-start | bytes 196616 | tf_op jit(solution)/shard_map/ppermute | solution.py:43
  25.1 1.4 %collective-permute-start.12 = (bf16[256,128]{1,0:T(8,128)(2,1)S(1)}, bf16[256,128]{1,0:T(8,128)(2,1)S(1)}, u32[]{:S(2)}, u32[]{:S(2)}) collective-permute-start(bf16[256,128]{1,0:T(8,128)(2,1)S(1)} %get-tuple-element.26), channel_id=1, source_target_pairs={{0,12},{4,0},{8,4},{12,8},{1,13},{5,1},{9,5},{13,9},{2,14},{6,2},{... | collective-permute-start | bytes 196616 | tf_op jit(solution)/shard_map/ppermute | solution.py:43
  26.5 0.7 %shard_map.99 = bf16[128,256]{1,0:T(8,128)(2,1)} custom-call(f32[128,256]{1,0:T(8,128)S(1)} %get-tuple-element.18.pre), custom_call_target="tpu_custom_call" | custom-call | tf_op jit(solution)/shard_map/pallas_call | solution.py:300
  27.2 0.4 %collective-permute-done.10.refs_0_ = bf16[256,128]{1,0:T(8,128)(2,1)S(1)} collective-permute-done((bf16[256,128]{1,0:T(8,128)(2,1)S(1)}, bf16[256,128]{1,0:T(8,128)(2,1)S(1)}, u32[]{:S(2)}, u32[]{:S(2)}) %collective-permute-start.10) | collective-permute-done | bytes 65568 | tf_op jit(solution)/shard_map/ppermute | solution.py:43
  27.6 1.0 %collective-permute-done.11.refs_1_ = bf16[256,128]{1,0:T(8,128)(2,1)S(1)} collective-permute-done((bf16[256,128]{1,0:T(8,128)(2,1)S(1)}, bf16[256,128]{1,0:T(8,128)(2,1)S(1)}, u32[]{:S(2)}, u32[]{:S(2)}) %collective-permute-start.11) | collective-permute-done | bytes 65568 | tf_op jit(solution)/shard_map/ppermute | solution.py:43
  28.6 0.0 collective-permute-done.12.refs_2_
  28.6 0.7 %shard_map.102 = (bf16[128,128]{1,0:T(8,128)(2,1)}, f32[128,256]{1,0:T(8,128)}) custom-call(f32[128,128]{1,0:T(8,128)S(1)} %get-tuple-element.22.own, bf16[128,128]{1,0:T(8,128)(2,1)S(1)} %get-tuple-element.23.kept, bf16[256,128]{1,0:T(8,128)(2,1)S(1)} %collective-permute-done.10.refs_0_, bf16[256,128]{1,0:T(8,128)(2,1)S(1)} %collective-permute-done.11.refs_1_, ...), custom_call_target="tpu_custom_call" | custom-call | tf_op jit(solution)/shard_map/pallas_call | solution.py:313
  (2 shorter events, 0.0 us)
Async XLA Ops:
  0.6 6.7 %copy-start = (bf16[1,1,8,128,128]{4,3,2,1,0:T(8,128)(2,1)S(1)}, bf16[1,1,8,128,128]{4,3,2,1,0:T(8,128)(2,1)}, u32[]{:S(2)}) copy-start(bf16[1,1,8,128,128]{4,3,2,1,0:T(8,128)(2,1)} %vals.1) | copy-start | bytes 786436
  0.6 7.4 %collective-permute-start.1 = (bf16[128,128]{1,0:T(8,128)(2,1)}, bf16[128,128]{1,0:T(8,128)(2,1)S(1)}, u32[]{:S(2)}, u32[]{:S(2)}) collective-permute-start(bf16[128,128]{1,0:T(8,128)(2,1)} %refs_0_.1), channel_id=1, source_target_pairs={{0,12},{4,8},{8,4},{12,0},{1,13},{5,9},{9,5},{13,1},{2,14},{6,10},... | collective-permute-start | bytes 98312 | tf_op jit(solution)/shard_map/ppermute | solution.py:58
  3.1 5.0 %collective-permute-start = (bf16[128,128]{1,0:T(8,128)(2,1)}, bf16[128,128]{1,0:T(8,128)(2,1)S(1)}, u32[]{:S(2)}, u32[]{:S(2)}) collective-permute-start(bf16[128,128]{1,0:T(8,128)(2,1)} %refs_0_.1), channel_id=1, source_target_pairs={{0,8},{4,12},{8,0},{12,4},{1,9},{5,13},{9,1},{13,5},{2,10},{6,14},... | collective-permute-start | bytes 98312 | tf_op jit(solution)/shard_map/ppermute | solution.py:58
  3.7 4.3 %collective-permute-start.2 = (bf16[128,128]{1,0:T(8,128)(2,1)}, bf16[128,128]{1,0:T(8,128)(2,1)S(1)}, u32[]{:S(2)}, u32[]{:S(2)}) collective-permute-start(bf16[128,128]{1,0:T(8,128)(2,1)} %refs_0_.1), channel_id=1, source_target_pairs={{0,4},{4,0},{8,12},{12,8},{1,5},{5,1},{9,13},{13,9},{2,6},{6,2},{1... | collective-permute-start | bytes 98312 | tf_op jit(solution)/shard_map/ppermute | solution.py:58
  3.8 9.0 %collective-permute-start.6 = (bf16[128,256]{1,0:T(8,128)(2,1)}, bf16[128,256]{1,0:T(8,128)(2,1)S(1)}, u32[]{:S(2)}, u32[]{:S(2)}) collective-permute-start(bf16[128,256]{1,0:T(8,128)(2,1)} %refs_6_.1), channel_id=1, source_target_pairs={{0,2},{1,3},{2,0},{3,1},{4,6},{5,7},{6,4},{7,5},{8,10},{9,11},{10,... | collective-permute-start | bytes 196616 | tf_op jit(solution)/shard_map/ppermute | solution.py:58
  6.6 0.7 %copy-start.4 = (s32[1,1,8]{2,1,0:T(1,128)S(1)}, s32[1,1,8]{2,1,0:T(1,128)}, u32[]{:S(2)}) copy-start(s32[1,1,8]{2,1,0:T(1,128)} %rows_in.1) | copy-start | bytes 100
  6.7 0.7 %copy-start.5 = (s32[1,1,8]{2,1,0:T(1,128)S(1)}, s32[1,1,8]{2,1,0:T(1,128)}, u32[]{:S(2)}) copy-start(s32[1,1,8]{2,1,0:T(1,128)} %cols_in.1) | copy-start | bytes 100
  7.4 0.8 %copy-start.3 = (bf16[128,128]{1,0:T(8,128)(2,1)S(1)}, bf16[128,128]{1,0:T(8,128)(2,1)}, u32[]{:S(2)}) copy-start(bf16[128,128]{1,0:T(8,128)(2,1)} %refs_0_.1) | copy-start | bytes 98308
  8.4 8.7 %collective-permute-start.4 = (bf16[256,128]{1,0:T(8,128)(2,1)S(1)}, bf16[256,128]{1,0:T(8,128)(2,1)S(1)}, u32[]{:S(2)}, u32[]{:S(2)}) collective-permute-start(bf16[256,128]{1,0:T(8,128)(2,1)S(1)} %get-tuple-element.16.refs_1_), channel_id=1, source_target_pairs={{0,2},{1,3},{2,0},{3,1},{4,6},{5,7},{6,4},{7,5},{8,10},{9,11},{10,... | collective-permute-start | bytes 196616 | tf_op jit(solution)/shard_map/ppermute | solution.py:58
  10.2 7.4 %copy-start.1 = (bf16[128,256]{1,0:T(8,128)(2,1)S(1)}, bf16[128,256]{1,0:T(8,128)(2,1)}, u32[]{:S(2)}) copy-start(bf16[128,256]{1,0:T(8,128)(2,1)} %refs_5_.1) | copy-start | bytes 196612
  10.2 7.4 %copy-start.2 = (bf16[128,256]{1,0:T(8,128)(2,1)S(1)}, bf16[128,256]{1,0:T(8,128)(2,1)}, u32[]{:S(2)}) copy-start(bf16[128,256]{1,0:T(8,128)(2,1)} %refs_6_.1) | copy-start | bytes 196612
  10.2 6.9 %collective-permute-start.5 = (bf16[256,128]{1,0:T(8,128)(2,1)S(1)}, bf16[256,128]{1,0:T(8,128)(2,1)S(1)}, u32[]{:S(2)}, u32[]{:S(2)}) collective-permute-start(bf16[256,128]{1,0:T(8,128)(2,1)S(1)} %get-tuple-element.17), channel_id=1, source_target_pairs={{0,3},{1,2},{2,1},{3,0},{4,7},{5,6},{6,5},{7,4},{8,11},{9,10},{10,... | collective-permute-start | bytes 196616 | tf_op jit(solution)/shard_map/ppermute | solution.py:58
  12.4 5.2 %collective-permute-start.3 = (bf16[256,128]{1,0:T(8,128)(2,1)S(1)}, bf16[256,128]{1,0:T(8,128)(2,1)S(1)}, u32[]{:S(2)}, u32[]{:S(2)}) collective-permute-start(bf16[256,128]{1,0:T(8,128)(2,1)S(1)} %get-tuple-element.17), channel_id=1, source_target_pairs={{0,1},{1,0},{2,3},{3,2},{4,5},{5,4},{6,7},{7,6},{8,9},{9,8},{10,11... | collective-permute-start | bytes 196616 | tf_op jit(solution)/shard_map/ppermute | solution.py:58
  18.1 1.3 %collective-permute-start.8 = (bf16[128,128]{1,0:T(8,128)(2,1)S(1)}, bf16[128,128]{1,0:T(8,128)(2,1)S(1)}, u32[]{:S(2)}, u32[]{:S(2)}) collective-permute-start(bf16[128,128]{1,0:T(8,128)(2,1)S(1)} %get-tuple-element.21), channel_id=1, source_target_pairs={{0,4},{4,0},{8,12},{12,8},{1,5},{5,1},{9,13},{13,9},{2,6},{6,2},{1... | collective-permute-start | bytes 98312 | tf_op jit(solution)/shard_map/ppermute | solution.py:58
  18.2 5.2 %collective-permute-start.7 = (bf16[256,128]{1,0:T(8,128)(2,1)S(1)}, bf16[256,128]{1,0:T(8,128)(2,1)S(1)}, u32[]{:S(2)}, u32[]{:S(2)}) collective-permute-start(bf16[256,128]{1,0:T(8,128)(2,1)S(1)} %get-tuple-element.19.refs_0_), channel_id=1, source_target_pairs={{0,1},{1,0},{2,3},{3,2},{4,5},{5,4},{6,7},{7,6},{8,9},{9,8},{10,11... | collective-permute-start | bytes 196616 | tf_op jit(solution)/shard_map/ppermute | solution.py:58
  19.4 4.0 %collective-permute-start.9 = (bf16[128,128]{1,0:T(8,128)(2,1)S(1)}, bf16[128,128]{1,0:T(8,128)(2,1)S(1)}, u32[]{:S(2)}, u32[]{:S(2)}) collective-permute-start(bf16[128,128]{1,0:T(8,128)(2,1)S(1)} %shard_map.100.refs_2_), channel_id=1, source_target_pairs={{0,1},{1,0},{2,3},{3,2},{4,5},{5,4},{6,7},{7,6},{8,9},{9,8},{10,11... | collective-permute-start | bytes 98312 | tf_op jit(solution)/shard_map/ppermute | solution.py:58
  23.7 3.8 %collective-permute-start.10 = (bf16[256,128]{1,0:T(8,128)(2,1)S(1)}, bf16[256,128]{1,0:T(8,128)(2,1)S(1)}, u32[]{:S(2)}, u32[]{:S(2)}) collective-permute-start(bf16[256,128]{1,0:T(8,128)(2,1)S(1)} %get-tuple-element.24), channel_id=1, source_target_pairs={{0,4},{4,8},{8,12},{12,0},{1,5},{5,9},{9,13},{13,1},{2,6},{6,10},{... | collective-permute-start | bytes 196616 | tf_op jit(solution)/shard_map/ppermute | solution.py:43
  23.8 4.8 %collective-permute-start.11 = (bf16[256,128]{1,0:T(8,128)(2,1)S(1)}, bf16[256,128]{1,0:T(8,128)(2,1)S(1)}, u32[]{:S(2)}, u32[]{:S(2)}) collective-permute-start(bf16[256,128]{1,0:T(8,128)(2,1)S(1)} %get-tuple-element.25), channel_id=1, source_target_pairs={{0,8},{4,12},{8,0},{12,4},{1,9},{5,13},{9,1},{13,5},{2,10},{6,14},... | collective-permute-start | bytes 196616 | tf_op jit(solution)/shard_map/ppermute | solution.py:43
  25.1 3.4 %collective-permute-start.12 = (bf16[256,128]{1,0:T(8,128)(2,1)S(1)}, bf16[256,128]{1,0:T(8,128)(2,1)S(1)}, u32[]{:S(2)}, u32[]{:S(2)}) collective-permute-start(bf16[256,128]{1,0:T(8,128)(2,1)S(1)} %get-tuple-element.26), channel_id=1, source_target_pairs={{0,12},{4,0},{8,4},{12,8},{1,13},{5,1},{9,5},{13,9},{2,14},{6,2},{... | collective-permute-start | bytes 196616 | tf_op jit(solution)/shard_map/ppermute | solution.py:43

commit v22 on v19

--- a/solution.py
+++ b/solution.py
@@ -183,7 +183,7 @@
     third[...] = jnp.where(middle, other, same)
 
 
-def paired_layer_kernel(own, first, second, third, weight, cotangent, beyond, *refs):
+def paired_layer_kernel(own, first, third, second, weight, cotangent, beyond, *refs):
     back_out, mine, other, pre_out = refs
     nodes = cotangent.shape[0]
     middle = in_middle()
@@ -209,10 +209,16 @@
     act[...] = (pre[...] * jax.nn.sigmoid(pre[...])).astype(act.dtype)
 
 
-def backward_kernel(n, matrix, *refs):
-    backs, halves, (own, kept, *sends, product) = refs[:n], refs[n : 2 * n], refs[2 * n :]
+def begin_kernel(matrix, back, product):
+    product[...] = dot(matrix[:, : back.shape[0]], back[...])
+
+
+def backward_kernel(n, matrix, begun, *refs):
+    backs, halves, (own, kept, *sends, product) = refs[: n - 1], refs[n - 1 : 2 * n - 1], refs[2 * n - 1 :]
     rows = own.shape[0]
-    product[...] = dot(matrix[...], jnp.concatenate([back[...] for back in backs], axis=0))
+    late = sum(back.shape[0] for back in backs)
+    stacked = jnp.concatenate([back[...] for back in backs], axis=0)
+    product[...] = begun[...] + dot(matrix[:, -late:], stacked)
     own[...] = product[:rows]
     term = tree([wide(half[...]) for half in halves]).astype(kept.dtype)
     kept[...] = term
@@ -225,6 +231,7 @@
 
 def last_kernel(scale, own, kept, *refs):
     *messages, features_out, weight_out = refs
+    messages = messages[:1] + messages[-1:] + messages[1:-1]
     nodes, half = own.shape[0], kept.shape[1]
     features_out[...] = tree(
         [own[...]] + [wide(message[:nodes]) for message in messages]
@@ -271,6 +278,8 @@
             **forward,
         )(near, features, *gathered)
         layer_call, cotangents = paired_layer_kernel, [cotangent, swap(cotangent, "col", 2)]
+        first, second, third = exchange(sends, "col", True)
+        parts = [first, third, second]
     else:
         layers = 1
         own, *sends = call(
@@ -280,7 +289,7 @@
             **forward,
         )(near, features, *gathered)
         layer_call, cotangents = layer_kernel, [cotangent]
-    parts = exchange(sends, "col", True)
+        parts = exchange(sends, "col", True)
     (far,) = call(
         functools.partial(turn_kernel, side),
         [((across, down), NARROW)],
@@ -311,13 +320,14 @@
     (act,) = call(act_kernel, [((nodes, hidden), NARROW)], [VMEM])(pre)
 
     message = ((nodes + width, width), NARROW)
+    (begun,) = call(begin_kernel, [((across, width), jnp.float32)], [VMEM] * 2, **forward)(far, back)
     own, kept, *sends = call(
         functools.partial(backward_kernel, len(backs)),
         [((nodes, width), jnp.float32), (square, NARROW)] + [message] * (n_row - 1),
         [VMEM] * (1 + 2 * len(backs)),
         scratch=[pltpu.VMEM((across, width), jnp.float32)],
         **forward,
-    )(far, *backs, *terms)
+    )(far, begun, *backs[1:], *terms)
     parts = exchange(sends, "row", True)
 
     scale = float(nodes * n_row * n_col) ** -0.5
@@ -325,7 +335,7 @@
         functools.partial(last_kernel, scale),
         [((nodes, width), NARROW), ((width, hidden), jnp.float32)],
         [VMEM] * (n_row + 1),
-    )(own, kept, *parts)
+    )(own, kept, parts[0], *parts[2:], parts[1])
     return act, grad_features, grad_weight
 
 

time: 29.8 us -> 31.2 us (1.047); the launches traced: 29.2 us -> 31 us
  waiting for transfers between devices: 7.72 us -> 8.76 us
  starting transfers between devices: 16.4 us -> 17.1 us
    ppermute x6, starting transfers between devices: 7.4 us -> 8.82 us  [exchange(): lax.ppermute(send, axis, [(s, target(s, d)) for s in range(n)])]
    ppermute x7, starting transfers between devices: 9.03 us -> 8.24 us  [swap(): return lax.ppermute(value, axis, [(s, s ^ distance) for s in range(n)])]
    ppermute x6, waiting for transfers between devices: 4.92 us -> 5.7 us  [exchange(): lax.ppermute(send, axis, [(s, target(s, d)) for s in range(n)])]
  transfers between devices with their start and end apart: 13 -> 13, of which waited for: 4 -> 6; matrix products, arithmetic and copies ran while one was open for 0% -> 0% of each run, Pallas kernels for 7% -> 7%
where the time goes in v22:
time: 31.2 us; the launch traced here: 31 us
  starting transfers between devices  17.1 us (55%)
  waiting for transfers between devices  8.76 us (28%)
  Pallas kernels  3.63 us (12%)
  between operations  1.46 us (5%)
    ppermute x6, starting transfers between devices, exchange(): lax.ppermute(send, axis, [(s, target(s, d)) for s in range(n)])  8.82 us
    ppermute x7, starting transfers between devices, swap(): return lax.ppermute(value, axis, [(s, s ^ distance) for s in range(n)])  8.24 us
    ppermute x6, waiting for transfers between devices, exchange(): lax.ppermute(send, axis, [(s, target(s, d)) for s in range(n)])  5.7 us
    ppermute x7, waiting for transfers between devices, swap(): return lax.ppermute(value, axis, [(s, s ^ distance) for s in range(n)])  3.07 us
    pallas_call x1, Pallas kernels, per_device(): call(functools.partial(last_kernel, scale), [((nodes, width), NARROW), ((...  0.69 us
    pallas_call x1, Pallas kernels, per_device(): call(functools.partial(dense_kernel, nodes // side, paired), [((down, acr...  0.66 us
    pallas_call x1, Pallas kernels, per_device(): act, = call(act_kernel, [((nodes, hidden), NARROW)], [VMEM])(pre)  0.65 us
  transfers between devices with their start and end apart: 13, of which 6 were waited for; matrix products, arithmetic and copies ran while one was open for 0% of the time, Pallas kernels for 7%

profile of v22, /device:TPU:0, one launch (start us, length us, event | category | flops | bytes accessed | tf_op | source)
XLA Modules:
  0.0 31.0 jit_solution(10499650874153699892)
XLA Ops:
  0.6 0.0 copy-start
  0.6 3.0 %collective-permute-start = (bf16[128,128]{1,0:T(8,128)(2,1)}, bf16[128,128]{1,0:T(8,128)(2,1)S(1)}, u32[]{:S(2)}, u32[]{:S(2)}) collective-permute-start(bf16[128,128]{1,0:T(8,128)(2,1)} %refs_0_.1), channel_id=1, source_target_pairs={{0,8},{4,12},{8,0},{12,4},{1,9},{5,13},{9,1},{13,5},{2,10},{6,14},... | collective-permute-start | bytes 98312 | tf_op jit(solution)/shard_map/ppermute | solution.py:58
  3.6 0.0 collective-permute-start.1
  3.6 0.2 collective-permute-start.2
  3.8 3.0 %collective-permute-start.6 = (bf16[128,256]{1,0:T(8,128)(2,1)}, bf16[128,256]{1,0:T(8,128)(2,1)S(1)}, u32[]{:S(2)}, u32[]{:S(2)}) collective-permute-start(bf16[128,256]{1,0:T(8,128)(2,1)} %refs_6_.1), channel_id=1, source_target_pairs={{0,2},{1,3},{2,0},{3,1},{4,6},{5,7},{6,4},{7,5},{8,10},{9,11},{10,... | collective-permute-start | bytes 196616 | tf_op jit(solution)/shard_map/ppermute | solution.py:58
  6.9 0.0 copy-start.4
  6.9 0.0 copy-start.5
  7.6 0.0 copy-done
  7.6 0.0 copy-done.4
  7.6 0.0 copy-done.5
  7.6 0.0 copy-start.3
  7.7 0.7 %shard_map.95.near.matrix = bf16[512,512]{1,0:T(8,128)(2,1)S(1)} custom-call(bf16[512,512]{1,0:T(8,128)(2,1)S(1)} %shard_map.94.blank, bf16[1,1,8,128,128]{4,3,2,1,0:T(8,128)(2,1)S(1)} %copy-done, s32[1,1,8]{2,1,0:T(1,128)S(1)} %copy-done.4, s32[1,1,8]{2,1,0:T(1,128)S(1)} %copy-done.5, s32[1,1]{1,0:T(1,128)S(6)} %copy.12.count_in), custom_call_target="tpu_custom_call", output_to_operand_aliasing={{}: (0, {})} | custom-call | bytes 1048576 | tf_op jit(solution)/shard_map/pallas_call | solution.py:257
  8.3 0.0 collective-permute-done.refs_1_
  8.3 0.0 collective-permute-done.1.refs_2_
  8.3 0.0 collective-permute-done.2.refs_3_
  8.3 0.1 copy-done.3
  8.4 0.3 shard_map.97
  8.7 1.6 %collective-permute-start.3 = (bf16[256,128]{1,0:T(8,128)(2,1)S(1)}, bf16[256,128]{1,0:T(8,128)(2,1)S(1)}, u32[]{:S(2)}, u32[]{:S(2)}) collective-permute-start(bf16[256,128]{1,0:T(8,128)(2,1)S(1)} %get-tuple-element.19), channel_id=1, source_target_pairs={{0,1},{1,3},{2,0},{3,2},{4,5},{5,7},{6,4},{7,6},{8,9},{9,11},{10,8... | collective-permute-start | bytes 196616 | tf_op jit(solution)/shard_map/ppermute | solution.py:43
  10.3 1.3 %collective-permute-start.4 = (bf16[256,128]{1,0:T(8,128)(2,1)S(1)}, bf16[256,128]{1,0:T(8,128)(2,1)S(1)}, u32[]{:S(2)}, u32[]{:S(2)}) collective-permute-start(bf16[256,128]{1,0:T(8,128)(2,1)S(1)} %get-tuple-element.20), channel_id=1, source_target_pairs={{0,2},{1,0},{2,3},{3,1},{4,6},{5,4},{6,7},{7,5},{8,10},{9,8},{10,1... | collective-permute-start | bytes 196616 | tf_op jit(solution)/shard_map/ppermute | solution.py:43
  11.7 0.0 copy-start.1
  11.7 0.0 copy-start.2
  11.7 2.5 %collective-permute-start.5 = (bf16[256,128]{1,0:T(8,128)(2,1)S(1)}, bf16[256,128]{1,0:T(8,128)(2,1)S(1)}, u32[]{:S(2)}, u32[]{:S(2)}) collective-permute-start(bf16[256,128]{1,0:T(8,128)(2,1)S(1)} %get-tuple-element.21), channel_id=1, source_target_pairs={{0,3},{1,2},{2,1},{3,0},{4,7},{5,6},{6,5},{7,4},{8,11},{9,10},{10,... | collective-permute-start | bytes 196616 | tf_op jit(solution)/shard_map/ppermute | solution.py:43
  14.2 0.3 %shard_map.96.refs_0_.matrix = bf16[512,512]{1,0:T(8,128)(2,1)S(1)} custom-call(bf16[512,512]{1,0:T(8,128)(2,1)S(1)} %shard_map.95.near.matrix), custom_call_target="tpu_custom_call" | custom-call | bytes 1572864 | tf_op jit(solution)/shard_map/pallas_call | solution.py:293
  14.5 0.0 collective-permute-done.6.refs_7_
  14.5 0.0 collective-permute-done.3.refs_2_
  14.5 0.2 collective-permute-done.4.refs_3_
  14.8 3.0 %collective-permute-done.5.refs_4_ = bf16[256,128]{1,0:T(8,128)(2,1)S(1)} collective-permute-done((bf16[256,128]{1,0:T(8,128)(2,1)S(1)}, bf16[256,128]{1,0:T(8,128)(2,1)S(1)}, u32[]{:S(2)}, u32[]{:S(2)}) %collective-permute-start.5) | collective-permute-done | bytes 65568 | tf_op jit(solution)/shard_map/ppermute | solution.py:43
  17.8 0.0 copy-done.1
  17.8 0.0 copy-done.2
  17.8 0.5 %shard_map.98 = (bf16[256,128]{1,0:T(8,128)(2,1)S(1)}, f32[128,128]{1,0:T(8,128)S(1)}, bf16[128,128]{1,0:T(8,128)(2,1)S(1)}, f32[128,256]{1,0:T(8,128)S(1)}) custom-call(bf16[512,512]{1,0:T(8,128)(2,1)S(1)} %shard_map.96.refs_0_.matrix, bf16[256,128]{1,0:T(8,128)(2,1)S(1)} %get-tuple-element.18.refs_1_, bf16[256,128]{1,0:T(8,128)(2,1)S(1)} %collective-permute-done.3.refs_2_, ...), custom_call_target="tpu_custom_call" | custom-call | flops 117440512 | tf_op jit(solution)/shard_map/pallas_call | solution.py:302
  18.3 0.1 collective-permute-start.8
  18.4 1.0 %collective-permute-start.7 = (bf16[256,128]{1,0:T(8,128)(2,1)S(1)}, bf16[256,128]{1,0:T(8,128)(2,1)S(1)}, u32[]{:S(2)}, u32[]{:S(2)}) collective-permute-start(bf16[256,128]{1,0:T(8,128)(2,1)S(1)} %get-tuple-element.23.back), channel_id=1, source_target_pairs={{0,1},{1,0},{2,3},{3,2},{4,5},{5,4},{6,7},{7,6},{8,9},{9,8},{10,11... | collective-permute-start | bytes 196616 | tf_op jit(solution)/shard_map/ppermute | solution.py:58
  19.3 0.2 collective-permute-done.8.came
  19.6 1.0 %collective-permute-start.9 = (bf16[128,128]{1,0:T(8,128)(2,1)S(1)}, bf16[128,128]{1,0:T(8,128)(2,1)S(1)}, u32[]{:S(2)}, u32[]{:S(2)}) collective-permute-start(bf16[128,128]{1,0:T(8,128)(2,1)S(1)} %shard_map.101.refs_1_), channel_id=1, source_target_pairs={{0,1},{1,0},{2,3},{3,2},{4,5},{5,4},{6,7},{7,6},{8,9},{9,8},{10,11... | collective-permute-start | bytes 98312 | tf_op jit(solution)/shard_map/ppermute | solution.py:58
  20.6 0.2 shard_map.100.begun
  20.8 2.8 %collective-permute-done.9.refs_2_ = bf16[128,128]{1,0:T(8,128)(2,1)S(1)} collective-permute-done((bf16[128,128]{1,0:T(8,128)(2,1)S(1)}, bf16[128,128]{1,0:T(8,128)(2,1)S(1)}, u32[]{:S(2)}, u32[]{:S(2)}) %collective-permute-start.9) | collective-permute-done | bytes 32800 | tf_op jit(solution)/shard_map/ppermute | solution.py:58
  23.6 0.0 collective-permute-done.7.refs_0_
  23.6 0.2 shard_map.102
  23.8 0.1 collective-permute-start.10
  23.9 1.7 %collective-permute-start.11 = (bf16[256,128]{1,0:T(8,128)(2,1)S(1)}, bf16[256,128]{1,0:T(8,128)(2,1)S(1)}, u32[]{:S(2)}, u32[]{:S(2)}) collective-permute-start(bf16[256,128]{1,0:T(8,128)(2,1)S(1)} %get-tuple-element.29), channel_id=1, source_target_pairs={{0,12},{4,0},{8,4},{12,8},{1,13},{5,1},{9,5},{13,9},{2,14},{6,2},{... | collective-permute-start | bytes 196616 | tf_op jit(solution)/shard_map/ppermute | solution.py:43
  25.6 1.6 %collective-permute-start.12 = (bf16[256,128]{1,0:T(8,128)(2,1)S(1)}, bf16[256,128]{1,0:T(8,128)(2,1)S(1)}, u32[]{:S(2)}, u32[]{:S(2)}) collective-permute-start(bf16[256,128]{1,0:T(8,128)(2,1)S(1)} %get-tuple-element.30), channel_id=1, source_target_pairs={{0,8},{4,12},{8,0},{12,4},{1,9},{5,13},{9,1},{13,5},{2,10},{6,14},... | collective-permute-start | bytes 196616 | tf_op jit(solution)/shard_map/ppermute | solution.py:43
  27.2 0.7 %shard_map.99 = bf16[128,256]{1,0:T(8,128)(2,1)} custom-call(f32[128,256]{1,0:T(8,128)S(1)} %get-tuple-element.22.pre), custom_call_target="tpu_custom_call" | custom-call | tf_op jit(solution)/shard_map/pallas_call | solution.py:320
  27.9 0.0 collective-permute-done.10.refs_0_
  27.9 0.2 collective-permute-done.11.refs_1_
  28.1 2.2 %collective-permute-done.12.refs_2_ = bf16[256,128]{1,0:T(8,128)(2,1)S(1)} collective-permute-done((bf16[256,128]{1,0:T(8,128)(2,1)S(1)}, bf16[256,128]{1,0:T(8,128)(2,1)S(1)}, u32[]{:S(2)}, u32[]{:S(2)}) %collective-permute-start.12) | collective-permute-done | bytes 65568 | tf_op jit(solution)/shard_map/ppermute | solution.py:43
  30.3 0.7 %shard_map.103 = (bf16[128,128]{1,0:T(8,128)(2,1)}, f32[128,256]{1,0:T(8,128)}) custom-call(f32[128,128]{1,0:T(8,128)S(1)} %get-tuple-element.26.own, bf16[128,128]{1,0:T(8,128)(2,1)S(1)} %get-tuple-element.27.kept, bf16[256,128]{1,0:T(8,128)(2,1)S(1)} %collective-permute-done.10.refs_0_, bf16[256,128]{1,0:T(8,128)(2,1)S(1)} %collective-permute-done.11.refs_1_, ...), custom_call_target="tpu_custom_call" | custom-call | tf_op jit(solution)/shard_map/pallas_call | solution.py:334
  (2 shorter events, 0.0 us)
Async XLA Ops:
  0.6 7.0 %copy-start = (bf16[1,1,8,128,128]{4,3,2,1,0:T(8,128)(2,1)S(1)}, bf16[1,1,8,128,128]{4,3,2,1,0:T(8,128)(2,1)}, u32[]{:S(2)}) copy-start(bf16[1,1,8,128,128]{4,3,2,1,0:T(8,128)(2,1)} %vals.1) | copy-start | bytes 786436
  0.6 7.7 %collective-permute-start = (bf16[128,128]{1,0:T(8,128)(2,1)}, bf16[128,128]{1,0:T(8,128)(2,1)S(1)}, u32[]{:S(2)}, u32[]{:S(2)}) collective-permute-start(bf16[128,128]{1,0:T(8,128)(2,1)} %refs_0_.1), channel_id=1, source_target_pairs={{0,8},{4,12},{8,0},{12,4},{1,9},{5,13},{9,1},{13,5},{2,10},{6,14},... | collective-permute-start | bytes 98312 | tf_op jit(solution)/shard_map/ppermute | solution.py:58
  3.6 4.7 %collective-permute-start.1 = (bf16[128,128]{1,0:T(8,128)(2,1)}, bf16[128,128]{1,0:T(8,128)(2,1)S(1)}, u32[]{:S(2)}, u32[]{:S(2)}) collective-permute-start(bf16[128,128]{1,0:T(8,128)(2,1)} %refs_0_.1), channel_id=1, source_target_pairs={{0,12},{4,8},{8,4},{12,0},{1,13},{5,9},{9,5},{13,1},{2,14},{6,10},... | collective-permute-start | bytes 98312 | tf_op jit(solution)/shard_map/ppermute | solution.py:58
  3.6 4.7 %collective-permute-start.2 = (bf16[128,128]{1,0:T(8,128)(2,1)}, bf16[128,128]{1,0:T(8,128)(2,1)S(1)}, u32[]{:S(2)}, u32[]{:S(2)}) collective-permute-start(bf16[128,128]{1,0:T(8,128)(2,1)} %refs_0_.1), channel_id=1, source_target_pairs={{0,4},{4,0},{8,12},{12,8},{1,5},{5,1},{9,13},{13,9},{2,6},{6,2},{1... | collective-permute-start | bytes 98312 | tf_op jit(solution)/shard_map/ppermute | solution.py:58
  3.8 10.7 %collective-permute-start.6 = (bf16[128,256]{1,0:T(8,128)(2,1)}, bf16[128,256]{1,0:T(8,128)(2,1)S(1)}, u32[]{:S(2)}, u32[]{:S(2)}) collective-permute-start(bf16[128,256]{1,0:T(8,128)(2,1)} %refs_6_.1), channel_id=1, source_target_pairs={{0,2},{1,3},{2,0},{3,1},{4,6},{5,7},{6,4},{7,5},{8,10},{9,11},{10,... | collective-permute-start | bytes 196616 | tf_op jit(solution)/shard_map/ppermute | solution.py:58
  6.9 0.7 %copy-start.4 = (s32[1,1,8]{2,1,0:T(1,128)S(1)}, s32[1,1,8]{2,1,0:T(1,128)}, u32[]{:S(2)}) copy-start(s32[1,1,8]{2,1,0:T(1,128)} %rows_in.1) | copy-start | bytes 100
  6.9 0.7 %copy-start.5 = (s32[1,1,8]{2,1,0:T(1,128)S(1)}, s32[1,1,8]{2,1,0:T(1,128)}, u32[]{:S(2)}) copy-start(s32[1,1,8]{2,1,0:T(1,128)} %cols_in.1) | copy-start | bytes 100
  7.6 0.8 %copy-start.3 = (bf16[128,128]{1,0:T(8,128)(2,1)S(1)}, bf16[128,128]{1,0:T(8,128)(2,1)}, u32[]{:S(2)}) copy-start(bf16[128,128]{1,0:T(8,128)(2,1)} %refs_0_.1) | copy-start | bytes 98308
  8.7 5.8 %collective-permute-start.3 = (bf16[256,128]{1,0:T(8,128)(2,1)S(1)}, bf16[256,128]{1,0:T(8,128)(2,1)S(1)}, u32[]{:S(2)}, u32[]{:S(2)}) collective-permute-start(bf16[256,128]{1,0:T(8,128)(2,1)S(1)} %get-tuple-element.19), channel_id=1, source_target_pairs={{0,1},{1,3},{2,0},{3,2},{4,5},{5,7},{6,4},{7,6},{8,9},{9,11},{10,8... | collective-permute-start | bytes 196616 | tf_op jit(solution)/shard_map/ppermute | solution.py:43
  10.3 4.5 %collective-permute-start.4 = (bf16[256,128]{1,0:T(8,128)(2,1)S(1)}, bf16[256,128]{1,0:T(8,128)(2,1)S(1)}, u32[]{:S(2)}, u32[]{:S(2)}) collective-permute-start(bf16[256,128]{1,0:T(8,128)(2,1)S(1)} %get-tuple-element.20), channel_id=1, source_target_pairs={{0,2},{1,0},{2,3},{3,1},{4,6},{5,4},{6,7},{7,5},{8,10},{9,8},{10,1... | collective-permute-start | bytes 196616 | tf_op jit(solution)/shard_map/ppermute | solution.py:43
  11.7 6.1 %copy-start.1 = (bf16[128,256]{1,0:T(8,128)(2,1)S(1)}, bf16[128,256]{1,0:T(8,128)(2,1)}, u32[]{:S(2)}) copy-start(bf16[128,256]{1,0:T(8,128)(2,1)} %refs_5_.1) | copy-start | bytes 196612
  11.7 6.1 %copy-start.2 = (bf16[128,256]{1,0:T(8,128)(2,1)S(1)}, bf16[128,256]{1,0:T(8,128)(2,1)}, u32[]{:S(2)}) copy-start(bf16[128,256]{1,0:T(8,128)(2,1)} %refs_6_.1) | copy-start | bytes 196612
  11.7 6.1 %collective-permute-start.5 = (bf16[256,128]{1,0:T(8,128)(2,1)S(1)}, bf16[256,128]{1,0:T(8,128)(2,1)S(1)}, u32[]{:S(2)}, u32[]{:S(2)}) collective-permute-start(bf16[256,128]{1,0:T(8,128)(2,1)S(1)} %get-tuple-element.21), channel_id=1, source_target_pairs={{0,3},{1,2},{2,1},{3,0},{4,7},{5,6},{6,5},{7,4},{8,11},{9,10},{10,... | collective-permute-start | bytes 196616 | tf_op jit(solution)/shard_map/ppermute | solution.py:43
  18.3 1.3 %collective-permute-start.8 = (bf16[128,128]{1,0:T(8,128)(2,1)S(1)}, bf16[128,128]{1,0:T(8,128)(2,1)S(1)}, u32[]{:S(2)}, u32[]{:S(2)}) collective-permute-start(bf16[128,128]{1,0:T(8,128)(2,1)S(1)} %get-tuple-element.25), channel_id=1, source_target_pairs={{0,4},{4,0},{8,12},{12,8},{1,5},{5,1},{9,13},{13,9},{2,6},{6,2},{1... | collective-permute-start | bytes 98312 | tf_op jit(solution)/shard_map/ppermute | solution.py:58
  18.4 5.2 %collective-permute-start.7 = (bf16[256,128]{1,0:T(8,128)(2,1)S(1)}, bf16[256,128]{1,0:T(8,128)(2,1)S(1)}, u32[]{:S(2)}, u32[]{:S(2)}) collective-permute-start(bf16[256,128]{1,0:T(8,128)(2,1)S(1)} %get-tuple-element.23.back), channel_id=1, source_target_pairs={{0,1},{1,0},{2,3},{3,2},{4,5},{5,4},{6,7},{7,6},{8,9},{9,8},{10,11... | collective-permute-start | bytes 196616 | tf_op jit(solution)/shard_map/ppermute | solution.py:58
  19.6 4.0 %collective-permute-start.9 = (bf16[128,128]{1,0:T(8,128)(2,1)S(1)}, bf16[128,128]{1,0:T(8,128)(2,1)S(1)}, u32[]{:S(2)}, u32[]{:S(2)}) collective-permute-start(bf16[128,128]{1,0:T(8,128)(2,1)S(1)} %shard_map.101.refs_1_), channel_id=1, source_target_pairs={{0,1},{1,0},{2,3},{3,2},{4,5},{5,4},{6,7},{7,6},{8,9},{9,8},{10,11... | collective-permute-start | bytes 98312 | tf_op jit(solution)/shard_map/ppermute | solution.py:58
  23.8 4.0 %collective-permute-start.10 = (bf16[256,128]{1,0:T(8,128)(2,1)S(1)}, bf16[256,128]{1,0:T(8,128)(2,1)S(1)}, u32[]{:S(2)}, u32[]{:S(2)}) collective-permute-start(bf16[256,128]{1,0:T(8,128)(2,1)S(1)} %get-tuple-element.28), channel_id=1, source_target_pairs={{0,4},{4,8},{8,12},{12,0},{1,5},{5,9},{9,13},{13,1},{2,6},{6,10},{... | collective-permute-start | bytes 196616 | tf_op jit(solution)/shard_map/ppermute | solution.py:43
  23.9 4.2 %collective-permute-start.11 = (bf16[256,128]{1,0:T(8,128)(2,1)S(1)}, bf16[256,128]{1,0:T(8,128)(2,1)S(1)}, u32[]{:S(2)}, u32[]{:S(2)}) collective-permute-start(bf16[256,128]{1,0:T(8,128)(2,1)S(1)} %get-tuple-element.29), channel_id=1, source_target_pairs={{0,12},{4,0},{8,4},{12,8},{1,13},{5,1},{9,5},{13,9},{2,14},{6,2},{... | collective-permute-start | bytes 196616 | tf_op jit(solution)/shard_map/ppermute | solution.py:43
  25.6 4.7 %collective-permute-start.12 = (bf16[256,128]{1,0:T(8,128)(2,1)S(1)}, bf16[256,128]{1,0:T(8,128)(2,1)S(1)}, u32[]{:S(2)}, u32[]{:S(2)}) collective-permute-start(bf16[256,128]{1,0:T(8,128)(2,1)S(1)} %get-tuple-element.30), channel_id=1, source_target_pairs={{0,8},{4,12},{8,0},{12,4},{1,9},{5,13},{9,1},{13,5},{2,10},{6,14},... | collective-permute-start | bytes 196616 | tf_op jit(solution)/shard_map/ppermute | solution.py:43

commit v23 on v22

--- a/solution.py
+++ b/solution.py
@@ -140,7 +140,7 @@
 def layer(total, weight, cotangent):
     high, low = split(total)
     pre = dot(high, weight) + dot(low, weight)
-    sigma = jax.nn.sigmoid(pre)
+    sigma = 0.5 + 0.5 * jnp.tanh(0.5 * pre)
     grad = wide(cotangent) * sigma * (1.0 + pre * (1.0 - sigma))
     grad_high, grad_low = split(grad)
     across, down = ((1,), (1,)), ((0,), (0,))
@@ -183,7 +183,7 @@
     third[...] = jnp.where(middle, other, same)
 
 
-def paired_layer_kernel(own, first, third, second, weight, cotangent, beyond, *refs):
+def paired_layer_kernel(own, first, second, third, weight, cotangent, beyond, *refs):
     back_out, mine, other, pre_out = refs
     nodes = cotangent.shape[0]
     middle = in_middle()
@@ -231,7 +231,6 @@
 
 def last_kernel(scale, own, kept, *refs):
     *messages, features_out, weight_out = refs
-    messages = messages[:1] + messages[-1:] + messages[1:-1]
     nodes, half = own.shape[0], kept.shape[1]
     features_out[...] = tree(
         [own[...]] + [wide(message[:nodes]) for message in messages]
@@ -278,8 +277,6 @@
             **forward,
         )(near, features, *gathered)
         layer_call, cotangents = paired_layer_kernel, [cotangent, swap(cotangent, "col", 2)]
-        first, second, third = exchange(sends, "col", True)
-        parts = [first, third, second]
     else:
         layers = 1
         own, *sends = call(
@@ -289,7 +286,7 @@
             **forward,
         )(near, features, *gathered)
         layer_call, cotangents = layer_kernel, [cotangent]
-        parts = exchange(sends, "col", True)
+    parts = exchange(sends, "col", True)
     (far,) = call(
         functools.partial(turn_kernel, side),
         [((across, down), NARROW)],
@@ -335,7 +332,7 @@
         functools.partial(last_kernel, scale),
         [((nodes, width), NARROW), ((width, hidden), jnp.float32)],
         [VMEM] * (n_row + 1),
-    )(own, kept, parts[0], *parts[2:], parts[1])
+    )(own, kept, *parts)
     return act, grad_features, grad_weight
 
 

time: 31.2 us -> 29.7 us (0.952); the launches traced: 31 us -> 29.1 us
  waiting for transfers between devices: 8.76 us -> 7.5 us
  starting transfers between devices: 17.1 us -> 16.4 us
    ppermute x6, starting transfers between devices: 8.82 us -> 7.4 us  [exchange(): lax.ppermute(send, axis, [(s, target(s, d)) for s in range(n)])]
    ppermute x7, starting transfers between devices: 8.24 us -> 9.02 us  [swap(): return lax.ppermute(value, axis, [(s, s ^ distance) for s in range(n)])]
    ppermute x6, waiting for transfers between devices: 5.7 us -> 4.92 us  [exchange(): lax.ppermute(send, axis, [(s, target(s, d)) for s in range(n)])]
    ppermute x7, waiting for transfers between devices: 3.07 us -> 2.58 us  [swap(): return lax.ppermute(value, axis, [(s, s ^ distance) for s in range(n)])]
  transfers between devices with their start and end apart: 13 -> 13, of which waited for: 6 -> 4; matrix products, arithmetic and copies ran while one was open for 0% -> 0% of each run, Pallas kernels for 7% -> 8%
where the time goes in v23:
time: 29.7 us; the launch traced here: 29.1 us
  starting transfers between devices  16.4 us (55%)
  waiting for transfers between devices  7.5 us (25%)
  Pallas kernels  3.67 us (12%)
  between operations  1.47 us (5%)
    ppermute x7, starting transfers between devices, swap(): return lax.ppermute(value, axis, [(s, s ^ distance) for s in range(n)])  9.02 us
    ppermute x6, starting transfers between devices, exchange(): lax.ppermute(send, axis, [(s, target(s, d)) for s in range(n)])  7.4 us
    ppermute x6, waiting for transfers between devices, exchange(): lax.ppermute(send, axis, [(s, target(s, d)) for s in range(n)])  4.92 us
    ppermute x7, waiting for transfers between devices, swap(): return lax.ppermute(value, axis, [(s, s ^ distance) for s in range(n)])  2.58 us
    pallas_call x1, Pallas kernels, per_device(): call(functools.partial(last_kernel, scale), [((nodes, width), NARROW), ((...  0.7 us
    pallas_call x1, Pallas kernels, per_device(): call(functools.partial(dense_kernel, nodes // side, paired), [((down, acr...  0.66 us
    pallas_call x1, Pallas kernels, per_device(): act, = call(act_kernel, [((nodes, hidden), NARROW)], [VMEM])(pre)  0.65 us
  transfers between devices with their start and end apart: 13, of which 4 were waited for; matrix products, arithmetic and copies ran while one was open for 0% of the time, Pallas kernels for 8%

profile of v23, /device:TPU:0, one launch (start us, length us, event | category | flops | bytes accessed | tf_op | source)
XLA Modules:
  0.0 29.1 jit_solution(8230798898693316828)
XLA Ops:
  0.6 0.0 copy-start
  0.6 3.0 %collective-permute-start = (bf16[128,128]{1,0:T(8,128)(2,1)}, bf16[128,128]{1,0:T(8,128)(2,1)S(1)}, u32[]{:S(2)}, u32[]{:S(2)}) collective-permute-start(bf16[128,128]{1,0:T(8,128)(2,1)} %refs_0_.1), channel_id=1, source_target_pairs={{0,8},{4,12},{8,0},{12,4},{1,9},{5,13},{9,1},{13,5},{2,10},{6,14},... | collective-permute-start | bytes 98312 | tf_op jit(solution)/shard_map/ppermute | solution.py:58
  3.6 0.0 collective-permute-start.1
  3.6 0.2 collective-permute-start.2
  3.8 3.0 %collective-permute-start.6 = (bf16[128,256]{1,0:T(8,128)(2,1)}, bf16[128,256]{1,0:T(8,128)(2,1)S(1)}, u32[]{:S(2)}, u32[]{:S(2)}) collective-permute-start(bf16[128,256]{1,0:T(8,128)(2,1)} %refs_6_.1), channel_id=1, source_target_pairs={{0,2},{1,3},{2,0},{3,1},{4,6},{5,7},{6,4},{7,5},{8,10},{9,11},{10,... | collective-permute-start | bytes 196616 | tf_op jit(solution)/shard_map/ppermute | solution.py:58
  6.9 0.0 copy-start.4
  6.9 0.0 copy-start.5
  7.6 0.0 copy-done
  7.6 0.0 copy-done.4
  7.6 0.0 copy-done.5
  7.6 0.0 copy-start.3
  7.7 0.7 %shard_map.95.near.matrix = bf16[512,512]{1,0:T(8,128)(2,1)S(1)} custom-call(bf16[512,512]{1,0:T(8,128)(2,1)S(1)} %shard_map.94.blank, bf16[1,1,8,128,128]{4,3,2,1,0:T(8,128)(2,1)S(1)} %copy-done, s32[1,1,8]{2,1,0:T(1,128)S(1)} %copy-done.4, s32[1,1,8]{2,1,0:T(1,128)S(1)} %copy-done.5, s32[1,1]{1,0:T(1,128)S(6)} %copy.12.count_in), custom_call_target="tpu_custom_call", output_to_operand_aliasing={{}: (0, {})} | custom-call | bytes 1048576 | tf_op jit(solution)/shard_map/pallas_call | solution.py:256
  8.3 0.0 collective-permute-done.refs_1_
  8.3 0.0 collective-permute-done.1.refs_2_
  8.3 0.0 collective-permute-done.2.refs_3_
  8.3 0.1 copy-done.3
  8.4 0.3 shard_map.97
  8.7 1.6 %collective-permute-start.3 = (bf16[256,128]{1,0:T(8,128)(2,1)S(1)}, bf16[256,128]{1,0:T(8,128)(2,1)S(1)}, u32[]{:S(2)}, u32[]{:S(2)}) collective-permute-start(bf16[256,128]{1,0:T(8,128)(2,1)S(1)} %get-tuple-element.19), channel_id=1, source_target_pairs={{0,1},{1,3},{2,0},{3,2},{4,5},{5,7},{6,4},{7,6},{8,9},{9,11},{10,8... | collective-permute-start | bytes 196616 | tf_op jit(solution)/shard_map/ppermute | solution.py:43
  10.3 1.4 %collective-permute-start.4 = (bf16[256,128]{1,0:T(8,128)(2,1)S(1)}, bf16[256,128]{1,0:T(8,128)(2,1)S(1)}, u32[]{:S(2)}, u32[]{:S(2)}) collective-permute-start(bf16[256,128]{1,0:T(8,128)(2,1)S(1)} %get-tuple-element.20), channel_id=1, source_target_pairs={{0,3},{1,2},{2,1},{3,0},{4,7},{5,6},{6,5},{7,4},{8,11},{9,10},{10,... | collective-permute-start | bytes 196616 | tf_op jit(solution)/shard_map/ppermute | solution.py:43
  11.7 0.0 copy-start.1
  11.7 0.0 copy-start.2
  11.7 1.6 %collective-permute-start.5 = (bf16[256,128]{1,0:T(8,128)(2,1)S(1)}, bf16[256,128]{1,0:T(8,128)(2,1)S(1)}, u32[]{:S(2)}, u32[]{:S(2)}) collective-permute-start(bf16[256,128]{1,0:T(8,128)(2,1)S(1)} %get-tuple-element.21), channel_id=1, source_target_pairs={{0,2},{1,0},{2,3},{3,1},{4,6},{5,4},{6,7},{7,5},{8,10},{9,8},{10,1... | collective-permute-start | bytes 196616 | tf_op jit(solution)/shard_map/ppermute | solution.py:43
  13.3 0.3 %shard_map.96.refs_0_.matrix = bf16[512,512]{1,0:T(8,128)(2,1)S(1)} custom-call(bf16[512,512]{1,0:T(8,128)(2,1)S(1)} %shard_map.95.near.matrix), custom_call_target="tpu_custom_call" | custom-call | bytes 1572864 | tf_op jit(solution)/shard_map/pallas_call | solution.py:290
  13.6 0.0 collective-permute-done.6.refs_7_
  13.6 3.6 %collective-permute-done.3.refs_2_ = bf16[256,128]{1,0:T(8,128)(2,1)S(1)} collective-permute-done((bf16[256,128]{1,0:T(8,128)(2,1)S(1)}, bf16[256,128]{1,0:T(8,128)(2,1)S(1)}, u32[]{:S(2)}, u32[]{:S(2)}) %collective-permute-start.3) | collective-permute-done | bytes 65568 | tf_op jit(solution)/shard_map/ppermute | solution.py:43
  17.2 0.0 collective-permute-done.4.refs_3_
  17.2 0.0 collective-permute-done.5.refs_4_
  17.2 0.0 copy-done.1
  17.2 0.0 copy-done.2
  17.2 0.5 %shard_map.98 = (bf16[256,128]{1,0:T(8,128)(2,1)S(1)}, f32[128,128]{1,0:T(8,128)S(1)}, bf16[128,128]{1,0:T(8,128)(2,1)S(1)}, f32[128,256]{1,0:T(8,128)S(1)}) custom-call(bf16[512,512]{1,0:T(8,128)(2,1)S(1)} %shard_map.96.refs_0_.matrix, bf16[256,128]{1,0:T(8,128)(2,1)S(1)} %get-tuple-element.18.refs_1_, bf16[256,128]{1,0:T(8,128)(2,1)S(1)} %collective-permute-done.3.refs_2_, ...), custom_call_target="tpu_custom_call" | custom-call | flops 117440512 | tf_op jit(solution)/shard_map/pallas_call | solution.py:299
  17.8 0.1 collective-permute-start.8
  17.9 1.5 %collective-permute-start.7 = (bf16[256,128]{1,0:T(8,128)(2,1)S(1)}, bf16[256,128]{1,0:T(8,128)(2,1)S(1)}, u32[]{:S(2)}, u32[]{:S(2)}) collective-permute-start(bf16[256,128]{1,0:T(8,128)(2,1)S(1)} %get-tuple-element.23.back), channel_id=1, source_target_pairs={{0,1},{1,0},{2,3},{3,2},{4,5},{5,4},{6,7},{7,6},{8,9},{9,8},{10,11... | collective-permute-start | bytes 196616 | tf_op jit(solution)/shard_map/ppermute | solution.py:58
  19.4 0.0 collective-permute-done.8.came
  19.4 1.2 %collective-permute-start.9 = (bf16[128,128]{1,0:T(8,128)(2,1)S(1)}, bf16[128,128]{1,0:T(8,128)(2,1)S(1)}, u32[]{:S(2)}, u32[]{:S(2)}) collective-permute-start(bf16[128,128]{1,0:T(8,128)(2,1)S(1)} %shard_map.101.refs_1_), channel_id=1, source_target_pairs={{0,1},{1,0},{2,3},{3,2},{4,5},{5,4},{6,7},{7,6},{8,9},{9,8},{10,11... | collective-permute-start | bytes 98312 | tf_op jit(solution)/shard_map/ppermute | solution.py:58
  20.6 0.2 shard_map.100.begun
  20.8 2.6 %collective-permute-done.9.refs_2_ = bf16[128,128]{1,0:T(8,128)(2,1)S(1)} collective-permute-done((bf16[128,128]{1,0:T(8,128)(2,1)S(1)}, bf16[128,128]{1,0:T(8,128)(2,1)S(1)}, u32[]{:S(2)}, u32[]{:S(2)}) %collective-permute-start.9) | collective-permute-done | bytes 32800 | tf_op jit(solution)/shard_map/ppermute | solution.py:58
  23.4 0.0 collective-permute-done.7.refs_0_
  23.4 0.2 shard_map.102
  23.6 0.1 collective-permute-start.10
  23.7 1.4 %collective-permute-start.11 = (bf16[256,128]{1,0:T(8,128)(2,1)S(1)}, bf16[256,128]{1,0:T(8,128)(2,1)S(1)}, u32[]{:S(2)}, u32[]{:S(2)}) collective-permute-start(bf16[256,128]{1,0:T(8,128)(2,1)S(1)} %get-tuple-element.29), channel_id=1, source_target_pairs={{0,8},{4,12},{8,0},{12,4},{1,9},{5,13},{9,1},{13,5},{2,10},{6,14},... | collective-permute-start | bytes 196616 | tf_op jit(solution)/shard_map/ppermute | solution.py:43
  25.1 1.4 %collective-permute-start.12 = (bf16[256,128]{1,0:T(8,128)(2,1)S(1)}, bf16[256,128]{1,0:T(8,128)(2,1)S(1)}, u32[]{:S(2)}, u32[]{:S(2)}) collective-permute-start(bf16[256,128]{1,0:T(8,128)(2,1)S(1)} %get-tuple-element.30), channel_id=1, source_target_pairs={{0,12},{4,0},{8,4},{12,8},{1,13},{5,1},{9,5},{13,9},{2,14},{6,2},{... | collective-permute-start | bytes 196616 | tf_op jit(solution)/shard_map/ppermute | solution.py:43
  26.5 0.7 %shard_map.99 = bf16[128,256]{1,0:T(8,128)(2,1)} custom-call(f32[128,256]{1,0:T(8,128)S(1)} %get-tuple-element.22.pre), custom_call_target="tpu_custom_call" | custom-call | tf_op jit(solution)/shard_map/pallas_call | solution.py:317
  27.1 0.3 %collective-permute-done.10.refs_0_ = bf16[256,128]{1,0:T(8,128)(2,1)S(1)} collective-permute-done((bf16[256,128]{1,0:T(8,128)(2,1)S(1)}, bf16[256,128]{1,0:T(8,128)(2,1)S(1)}, u32[]{:S(2)}, u32[]{:S(2)}) %collective-permute-start.10) | collective-permute-done | bytes 65568 | tf_op jit(solution)/shard_map/ppermute | solution.py:43
  27.5 1.0 %collective-permute-done.11.refs_1_ = bf16[256,128]{1,0:T(8,128)(2,1)S(1)} collective-permute-done((bf16[256,128]{1,0:T(8,128)(2,1)S(1)}, bf16[256,128]{1,0:T(8,128)(2,1)S(1)}, u32[]{:S(2)}, u32[]{:S(2)}) %collective-permute-start.11) | collective-permute-done | bytes 65568 | tf_op jit(solution)/shard_map/ppermute | solution.py:43
  28.4 0.0 collective-permute-done.12.refs_2_
  28.4 0.7 %shard_map.103 = (bf16[128,128]{1,0:T(8,128)(2,1)}, f32[128,256]{1,0:T(8,128)}) custom-call(f32[128,128]{1,0:T(8,128)S(1)} %get-tuple-element.26.own, bf16[128,128]{1,0:T(8,128)(2,1)S(1)} %get-tuple-element.27.kept, bf16[256,128]{1,0:T(8,128)(2,1)S(1)} %collective-permute-done.10.refs_0_, bf16[256,128]{1,0:T(8,128)(2,1)S(1)} %collective-permute-done.11.refs_1_, ...), custom_call_target="tpu_custom_call" | custom-call | tf_op jit(solution)/shard_map/pallas_call | solution.py:331
  (2 shorter events, 0.0 us)
Async XLA Ops:
  0.6 7.0 %copy-start = (bf16[1,1,8,128,128]{4,3,2,1,0:T(8,128)(2,1)S(1)}, bf16[1,1,8,128,128]{4,3,2,1,0:T(8,128)(2,1)}, u32[]{:S(2)}) copy-start(bf16[1,1,8,128,128]{4,3,2,1,0:T(8,128)(2,1)} %vals.1) | copy-start | bytes 786436
  0.6 7.7 %collective-permute-start = (bf16[128,128]{1,0:T(8,128)(2,1)}, bf16[128,128]{1,0:T(8,128)(2,1)S(1)}, u32[]{:S(2)}, u32[]{:S(2)}) collective-permute-start(bf16[128,128]{1,0:T(8,128)(2,1)} %refs_0_.1), channel_id=1, source_target_pairs={{0,8},{4,12},{8,0},{12,4},{1,9},{5,13},{9,1},{13,5},{2,10},{6,14},... | collective-permute-start | bytes 98312 | tf_op jit(solution)/shard_map/ppermute | solution.py:58
  3.6 4.7 %collective-permute-start.1 = (bf16[128,128]{1,0:T(8,128)(2,1)}, bf16[128,128]{1,0:T(8,128)(2,1)S(1)}, u32[]{:S(2)}, u32[]{:S(2)}) collective-permute-start(bf16[128,128]{1,0:T(8,128)(2,1)} %refs_0_.1), channel_id=1, source_target_pairs={{0,12},{4,8},{8,4},{12,0},{1,13},{5,9},{9,5},{13,1},{2,14},{6,10},... | collective-permute-start | bytes 98312 | tf_op jit(solution)/shard_map/ppermute | solution.py:58
  3.6 4.7 %collective-permute-start.2 = (bf16[128,128]{1,0:T(8,128)(2,1)}, bf16[128,128]{1,0:T(8,128)(2,1)S(1)}, u32[]{:S(2)}, u32[]{:S(2)}) collective-permute-start(bf16[128,128]{1,0:T(8,128)(2,1)} %refs_0_.1), channel_id=1, source_target_pairs={{0,4},{4,0},{8,12},{12,8},{1,5},{5,1},{9,13},{13,9},{2,6},{6,2},{1... | collective-permute-start | bytes 98312 | tf_op jit(solution)/shard_map/ppermute | solution.py:58
  3.8 9.8 %collective-permute-start.6 = (bf16[128,256]{1,0:T(8,128)(2,1)}, bf16[128,256]{1,0:T(8,128)(2,1)S(1)}, u32[]{:S(2)}, u32[]{:S(2)}) collective-permute-start(bf16[128,256]{1,0:T(8,128)(2,1)} %refs_6_.1), channel_id=1, source_target_pairs={{0,2},{1,3},{2,0},{3,1},{4,6},{5,7},{6,4},{7,5},{8,10},{9,11},{10,... | collective-permute-start | bytes 196616 | tf_op jit(solution)/shard_map/ppermute | solution.py:58
  6.9 0.7 %copy-start.4 = (s32[1,1,8]{2,1,0:T(1,128)S(1)}, s32[1,1,8]{2,1,0:T(1,128)}, u32[]{:S(2)}) copy-start(s32[1,1,8]{2,1,0:T(1,128)} %rows_in.1) | copy-start | bytes 100
  6.9 0.7 %copy-start.5 = (s32[1,1,8]{2,1,0:T(1,128)S(1)}, s32[1,1,8]{2,1,0:T(1,128)}, u32[]{:S(2)}) copy-start(s32[1,1,8]{2,1,0:T(1,128)} %cols_in.1) | copy-start | bytes 100
  7.6 0.8 %copy-start.3 = (bf16[128,128]{1,0:T(8,128)(2,1)S(1)}, bf16[128,128]{1,0:T(8,128)(2,1)}, u32[]{:S(2)}) copy-start(bf16[128,128]{1,0:T(8,128)(2,1)} %refs_0_.1) | copy-start | bytes 98308
  8.7 8.5 %collective-permute-start.3 = (bf16[256,128]{1,0:T(8,128)(2,1)S(1)}, bf16[256,128]{1,0:T(8,128)(2,1)S(1)}, u32[]{:S(2)}, u32[]{:S(2)}) collective-permute-start(bf16[256,128]{1,0:T(8,128)(2,1)S(1)} %get-tuple-element.19), channel_id=1, source_target_pairs={{0,1},{1,3},{2,0},{3,2},{4,5},{5,7},{6,4},{7,6},{8,9},{9,11},{10,8... | collective-permute-start | bytes 196616 | tf_op jit(solution)/shard_map/ppermute | solution.py:43
  10.3 6.9 %collective-permute-start.4 = (bf16[256,128]{1,0:T(8,128)(2,1)S(1)}, bf16[256,128]{1,0:T(8,128)(2,1)S(1)}, u32[]{:S(2)}, u32[]{:S(2)}) collective-permute-start(bf16[256,128]{1,0:T(8,128)(2,1)S(1)} %get-tuple-element.20), channel_id=1, source_target_pairs={{0,3},{1,2},{2,1},{3,0},{4,7},{5,6},{6,5},{7,4},{8,11},{9,10},{10,... | collective-permute-start | bytes 196616 | tf_op jit(solution)/shard_map/ppermute | solution.py:43
  11.7 5.5 %copy-start.1 = (bf16[128,256]{1,0:T(8,128)(2,1)S(1)}, bf16[128,256]{1,0:T(8,128)(2,1)}, u32[]{:S(2)}) copy-start(bf16[128,256]{1,0:T(8,128)(2,1)} %refs_5_.1) | copy-start | bytes 196612
  11.7 5.5 %copy-start.2 = (bf16[128,256]{1,0:T(8,128)(2,1)S(1)}, bf16[128,256]{1,0:T(8,128)(2,1)}, u32[]{:S(2)}) copy-start(bf16[128,256]{1,0:T(8,128)(2,1)} %refs_6_.1) | copy-start | bytes 196612
  11.7 5.5 %collective-permute-start.5 = (bf16[256,128]{1,0:T(8,128)(2,1)S(1)}, bf16[256,128]{1,0:T(8,128)(2,1)S(1)}, u32[]{:S(2)}, u32[]{:S(2)}) collective-permute-start(bf16[256,128]{1,0:T(8,128)(2,1)S(1)} %get-tuple-element.21), channel_id=1, source_target_pairs={{0,2},{1,0},{2,3},{3,1},{4,6},{5,4},{6,7},{7,5},{8,10},{9,8},{10,1... | collective-permute-start | bytes 196616 | tf_op jit(solution)/shard_map/ppermute | solution.py:43
  17.8 1.6 %collective-permute-start.8 = (bf16[128,128]{1,0:T(8,128)(2,1)S(1)}, bf16[128,128]{1,0:T(8,128)(2,1)S(1)}, u32[]{:S(2)}, u32[]{:S(2)}) collective-permute-start(bf16[128,128]{1,0:T(8,128)(2,1)S(1)} %get-tuple-element.25), channel_id=1, source_target_pairs={{0,4},{4,0},{8,12},{12,8},{1,5},{5,1},{9,13},{13,9},{2,6},{6,2},{1... | collective-permute-start | bytes 98312 | tf_op jit(solution)/shard_map/ppermute | solution.py:58
  17.9 5.5 %collective-permute-start.7 = (bf16[256,128]{1,0:T(8,128)(2,1)S(1)}, bf16[256,128]{1,0:T(8,128)(2,1)S(1)}, u32[]{:S(2)}, u32[]{:S(2)}) collective-permute-start(bf16[256,128]{1,0:T(8,128)(2,1)S(1)} %get-tuple-element.23.back), channel_id=1, source_target_pairs={{0,1},{1,0},{2,3},{3,2},{4,5},{5,4},{6,7},{7,6},{8,9},{9,8},{10,11... | collective-permute-start | bytes 196616 | tf_op jit(solution)/shard_map/ppermute | solution.py:58
  19.4 4.0 %collective-permute-start.9 = (bf16[128,128]{1,0:T(8,128)(2,1)S(1)}, bf16[128,128]{1,0:T(8,128)(2,1)S(1)}, u32[]{:S(2)}, u32[]{:S(2)}) collective-permute-start(bf16[128,128]{1,0:T(8,128)(2,1)S(1)} %shard_map.101.refs_1_), channel_id=1, source_target_pairs={{0,1},{1,0},{2,3},{3,2},{4,5},{5,4},{6,7},{7,6},{8,9},{9,8},{10,11... | collective-permute-start | bytes 98312 | tf_op jit(solution)/shard_map/ppermute | solution.py:58
  23.6 3.8 %collective-permute-start.10 = (bf16[256,128]{1,0:T(8,128)(2,1)S(1)}, bf16[256,128]{1,0:T(8,128)(2,1)S(1)}, u32[]{:S(2)}, u32[]{:S(2)}) collective-permute-start(bf16[256,128]{1,0:T(8,128)(2,1)S(1)} %get-tuple-element.28), channel_id=1, source_target_pairs={{0,4},{4,8},{8,12},{12,0},{1,5},{5,9},{9,13},{13,1},{2,6},{6,10},{... | collective-permute-start | bytes 196616 | tf_op jit(solution)/shard_map/ppermute | solution.py:43
  23.7 4.7 %collective-permute-start.11 = (bf16[256,128]{1,0:T(8,128)(2,1)S(1)}, bf16[256,128]{1,0:T(8,128)(2,1)S(1)}, u32[]{:S(2)}, u32[]{:S(2)}) collective-permute-start(bf16[256,128]{1,0:T(8,128)(2,1)S(1)} %get-tuple-element.29), channel_id=1, source_target_pairs={{0,8},{4,12},{8,0},{12,4},{1,9},{5,13},{9,1},{13,5},{2,10},{6,14},... | collective-permute-start | bytes 196616 | tf_op jit(solution)/shard_map/ppermute | solution.py:43
  25.1 3.4 %collective-permute-start.12 = (bf16[256,128]{1,0:T(8,128)(2,1)S(1)}, bf16[256,128]{1,0:T(8,128)(2,1)S(1)}, u32[]{:S(2)}, u32[]{:S(2)}) collective-permute-start(bf16[256,128]{1,0:T(8,128)(2,1)S(1)} %get-tuple-element.30), channel_id=1, source_target_pairs={{0,12},{4,0},{8,4},{12,8},{1,13},{5,1},{9,5},{13,9},{2,14},{6,2},{... | collective-permute-start | bytes 196616 | tf_op jit(solution)/shard_map/ppermute | solution.py:43

commit v24 on v19

--- a/solution.py
+++ b/solution.py
@@ -149,21 +149,21 @@
     return pre, back, term
 
 
-def halve(term, mine, other):
-    half = mine.shape[1]
+def store_layer(back, term, message, other):
+    nodes, half = back.shape[0], other.shape[1]
     odd = odd_row()
     left, right = term[:, :half], term[:, half:]
-    mine[...] = jnp.where(odd, right, left)
+    message[:nodes] = back.astype(message.dtype)
+    message[nodes:] = jnp.where(odd, right, left).astype(message.dtype)
     other[...] = jnp.where(odd, left, right).astype(other.dtype)
 
 
 def layer_kernel(*refs):
-    *parts, weight, cotangent, back_out, mine, other, pre_out = refs
+    *parts, weight, cotangent, message, other, pre_out = refs
     total = tree([wide(part[...]) for part in parts])
     pre, back, term = layer(total, weight[...], cotangent[...])
     pre_out[...] = pre
-    back_out[...] = back.astype(back_out.dtype)
-    halve(term, mine, other)
+    store_layer(back, term, message, other)
 
 
 def in_middle():
@@ -184,7 +184,7 @@
 
 
 def paired_layer_kernel(own, first, second, third, weight, cotangent, beyond, *refs):
-    back_out, mine, other, pre_out = refs
+    message, other, pre_out = refs
     nodes = cotangent.shape[0]
     middle = in_middle()
     partner = jnp.where(middle, third[...], first[...])
@@ -197,24 +197,35 @@
     )
     pre, back, term = layer(total, weight[...], both)
     pre_out[...] = jnp.where(high_col, pre[nodes:], pre[:nodes])
-    back_out[...] = back.astype(back_out.dtype)
-    halve(term, mine, other)
-
-
-def add_kernel(mine, came, out):
-    out[...] = (mine[...] + wide(came[...])).astype(out.dtype)
+    store_layer(back, term, message, other)
+
+
+def message_kernel(sent, came, message):
+    nodes = sent.shape[0] - came.shape[0]
+    message[:nodes] = sent[:nodes]
+    message[nodes:] = (wide(sent[nodes:]) + wide(came[...])).astype(message.dtype)
 
 
 def act_kernel(pre, act):
     act[...] = (pre[...] * jax.nn.sigmoid(pre[...])).astype(act.dtype)
 
 
-def backward_kernel(n, matrix, *refs):
-    backs, halves, (own, kept, *sends, product) = refs[:n], refs[n : 2 * n], refs[2 * n :]
+def begin_kernel(backs, matrix, message, product):
+    product[...] = dot(matrix[:, :backs], message[:backs])
+
+
+def backward_kernel(n, n_others, matrix, begun, *refs):
+    messages, others, refs = refs[:n], refs[n : n + n_others], refs[n + n_others :]
+    own, kept, *sends, product = refs
     rows = own.shape[0]
-    product[...] = dot(matrix[...], jnp.concatenate([back[...] for back in backs], axis=0))
+    backs = messages[0].shape[0] - kept.shape[0]
+    stacked = jnp.concatenate([message[:backs] for message in messages[1:]], axis=0)
+    product[...] = begun[...] + dot(matrix[:, backs:], stacked)
     own[...] = product[:rows]
-    term = tree([wide(half[...]) for half in halves]).astype(kept.dtype)
+    term = tree([wide(message[backs:]) for message in messages])
+    if others:
+        term = term + tree([wide(other[...]) for other in others])
+    term = term.astype(kept.dtype)
     kept[...] = term
     here, size = lax.axis_index("row"), lax.axis_size("row")
     for d, send in enumerate(sends, 1):
@@ -290,34 +301,41 @@
 
     half = hidden // 2
     square = (width, half)
-    back, mine, other, pre = call(
+    message = ((layers * nodes + width, width), NARROW)
+    sent, other, pre = call(
         layer_call,
-        [
-            ((layers * nodes, width), NARROW),
-            (square, jnp.float32),
-            (square, NARROW),
-            ((nodes, hidden), jnp.float32),
-        ],
+        [message, (square, NARROW), ((nodes, hidden), jnp.float32)],
         [VMEM] * (n_col + 1 + len(cotangents)),
         flops=14 * layers * nodes * width * hidden,
         after=[far],
     )(own, *parts, weight, *cotangents)
-    (term,) = call(add_kernel, [(square, NARROW)], [VMEM] * 2)(mine, swap(other, "row", 1))
     if paired:
-        backs, terms = [back, swap(back, "col", 1)], [term, swap(term, "col", 1)]
+        corner = [
+            (r * n_col + c, (r ^ 1) * n_col + (c ^ 1)) for r in range(n_row) for c in range(n_col)
+        ]
+        messages = [sent, swap(sent, "col", 1)]
+        others = [swap(other, "row", 1), lax.ppermute(other, ("row", "col"), corner)]
     else:
-        backs = [back] + exchange([back] * (n_col - 1), "col", False)
-        terms = [term] + exchange([term] * (n_col - 1), "col", False)
+        (sent,) = call(message_kernel, [message], [VMEM] * 2)(sent, swap(other, "row", 1))
+        messages = [sent] + exchange([sent] * (n_col - 1), "col", False)
+        others = []
     (act,) = call(act_kernel, [((nodes, hidden), NARROW)], [VMEM])(pre)
 
+    message = ((nodes + width, width), NARROW)
+    (begun,) = call(
+        functools.partial(begin_kernel, layers * nodes),
+        [((across, width), jnp.float32)],
+        [VMEM] * 2,
+        **forward,
+    )(far, sent)
     message = ((nodes + width, width), NARROW)
     own, kept, *sends = call(
-        functools.partial(backward_kernel, len(backs)),
+        functools.partial(backward_kernel, len(messages), len(others)),
         [((nodes, width), jnp.float32), (square, NARROW)] + [message] * (n_row - 1),
-        [VMEM] * (1 + 2 * len(backs)),
+        [VMEM] * (2 + len(messages) + len(others)),
         scratch=[pltpu.VMEM((across, width), jnp.float32)],
         **forward,
-    )(far, *backs, *terms)
+    )(far, begun, *messages, *others)
     parts = exchange(sends, "row", True)
 
     scale = float(nodes * n_row * n_col) ** -0.5

time: 29.8 us -> 28.9 us (0.970)
  waiting for transfers between devices: 7.72 us -> 7.25 us
  starting transfers between devices: 16.4 us -> 16.1 us
    ppermute x0 -> x1, waiting for transfers between devices: none -> 2.96 us  [per_device(): lax.ppermute(other, ('row', 'col'), corner)]
    ppermute x7 -> x6, waiting for transfers between devices: 2.8 us -> 0.02 us  [swap(): return lax.ppermute(value, axis, [(s, s ^ distance) for s in range(n)])]
    ppermute x7 -> x6, starting transfers between devices: 9.03 us -> 8.17 us  [swap(): return lax.ppermute(value, axis, [(s, s ^ distance) for s in range(n)])]
    ppermute x6, waiting for transfers between devices: 4.92 us -> 4.27 us  [exchange(): lax.ppermute(send, axis, [(s, target(s, d)) for s in range(n)])]
    ppermute x6, starting transfers between devices: 7.4 us -> 7.97 us  [exchange(): lax.ppermute(send, axis, [(s, target(s, d)) for s in range(n)])]
  transfers between devices with their start and end apart: 13 -> 13, of which waited for: 4 -> 6; matrix products, arithmetic and copies ran while one was open for 0% -> 0% of each run, Pallas kernels for 7% -> 8%
where the time goes in v24:
time: 28.9 us; the launch traced here: 28.5 us
  starting transfers between devices  16.1 us (56%)
  waiting for transfers between devices  7.25 us (25%)
  Pallas kernels  3.63 us (13%)
  between operations  1.44 us (5%)
    ppermute x6, starting transfers between devices, swap(): return lax.ppermute(value, axis, [(s, s ^ distance) for s in range(n)])  8.17 us
    ppermute x6, starting transfers between devices, exchange(): lax.ppermute(send, axis, [(s, target(s, d)) for s in range(n)])  7.97 us
    ppermute x6, waiting for transfers between devices, exchange(): lax.ppermute(send, axis, [(s, target(s, d)) for s in range(n)])  4.27 us
    ppermute x1, waiting for transfers between devices, per_device(): lax.ppermute(other, ('row', 'col'), corner)  2.96 us
    pallas_call x1, Pallas kernels, per_device(): call(functools.partial(last_kernel, scale), [((nodes, width), NARROW), ((...  0.69 us
    pallas_call x1, Pallas kernels, per_device(): call(functools.partial(dense_kernel, nodes // side, paired), [((down, acr...  0.66 us
    pallas_call x1, Pallas kernels, per_device(): act, = call(act_kernel, [((nodes, hidden), NARROW)], [VMEM])(pre)  0.65 us
  transfers between devices with their start and end apart: 13, of which 6 were waited for; matrix products, arithmetic and copies ran while one was open for 0% of the time, Pallas kernels for 8%

profile of v24, /device:TPU:0, one launch (start us, length us, event | category | flops | bytes accessed | tf_op | source)
XLA Modules:
  0.0 28.5 jit_solution(10544472889112186848)
XLA Ops:
  0.6 0.0 copy-start
  0.6 2.4 %collective-permute-start.1 = (bf16[128,128]{1,0:T(8,128)(2,1)}, bf16[128,128]{1,0:T(8,128)(2,1)S(1)}, u32[]{:S(2)}, u32[]{:S(2)}) collective-permute-start(bf16[128,128]{1,0:T(8,128)(2,1)} %refs_0_.1), channel_id=1, source_target_pairs={{0,12},{4,8},{8,4},{12,0},{1,13},{5,9},{9,5},{13,1},{2,14},{6,10},... | collective-permute-start | bytes 98312 | tf_op jit(solution)/shard_map/ppermute | solution.py:58
  3.1 0.6 %collective-permute-start = (bf16[128,128]{1,0:T(8,128)(2,1)}, bf16[128,128]{1,0:T(8,128)(2,1)S(1)}, u32[]{:S(2)}, u32[]{:S(2)}) collective-permute-start(bf16[128,128]{1,0:T(8,128)(2,1)} %refs_0_.1), channel_id=1, source_target_pairs={{0,8},{4,12},{8,0},{12,4},{1,9},{5,13},{9,1},{13,5},{2,10},{6,14},... | collective-permute-start | bytes 98312 | tf_op jit(solution)/shard_map/ppermute | solution.py:58
  3.7 0.0 collective-permute-start.2
  3.8 2.8 %collective-permute-start.6 = (bf16[128,256]{1,0:T(8,128)(2,1)}, bf16[128,256]{1,0:T(8,128)(2,1)S(1)}, u32[]{:S(2)}, u32[]{:S(2)}) collective-permute-start(bf16[128,256]{1,0:T(8,128)(2,1)} %refs_6_.1), channel_id=1, source_target_pairs={{0,2},{1,3},{2,0},{3,1},{4,6},{5,7},{6,4},{7,5},{8,10},{9,11},{10,... | collective-permute-start | bytes 196616 | tf_op jit(solution)/shard_map/ppermute | solution.py:58
  6.6 0.0 copy-start.4
  6.7 0.0 copy-start.5
  7.3 0.0 copy-done
  7.3 0.0 copy-done.4
  7.3 0.0 copy-done.5
  7.4 0.0 copy-start.3
  7.4 0.7 %shard_map.95.near.matrix = bf16[512,512]{1,0:T(8,128)(2,1)S(1)} custom-call(bf16[512,512]{1,0:T(8,128)(2,1)S(1)} %shard_map.94.blank, bf16[1,1,8,128,128]{4,3,2,1,0:T(8,128)(2,1)S(1)} %copy-done, s32[1,1,8]{2,1,0:T(1,128)S(1)} %copy-done.4, s32[1,1,8]{2,1,0:T(1,128)S(1)} %copy-done.5, s32[1,1]{1,0:T(1,128)S(6)} %copy.12.count_in), custom_call_target="tpu_custom_call", output_to_operand_aliasing={{}: (0, {})} | custom-call | bytes 1048576 | tf_op jit(solution)/shard_map/pallas_call | solution.py:261
  8.0 0.0 collective-permute-done.1.refs_2_
  8.0 0.0 collective-permute-done.refs_1_
  8.1 0.0 collective-permute-done.2.refs_3_
  8.1 0.1 copy-done.3
  8.1 0.3 %shard_map.97 = (bf16[256,128]{1,0:T(8,128)(2,1)S(1)}, bf16[256,128]{1,0:T(8,128)(2,1)S(1)}, bf16[256,128]{1,0:T(8,128)(2,1)S(1)}, bf16[256,128]{1,0:T(8,128)(2,1)S(1)}) custom-call(bf16[512,512]{1,0:T(8,128)(2,1)S(1)} %shard_map.95.near.matrix, bf16[128,128]{1,0:T(8,128)(2,1)S(1)} %copy-done.3, bf16[128,128]{1,0:T(8,128)(2,1)S(1)} %collective-permute-done.refs_1_, ...), custom_call_target="tpu_custom_call" | custom-call | flops 67108864 | bytes 1048576 | tf_op jit(solution)/shard_map/pallas_call | solution.py:278
  8.4 1.6 %collective-permute-start.3 = (bf16[256,128]{1,0:T(8,128)(2,1)S(1)}, bf16[256,128]{1,0:T(8,128)(2,1)S(1)}, u32[]{:S(2)}, u32[]{:S(2)}) collective-permute-start(bf16[256,128]{1,0:T(8,128)(2,1)S(1)} %get-tuple-element.18), channel_id=1, source_target_pairs={{0,1},{1,3},{2,0},{3,2},{4,5},{5,7},{6,4},{7,6},{8,9},{9,11},{10,8... | collective-permute-start | bytes 196616 | tf_op jit(solution)/shard_map/ppermute | solution.py:43
  10.1 1.6 %collective-permute-start.4 = (bf16[256,128]{1,0:T(8,128)(2,1)S(1)}, bf16[256,128]{1,0:T(8,128)(2,1)S(1)}, u32[]{:S(2)}, u32[]{:S(2)}) collective-permute-start(bf16[256,128]{1,0:T(8,128)(2,1)S(1)} %get-tuple-element.19), channel_id=1, source_target_pairs={{0,3},{1,2},{2,1},{3,0},{4,7},{5,6},{6,5},{7,4},{8,11},{9,10},{10,... | collective-permute-start | bytes 196616 | tf_op jit(solution)/shard_map/ppermute | solution.py:43
  11.7 0.0 copy-start.1
  11.7 0.0 copy-start.2
  11.7 1.6 %collective-permute-start.5 = (bf16[256,128]{1,0:T(8,128)(2,1)S(1)}, bf16[256,128]{1,0:T(8,128)(2,1)S(1)}, u32[]{:S(2)}, u32[]{:S(2)}) collective-permute-start(bf16[256,128]{1,0:T(8,128)(2,1)S(1)} %get-tuple-element.20), channel_id=1, source_target_pairs={{0,2},{1,0},{2,3},{3,1},{4,6},{5,4},{6,7},{7,5},{8,10},{9,8},{10,1... | collective-permute-start | bytes 196616 | tf_op jit(solution)/shard_map/ppermute | solution.py:43
  13.3 0.3 %shard_map.96.refs_0_.matrix = bf16[512,512]{1,0:T(8,128)(2,1)S(1)} custom-call(bf16[512,512]{1,0:T(8,128)(2,1)S(1)} %shard_map.95.near.matrix), custom_call_target="tpu_custom_call" | custom-call | bytes 1572864 | tf_op jit(solution)/shard_map/pallas_call | solution.py:295
  13.6 0.0 collective-permute-done.6.refs_7_
  13.6 0.4 %collective-permute-done.3.refs_2_ = bf16[256,128]{1,0:T(8,128)(2,1)S(1)} collective-permute-done((bf16[256,128]{1,0:T(8,128)(2,1)S(1)}, bf16[256,128]{1,0:T(8,128)(2,1)S(1)}, u32[]{:S(2)}, u32[]{:S(2)}) %collective-permute-start.3) | collective-permute-done | bytes 65568 | tf_op jit(solution)/shard_map/ppermute | solution.py:43
  14.0 2.4 %collective-permute-done.4.refs_3_ = bf16[256,128]{1,0:T(8,128)(2,1)S(1)} collective-permute-done((bf16[256,128]{1,0:T(8,128)(2,1)S(1)}, bf16[256,128]{1,0:T(8,128)(2,1)S(1)}, u32[]{:S(2)}, u32[]{:S(2)}) %collective-permute-start.4) | collective-permute-done | bytes 65568 | tf_op jit(solution)/shard_map/ppermute | solution.py:43
  16.4 0.2 collective-permute-done.5.refs_4_
  16.6 0.0 copy-done.1
  16.6 0.0 copy-done.2
  16.7 0.5 %shard_map.98 = (bf16[384,128]{1,0:T(8,128)(2,1)S(1)}, bf16[128,128]{1,0:T(8,128)(2,1)S(1)}, f32[128,256]{1,0:T(8,128)S(1)}) custom-call(bf16[512,512]{1,0:T(8,128)(2,1)S(1)} %shard_map.96.refs_0_.matrix, bf16[256,128]{1,0:T(8,128)(2,1)S(1)} %get-tuple-element.17.refs_1_, bf16[256,128]{1,0:T(8,128)(2,1)S(1)} %collective-permute-done.3.refs_2_, ...), custom_call_target="tpu_custom_call" | custom-call | flops 117440512 | tf_op jit(solution)/shard_map/pallas_call | solution.py:305
  17.2 1.8 %collective-permute-start.7 = (bf16[384,128]{1,0:T(8,128)(2,1)S(1)}, bf16[384,128]{1,0:T(8,128)(2,1)S(1)}, u32[]{:S(2)}, u32[]{:S(2)}) collective-permute-start(bf16[384,128]{1,0:T(8,128)(2,1)S(1)} %get-tuple-element.22.message.refs_0_), channel_id=1, source_target_pairs={{0,1},{1,0},{2,3},{3,2},{4,5},{5,4},{6,7},{7,6},{8,9},{9,8},{10,11... | collective-permute-start | bytes 294920 | tf_op jit(solution)/shard_map/ppermute | solution.py:58
  19.0 0.0 collective-permute-start.9
  19.0 0.4 %collective-permute-start.8 = (bf16[128,128]{1,0:T(8,128)(2,1)S(1)}, bf16[128,128]{1,0:T(8,128)(2,1)S(1)}, u32[]{:S(2)}, u32[]{:S(2)}) collective-permute-start(bf16[128,128]{1,0:T(8,128)(2,1)S(1)} %get-tuple-element.23), channel_id=1, source_target_pairs={{0,4},{4,0},{8,12},{12,8},{1,5},{5,1},{9,13},{13,9},{2,6},{6,2},{1... | collective-permute-start | bytes 98312 | tf_op jit(solution)/shard_map/ppermute | solution.py:58
  19.4 0.2 shard_map.100.begun
  19.6 3.0 %collective-permute-done.9.refs_3_ = bf16[128,128]{1,0:T(8,128)(2,1)S(1)} collective-permute-done((bf16[128,128]{1,0:T(8,128)(2,1)S(1)}, bf16[128,128]{1,0:T(8,128)(2,1)S(1)}, u32[]{:S(2)}, u32[]{:S(2)}) %collective-permute-start.9) | collective-permute-done | bytes 32800 | tf_op jit(solution)/shard_map/ppermute | solution.py:317
  22.5 0.0 collective-permute-done.8.refs_2_
  22.5 0.0 collective-permute-done.7.refs_1_
  22.5 0.2 shard_map.101
  22.8 0.1 collective-permute-start.10
  22.9 1.7 %collective-permute-start.11 = (bf16[256,128]{1,0:T(8,128)(2,1)S(1)}, bf16[256,128]{1,0:T(8,128)(2,1)S(1)}, u32[]{:S(2)}, u32[]{:S(2)}) collective-permute-start(bf16[256,128]{1,0:T(8,128)(2,1)S(1)} %get-tuple-element.27), channel_id=1, source_target_pairs={{0,8},{4,12},{8,0},{12,4},{1,9},{5,13},{9,1},{13,5},{2,10},{6,14},... | collective-permute-start | bytes 196616 | tf_op jit(solution)/shard_map/ppermute | solution.py:43
  24.6 1.4 %collective-permute-start.12 = (bf16[256,128]{1,0:T(8,128)(2,1)S(1)}, bf16[256,128]{1,0:T(8,128)(2,1)S(1)}, u32[]{:S(2)}, u32[]{:S(2)}) collective-permute-start(bf16[256,128]{1,0:T(8,128)(2,1)S(1)} %get-tuple-element.28), channel_id=1, source_target_pairs={{0,12},{4,0},{8,4},{12,8},{1,13},{5,1},{9,5},{13,9},{2,14},{6,2},{... | collective-permute-start | bytes 196616 | tf_op jit(solution)/shard_map/ppermute | solution.py:43
  25.9 0.7 %shard_map.99 = bf16[128,256]{1,0:T(8,128)(2,1)} custom-call(f32[128,256]{1,0:T(8,128)S(1)} %get-tuple-element.21.pre), custom_call_target="tpu_custom_call" | custom-call | tf_op jit(solution)/shard_map/pallas_call | solution.py:322
  26.6 0.0 collective-permute-done.10.refs_0_
  26.6 0.7 %collective-permute-done.11.refs_1_ = bf16[256,128]{1,0:T(8,128)(2,1)S(1)} collective-permute-done((bf16[256,128]{1,0:T(8,128)(2,1)S(1)}, bf16[256,128]{1,0:T(8,128)(2,1)S(1)}, u32[]{:S(2)}, u32[]{:S(2)}) %collective-permute-start.11) | collective-permute-done | bytes 65568 | tf_op jit(solution)/shard_map/ppermute | solution.py:43
  27.3 0.5 %collective-permute-done.12.refs_2_ = bf16[256,128]{1,0:T(8,128)(2,1)S(1)} collective-permute-done((bf16[256,128]{1,0:T(8,128)(2,1)S(1)}, bf16[256,128]{1,0:T(8,128)(2,1)S(1)}, u32[]{:S(2)}, u32[]{:S(2)}) %collective-permute-start.12) | collective-permute-done | bytes 65568 | tf_op jit(solution)/shard_map/ppermute | solution.py:43
  27.8 0.7 %shard_map.102 = (bf16[128,128]{1,0:T(8,128)(2,1)}, f32[128,256]{1,0:T(8,128)}) custom-call(f32[128,128]{1,0:T(8,128)S(1)} %get-tuple-element.24.own, bf16[128,128]{1,0:T(8,128)(2,1)S(1)} %get-tuple-element.25.kept, bf16[256,128]{1,0:T(8,128)(2,1)S(1)} %collective-permute-done.10.refs_0_, bf16[256,128]{1,0:T(8,128)(2,1)S(1)} %collective-permute-done.11.refs_1_, ...), custom_call_target="tpu_custom_call" | custom-call | tf_op jit(solution)/shard_map/pallas_call | solution.py:342
  (1 shorter events, 0.0 us)
Async XLA Ops:
  0.6 6.7 %copy-start = (bf16[1,1,8,128,128]{4,3,2,1,0:T(8,128)(2,1)S(1)}, bf16[1,1,8,128,128]{4,3,2,1,0:T(8,128)(2,1)}, u32[]{:S(2)}) copy-start(bf16[1,1,8,128,128]{4,3,2,1,0:T(8,128)(2,1)} %vals.1) | copy-start | bytes 786436
  0.6 7.4 %collective-permute-start.1 = (bf16[128,128]{1,0:T(8,128)(2,1)}, bf16[128,128]{1,0:T(8,128)(2,1)S(1)}, u32[]{:S(2)}, u32[]{:S(2)}) collective-permute-start(bf16[128,128]{1,0:T(8,128)(2,1)} %refs_0_.1), channel_id=1, source_target_pairs={{0,12},{4,8},{8,4},{12,0},{1,13},{5,9},{9,5},{13,1},{2,14},{6,10},... | collective-permute-start | bytes 98312 | tf_op jit(solution)/shard_map/ppermute | solution.py:58
  3.1 5.0 %collective-permute-start = (bf16[128,128]{1,0:T(8,128)(2,1)}, bf16[128,128]{1,0:T(8,128)(2,1)S(1)}, u32[]{:S(2)}, u32[]{:S(2)}) collective-permute-start(bf16[128,128]{1,0:T(8,128)(2,1)} %refs_0_.1), channel_id=1, source_target_pairs={{0,8},{4,12},{8,0},{12,4},{1,9},{5,13},{9,1},{13,5},{2,10},{6,14},... | collective-permute-start | bytes 98312 | tf_op jit(solution)/shard_map/ppermute | solution.py:58
  3.7 4.3 %collective-permute-start.2 = (bf16[128,128]{1,0:T(8,128)(2,1)}, bf16[128,128]{1,0:T(8,128)(2,1)S(1)}, u32[]{:S(2)}, u32[]{:S(2)}) collective-permute-start(bf16[128,128]{1,0:T(8,128)(2,1)} %refs_0_.1), channel_id=1, source_target_pairs={{0,4},{4,0},{8,12},{12,8},{1,5},{5,1},{9,13},{13,9},{2,6},{6,2},{1... | collective-permute-start | bytes 98312 | tf_op jit(solution)/shard_map/ppermute | solution.py:58
  3.8 9.9 %collective-permute-start.6 = (bf16[128,256]{1,0:T(8,128)(2,1)}, bf16[128,256]{1,0:T(8,128)(2,1)S(1)}, u32[]{:S(2)}, u32[]{:S(2)}) collective-permute-start(bf16[128,256]{1,0:T(8,128)(2,1)} %refs_6_.1), channel_id=1, source_target_pairs={{0,2},{1,3},{2,0},{3,1},{4,6},{5,7},{6,4},{7,5},{8,10},{9,11},{10,... | collective-permute-start | bytes 196616 | tf_op jit(solution)/shard_map/ppermute | solution.py:58
  6.6 0.7 %copy-start.4 = (s32[1,1,8]{2,1,0:T(1,128)S(1)}, s32[1,1,8]{2,1,0:T(1,128)}, u32[]{:S(2)}) copy-start(s32[1,1,8]{2,1,0:T(1,128)} %rows_in.1) | copy-start | bytes 100
  6.7 0.7 %copy-start.5 = (s32[1,1,8]{2,1,0:T(1,128)S(1)}, s32[1,1,8]{2,1,0:T(1,128)}, u32[]{:S(2)}) copy-start(s32[1,1,8]{2,1,0:T(1,128)} %cols_in.1) | copy-start | bytes 100
  7.4 0.8 %copy-start.3 = (bf16[128,128]{1,0:T(8,128)(2,1)S(1)}, bf16[128,128]{1,0:T(8,128)(2,1)}, u32[]{:S(2)}) copy-start(bf16[128,128]{1,0:T(8,128)(2,1)} %refs_0_.1) | copy-start | bytes 98308
  8.4 5.6 %collective-permute-start.3 = (bf16[256,128]{1,0:T(8,128)(2,1)S(1)}, bf16[256,128]{1,0:T(8,128)(2,1)S(1)}, u32[]{:S(2)}, u32[]{:S(2)}) collective-permute-start(bf16[256,128]{1,0:T(8,128)(2,1)S(1)} %get-tuple-element.18), channel_id=1, source_target_pairs={{0,1},{1,3},{2,0},{3,2},{4,5},{5,7},{6,4},{7,6},{8,9},{9,11},{10,8... | collective-permute-start | bytes 196616 | tf_op jit(solution)/shard_map/ppermute | solution.py:43
  10.1 6.4 %collective-permute-start.4 = (bf16[256,128]{1,0:T(8,128)(2,1)S(1)}, bf16[256,128]{1,0:T(8,128)(2,1)S(1)}, u32[]{:S(2)}, u32[]{:S(2)}) collective-permute-start(bf16[256,128]{1,0:T(8,128)(2,1)S(1)} %get-tuple-element.19), channel_id=1, source_target_pairs={{0,3},{1,2},{2,1},{3,0},{4,7},{5,6},{6,5},{7,4},{8,11},{9,10},{10,... | collective-permute-start | bytes 196616 | tf_op jit(solution)/shard_map/ppermute | solution.py:43
  11.7 5.0 %copy-start.1 = (bf16[128,256]{1,0:T(8,128)(2,1)S(1)}, bf16[128,256]{1,0:T(8,128)(2,1)}, u32[]{:S(2)}) copy-start(bf16[128,256]{1,0:T(8,128)(2,1)} %refs_5_.1) | copy-start | bytes 196612
  11.7 5.0 %copy-start.2 = (bf16[128,256]{1,0:T(8,128)(2,1)S(1)}, bf16[128,256]{1,0:T(8,128)(2,1)}, u32[]{:S(2)}) copy-start(bf16[128,256]{1,0:T(8,128)(2,1)} %refs_6_.1) | copy-start | bytes 196612
  11.7 5.0 %collective-permute-start.5 = (bf16[256,128]{1,0:T(8,128)(2,1)S(1)}, bf16[256,128]{1,0:T(8,128)(2,1)S(1)}, u32[]{:S(2)}, u32[]{:S(2)}) collective-permute-start(bf16[256,128]{1,0:T(8,128)(2,1)S(1)} %get-tuple-element.20), channel_id=1, source_target_pairs={{0,2},{1,0},{2,3},{3,1},{4,6},{5,4},{6,7},{7,5},{8,10},{9,8},{10,1... | collective-permute-start | bytes 196616 | tf_op jit(solution)/shard_map/ppermute | solution.py:43
  17.2 5.4 %collective-permute-start.7 = (bf16[384,128]{1,0:T(8,128)(2,1)S(1)}, bf16[384,128]{1,0:T(8,128)(2,1)S(1)}, u32[]{:S(2)}, u32[]{:S(2)}) collective-permute-start(bf16[384,128]{1,0:T(8,128)(2,1)S(1)} %get-tuple-element.22.message.refs_0_), channel_id=1, source_target_pairs={{0,1},{1,0},{2,3},{3,2},{4,5},{5,4},{6,7},{7,6},{8,9},{9,8},{10,11... | collective-permute-start | bytes 294920 | tf_op jit(solution)/shard_map/ppermute | solution.py:58
  19.0 3.5 %collective-permute-start.9 = (bf16[128,128]{1,0:T(8,128)(2,1)S(1)}, bf16[128,128]{1,0:T(8,128)(2,1)S(1)}, u32[]{:S(2)}, u32[]{:S(2)}) collective-permute-start(bf16[128,128]{1,0:T(8,128)(2,1)S(1)} %get-tuple-element.23), channel_id=1, source_target_pairs={{0,5},{1,4},{2,7},{3,6},{4,1},{5,0},{6,3},{7,2},{8,13},{9,12},{10,... | collective-permute-start | bytes 98312 | tf_op jit(solution)/shard_map/ppermute | solution.py:317
  19.0 3.5 %collective-permute-start.8 = (bf16[128,128]{1,0:T(8,128)(2,1)S(1)}, bf16[128,128]{1,0:T(8,128)(2,1)S(1)}, u32[]{:S(2)}, u32[]{:S(2)}) collective-permute-start(bf16[128,128]{1,0:T(8,128)(2,1)S(1)} %get-tuple-element.23), channel_id=1, source_target_pairs={{0,4},{4,0},{8,12},{12,8},{1,5},{5,1},{9,13},{13,9},{2,6},{6,2},{1... | collective-permute-start | bytes 98312 | tf_op jit(solution)/shard_map/ppermute | solution.py:58
  22.8 3.8 %collective-permute-start.10 = (bf16[256,128]{1,0:T(8,128)(2,1)S(1)}, bf16[256,128]{1,0:T(8,128)(2,1)S(1)}, u32[]{:S(2)}, u32[]{:S(2)}) collective-permute-start(bf16[256,128]{1,0:T(8,128)(2,1)S(1)} %get-tuple-element.26), channel_id=1, source_target_pairs={{0,4},{4,8},{8,12},{12,0},{1,5},{5,9},{9,13},{13,1},{2,6},{6,10},{... | collective-permute-start | bytes 196616 | tf_op jit(solution)/shard_map/ppermute | solution.py:43
  22.9 4.5 %collective-permute-start.11 = (bf16[256,128]{1,0:T(8,128)(2,1)S(1)}, bf16[256,128]{1,0:T(8,128)(2,1)S(1)}, u32[]{:S(2)}, u32[]{:S(2)}) collective-permute-start(bf16[256,128]{1,0:T(8,128)(2,1)S(1)} %get-tuple-element.27), channel_id=1, source_target_pairs={{0,8},{4,12},{8,0},{12,4},{1,9},{5,13},{9,1},{13,5},{2,10},{6,14},... | collective-permute-start | bytes 196616 | tf_op jit(solution)/shard_map/ppermute | solution.py:43
  24.6 3.3 %collective-permute-start.12 = (bf16[256,128]{1,0:T(8,128)(2,1)S(1)}, bf16[256,128]{1,0:T(8,128)(2,1)S(1)}, u32[]{:S(2)}, u32[]{:S(2)}) collective-permute-start(bf16[256,128]{1,0:T(8,128)(2,1)S(1)} %get-tuple-element.28), channel_id=1, source_target_pairs={{0,12},{4,0},{8,4},{12,8},{1,13},{5,1},{9,5},{13,9},{2,14},{6,2},{... | collective-permute-start | bytes 196616 | tf_op jit(solution)/shard_map/ppermute | solution.py:43

commit v25 on v24

--- a/solution.py
+++ b/solution.py
@@ -183,7 +183,7 @@
     third[...] = jnp.where(middle, other, same)
 
 
-def paired_layer_kernel(own, first, second, third, weight, cotangent, beyond, *refs):
+def paired_layer_kernel(own, third, second, first, weight, cotangent, beyond, *refs):
     message, other, pre_out = refs
     nodes = cotangent.shape[0]
     middle = in_middle()
@@ -282,6 +282,7 @@
             **forward,
         )(near, features, *gathered)
         layer_call, cotangents = paired_layer_kernel, [cotangent, swap(cotangent, "col", 2)]
+        parts = exchange(sends, "col", True)[::-1]
     else:
         layers = 1
         own, *sends = call(
@@ -291,7 +292,7 @@
             **forward,
         )(near, features, *gathered)
         layer_call, cotangents = layer_kernel, [cotangent]
-    parts = exchange(sends, "col", True)
+        parts = exchange(sends, "col", True)
     (far,) = call(
         functools.partial(turn_kernel, side),
         [((across, down), NARROW)],

time: 28.9 us -> 29.5 us (1.021)
  the two profiles are of different devices: /device:TPU:0 before, /device:TPU:1 now
where the time goes in v25:
time: 29.5 us; the launch traced here: 29.3 us
  starting transfers between devices  13.4 us (45%)
  waiting for transfers between devices  10.7 us (36%)
  Pallas kernels  3.61 us (12%)
  between operations  1.45 us (5%)
    ppermute x6, waiting for transfers between devices, exchange(): lax.ppermute(send, axis, [(s, target(s, d)) for s in range(n)])  8.22 us
    ppermute x6, starting transfers between devices, swap(): return lax.ppermute(value, axis, [(s, s ^ distance) for s in range(n)])  5.52 us
    ppermute x6, starting transfers between devices, exchange(): lax.ppermute(send, axis, [(s, target(s, d)) for s in range(n)])  5.35 us
    ppermute x1, starting transfers between devices, per_device(): lax.ppermute(other, ('row', 'col'), corner)  2.53 us
    ppermute x1, waiting for transfers between devices, per_device(): lax.ppermute(other, ('row', 'col'), corner)  2.45 us
    pallas_call x1, Pallas kernels, per_device(): call(functools.partial(last_kernel, scale), [((nodes, width), NARROW), ((...  0.69 us
    pallas_call x1, Pallas kernels, per_device(): act, = call(act_kernel, [((nodes, hidden), NARROW)], [VMEM])(pre)  0.65 us
    pallas_call x1, Pallas kernels, per_device(): call(functools.partial(dense_kernel, nodes // side, paired), [((down, acr...  0.64 us
  transfers between devices with their start and end apart: 13, of which 6 were waited for; matrix products, arithmetic and copies ran while one was open for 0% of the time, Pallas kernels for 7%

profile of v25, /device:TPU:1, one launch (start us, length us, event | category | flops | bytes accessed | tf_op | source)
XLA Modules:
  0.0 29.3 jit_solution(8375665279380919673)
XLA Ops:
  0.6 0.0 copy-start
  0.6 2.7 %collective-permute-start.1 = (bf16[128,128]{1,0:T(8,128)(2,1)}, bf16[128,128]{1,0:T(8,128)(2,1)S(1)}, u32[]{:S(2)}, u32[]{:S(2)}) collective-permute-start(bf16[128,128]{1,0:T(8,128)(2,1)} %refs_0_.1), channel_id=1, source_target_pairs={{0,12},{4,8},{8,4},{12,0},{1,13},{5,9},{9,5},{13,1},{2,14},{6,10},... | collective-permute-start | bytes 98312 | tf_op jit(solution)/shard_map/ppermute | solution.py:58
  3.3 0.0 collective-permute-start
  3.3 0.5 %collective-permute-start.2 = (bf16[128,128]{1,0:T(8,128)(2,1)}, bf16[128,128]{1,0:T(8,128)(2,1)S(1)}, u32[]{:S(2)}, u32[]{:S(2)}) collective-permute-start(bf16[128,128]{1,0:T(8,128)(2,1)} %refs_0_.1), channel_id=1, source_target_pairs={{0,4},{4,0},{8,12},{12,8},{1,5},{5,1},{9,13},{13,9},{2,6},{6,2},{1... | collective-permute-start | bytes 98312 | tf_op jit(solution)/shard_map/ppermute | solution.py:58
  3.8 2.3 %collective-permute-start.6 = (bf16[128,256]{1,0:T(8,128)(2,1)}, bf16[128,256]{1,0:T(8,128)(2,1)S(1)}, u32[]{:S(2)}, u32[]{:S(2)}) collective-permute-start(bf16[128,256]{1,0:T(8,128)(2,1)} %refs_6_.1), channel_id=1, source_target_pairs={{0,2},{1,3},{2,0},{3,1},{4,6},{5,7},{6,4},{7,5},{8,10},{9,11},{10,... | collective-permute-start | bytes 196616 | tf_op jit(solution)/shard_map/ppermute | solution.py:58
  6.1 0.0 copy-start.4
  6.1 0.0 copy-start.5
  6.8 0.0 copy-done
  6.8 0.0 copy-done.4
  6.8 0.0 copy-done.5
  6.8 0.0 copy-start.3
  6.9 0.6 %shard_map.95.near.matrix = bf16[512,512]{1,0:T(8,128)(2,1)S(1)} custom-call(bf16[512,512]{1,0:T(8,128)(2,1)S(1)} %shard_map.94.blank, bf16[1,1,8,128,128]{4,3,2,1,0:T(8,128)(2,1)S(1)} %copy-done, s32[1,1,8]{2,1,0:T(1,128)S(1)} %copy-done.4, s32[1,1,8]{2,1,0:T(1,128)S(1)} %copy-done.5, s32[1,1]{1,0:T(1,128)S(6)} %copy.12.count_in), custom_call_target="tpu_custom_call", output_to_operand_aliasing={{}: (0, {})} | custom-call | bytes 1048576 | tf_op jit(solution)/shard_map/pallas_call | solution.py:261
  7.5 0.0 collective-permute-done.1.refs_2_
  7.5 0.0 collective-permute-done.refs_1_
  7.5 0.0 collective-permute-done.2.refs_3_
  7.5 0.1 copy-done.3
  7.6 0.3 shard_map.97
  7.9 1.4 %collective-permute-start.3 = (bf16[256,128]{1,0:T(8,128)(2,1)S(1)}, bf16[256,128]{1,0:T(8,128)(2,1)S(1)}, u32[]{:S(2)}, u32[]{:S(2)}) collective-permute-start(bf16[256,128]{1,0:T(8,128)(2,1)S(1)} %get-tuple-element.18), channel_id=1, source_target_pairs={{0,2},{1,0},{2,3},{3,1},{4,6},{5,4},{6,7},{7,5},{8,10},{9,8},{10,1... | collective-permute-start | bytes 196616 | tf_op jit(solution)/shard_map/ppermute | solution.py:43
  9.3 2.0 %collective-permute-start.4 = (bf16[256,128]{1,0:T(8,128)(2,1)S(1)}, bf16[256,128]{1,0:T(8,128)(2,1)S(1)}, u32[]{:S(2)}, u32[]{:S(2)}) collective-permute-start(bf16[256,128]{1,0:T(8,128)(2,1)S(1)} %get-tuple-element.19), channel_id=1, source_target_pairs={{0,3},{1,2},{2,1},{3,0},{4,7},{5,6},{6,5},{7,4},{8,11},{9,10},{10,... | collective-permute-start | bytes 196616 | tf_op jit(solution)/shard_map/ppermute | solution.py:43
  11.3 0.0 copy-start.1
  11.3 0.0 copy-start.2
  11.3 0.0 collective-permute-start.5
  11.3 0.3 %shard_map.96.refs_0_.matrix = bf16[512,512]{1,0:T(8,128)(2,1)S(1)} custom-call(bf16[512,512]{1,0:T(8,128)(2,1)S(1)} %shard_map.95.near.matrix), custom_call_target="tpu_custom_call" | custom-call | bytes 1572864 | tf_op jit(solution)/shard_map/pallas_call | solution.py:296
  11.7 0.0 collective-permute-done.6.refs_7_
  11.7 0.0 collective-permute-done.3.refs_2_
  11.7 3.1 %collective-permute-done.4.refs_3_ = bf16[256,128]{1,0:T(8,128)(2,1)S(1)} collective-permute-done((bf16[256,128]{1,0:T(8,128)(2,1)S(1)}, bf16[256,128]{1,0:T(8,128)(2,1)S(1)}, u32[]{:S(2)}, u32[]{:S(2)}) %collective-permute-start.4) | collective-permute-done | bytes 65568 | tf_op jit(solution)/shard_map/ppermute | solution.py:43
  14.8 2.2 %collective-permute-done.5.refs_4_ = bf16[256,128]{1,0:T(8,128)(2,1)S(1)} collective-permute-done((bf16[256,128]{1,0:T(8,128)(2,1)S(1)}, bf16[256,128]{1,0:T(8,128)(2,1)S(1)}, u32[]{:S(2)}, u32[]{:S(2)}) %collective-permute-start.5) | collective-permute-done | bytes 65568 | tf_op jit(solution)/shard_map/ppermute | solution.py:43
  17.0 0.0 copy-done.1
  17.0 0.0 copy-done.2
  17.0 0.5 %shard_map.98 = (bf16[384,128]{1,0:T(8,128)(2,1)S(1)}, bf16[128,128]{1,0:T(8,128)(2,1)S(1)}, f32[128,256]{1,0:T(8,128)S(1)}) custom-call(bf16[512,512]{1,0:T(8,128)(2,1)S(1)} %shard_map.96.refs_0_.matrix, bf16[256,128]{1,0:T(8,128)(2,1)S(1)} %get-tuple-element.17.refs_1_, bf16[256,128]{1,0:T(8,128)(2,1)S(1)} %collective-permute-done.3.refs_2_, ...), custom_call_target="tpu_custom_call" | custom-call | flops 117440512 | tf_op jit(solution)/shard_map/pallas_call | solution.py:306
  17.5 0.1 collective-permute-start.7
  17.6 2.5 %collective-permute-start.9 = (bf16[128,128]{1,0:T(8,128)(2,1)S(1)}, bf16[128,128]{1,0:T(8,128)(2,1)S(1)}, u32[]{:S(2)}, u32[]{:S(2)}) collective-permute-start(bf16[128,128]{1,0:T(8,128)(2,1)S(1)} %get-tuple-element.23), channel_id=1, source_target_pairs={{0,5},{1,4},{2,7},{3,6},{4,1},{5,0},{6,3},{7,2},{8,13},{9,12},{10,... | collective-permute-start | bytes 98312 | tf_op jit(solution)/shard_map/ppermute | solution.py:318
  20.1 0.0 collective-permute-start.8
  20.1 0.2 shard_map.100.begun
  20.3 2.5 %collective-permute-done.9.refs_3_ = bf16[128,128]{1,0:T(8,128)(2,1)S(1)} collective-permute-done((bf16[128,128]{1,0:T(8,128)(2,1)S(1)}, bf16[128,128]{1,0:T(8,128)(2,1)S(1)}, u32[]{:S(2)}, u32[]{:S(2)}) %collective-permute-start.9) | collective-permute-done | bytes 32800 | tf_op jit(solution)/shard_map/ppermute | solution.py:318
  22.8 0.0 collective-permute-done.8.refs_2_
  22.8 0.0 collective-permute-done.7.refs_1_
  22.8 0.2 shard_map.101
  23.0 1.3 %collective-permute-start.10 = (bf16[256,128]{1,0:T(8,128)(2,1)S(1)}, bf16[256,128]{1,0:T(8,128)(2,1)S(1)}, u32[]{:S(2)}, u32[]{:S(2)}) collective-permute-start(bf16[256,128]{1,0:T(8,128)(2,1)S(1)} %get-tuple-element.26), channel_id=1, source_target_pairs={{0,4},{4,8},{8,12},{12,0},{1,5},{5,9},{9,13},{13,1},{2,6},{6,10},{... | collective-permute-start | bytes 196616 | tf_op jit(solution)/shard_map/ppermute | solution.py:43
  24.4 0.4 %collective-permute-start.11 = (bf16[256,128]{1,0:T(8,128)(2,1)S(1)}, bf16[256,128]{1,0:T(8,128)(2,1)S(1)}, u32[]{:S(2)}, u32[]{:S(2)}) collective-permute-start(bf16[256,128]{1,0:T(8,128)(2,1)S(1)} %get-tuple-element.27), channel_id=1, source_target_pairs={{0,8},{4,12},{8,0},{12,4},{1,9},{5,13},{9,1},{13,5},{2,10},{6,14},... | collective-permute-start | bytes 196616 | tf_op jit(solution)/shard_map/ppermute | solution.py:43
  24.8 0.2 collective-permute-start.12
  24.9 0.7 %shard_map.99 = bf16[128,256]{1,0:T(8,128)(2,1)} custom-call(f32[128,256]{1,0:T(8,128)S(1)} %get-tuple-element.21.pre), custom_call_target="tpu_custom_call" | custom-call | tf_op jit(solution)/shard_map/pallas_call | solution.py:323
  25.6 0.1 collective-permute-done.10.refs_0_
  25.7 2.3 %collective-permute-done.11.refs_1_ = bf16[256,128]{1,0:T(8,128)(2,1)S(1)} collective-permute-done((bf16[256,128]{1,0:T(8,128)(2,1)S(1)}, bf16[256,128]{1,0:T(8,128)(2,1)S(1)}, u32[]{:S(2)}, u32[]{:S(2)}) %collective-permute-start.11) | collective-permute-done | bytes 65568 | tf_op jit(solution)/shard_map/ppermute | solution.py:43
  28.0 0.6 %collective-permute-done.12.refs_2_ = bf16[256,128]{1,0:T(8,128)(2,1)S(1)} collective-permute-done((bf16[256,128]{1,0:T(8,128)(2,1)S(1)}, bf16[256,128]{1,0:T(8,128)(2,1)S(1)}, u32[]{:S(2)}, u32[]{:S(2)}) %collective-permute-start.12) | collective-permute-done | bytes 65568 | tf_op jit(solution)/shard_map/ppermute | solution.py:43
  28.6 0.7 %shard_map.102 = (bf16[128,128]{1,0:T(8,128)(2,1)}, f32[128,256]{1,0:T(8,128)}) custom-call(f32[128,128]{1,0:T(8,128)S(1)} %get-tuple-element.24.own, bf16[128,128]{1,0:T(8,128)(2,1)S(1)} %get-tuple-element.25.kept, bf16[256,128]{1,0:T(8,128)(2,1)S(1)} %collective-permute-done.10.refs_0_, bf16[256,128]{1,0:T(8,128)(2,1)S(1)} %collective-permute-done.11.refs_1_, ...), custom_call_target="tpu_custom_call" | custom-call | tf_op jit(solution)/shard_map/pallas_call | solution.py:343
  (1 shorter events, 0.0 us)
Async XLA Ops:
  0.6 6.2 %copy-start = (bf16[1,1,8,128,128]{4,3,2,1,0:T(8,128)(2,1)S(1)}, bf16[1,1,8,128,128]{4,3,2,1,0:T(8,128)(2,1)}, u32[]{:S(2)}) copy-start(bf16[1,1,8,128,128]{4,3,2,1,0:T(8,128)(2,1)} %vals.1) | copy-start | bytes 786436
  0.6 6.9 %collective-permute-start.1 = (bf16[128,128]{1,0:T(8,128)(2,1)}, bf16[128,128]{1,0:T(8,128)(2,1)S(1)}, u32[]{:S(2)}, u32[]{:S(2)}) collective-permute-start(bf16[128,128]{1,0:T(8,128)(2,1)} %refs_0_.1), channel_id=1, source_target_pairs={{0,12},{4,8},{8,4},{12,0},{1,13},{5,9},{9,5},{13,1},{2,14},{6,10},... | collective-permute-start | bytes 98312 | tf_op jit(solution)/shard_map/ppermute | solution.py:58
  3.3 4.2 %collective-permute-start = (bf16[128,128]{1,0:T(8,128)(2,1)}, bf16[128,128]{1,0:T(8,128)(2,1)S(1)}, u32[]{:S(2)}, u32[]{:S(2)}) collective-permute-start(bf16[128,128]{1,0:T(8,128)(2,1)} %refs_0_.1), channel_id=1, source_target_pairs={{0,8},{4,12},{8,0},{12,4},{1,9},{5,13},{9,1},{13,5},{2,10},{6,14},... | collective-permute-start | bytes 98312 | tf_op jit(solution)/shard_map/ppermute | solution.py:58
  3.3 4.2 %collective-permute-start.2 = (bf16[128,128]{1,0:T(8,128)(2,1)}, bf16[128,128]{1,0:T(8,128)(2,1)S(1)}, u32[]{:S(2)}, u32[]{:S(2)}) collective-permute-start(bf16[128,128]{1,0:T(8,128)(2,1)} %refs_0_.1), channel_id=1, source_target_pairs={{0,4},{4,0},{8,12},{12,8},{1,5},{5,1},{9,13},{13,9},{2,6},{6,2},{1... | collective-permute-start | bytes 98312 | tf_op jit(solution)/shard_map/ppermute | solution.py:58
  3.8 7.9 %collective-permute-start.6 = (bf16[128,256]{1,0:T(8,128)(2,1)}, bf16[128,256]{1,0:T(8,128)(2,1)S(1)}, u32[]{:S(2)}, u32[]{:S(2)}) collective-permute-start(bf16[128,256]{1,0:T(8,128)(2,1)} %refs_6_.1), channel_id=1, source_target_pairs={{0,2},{1,3},{2,0},{3,1},{4,6},{5,7},{6,4},{7,5},{8,10},{9,11},{10,... | collective-permute-start | bytes 196616 | tf_op jit(solution)/shard_map/ppermute | solution.py:58
  6.1 0.7 %copy-start.4 = (s32[1,1,8]{2,1,0:T(1,128)S(1)}, s32[1,1,8]{2,1,0:T(1,128)}, u32[]{:S(2)}) copy-start(s32[1,1,8]{2,1,0:T(1,128)} %rows_in.1) | copy-start | bytes 100
  6.1 0.7 %copy-start.5 = (s32[1,1,8]{2,1,0:T(1,128)S(1)}, s32[1,1,8]{2,1,0:T(1,128)}, u32[]{:S(2)}) copy-start(s32[1,1,8]{2,1,0:T(1,128)} %cols_in.1) | copy-start | bytes 100
  6.8 0.8 %copy-start.3 = (bf16[128,128]{1,0:T(8,128)(2,1)S(1)}, bf16[128,128]{1,0:T(8,128)(2,1)}, u32[]{:S(2)}) copy-start(bf16[128,128]{1,0:T(8,128)(2,1)} %refs_0_.1) | copy-start | bytes 98308
  7.9 3.8 %collective-permute-start.3 = (bf16[256,128]{1,0:T(8,128)(2,1)S(1)}, bf16[256,128]{1,0:T(8,128)(2,1)S(1)}, u32[]{:S(2)}, u32[]{:S(2)}) collective-permute-start(bf16[256,128]{1,0:T(8,128)(2,1)S(1)} %get-tuple-element.18), channel_id=1, source_target_pairs={{0,2},{1,0},{2,3},{3,1},{4,6},{5,4},{6,7},{7,5},{8,10},{9,8},{10,1... | collective-permute-start | bytes 196616 | tf_op jit(solution)/shard_map/ppermute | solution.py:43
  9.3 5.5 %collective-permute-start.4 = (bf16[256,128]{1,0:T(8,128)(2,1)S(1)}, bf16[256,128]{1,0:T(8,128)(2,1)S(1)}, u32[]{:S(2)}, u32[]{:S(2)}) collective-permute-start(bf16[256,128]{1,0:T(8,128)(2,1)S(1)} %get-tuple-element.19), channel_id=1, source_target_pairs={{0,3},{1,2},{2,1},{3,0},{4,7},{5,6},{6,5},{7,4},{8,11},{9,10},{10,... | collective-permute-start | bytes 196616 | tf_op jit(solution)/shard_map/ppermute | solution.py:43
  11.3 5.6 %copy-start.1 = (bf16[128,256]{1,0:T(8,128)(2,1)S(1)}, bf16[128,256]{1,0:T(8,128)(2,1)}, u32[]{:S(2)}) copy-start(bf16[128,256]{1,0:T(8,128)(2,1)} %refs_5_.1) | copy-start | bytes 196612
  11.3 5.6 %copy-start.2 = (bf16[128,256]{1,0:T(8,128)(2,1)S(1)}, bf16[128,256]{1,0:T(8,128)(2,1)}, u32[]{:S(2)}) copy-start(bf16[128,256]{1,0:T(8,128)(2,1)} %refs_6_.1) | copy-start | bytes 196612
  11.3 5.6 %collective-permute-start.5 = (bf16[256,128]{1,0:T(8,128)(2,1)S(1)}, bf16[256,128]{1,0:T(8,128)(2,1)S(1)}, u32[]{:S(2)}, u32[]{:S(2)}) collective-permute-start(bf16[256,128]{1,0:T(8,128)(2,1)S(1)} %get-tuple-element.20), channel_id=1, source_target_pairs={{0,1},{1,3},{2,0},{3,2},{4,5},{5,7},{6,4},{7,6},{8,9},{9,11},{10,8... | collective-permute-start | bytes 196616 | tf_op jit(solution)/shard_map/ppermute | solution.py:43
  17.5 5.3 %collective-permute-start.7 = (bf16[384,128]{1,0:T(8,128)(2,1)S(1)}, bf16[384,128]{1,0:T(8,128)(2,1)S(1)}, u32[]{:S(2)}, u32[]{:S(2)}) collective-permute-start(bf16[384,128]{1,0:T(8,128)(2,1)S(1)} %get-tuple-element.22.message.refs_0_), channel_id=1, source_target_pairs={{0,1},{1,0},{2,3},{3,2},{4,5},{5,4},{6,7},{7,6},{8,9},{9,8},{10,11... | collective-permute-start | bytes 294920 | tf_op jit(solution)/shard_map/ppermute | solution.py:58
  17.6 5.2 %collective-permute-start.9 = (bf16[128,128]{1,0:T(8,128)(2,1)S(1)}, bf16[128,128]{1,0:T(8,128)(2,1)S(1)}, u32[]{:S(2)}, u32[]{:S(2)}) collective-permute-start(bf16[128,128]{1,0:T(8,128)(2,1)S(1)} %get-tuple-element.23), channel_id=1, source_target_pairs={{0,5},{1,4},{2,7},{3,6},{4,1},{5,0},{6,3},{7,2},{8,13},{9,12},{10,... | collective-permute-start | bytes 98312 | tf_op jit(solution)/shard_map/ppermute | solution.py:318
  20.1 2.7 %collective-permute-start.8 = (bf16[128,128]{1,0:T(8,128)(2,1)S(1)}, bf16[128,128]{1,0:T(8,128)(2,1)S(1)}, u32[]{:S(2)}, u32[]{:S(2)}) collective-permute-start(bf16[128,128]{1,0:T(8,128)(2,1)S(1)} %get-tuple-element.23), channel_id=1, source_target_pairs={{0,4},{4,0},{8,12},{12,8},{1,5},{5,1},{9,13},{13,9},{2,6},{6,2},{1... | collective-permute-start | bytes 98312 | tf_op jit(solution)/shard_map/ppermute | solution.py:58
  23.0 2.7 %collective-permute-start.10 = (bf16[256,128]{1,0:T(8,128)(2,1)S(1)}, bf16[256,128]{1,0:T(8,128)(2,1)S(1)}, u32[]{:S(2)}, u32[]{:S(2)}) collective-permute-start(bf16[256,128]{1,0:T(8,128)(2,1)S(1)} %get-tuple-element.26), channel_id=1, source_target_pairs={{0,4},{4,8},{8,12},{12,0},{1,5},{5,9},{9,13},{13,1},{2,6},{6,10},{... | collective-permute-start | bytes 196616 | tf_op jit(solution)/shard_map/ppermute | solution.py:43
  24.4 3.6 %collective-permute-start.11 = (bf16[256,128]{1,0:T(8,128)(2,1)S(1)}, bf16[256,128]{1,0:T(8,128)(2,1)S(1)}, u32[]{:S(2)}, u32[]{:S(2)}) collective-permute-start(bf16[256,128]{1,0:T(8,128)(2,1)S(1)} %get-tuple-element.27), channel_id=1, source_target_pairs={{0,8},{4,12},{8,0},{12,4},{1,9},{5,13},{9,1},{13,5},{2,10},{6,14},... | collective-permute-start | bytes 196616 | tf_op jit(solution)/shard_map/ppermute | solution.py:43
  24.8 3.8 %collective-permute-start.12 = (bf16[256,128]{1,0:T(8,128)(2,1)S(1)}, bf16[256,128]{1,0:T(8,128)(2,1)S(1)}, u32[]{:S(2)}, u32[]{:S(2)}) collective-permute-start(bf16[256,128]{1,0:T(8,128)(2,1)S(1)} %get-tuple-element.28), channel_id=1, source_target_pairs={{0,12},{4,0},{8,4},{12,8},{1,13},{5,1},{9,5},{13,9},{2,14},{6,2},{... | collective-permute-start | bytes 196616 | tf_op jit(solution)/shard_map/ppermute | solution.py:43

commit v26 on v24

--- a/solution.py
+++ b/solution.py
@@ -50,7 +50,7 @@
 
 
 def start_order(n):
-    return [*range(2, n), 1]
+    return [*range(n - 1, 0, -1)]
 
 
 def swap(value, axis, distance):
@@ -236,6 +236,7 @@
 
 def last_kernel(scale, own, kept, *refs):
     *messages, features_out, weight_out = refs
+    messages = messages[::-1]
     nodes, half = own.shape[0], kept.shape[1]
     features_out[...] = tree(
         [own[...]] + [wide(message[:nodes]) for message in messages]
@@ -314,7 +315,7 @@
             (r * n_col + c, (r ^ 1) * n_col + (c ^ 1)) for r in range(n_row) for c in range(n_col)
         ]
         messages = [sent, swap(sent, "col", 1)]
-        others = [swap(other, "row", 1), lax.ppermute(other, ("row", "col"), corner)]
+        others = [lax.ppermute(other, ("row", "col"), corner), swap(other, "row", 1)]
     else:
         (sent,) = call(message_kernel, [message], [VMEM] * 2)(sent, swap(other, "row", 1))
         messages = [sent] + exchange([sent] * (n_col - 1), "col", False)
@@ -343,7 +344,7 @@
         functools.partial(last_kernel, scale),
         [((nodes, width), NARROW), ((width, hidden), jnp.float32)],
         [VMEM] * (n_row + 1),
-    )(own, kept, *parts)
+    )(own, kept, *parts[::-1])
     return act, grad_features, grad_weight
 
 

time: 28.9 us -> 30.2 us (1.045)
  waiting for transfers between devices: 7.25 us -> 9.84 us
  starting transfers between devices: 16.1 us -> 15.1 us
    ppermute x6, waiting for transfers between devices: 4.27 us -> 7.22 us  [exchange(): lax.ppermute(send, axis, [(s, target(s, d)) for s in range(n)])]
    ppermute x6, starting transfers between devices: 7.97 us -> 6.6 us  [exchange(): lax.ppermute(send, axis, [(s, target(s, d)) for s in range(n)])]
    ppermute x1, starting transfers between devices: 0.01 us -> 0.68 us  [per_device(): lax.ppermute(other, ('row', 'col'), corner)]
    ppermute x1, waiting for transfers between devices: 2.96 us -> 2.3 us  [per_device(): lax.ppermute(other, ('row', 'col'), corner)]
    ppermute x6, starting transfers between devices: 8.17 us -> 7.77 us  [swap(): return lax.ppermute(value, axis, [(s, s ^ distance) for s in range(n)])]
  transfers between devices with their start and end apart: 13 -> 13, of which waited for: 6 -> 6; matrix products, arithmetic and copies ran while one was open for 0% -> 0% of each run, Pallas kernels for 8% -> 7%
where the time goes in v26:
time: 30.2 us; the launch traced here: 30 us
  starting transfers between devices  15.1 us (50%)
  waiting for transfers between devices  9.84 us (33%)
  Pallas kernels  3.63 us (12%)
  between operations  1.45 us (5%)
    ppermute x6, starting transfers between devices, swap(): return lax.ppermute(value, axis, [(s, s ^ distance) for s in range(n)])  7.77 us
    ppermute x6, waiting for transfers between devices, exchange(): lax.ppermute(send, axis, [(s, target(s, d)) for s in range(n)])  7.22 us
    ppermute x6, starting transfers between devices, exchange(): lax.ppermute(send, axis, [(s, target(s, d)) for s in range(n)])  6.6 us
    ppermute x1, waiting for transfers between devices, per_device(): lax.ppermute(other, ('row', 'col'), corner)  2.3 us
    pallas_call x1, Pallas kernels, per_device(): call(functools.partial(last_kernel, scale), [((nodes, width), NARROW), ((...  0.69 us
    ppermute x1, starting transfers between devices, per_device(): lax.ppermute(other, ('row', 'col'), corner)  0.68 us
    pallas_call x1, Pallas kernels, per_device(): call(functools.partial(dense_kernel, nodes // side, paired), [((down, acr...  0.66 us
    pallas_call x1, Pallas kernels, per_device(): act, = call(act_kernel, [((nodes, hidden), NARROW)], [VMEM])(pre)  0.66 us
  transfers between devices with their start and end apart: 13, of which 6 were waited for; matrix products, arithmetic and copies ran while one was open for 0% of the time, Pallas kernels for 7%

profile of v26, /device:TPU:0, one launch (start us, length us, event | category | flops | bytes accessed | tf_op | source)
XLA Modules:
  0.0 30.0 jit_solution(15867636437125422622)
XLA Ops:
  0.6 0.0 copy-start
  0.6 3.0 %collective-permute-start.1 = (bf16[128,128]{1,0:T(8,128)(2,1)}, bf16[128,128]{1,0:T(8,128)(2,1)S(1)}, u32[]{:S(2)}, u32[]{:S(2)}) collective-permute-start(bf16[128,128]{1,0:T(8,128)(2,1)} %refs_0_.1), channel_id=1, source_target_pairs={{0,8},{4,12},{8,0},{12,4},{1,9},{5,13},{9,1},{13,5},{2,10},{6,14},... | collective-permute-start | bytes 98312 | tf_op jit(solution)/shard_map/ppermute | solution.py:58
  3.6 0.0 collective-permute-start
  3.6 0.2 collective-permute-start.2
  3.8 3.0 %collective-permute-start.6 = (bf16[128,256]{1,0:T(8,128)(2,1)}, bf16[128,256]{1,0:T(8,128)(2,1)S(1)}, u32[]{:S(2)}, u32[]{:S(2)}) collective-permute-start(bf16[128,256]{1,0:T(8,128)(2,1)} %refs_6_.1), channel_id=1, source_target_pairs={{0,2},{1,3},{2,0},{3,1},{4,6},{5,7},{6,4},{7,5},{8,10},{9,11},{10,... | collective-permute-start | bytes 196616 | tf_op jit(solution)/shard_map/ppermute | solution.py:58
  6.9 0.0 copy-start.4
  6.9 0.0 copy-start.5
  7.6 0.0 copy-done
  7.6 0.0 copy-done.4
  7.6 0.0 copy-done.5
  7.6 0.0 copy-start.3
  7.7 0.7 %shard_map.95.near.matrix = bf16[512,512]{1,0:T(8,128)(2,1)S(1)} custom-call(bf16[512,512]{1,0:T(8,128)(2,1)S(1)} %shard_map.94.blank, bf16[1,1,8,128,128]{4,3,2,1,0:T(8,128)(2,1)S(1)} %copy-done, s32[1,1,8]{2,1,0:T(1,128)S(1)} %copy-done.4, s32[1,1,8]{2,1,0:T(1,128)S(1)} %copy-done.5, s32[1,1]{1,0:T(1,128)S(6)} %copy.12.count_in), custom_call_target="tpu_custom_call", output_to_operand_aliasing={{}: (0, {})} | custom-call | bytes 1048576 | tf_op jit(solution)/shard_map/pallas_call | solution.py:262
  8.3 0.0 collective-permute-done.1.refs_2_
  8.3 0.0 collective-permute-done.refs_1_
  8.3 0.0 collective-permute-done.2.refs_3_
  8.3 0.1 copy-done.3
  8.4 0.3 shard_map.97
  8.7 1.6 %collective-permute-start.3 = (bf16[256,128]{1,0:T(8,128)(2,1)S(1)}, bf16[256,128]{1,0:T(8,128)(2,1)S(1)}, u32[]{:S(2)}, u32[]{:S(2)}) collective-permute-start(bf16[256,128]{1,0:T(8,128)(2,1)S(1)} %get-tuple-element.18), channel_id=1, source_target_pairs={{0,1},{1,3},{2,0},{3,2},{4,5},{5,7},{6,4},{7,6},{8,9},{9,11},{10,8... | collective-permute-start | bytes 196616 | tf_op jit(solution)/shard_map/ppermute | solution.py:43
  10.3 1.4 %collective-permute-start.4 = (bf16[256,128]{1,0:T(8,128)(2,1)S(1)}, bf16[256,128]{1,0:T(8,128)(2,1)S(1)}, u32[]{:S(2)}, u32[]{:S(2)}) collective-permute-start(bf16[256,128]{1,0:T(8,128)(2,1)S(1)} %get-tuple-element.19), channel_id=1, source_target_pairs={{0,3},{1,2},{2,1},{3,0},{4,7},{5,6},{6,5},{7,4},{8,11},{9,10},{10,... | collective-permute-start | bytes 196616 | tf_op jit(solution)/shard_map/ppermute | solution.py:43
  11.7 0.0 copy-start.1
  11.7 0.0 copy-start.2
  11.7 1.6 %collective-permute-start.5 = (bf16[256,128]{1,0:T(8,128)(2,1)S(1)}, bf16[256,128]{1,0:T(8,128)(2,1)S(1)}, u32[]{:S(2)}, u32[]{:S(2)}) collective-permute-start(bf16[256,128]{1,0:T(8,128)(2,1)S(1)} %get-tuple-element.20), channel_id=1, source_target_pairs={{0,2},{1,0},{2,3},{3,1},{4,6},{5,4},{6,7},{7,5},{8,10},{9,8},{10,1... | collective-permute-start | bytes 196616 | tf_op jit(solution)/shard_map/ppermute | solution.py:43
  13.3 0.3 %shard_map.96.refs_0_.matrix = bf16[512,512]{1,0:T(8,128)(2,1)S(1)} custom-call(bf16[512,512]{1,0:T(8,128)(2,1)S(1)} %shard_map.95.near.matrix), custom_call_target="tpu_custom_call" | custom-call | bytes 1572864 | tf_op jit(solution)/shard_map/pallas_call | solution.py:296
  13.6 0.0 collective-permute-done.6.refs_7_
  13.6 3.6 %collective-permute-done.3.refs_2_ = bf16[256,128]{1,0:T(8,128)(2,1)S(1)} collective-permute-done((bf16[256,128]{1,0:T(8,128)(2,1)S(1)}, bf16[256,128]{1,0:T(8,128)(2,1)S(1)}, u32[]{:S(2)}, u32[]{:S(2)}) %collective-permute-start.3) | collective-permute-done | bytes 65568 | tf_op jit(solution)/shard_map/ppermute | solution.py:43
  17.2 0.0 collective-permute-done.4.refs_3_
  17.2 0.0 collective-permute-done.5.refs_4_
  17.2 0.0 copy-done.1
  17.2 0.0 copy-done.2
  17.2 0.5 %shard_map.98 = (bf16[384,128]{1,0:T(8,128)(2,1)S(1)}, bf16[128,128]{1,0:T(8,128)(2,1)S(1)}, f32[128,256]{1,0:T(8,128)S(1)}) custom-call(bf16[512,512]{1,0:T(8,128)(2,1)S(1)} %shard_map.96.refs_0_.matrix, bf16[256,128]{1,0:T(8,128)(2,1)S(1)} %get-tuple-element.17.refs_1_, bf16[256,128]{1,0:T(8,128)(2,1)S(1)} %collective-permute-done.3.refs_2_, ...), custom_call_target="tpu_custom_call" | custom-call | flops 117440512 | tf_op jit(solution)/shard_map/pallas_call | solution.py:306
  17.8 1.5 %collective-permute-start.7 = (bf16[384,128]{1,0:T(8,128)(2,1)S(1)}, bf16[384,128]{1,0:T(8,128)(2,1)S(1)}, u32[]{:S(2)}, u32[]{:S(2)}) collective-permute-start(bf16[384,128]{1,0:T(8,128)(2,1)S(1)} %get-tuple-element.22.message.refs_0_), channel_id=1, source_target_pairs={{0,1},{1,0},{2,3},{3,2},{4,5},{5,4},{6,7},{7,6},{8,9},{9,8},{10,11... | collective-permute-start | bytes 294920 | tf_op jit(solution)/shard_map/ppermute | solution.py:58
  19.3 0.0 collective-permute-start.9
  19.3 0.7 %collective-permute-start.8 = (bf16[128,128]{1,0:T(8,128)(2,1)S(1)}, bf16[128,128]{1,0:T(8,128)(2,1)S(1)}, u32[]{:S(2)}, u32[]{:S(2)}) collective-permute-start(bf16[128,128]{1,0:T(8,128)(2,1)S(1)} %get-tuple-element.23), channel_id=1, source_target_pairs={{0,5},{1,4},{2,7},{3,6},{4,1},{5,0},{6,3},{7,2},{8,13},{9,12},{10,... | collective-permute-start | bytes 98312 | tf_op jit(solution)/shard_map/ppermute | solution.py:318
  20.0 0.2 shard_map.100.begun
  20.2 0.3 collective-permute-done.9.refs_3_
  20.5 2.3 %collective-permute-done.8.refs_2_ = bf16[128,128]{1,0:T(8,128)(2,1)S(1)} collective-permute-done((bf16[128,128]{1,0:T(8,128)(2,1)S(1)}, bf16[128,128]{1,0:T(8,128)(2,1)S(1)}, u32[]{:S(2)}, u32[]{:S(2)}) %collective-permute-start.8) | collective-permute-done | bytes 32800 | tf_op jit(solution)/shard_map/ppermute | solution.py:318
  22.8 0.0 collective-permute-done.7.refs_1_
  22.8 0.2 shard_map.101
  23.0 1.4 %collective-permute-start.10 = (bf16[256,128]{1,0:T(8,128)(2,1)S(1)}, bf16[256,128]{1,0:T(8,128)(2,1)S(1)}, u32[]{:S(2)}, u32[]{:S(2)}) collective-permute-start(bf16[256,128]{1,0:T(8,128)(2,1)S(1)} %get-tuple-element.26), channel_id=1, source_target_pairs={{0,12},{4,0},{8,4},{12,8},{1,13},{5,1},{9,5},{13,9},{2,14},{6,2},{... | collective-permute-start | bytes 196616 | tf_op jit(solution)/shard_map/ppermute | solution.py:43
  24.4 0.7 %collective-permute-start.11 = (bf16[256,128]{1,0:T(8,128)(2,1)S(1)}, bf16[256,128]{1,0:T(8,128)(2,1)S(1)}, u32[]{:S(2)}, u32[]{:S(2)}) collective-permute-start(bf16[256,128]{1,0:T(8,128)(2,1)S(1)} %get-tuple-element.27), channel_id=1, source_target_pairs={{0,8},{4,12},{8,0},{12,4},{1,9},{5,13},{9,1},{13,5},{2,10},{6,14},... | collective-permute-start | bytes 196616 | tf_op jit(solution)/shard_map/ppermute | solution.py:43
  25.1 0.0 collective-permute-start.12
  25.1 0.7 %shard_map.99 = bf16[128,256]{1,0:T(8,128)(2,1)} custom-call(f32[128,256]{1,0:T(8,128)S(1)} %get-tuple-element.21.pre), custom_call_target="tpu_custom_call" | custom-call | tf_op jit(solution)/shard_map/pallas_call | solution.py:323
  25.7 0.9 %collective-permute-done.10.refs_0_ = bf16[256,128]{1,0:T(8,128)(2,1)S(1)} collective-permute-done((bf16[256,128]{1,0:T(8,128)(2,1)S(1)}, bf16[256,128]{1,0:T(8,128)(2,1)S(1)}, u32[]{:S(2)}, u32[]{:S(2)}) %collective-permute-start.10) | collective-permute-done | bytes 65568 | tf_op jit(solution)/shard_map/ppermute | solution.py:43
  26.6 2.6 %collective-permute-done.11.refs_1_ = bf16[256,128]{1,0:T(8,128)(2,1)S(1)} collective-permute-done((bf16[256,128]{1,0:T(8,128)(2,1)S(1)}, bf16[256,128]{1,0:T(8,128)(2,1)S(1)}, u32[]{:S(2)}, u32[]{:S(2)}) %collective-permute-start.11) | collective-permute-done | bytes 65568 | tf_op jit(solution)/shard_map/ppermute | solution.py:43
  29.2 0.1 collective-permute-done.12.refs_2_
  29.4 0.7 %shard_map.102 = (bf16[128,128]{1,0:T(8,128)(2,1)}, f32[128,256]{1,0:T(8,128)}) custom-call(f32[128,128]{1,0:T(8,128)S(1)} %get-tuple-element.24.own, bf16[128,128]{1,0:T(8,128)(2,1)S(1)} %get-tuple-element.25.kept, bf16[256,128]{1,0:T(8,128)(2,1)S(1)} %collective-permute-done.10.refs_0_, bf16[256,128]{1,0:T(8,128)(2,1)S(1)} %collective-permute-done.11.refs_1_, ...), custom_call_target="tpu_custom_call" | custom-call | tf_op jit(solution)/shard_map/pallas_call | solution.py:343
  (1 shorter events, 0.0 us)
Async XLA Ops:
  0.6 7.0 %copy-start = (bf16[1,1,8,128,128]{4,3,2,1,0:T(8,128)(2,1)S(1)}, bf16[1,1,8,128,128]{4,3,2,1,0:T(8,128)(2,1)}, u32[]{:S(2)}) copy-start(bf16[1,1,8,128,128]{4,3,2,1,0:T(8,128)(2,1)} %vals.1) | copy-start | bytes 786436
  0.6 7.7 %collective-permute-start.1 = (bf16[128,128]{1,0:T(8,128)(2,1)}, bf16[128,128]{1,0:T(8,128)(2,1)S(1)}, u32[]{:S(2)}, u32[]{:S(2)}) collective-permute-start(bf16[128,128]{1,0:T(8,128)(2,1)} %refs_0_.1), channel_id=1, source_target_pairs={{0,8},{4,12},{8,0},{12,4},{1,9},{5,13},{9,1},{13,5},{2,10},{6,14},... | collective-permute-start | bytes 98312 | tf_op jit(solution)/shard_map/ppermute | solution.py:58
  3.6 4.7 %collective-permute-start = (bf16[128,128]{1,0:T(8,128)(2,1)}, bf16[128,128]{1,0:T(8,128)(2,1)S(1)}, u32[]{:S(2)}, u32[]{:S(2)}) collective-permute-start(bf16[128,128]{1,0:T(8,128)(2,1)} %refs_0_.1), channel_id=1, source_target_pairs={{0,12},{4,8},{8,4},{12,0},{1,13},{5,9},{9,5},{13,1},{2,14},{6,10},... | collective-permute-start | bytes 98312 | tf_op jit(solution)/shard_map/ppermute | solution.py:58
  3.6 4.7 %collective-permute-start.2 = (bf16[128,128]{1,0:T(8,128)(2,1)}, bf16[128,128]{1,0:T(8,128)(2,1)S(1)}, u32[]{:S(2)}, u32[]{:S(2)}) collective-permute-start(bf16[128,128]{1,0:T(8,128)(2,1)} %refs_0_.1), channel_id=1, source_target_pairs={{0,4},{4,0},{8,12},{12,8},{1,5},{5,1},{9,13},{13,9},{2,6},{6,2},{1... | collective-permute-start | bytes 98312 | tf_op jit(solution)/shard_map/ppermute | solution.py:58
  3.8 9.8 %collective-permute-start.6 = (bf16[128,256]{1,0:T(8,128)(2,1)}, bf16[128,256]{1,0:T(8,128)(2,1)S(1)}, u32[]{:S(2)}, u32[]{:S(2)}) collective-permute-start(bf16[128,256]{1,0:T(8,128)(2,1)} %refs_6_.1), channel_id=1, source_target_pairs={{0,2},{1,3},{2,0},{3,1},{4,6},{5,7},{6,4},{7,5},{8,10},{9,11},{10,... | collective-permute-start | bytes 196616 | tf_op jit(solution)/shard_map/ppermute | solution.py:58
  6.9 0.7 %copy-start.4 = (s32[1,1,8]{2,1,0:T(1,128)S(1)}, s32[1,1,8]{2,1,0:T(1,128)}, u32[]{:S(2)}) copy-start(s32[1,1,8]{2,1,0:T(1,128)} %rows_in.1) | copy-start | bytes 100
  6.9 0.7 %copy-start.5 = (s32[1,1,8]{2,1,0:T(1,128)S(1)}, s32[1,1,8]{2,1,0:T(1,128)}, u32[]{:S(2)}) copy-start(s32[1,1,8]{2,1,0:T(1,128)} %cols_in.1) | copy-start | bytes 100
  7.6 0.8 %copy-start.3 = (bf16[128,128]{1,0:T(8,128)(2,1)S(1)}, bf16[128,128]{1,0:T(8,128)(2,1)}, u32[]{:S(2)}) copy-start(bf16[128,128]{1,0:T(8,128)(2,1)} %refs_0_.1) | copy-start | bytes 98308
  8.7 8.5 %collective-permute-start.3 = (bf16[256,128]{1,0:T(8,128)(2,1)S(1)}, bf16[256,128]{1,0:T(8,128)(2,1)S(1)}, u32[]{:S(2)}, u32[]{:S(2)}) collective-permute-start(bf16[256,128]{1,0:T(8,128)(2,1)S(1)} %get-tuple-element.18), channel_id=1, source_target_pairs={{0,1},{1,3},{2,0},{3,2},{4,5},{5,7},{6,4},{7,6},{8,9},{9,11},{10,8... | collective-permute-start | bytes 196616 | tf_op jit(solution)/shard_map/ppermute | solution.py:43
  10.3 6.9 %collective-permute-start.4 = (bf16[256,128]{1,0:T(8,128)(2,1)S(1)}, bf16[256,128]{1,0:T(8,128)(2,1)S(1)}, u32[]{:S(2)}, u32[]{:S(2)}) collective-permute-start(bf16[256,128]{1,0:T(8,128)(2,1)S(1)} %get-tuple-element.19), channel_id=1, source_target_pairs={{0,3},{1,2},{2,1},{3,0},{4,7},{5,6},{6,5},{7,4},{8,11},{9,10},{10,... | collective-permute-start | bytes 196616 | tf_op jit(solution)/shard_map/ppermute | solution.py:43
  11.7 5.5 %copy-start.1 = (bf16[128,256]{1,0:T(8,128)(2,1)S(1)}, bf16[128,256]{1,0:T(8,128)(2,1)}, u32[]{:S(2)}) copy-start(bf16[128,256]{1,0:T(8,128)(2,1)} %refs_5_.1) | copy-start | bytes 196612
  11.7 5.5 %copy-start.2 = (bf16[128,256]{1,0:T(8,128)(2,1)S(1)}, bf16[128,256]{1,0:T(8,128)(2,1)}, u32[]{:S(2)}) copy-start(bf16[128,256]{1,0:T(8,128)(2,1)} %refs_6_.1) | copy-start | bytes 196612
  11.7 5.5 %collective-permute-start.5 = (bf16[256,128]{1,0:T(8,128)(2,1)S(1)}, bf16[256,128]{1,0:T(8,128)(2,1)S(1)}, u32[]{:S(2)}, u32[]{:S(2)}) collective-permute-start(bf16[256,128]{1,0:T(8,128)(2,1)S(1)} %get-tuple-element.20), channel_id=1, source_target_pairs={{0,2},{1,0},{2,3},{3,1},{4,6},{5,4},{6,7},{7,5},{8,10},{9,8},{10,1... | collective-permute-start | bytes 196616 | tf_op jit(solution)/shard_map/ppermute | solution.py:43
  17.8 5.0 %collective-permute-start.7 = (bf16[384,128]{1,0:T(8,128)(2,1)S(1)}, bf16[384,128]{1,0:T(8,128)(2,1)S(1)}, u32[]{:S(2)}, u32[]{:S(2)}) collective-permute-start(bf16[384,128]{1,0:T(8,128)(2,1)S(1)} %get-tuple-element.22.message.refs_0_), channel_id=1, source_target_pairs={{0,1},{1,0},{2,3},{3,2},{4,5},{5,4},{6,7},{7,6},{8,9},{9,8},{10,11... | collective-permute-start | bytes 294920 | tf_op jit(solution)/shard_map/ppermute | solution.py:58
  19.3 1.2 %collective-permute-start.9 = (bf16[128,128]{1,0:T(8,128)(2,1)S(1)}, bf16[128,128]{1,0:T(8,128)(2,1)S(1)}, u32[]{:S(2)}, u32[]{:S(2)}) collective-permute-start(bf16[128,128]{1,0:T(8,128)(2,1)S(1)} %get-tuple-element.23), channel_id=1, source_target_pairs={{0,4},{4,0},{8,12},{12,8},{1,5},{5,1},{9,13},{13,9},{2,6},{6,2},{1... | collective-permute-start | bytes 98312 | tf_op jit(solution)/shard_map/ppermute | solution.py:58
  19.3 3.5 %collective-permute-start.8 = (bf16[128,128]{1,0:T(8,128)(2,1)S(1)}, bf16[128,128]{1,0:T(8,128)(2,1)S(1)}, u32[]{:S(2)}, u32[]{:S(2)}) collective-permute-start(bf16[128,128]{1,0:T(8,128)(2,1)S(1)} %get-tuple-element.23), channel_id=1, source_target_pairs={{0,5},{1,4},{2,7},{3,6},{4,1},{5,0},{6,3},{7,2},{8,13},{9,12},{10,... | collective-permute-start | bytes 98312 | tf_op jit(solution)/shard_map/ppermute | solution.py:318
  23.0 3.6 %collective-permute-start.10 = (bf16[256,128]{1,0:T(8,128)(2,1)S(1)}, bf16[256,128]{1,0:T(8,128)(2,1)S(1)}, u32[]{:S(2)}, u32[]{:S(2)}) collective-permute-start(bf16[256,128]{1,0:T(8,128)(2,1)S(1)} %get-tuple-element.26), channel_id=1, source_target_pairs={{0,12},{4,0},{8,4},{12,8},{1,13},{5,1},{9,5},{13,9},{2,14},{6,2},{... | collective-permute-start | bytes 196616 | tf_op jit(solution)/shard_map/ppermute | solution.py:43
  24.4 4.9 %collective-permute-start.11 = (bf16[256,128]{1,0:T(8,128)(2,1)S(1)}, bf16[256,128]{1,0:T(8,128)(2,1)S(1)}, u32[]{:S(2)}, u32[]{:S(2)}) collective-permute-start(bf16[256,128]{1,0:T(8,128)(2,1)S(1)} %get-tuple-element.27), channel_id=1, source_target_pairs={{0,8},{4,12},{8,0},{12,4},{1,9},{5,13},{9,1},{13,5},{2,10},{6,14},... | collective-permute-start | bytes 196616 | tf_op jit(solution)/shard_map/ppermute | solution.py:43
  25.1 4.3 %collective-permute-start.12 = (bf16[256,128]{1,0:T(8,128)(2,1)S(1)}, bf16[256,128]{1,0:T(8,128)(2,1)S(1)}, u32[]{:S(2)}, u32[]{:S(2)}) collective-permute-start(bf16[256,128]{1,0:T(8,128)(2,1)S(1)} %get-tuple-element.28), channel_id=1, source_target_pairs={{0,4},{4,8},{8,12},{12,0},{1,5},{5,9},{9,13},{13,1},{2,6},{6,10},{... | collective-permute-start | bytes 196616 | tf_op jit(solution)/shard_map/ppermute | solution.py:43

commit v27 on v24

--- a/solution.py
+++ b/solution.py
@@ -228,8 +228,10 @@
     term = term.astype(kept.dtype)
     kept[...] = term
     here, size = lax.axis_index("row"), lax.axis_size("row")
+    odd_col = lax.rem(lax.axis_index("col"), 2) == 1
     for d, send in enumerate(sends, 1):
-        start = pl.multiple_of((lax.rem(here + d, size) ^ here) * rows, rows)
+        there = lax.rem(here + jnp.where(odd_col, size - d, d), size)
+        start = pl.multiple_of((there ^ here) * rows, rows)
         send[:rows] = product[pl.ds(start, rows)].astype(send.dtype)
         send[rows:] = term
 
@@ -336,7 +338,14 @@
         scratch=[pltpu.VMEM((across, width), jnp.float32)],
         **forward,
     )(far, begun, *messages, *others)
-    parts = exchange(sends, "row", True)
+    parts = []
+    for d, send in enumerate(sends, 1):
+        pairs = []
+        for r in range(n_row):
+            for c in range(n_col):
+                there = (r + (-d if c % 2 else d)) % n_row
+                pairs.append((r * n_col + c, there * n_col + c))
+        parts.append(lax.ppermute(send, ("row", "col"), pairs))
 
     scale = float(nodes * n_row * n_col) ** -0.5
     grad_features, grad_weight = call(

time: 28.9 us -> 28.9 us (level)
    ppermute x0 -> x3, starting transfers between devices: none -> 3.14 us  [per_device(): parts.append(lax.ppermute(send, ('row', 'col'), pairs))]
    ppermute x6 -> x3, starting transfers between devices: 7.97 us -> 4.83 us  [exchange(): lax.ppermute(send, axis, [(s, target(s, d)) for s in range(n)])]
    ppermute x0 -> x3, waiting for transfers between devices: none -> 1.25 us  [per_device(): parts.append(lax.ppermute(send, ('row', 'col'), pairs))]
    ppermute x6 -> x3, waiting for transfers between devices: 4.27 us -> 3.02 us  [exchange(): lax.ppermute(send, axis, [(s, target(s, d)) for s in range(n)])]
where the time goes in v27:
time: 28.9 us; the launch traced here: 28.5 us
  starting transfers between devices  16.1 us (56%)
  waiting for transfers between devices  7.25 us (25%)
  Pallas kernels  3.65 us (13%)
  between operations  1.44 us (5%)
    ppermute x6, starting transfers between devices, swap(): return lax.ppermute(value, axis, [(s, s ^ distance) for s in range(n)])  8.17 us
    ppermute x3, starting transfers between devices, exchange(): lax.ppermute(send, axis, [(s, target(s, d)) for s in range(n)])  4.83 us
    ppermute x3, starting transfers between devices, per_device(): parts.append(lax.ppermute(send, ('row', 'col'), pairs))  3.14 us
    ppermute x3, waiting for transfers between devices, exchange(): lax.ppermute(send, axis, [(s, target(s, d)) for s in range(n)])  3.02 us
    ppermute x1, waiting for transfers between devices, per_device(): lax.ppermute(other, ('row', 'col'), corner)  2.96 us
    ppermute x3, waiting for transfers between devices, per_device(): parts.append(lax.ppermute(send, ('row', 'col'), pairs))  1.25 us
    pallas_call x1, Pallas kernels, per_device(): call(functools.partial(last_kernel, scale), [((nodes, width), NARROW), ((...  0.69 us
    pallas_call x1, Pallas kernels, per_device(): call(functools.partial(dense_kernel, nodes // side, paired), [((down, acr...  0.68 us
  transfers between devices with their start and end apart: 13, of which 6 were waited for; matrix products, arithmetic and copies ran while one was open for 0% of the time, Pallas kernels for 8%

profile of v27, /device:TPU:0, one launch (start us, length us, event | category | flops | bytes accessed | tf_op | source)
XLA Modules:
  0.0 28.5 jit_solution(13983050588200731961)
XLA Ops:
  0.6 0.0 copy-start
  0.6 2.4 %collective-permute-start.1 = (bf16[128,128]{1,0:T(8,128)(2,1)}, bf16[128,128]{1,0:T(8,128)(2,1)S(1)}, u32[]{:S(2)}, u32[]{:S(2)}) collective-permute-start(bf16[128,128]{1,0:T(8,128)(2,1)} %refs_0_.1), channel_id=1, source_target_pairs={{0,12},{4,8},{8,4},{12,0},{1,13},{5,9},{9,5},{13,1},{2,14},{6,10},... | collective-permute-start | bytes 98312 | tf_op jit(solution)/shard_map/ppermute | solution.py:58
  3.1 0.6 %collective-permute-start = (bf16[128,128]{1,0:T(8,128)(2,1)}, bf16[128,128]{1,0:T(8,128)(2,1)S(1)}, u32[]{:S(2)}, u32[]{:S(2)}) collective-permute-start(bf16[128,128]{1,0:T(8,128)(2,1)} %refs_0_.1), channel_id=1, source_target_pairs={{0,8},{4,12},{8,0},{12,4},{1,9},{5,13},{9,1},{13,5},{2,10},{6,14},... | collective-permute-start | bytes 98312 | tf_op jit(solution)/shard_map/ppermute | solution.py:58
  3.7 0.0 collective-permute-start.2
  3.8 2.8 %collective-permute-start.6 = (bf16[128,256]{1,0:T(8,128)(2,1)}, bf16[128,256]{1,0:T(8,128)(2,1)S(1)}, u32[]{:S(2)}, u32[]{:S(2)}) collective-permute-start(bf16[128,256]{1,0:T(8,128)(2,1)} %refs_6_.1), channel_id=1, source_target_pairs={{0,2},{1,3},{2,0},{3,1},{4,6},{5,7},{6,4},{7,5},{8,10},{9,11},{10,... | collective-permute-start | bytes 196616 | tf_op jit(solution)/shard_map/ppermute | solution.py:58
  6.6 0.0 copy-start.4
  6.7 0.0 copy-start.5
  7.3 0.0 copy-done
  7.3 0.0 copy-done.4
  7.3 0.0 copy-done.5
  7.4 0.0 copy-start.3
  7.4 0.7 %shard_map.95.near.matrix = bf16[512,512]{1,0:T(8,128)(2,1)S(1)} custom-call(bf16[512,512]{1,0:T(8,128)(2,1)S(1)} %shard_map.94.blank, bf16[1,1,8,128,128]{4,3,2,1,0:T(8,128)(2,1)S(1)} %copy-done, s32[1,1,8]{2,1,0:T(1,128)S(1)} %copy-done.4, s32[1,1,8]{2,1,0:T(1,128)S(1)} %copy-done.5, s32[1,1]{1,0:T(1,128)S(6)} %copy.12.count_in), custom_call_target="tpu_custom_call", output_to_operand_aliasing={{}: (0, {})} | custom-call | bytes 1048576 | tf_op jit(solution)/shard_map/pallas_call | solution.py:263
  8.1 0.0 collective-permute-done.1.refs_2_
  8.1 0.0 collective-permute-done.refs_1_
  8.1 0.0 collective-permute-done.2.refs_3_
  8.1 0.0 copy-done.3
  8.1 0.3 %shard_map.97 = (bf16[256,128]{1,0:T(8,128)(2,1)S(1)}, bf16[256,128]{1,0:T(8,128)(2,1)S(1)}, bf16[256,128]{1,0:T(8,128)(2,1)S(1)}, bf16[256,128]{1,0:T(8,128)(2,1)S(1)}) custom-call(bf16[512,512]{1,0:T(8,128)(2,1)S(1)} %shard_map.95.near.matrix, bf16[128,128]{1,0:T(8,128)(2,1)S(1)} %copy-done.3, bf16[128,128]{1,0:T(8,128)(2,1)S(1)} %collective-permute-done.refs_1_, ...), custom_call_target="tpu_custom_call" | custom-call | flops 67108864 | bytes 1048576 | tf_op jit(solution)/shard_map/pallas_call | solution.py:280
  8.4 1.6 %collective-permute-start.3 = (bf16[256,128]{1,0:T(8,128)(2,1)S(1)}, bf16[256,128]{1,0:T(8,128)(2,1)S(1)}, u32[]{:S(2)}, u32[]{:S(2)}) collective-permute-start(bf16[256,128]{1,0:T(8,128)(2,1)S(1)} %get-tuple-element.18), channel_id=1, source_target_pairs={{0,1},{1,3},{2,0},{3,2},{4,5},{5,7},{6,4},{7,6},{8,9},{9,11},{10,8... | collective-permute-start | bytes 196616 | tf_op jit(solution)/shard_map/ppermute | solution.py:43
  10.1 1.6 %collective-permute-start.4 = (bf16[256,128]{1,0:T(8,128)(2,1)S(1)}, bf16[256,128]{1,0:T(8,128)(2,1)S(1)}, u32[]{:S(2)}, u32[]{:S(2)}) collective-permute-start(bf16[256,128]{1,0:T(8,128)(2,1)S(1)} %get-tuple-element.19), channel_id=1, source_target_pairs={{0,3},{1,2},{2,1},{3,0},{4,7},{5,6},{6,5},{7,4},{8,11},{9,10},{10,... | collective-permute-start | bytes 196616 | tf_op jit(solution)/shard_map/ppermute | solution.py:43
  11.7 0.0 copy-start.1
  11.7 0.0 copy-start.2
  11.7 1.6 %collective-permute-start.5 = (bf16[256,128]{1,0:T(8,128)(2,1)S(1)}, bf16[256,128]{1,0:T(8,128)(2,1)S(1)}, u32[]{:S(2)}, u32[]{:S(2)}) collective-permute-start(bf16[256,128]{1,0:T(8,128)(2,1)S(1)} %get-tuple-element.20), channel_id=1, source_target_pairs={{0,2},{1,0},{2,3},{3,1},{4,6},{5,4},{6,7},{7,5},{8,10},{9,8},{10,1... | collective-permute-start | bytes 196616 | tf_op jit(solution)/shard_map/ppermute | solution.py:43
  13.3 0.3 %shard_map.96.refs_0_.matrix = bf16[512,512]{1,0:T(8,128)(2,1)S(1)} custom-call(bf16[512,512]{1,0:T(8,128)(2,1)S(1)} %shard_map.95.near.matrix), custom_call_target="tpu_custom_call" | custom-call | bytes 1572864 | tf_op jit(solution)/shard_map/pallas_call | solution.py:297
  13.6 0.0 collective-permute-done.6.refs_7_
  13.6 0.4 %collective-permute-done.3.refs_2_ = bf16[256,128]{1,0:T(8,128)(2,1)S(1)} collective-permute-done((bf16[256,128]{1,0:T(8,128)(2,1)S(1)}, bf16[256,128]{1,0:T(8,128)(2,1)S(1)}, u32[]{:S(2)}, u32[]{:S(2)}) %collective-permute-start.3) | collective-permute-done | bytes 65568 | tf_op jit(solution)/shard_map/ppermute | solution.py:43
  14.0 2.4 %collective-permute-done.4.refs_3_ = bf16[256,128]{1,0:T(8,128)(2,1)S(1)} collective-permute-done((bf16[256,128]{1,0:T(8,128)(2,1)S(1)}, bf16[256,128]{1,0:T(8,128)(2,1)S(1)}, u32[]{:S(2)}, u32[]{:S(2)}) %collective-permute-start.4) | collective-permute-done | bytes 65568 | tf_op jit(solution)/shard_map/ppermute | solution.py:43
  16.4 0.2 collective-permute-done.5.refs_4_
  16.6 0.0 copy-done.1
  16.6 0.0 copy-done.2
  16.7 0.5 %shard_map.98 = (bf16[384,128]{1,0:T(8,128)(2,1)S(1)}, bf16[128,128]{1,0:T(8,128)(2,1)S(1)}, f32[128,256]{1,0:T(8,128)S(1)}) custom-call(bf16[512,512]{1,0:T(8,128)(2,1)S(1)} %shard_map.96.refs_0_.matrix, bf16[256,128]{1,0:T(8,128)(2,1)S(1)} %get-tuple-element.17.refs_1_, bf16[256,128]{1,0:T(8,128)(2,1)S(1)} %collective-permute-done.3.refs_2_, ...), custom_call_target="tpu_custom_call" | custom-call | flops 117440512 | tf_op jit(solution)/shard_map/pallas_call | solution.py:307
  17.2 1.8 %collective-permute-start.7 = (bf16[384,128]{1,0:T(8,128)(2,1)S(1)}, bf16[384,128]{1,0:T(8,128)(2,1)S(1)}, u32[]{:S(2)}, u32[]{:S(2)}) collective-permute-start(bf16[384,128]{1,0:T(8,128)(2,1)S(1)} %get-tuple-element.22.message.refs_0_), channel_id=1, source_target_pairs={{0,1},{1,0},{2,3},{3,2},{4,5},{5,4},{6,7},{7,6},{8,9},{9,8},{10,11... | collective-permute-start | bytes 294920 | tf_op jit(solution)/shard_map/ppermute | solution.py:58
  19.0 0.0 collective-permute-start.9
  19.0 0.4 %collective-permute-start.8 = (bf16[128,128]{1,0:T(8,128)(2,1)S(1)}, bf16[128,128]{1,0:T(8,128)(2,1)S(1)}, u32[]{:S(2)}, u32[]{:S(2)}) collective-permute-start(bf16[128,128]{1,0:T(8,128)(2,1)S(1)} %get-tuple-element.23), channel_id=1, source_target_pairs={{0,4},{4,0},{8,12},{12,8},{1,5},{5,1},{9,13},{13,9},{2,6},{6,2},{1... | collective-permute-start | bytes 98312 | tf_op jit(solution)/shard_map/ppermute | solution.py:58
  19.4 0.2 shard_map.100.begun
  19.6 3.0 %collective-permute-done.9.refs_3_ = bf16[128,128]{1,0:T(8,128)(2,1)S(1)} collective-permute-done((bf16[128,128]{1,0:T(8,128)(2,1)S(1)}, bf16[128,128]{1,0:T(8,128)(2,1)S(1)}, u32[]{:S(2)}, u32[]{:S(2)}) %collective-permute-start.9) | collective-permute-done | bytes 32800 | tf_op jit(solution)/shard_map/ppermute | solution.py:319
  22.5 0.0 collective-permute-done.8.refs_2_
  22.5 0.0 collective-permute-done.7.refs_1_
  22.5 0.2 shard_map.101
  22.8 0.1 collective-permute-start.10
  22.9 1.7 %collective-permute-start.11 = (bf16[256,128]{1,0:T(8,128)(2,1)S(1)}, bf16[256,128]{1,0:T(8,128)(2,1)S(1)}, u32[]{:S(2)}, u32[]{:S(2)}) collective-permute-start(bf16[256,128]{1,0:T(8,128)(2,1)S(1)} %get-tuple-element.27), channel_id=1, source_target_pairs={{0,8},{1,9},{2,10},{3,11},{4,12},{5,13},{6,14},{7,15},{8,0},{9,1},... | collective-permute-start | bytes 196616 | tf_op jit(solution)/shard_map/ppermute | solution.py:348
  24.6 1.4 %collective-permute-start.12 = (bf16[256,128]{1,0:T(8,128)(2,1)S(1)}, bf16[256,128]{1,0:T(8,128)(2,1)S(1)}, u32[]{:S(2)}, u32[]{:S(2)}) collective-permute-start(bf16[256,128]{1,0:T(8,128)(2,1)S(1)} %get-tuple-element.28), channel_id=1, source_target_pairs={{0,12},{1,5},{2,14},{3,7},{4,0},{5,9},{6,2},{7,11},{8,4},{9,13},{1... | collective-permute-start | bytes 196616 | tf_op jit(solution)/shard_map/ppermute | solution.py:348
  25.9 0.7 %shard_map.99 = bf16[128,256]{1,0:T(8,128)(2,1)} custom-call(f32[128,256]{1,0:T(8,128)S(1)} %get-tuple-element.21.pre), custom_call_target="tpu_custom_call" | custom-call | tf_op jit(solution)/shard_map/pallas_call | solution.py:324
  26.6 0.0 collective-permute-done.10.refs_0_
  26.6 0.7 %collective-permute-done.11.refs_1_ = bf16[256,128]{1,0:T(8,128)(2,1)S(1)} collective-permute-done((bf16[256,128]{1,0:T(8,128)(2,1)S(1)}, bf16[256,128]{1,0:T(8,128)(2,1)S(1)}, u32[]{:S(2)}, u32[]{:S(2)}) %collective-permute-start.11) | collective-permute-done | bytes 65568 | tf_op jit(solution)/shard_map/ppermute | solution.py:348
  27.3 0.5 %collective-permute-done.12.refs_2_ = bf16[256,128]{1,0:T(8,128)(2,1)S(1)} collective-permute-done((bf16[256,128]{1,0:T(8,128)(2,1)S(1)}, bf16[256,128]{1,0:T(8,128)(2,1)S(1)}, u32[]{:S(2)}, u32[]{:S(2)}) %collective-permute-start.12) | collective-permute-done | bytes 65568 | tf_op jit(solution)/shard_map/ppermute | solution.py:348
  27.8 0.7 %shard_map.102 = (bf16[128,128]{1,0:T(8,128)(2,1)}, f32[128,256]{1,0:T(8,128)}) custom-call(f32[128,128]{1,0:T(8,128)S(1)} %get-tuple-element.24.own, bf16[128,128]{1,0:T(8,128)(2,1)S(1)} %get-tuple-element.25.kept, bf16[256,128]{1,0:T(8,128)(2,1)S(1)} %collective-permute-done.10.refs_0_, bf16[256,128]{1,0:T(8,128)(2,1)S(1)} %collective-permute-done.11.refs_1_, ...), custom_call_target="tpu_custom_call" | custom-call | tf_op jit(solution)/shard_map/pallas_call | solution.py:351
  (1 shorter events, 0.0 us)
Async XLA Ops:
  0.6 6.7 %copy-start = (bf16[1,1,8,128,128]{4,3,2,1,0:T(8,128)(2,1)S(1)}, bf16[1,1,8,128,128]{4,3,2,1,0:T(8,128)(2,1)}, u32[]{:S(2)}) copy-start(bf16[1,1,8,128,128]{4,3,2,1,0:T(8,128)(2,1)} %vals.1) | copy-start | bytes 786436
  0.6 7.4 %collective-permute-start.1 = (bf16[128,128]{1,0:T(8,128)(2,1)}, bf16[128,128]{1,0:T(8,128)(2,1)S(1)}, u32[]{:S(2)}, u32[]{:S(2)}) collective-permute-start(bf16[128,128]{1,0:T(8,128)(2,1)} %refs_0_.1), channel_id=1, source_target_pairs={{0,12},{4,8},{8,4},{12,0},{1,13},{5,9},{9,5},{13,1},{2,14},{6,10},... | collective-permute-start | bytes 98312 | tf_op jit(solution)/shard_map/ppermute | solution.py:58
  3.1 5.0 %collective-permute-start = (bf16[128,128]{1,0:T(8,128)(2,1)}, bf16[128,128]{1,0:T(8,128)(2,1)S(1)}, u32[]{:S(2)}, u32[]{:S(2)}) collective-permute-start(bf16[128,128]{1,0:T(8,128)(2,1)} %refs_0_.1), channel_id=1, source_target_pairs={{0,8},{4,12},{8,0},{12,4},{1,9},{5,13},{9,1},{13,5},{2,10},{6,14},... | collective-permute-start | bytes 98312 | tf_op jit(solution)/shard_map/ppermute | solution.py:58
  3.7 4.4 %collective-permute-start.2 = (bf16[128,128]{1,0:T(8,128)(2,1)}, bf16[128,128]{1,0:T(8,128)(2,1)S(1)}, u32[]{:S(2)}, u32[]{:S(2)}) collective-permute-start(bf16[128,128]{1,0:T(8,128)(2,1)} %refs_0_.1), channel_id=1, source_target_pairs={{0,4},{4,0},{8,12},{12,8},{1,5},{5,1},{9,13},{13,9},{2,6},{6,2},{1... | collective-permute-start | bytes 98312 | tf_op jit(solution)/shard_map/ppermute | solution.py:58
  3.8 9.9 %collective-permute-start.6 = (bf16[128,256]{1,0:T(8,128)(2,1)}, bf16[128,256]{1,0:T(8,128)(2,1)S(1)}, u32[]{:S(2)}, u32[]{:S(2)}) collective-permute-start(bf16[128,256]{1,0:T(8,128)(2,1)} %refs_6_.1), channel_id=1, source_target_pairs={{0,2},{1,3},{2,0},{3,1},{4,6},{5,7},{6,4},{7,5},{8,10},{9,11},{10,... | collective-permute-start | bytes 196616 | tf_op jit(solution)/shard_map/ppermute | solution.py:58
  6.6 0.7 %copy-start.4 = (s32[1,1,8]{2,1,0:T(1,128)S(1)}, s32[1,1,8]{2,1,0:T(1,128)}, u32[]{:S(2)}) copy-start(s32[1,1,8]{2,1,0:T(1,128)} %rows_in.1) | copy-start | bytes 100
  6.7 0.7 %copy-start.5 = (s32[1,1,8]{2,1,0:T(1,128)S(1)}, s32[1,1,8]{2,1,0:T(1,128)}, u32[]{:S(2)}) copy-start(s32[1,1,8]{2,1,0:T(1,128)} %cols_in.1) | copy-start | bytes 100
  7.4 0.8 %copy-start.3 = (bf16[128,128]{1,0:T(8,128)(2,1)S(1)}, bf16[128,128]{1,0:T(8,128)(2,1)}, u32[]{:S(2)}) copy-start(bf16[128,128]{1,0:T(8,128)(2,1)} %refs_0_.1) | copy-start | bytes 98308
  8.4 5.6 %collective-permute-start.3 = (bf16[256,128]{1,0:T(8,128)(2,1)S(1)}, bf16[256,128]{1,0:T(8,128)(2,1)S(1)}, u32[]{:S(2)}, u32[]{:S(2)}) collective-permute-start(bf16[256,128]{1,0:T(8,128)(2,1)S(1)} %get-tuple-element.18), channel_id=1, source_target_pairs={{0,1},{1,3},{2,0},{3,2},{4,5},{5,7},{6,4},{7,6},{8,9},{9,11},{10,8... | collective-permute-start | bytes 196616 | tf_op jit(solution)/shard_map/ppermute | solution.py:43
  10.1 6.4 %collective-permute-start.4 = (bf16[256,128]{1,0:T(8,128)(2,1)S(1)}, bf16[256,128]{1,0:T(8,128)(2,1)S(1)}, u32[]{:S(2)}, u32[]{:S(2)}) collective-permute-start(bf16[256,128]{1,0:T(8,128)(2,1)S(1)} %get-tuple-element.19), channel_id=1, source_target_pairs={{0,3},{1,2},{2,1},{3,0},{4,7},{5,6},{6,5},{7,4},{8,11},{9,10},{10,... | collective-permute-start | bytes 196616 | tf_op jit(solution)/shard_map/ppermute | solution.py:43
  11.7 5.0 %copy-start.1 = (bf16[128,256]{1,0:T(8,128)(2,1)S(1)}, bf16[128,256]{1,0:T(8,128)(2,1)}, u32[]{:S(2)}) copy-start(bf16[128,256]{1,0:T(8,128)(2,1)} %refs_5_.1) | copy-start | bytes 196612
  11.7 5.0 %copy-start.2 = (bf16[128,256]{1,0:T(8,128)(2,1)S(1)}, bf16[128,256]{1,0:T(8,128)(2,1)}, u32[]{:S(2)}) copy-start(bf16[128,256]{1,0:T(8,128)(2,1)} %refs_6_.1) | copy-start | bytes 196612
  11.7 5.0 %collective-permute-start.5 = (bf16[256,128]{1,0:T(8,128)(2,1)S(1)}, bf16[256,128]{1,0:T(8,128)(2,1)S(1)}, u32[]{:S(2)}, u32[]{:S(2)}) collective-permute-start(bf16[256,128]{1,0:T(8,128)(2,1)S(1)} %get-tuple-element.20), channel_id=1, source_target_pairs={{0,2},{1,0},{2,3},{3,1},{4,6},{5,4},{6,7},{7,5},{8,10},{9,8},{10,1... | collective-permute-start | bytes 196616 | tf_op jit(solution)/shard_map/ppermute | solution.py:43
  17.2 5.4 %collective-permute-start.7 = (bf16[384,128]{1,0:T(8,128)(2,1)S(1)}, bf16[384,128]{1,0:T(8,128)(2,1)S(1)}, u32[]{:S(2)}, u32[]{:S(2)}) collective-permute-start(bf16[384,128]{1,0:T(8,128)(2,1)S(1)} %get-tuple-element.22.message.refs_0_), channel_id=1, source_target_pairs={{0,1},{1,0},{2,3},{3,2},{4,5},{5,4},{6,7},{7,6},{8,9},{9,8},{10,11... | collective-permute-start | bytes 294920 | tf_op jit(solution)/shard_map/ppermute | solution.py:58
  19.0 3.5 %collective-permute-start.9 = (bf16[128,128]{1,0:T(8,128)(2,1)S(1)}, bf16[128,128]{1,0:T(8,128)(2,1)S(1)}, u32[]{:S(2)}, u32[]{:S(2)}) collective-permute-start(bf16[128,128]{1,0:T(8,128)(2,1)S(1)} %get-tuple-element.23), channel_id=1, source_target_pairs={{0,5},{1,4},{2,7},{3,6},{4,1},{5,0},{6,3},{7,2},{8,13},{9,12},{10,... | collective-permute-start | bytes 98312 | tf_op jit(solution)/shard_map/ppermute | solution.py:319
  19.0 3.5 %collective-permute-start.8 = (bf16[128,128]{1,0:T(8,128)(2,1)S(1)}, bf16[128,128]{1,0:T(8,128)(2,1)S(1)}, u32[]{:S(2)}, u32[]{:S(2)}) collective-permute-start(bf16[128,128]{1,0:T(8,128)(2,1)S(1)} %get-tuple-element.23), channel_id=1, source_target_pairs={{0,4},{4,0},{8,12},{12,8},{1,5},{5,1},{9,13},{13,9},{2,6},{6,2},{1... | collective-permute-start | bytes 98312 | tf_op jit(solution)/shard_map/ppermute | solution.py:58
  22.8 3.8 %collective-permute-start.10 = (bf16[256,128]{1,0:T(8,128)(2,1)S(1)}, bf16[256,128]{1,0:T(8,128)(2,1)S(1)}, u32[]{:S(2)}, u32[]{:S(2)}) collective-permute-start(bf16[256,128]{1,0:T(8,128)(2,1)S(1)} %get-tuple-element.26), channel_id=1, source_target_pairs={{0,4},{1,13},{2,6},{3,15},{4,8},{5,1},{6,10},{7,3},{8,12},{9,5},{1... | collective-permute-start | bytes 196616 | tf_op jit(solution)/shard_map/ppermute | solution.py:348
  22.9 4.5 %collective-permute-start.11 = (bf16[256,128]{1,0:T(8,128)(2,1)S(1)}, bf16[256,128]{1,0:T(8,128)(2,1)S(1)}, u32[]{:S(2)}, u32[]{:S(2)}) collective-permute-start(bf16[256,128]{1,0:T(8,128)(2,1)S(1)} %get-tuple-element.27), channel_id=1, source_target_pairs={{0,8},{1,9},{2,10},{3,11},{4,12},{5,13},{6,14},{7,15},{8,0},{9,1},... | collective-permute-start | bytes 196616 | tf_op jit(solution)/shard_map/ppermute | solution.py:348
  24.6 3.3 %collective-permute-start.12 = (bf16[256,128]{1,0:T(8,128)(2,1)S(1)}, bf16[256,128]{1,0:T(8,128)(2,1)S(1)}, u32[]{:S(2)}, u32[]{:S(2)}) collective-permute-start(bf16[256,128]{1,0:T(8,128)(2,1)S(1)} %get-tuple-element.28), channel_id=1, source_target_pairs={{0,12},{1,5},{2,14},{3,7},{4,0},{5,9},{6,2},{7,11},{8,4},{9,13},{1... | collective-permute-start | bytes 196616 | tf_op jit(solution)/shard_map/ppermute | solution.py:348

commit v28 on v24

--- a/solution.py
+++ b/solution.py
@@ -138,14 +138,18 @@
 
 
 def layer(total, weight, cotangent):
+    nodes = total.shape[0]
     high, low = split(total)
-    pre = dot(high, weight) + dot(low, weight)
+    pre = dot(jnp.concatenate([high, low], axis=0), weight)
+    pre = pre[:nodes] + pre[nodes:]
     sigma = jax.nn.sigmoid(pre)
     grad = wide(cotangent) * sigma * (1.0 + pre * (1.0 - sigma))
     grad_high, grad_low = split(grad)
     across, down = ((1,), (1,)), ((0,), (0,))
-    back = dot(grad_high, weight, across) + dot(grad_low, weight, across)
-    term = dot(high, grad_high, down) + dot(low, grad_high, down) + dot(high, grad_low, down)
+    back = dot(jnp.concatenate([grad_high, grad_low], axis=0), weight, across)
+    back = back[:nodes] + back[nodes:]
+    left = jnp.concatenate([high, low, high], axis=0)
+    term = dot(left, jnp.concatenate([grad_high, grad_high, grad_low], axis=0), down)
     return pre, back, term
 
 

time: 28.9 us -> 28.9 us (level)
  transfers between devices with their start and end apart: 13 -> 13, of which waited for: 6 -> 7; matrix products, arithmetic and copies ran while one was open for 0% -> 0% of each run, Pallas kernels for 8% -> 8%
where the time goes in v28:
time: 28.9 us; the launch traced here: 28.5 us
  starting transfers between devices  16.1 us (56%)
  waiting for transfers between devices  7.25 us (25%)
  Pallas kernels  3.66 us (13%)
  between operations  1.45 us (5%)
    ppermute x6, starting transfers between devices, swap(): return lax.ppermute(value, axis, [(s, s ^ distance) for s in range(n)])  8.17 us
    ppermute x6, starting transfers between devices, exchange(): lax.ppermute(send, axis, [(s, target(s, d)) for s in range(n)])  7.95 us
    ppermute x6, waiting for transfers between devices, exchange(): lax.ppermute(send, axis, [(s, target(s, d)) for s in range(n)])  4.27 us
    ppermute x1, waiting for transfers between devices, per_device(): lax.ppermute(other, ('row', 'col'), corner)  2.96 us
    pallas_call x1, Pallas kernels, per_device(): call(functools.partial(last_kernel, scale), [((nodes, width), NARROW), ((...  0.69 us
    pallas_call x1, Pallas kernels, per_device(): call(functools.partial(dense_kernel, nodes // side, paired), [((down, acr...  0.68 us
    pallas_call x1, Pallas kernels, per_device(): act, = call(act_kernel, [((nodes, hidden), NARROW)], [VMEM])(pre)  0.65 us
  transfers between devices with their start and end apart: 13, of which 7 were waited for; matrix products, arithmetic and copies ran while one was open for 0% of the time, Pallas kernels for 8%

profile of v28, /device:TPU:0, one launch (start us, length us, event | category | flops | bytes accessed | tf_op | source)
XLA Modules:
  0.0 28.5 jit_solution(2026760359078607590)
XLA Ops:
  0.6 0.0 copy-start
  0.6 2.4 %collective-permute-start.1 = (bf16[128,128]{1,0:T(8,128)(2,1)}, bf16[128,128]{1,0:T(8,128)(2,1)S(1)}, u32[]{:S(2)}, u32[]{:S(2)}) collective-permute-start(bf16[128,128]{1,0:T(8,128)(2,1)} %refs_0_.1), channel_id=1, source_target_pairs={{0,12},{4,8},{8,4},{12,0},{1,13},{5,9},{9,5},{13,1},{2,14},{6,10},... | collective-permute-start | bytes 98312 | tf_op jit(solution)/shard_map/ppermute | solution.py:58
  3.1 0.6 %collective-permute-start = (bf16[128,128]{1,0:T(8,128)(2,1)}, bf16[128,128]{1,0:T(8,128)(2,1)S(1)}, u32[]{:S(2)}, u32[]{:S(2)}) collective-permute-start(bf16[128,128]{1,0:T(8,128)(2,1)} %refs_0_.1), channel_id=1, source_target_pairs={{0,8},{4,12},{8,0},{12,4},{1,9},{5,13},{9,1},{13,5},{2,10},{6,14},... | collective-permute-start | bytes 98312 | tf_op jit(solution)/shard_map/ppermute | solution.py:58
  3.7 0.0 collective-permute-start.2
  3.8 2.8 %collective-permute-start.6 = (bf16[128,256]{1,0:T(8,128)(2,1)}, bf16[128,256]{1,0:T(8,128)(2,1)S(1)}, u32[]{:S(2)}, u32[]{:S(2)}) collective-permute-start(bf16[128,256]{1,0:T(8,128)(2,1)} %refs_6_.1), channel_id=1, source_target_pairs={{0,2},{1,3},{2,0},{3,1},{4,6},{5,7},{6,4},{7,5},{8,10},{9,11},{10,... | collective-permute-start | bytes 196616 | tf_op jit(solution)/shard_map/ppermute | solution.py:58
  6.6 0.0 copy-start.4
  6.7 0.0 copy-start.5
  7.3 0.0 copy-done
  7.3 0.0 copy-done.4
  7.3 0.0 copy-done.5
  7.4 0.0 copy-start.3
  7.4 0.7 %shard_map.95.near.matrix = bf16[512,512]{1,0:T(8,128)(2,1)S(1)} custom-call(bf16[512,512]{1,0:T(8,128)(2,1)S(1)} %shard_map.94.blank, bf16[1,1,8,128,128]{4,3,2,1,0:T(8,128)(2,1)S(1)} %copy-done, s32[1,1,8]{2,1,0:T(1,128)S(1)} %copy-done.4, s32[1,1,8]{2,1,0:T(1,128)S(1)} %copy-done.5, s32[1,1]{1,0:T(1,128)S(6)} %copy.12.count_in), custom_call_target="tpu_custom_call", output_to_operand_aliasing={{}: (0, {})} | custom-call | bytes 1048576 | tf_op jit(solution)/shard_map/pallas_call | solution.py:265
  8.1 0.0 collective-permute-done.1.refs_2_
  8.1 0.0 collective-permute-done.refs_1_
  8.1 0.0 collective-permute-done.2.refs_3_
  8.1 0.0 copy-done.3
  8.1 0.3 %shard_map.97 = (bf16[256,128]{1,0:T(8,128)(2,1)S(1)}, bf16[256,128]{1,0:T(8,128)(2,1)S(1)}, bf16[256,128]{1,0:T(8,128)(2,1)S(1)}, bf16[256,128]{1,0:T(8,128)(2,1)S(1)}) custom-call(bf16[512,512]{1,0:T(8,128)(2,1)S(1)} %shard_map.95.near.matrix, bf16[128,128]{1,0:T(8,128)(2,1)S(1)} %copy-done.3, bf16[128,128]{1,0:T(8,128)(2,1)S(1)} %collective-permute-done.refs_1_, ...), custom_call_target="tpu_custom_call" | custom-call | flops 67108864 | bytes 1048576 | tf_op jit(solution)/shard_map/pallas_call | solution.py:282
  8.4 1.6 %collective-permute-start.3 = (bf16[256,128]{1,0:T(8,128)(2,1)S(1)}, bf16[256,128]{1,0:T(8,128)(2,1)S(1)}, u32[]{:S(2)}, u32[]{:S(2)}) collective-permute-start(bf16[256,128]{1,0:T(8,128)(2,1)S(1)} %get-tuple-element.18), channel_id=1, source_target_pairs={{0,1},{1,3},{2,0},{3,2},{4,5},{5,7},{6,4},{7,6},{8,9},{9,11},{10,8... | collective-permute-start | bytes 196616 | tf_op jit(solution)/shard_map/ppermute | solution.py:43
  10.1 1.6 %collective-permute-start.4 = (bf16[256,128]{1,0:T(8,128)(2,1)S(1)}, bf16[256,128]{1,0:T(8,128)(2,1)S(1)}, u32[]{:S(2)}, u32[]{:S(2)}) collective-permute-start(bf16[256,128]{1,0:T(8,128)(2,1)S(1)} %get-tuple-element.19), channel_id=1, source_target_pairs={{0,3},{1,2},{2,1},{3,0},{4,7},{5,6},{6,5},{7,4},{8,11},{9,10},{10,... | collective-permute-start | bytes 196616 | tf_op jit(solution)/shard_map/ppermute | solution.py:43
  11.7 0.0 copy-start.1
  11.7 0.0 copy-start.2
  11.7 1.6 %collective-permute-start.5 = (bf16[256,128]{1,0:T(8,128)(2,1)S(1)}, bf16[256,128]{1,0:T(8,128)(2,1)S(1)}, u32[]{:S(2)}, u32[]{:S(2)}) collective-permute-start(bf16[256,128]{1,0:T(8,128)(2,1)S(1)} %get-tuple-element.20), channel_id=1, source_target_pairs={{0,2},{1,0},{2,3},{3,1},{4,6},{5,4},{6,7},{7,5},{8,10},{9,8},{10,1... | collective-permute-start | bytes 196616 | tf_op jit(solution)/shard_map/ppermute | solution.py:43
  13.3 0.3 %shard_map.96.refs_0_.matrix = bf16[512,512]{1,0:T(8,128)(2,1)S(1)} custom-call(bf16[512,512]{1,0:T(8,128)(2,1)S(1)} %shard_map.95.near.matrix), custom_call_target="tpu_custom_call" | custom-call | bytes 1572864 | tf_op jit(solution)/shard_map/pallas_call | solution.py:299
  13.6 0.0 collective-permute-done.6.refs_7_
  13.6 0.4 %collective-permute-done.3.refs_2_ = bf16[256,128]{1,0:T(8,128)(2,1)S(1)} collective-permute-done((bf16[256,128]{1,0:T(8,128)(2,1)S(1)}, bf16[256,128]{1,0:T(8,128)(2,1)S(1)}, u32[]{:S(2)}, u32[]{:S(2)}) %collective-permute-start.3) | collective-permute-done | bytes 65568 | tf_op jit(solution)/shard_map/ppermute | solution.py:43
  14.0 2.4 %collective-permute-done.4.refs_3_ = bf16[256,128]{1,0:T(8,128)(2,1)S(1)} collective-permute-done((bf16[256,128]{1,0:T(8,128)(2,1)S(1)}, bf16[256,128]{1,0:T(8,128)(2,1)S(1)}, u32[]{:S(2)}, u32[]{:S(2)}) %collective-permute-start.4) | collective-permute-done | bytes 65568 | tf_op jit(solution)/shard_map/ppermute | solution.py:43
  16.4 0.2 collective-permute-done.5.refs_4_
  16.6 0.0 copy-done.1
  16.6 0.0 copy-done.2
  16.7 0.5 %shard_map.98 = (bf16[384,128]{1,0:T(8,128)(2,1)S(1)}, bf16[128,128]{1,0:T(8,128)(2,1)S(1)}, f32[128,256]{1,0:T(8,128)S(1)}) custom-call(bf16[512,512]{1,0:T(8,128)(2,1)S(1)} %shard_map.96.refs_0_.matrix, bf16[256,128]{1,0:T(8,128)(2,1)S(1)} %get-tuple-element.17.refs_1_, bf16[256,128]{1,0:T(8,128)(2,1)S(1)} %collective-permute-done.3.refs_2_, ...), custom_call_target="tpu_custom_call" | custom-call | flops 117440512 | tf_op jit(solution)/shard_map/pallas_call | solution.py:309
  17.2 1.8 %collective-permute-start.7 = (bf16[384,128]{1,0:T(8,128)(2,1)S(1)}, bf16[384,128]{1,0:T(8,128)(2,1)S(1)}, u32[]{:S(2)}, u32[]{:S(2)}) collective-permute-start(bf16[384,128]{1,0:T(8,128)(2,1)S(1)} %get-tuple-element.22.message.refs_0_), channel_id=1, source_target_pairs={{0,1},{1,0},{2,3},{3,2},{4,5},{5,4},{6,7},{7,6},{8,9},{9,8},{10,11... | collective-permute-start | bytes 294920 | tf_op jit(solution)/shard_map/ppermute | solution.py:58
  19.0 0.0 collective-permute-start.9
  19.0 0.4 %collective-permute-start.8 = (bf16[128,128]{1,0:T(8,128)(2,1)S(1)}, bf16[128,128]{1,0:T(8,128)(2,1)S(1)}, u32[]{:S(2)}, u32[]{:S(2)}) collective-permute-start(bf16[128,128]{1,0:T(8,128)(2,1)S(1)} %get-tuple-element.23), channel_id=1, source_target_pairs={{0,4},{4,0},{8,12},{12,8},{1,5},{5,1},{9,13},{13,9},{2,6},{6,2},{1... | collective-permute-start | bytes 98312 | tf_op jit(solution)/shard_map/ppermute | solution.py:58
  19.4 0.2 shard_map.100.begun
  19.6 3.0 %collective-permute-done.9.refs_3_ = bf16[128,128]{1,0:T(8,128)(2,1)S(1)} collective-permute-done((bf16[128,128]{1,0:T(8,128)(2,1)S(1)}, bf16[128,128]{1,0:T(8,128)(2,1)S(1)}, u32[]{:S(2)}, u32[]{:S(2)}) %collective-permute-start.9) | collective-permute-done | bytes 32800 | tf_op jit(solution)/shard_map/ppermute | solution.py:321
  22.6 0.0 collective-permute-done.8.refs_2_
  22.6 0.0 collective-permute-done.7.refs_1_
  22.6 0.2 shard_map.101
  22.8 0.1 collective-permute-start.10
  22.9 1.7 %collective-permute-start.11 = (bf16[256,128]{1,0:T(8,128)(2,1)S(1)}, bf16[256,128]{1,0:T(8,128)(2,1)S(1)}, u32[]{:S(2)}, u32[]{:S(2)}) collective-permute-start(bf16[256,128]{1,0:T(8,128)(2,1)S(1)} %get-tuple-element.27), channel_id=1, source_target_pairs={{0,8},{4,12},{8,0},{12,4},{1,9},{5,13},{9,1},{13,5},{2,10},{6,14},... | collective-permute-start | bytes 196616 | tf_op jit(solution)/shard_map/ppermute | solution.py:43
  24.6 1.3 %collective-permute-start.12 = (bf16[256,128]{1,0:T(8,128)(2,1)S(1)}, bf16[256,128]{1,0:T(8,128)(2,1)S(1)}, u32[]{:S(2)}, u32[]{:S(2)}) collective-permute-start(bf16[256,128]{1,0:T(8,128)(2,1)S(1)} %get-tuple-element.28), channel_id=1, source_target_pairs={{0,12},{4,0},{8,4},{12,8},{1,13},{5,1},{9,5},{13,9},{2,14},{6,2},{... | collective-permute-start | bytes 196616 | tf_op jit(solution)/shard_map/ppermute | solution.py:43
  25.9 0.7 %shard_map.99 = bf16[128,256]{1,0:T(8,128)(2,1)} custom-call(f32[128,256]{1,0:T(8,128)S(1)} %get-tuple-element.21.pre), custom_call_target="tpu_custom_call" | custom-call | tf_op jit(solution)/shard_map/pallas_call | solution.py:326
  26.6 0.1 collective-permute-done.10.refs_0_
  26.6 0.7 %collective-permute-done.11.refs_1_ = bf16[256,128]{1,0:T(8,128)(2,1)S(1)} collective-permute-done((bf16[256,128]{1,0:T(8,128)(2,1)S(1)}, bf16[256,128]{1,0:T(8,128)(2,1)S(1)}, u32[]{:S(2)}, u32[]{:S(2)}) %collective-permute-start.11) | collective-permute-done | bytes 65568 | tf_op jit(solution)/shard_map/ppermute | solution.py:43
  27.4 0.5 %collective-permute-done.12.refs_2_ = bf16[256,128]{1,0:T(8,128)(2,1)S(1)} collective-permute-done((bf16[256,128]{1,0:T(8,128)(2,1)S(1)}, bf16[256,128]{1,0:T(8,128)(2,1)S(1)}, u32[]{:S(2)}, u32[]{:S(2)}) %collective-permute-start.12) | collective-permute-done | bytes 65568 | tf_op jit(solution)/shard_map/ppermute | solution.py:43
  27.8 0.7 %shard_map.102 = (bf16[128,128]{1,0:T(8,128)(2,1)}, f32[128,256]{1,0:T(8,128)}) custom-call(f32[128,128]{1,0:T(8,128)S(1)} %get-tuple-element.24.own, bf16[128,128]{1,0:T(8,128)(2,1)S(1)} %get-tuple-element.25.kept, bf16[256,128]{1,0:T(8,128)(2,1)S(1)} %collective-permute-done.10.refs_0_, bf16[256,128]{1,0:T(8,128)(2,1)S(1)} %collective-permute-done.11.refs_1_, ...), custom_call_target="tpu_custom_call" | custom-call | tf_op jit(solution)/shard_map/pallas_call | solution.py:346
  (1 shorter events, 0.0 us)
Async XLA Ops:
  0.6 6.7 %copy-start = (bf16[1,1,8,128,128]{4,3,2,1,0:T(8,128)(2,1)S(1)}, bf16[1,1,8,128,128]{4,3,2,1,0:T(8,128)(2,1)}, u32[]{:S(2)}) copy-start(bf16[1,1,8,128,128]{4,3,2,1,0:T(8,128)(2,1)} %vals.1) | copy-start | bytes 786436
  0.6 7.4 %collective-permute-start.1 = (bf16[128,128]{1,0:T(8,128)(2,1)}, bf16[128,128]{1,0:T(8,128)(2,1)S(1)}, u32[]{:S(2)}, u32[]{:S(2)}) collective-permute-start(bf16[128,128]{1,0:T(8,128)(2,1)} %refs_0_.1), channel_id=1, source_target_pairs={{0,12},{4,8},{8,4},{12,0},{1,13},{5,9},{9,5},{13,1},{2,14},{6,10},... | collective-permute-start | bytes 98312 | tf_op jit(solution)/shard_map/ppermute | solution.py:58
  3.1 5.0 %collective-permute-start = (bf16[128,128]{1,0:T(8,128)(2,1)}, bf16[128,128]{1,0:T(8,128)(2,1)S(1)}, u32[]{:S(2)}, u32[]{:S(2)}) collective-permute-start(bf16[128,128]{1,0:T(8,128)(2,1)} %refs_0_.1), channel_id=1, source_target_pairs={{0,8},{4,12},{8,0},{12,4},{1,9},{5,13},{9,1},{13,5},{2,10},{6,14},... | collective-permute-start | bytes 98312 | tf_op jit(solution)/shard_map/ppermute | solution.py:58
  3.7 4.4 %collective-permute-start.2 = (bf16[128,128]{1,0:T(8,128)(2,1)}, bf16[128,128]{1,0:T(8,128)(2,1)S(1)}, u32[]{:S(2)}, u32[]{:S(2)}) collective-permute-start(bf16[128,128]{1,0:T(8,128)(2,1)} %refs_0_.1), channel_id=1, source_target_pairs={{0,4},{4,0},{8,12},{12,8},{1,5},{5,1},{9,13},{13,9},{2,6},{6,2},{1... | collective-permute-start | bytes 98312 | tf_op jit(solution)/shard_map/ppermute | solution.py:58
  3.8 9.9 %collective-permute-start.6 = (bf16[128,256]{1,0:T(8,128)(2,1)}, bf16[128,256]{1,0:T(8,128)(2,1)S(1)}, u32[]{:S(2)}, u32[]{:S(2)}) collective-permute-start(bf16[128,256]{1,0:T(8,128)(2,1)} %refs_6_.1), channel_id=1, source_target_pairs={{0,2},{1,3},{2,0},{3,1},{4,6},{5,7},{6,4},{7,5},{8,10},{9,11},{10,... | collective-permute-start | bytes 196616 | tf_op jit(solution)/shard_map/ppermute | solution.py:58
  6.6 0.7 %copy-start.4 = (s32[1,1,8]{2,1,0:T(1,128)S(1)}, s32[1,1,8]{2,1,0:T(1,128)}, u32[]{:S(2)}) copy-start(s32[1,1,8]{2,1,0:T(1,128)} %rows_in.1) | copy-start | bytes 100
  6.7 0.7 %copy-start.5 = (s32[1,1,8]{2,1,0:T(1,128)S(1)}, s32[1,1,8]{2,1,0:T(1,128)}, u32[]{:S(2)}) copy-start(s32[1,1,8]{2,1,0:T(1,128)} %cols_in.1) | copy-start | bytes 100
  7.4 0.8 %copy-start.3 = (bf16[128,128]{1,0:T(8,128)(2,1)S(1)}, bf16[128,128]{1,0:T(8,128)(2,1)}, u32[]{:S(2)}) copy-start(bf16[128,128]{1,0:T(8,128)(2,1)} %refs_0_.1) | copy-start | bytes 98308
  8.4 5.6 %collective-permute-start.3 = (bf16[256,128]{1,0:T(8,128)(2,1)S(1)}, bf16[256,128]{1,0:T(8,128)(2,1)S(1)}, u32[]{:S(2)}, u32[]{:S(2)}) collective-permute-start(bf16[256,128]{1,0:T(8,128)(2,1)S(1)} %get-tuple-element.18), channel_id=1, source_target_pairs={{0,1},{1,3},{2,0},{3,2},{4,5},{5,7},{6,4},{7,6},{8,9},{9,11},{10,8... | collective-permute-start | bytes 196616 | tf_op jit(solution)/shard_map/ppermute | solution.py:43
  10.1 6.4 %collective-permute-start.4 = (bf16[256,128]{1,0:T(8,128)(2,1)S(1)}, bf16[256,128]{1,0:T(8,128)(2,1)S(1)}, u32[]{:S(2)}, u32[]{:S(2)}) collective-permute-start(bf16[256,128]{1,0:T(8,128)(2,1)S(1)} %get-tuple-element.19), channel_id=1, source_target_pairs={{0,3},{1,2},{2,1},{3,0},{4,7},{5,6},{6,5},{7,4},{8,11},{9,10},{10,... | collective-permute-start | bytes 196616 | tf_op jit(solution)/shard_map/ppermute | solution.py:43
  11.7 5.0 %copy-start.1 = (bf16[128,256]{1,0:T(8,128)(2,1)S(1)}, bf16[128,256]{1,0:T(8,128)(2,1)}, u32[]{:S(2)}) copy-start(bf16[128,256]{1,0:T(8,128)(2,1)} %refs_5_.1) | copy-start | bytes 196612
  11.7 5.0 %copy-start.2 = (bf16[128,256]{1,0:T(8,128)(2,1)S(1)}, bf16[128,256]{1,0:T(8,128)(2,1)}, u32[]{:S(2)}) copy-start(bf16[128,256]{1,0:T(8,128)(2,1)} %refs_6_.1) | copy-start | bytes 196612
  11.7 5.0 %collective-permute-start.5 = (bf16[256,128]{1,0:T(8,128)(2,1)S(1)}, bf16[256,128]{1,0:T(8,128)(2,1)S(1)}, u32[]{:S(2)}, u32[]{:S(2)}) collective-permute-start(bf16[256,128]{1,0:T(8,128)(2,1)S(1)} %get-tuple-element.20), channel_id=1, source_target_pairs={{0,2},{1,0},{2,3},{3,1},{4,6},{5,4},{6,7},{7,5},{8,10},{9,8},{10,1... | collective-permute-start | bytes 196616 | tf_op jit(solution)/shard_map/ppermute | solution.py:43
  17.2 5.4 %collective-permute-start.7 = (bf16[384,128]{1,0:T(8,128)(2,1)S(1)}, bf16[384,128]{1,0:T(8,128)(2,1)S(1)}, u32[]{:S(2)}, u32[]{:S(2)}) collective-permute-start(bf16[384,128]{1,0:T(8,128)(2,1)S(1)} %get-tuple-element.22.message.refs_0_), channel_id=1, source_target_pairs={{0,1},{1,0},{2,3},{3,2},{4,5},{5,4},{6,7},{7,6},{8,9},{9,8},{10,11... | collective-permute-start | bytes 294920 | tf_op jit(solution)/shard_map/ppermute | solution.py:58
  19.0 3.5 %collective-permute-start.9 = (bf16[128,128]{1,0:T(8,128)(2,1)S(1)}, bf16[128,128]{1,0:T(8,128)(2,1)S(1)}, u32[]{:S(2)}, u32[]{:S(2)}) collective-permute-start(bf16[128,128]{1,0:T(8,128)(2,1)S(1)} %get-tuple-element.23), channel_id=1, source_target_pairs={{0,5},{1,4},{2,7},{3,6},{4,1},{5,0},{6,3},{7,2},{8,13},{9,12},{10,... | collective-permute-start | bytes 98312 | tf_op jit(solution)/shard_map/ppermute | solution.py:321
  19.0 3.5 %collective-permute-start.8 = (bf16[128,128]{1,0:T(8,128)(2,1)S(1)}, bf16[128,128]{1,0:T(8,128)(2,1)S(1)}, u32[]{:S(2)}, u32[]{:S(2)}) collective-permute-start(bf16[128,128]{1,0:T(8,128)(2,1)S(1)} %get-tuple-element.23), channel_id=1, source_target_pairs={{0,4},{4,0},{8,12},{12,8},{1,5},{5,1},{9,13},{13,9},{2,6},{6,2},{1... | collective-permute-start | bytes 98312 | tf_op jit(solution)/shard_map/ppermute | solution.py:58
  22.8 3.8 %collective-permute-start.10 = (bf16[256,128]{1,0:T(8,128)(2,1)S(1)}, bf16[256,128]{1,0:T(8,128)(2,1)S(1)}, u32[]{:S(2)}, u32[]{:S(2)}) collective-permute-start(bf16[256,128]{1,0:T(8,128)(2,1)S(1)} %get-tuple-element.26), channel_id=1, source_target_pairs={{0,4},{4,8},{8,12},{12,0},{1,5},{5,9},{9,13},{13,1},{2,6},{6,10},{... | collective-permute-start | bytes 196616 | tf_op jit(solution)/shard_map/ppermute | solution.py:43
  22.9 4.5 %collective-permute-start.11 = (bf16[256,128]{1,0:T(8,128)(2,1)S(1)}, bf16[256,128]{1,0:T(8,128)(2,1)S(1)}, u32[]{:S(2)}, u32[]{:S(2)}) collective-permute-start(bf16[256,128]{1,0:T(8,128)(2,1)S(1)} %get-tuple-element.27), channel_id=1, source_target_pairs={{0,8},{4,12},{8,0},{12,4},{1,9},{5,13},{9,1},{13,5},{2,10},{6,14},... | collective-permute-start | bytes 196616 | tf_op jit(solution)/shard_map/ppermute | solution.py:43
  24.6 3.3 %collective-permute-start.12 = (bf16[256,128]{1,0:T(8,128)(2,1)S(1)}, bf16[256,128]{1,0:T(8,128)(2,1)S(1)}, u32[]{:S(2)}, u32[]{:S(2)}) collective-permute-start(bf16[256,128]{1,0:T(8,128)(2,1)S(1)} %get-tuple-element.28), channel_id=1, source_target_pairs={{0,12},{4,0},{8,4},{12,8},{1,13},{5,1},{9,5},{13,9},{2,14},{6,2},{... | collective-permute-start | bytes 196616 | tf_op jit(solution)/shard_map/ppermute | solution.py:43

commit v29 on v28

--- a/solution.py
+++ b/solution.py
@@ -13,7 +13,7 @@
 NARROW = jnp.bfloat16
 
 
-def call(kernel, outs, in_specs, scratch=(), flops=0, need=0, after=(), aliases=None):
+def call(kernel, outs, in_specs, scratch=(), flops=0, need=0, after=()):
     outs = tuple(jax.ShapeDtypeStruct(shape, dtype) for shape, dtype in outs)
     late = len(after)
     run = pl.pallas_call(
@@ -21,7 +21,6 @@
         out_shape=outs,
         in_specs=[ANY] * late + list(in_specs),
         out_specs=(VMEM,) * len(outs),
-        input_output_aliases=aliases or {},
         scratch_shapes=scratch,
         compiler_params=pltpu.CompilerParams(vmem_limit_bytes=LEAST + need),
         cost_estimate=pl.CostEstimate(flops=flops, bytes_accessed=need, transcendentals=0),
@@ -83,6 +82,7 @@
     for copy in copies:
         copy.start()
     side = vals.shape[-1]
+    near[...] = blank[...]
     for copy in copies:
         copy.wait()
 
@@ -266,7 +266,6 @@
         functools.partial(dense_kernel, nodes // side, paired),
         [((down, across), NARROW)],
         [VMEM] * 5,
-        aliases={0: 0},
         scratch=[
             pltpu.SMEM(tile_rows.shape, jnp.int32),
             pltpu.SMEM(tile_cols.shape, jnp.int32),

time: 28.9 us -> 28.9 us (level)
  no operation moved by 1% of the time
where the time goes in v29:
time: 28.9 us; the launch traced here: 28.5 us
  starting transfers between devices  16.1 us (56%)
  waiting for transfers between devices  7.25 us (25%)
  Pallas kernels  3.64 us (13%)
  between operations  1.45 us (5%)
    ppermute x6, starting transfers between devices, swap(): return lax.ppermute(value, axis, [(s, s ^ distance) for s in range(n)])  8.17 us
    ppermute x6, starting transfers between devices, exchange(): lax.ppermute(send, axis, [(s, target(s, d)) for s in range(n)])  7.95 us
    ppermute x6, waiting for transfers between devices, exchange(): lax.ppermute(send, axis, [(s, target(s, d)) for s in range(n)])  4.27 us
    ppermute x1, waiting for transfers between devices, per_device(): lax.ppermute(other, ('row', 'col'), corner)  2.96 us
    pallas_call x1, Pallas kernels, per_device(): call(functools.partial(last_kernel, scale), [((nodes, width), NARROW), ((...  0.69 us
    pallas_call x1, Pallas kernels, per_device(): call(functools.partial(dense_kernel, nodes // side, paired), [((down, acr...  0.66 us
    pallas_call x1, Pallas kernels, per_device(): act, = call(act_kernel, [((nodes, hidden), NARROW)], [VMEM])(pre)  0.65 us
  transfers between devices with their start and end apart: 13, of which 7 were waited for; matrix products, arithmetic and copies ran while one was open for 0% of the time, Pallas kernels for 8%

profile of v29, /device:TPU:0, one launch (start us, length us, event | category | flops | bytes accessed | tf_op | source)
XLA Modules:
  0.0 28.5 jit_solution(17529225645534665381)
XLA Ops:
  0.6 0.0 copy-start
  0.6 2.4 %collective-permute-start.1 = (bf16[128,128]{1,0:T(8,128)(2,1)}, bf16[128,128]{1,0:T(8,128)(2,1)S(1)}, u32[]{:S(2)}, u32[]{:S(2)}) collective-permute-start(bf16[128,128]{1,0:T(8,128)(2,1)} %refs_0_.1), channel_id=1, source_target_pairs={{0,12},{4,8},{8,4},{12,0},{1,13},{5,9},{9,5},{13,1},{2,14},{6,10},... | collective-permute-start | bytes 98312 | tf_op jit(solution)/shard_map/ppermute | solution.py:57
  3.1 0.6 %collective-permute-start = (bf16[128,128]{1,0:T(8,128)(2,1)}, bf16[128,128]{1,0:T(8,128)(2,1)S(1)}, u32[]{:S(2)}, u32[]{:S(2)}) collective-permute-start(bf16[128,128]{1,0:T(8,128)(2,1)} %refs_0_.1), channel_id=1, source_target_pairs={{0,8},{4,12},{8,0},{12,4},{1,9},{5,13},{9,1},{13,5},{2,10},{6,14},... | collective-permute-start | bytes 98312 | tf_op jit(solution)/shard_map/ppermute | solution.py:57
  3.7 0.0 collective-permute-start.2
  3.8 2.8 %collective-permute-start.6 = (bf16[128,256]{1,0:T(8,128)(2,1)}, bf16[128,256]{1,0:T(8,128)(2,1)S(1)}, u32[]{:S(2)}, u32[]{:S(2)}) collective-permute-start(bf16[128,256]{1,0:T(8,128)(2,1)} %refs_6_.1), channel_id=1, source_target_pairs={{0,2},{1,3},{2,0},{3,1},{4,6},{5,7},{6,4},{7,5},{8,10},{9,11},{10,... | collective-permute-start | bytes 196616 | tf_op jit(solution)/shard_map/ppermute | solution.py:57
  6.6 0.0 copy-start.4
  6.7 0.0 copy-start.5
  7.3 0.0 copy-done
  7.3 0.0 copy-done.4
  7.3 0.0 copy-done.5
  7.4 0.0 copy-start.3
  7.4 0.7 %shard_map.95.near.matrix = bf16[512,512]{1,0:T(8,128)(2,1)S(1)} custom-call(bf16[512,512]{1,0:T(8,128)(2,1)S(1)} %shard_map.94.blank, bf16[1,1,8,128,128]{4,3,2,1,0:T(8,128)(2,1)S(1)} %copy-done, s32[1,1,8]{2,1,0:T(1,128)S(1)} %copy-done.4, s32[1,1,8]{2,1,0:T(1,128)S(1)} %copy-done.5, s32[1,1]{1,0:T(1,128)S(6)} %copy.10.count_in), custom_call_target="tpu_custom_call" | custom-call | bytes 1048576 | tf_op jit(solution)/shard_map/pallas_call | solution.py:265
  8.0 0.0 collective-permute-done.1.refs_2_
  8.0 0.0 collective-permute-done.refs_1_
  8.1 0.0 collective-permute-done.2.refs_3_
  8.1 0.1 copy-done.3
  8.1 0.3 %shard_map.97 = (bf16[256,128]{1,0:T(8,128)(2,1)S(1)}, bf16[256,128]{1,0:T(8,128)(2,1)S(1)}, bf16[256,128]{1,0:T(8,128)(2,1)S(1)}, bf16[256,128]{1,0:T(8,128)(2,1)S(1)}) custom-call(bf16[512,512]{1,0:T(8,128)(2,1)S(1)} %shard_map.95.near.matrix, bf16[128,128]{1,0:T(8,128)(2,1)S(1)} %copy-done.3, bf16[128,128]{1,0:T(8,128)(2,1)S(1)} %collective-permute-done.refs_1_, ...), custom_call_target="tpu_custom_call" | custom-call | flops 67108864 | bytes 1048576 | tf_op jit(solution)/shard_map/pallas_call | solution.py:281
  8.4 1.6 %collective-permute-start.3 = (bf16[256,128]{1,0:T(8,128)(2,1)S(1)}, bf16[256,128]{1,0:T(8,128)(2,1)S(1)}, u32[]{:S(2)}, u32[]{:S(2)}) collective-permute-start(bf16[256,128]{1,0:T(8,128)(2,1)S(1)} %get-tuple-element.18), channel_id=1, source_target_pairs={{0,1},{1,3},{2,0},{3,2},{4,5},{5,7},{6,4},{7,6},{8,9},{9,11},{10,8... | collective-permute-start | bytes 196616 | tf_op jit(solution)/shard_map/ppermute | solution.py:42
  10.1 1.6 %collective-permute-start.4 = (bf16[256,128]{1,0:T(8,128)(2,1)S(1)}, bf16[256,128]{1,0:T(8,128)(2,1)S(1)}, u32[]{:S(2)}, u32[]{:S(2)}) collective-permute-start(bf16[256,128]{1,0:T(8,128)(2,1)S(1)} %get-tuple-element.19), channel_id=1, source_target_pairs={{0,3},{1,2},{2,1},{3,0},{4,7},{5,6},{6,5},{7,4},{8,11},{9,10},{10,... | collective-permute-start | bytes 196616 | tf_op jit(solution)/shard_map/ppermute | solution.py:42
  11.7 0.0 copy-start.1
  11.7 0.0 copy-start.2
  11.7 1.6 %collective-permute-start.5 = (bf16[256,128]{1,0:T(8,128)(2,1)S(1)}, bf16[256,128]{1,0:T(8,128)(2,1)S(1)}, u32[]{:S(2)}, u32[]{:S(2)}) collective-permute-start(bf16[256,128]{1,0:T(8,128)(2,1)S(1)} %get-tuple-element.20), channel_id=1, source_target_pairs={{0,2},{1,0},{2,3},{3,1},{4,6},{5,4},{6,7},{7,5},{8,10},{9,8},{10,1... | collective-permute-start | bytes 196616 | tf_op jit(solution)/shard_map/ppermute | solution.py:42
  13.3 0.3 %shard_map.96.refs_0_.matrix = bf16[512,512]{1,0:T(8,128)(2,1)S(1)} custom-call(bf16[512,512]{1,0:T(8,128)(2,1)S(1)} %shard_map.95.near.matrix), custom_call_target="tpu_custom_call" | custom-call | bytes 1572864 | tf_op jit(solution)/shard_map/pallas_call | solution.py:298
  13.6 0.0 collective-permute-done.6.refs_7_
  13.6 0.4 %collective-permute-done.3.refs_2_ = bf16[256,128]{1,0:T(8,128)(2,1)S(1)} collective-permute-done((bf16[256,128]{1,0:T(8,128)(2,1)S(1)}, bf16[256,128]{1,0:T(8,128)(2,1)S(1)}, u32[]{:S(2)}, u32[]{:S(2)}) %collective-permute-start.3) | collective-permute-done | bytes 65568 | tf_op jit(solution)/shard_map/ppermute | solution.py:42
  14.0 2.4 %collective-permute-done.4.refs_3_ = bf16[256,128]{1,0:T(8,128)(2,1)S(1)} collective-permute-done((bf16[256,128]{1,0:T(8,128)(2,1)S(1)}, bf16[256,128]{1,0:T(8,128)(2,1)S(1)}, u32[]{:S(2)}, u32[]{:S(2)}) %collective-permute-start.4) | collective-permute-done | bytes 65568 | tf_op jit(solution)/shard_map/ppermute | solution.py:42
  16.4 0.2 collective-permute-done.5.refs_4_
  16.6 0.0 copy-done.1
  16.6 0.0 copy-done.2
  16.7 0.5 %shard_map.98 = (bf16[384,128]{1,0:T(8,128)(2,1)S(1)}, bf16[128,128]{1,0:T(8,128)(2,1)S(1)}, f32[128,256]{1,0:T(8,128)S(1)}) custom-call(bf16[512,512]{1,0:T(8,128)(2,1)S(1)} %shard_map.96.refs_0_.matrix, bf16[256,128]{1,0:T(8,128)(2,1)S(1)} %get-tuple-element.17.refs_1_, bf16[256,128]{1,0:T(8,128)(2,1)S(1)} %collective-permute-done.3.refs_2_, ...), custom_call_target="tpu_custom_call" | custom-call | flops 117440512 | tf_op jit(solution)/shard_map/pallas_call | solution.py:308
  17.2 1.8 %collective-permute-start.7 = (bf16[384,128]{1,0:T(8,128)(2,1)S(1)}, bf16[384,128]{1,0:T(8,128)(2,1)S(1)}, u32[]{:S(2)}, u32[]{:S(2)}) collective-permute-start(bf16[384,128]{1,0:T(8,128)(2,1)S(1)} %get-tuple-element.22.message.refs_0_), channel_id=1, source_target_pairs={{0,1},{1,0},{2,3},{3,2},{4,5},{5,4},{6,7},{7,6},{8,9},{9,8},{10,11... | collective-permute-start | bytes 294920 | tf_op jit(solution)/shard_map/ppermute | solution.py:57
  19.0 0.0 collective-permute-start.9
  19.0 0.4 %collective-permute-start.8 = (bf16[128,128]{1,0:T(8,128)(2,1)S(1)}, bf16[128,128]{1,0:T(8,128)(2,1)S(1)}, u32[]{:S(2)}, u32[]{:S(2)}) collective-permute-start(bf16[128,128]{1,0:T(8,128)(2,1)S(1)} %get-tuple-element.23), channel_id=1, source_target_pairs={{0,4},{4,0},{8,12},{12,8},{1,5},{5,1},{9,13},{13,9},{2,6},{6,2},{1... | collective-permute-start | bytes 98312 | tf_op jit(solution)/shard_map/ppermute | solution.py:57
  19.4 0.2 shard_map.100.begun
  19.6 3.0 %collective-permute-done.9.refs_3_ = bf16[128,128]{1,0:T(8,128)(2,1)S(1)} collective-permute-done((bf16[128,128]{1,0:T(8,128)(2,1)S(1)}, bf16[128,128]{1,0:T(8,128)(2,1)S(1)}, u32[]{:S(2)}, u32[]{:S(2)}) %collective-permute-start.9) | collective-permute-done | bytes 32800 | tf_op jit(solution)/shard_map/ppermute | solution.py:320
  22.6 0.0 collective-permute-done.8.refs_2_
  22.6 0.0 collective-permute-done.7.refs_1_
  22.6 0.2 shard_map.101
  22.8 0.1 collective-permute-start.10
  22.9 1.7 %collective-permute-start.11 = (bf16[256,128]{1,0:T(8,128)(2,1)S(1)}, bf16[256,128]{1,0:T(8,128)(2,1)S(1)}, u32[]{:S(2)}, u32[]{:S(2)}) collective-permute-start(bf16[256,128]{1,0:T(8,128)(2,1)S(1)} %get-tuple-element.27), channel_id=1, source_target_pairs={{0,8},{4,12},{8,0},{12,4},{1,9},{5,13},{9,1},{13,5},{2,10},{6,14},... | collective-permute-start | bytes 196616 | tf_op jit(solution)/shard_map/ppermute | solution.py:42
  24.6 1.3 %collective-permute-start.12 = (bf16[256,128]{1,0:T(8,128)(2,1)S(1)}, bf16[256,128]{1,0:T(8,128)(2,1)S(1)}, u32[]{:S(2)}, u32[]{:S(2)}) collective-permute-start(bf16[256,128]{1,0:T(8,128)(2,1)S(1)} %get-tuple-element.28), channel_id=1, source_target_pairs={{0,12},{4,0},{8,4},{12,8},{1,13},{5,1},{9,5},{13,9},{2,14},{6,2},{... | collective-permute-start | bytes 196616 | tf_op jit(solution)/shard_map/ppermute | solution.py:42
  25.9 0.7 %shard_map.99 = bf16[128,256]{1,0:T(8,128)(2,1)} custom-call(f32[128,256]{1,0:T(8,128)S(1)} %get-tuple-element.21.pre), custom_call_target="tpu_custom_call" | custom-call | tf_op jit(solution)/shard_map/pallas_call | solution.py:325
  26.6 0.1 collective-permute-done.10.refs_0_
  26.6 0.7 %collective-permute-done.11.refs_1_ = bf16[256,128]{1,0:T(8,128)(2,1)S(1)} collective-permute-done((bf16[256,128]{1,0:T(8,128)(2,1)S(1)}, bf16[256,128]{1,0:T(8,128)(2,1)S(1)}, u32[]{:S(2)}, u32[]{:S(2)}) %collective-permute-start.11) | collective-permute-done | bytes 65568 | tf_op jit(solution)/shard_map/ppermute | solution.py:42
  27.4 0.5 %collective-permute-done.12.refs_2_ = bf16[256,128]{1,0:T(8,128)(2,1)S(1)} collective-permute-done((bf16[256,128]{1,0:T(8,128)(2,1)S(1)}, bf16[256,128]{1,0:T(8,128)(2,1)S(1)}, u32[]{:S(2)}, u32[]{:S(2)}) %collective-permute-start.12) | collective-permute-done | bytes 65568 | tf_op jit(solution)/shard_map/ppermute | solution.py:42
  27.8 0.7 %shard_map.102 = (bf16[128,128]{1,0:T(8,128)(2,1)}, f32[128,256]{1,0:T(8,128)}) custom-call(f32[128,128]{1,0:T(8,128)S(1)} %get-tuple-element.24.own, bf16[128,128]{1,0:T(8,128)(2,1)S(1)} %get-tuple-element.25.kept, bf16[256,128]{1,0:T(8,128)(2,1)S(1)} %collective-permute-done.10.refs_0_, bf16[256,128]{1,0:T(8,128)(2,1)S(1)} %collective-permute-done.11.refs_1_, ...), custom_call_target="tpu_custom_call" | custom-call | tf_op jit(solution)/shard_map/pallas_call | solution.py:345
  (1 shorter events, 0.0 us)
Async XLA Ops:
  0.6 6.7 %copy-start = (bf16[1,1,8,128,128]{4,3,2,1,0:T(8,128)(2,1)S(1)}, bf16[1,1,8,128,128]{4,3,2,1,0:T(8,128)(2,1)}, u32[]{:S(2)}) copy-start(bf16[1,1,8,128,128]{4,3,2,1,0:T(8,128)(2,1)} %vals.1) | copy-start | bytes 786436
  0.6 7.4 %collective-permute-start.1 = (bf16[128,128]{1,0:T(8,128)(2,1)}, bf16[128,128]{1,0:T(8,128)(2,1)S(1)}, u32[]{:S(2)}, u32[]{:S(2)}) collective-permute-start(bf16[128,128]{1,0:T(8,128)(2,1)} %refs_0_.1), channel_id=1, source_target_pairs={{0,12},{4,8},{8,4},{12,0},{1,13},{5,9},{9,5},{13,1},{2,14},{6,10},... | collective-permute-start | bytes 98312 | tf_op jit(solution)/shard_map/ppermute | solution.py:57
  3.1 5.0 %collective-permute-start = (bf16[128,128]{1,0:T(8,128)(2,1)}, bf16[128,128]{1,0:T(8,128)(2,1)S(1)}, u32[]{:S(2)}, u32[]{:S(2)}) collective-permute-start(bf16[128,128]{1,0:T(8,128)(2,1)} %refs_0_.1), channel_id=1, source_target_pairs={{0,8},{4,12},{8,0},{12,4},{1,9},{5,13},{9,1},{13,5},{2,10},{6,14},... | collective-permute-start | bytes 98312 | tf_op jit(solution)/shard_map/ppermute | solution.py:57
  3.7 4.3 %collective-permute-start.2 = (bf16[128,128]{1,0:T(8,128)(2,1)}, bf16[128,128]{1,0:T(8,128)(2,1)S(1)}, u32[]{:S(2)}, u32[]{:S(2)}) collective-permute-start(bf16[128,128]{1,0:T(8,128)(2,1)} %refs_0_.1), channel_id=1, source_target_pairs={{0,4},{4,0},{8,12},{12,8},{1,5},{5,1},{9,13},{13,9},{2,6},{6,2},{1... | collective-permute-start | bytes 98312 | tf_op jit(solution)/shard_map/ppermute | solution.py:57
  3.8 9.9 %collective-permute-start.6 = (bf16[128,256]{1,0:T(8,128)(2,1)}, bf16[128,256]{1,0:T(8,128)(2,1)S(1)}, u32[]{:S(2)}, u32[]{:S(2)}) collective-permute-start(bf16[128,256]{1,0:T(8,128)(2,1)} %refs_6_.1), channel_id=1, source_target_pairs={{0,2},{1,3},{2,0},{3,1},{4,6},{5,7},{6,4},{7,5},{8,10},{9,11},{10,... | collective-permute-start | bytes 196616 | tf_op jit(solution)/shard_map/ppermute | solution.py:57
  6.6 0.7 %copy-start.4 = (s32[1,1,8]{2,1,0:T(1,128)S(1)}, s32[1,1,8]{2,1,0:T(1,128)}, u32[]{:S(2)}) copy-start(s32[1,1,8]{2,1,0:T(1,128)} %rows_in.1) | copy-start | bytes 100
  6.7 0.7 %copy-start.5 = (s32[1,1,8]{2,1,0:T(1,128)S(1)}, s32[1,1,8]{2,1,0:T(1,128)}, u32[]{:S(2)}) copy-start(s32[1,1,8]{2,1,0:T(1,128)} %cols_in.1) | copy-start | bytes 100
  7.4 0.8 %copy-start.3 = (bf16[128,128]{1,0:T(8,128)(2,1)S(1)}, bf16[128,128]{1,0:T(8,128)(2,1)}, u32[]{:S(2)}) copy-start(bf16[128,128]{1,0:T(8,128)(2,1)} %refs_0_.1) | copy-start | bytes 98308
  8.4 5.6 %collective-permute-start.3 = (bf16[256,128]{1,0:T(8,128)(2,1)S(1)}, bf16[256,128]{1,0:T(8,128)(2,1)S(1)}, u32[]{:S(2)}, u32[]{:S(2)}) collective-permute-start(bf16[256,128]{1,0:T(8,128)(2,1)S(1)} %get-tuple-element.18), channel_id=1, source_target_pairs={{0,1},{1,3},{2,0},{3,2},{4,5},{5,7},{6,4},{7,6},{8,9},{9,11},{10,8... | collective-permute-start | bytes 196616 | tf_op jit(solution)/shard_map/ppermute | solution.py:42
  10.1 6.4 %collective-permute-start.4 = (bf16[256,128]{1,0:T(8,128)(2,1)S(1)}, bf16[256,128]{1,0:T(8,128)(2,1)S(1)}, u32[]{:S(2)}, u32[]{:S(2)}) collective-permute-start(bf16[256,128]{1,0:T(8,128)(2,1)S(1)} %get-tuple-element.19), channel_id=1, source_target_pairs={{0,3},{1,2},{2,1},{3,0},{4,7},{5,6},{6,5},{7,4},{8,11},{9,10},{10,... | collective-permute-start | bytes 196616 | tf_op jit(solution)/shard_map/ppermute | solution.py:42
  11.7 5.0 %copy-start.1 = (bf16[128,256]{1,0:T(8,128)(2,1)S(1)}, bf16[128,256]{1,0:T(8,128)(2,1)}, u32[]{:S(2)}) copy-start(bf16[128,256]{1,0:T(8,128)(2,1)} %refs_5_.1) | copy-start | bytes 196612
  11.7 5.0 %copy-start.2 = (bf16[128,256]{1,0:T(8,128)(2,1)S(1)}, bf16[128,256]{1,0:T(8,128)(2,1)}, u32[]{:S(2)}) copy-start(bf16[128,256]{1,0:T(8,128)(2,1)} %refs_6_.1) | copy-start | bytes 196612
  11.7 5.0 %collective-permute-start.5 = (bf16[256,128]{1,0:T(8,128)(2,1)S(1)}, bf16[256,128]{1,0:T(8,128)(2,1)S(1)}, u32[]{:S(2)}, u32[]{:S(2)}) collective-permute-start(bf16[256,128]{1,0:T(8,128)(2,1)S(1)} %get-tuple-element.20), channel_id=1, source_target_pairs={{0,2},{1,0},{2,3},{3,1},{4,6},{5,4},{6,7},{7,5},{8,10},{9,8},{10,1... | collective-permute-start | bytes 196616 | tf_op jit(solution)/shard_map/ppermute | solution.py:42
  17.2 5.4 %collective-permute-start.7 = (bf16[384,128]{1,0:T(8,128)(2,1)S(1)}, bf16[384,128]{1,0:T(8,128)(2,1)S(1)}, u32[]{:S(2)}, u32[]{:S(2)}) collective-permute-start(bf16[384,128]{1,0:T(8,128)(2,1)S(1)} %get-tuple-element.22.message.refs_0_), channel_id=1, source_target_pairs={{0,1},{1,0},{2,3},{3,2},{4,5},{5,4},{6,7},{7,6},{8,9},{9,8},{10,11... | collective-permute-start | bytes 294920 | tf_op jit(solution)/shard_map/ppermute | solution.py:57
  19.0 3.5 %collective-permute-start.9 = (bf16[128,128]{1,0:T(8,128)(2,1)S(1)}, bf16[128,128]{1,0:T(8,128)(2,1)S(1)}, u32[]{:S(2)}, u32[]{:S(2)}) collective-permute-start(bf16[128,128]{1,0:T(8,128)(2,1)S(1)} %get-tuple-element.23), channel_id=1, source_target_pairs={{0,5},{1,4},{2,7},{3,6},{4,1},{5,0},{6,3},{7,2},{8,13},{9,12},{10,... | collective-permute-start | bytes 98312 | tf_op jit(solution)/shard_map/ppermute | solution.py:320
  19.0 3.5 %collective-permute-start.8 = (bf16[128,128]{1,0:T(8,128)(2,1)S(1)}, bf16[128,128]{1,0:T(8,128)(2,1)S(1)}, u32[]{:S(2)}, u32[]{:S(2)}) collective-permute-start(bf16[128,128]{1,0:T(8,128)(2,1)S(1)} %get-tuple-element.23), channel_id=1, source_target_pairs={{0,4},{4,0},{8,12},{12,8},{1,5},{5,1},{9,13},{13,9},{2,6},{6,2},{1... | collective-permute-start | bytes 98312 | tf_op jit(solution)/shard_map/ppermute | solution.py:57
  22.8 3.8 %collective-permute-start.10 = (bf16[256,128]{1,0:T(8,128)(2,1)S(1)}, bf16[256,128]{1,0:T(8,128)(2,1)S(1)}, u32[]{:S(2)}, u32[]{:S(2)}) collective-permute-start(bf16[256,128]{1,0:T(8,128)(2,1)S(1)} %get-tuple-element.26), channel_id=1, source_target_pairs={{0,4},{4,8},{8,12},{12,0},{1,5},{5,9},{9,13},{13,1},{2,6},{6,10},{... | collective-permute-start | bytes 196616 | tf_op jit(solution)/shard_map/ppermute | solution.py:42
  22.9 4.5 %collective-permute-start.11 = (bf16[256,128]{1,0:T(8,128)(2,1)S(1)}, bf16[256,128]{1,0:T(8,128)(2,1)S(1)}, u32[]{:S(2)}, u32[]{:S(2)}) collective-permute-start(bf16[256,128]{1,0:T(8,128)(2,1)S(1)} %get-tuple-element.27), channel_id=1, source_target_pairs={{0,8},{4,12},{8,0},{12,4},{1,9},{5,13},{9,1},{13,5},{2,10},{6,14},... | collective-permute-start | bytes 196616 | tf_op jit(solution)/shard_map/ppermute | solution.py:42
  24.6 3.3 %collective-permute-start.12 = (bf16[256,128]{1,0:T(8,128)(2,1)S(1)}, bf16[256,128]{1,0:T(8,128)(2,1)S(1)}, u32[]{:S(2)}, u32[]{:S(2)}) collective-permute-start(bf16[256,128]{1,0:T(8,128)(2,1)S(1)} %get-tuple-element.28), channel_id=1, source_target_pairs={{0,12},{4,0},{8,4},{12,8},{1,13},{5,1},{9,5},{13,9},{2,14},{6,2},{... | collective-permute-start | bytes 196616 | tf_op jit(solution)/shard_map/ppermute | solution.py:42

commit v30 on v29

--- a/solution.py
+++ b/solution.py
@@ -239,7 +239,8 @@
 
 
 def last_kernel(scale, own, kept, *refs):
-    *messages, features_out, weight_out = refs
+    second, first, *messages, features_out, weight_out = refs
+    messages = [first, second, *messages]
     nodes, half = own.shape[0], kept.shape[1]
     features_out[...] = tree(
         [own[...]] + [wide(message[:nodes]) for message in messages]
@@ -346,7 +347,7 @@
         functools.partial(last_kernel, scale),
         [((nodes, width), NARROW), ((width, hidden), jnp.float32)],
         [VMEM] * (n_row + 1),
-    )(own, kept, *parts)
+    )(own, kept, parts[1], parts[0], *parts[2:])
     return act, grad_features, grad_weight
 
 

time: 28.9 us -> 29.1 us (level)
  transfers between devices with their start and end apart: 13 -> 13, of which waited for: 7 -> 6; matrix products, arithmetic and copies ran while one was open for 0% -> 0% of each run, Pallas kernels for 8% -> 8%
where the time goes in v30:
time: 29.1 us; the launch traced here: 28.9 us
  starting transfers between devices  16.3 us (56%)
  waiting for transfers between devices  7.3 us (25%)
  Pallas kernels  3.76 us (13%)
  between operations  1.45 us (5%)
    ppermute x6, starting transfers between devices, swap(): return lax.ppermute(value, axis, [(s, s ^ distance) for s in range(n)])  8.17 us
    ppermute x6, starting transfers between devices, exchange(): lax.ppermute(send, axis, [(s, target(s, d)) for s in range(n)])  8.17 us
    ppermute x6, waiting for transfers between devices, exchange(): lax.ppermute(send, axis, [(s, target(s, d)) for s in range(n)])  4.32 us
    ppermute x1, waiting for transfers between devices, per_device(): lax.ppermute(other, ('row', 'col'), corner)  2.96 us
    pallas_call x1, Pallas kernels, per_device(): call(functools.partial(dense_kernel, nodes // side, paired), [((down, acr...  0.77 us
    pallas_call x1, Pallas kernels, per_device(): call(functools.partial(last_kernel, scale), [((nodes, width), NARROW), ((...  0.7 us
    pallas_call x1, Pallas kernels, per_device(): act, = call(act_kernel, [((nodes, hidden), NARROW)], [VMEM])(pre)  0.65 us
  transfers between devices with their start and end apart: 13, of which 6 were waited for; matrix products, arithmetic and copies ran while one was open for 0% of the time, Pallas kernels for 8%

profile of v30, /device:TPU:0, one launch (start us, length us, event | category | flops | bytes accessed | tf_op | source)
XLA Modules:
  0.0 28.9 jit_solution(1284747442468301101)
XLA Ops:
  0.6 0.0 copy-start
  0.6 2.4 %collective-permute-start.1 = (bf16[128,128]{1,0:T(8,128)(2,1)}, bf16[128,128]{1,0:T(8,128)(2,1)S(1)}, u32[]{:S(2)}, u32[]{:S(2)}) collective-permute-start(bf16[128,128]{1,0:T(8,128)(2,1)} %refs_0_.1), channel_id=1, source_target_pairs={{0,12},{4,8},{8,4},{12,0},{1,13},{5,9},{9,5},{13,1},{2,14},{6,10},... | collective-permute-start | bytes 98312 | tf_op jit(solution)/shard_map/ppermute | solution.py:57
  3.1 0.6 %collective-permute-start = (bf16[128,128]{1,0:T(8,128)(2,1)}, bf16[128,128]{1,0:T(8,128)(2,1)S(1)}, u32[]{:S(2)}, u32[]{:S(2)}) collective-permute-start(bf16[128,128]{1,0:T(8,128)(2,1)} %refs_0_.1), channel_id=1, source_target_pairs={{0,8},{4,12},{8,0},{12,4},{1,9},{5,13},{9,1},{13,5},{2,10},{6,14},... | collective-permute-start | bytes 98312 | tf_op jit(solution)/shard_map/ppermute | solution.py:57
  3.7 0.0 collective-permute-start.2
  3.8 2.8 %collective-permute-start.6 = (bf16[128,256]{1,0:T(8,128)(2,1)}, bf16[128,256]{1,0:T(8,128)(2,1)S(1)}, u32[]{:S(2)}, u32[]{:S(2)}) collective-permute-start(bf16[128,256]{1,0:T(8,128)(2,1)} %refs_6_.1), channel_id=1, source_target_pairs={{0,2},{1,3},{2,0},{3,1},{4,6},{5,7},{6,4},{7,5},{8,10},{9,11},{10,... | collective-permute-start | bytes 196616 | tf_op jit(solution)/shard_map/ppermute | solution.py:57
  6.6 0.0 copy-start.4
  6.7 0.0 copy-start.5
  7.3 0.0 copy-done
  7.3 0.0 copy-done.4
  7.3 0.0 copy-done.5
  7.4 0.0 copy-start.3
  7.4 0.8 %shard_map.95.near.matrix = bf16[512,512]{1,0:T(8,128)(2,1)S(1)} custom-call(bf16[512,512]{1,0:T(8,128)(2,1)S(1)} %shard_map.94.blank, bf16[1,1,8,128,128]{4,3,2,1,0:T(8,128)(2,1)S(1)} %copy-done, s32[1,1,8]{2,1,0:T(1,128)S(1)} %copy-done.4, s32[1,1,8]{2,1,0:T(1,128)S(1)} %copy-done.5, s32[1,1]{1,0:T(1,128)S(6)} %copy.10.count_in), custom_call_target="tpu_custom_call" | custom-call | bytes 1048576 | tf_op jit(solution)/shard_map/pallas_call | solution.py:266
  8.2 0.0 collective-permute-done.1.refs_2_
  8.2 0.0 collective-permute-done.refs_1_
  8.2 0.0 collective-permute-done.2.refs_3_
  8.2 0.0 copy-done.3
  8.2 0.3 %shard_map.97 = (bf16[256,128]{1,0:T(8,128)(2,1)S(1)}, bf16[256,128]{1,0:T(8,128)(2,1)S(1)}, bf16[256,128]{1,0:T(8,128)(2,1)S(1)}, bf16[256,128]{1,0:T(8,128)(2,1)S(1)}) custom-call(bf16[512,512]{1,0:T(8,128)(2,1)S(1)} %shard_map.95.near.matrix, bf16[128,128]{1,0:T(8,128)(2,1)S(1)} %copy-done.3, bf16[128,128]{1,0:T(8,128)(2,1)S(1)} %collective-permute-done.refs_1_, ...), custom_call_target="tpu_custom_call" | custom-call | flops 67108864 | bytes 1048576 | tf_op jit(solution)/shard_map/pallas_call | solution.py:282
  8.5 1.6 %collective-permute-start.3 = (bf16[256,128]{1,0:T(8,128)(2,1)S(1)}, bf16[256,128]{1,0:T(8,128)(2,1)S(1)}, u32[]{:S(2)}, u32[]{:S(2)}) collective-permute-start(bf16[256,128]{1,0:T(8,128)(2,1)S(1)} %get-tuple-element.18), channel_id=1, source_target_pairs={{0,1},{1,3},{2,0},{3,2},{4,5},{5,7},{6,4},{7,6},{8,9},{9,11},{10,8... | collective-permute-start | bytes 196616 | tf_op jit(solution)/shard_map/ppermute | solution.py:42
  10.1 1.6 %collective-permute-start.4 = (bf16[256,128]{1,0:T(8,128)(2,1)S(1)}, bf16[256,128]{1,0:T(8,128)(2,1)S(1)}, u32[]{:S(2)}, u32[]{:S(2)}) collective-permute-start(bf16[256,128]{1,0:T(8,128)(2,1)S(1)} %get-tuple-element.19), channel_id=1, source_target_pairs={{0,3},{1,2},{2,1},{3,0},{4,7},{5,6},{6,5},{7,4},{8,11},{9,10},{10,... | collective-permute-start | bytes 196616 | tf_op jit(solution)/shard_map/ppermute | solution.py:42
  11.7 0.0 copy-start.1
  11.7 0.0 copy-start.2
  11.7 1.6 %collective-permute-start.5 = (bf16[256,128]{1,0:T(8,128)(2,1)S(1)}, bf16[256,128]{1,0:T(8,128)(2,1)S(1)}, u32[]{:S(2)}, u32[]{:S(2)}) collective-permute-start(bf16[256,128]{1,0:T(8,128)(2,1)S(1)} %get-tuple-element.20), channel_id=1, source_target_pairs={{0,2},{1,0},{2,3},{3,1},{4,6},{5,4},{6,7},{7,5},{8,10},{9,8},{10,1... | collective-permute-start | bytes 196616 | tf_op jit(solution)/shard_map/ppermute | solution.py:42
  13.3 0.3 %shard_map.96.refs_0_.matrix = bf16[512,512]{1,0:T(8,128)(2,1)S(1)} custom-call(bf16[512,512]{1,0:T(8,128)(2,1)S(1)} %shard_map.95.near.matrix), custom_call_target="tpu_custom_call" | custom-call | bytes 1572864 | tf_op jit(solution)/shard_map/pallas_call | solution.py:299
  13.6 0.0 collective-permute-done.6.refs_7_
  13.6 0.6 %collective-permute-done.3.refs_2_ = bf16[256,128]{1,0:T(8,128)(2,1)S(1)} collective-permute-done((bf16[256,128]{1,0:T(8,128)(2,1)S(1)}, bf16[256,128]{1,0:T(8,128)(2,1)S(1)}, u32[]{:S(2)}, u32[]{:S(2)}) %collective-permute-start.3) | collective-permute-done | bytes 65568 | tf_op jit(solution)/shard_map/ppermute | solution.py:42
  14.2 2.2 %collective-permute-done.4.refs_3_ = bf16[256,128]{1,0:T(8,128)(2,1)S(1)} collective-permute-done((bf16[256,128]{1,0:T(8,128)(2,1)S(1)}, bf16[256,128]{1,0:T(8,128)(2,1)S(1)}, u32[]{:S(2)}, u32[]{:S(2)}) %collective-permute-start.4) | collective-permute-done | bytes 65568 | tf_op jit(solution)/shard_map/ppermute | solution.py:42
  16.4 0.2 collective-permute-done.5.refs_4_
  16.7 0.0 copy-done.1
  16.7 0.0 copy-done.2
  16.7 0.5 %shard_map.98 = (bf16[384,128]{1,0:T(8,128)(2,1)S(1)}, bf16[128,128]{1,0:T(8,128)(2,1)S(1)}, f32[128,256]{1,0:T(8,128)S(1)}) custom-call(bf16[512,512]{1,0:T(8,128)(2,1)S(1)} %shard_map.96.refs_0_.matrix, bf16[256,128]{1,0:T(8,128)(2,1)S(1)} %get-tuple-element.17.refs_1_, bf16[256,128]{1,0:T(8,128)(2,1)S(1)} %collective-permute-done.3.refs_2_, ...), custom_call_target="tpu_custom_call" | custom-call | flops 117440512 | tf_op jit(solution)/shard_map/pallas_call | solution.py:309
  17.2 1.9 %collective-permute-start.7 = (bf16[384,128]{1,0:T(8,128)(2,1)S(1)}, bf16[384,128]{1,0:T(8,128)(2,1)S(1)}, u32[]{:S(2)}, u32[]{:S(2)}) collective-permute-start(bf16[384,128]{1,0:T(8,128)(2,1)S(1)} %get-tuple-element.22.message.refs_0_), channel_id=1, source_target_pairs={{0,1},{1,0},{2,3},{3,2},{4,5},{5,4},{6,7},{7,6},{8,9},{9,8},{10,11... | collective-permute-start | bytes 294920 | tf_op jit(solution)/shard_map/ppermute | solution.py:57
  19.1 0.0 collective-permute-start.9
  19.1 0.3 %collective-permute-start.8 = (bf16[128,128]{1,0:T(8,128)(2,1)S(1)}, bf16[128,128]{1,0:T(8,128)(2,1)S(1)}, u32[]{:S(2)}, u32[]{:S(2)}) collective-permute-start(bf16[128,128]{1,0:T(8,128)(2,1)S(1)} %get-tuple-element.23), channel_id=1, source_target_pairs={{0,4},{4,0},{8,12},{12,8},{1,5},{5,1},{9,13},{13,9},{2,6},{6,2},{1... | collective-permute-start | bytes 98312 | tf_op jit(solution)/shard_map/ppermute | solution.py:57
  19.4 0.2 shard_map.100.begun
  19.6 3.0 %collective-permute-done.9.refs_3_ = bf16[128,128]{1,0:T(8,128)(2,1)S(1)} collective-permute-done((bf16[128,128]{1,0:T(8,128)(2,1)S(1)}, bf16[128,128]{1,0:T(8,128)(2,1)S(1)}, u32[]{:S(2)}, u32[]{:S(2)}) %collective-permute-start.9) | collective-permute-done | bytes 32800 | tf_op jit(solution)/shard_map/ppermute | solution.py:321
  22.6 0.0 collective-permute-done.8.refs_2_
  22.6 0.0 collective-permute-done.7.refs_1_
  22.6 0.2 shard_map.101
  22.8 1.7 %collective-permute-start.10 = (bf16[256,128]{1,0:T(8,128)(2,1)S(1)}, bf16[256,128]{1,0:T(8,128)(2,1)S(1)}, u32[]{:S(2)}, u32[]{:S(2)}) collective-permute-start(bf16[256,128]{1,0:T(8,128)(2,1)S(1)} %get-tuple-element.26), channel_id=1, source_target_pairs={{0,8},{4,12},{8,0},{12,4},{1,9},{5,13},{9,1},{13,5},{2,10},{6,14},... | collective-permute-start | bytes 196616 | tf_op jit(solution)/shard_map/ppermute | solution.py:42
  24.5 0.0 collective-permute-start.11
  24.5 1.7 %collective-permute-start.12 = (bf16[256,128]{1,0:T(8,128)(2,1)S(1)}, bf16[256,128]{1,0:T(8,128)(2,1)S(1)}, u32[]{:S(2)}, u32[]{:S(2)}) collective-permute-start(bf16[256,128]{1,0:T(8,128)(2,1)S(1)} %get-tuple-element.28), channel_id=1, source_target_pairs={{0,12},{4,0},{8,4},{12,8},{1,13},{5,1},{9,5},{13,9},{2,14},{6,2},{... | collective-permute-start | bytes 196616 | tf_op jit(solution)/shard_map/ppermute | solution.py:42
  26.2 0.7 %shard_map.99 = bf16[128,256]{1,0:T(8,128)(2,1)} custom-call(f32[128,256]{1,0:T(8,128)S(1)} %get-tuple-element.21.pre), custom_call_target="tpu_custom_call" | custom-call | tf_op jit(solution)/shard_map/pallas_call | solution.py:326
  26.9 0.3 collective-permute-done.10.refs_0_
  27.1 1.0 %collective-permute-done.11.refs_1_ = bf16[256,128]{1,0:T(8,128)(2,1)S(1)} collective-permute-done((bf16[256,128]{1,0:T(8,128)(2,1)S(1)}, bf16[256,128]{1,0:T(8,128)(2,1)S(1)}, u32[]{:S(2)}, u32[]{:S(2)}) %collective-permute-start.11) | collective-permute-done | bytes 65568 | tf_op jit(solution)/shard_map/ppermute | solution.py:42
  28.2 0.0 collective-permute-done.12.refs_2_
  28.2 0.7 %shard_map.102 = (bf16[128,128]{1,0:T(8,128)(2,1)}, f32[128,256]{1,0:T(8,128)}) custom-call(f32[128,128]{1,0:T(8,128)S(1)} %get-tuple-element.24.own, bf16[128,128]{1,0:T(8,128)(2,1)S(1)} %get-tuple-element.25.kept, bf16[256,128]{1,0:T(8,128)(2,1)S(1)} %collective-permute-done.10.refs_0_, bf16[256,128]{1,0:T(8,128)(2,1)S(1)} %collective-permute-done.11.refs_1_, ...), custom_call_target="tpu_custom_call" | custom-call | tf_op jit(solution)/shard_map/pallas_call | solution.py:346
  (1 shorter events, 0.0 us)
Async XLA Ops:
  0.6 6.7 %copy-start = (bf16[1,1,8,128,128]{4,3,2,1,0:T(8,128)(2,1)S(1)}, bf16[1,1,8,128,128]{4,3,2,1,0:T(8,128)(2,1)}, u32[]{:S(2)}) copy-start(bf16[1,1,8,128,128]{4,3,2,1,0:T(8,128)(2,1)} %vals.1) | copy-start | bytes 786436
  0.6 7.5 %collective-permute-start.1 = (bf16[128,128]{1,0:T(8,128)(2,1)}, bf16[128,128]{1,0:T(8,128)(2,1)S(1)}, u32[]{:S(2)}, u32[]{:S(2)}) collective-permute-start(bf16[128,128]{1,0:T(8,128)(2,1)} %refs_0_.1), channel_id=1, source_target_pairs={{0,12},{4,8},{8,4},{12,0},{1,13},{5,9},{9,5},{13,1},{2,14},{6,10},... | collective-permute-start | bytes 98312 | tf_op jit(solution)/shard_map/ppermute | solution.py:57
  3.1 5.1 %collective-permute-start = (bf16[128,128]{1,0:T(8,128)(2,1)}, bf16[128,128]{1,0:T(8,128)(2,1)S(1)}, u32[]{:S(2)}, u32[]{:S(2)}) collective-permute-start(bf16[128,128]{1,0:T(8,128)(2,1)} %refs_0_.1), channel_id=1, source_target_pairs={{0,8},{4,12},{8,0},{12,4},{1,9},{5,13},{9,1},{13,5},{2,10},{6,14},... | collective-permute-start | bytes 98312 | tf_op jit(solution)/shard_map/ppermute | solution.py:57
  3.7 4.4 %collective-permute-start.2 = (bf16[128,128]{1,0:T(8,128)(2,1)}, bf16[128,128]{1,0:T(8,128)(2,1)S(1)}, u32[]{:S(2)}, u32[]{:S(2)}) collective-permute-start(bf16[128,128]{1,0:T(8,128)(2,1)} %refs_0_.1), channel_id=1, source_target_pairs={{0,4},{4,0},{8,12},{12,8},{1,5},{5,1},{9,13},{13,9},{2,6},{6,2},{1... | collective-permute-start | bytes 98312 | tf_op jit(solution)/shard_map/ppermute | solution.py:57
  3.8 9.9 %collective-permute-start.6 = (bf16[128,256]{1,0:T(8,128)(2,1)}, bf16[128,256]{1,0:T(8,128)(2,1)S(1)}, u32[]{:S(2)}, u32[]{:S(2)}) collective-permute-start(bf16[128,256]{1,0:T(8,128)(2,1)} %refs_6_.1), channel_id=1, source_target_pairs={{0,2},{1,3},{2,0},{3,1},{4,6},{5,7},{6,4},{7,5},{8,10},{9,11},{10,... | collective-permute-start | bytes 196616 | tf_op jit(solution)/shard_map/ppermute | solution.py:57
  6.6 0.7 %copy-start.4 = (s32[1,1,8]{2,1,0:T(1,128)S(1)}, s32[1,1,8]{2,1,0:T(1,128)}, u32[]{:S(2)}) copy-start(s32[1,1,8]{2,1,0:T(1,128)} %rows_in.1) | copy-start | bytes 100
  6.7 0.7 %copy-start.5 = (s32[1,1,8]{2,1,0:T(1,128)S(1)}, s32[1,1,8]{2,1,0:T(1,128)}, u32[]{:S(2)}) copy-start(s32[1,1,8]{2,1,0:T(1,128)} %cols_in.1) | copy-start | bytes 100
  7.4 0.8 %copy-start.3 = (bf16[128,128]{1,0:T(8,128)(2,1)S(1)}, bf16[128,128]{1,0:T(8,128)(2,1)}, u32[]{:S(2)}) copy-start(bf16[128,128]{1,0:T(8,128)(2,1)} %refs_0_.1) | copy-start | bytes 98308
  8.5 5.7 %collective-permute-start.3 = (bf16[256,128]{1,0:T(8,128)(2,1)S(1)}, bf16[256,128]{1,0:T(8,128)(2,1)S(1)}, u32[]{:S(2)}, u32[]{:S(2)}) collective-permute-start(bf16[256,128]{1,0:T(8,128)(2,1)S(1)} %get-tuple-element.18), channel_id=1, source_target_pairs={{0,1},{1,3},{2,0},{3,2},{4,5},{5,7},{6,4},{7,6},{8,9},{9,11},{10,8... | collective-permute-start | bytes 196616 | tf_op jit(solution)/shard_map/ppermute | solution.py:42
  10.1 6.4 %collective-permute-start.4 = (bf16[256,128]{1,0:T(8,128)(2,1)S(1)}, bf16[256,128]{1,0:T(8,128)(2,1)S(1)}, u32[]{:S(2)}, u32[]{:S(2)}) collective-permute-start(bf16[256,128]{1,0:T(8,128)(2,1)S(1)} %get-tuple-element.19), channel_id=1, source_target_pairs={{0,3},{1,2},{2,1},{3,0},{4,7},{5,6},{6,5},{7,4},{8,11},{9,10},{10,... | collective-permute-start | bytes 196616 | tf_op jit(solution)/shard_map/ppermute | solution.py:42
  11.7 5.0 %copy-start.1 = (bf16[128,256]{1,0:T(8,128)(2,1)S(1)}, bf16[128,256]{1,0:T(8,128)(2,1)}, u32[]{:S(2)}) copy-start(bf16[128,256]{1,0:T(8,128)(2,1)} %refs_5_.1) | copy-start | bytes 196612
  11.7 5.0 %copy-start.2 = (bf16[128,256]{1,0:T(8,128)(2,1)S(1)}, bf16[128,256]{1,0:T(8,128)(2,1)}, u32[]{:S(2)}) copy-start(bf16[128,256]{1,0:T(8,128)(2,1)} %refs_6_.1) | copy-start | bytes 196612
  11.7 5.0 %collective-permute-start.5 = (bf16[256,128]{1,0:T(8,128)(2,1)S(1)}, bf16[256,128]{1,0:T(8,128)(2,1)S(1)}, u32[]{:S(2)}, u32[]{:S(2)}) collective-permute-start(bf16[256,128]{1,0:T(8,128)(2,1)S(1)} %get-tuple-element.20), channel_id=1, source_target_pairs={{0,2},{1,0},{2,3},{3,1},{4,6},{5,4},{6,7},{7,5},{8,10},{9,8},{10,1... | collective-permute-start | bytes 196616 | tf_op jit(solution)/shard_map/ppermute | solution.py:42
  17.2 5.4 %collective-permute-start.7 = (bf16[384,128]{1,0:T(8,128)(2,1)S(1)}, bf16[384,128]{1,0:T(8,128)(2,1)S(1)}, u32[]{:S(2)}, u32[]{:S(2)}) collective-permute-start(bf16[384,128]{1,0:T(8,128)(2,1)S(1)} %get-tuple-element.22.message.refs_0_), channel_id=1, source_target_pairs={{0,1},{1,0},{2,3},{3,2},{4,5},{5,4},{6,7},{7,6},{8,9},{9,8},{10,11... | collective-permute-start | bytes 294920 | tf_op jit(solution)/shard_map/ppermute | solution.py:57
  19.1 3.5 %collective-permute-start.9 = (bf16[128,128]{1,0:T(8,128)(2,1)S(1)}, bf16[128,128]{1,0:T(8,128)(2,1)S(1)}, u32[]{:S(2)}, u32[]{:S(2)}) collective-permute-start(bf16[128,128]{1,0:T(8,128)(2,1)S(1)} %get-tuple-element.23), channel_id=1, source_target_pairs={{0,5},{1,4},{2,7},{3,6},{4,1},{5,0},{6,3},{7,2},{8,13},{9,12},{10,... | collective-permute-start | bytes 98312 | tf_op jit(solution)/shard_map/ppermute | solution.py:321
  19.1 3.5 %collective-permute-start.8 = (bf16[128,128]{1,0:T(8,128)(2,1)S(1)}, bf16[128,128]{1,0:T(8,128)(2,1)S(1)}, u32[]{:S(2)}, u32[]{:S(2)}) collective-permute-start(bf16[128,128]{1,0:T(8,128)(2,1)S(1)} %get-tuple-element.23), channel_id=1, source_target_pairs={{0,4},{4,0},{8,12},{12,8},{1,5},{5,1},{9,13},{13,9},{2,6},{6,2},{1... | collective-permute-start | bytes 98312 | tf_op jit(solution)/shard_map/ppermute | solution.py:57
  22.8 4.3 %collective-permute-start.10 = (bf16[256,128]{1,0:T(8,128)(2,1)S(1)}, bf16[256,128]{1,0:T(8,128)(2,1)S(1)}, u32[]{:S(2)}, u32[]{:S(2)}) collective-permute-start(bf16[256,128]{1,0:T(8,128)(2,1)S(1)} %get-tuple-element.26), channel_id=1, source_target_pairs={{0,8},{4,12},{8,0},{12,4},{1,9},{5,13},{9,1},{13,5},{2,10},{6,14},... | collective-permute-start | bytes 196616 | tf_op jit(solution)/shard_map/ppermute | solution.py:42
  24.5 3.7 %collective-permute-start.11 = (bf16[256,128]{1,0:T(8,128)(2,1)S(1)}, bf16[256,128]{1,0:T(8,128)(2,1)S(1)}, u32[]{:S(2)}, u32[]{:S(2)}) collective-permute-start(bf16[256,128]{1,0:T(8,128)(2,1)S(1)} %get-tuple-element.27), channel_id=1, source_target_pairs={{0,4},{4,8},{8,12},{12,0},{1,5},{5,9},{9,13},{13,1},{2,6},{6,10},{... | collective-permute-start | bytes 196616 | tf_op jit(solution)/shard_map/ppermute | solution.py:42
  24.5 3.7 %collective-permute-start.12 = (bf16[256,128]{1,0:T(8,128)(2,1)S(1)}, bf16[256,128]{1,0:T(8,128)(2,1)S(1)}, u32[]{:S(2)}, u32[]{:S(2)}) collective-permute-start(bf16[256,128]{1,0:T(8,128)(2,1)S(1)} %get-tuple-element.28), channel_id=1, source_target_pairs={{0,12},{4,0},{8,4},{12,8},{1,13},{5,1},{9,5},{13,9},{2,14},{6,2},{... | collective-permute-start | bytes 196616 | tf_op jit(solution)/shard_map/ppermute | solution.py:42

commit v31 on v29

--- a/solution.py
+++ b/solution.py
@@ -170,30 +170,20 @@
     store_layer(back, term, message, other)
 
 
-def in_middle():
-    my_col = lax.axis_index("col")
-    return (my_col == 1) | (my_col == 2)
-
-
 def paired_forward_kernel(n, matrix, *refs):
-    operands, (own, first, second, third) = refs[:n], refs[n:]
+    operands, (own, first, third, second) = refs[:n], refs[n:]
     product = dot(matrix[...], stack(operands)).astype(own.dtype)
     rows = own.shape[0]
-    same, other = product[:rows], product[rows:]
-    middle = in_middle()
-    own[...] = same
-    first[...] = jnp.where(middle, same, other)
-    second[...] = other
-    third[...] = jnp.where(middle, other, same)
-
-
-def paired_layer_kernel(own, first, second, third, weight, cotangent, beyond, *refs):
+    for target in (own, second):
+        target[...] = product[:rows]
+    for target in (first, third):
+        target[...] = product[rows:]
+
+
+def paired_layer_kernel(own, first, third, second, weight, cotangent, beyond, *refs):
     message, other, pre_out = refs
     nodes = cotangent.shape[0]
-    middle = in_middle()
-    partner = jnp.where(middle, third[...], first[...])
-    side = jnp.where(middle, first[...], third[...])
-    total = (wide(own[...]) + wide(partner)) + (wide(second[...]) + wide(side))
+    total = (wide(own[...]) + wide(second[...])) + (wide(first[...]) + wide(third[...]))
     high_col = lax.axis_index("col") >= 2
     here, there = cotangent[...], beyond[...]
     both = jnp.concatenate(
@@ -284,6 +274,7 @@
             [VMEM] * (1 + n_row),
             **forward,
         )(near, features, *gathered)
+        parts = [swap(send, "col", d) for d, send in zip((1, 3, 2), sends)]
         layer_call, cotangents = paired_layer_kernel, [cotangent, swap(cotangent, "col", 2)]
     else:
         layers = 1
@@ -294,7 +285,7 @@
             **forward,
         )(near, features, *gathered)
         layer_call, cotangents = layer_kernel, [cotangent]
-    parts = exchange(sends, "col", True)
+        parts = exchange(sends, "col", True)
     (far,) = call(
         functools.partial(turn_kernel, side),
         [((across, down), NARROW)],

time: 28.9 us -> 30.5 us (1.055)
  waiting for transfers between devices: 7.25 us -> 10.1 us
  starting transfers between devices: 16.1 us -> 14.6 us
    ppermute x6 -> x9, waiting for transfers between devices: 0.02 us -> 6.7 us  [swap(): return lax.ppermute(value, axis, [(s, s ^ distance) for s in range(n)])]
    ppermute x6 -> x3, starting transfers between devices: 7.95 us -> 2.88 us  [exchange(): lax.ppermute(send, axis, [(s, target(s, d)) for s in range(n)])]
    ppermute x6 -> x3, waiting for transfers between devices: 4.27 us -> 1.32 us  [exchange(): lax.ppermute(send, axis, [(s, target(s, d)) for s in range(n)])]
    ppermute x6 -> x9, starting transfers between devices: 8.17 us -> 10.4 us  [swap(): return lax.ppermute(value, axis, [(s, s ^ distance) for s in range(n)])]
    ppermute x1, starting transfers between devices: 0.01 us -> 1.34 us  [per_device(): lax.ppermute(other, ('row', 'col'), corner)]
    ppermute x1, waiting for transfers between devices: 2.96 us -> 2.09 us  [per_device(): lax.ppermute(other, ('row', 'col'), corner)]
where the time goes in v31:
time: 30.5 us; the launch traced here: 30 us
  starting transfers between devices  14.6 us (48%)
  waiting for transfers between devices  10.1 us (33%)
  Pallas kernels  3.76 us (12%)
  between operations  1.45 us (5%)
    ppermute x9, starting transfers between devices, swap(): return lax.ppermute(value, axis, [(s, s ^ distance) for s in range(n)])  10.4 us
    ppermute x9, waiting for transfers between devices, swap(): return lax.ppermute(value, axis, [(s, s ^ distance) for s in range(n)])  6.7 us
    ppermute x3, starting transfers between devices, exchange(): lax.ppermute(send, axis, [(s, target(s, d)) for s in range(n)])  2.88 us
    ppermute x1, waiting for transfers between devices, per_device(): lax.ppermute(other, ('row', 'col'), corner)  2.09 us
    ppermute x1, starting transfers between devices, per_device(): lax.ppermute(other, ('row', 'col'), corner)  1.34 us
    ppermute x3, waiting for transfers between devices, exchange(): lax.ppermute(send, axis, [(s, target(s, d)) for s in range(n)])  1.32 us
    pallas_call x1, Pallas kernels, per_device(): call(functools.partial(dense_kernel, nodes // side, paired), [((down, acr...  0.77 us
    pallas_call x1, Pallas kernels, per_device(): call(functools.partial(last_kernel, scale), [((nodes, width), NARROW), ((...  0.7 us
  transfers between devices with their start and end apart: 13, of which 7 were waited for; matrix products, arithmetic and copies ran while one was open for 0% of the time, Pallas kernels for 8%

profile of v31, /device:TPU:0, one launch (start us, length us, event | category | flops | bytes accessed | tf_op | source)
XLA Modules:
  0.0 30.0 jit_solution(15113192056401535196)
XLA Ops:
  0.6 0.0 copy-start
  0.6 2.4 %collective-permute-start.1 = (bf16[128,128]{1,0:T(8,128)(2,1)}, bf16[128,128]{1,0:T(8,128)(2,1)S(1)}, u32[]{:S(2)}, u32[]{:S(2)}) collective-permute-start(bf16[128,128]{1,0:T(8,128)(2,1)} %refs_0_.1), channel_id=1, source_target_pairs={{0,12},{4,8},{8,4},{12,0},{1,13},{5,9},{9,5},{13,1},{2,14},{6,10},... | collective-permute-start | bytes 98312 | tf_op jit(solution)/shard_map/ppermute | solution.py:57
  3.1 0.6 %collective-permute-start = (bf16[128,128]{1,0:T(8,128)(2,1)}, bf16[128,128]{1,0:T(8,128)(2,1)S(1)}, u32[]{:S(2)}, u32[]{:S(2)}) collective-permute-start(bf16[128,128]{1,0:T(8,128)(2,1)} %refs_0_.1), channel_id=1, source_target_pairs={{0,8},{4,12},{8,0},{12,4},{1,9},{5,13},{9,1},{13,5},{2,10},{6,14},... | collective-permute-start | bytes 98312 | tf_op jit(solution)/shard_map/ppermute | solution.py:57
  3.7 0.0 collective-permute-start.2
  3.8 2.8 %collective-permute-start.6 = (bf16[128,256]{1,0:T(8,128)(2,1)}, bf16[128,256]{1,0:T(8,128)(2,1)S(1)}, u32[]{:S(2)}, u32[]{:S(2)}) collective-permute-start(bf16[128,256]{1,0:T(8,128)(2,1)} %refs_6_.1), channel_id=1, source_target_pairs={{0,2},{1,3},{2,0},{3,1},{4,6},{5,7},{6,4},{7,5},{8,10},{9,11},{10,... | collective-permute-start | bytes 196616 | tf_op jit(solution)/shard_map/ppermute | solution.py:57
  6.6 0.0 copy-start.4
  6.7 0.0 copy-start.5
  7.3 0.0 copy-done
  7.3 0.0 copy-done.4
  7.3 0.0 copy-done.5
  7.4 0.0 copy-start.3
  7.4 0.8 %shard_map.95.near.matrix = bf16[512,512]{1,0:T(8,128)(2,1)S(1)} custom-call(bf16[512,512]{1,0:T(8,128)(2,1)S(1)} %shard_map.94.blank, bf16[1,1,8,128,128]{4,3,2,1,0:T(8,128)(2,1)S(1)} %copy-done, s32[1,1,8]{2,1,0:T(1,128)S(1)} %copy-done.4, s32[1,1,8]{2,1,0:T(1,128)S(1)} %copy-done.5, s32[1,1]{1,0:T(1,128)S(6)} %copy.10.count_in), custom_call_target="tpu_custom_call" | custom-call | bytes 1048576 | tf_op jit(solution)/shard_map/pallas_call | solution.py:255
  8.2 0.0 collective-permute-done.1.refs_2_
  8.2 0.0 collective-permute-done.refs_1_
  8.2 0.0 collective-permute-done.2.refs_3_
  8.2 0.0 copy-done.3
  8.2 0.3 shard_map.97
  8.5 1.6 %collective-permute-start.3 = (bf16[256,128]{1,0:T(8,128)(2,1)S(1)}, bf16[256,128]{1,0:T(8,128)(2,1)S(1)}, u32[]{:S(2)}, u32[]{:S(2)}) collective-permute-start(bf16[256,128]{1,0:T(8,128)(2,1)S(1)} %get-tuple-element.18), channel_id=1, source_target_pairs={{0,1},{1,0},{2,3},{3,2},{4,5},{5,4},{6,7},{7,6},{8,9},{9,8},{10,11... | collective-permute-start | bytes 196616 | tf_op jit(solution)/shard_map/ppermute | solution.py:57
  10.1 1.6 %collective-permute-start.4 = (bf16[256,128]{1,0:T(8,128)(2,1)S(1)}, bf16[256,128]{1,0:T(8,128)(2,1)S(1)}, u32[]{:S(2)}, u32[]{:S(2)}) collective-permute-start(bf16[256,128]{1,0:T(8,128)(2,1)S(1)} %get-tuple-element.19), channel_id=1, source_target_pairs={{0,3},{1,2},{2,1},{3,0},{4,7},{5,6},{6,5},{7,4},{8,11},{9,10},{10,... | collective-permute-start | bytes 196616 | tf_op jit(solution)/shard_map/ppermute | solution.py:57
  11.7 0.0 copy-start.1
  11.7 0.0 copy-start.2
  11.7 0.4 %collective-permute-start.5 = (bf16[256,128]{1,0:T(8,128)(2,1)S(1)}, bf16[256,128]{1,0:T(8,128)(2,1)S(1)}, u32[]{:S(2)}, u32[]{:S(2)}) collective-permute-start(bf16[256,128]{1,0:T(8,128)(2,1)S(1)} %get-tuple-element.20), channel_id=1, source_target_pairs={{0,2},{1,3},{2,0},{3,1},{4,6},{5,7},{6,4},{7,5},{8,10},{9,11},{10,... | collective-permute-start | bytes 196616 | tf_op jit(solution)/shard_map/ppermute | solution.py:57
  12.1 0.3 %shard_map.96.refs_0_.matrix = bf16[512,512]{1,0:T(8,128)(2,1)S(1)} custom-call(bf16[512,512]{1,0:T(8,128)(2,1)S(1)} %shard_map.95.near.matrix), custom_call_target="tpu_custom_call" | custom-call | bytes 1572864 | tf_op jit(solution)/shard_map/pallas_call | solution.py:289
  12.4 0.0 collective-permute-done.6.refs_7_
  12.4 0.4 %collective-permute-done.3.refs_2_ = bf16[256,128]{1,0:T(8,128)(2,1)S(1)} collective-permute-done((bf16[256,128]{1,0:T(8,128)(2,1)S(1)}, bf16[256,128]{1,0:T(8,128)(2,1)S(1)}, u32[]{:S(2)}, u32[]{:S(2)}) %collective-permute-start.3) | collective-permute-done | bytes 65568 | tf_op jit(solution)/shard_map/ppermute | solution.py:57
  12.8 3.5 %collective-permute-done.4.refs_3_ = bf16[256,128]{1,0:T(8,128)(2,1)S(1)} collective-permute-done((bf16[256,128]{1,0:T(8,128)(2,1)S(1)}, bf16[256,128]{1,0:T(8,128)(2,1)S(1)}, u32[]{:S(2)}, u32[]{:S(2)}) %collective-permute-start.4) | collective-permute-done | bytes 65568 | tf_op jit(solution)/shard_map/ppermute | solution.py:57
  16.3 2.2 %collective-permute-done.5.refs_4_ = bf16[256,128]{1,0:T(8,128)(2,1)S(1)} collective-permute-done((bf16[256,128]{1,0:T(8,128)(2,1)S(1)}, bf16[256,128]{1,0:T(8,128)(2,1)S(1)}, u32[]{:S(2)}, u32[]{:S(2)}) %collective-permute-start.5) | collective-permute-done | bytes 65568 | tf_op jit(solution)/shard_map/ppermute | solution.py:57
  18.5 0.0 copy-done.1
  18.5 0.0 copy-done.2
  18.5 0.5 %shard_map.98 = (bf16[384,128]{1,0:T(8,128)(2,1)S(1)}, bf16[128,128]{1,0:T(8,128)(2,1)S(1)}, f32[128,256]{1,0:T(8,128)S(1)}) custom-call(bf16[512,512]{1,0:T(8,128)(2,1)S(1)} %shard_map.96.refs_0_.matrix, bf16[256,128]{1,0:T(8,128)(2,1)S(1)} %get-tuple-element.17.refs_1_, bf16[256,128]{1,0:T(8,128)(2,1)S(1)} %collective-permute-done.3.refs_2_, ...), custom_call_target="tpu_custom_call" | custom-call | flops 117440512 | tf_op jit(solution)/shard_map/pallas_call | solution.py:299
  19.0 0.1 collective-permute-start.7
  19.1 1.3 %collective-permute-start.9 = (bf16[128,128]{1,0:T(8,128)(2,1)S(1)}, bf16[128,128]{1,0:T(8,128)(2,1)S(1)}, u32[]{:S(2)}, u32[]{:S(2)}) collective-permute-start(bf16[128,128]{1,0:T(8,128)(2,1)S(1)} %get-tuple-element.23), channel_id=1, source_target_pairs={{0,5},{1,4},{2,7},{3,6},{4,1},{5,0},{6,3},{7,2},{8,13},{9,12},{10,... | collective-permute-start | bytes 98312 | tf_op jit(solution)/shard_map/ppermute | solution.py:311
  20.4 0.8 %collective-permute-start.8 = (bf16[128,128]{1,0:T(8,128)(2,1)S(1)}, bf16[128,128]{1,0:T(8,128)(2,1)S(1)}, u32[]{:S(2)}, u32[]{:S(2)}) collective-permute-start(bf16[128,128]{1,0:T(8,128)(2,1)S(1)} %get-tuple-element.23), channel_id=1, source_target_pairs={{0,4},{4,0},{8,12},{12,8},{1,5},{5,1},{9,13},{13,9},{2,6},{6,2},{1... | collective-permute-start | bytes 98312 | tf_op jit(solution)/shard_map/ppermute | solution.py:57
  21.2 0.2 shard_map.100.begun
  21.4 2.1 %collective-permute-done.9.refs_3_ = bf16[128,128]{1,0:T(8,128)(2,1)S(1)} collective-permute-done((bf16[128,128]{1,0:T(8,128)(2,1)S(1)}, bf16[128,128]{1,0:T(8,128)(2,1)S(1)}, u32[]{:S(2)}, u32[]{:S(2)}) %collective-permute-start.9) | collective-permute-done | bytes 32800 | tf_op jit(solution)/shard_map/ppermute | solution.py:311
  23.5 0.0 collective-permute-done.8.refs_2_
  23.5 0.6 %collective-permute-done.7.refs_1_ = bf16[384,128]{1,0:T(8,128)(2,1)S(1)} collective-permute-done((bf16[384,128]{1,0:T(8,128)(2,1)S(1)}, bf16[384,128]{1,0:T(8,128)(2,1)S(1)}, u32[]{:S(2)}, u32[]{:S(2)}) %collective-permute-start.7) | collective-permute-done | bytes 98336 | tf_op jit(solution)/shard_map/ppermute | solution.py:57
  24.1 0.2 shard_map.101
  24.4 0.2 collective-permute-start.10
  24.6 1.4 %collective-permute-start.11 = (bf16[256,128]{1,0:T(8,128)(2,1)S(1)}, bf16[256,128]{1,0:T(8,128)(2,1)S(1)}, u32[]{:S(2)}, u32[]{:S(2)}) collective-permute-start(bf16[256,128]{1,0:T(8,128)(2,1)S(1)} %get-tuple-element.27), channel_id=1, source_target_pairs={{0,8},{4,12},{8,0},{12,4},{1,9},{5,13},{9,1},{13,5},{2,10},{6,14},... | collective-permute-start | bytes 196616 | tf_op jit(solution)/shard_map/ppermute | solution.py:42
  26.0 1.3 %collective-permute-start.12 = (bf16[256,128]{1,0:T(8,128)(2,1)S(1)}, bf16[256,128]{1,0:T(8,128)(2,1)S(1)}, u32[]{:S(2)}, u32[]{:S(2)}) collective-permute-start(bf16[256,128]{1,0:T(8,128)(2,1)S(1)} %get-tuple-element.28), channel_id=1, source_target_pairs={{0,12},{4,0},{8,4},{12,8},{1,13},{5,1},{9,5},{13,9},{2,14},{6,2},{... | collective-permute-start | bytes 196616 | tf_op jit(solution)/shard_map/ppermute | solution.py:42
  27.3 0.7 %shard_map.99 = bf16[128,256]{1,0:T(8,128)(2,1)} custom-call(f32[128,256]{1,0:T(8,128)S(1)} %get-tuple-element.21.pre), custom_call_target="tpu_custom_call" | custom-call | tf_op jit(solution)/shard_map/pallas_call | solution.py:316
  27.9 0.2 collective-permute-done.10.refs_0_
  28.1 1.1 %collective-permute-done.11.refs_1_ = bf16[256,128]{1,0:T(8,128)(2,1)S(1)} collective-permute-done((bf16[256,128]{1,0:T(8,128)(2,1)S(1)}, bf16[256,128]{1,0:T(8,128)(2,1)S(1)}, u32[]{:S(2)}, u32[]{:S(2)}) %collective-permute-start.11) | collective-permute-done | bytes 65568 | tf_op jit(solution)/shard_map/ppermute | solution.py:42
  29.3 0.0 collective-permute-done.12.refs_2_
  29.3 0.7 %shard_map.102 = (bf16[128,128]{1,0:T(8,128)(2,1)}, f32[128,256]{1,0:T(8,128)}) custom-call(f32[128,128]{1,0:T(8,128)S(1)} %get-tuple-element.24.own, bf16[128,128]{1,0:T(8,128)(2,1)S(1)} %get-tuple-element.25.kept, bf16[256,128]{1,0:T(8,128)(2,1)S(1)} %collective-permute-done.10.refs_0_, bf16[256,128]{1,0:T(8,128)(2,1)S(1)} %collective-permute-done.11.refs_1_, ...), custom_call_target="tpu_custom_call" | custom-call | tf_op jit(solution)/shard_map/pallas_call | solution.py:336
  (1 shorter events, 0.0 us)
Async XLA Ops:
  0.6 6.7 %copy-start = (bf16[1,1,8,128,128]{4,3,2,1,0:T(8,128)(2,1)S(1)}, bf16[1,1,8,128,128]{4,3,2,1,0:T(8,128)(2,1)}, u32[]{:S(2)}) copy-start(bf16[1,1,8,128,128]{4,3,2,1,0:T(8,128)(2,1)} %vals.1) | copy-start | bytes 786436
  0.6 7.5 %collective-permute-start.1 = (bf16[128,128]{1,0:T(8,128)(2,1)}, bf16[128,128]{1,0:T(8,128)(2,1)S(1)}, u32[]{:S(2)}, u32[]{:S(2)}) collective-permute-start(bf16[128,128]{1,0:T(8,128)(2,1)} %refs_0_.1), channel_id=1, source_target_pairs={{0,12},{4,8},{8,4},{12,0},{1,13},{5,9},{9,5},{13,1},{2,14},{6,10},... | collective-permute-start | bytes 98312 | tf_op jit(solution)/shard_map/ppermute | solution.py:57
  3.1 5.1 %collective-permute-start = (bf16[128,128]{1,0:T(8,128)(2,1)}, bf16[128,128]{1,0:T(8,128)(2,1)S(1)}, u32[]{:S(2)}, u32[]{:S(2)}) collective-permute-start(bf16[128,128]{1,0:T(8,128)(2,1)} %refs_0_.1), channel_id=1, source_target_pairs={{0,8},{4,12},{8,0},{12,4},{1,9},{5,13},{9,1},{13,5},{2,10},{6,14},... | collective-permute-start | bytes 98312 | tf_op jit(solution)/shard_map/ppermute | solution.py:57
  3.7 4.4 %collective-permute-start.2 = (bf16[128,128]{1,0:T(8,128)(2,1)}, bf16[128,128]{1,0:T(8,128)(2,1)S(1)}, u32[]{:S(2)}, u32[]{:S(2)}) collective-permute-start(bf16[128,128]{1,0:T(8,128)(2,1)} %refs_0_.1), channel_id=1, source_target_pairs={{0,4},{4,0},{8,12},{12,8},{1,5},{5,1},{9,13},{13,9},{2,6},{6,2},{1... | collective-permute-start | bytes 98312 | tf_op jit(solution)/shard_map/ppermute | solution.py:57
  3.8 8.6 %collective-permute-start.6 = (bf16[128,256]{1,0:T(8,128)(2,1)}, bf16[128,256]{1,0:T(8,128)(2,1)S(1)}, u32[]{:S(2)}, u32[]{:S(2)}) collective-permute-start(bf16[128,256]{1,0:T(8,128)(2,1)} %refs_6_.1), channel_id=1, source_target_pairs={{0,2},{1,3},{2,0},{3,1},{4,6},{5,7},{6,4},{7,5},{8,10},{9,11},{10,... | collective-permute-start | bytes 196616 | tf_op jit(solution)/shard_map/ppermute | solution.py:57
  6.6 0.7 %copy-start.4 = (s32[1,1,8]{2,1,0:T(1,128)S(1)}, s32[1,1,8]{2,1,0:T(1,128)}, u32[]{:S(2)}) copy-start(s32[1,1,8]{2,1,0:T(1,128)} %rows_in.1) | copy-start | bytes 100
  6.7 0.7 %copy-start.5 = (s32[1,1,8]{2,1,0:T(1,128)S(1)}, s32[1,1,8]{2,1,0:T(1,128)}, u32[]{:S(2)}) copy-start(s32[1,1,8]{2,1,0:T(1,128)} %cols_in.1) | copy-start | bytes 100
  7.4 0.8 %copy-start.3 = (bf16[128,128]{1,0:T(8,128)(2,1)S(1)}, bf16[128,128]{1,0:T(8,128)(2,1)}, u32[]{:S(2)}) copy-start(bf16[128,128]{1,0:T(8,128)(2,1)} %refs_0_.1) | copy-start | bytes 98308
  8.5 4.3 %collective-permute-start.3 = (bf16[256,128]{1,0:T(8,128)(2,1)S(1)}, bf16[256,128]{1,0:T(8,128)(2,1)S(1)}, u32[]{:S(2)}, u32[]{:S(2)}) collective-permute-start(bf16[256,128]{1,0:T(8,128)(2,1)S(1)} %get-tuple-element.18), channel_id=1, source_target_pairs={{0,1},{1,0},{2,3},{3,2},{4,5},{5,4},{6,7},{7,6},{8,9},{9,8},{10,11... | collective-permute-start | bytes 196616 | tf_op jit(solution)/shard_map/ppermute | solution.py:57
  10.1 6.3 %collective-permute-start.4 = (bf16[256,128]{1,0:T(8,128)(2,1)S(1)}, bf16[256,128]{1,0:T(8,128)(2,1)S(1)}, u32[]{:S(2)}, u32[]{:S(2)}) collective-permute-start(bf16[256,128]{1,0:T(8,128)(2,1)S(1)} %get-tuple-element.19), channel_id=1, source_target_pairs={{0,3},{1,2},{2,1},{3,0},{4,7},{5,6},{6,5},{7,4},{8,11},{9,10},{10,... | collective-permute-start | bytes 196616 | tf_op jit(solution)/shard_map/ppermute | solution.py:57
  11.7 6.8 %copy-start.1 = (bf16[128,256]{1,0:T(8,128)(2,1)S(1)}, bf16[128,256]{1,0:T(8,128)(2,1)}, u32[]{:S(2)}) copy-start(bf16[128,256]{1,0:T(8,128)(2,1)} %refs_5_.1) | copy-start | bytes 196612
  11.7 6.8 %copy-start.2 = (bf16[128,256]{1,0:T(8,128)(2,1)S(1)}, bf16[128,256]{1,0:T(8,128)(2,1)}, u32[]{:S(2)}) copy-start(bf16[128,256]{1,0:T(8,128)(2,1)} %refs_6_.1) | copy-start | bytes 196612
  11.7 6.8 %collective-permute-start.5 = (bf16[256,128]{1,0:T(8,128)(2,1)S(1)}, bf16[256,128]{1,0:T(8,128)(2,1)S(1)}, u32[]{:S(2)}, u32[]{:S(2)}) collective-permute-start(bf16[256,128]{1,0:T(8,128)(2,1)S(1)} %get-tuple-element.20), channel_id=1, source_target_pairs={{0,2},{1,3},{2,0},{3,1},{4,6},{5,7},{6,4},{7,5},{8,10},{9,11},{10,... | collective-permute-start | bytes 196616 | tf_op jit(solution)/shard_map/ppermute | solution.py:57
  19.0 5.1 %collective-permute-start.7 = (bf16[384,128]{1,0:T(8,128)(2,1)S(1)}, bf16[384,128]{1,0:T(8,128)(2,1)S(1)}, u32[]{:S(2)}, u32[]{:S(2)}) collective-permute-start(bf16[384,128]{1,0:T(8,128)(2,1)S(1)} %get-tuple-element.22.message.refs_0_), channel_id=1, source_target_pairs={{0,1},{1,0},{2,3},{3,2},{4,5},{5,4},{6,7},{7,6},{8,9},{9,8},{10,11... | collective-permute-start | bytes 294920 | tf_op jit(solution)/shard_map/ppermute | solution.py:57
  19.1 4.4 %collective-permute-start.9 = (bf16[128,128]{1,0:T(8,128)(2,1)S(1)}, bf16[128,128]{1,0:T(8,128)(2,1)S(1)}, u32[]{:S(2)}, u32[]{:S(2)}) collective-permute-start(bf16[128,128]{1,0:T(8,128)(2,1)S(1)} %get-tuple-element.23), channel_id=1, source_target_pairs={{0,5},{1,4},{2,7},{3,6},{4,1},{5,0},{6,3},{7,2},{8,13},{9,12},{10,... | collective-permute-start | bytes 98312 | tf_op jit(solution)/shard_map/ppermute | solution.py:311
  20.4 3.1 %collective-permute-start.8 = (bf16[128,128]{1,0:T(8,128)(2,1)S(1)}, bf16[128,128]{1,0:T(8,128)(2,1)S(1)}, u32[]{:S(2)}, u32[]{:S(2)}) collective-permute-start(bf16[128,128]{1,0:T(8,128)(2,1)S(1)} %get-tuple-element.23), channel_id=1, source_target_pairs={{0,4},{4,0},{8,12},{12,8},{1,5},{5,1},{9,13},{13,9},{2,6},{6,2},{1... | collective-permute-start | bytes 98312 | tf_op jit(solution)/shard_map/ppermute | solution.py:57
  24.4 3.7 %collective-permute-start.10 = (bf16[256,128]{1,0:T(8,128)(2,1)S(1)}, bf16[256,128]{1,0:T(8,128)(2,1)S(1)}, u32[]{:S(2)}, u32[]{:S(2)}) collective-permute-start(bf16[256,128]{1,0:T(8,128)(2,1)S(1)} %get-tuple-element.26), channel_id=1, source_target_pairs={{0,4},{4,8},{8,12},{12,0},{1,5},{5,9},{9,13},{13,1},{2,6},{6,10},{... | collective-permute-start | bytes 196616 | tf_op jit(solution)/shard_map/ppermute | solution.py:42
  24.6 4.6 %collective-permute-start.11 = (bf16[256,128]{1,0:T(8,128)(2,1)S(1)}, bf16[256,128]{1,0:T(8,128)(2,1)S(1)}, u32[]{:S(2)}, u32[]{:S(2)}) collective-permute-start(bf16[256,128]{1,0:T(8,128)(2,1)S(1)} %get-tuple-element.27), channel_id=1, source_target_pairs={{0,8},{4,12},{8,0},{12,4},{1,9},{5,13},{9,1},{13,5},{2,10},{6,14},... | collective-permute-start | bytes 196616 | tf_op jit(solution)/shard_map/ppermute | solution.py:42
  26.0 3.3 %collective-permute-start.12 = (bf16[256,128]{1,0:T(8,128)(2,1)S(1)}, bf16[256,128]{1,0:T(8,128)(2,1)S(1)}, u32[]{:S(2)}, u32[]{:S(2)}) collective-permute-start(bf16[256,128]{1,0:T(8,128)(2,1)S(1)} %get-tuple-element.28), channel_id=1, source_target_pairs={{0,12},{4,0},{8,4},{12,8},{1,13},{5,1},{9,5},{13,9},{2,14},{6,2},{... | collective-permute-start | bytes 196616 | tf_op jit(solution)/shard_map/ppermute | solution.py:42

commit v32 on v29

--- a/solution.py
+++ b/solution.py
@@ -317,7 +317,7 @@
             (r * n_col + c, (r ^ 1) * n_col + (c ^ 1)) for r in range(n_row) for c in range(n_col)
         ]
         messages = [sent, swap(sent, "col", 1)]
-        others = [swap(other, "row", 1), lax.ppermute(other, ("row", "col"), corner)]
+        others = [lax.ppermute(other, ("row", "col"), corner), swap(other, "row", 1)]
     else:
         (sent,) = call(message_kernel, [message], [VMEM] * 2)(sent, swap(other, "row", 1))
         messages = [sent] + exchange([sent] * (n_col - 1), "col", False)

time: 28.9 us -> 29.1 us (level)
    ppermute x1, waiting for transfers between devices: 2.96 us -> 2.13 us  [per_device(): lax.ppermute(other, ('row', 'col'), corner)]
    ppermute x6, waiting for transfers between devices: 0.02 us -> 0.64 us  [swap(): return lax.ppermute(value, axis, [(s, s ^ distance) for s in range(n)])]
    ppermute x6, starting transfers between devices: 8.17 us -> 7.8 us  [swap(): return lax.ppermute(value, axis, [(s, s ^ distance) for s in range(n)])]
    ppermute x1, starting transfers between devices: 0.01 us -> 0.36 us  [per_device(): lax.ppermute(other, ('row', 'col'), corner)]
  transfers between devices with their start and end apart: 13 -> 13, of which waited for: 7 -> 6; matrix products, arithmetic and copies ran while one was open for 0% -> 0% of each run, Pallas kernels for 8% -> 8%
where the time goes in v32:
time: 29.1 us; the launch traced here: 28.6 us
  starting transfers between devices  16.2 us (56%)
  waiting for transfers between devices  7.23 us (25%)
  Pallas kernels  3.67 us (13%)
  between operations  1.44 us (5%)
    ppermute x6, starting transfers between devices, exchange(): lax.ppermute(send, axis, [(s, target(s, d)) for s in range(n)])  7.99 us
    ppermute x6, starting transfers between devices, swap(): return lax.ppermute(value, axis, [(s, s ^ distance) for s in range(n)])  7.8 us
    ppermute x6, waiting for transfers between devices, exchange(): lax.ppermute(send, axis, [(s, target(s, d)) for s in range(n)])  4.46 us
    ppermute x1, waiting for transfers between devices, per_device(): lax.ppermute(other, ('row', 'col'), corner)  2.13 us
    pallas_call x1, Pallas kernels, per_device(): call(functools.partial(last_kernel, scale), [((nodes, width), NARROW), ((...  0.7 us
    pallas_call x1, Pallas kernels, per_device(): call(functools.partial(dense_kernel, nodes // side, paired), [((down, acr...  0.68 us
    pallas_call x1, Pallas kernels, per_device(): act, = call(act_kernel, [((nodes, hidden), NARROW)], [VMEM])(pre)  0.65 us
    ppermute x6, waiting for transfers between devices, swap(): return lax.ppermute(value, axis, [(s, s ^ distance) for s in range(n)])  0.64 us
  transfers between devices with their start and end apart: 13, of which 6 were waited for; matrix products, arithmetic and copies ran while one was open for 0% of the time, Pallas kernels for 8%

profile of v32, /device:TPU:0, one launch (start us, length us, event | category | flops | bytes accessed | tf_op | source)
XLA Modules:
  0.0 28.6 jit_solution(4578079523091061291)
XLA Ops:
  0.6 0.0 copy-start
  0.6 2.4 %collective-permute-start.1 = (bf16[128,128]{1,0:T(8,128)(2,1)}, bf16[128,128]{1,0:T(8,128)(2,1)S(1)}, u32[]{:S(2)}, u32[]{:S(2)}) collective-permute-start(bf16[128,128]{1,0:T(8,128)(2,1)} %refs_0_.1), channel_id=1, source_target_pairs={{0,12},{4,8},{8,4},{12,0},{1,13},{5,9},{9,5},{13,1},{2,14},{6,10},... | collective-permute-start | bytes 98312 | tf_op jit(solution)/shard_map/ppermute | solution.py:57
  3.1 0.6 %collective-permute-start = (bf16[128,128]{1,0:T(8,128)(2,1)}, bf16[128,128]{1,0:T(8,128)(2,1)S(1)}, u32[]{:S(2)}, u32[]{:S(2)}) collective-permute-start(bf16[128,128]{1,0:T(8,128)(2,1)} %refs_0_.1), channel_id=1, source_target_pairs={{0,8},{4,12},{8,0},{12,4},{1,9},{5,13},{9,1},{13,5},{2,10},{6,14},... | collective-permute-start | bytes 98312 | tf_op jit(solution)/shard_map/ppermute | solution.py:57
  3.7 0.0 collective-permute-start.2
  3.8 2.8 %collective-permute-start.6 = (bf16[128,256]{1,0:T(8,128)(2,1)}, bf16[128,256]{1,0:T(8,128)(2,1)S(1)}, u32[]{:S(2)}, u32[]{:S(2)}) collective-permute-start(bf16[128,256]{1,0:T(8,128)(2,1)} %refs_6_.1), channel_id=1, source_target_pairs={{0,2},{1,3},{2,0},{3,1},{4,6},{5,7},{6,4},{7,5},{8,10},{9,11},{10,... | collective-permute-start | bytes 196616 | tf_op jit(solution)/shard_map/ppermute | solution.py:57
  6.6 0.0 copy-start.4
  6.7 0.0 copy-start.5
  7.3 0.0 copy-done
  7.3 0.0 copy-done.4
  7.3 0.0 copy-done.5
  7.4 0.0 copy-start.3
  7.4 0.7 %shard_map.95.near.matrix = bf16[512,512]{1,0:T(8,128)(2,1)S(1)} custom-call(bf16[512,512]{1,0:T(8,128)(2,1)S(1)} %shard_map.94.blank, bf16[1,1,8,128,128]{4,3,2,1,0:T(8,128)(2,1)S(1)} %copy-done, s32[1,1,8]{2,1,0:T(1,128)S(1)} %copy-done.4, s32[1,1,8]{2,1,0:T(1,128)S(1)} %copy-done.5, s32[1,1]{1,0:T(1,128)S(6)} %copy.10.count_in), custom_call_target="tpu_custom_call" | custom-call | bytes 1048576 | tf_op jit(solution)/shard_map/pallas_call | solution.py:265
  8.1 0.0 collective-permute-done.1.refs_2_
  8.1 0.0 collective-permute-done.refs_1_
  8.1 0.0 collective-permute-done.2.refs_3_
  8.1 0.0 copy-done.3
  8.1 0.3 %shard_map.97 = (bf16[256,128]{1,0:T(8,128)(2,1)S(1)}, bf16[256,128]{1,0:T(8,128)(2,1)S(1)}, bf16[256,128]{1,0:T(8,128)(2,1)S(1)}, bf16[256,128]{1,0:T(8,128)(2,1)S(1)}) custom-call(bf16[512,512]{1,0:T(8,128)(2,1)S(1)} %shard_map.95.near.matrix, bf16[128,128]{1,0:T(8,128)(2,1)S(1)} %copy-done.3, bf16[128,128]{1,0:T(8,128)(2,1)S(1)} %collective-permute-done.refs_1_, ...), custom_call_target="tpu_custom_call" | custom-call | flops 67108864 | bytes 1048576 | tf_op jit(solution)/shard_map/pallas_call | solution.py:281
  8.4 1.6 %collective-permute-start.3 = (bf16[256,128]{1,0:T(8,128)(2,1)S(1)}, bf16[256,128]{1,0:T(8,128)(2,1)S(1)}, u32[]{:S(2)}, u32[]{:S(2)}) collective-permute-start(bf16[256,128]{1,0:T(8,128)(2,1)S(1)} %get-tuple-element.18), channel_id=1, source_target_pairs={{0,1},{1,3},{2,0},{3,2},{4,5},{5,7},{6,4},{7,6},{8,9},{9,11},{10,8... | collective-permute-start | bytes 196616 | tf_op jit(solution)/shard_map/ppermute | solution.py:42
  10.1 1.6 %collective-permute-start.4 = (bf16[256,128]{1,0:T(8,128)(2,1)S(1)}, bf16[256,128]{1,0:T(8,128)(2,1)S(1)}, u32[]{:S(2)}, u32[]{:S(2)}) collective-permute-start(bf16[256,128]{1,0:T(8,128)(2,1)S(1)} %get-tuple-element.19), channel_id=1, source_target_pairs={{0,3},{1,2},{2,1},{3,0},{4,7},{5,6},{6,5},{7,4},{8,11},{9,10},{10,... | collective-permute-start | bytes 196616 | tf_op jit(solution)/shard_map/ppermute | solution.py:42
  11.7 0.0 copy-start.1
  11.7 0.0 copy-start.2
  11.7 1.6 %collective-permute-start.5 = (bf16[256,128]{1,0:T(8,128)(2,1)S(1)}, bf16[256,128]{1,0:T(8,128)(2,1)S(1)}, u32[]{:S(2)}, u32[]{:S(2)}) collective-permute-start(bf16[256,128]{1,0:T(8,128)(2,1)S(1)} %get-tuple-element.20), channel_id=1, source_target_pairs={{0,2},{1,0},{2,3},{3,1},{4,6},{5,4},{6,7},{7,5},{8,10},{9,8},{10,1... | collective-permute-start | bytes 196616 | tf_op jit(solution)/shard_map/ppermute | solution.py:42
  13.3 0.3 %shard_map.96.refs_0_.matrix = bf16[512,512]{1,0:T(8,128)(2,1)S(1)} custom-call(bf16[512,512]{1,0:T(8,128)(2,1)S(1)} %shard_map.95.near.matrix), custom_call_target="tpu_custom_call" | custom-call | bytes 1572864 | tf_op jit(solution)/shard_map/pallas_call | solution.py:298
  13.6 0.0 collective-permute-done.6.refs_7_
  13.6 0.4 %collective-permute-done.3.refs_2_ = bf16[256,128]{1,0:T(8,128)(2,1)S(1)} collective-permute-done((bf16[256,128]{1,0:T(8,128)(2,1)S(1)}, bf16[256,128]{1,0:T(8,128)(2,1)S(1)}, u32[]{:S(2)}, u32[]{:S(2)}) %collective-permute-start.3) | collective-permute-done | bytes 65568 | tf_op jit(solution)/shard_map/ppermute | solution.py:42
  14.0 2.4 %collective-permute-done.4.refs_3_ = bf16[256,128]{1,0:T(8,128)(2,1)S(1)} collective-permute-done((bf16[256,128]{1,0:T(8,128)(2,1)S(1)}, bf16[256,128]{1,0:T(8,128)(2,1)S(1)}, u32[]{:S(2)}, u32[]{:S(2)}) %collective-permute-start.4) | collective-permute-done | bytes 65568 | tf_op jit(solution)/shard_map/ppermute | solution.py:42
  16.4 0.2 collective-permute-done.5.refs_4_
  16.6 0.0 copy-done.1
  16.6 0.0 copy-done.2
  16.7 0.5 %shard_map.98 = (bf16[384,128]{1,0:T(8,128)(2,1)S(1)}, bf16[128,128]{1,0:T(8,128)(2,1)S(1)}, f32[128,256]{1,0:T(8,128)S(1)}) custom-call(bf16[512,512]{1,0:T(8,128)(2,1)S(1)} %shard_map.96.refs_0_.matrix, bf16[256,128]{1,0:T(8,128)(2,1)S(1)} %get-tuple-element.17.refs_1_, bf16[256,128]{1,0:T(8,128)(2,1)S(1)} %collective-permute-done.3.refs_2_, ...), custom_call_target="tpu_custom_call" | custom-call | flops 117440512 | tf_op jit(solution)/shard_map/pallas_call | solution.py:308
  17.2 1.8 %collective-permute-start.7 = (bf16[384,128]{1,0:T(8,128)(2,1)S(1)}, bf16[384,128]{1,0:T(8,128)(2,1)S(1)}, u32[]{:S(2)}, u32[]{:S(2)}) collective-permute-start(bf16[384,128]{1,0:T(8,128)(2,1)S(1)} %get-tuple-element.22.message.refs_0_), channel_id=1, source_target_pairs={{0,1},{1,0},{2,3},{3,2},{4,5},{5,4},{6,7},{7,6},{8,9},{9,8},{10,11... | collective-permute-start | bytes 294920 | tf_op jit(solution)/shard_map/ppermute | solution.py:57
  19.0 0.0 collective-permute-start.9
  19.0 0.4 %collective-permute-start.8 = (bf16[128,128]{1,0:T(8,128)(2,1)S(1)}, bf16[128,128]{1,0:T(8,128)(2,1)S(1)}, u32[]{:S(2)}, u32[]{:S(2)}) collective-permute-start(bf16[128,128]{1,0:T(8,128)(2,1)S(1)} %get-tuple-element.23), channel_id=1, source_target_pairs={{0,5},{1,4},{2,7},{3,6},{4,1},{5,0},{6,3},{7,2},{8,13},{9,12},{10,... | collective-permute-start | bytes 98312 | tf_op jit(solution)/shard_map/ppermute | solution.py:320
  19.4 0.2 shard_map.100.begun
  19.6 0.6 %collective-permute-done.9.refs_3_ = bf16[128,128]{1,0:T(8,128)(2,1)S(1)} collective-permute-done((bf16[128,128]{1,0:T(8,128)(2,1)S(1)}, bf16[128,128]{1,0:T(8,128)(2,1)S(1)}, u32[]{:S(2)}, u32[]{:S(2)}) %collective-permute-start.9) | collective-permute-done | bytes 32800 | tf_op jit(solution)/shard_map/ppermute | solution.py:57
  20.2 2.1 %collective-permute-done.8.refs_2_ = bf16[128,128]{1,0:T(8,128)(2,1)S(1)} collective-permute-done((bf16[128,128]{1,0:T(8,128)(2,1)S(1)}, bf16[128,128]{1,0:T(8,128)(2,1)S(1)}, u32[]{:S(2)}, u32[]{:S(2)}) %collective-permute-start.8) | collective-permute-done | bytes 32800 | tf_op jit(solution)/shard_map/ppermute | solution.py:320
  22.4 0.0 collective-permute-done.7.refs_1_
  22.4 0.2 shard_map.101
  22.6 0.6 %collective-permute-start.10 = (bf16[256,128]{1,0:T(8,128)(2,1)S(1)}, bf16[256,128]{1,0:T(8,128)(2,1)S(1)}, u32[]{:S(2)}, u32[]{:S(2)}) collective-permute-start(bf16[256,128]{1,0:T(8,128)(2,1)S(1)} %get-tuple-element.26), channel_id=1, source_target_pairs={{0,4},{4,8},{8,12},{12,0},{1,5},{5,9},{9,13},{13,1},{2,6},{6,10},{... | collective-permute-start | bytes 196616 | tf_op jit(solution)/shard_map/ppermute | solution.py:42
  23.2 1.5 %collective-permute-start.11 = (bf16[256,128]{1,0:T(8,128)(2,1)S(1)}, bf16[256,128]{1,0:T(8,128)(2,1)S(1)}, u32[]{:S(2)}, u32[]{:S(2)}) collective-permute-start(bf16[256,128]{1,0:T(8,128)(2,1)S(1)} %get-tuple-element.27), channel_id=1, source_target_pairs={{0,8},{4,12},{8,0},{12,4},{1,9},{5,13},{9,1},{13,5},{2,10},{6,14},... | collective-permute-start | bytes 196616 | tf_op jit(solution)/shard_map/ppermute | solution.py:42
  24.6 1.1 %collective-permute-start.12 = (bf16[256,128]{1,0:T(8,128)(2,1)S(1)}, bf16[256,128]{1,0:T(8,128)(2,1)S(1)}, u32[]{:S(2)}, u32[]{:S(2)}) collective-permute-start(bf16[256,128]{1,0:T(8,128)(2,1)S(1)} %get-tuple-element.28), channel_id=1, source_target_pairs={{0,12},{4,0},{8,4},{12,8},{1,13},{5,1},{9,5},{13,9},{2,14},{6,2},{... | collective-permute-start | bytes 196616 | tf_op jit(solution)/shard_map/ppermute | solution.py:42
  25.8 0.7 %shard_map.99 = bf16[128,256]{1,0:T(8,128)(2,1)} custom-call(f32[128,256]{1,0:T(8,128)S(1)} %get-tuple-element.21.pre), custom_call_target="tpu_custom_call" | custom-call | tf_op jit(solution)/shard_map/pallas_call | solution.py:325
  26.4 0.0 collective-permute-done.10.refs_0_
  26.4 1.4 %collective-permute-done.11.refs_1_ = bf16[256,128]{1,0:T(8,128)(2,1)S(1)} collective-permute-done((bf16[256,128]{1,0:T(8,128)(2,1)S(1)}, bf16[256,128]{1,0:T(8,128)(2,1)S(1)}, u32[]{:S(2)}, u32[]{:S(2)}) %collective-permute-start.11) | collective-permute-done | bytes 65568 | tf_op jit(solution)/shard_map/ppermute | solution.py:42
  27.9 0.0 collective-permute-done.12.refs_2_
  27.9 0.7 %shard_map.102 = (bf16[128,128]{1,0:T(8,128)(2,1)}, f32[128,256]{1,0:T(8,128)}) custom-call(f32[128,128]{1,0:T(8,128)S(1)} %get-tuple-element.24.own, bf16[128,128]{1,0:T(8,128)(2,1)S(1)} %get-tuple-element.25.kept, bf16[256,128]{1,0:T(8,128)(2,1)S(1)} %collective-permute-done.10.refs_0_, bf16[256,128]{1,0:T(8,128)(2,1)S(1)} %collective-permute-done.11.refs_1_, ...), custom_call_target="tpu_custom_call" | custom-call | tf_op jit(solution)/shard_map/pallas_call | solution.py:345
  (1 shorter events, 0.0 us)
Async XLA Ops:
  0.6 6.7 %copy-start = (bf16[1,1,8,128,128]{4,3,2,1,0:T(8,128)(2,1)S(1)}, bf16[1,1,8,128,128]{4,3,2,1,0:T(8,128)(2,1)}, u32[]{:S(2)}) copy-start(bf16[1,1,8,128,128]{4,3,2,1,0:T(8,128)(2,1)} %vals.1) | copy-start | bytes 786436
  0.6 7.4 %collective-permute-start.1 = (bf16[128,128]{1,0:T(8,128)(2,1)}, bf16[128,128]{1,0:T(8,128)(2,1)S(1)}, u32[]{:S(2)}, u32[]{:S(2)}) collective-permute-start(bf16[128,128]{1,0:T(8,128)(2,1)} %refs_0_.1), channel_id=1, source_target_pairs={{0,12},{4,8},{8,4},{12,0},{1,13},{5,9},{9,5},{13,1},{2,14},{6,10},... | collective-permute-start | bytes 98312 | tf_op jit(solution)/shard_map/ppermute | solution.py:57
  3.1 5.0 %collective-permute-start = (bf16[128,128]{1,0:T(8,128)(2,1)}, bf16[128,128]{1,0:T(8,128)(2,1)S(1)}, u32[]{:S(2)}, u32[]{:S(2)}) collective-permute-start(bf16[128,128]{1,0:T(8,128)(2,1)} %refs_0_.1), channel_id=1, source_target_pairs={{0,8},{4,12},{8,0},{12,4},{1,9},{5,13},{9,1},{13,5},{2,10},{6,14},... | collective-permute-start | bytes 98312 | tf_op jit(solution)/shard_map/ppermute | solution.py:57
  3.7 4.4 %collective-permute-start.2 = (bf16[128,128]{1,0:T(8,128)(2,1)}, bf16[128,128]{1,0:T(8,128)(2,1)S(1)}, u32[]{:S(2)}, u32[]{:S(2)}) collective-permute-start(bf16[128,128]{1,0:T(8,128)(2,1)} %refs_0_.1), channel_id=1, source_target_pairs={{0,4},{4,0},{8,12},{12,8},{1,5},{5,1},{9,13},{13,9},{2,6},{6,2},{1... | collective-permute-start | bytes 98312 | tf_op jit(solution)/shard_map/ppermute | solution.py:57
  3.8 9.9 %collective-permute-start.6 = (bf16[128,256]{1,0:T(8,128)(2,1)}, bf16[128,256]{1,0:T(8,128)(2,1)S(1)}, u32[]{:S(2)}, u32[]{:S(2)}) collective-permute-start(bf16[128,256]{1,0:T(8,128)(2,1)} %refs_6_.1), channel_id=1, source_target_pairs={{0,2},{1,3},{2,0},{3,1},{4,6},{5,7},{6,4},{7,5},{8,10},{9,11},{10,... | collective-permute-start | bytes 196616 | tf_op jit(solution)/shard_map/ppermute | solution.py:57
  6.6 0.7 %copy-start.4 = (s32[1,1,8]{2,1,0:T(1,128)S(1)}, s32[1,1,8]{2,1,0:T(1,128)}, u32[]{:S(2)}) copy-start(s32[1,1,8]{2,1,0:T(1,128)} %rows_in.1) | copy-start | bytes 100
  6.7 0.7 %copy-start.5 = (s32[1,1,8]{2,1,0:T(1,128)S(1)}, s32[1,1,8]{2,1,0:T(1,128)}, u32[]{:S(2)}) copy-start(s32[1,1,8]{2,1,0:T(1,128)} %cols_in.1) | copy-start | bytes 100
  7.4 0.8 %copy-start.3 = (bf16[128,128]{1,0:T(8,128)(2,1)S(1)}, bf16[128,128]{1,0:T(8,128)(2,1)}, u32[]{:S(2)}) copy-start(bf16[128,128]{1,0:T(8,128)(2,1)} %refs_0_.1) | copy-start | bytes 98308
  8.4 5.6 %collective-permute-start.3 = (bf16[256,128]{1,0:T(8,128)(2,1)S(1)}, bf16[256,128]{1,0:T(8,128)(2,1)S(1)}, u32[]{:S(2)}, u32[]{:S(2)}) collective-permute-start(bf16[256,128]{1,0:T(8,128)(2,1)S(1)} %get-tuple-element.18), channel_id=1, source_target_pairs={{0,1},{1,3},{2,0},{3,2},{4,5},{5,7},{6,4},{7,6},{8,9},{9,11},{10,8... | collective-permute-start | bytes 196616 | tf_op jit(solution)/shard_map/ppermute | solution.py:42
  10.1 6.4 %collective-permute-start.4 = (bf16[256,128]{1,0:T(8,128)(2,1)S(1)}, bf16[256,128]{1,0:T(8,128)(2,1)S(1)}, u32[]{:S(2)}, u32[]{:S(2)}) collective-permute-start(bf16[256,128]{1,0:T(8,128)(2,1)S(1)} %get-tuple-element.19), channel_id=1, source_target_pairs={{0,3},{1,2},{2,1},{3,0},{4,7},{5,6},{6,5},{7,4},{8,11},{9,10},{10,... | collective-permute-start | bytes 196616 | tf_op jit(solution)/shard_map/ppermute | solution.py:42
  11.7 5.0 %copy-start.1 = (bf16[128,256]{1,0:T(8,128)(2,1)S(1)}, bf16[128,256]{1,0:T(8,128)(2,1)}, u32[]{:S(2)}) copy-start(bf16[128,256]{1,0:T(8,128)(2,1)} %refs_5_.1) | copy-start | bytes 196612
  11.7 5.0 %copy-start.2 = (bf16[128,256]{1,0:T(8,128)(2,1)S(1)}, bf16[128,256]{1,0:T(8,128)(2,1)}, u32[]{:S(2)}) copy-start(bf16[128,256]{1,0:T(8,128)(2,1)} %refs_6_.1) | copy-start | bytes 196612
  11.7 5.0 %collective-permute-start.5 = (bf16[256,128]{1,0:T(8,128)(2,1)S(1)}, bf16[256,128]{1,0:T(8,128)(2,1)S(1)}, u32[]{:S(2)}, u32[]{:S(2)}) collective-permute-start(bf16[256,128]{1,0:T(8,128)(2,1)S(1)} %get-tuple-element.20), channel_id=1, source_target_pairs={{0,2},{1,0},{2,3},{3,1},{4,6},{5,4},{6,7},{7,5},{8,10},{9,8},{10,1... | collective-permute-start | bytes 196616 | tf_op jit(solution)/shard_map/ppermute | solution.py:42
  17.2 5.2 %collective-permute-start.7 = (bf16[384,128]{1,0:T(8,128)(2,1)S(1)}, bf16[384,128]{1,0:T(8,128)(2,1)S(1)}, u32[]{:S(2)}, u32[]{:S(2)}) collective-permute-start(bf16[384,128]{1,0:T(8,128)(2,1)S(1)} %get-tuple-element.22.message.refs_0_), channel_id=1, source_target_pairs={{0,1},{1,0},{2,3},{3,2},{4,5},{5,4},{6,7},{7,6},{8,9},{9,8},{10,11... | collective-permute-start | bytes 294920 | tf_op jit(solution)/shard_map/ppermute | solution.py:57
  19.0 1.2 %collective-permute-start.9 = (bf16[128,128]{1,0:T(8,128)(2,1)S(1)}, bf16[128,128]{1,0:T(8,128)(2,1)S(1)}, u32[]{:S(2)}, u32[]{:S(2)}) collective-permute-start(bf16[128,128]{1,0:T(8,128)(2,1)S(1)} %get-tuple-element.23), channel_id=1, source_target_pairs={{0,4},{4,0},{8,12},{12,8},{1,5},{5,1},{9,13},{13,9},{2,6},{6,2},{1... | collective-permute-start | bytes 98312 | tf_op jit(solution)/shard_map/ppermute | solution.py:57
  19.0 3.3 %collective-permute-start.8 = (bf16[128,128]{1,0:T(8,128)(2,1)S(1)}, bf16[128,128]{1,0:T(8,128)(2,1)S(1)}, u32[]{:S(2)}, u32[]{:S(2)}) collective-permute-start(bf16[128,128]{1,0:T(8,128)(2,1)S(1)} %get-tuple-element.23), channel_id=1, source_target_pairs={{0,5},{1,4},{2,7},{3,6},{4,1},{5,0},{6,3},{7,2},{8,13},{9,12},{10,... | collective-permute-start | bytes 98312 | tf_op jit(solution)/shard_map/ppermute | solution.py:320
  22.6 3.8 %collective-permute-start.10 = (bf16[256,128]{1,0:T(8,128)(2,1)S(1)}, bf16[256,128]{1,0:T(8,128)(2,1)S(1)}, u32[]{:S(2)}, u32[]{:S(2)}) collective-permute-start(bf16[256,128]{1,0:T(8,128)(2,1)S(1)} %get-tuple-element.26), channel_id=1, source_target_pairs={{0,4},{4,8},{8,12},{12,0},{1,5},{5,9},{9,13},{13,1},{2,6},{6,10},{... | collective-permute-start | bytes 196616 | tf_op jit(solution)/shard_map/ppermute | solution.py:42
  23.2 4.7 %collective-permute-start.11 = (bf16[256,128]{1,0:T(8,128)(2,1)S(1)}, bf16[256,128]{1,0:T(8,128)(2,1)S(1)}, u32[]{:S(2)}, u32[]{:S(2)}) collective-permute-start(bf16[256,128]{1,0:T(8,128)(2,1)S(1)} %get-tuple-element.27), channel_id=1, source_target_pairs={{0,8},{4,12},{8,0},{12,4},{1,9},{5,13},{9,1},{13,5},{2,10},{6,14},... | collective-permute-start | bytes 196616 | tf_op jit(solution)/shard_map/ppermute | solution.py:42
  24.6 3.2 %collective-permute-start.12 = (bf16[256,128]{1,0:T(8,128)(2,1)S(1)}, bf16[256,128]{1,0:T(8,128)(2,1)S(1)}, u32[]{:S(2)}, u32[]{:S(2)}) collective-permute-start(bf16[256,128]{1,0:T(8,128)(2,1)S(1)} %get-tuple-element.28), channel_id=1, source_target_pairs={{0,12},{4,0},{8,4},{12,8},{1,13},{5,1},{9,5},{13,9},{2,14},{6,2},{... | collective-permute-start | bytes 196616 | tf_op jit(solution)/shard_map/ppermute | solution.py:42

commit v33 on v29

--- a/solution.py
+++ b/solution.py
@@ -49,7 +49,7 @@
 
 
 def start_order(n):
-    return [*range(2, n), 1]
+    return [*range(n - 1, 0, -1)]
 
 
 def swap(value, axis, distance):

time: 28.9 us -> 29.3 us (1.014)
  waiting for transfers between devices: 7.25 us -> 7.81 us
  starting transfers between devices: 16.1 us -> 15.7 us
    ppermute x6, waiting for transfers between devices: 4.27 us -> 5.14 us  [exchange(): lax.ppermute(send, axis, [(s, target(s, d)) for s in range(n)])]
    ppermute x6, starting transfers between devices: 7.95 us -> 7.3 us  [exchange(): lax.ppermute(send, axis, [(s, target(s, d)) for s in range(n)])]
    ppermute x1, waiting for transfers between devices: 2.96 us -> 2.66 us  [per_device(): lax.ppermute(other, ('row', 'col'), corner)]
  transfers between devices with their start and end apart: 13 -> 13, of which waited for: 7 -> 4; matrix products, arithmetic and copies ran while one was open for 0% -> 0% of each run, Pallas kernels for 8% -> 8%
where the time goes in v33:
time: 29.3 us; the launch traced here: 28.8 us
  starting transfers between devices  15.7 us (54%)
  waiting for transfers between devices  7.81 us (27%)
  Pallas kernels  3.77 us (13%)
  between operations  1.46 us (5%)
    ppermute x6, starting transfers between devices, swap(): return lax.ppermute(value, axis, [(s, s ^ distance) for s in range(n)])  8.45 us
    ppermute x6, starting transfers between devices, exchange(): lax.ppermute(send, axis, [(s, target(s, d)) for s in range(n)])  7.3 us
    ppermute x6, waiting for transfers between devices, exchange(): lax.ppermute(send, axis, [(s, target(s, d)) for s in range(n)])  5.14 us
    ppermute x1, waiting for transfers between devices, per_device(): lax.ppermute(other, ('row', 'col'), corner)  2.66 us
    pallas_call x1, Pallas kernels, per_device(): call(functools.partial(dense_kernel, nodes // side, paired), [((down, acr...  0.77 us
    pallas_call x1, Pallas kernels, per_device(): call(functools.partial(last_kernel, scale), [((nodes, width), NARROW), ((...  0.7 us
    pallas_call x1, Pallas kernels, per_device(): act, = call(act_kernel, [((nodes, hidden), NARROW)], [VMEM])(pre)  0.65 us
  transfers between devices with their start and end apart: 13, of which 4 were waited for; matrix products, arithmetic and copies ran while one was open for 0% of the time, Pallas kernels for 8%

profile of v33, /device:TPU:0, one launch (start us, length us, event | category | flops | bytes accessed | tf_op | source)
XLA Modules:
  0.0 28.8 jit_solution(1599552525167179764)
XLA Ops:
  0.6 0.0 copy-start
  0.6 3.0 %collective-permute-start.1 = (bf16[128,128]{1,0:T(8,128)(2,1)}, bf16[128,128]{1,0:T(8,128)(2,1)S(1)}, u32[]{:S(2)}, u32[]{:S(2)}) collective-permute-start(bf16[128,128]{1,0:T(8,128)(2,1)} %refs_0_.1), channel_id=1, source_target_pairs={{0,8},{4,12},{8,0},{12,4},{1,9},{5,13},{9,1},{13,5},{2,10},{6,14},... | collective-permute-start | bytes 98312 | tf_op jit(solution)/shard_map/ppermute | solution.py:57
  3.6 0.0 collective-permute-start
  3.6 0.2 collective-permute-start.2
  3.8 3.0 %collective-permute-start.6 = (bf16[128,256]{1,0:T(8,128)(2,1)}, bf16[128,256]{1,0:T(8,128)(2,1)S(1)}, u32[]{:S(2)}, u32[]{:S(2)}) collective-permute-start(bf16[128,256]{1,0:T(8,128)(2,1)} %refs_6_.1), channel_id=1, source_target_pairs={{0,2},{1,3},{2,0},{3,1},{4,6},{5,7},{6,4},{7,5},{8,10},{9,11},{10,... | collective-permute-start | bytes 196616 | tf_op jit(solution)/shard_map/ppermute | solution.py:57
  6.9 0.0 copy-start.4
  6.9 0.0 copy-start.5
  7.6 0.0 copy-done
  7.6 0.0 copy-done.4
  7.6 0.0 copy-done.5
  7.6 0.0 copy-start.3
  7.7 0.8 %shard_map.95.near.matrix = bf16[512,512]{1,0:T(8,128)(2,1)S(1)} custom-call(bf16[512,512]{1,0:T(8,128)(2,1)S(1)} %shard_map.94.blank, bf16[1,1,8,128,128]{4,3,2,1,0:T(8,128)(2,1)S(1)} %copy-done, s32[1,1,8]{2,1,0:T(1,128)S(1)} %copy-done.4, s32[1,1,8]{2,1,0:T(1,128)S(1)} %copy-done.5, s32[1,1]{1,0:T(1,128)S(6)} %copy.10.count_in), custom_call_target="tpu_custom_call" | custom-call | bytes 1048576 | tf_op jit(solution)/shard_map/pallas_call | solution.py:265
  8.4 0.0 collective-permute-done.1.refs_2_
  8.4 0.0 collective-permute-done.refs_1_
  8.5 0.0 collective-permute-done.2.refs_3_
  8.5 0.0 copy-done.3
  8.5 0.3 %shard_map.97 = (bf16[256,128]{1,0:T(8,128)(2,1)S(1)}, bf16[256,128]{1,0:T(8,128)(2,1)S(1)}, bf16[256,128]{1,0:T(8,128)(2,1)S(1)}, bf16[256,128]{1,0:T(8,128)(2,1)S(1)}) custom-call(bf16[512,512]{1,0:T(8,128)(2,1)S(1)} %shard_map.95.near.matrix, bf16[128,128]{1,0:T(8,128)(2,1)S(1)} %copy-done.3, bf16[128,128]{1,0:T(8,128)(2,1)S(1)} %collective-permute-done.refs_1_, ...), custom_call_target="tpu_custom_call" | custom-call | flops 67108864 | bytes 1048576 | tf_op jit(solution)/shard_map/pallas_call | solution.py:281
  8.8 1.6 %collective-permute-start.3 = (bf16[256,128]{1,0:T(8,128)(2,1)S(1)}, bf16[256,128]{1,0:T(8,128)(2,1)S(1)}, u32[]{:S(2)}, u32[]{:S(2)}) collective-permute-start(bf16[256,128]{1,0:T(8,128)(2,1)S(1)} %get-tuple-element.18), channel_id=1, source_target_pairs={{0,1},{1,3},{2,0},{3,2},{4,5},{5,7},{6,4},{7,6},{8,9},{9,11},{10,8... | collective-permute-start | bytes 196616 | tf_op jit(solution)/shard_map/ppermute | solution.py:42
  10.3 1.4 %collective-permute-start.4 = (bf16[256,128]{1,0:T(8,128)(2,1)S(1)}, bf16[256,128]{1,0:T(8,128)(2,1)S(1)}, u32[]{:S(2)}, u32[]{:S(2)}) collective-permute-start(bf16[256,128]{1,0:T(8,128)(2,1)S(1)} %get-tuple-element.19), channel_id=1, source_target_pairs={{0,3},{1,2},{2,1},{3,0},{4,7},{5,6},{6,5},{7,4},{8,11},{9,10},{10,... | collective-permute-start | bytes 196616 | tf_op jit(solution)/shard_map/ppermute | solution.py:42
  11.7 0.0 copy-start.1
  11.7 0.0 copy-start.2
  11.7 1.6 %collective-permute-start.5 = (bf16[256,128]{1,0:T(8,128)(2,1)S(1)}, bf16[256,128]{1,0:T(8,128)(2,1)S(1)}, u32[]{:S(2)}, u32[]{:S(2)}) collective-permute-start(bf16[256,128]{1,0:T(8,128)(2,1)S(1)} %get-tuple-element.20), channel_id=1, source_target_pairs={{0,2},{1,0},{2,3},{3,1},{4,6},{5,4},{6,7},{7,5},{8,10},{9,8},{10,1... | collective-permute-start | bytes 196616 | tf_op jit(solution)/shard_map/ppermute | solution.py:42
  13.3 0.3 %shard_map.96.refs_0_.matrix = bf16[512,512]{1,0:T(8,128)(2,1)S(1)} custom-call(bf16[512,512]{1,0:T(8,128)(2,1)S(1)} %shard_map.95.near.matrix), custom_call_target="tpu_custom_call" | custom-call | bytes 1572864 | tf_op jit(solution)/shard_map/pallas_call | solution.py:298
  13.6 0.0 collective-permute-done.6.refs_7_
  13.6 3.7 %collective-permute-done.3.refs_2_ = bf16[256,128]{1,0:T(8,128)(2,1)S(1)} collective-permute-done((bf16[256,128]{1,0:T(8,128)(2,1)S(1)}, bf16[256,128]{1,0:T(8,128)(2,1)S(1)}, u32[]{:S(2)}, u32[]{:S(2)}) %collective-permute-start.3) | collective-permute-done | bytes 65568 | tf_op jit(solution)/shard_map/ppermute | solution.py:42
  17.4 0.0 collective-permute-done.4.refs_3_
  17.4 0.0 collective-permute-done.5.refs_4_
  17.4 0.0 copy-done.1
  17.4 0.0 copy-done.2
  17.4 0.5 %shard_map.98 = (bf16[384,128]{1,0:T(8,128)(2,1)S(1)}, bf16[128,128]{1,0:T(8,128)(2,1)S(1)}, f32[128,256]{1,0:T(8,128)S(1)}) custom-call(bf16[512,512]{1,0:T(8,128)(2,1)S(1)} %shard_map.96.refs_0_.matrix, bf16[256,128]{1,0:T(8,128)(2,1)S(1)} %get-tuple-element.17.refs_1_, bf16[256,128]{1,0:T(8,128)(2,1)S(1)} %collective-permute-done.3.refs_2_, ...), custom_call_target="tpu_custom_call" | custom-call | flops 117440512 | tf_op jit(solution)/shard_map/pallas_call | solution.py:308
  17.9 1.4 %collective-permute-start.7 = (bf16[384,128]{1,0:T(8,128)(2,1)S(1)}, bf16[384,128]{1,0:T(8,128)(2,1)S(1)}, u32[]{:S(2)}, u32[]{:S(2)}) collective-permute-start(bf16[384,128]{1,0:T(8,128)(2,1)S(1)} %get-tuple-element.22.message.refs_0_), channel_id=1, source_target_pairs={{0,1},{1,0},{2,3},{3,2},{4,5},{5,4},{6,7},{7,6},{8,9},{9,8},{10,11... | collective-permute-start | bytes 294920 | tf_op jit(solution)/shard_map/ppermute | solution.py:57
  19.4 0.0 collective-permute-start.9
  19.4 0.8 %collective-permute-start.8 = (bf16[128,128]{1,0:T(8,128)(2,1)S(1)}, bf16[128,128]{1,0:T(8,128)(2,1)S(1)}, u32[]{:S(2)}, u32[]{:S(2)}) collective-permute-start(bf16[128,128]{1,0:T(8,128)(2,1)S(1)} %get-tuple-element.23), channel_id=1, source_target_pairs={{0,4},{4,0},{8,12},{12,8},{1,5},{5,1},{9,13},{13,9},{2,6},{6,2},{1... | collective-permute-start | bytes 98312 | tf_op jit(solution)/shard_map/ppermute | solution.py:57
  20.1 0.2 shard_map.100.begun
  20.4 2.7 %collective-permute-done.9.refs_3_ = bf16[128,128]{1,0:T(8,128)(2,1)S(1)} collective-permute-done((bf16[128,128]{1,0:T(8,128)(2,1)S(1)}, bf16[128,128]{1,0:T(8,128)(2,1)S(1)}, u32[]{:S(2)}, u32[]{:S(2)}) %collective-permute-start.9) | collective-permute-done | bytes 32800 | tf_op jit(solution)/shard_map/ppermute | solution.py:320
  23.0 0.0 collective-permute-done.8.refs_2_
  23.0 0.0 collective-permute-done.7.refs_1_
  23.0 0.2 shard_map.101
  23.3 0.2 collective-permute-start.10
  23.4 1.3 %collective-permute-start.11 = (bf16[256,128]{1,0:T(8,128)(2,1)S(1)}, bf16[256,128]{1,0:T(8,128)(2,1)S(1)}, u32[]{:S(2)}, u32[]{:S(2)}) collective-permute-start(bf16[256,128]{1,0:T(8,128)(2,1)S(1)} %get-tuple-element.27), channel_id=1, source_target_pairs={{0,8},{4,12},{8,0},{12,4},{1,9},{5,13},{9,1},{13,5},{2,10},{6,14},... | collective-permute-start | bytes 196616 | tf_op jit(solution)/shard_map/ppermute | solution.py:42
  24.8 1.3 %collective-permute-start.12 = (bf16[256,128]{1,0:T(8,128)(2,1)S(1)}, bf16[256,128]{1,0:T(8,128)(2,1)S(1)}, u32[]{:S(2)}, u32[]{:S(2)}) collective-permute-start(bf16[256,128]{1,0:T(8,128)(2,1)S(1)} %get-tuple-element.28), channel_id=1, source_target_pairs={{0,12},{4,0},{8,4},{12,8},{1,13},{5,1},{9,5},{13,9},{2,14},{6,2},{... | collective-permute-start | bytes 196616 | tf_op jit(solution)/shard_map/ppermute | solution.py:42
  26.1 0.7 %shard_map.99 = bf16[128,256]{1,0:T(8,128)(2,1)} custom-call(f32[128,256]{1,0:T(8,128)S(1)} %get-tuple-element.21.pre), custom_call_target="tpu_custom_call" | custom-call | tf_op jit(solution)/shard_map/pallas_call | solution.py:325
  26.7 0.3 %collective-permute-done.10.refs_0_ = bf16[256,128]{1,0:T(8,128)(2,1)S(1)} collective-permute-done((bf16[256,128]{1,0:T(8,128)(2,1)S(1)}, bf16[256,128]{1,0:T(8,128)(2,1)S(1)}, u32[]{:S(2)}, u32[]{:S(2)}) %collective-permute-start.10) | collective-permute-done | bytes 65568 | tf_op jit(solution)/shard_map/ppermute | solution.py:42
  27.1 1.0 %collective-permute-done.11.refs_1_ = bf16[256,128]{1,0:T(8,128)(2,1)S(1)} collective-permute-done((bf16[256,128]{1,0:T(8,128)(2,1)S(1)}, bf16[256,128]{1,0:T(8,128)(2,1)S(1)}, u32[]{:S(2)}, u32[]{:S(2)}) %collective-permute-start.11) | collective-permute-done | bytes 65568 | tf_op jit(solution)/shard_map/ppermute | solution.py:42
  28.1 0.0 collective-permute-done.12.refs_2_
  28.1 0.7 %shard_map.102 = (bf16[128,128]{1,0:T(8,128)(2,1)}, f32[128,256]{1,0:T(8,128)}) custom-call(f32[128,128]{1,0:T(8,128)S(1)} %get-tuple-element.24.own, bf16[128,128]{1,0:T(8,128)(2,1)S(1)} %get-tuple-element.25.kept, bf16[256,128]{1,0:T(8,128)(2,1)S(1)} %collective-permute-done.10.refs_0_, bf16[256,128]{1,0:T(8,128)(2,1)S(1)} %collective-permute-done.11.refs_1_, ...), custom_call_target="tpu_custom_call" | custom-call | tf_op jit(solution)/shard_map/pallas_call | solution.py:345
  (1 shorter events, 0.0 us)
Async XLA Ops:
  0.6 7.0 %copy-start = (bf16[1,1,8,128,128]{4,3,2,1,0:T(8,128)(2,1)S(1)}, bf16[1,1,8,128,128]{4,3,2,1,0:T(8,128)(2,1)}, u32[]{:S(2)}) copy-start(bf16[1,1,8,128,128]{4,3,2,1,0:T(8,128)(2,1)} %vals.1) | copy-start | bytes 786436
  0.6 7.8 %collective-permute-start.1 = (bf16[128,128]{1,0:T(8,128)(2,1)}, bf16[128,128]{1,0:T(8,128)(2,1)S(1)}, u32[]{:S(2)}, u32[]{:S(2)}) collective-permute-start(bf16[128,128]{1,0:T(8,128)(2,1)} %refs_0_.1), channel_id=1, source_target_pairs={{0,8},{4,12},{8,0},{12,4},{1,9},{5,13},{9,1},{13,5},{2,10},{6,14},... | collective-permute-start | bytes 98312 | tf_op jit(solution)/shard_map/ppermute | solution.py:57
  3.6 4.8 %collective-permute-start = (bf16[128,128]{1,0:T(8,128)(2,1)}, bf16[128,128]{1,0:T(8,128)(2,1)S(1)}, u32[]{:S(2)}, u32[]{:S(2)}) collective-permute-start(bf16[128,128]{1,0:T(8,128)(2,1)} %refs_0_.1), channel_id=1, source_target_pairs={{0,12},{4,8},{8,4},{12,0},{1,13},{5,9},{9,5},{13,1},{2,14},{6,10},... | collective-permute-start | bytes 98312 | tf_op jit(solution)/shard_map/ppermute | solution.py:57
  3.6 4.8 %collective-permute-start.2 = (bf16[128,128]{1,0:T(8,128)(2,1)}, bf16[128,128]{1,0:T(8,128)(2,1)S(1)}, u32[]{:S(2)}, u32[]{:S(2)}) collective-permute-start(bf16[128,128]{1,0:T(8,128)(2,1)} %refs_0_.1), channel_id=1, source_target_pairs={{0,4},{4,0},{8,12},{12,8},{1,5},{5,1},{9,13},{13,9},{2,6},{6,2},{1... | collective-permute-start | bytes 98312 | tf_op jit(solution)/shard_map/ppermute | solution.py:57
  3.8 9.8 %collective-permute-start.6 = (bf16[128,256]{1,0:T(8,128)(2,1)}, bf16[128,256]{1,0:T(8,128)(2,1)S(1)}, u32[]{:S(2)}, u32[]{:S(2)}) collective-permute-start(bf16[128,256]{1,0:T(8,128)(2,1)} %refs_6_.1), channel_id=1, source_target_pairs={{0,2},{1,3},{2,0},{3,1},{4,6},{5,7},{6,4},{7,5},{8,10},{9,11},{10,... | collective-permute-start | bytes 196616 | tf_op jit(solution)/shard_map/ppermute | solution.py:57
  6.9 0.7 %copy-start.4 = (s32[1,1,8]{2,1,0:T(1,128)S(1)}, s32[1,1,8]{2,1,0:T(1,128)}, u32[]{:S(2)}) copy-start(s32[1,1,8]{2,1,0:T(1,128)} %rows_in.1) | copy-start | bytes 100
  6.9 0.7 %copy-start.5 = (s32[1,1,8]{2,1,0:T(1,128)S(1)}, s32[1,1,8]{2,1,0:T(1,128)}, u32[]{:S(2)}) copy-start(s32[1,1,8]{2,1,0:T(1,128)} %cols_in.1) | copy-start | bytes 100
  7.6 0.8 %copy-start.3 = (bf16[128,128]{1,0:T(8,128)(2,1)S(1)}, bf16[128,128]{1,0:T(8,128)(2,1)}, u32[]{:S(2)}) copy-start(bf16[128,128]{1,0:T(8,128)(2,1)} %refs_0_.1) | copy-start | bytes 98308
  8.8 8.6 %collective-permute-start.3 = (bf16[256,128]{1,0:T(8,128)(2,1)S(1)}, bf16[256,128]{1,0:T(8,128)(2,1)S(1)}, u32[]{:S(2)}, u32[]{:S(2)}) collective-permute-start(bf16[256,128]{1,0:T(8,128)(2,1)S(1)} %get-tuple-element.18), channel_id=1, source_target_pairs={{0,1},{1,3},{2,0},{3,2},{4,5},{5,7},{6,4},{7,6},{8,9},{9,11},{10,8... | collective-permute-start | bytes 196616 | tf_op jit(solution)/shard_map/ppermute | solution.py:42
  10.3 7.1 %collective-permute-start.4 = (bf16[256,128]{1,0:T(8,128)(2,1)S(1)}, bf16[256,128]{1,0:T(8,128)(2,1)S(1)}, u32[]{:S(2)}, u32[]{:S(2)}) collective-permute-start(bf16[256,128]{1,0:T(8,128)(2,1)S(1)} %get-tuple-element.19), channel_id=1, source_target_pairs={{0,3},{1,2},{2,1},{3,0},{4,7},{5,6},{6,5},{7,4},{8,11},{9,10},{10,... | collective-permute-start | bytes 196616 | tf_op jit(solution)/shard_map/ppermute | solution.py:42
  11.7 5.7 %copy-start.1 = (bf16[128,256]{1,0:T(8,128)(2,1)S(1)}, bf16[128,256]{1,0:T(8,128)(2,1)}, u32[]{:S(2)}) copy-start(bf16[128,256]{1,0:T(8,128)(2,1)} %refs_5_.1) | copy-start | bytes 196612
  11.7 5.7 %copy-start.2 = (bf16[128,256]{1,0:T(8,128)(2,1)S(1)}, bf16[128,256]{1,0:T(8,128)(2,1)}, u32[]{:S(2)}) copy-start(bf16[128,256]{1,0:T(8,128)(2,1)} %refs_6_.1) | copy-start | bytes 196612
  11.7 5.7 %collective-permute-start.5 = (bf16[256,128]{1,0:T(8,128)(2,1)S(1)}, bf16[256,128]{1,0:T(8,128)(2,1)S(1)}, u32[]{:S(2)}, u32[]{:S(2)}) collective-permute-start(bf16[256,128]{1,0:T(8,128)(2,1)S(1)} %get-tuple-element.20), channel_id=1, source_target_pairs={{0,2},{1,0},{2,3},{3,1},{4,6},{5,4},{6,7},{7,5},{8,10},{9,8},{10,1... | collective-permute-start | bytes 196616 | tf_op jit(solution)/shard_map/ppermute | solution.py:42
  17.9 5.1 %collective-permute-start.7 = (bf16[384,128]{1,0:T(8,128)(2,1)S(1)}, bf16[384,128]{1,0:T(8,128)(2,1)S(1)}, u32[]{:S(2)}, u32[]{:S(2)}) collective-permute-start(bf16[384,128]{1,0:T(8,128)(2,1)S(1)} %get-tuple-element.22.message.refs_0_), channel_id=1, source_target_pairs={{0,1},{1,0},{2,3},{3,2},{4,5},{5,4},{6,7},{7,6},{8,9},{9,8},{10,11... | collective-permute-start | bytes 294920 | tf_op jit(solution)/shard_map/ppermute | solution.py:57
  19.4 3.7 %collective-permute-start.9 = (bf16[128,128]{1,0:T(8,128)(2,1)S(1)}, bf16[128,128]{1,0:T(8,128)(2,1)S(1)}, u32[]{:S(2)}, u32[]{:S(2)}) collective-permute-start(bf16[128,128]{1,0:T(8,128)(2,1)S(1)} %get-tuple-element.23), channel_id=1, source_target_pairs={{0,5},{1,4},{2,7},{3,6},{4,1},{5,0},{6,3},{7,2},{8,13},{9,12},{10,... | collective-permute-start | bytes 98312 | tf_op jit(solution)/shard_map/ppermute | solution.py:320
  19.4 3.7 %collective-permute-start.8 = (bf16[128,128]{1,0:T(8,128)(2,1)S(1)}, bf16[128,128]{1,0:T(8,128)(2,1)S(1)}, u32[]{:S(2)}, u32[]{:S(2)}) collective-permute-start(bf16[128,128]{1,0:T(8,128)(2,1)S(1)} %get-tuple-element.23), channel_id=1, source_target_pairs={{0,4},{4,0},{8,12},{12,8},{1,5},{5,1},{9,13},{13,9},{2,6},{6,2},{1... | collective-permute-start | bytes 98312 | tf_op jit(solution)/shard_map/ppermute | solution.py:57
  23.3 3.8 %collective-permute-start.10 = (bf16[256,128]{1,0:T(8,128)(2,1)S(1)}, bf16[256,128]{1,0:T(8,128)(2,1)S(1)}, u32[]{:S(2)}, u32[]{:S(2)}) collective-permute-start(bf16[256,128]{1,0:T(8,128)(2,1)S(1)} %get-tuple-element.26), channel_id=1, source_target_pairs={{0,4},{4,8},{8,12},{12,0},{1,5},{5,9},{9,13},{13,1},{2,6},{6,10},{... | collective-permute-start | bytes 196616 | tf_op jit(solution)/shard_map/ppermute | solution.py:42
  23.4 4.7 %collective-permute-start.11 = (bf16[256,128]{1,0:T(8,128)(2,1)S(1)}, bf16[256,128]{1,0:T(8,128)(2,1)S(1)}, u32[]{:S(2)}, u32[]{:S(2)}) collective-permute-start(bf16[256,128]{1,0:T(8,128)(2,1)S(1)} %get-tuple-element.27), channel_id=1, source_target_pairs={{0,8},{4,12},{8,0},{12,4},{1,9},{5,13},{9,1},{13,5},{2,10},{6,14},... | collective-permute-start | bytes 196616 | tf_op jit(solution)/shard_map/ppermute | solution.py:42
  24.8 3.3 %collective-permute-start.12 = (bf16[256,128]{1,0:T(8,128)(2,1)S(1)}, bf16[256,128]{1,0:T(8,128)(2,1)S(1)}, u32[]{:S(2)}, u32[]{:S(2)}) collective-permute-start(bf16[256,128]{1,0:T(8,128)(2,1)S(1)} %get-tuple-element.28), channel_id=1, source_target_pairs={{0,12},{4,0},{8,4},{12,8},{1,13},{5,1},{9,5},{13,9},{2,14},{6,2},{... | collective-permute-start | bytes 196616 | tf_op jit(solution)/shard_map/ppermute | solution.py:42
